TPU v7x, 32 devices: a whole 2x2x4 slice. The times are simulated.
32 devices in a mesh: sta: 8 (over z, y), seg: 4 (over x, core).
Axes of the slice: x: 2, y: 2, z: 4, core: 2. Of those that a mesh axis runs over, the one named last changes fastest.
Arguments:
- records: float32 [128, 16, 2048], P('sta', 'seg'), as said below
- plan: int32 [4, 8], replicated, may hold values from 0 to 7, as said below
Outputs:
- correlations: float32 [2048, 4, 2048], P('seg', None, 'sta')
Inputs may be any that keep to these rules, and one draw needn't show every extreme that they name: Row r pairs the 8 blocks: plan[r, plan[r, b]] = b and plan[r, b] != b; no two rows pair the same two blocks. `records`: raw ground-motion samples.
All inputs are finite; a program needn't handle non-finite values.
Results may differ from a plain program's by a relative error of at most 0.0075.
Values may be sent and summed in bfloat16 or wider, within the bound.
No kernel may reach another device: no remote copies, remote signals or barrier semaphores. Data moves between devices by JAX's collectives and lax.ppermute only.
A program may use at most 128 MiB of HBM per device.

v0:
```python
import math

import jax
import jax.numpy as jnp
from jax import lax
from jax.sharding import PartitionSpec as P

WLEN = 2048
NBIN = 1024
HALF = 64
ROUNDS = 4
LAGS = 2048


def band_mean(values, half_width):
    row_count, length = values.shape
    block_width = 2 * half_width
    blocks_count = length // block_width
    inside = jnp.arange(block_width, dtype=jnp.int32)
    source = inside[:, None]
    target = inside[None, :]
    inner_band = (jnp.abs(source - target) <= half_width).astype(jnp.bfloat16)
    before = (target + block_width - source <= half_width).astype(jnp.bfloat16)
    after_band = (source + block_width - target <= half_width).astype(jnp.bfloat16)
    blocks = values.reshape(row_count, blocks_count, block_width)
    earlier = jnp.pad(blocks[:, :-1], ((0, 0), (1, 0), (0, 0)))
    following = jnp.pad(blocks[:, 1:], ((0, 0), (0, 1), (0, 0)))
    flat_shape = (row_count * blocks_count, block_width)
    running = jnp.dot(blocks.reshape(flat_shape), inner_band, preferred_element_type=jnp.float32)
    running = running + jnp.dot(
        earlier.reshape(flat_shape), before, preferred_element_type=jnp.float32
    )
    running = running + jnp.dot(
        following.reshape(flat_shape), after_band, preferred_element_type=jnp.float32
    )
    position = jnp.arange(length, dtype=jnp.int32)
    counted = (
        jnp.minimum(position, half_width) + jnp.minimum(length - 1 - position, half_width) + 1
    ).astype(jnp.float32)
    return running.reshape(row_count, length) / counted


def forward_table(first_bin, bin_count, length, transform):
    samples = jnp.arange(length, dtype=jnp.int32)
    bin_index = first_bin + jnp.arange(bin_count, dtype=jnp.int32)
    phase_int = samples[:, None] * bin_index[None, :] % transform
    angles = phase_int.astype(jnp.float32) * (2.0 * math.pi / transform)
    return jnp.concatenate([jnp.cos(angles), -jnp.sin(angles)], axis=1).astype(jnp.bfloat16)


def lag_rows(lag_count, bin_total, transform):
    lag_index = jnp.arange(lag_count, dtype=jnp.int32)
    bin_index = jnp.arange(bin_total, dtype=jnp.int32)
    phase_int = lag_index[:, None] * bin_index[None, :] % transform
    angles = phase_int.astype(jnp.float32) * (2.0 * math.pi / transform)
    weight = jnp.where(bin_index == 0, 1.0, 2.0).astype(jnp.float32)[None, :]
    return jnp.stack([weight * jnp.cos(angles), -weight * jnp.sin(angles)], axis=1).astype(
        jnp.bfloat16
    )


def apply_lags(table, operand):
    return lax.dot_general(
        table, operand, (((1, 2), (0, 3)), ((), ())), preferred_element_type=jnp.float32
    )


def per_device(records, plan):
    stations_dev, windows, length = records.shape
    sta_devices = lax.axis_size("sta")
    seg_devices = lax.axis_size("seg")
    transform = 2 * length
    row_count = stations_dev * windows
    signal = records.reshape(row_count, length)
    mean_level = band_mean(jnp.abs(signal).astype(jnp.bfloat16), HALF)
    flattened = (signal / (mean_level + 1e-05)).astype(jnp.bfloat16)
    part_size = min(NBIN, 256)
    real_parts = []
    imag_parts = []
    for first_bin in range(0, NBIN, part_size):
        fourier = forward_table(first_bin, part_size, length, transform)
        product = jnp.dot(flattened, fourier, preferred_element_type=jnp.float32)
        real_parts.append(product[:, :part_size])
        imag_parts.append(product[:, part_size:])
    spec_real = jnp.concatenate(real_parts, axis=1)
    spec_imag = jnp.concatenate(imag_parts, axis=1)
    magnitude = jnp.sqrt(spec_real * spec_real + spec_imag * spec_imag).astype(jnp.bfloat16)
    smooth = band_mean(magnitude, HALF)
    whitened = jnp.stack(
        [spec_real / (smooth + 1e-06), spec_imag / (smooth + 1e-06)], axis=0
    ).astype(jnp.bfloat16)
    whitened = whitened.reshape(2, stations_dev, windows, NBIN)
    spread = lax.all_to_all(whitened, "sta", split_axis=3, concat_axis=3, tiled=True)
    bin_count = NBIN // sta_devices
    square = stations_dev * stations_dev
    own_real = spread[0].astype(jnp.float32)[:, None]
    own_imag = spread[1].astype(jnp.float32)[:, None]
    viewed = spread.reshape(2, stations_dev, windows, sta_devices, bin_count)

    def round_cross(partners):
        partner = jnp.take(viewed, partners, axis=3).reshape(2, stations_dev, windows, NBIN)
        other_real = partner[0].astype(jnp.float32)[None]
        other_imag = partner[1].astype(jnp.float32)[None]
        real_cross = jnp.sum(own_real * other_real + own_imag * other_imag, axis=2)
        imag_cross = jnp.sum(own_imag * other_real - own_real * other_imag, axis=2)
        crossed = jnp.stack([real_cross, imag_cross], axis=0).astype(jnp.bfloat16)
        return crossed.reshape(2, square, NBIN)

    stacked = jnp.stack([round_cross(plan[number]) for number in range(ROUNDS)], axis=1)
    operand = lax.all_to_all(
        stacked.reshape(2 * ROUNDS * square, NBIN), "sta", split_axis=1, concat_axis=1, tiled=True
    )
    operand = operand.reshape(2, ROUNDS, square, NBIN)
    scaling = 1.0 / math.sqrt(4.0 * NBIN * windows * seg_devices)
    lag_share = LAGS // seg_devices
    table = lag_rows(lax.axis_size("seg") * lag_share, NBIN, 2 * WLEN)
    result = lax.psum_scatter(apply_lags(table, operand), "seg", scatter_dimension=0, tiled=True)
    return result * scaling


def solution(mesh):
    in_specs = (P("sta", "seg", None), P())
    out_specs = P("seg", None, "sta")
    return jax.shard_map(
        per_device, mesh=mesh, in_specs=in_specs, out_specs=out_specs, check_vma=False
    )
```

profile of v0, /device:TPU:0, one launch (start us, length us, event | category | flops | bytes accessed | tf_op | source)
XLA Modules:
  0.0 307.9 jit_solution(11850426183788729463)
XLA Ops:
  6.6 1.2 abs.21
  8.1 1.2 reshape.617
  10.8 8.6 %cosine_convert_fusion = (bf16[2048,256]{1,0:T(8,128)(2,1)S(1)}, bf16[2048,256]{1,0:T(8,128)(2,1)S(1)}) fusion(s32[256]{0:T(256)S(1)} %iota_add_fusion), kind=kLoop, calls=%fused_computation.71 | loop fusion | flops 8912896 | bytes 2098176 | tf_op jit(solution)/shard_map/convert.28
  20.2 8.6 %cosine_convert_fusion.1 = (bf16[2048,256]{1,0:T(8,128)(2,1)S(1)}, bf16[2048,256]{1,0:T(8,128)(2,1)S(1)}) fusion(s32[256]{0:T(256)S(1)} %iota_add_fusion.1), kind=kLoop, calls=%fused_computation.75 | loop fusion | flops 8912896 | bytes 2098176 | tf_op jit(solution)/shard_map/convert.30
  28.8 8.6 %cosine_convert_fusion.2 = (bf16[2048,256]{1,0:T(8,128)(2,1)S(1)}, bf16[2048,256]{1,0:T(8,128)(2,1)S(1)}) fusion(s32[256]{0:T(256)S(1)} %iota_add_fusion.2), kind=kLoop, calls=%fused_computation.79 | loop fusion | flops 8912896 | bytes 2098176 | tf_op jit(solution)/shard_map/convert.32
  38.7 8.5 %negate_convert_fusion.3 = (bf16[2048,256]{1,0:T(8,128)(2,1)S(1)}, bf16[2048,256]{1,0:T(8,128)(2,1)S(1)}) fusion(), kind=kLoop, calls=%fused_computation.82 | loop fusion | flops 8912896 | bytes 2097152 | tf_op jit(solution)/shard_map/convert.35
  49.7 1.4 copy.176
  51.0 2.8 reshape.682
  53.9 7.3 %all-to-all-start = ((bf16[8,2,8192]{2,1,0:T(2,128)(2,1)}), bf16[8,2,8192]{2,1,0:T(2,128)(2,1)S(1)}, u32[]{:S(2)}, u32[]{:S(2)}) async-start(bf16[8,2,8192]{2,1,0:T(2,128)(2,1)} %reshape.682), calls=%async_computation | async-start | bytes 524288 | tf_op jit(solution)/shard_map/all_to_all | solution.py:93
  61.2 8.9 %all-to-all-done = bf16[8,2,8192]{2,1,0:T(2,128)(2,1)S(1)} async-done(((bf16[8,2,8192]{2,1,0:T(2,128)(2,1)}), bf16[8,2,8192]{2,1,0:T(2,128)(2,1)S(1)}, u32[]{:S(2)}, u32[]{:S(2)}) %all-to-all-start) | async-done | bytes 262176 | tf_op jit(solution)/shard_map/all_to_all | solution.py:93
  70.1 1.4 reshape.683
  71.5 2.6 fusion.56
  74.0 1.8 copy.179
  79.2 0.7 reshape.627
  80.1 0.8 reshape.629
  81.2 0.8 reshape.632
  82.1 0.7 reshape.633
  83.2 0.7 reshape.634
  84.8 1.9 copy.177
  86.7 0.8 copy.181
  87.5 9.4 %add_reduce_fusion.3 = (bf16[16,16,1024]{2,1,0:T(8,128)(2,1)S(1)}, bf16[16,16,1024]{2,1,0:T(8,128)(2,1)S(1)}, bf16[16,16,1024]{2,1,0:T(8,128)(2,1)S(1)}, bf16[16...) fusion(f32[16,4,1024]{2,0,1:T(8,128)} %reshape.629, ...), kind=kLoop, calls=%fused_computation.29 | loop fusion | flops 31457280 | bytes 6815744 | tf_op jit(solution)/shard_map/reduce_sum | solution.py:104
  97.4 1.1 copy.204
  98.5 2.6 copy.192
  101.2 4.5 %all-to-all-start.1 = ((bf16[2048,8,128]{2,0,1:T(8,128)(2,1)}), bf16[2048,8,128]{2,0,1:T(8,128)(2,1)}, u32[]{:S(2)}, u32[]{:S(2)}) async-start(bf16[2048,8,128]{2,0,1:T(8,128)(2,1)} %copy.192), calls=%async_computation.1 | async-start | bytes 8388608 | tf_op jit(solution)/shard_map/all_to_all | solution.py:110
  106.0 35.3 %multiply_convert_fusion = (bf16[2048,1,1024]{2,0,1:T(8,128)(2,1)}, bf16[2048,1,1024]{2,0,1:T(8,128)(2,1)}) fusion(f32[1024]{0:T(1024)S(1)} %fusion.93, f32[1024]{0:T(1024)S(1)} %fusion.92), kind=kLoop, calls=%fused_computation.15 | loop fusion | flops 37748736 | bytes 8396800 | tf_op jit(solution)/shard_map/convert.37
  141.3 56.4 %all-to-all-done.1 = bf16[2048,8,128]{2,0,1:T(8,128)(2,1)} async-done(((bf16[2048,8,128]{2,0,1:T(8,128)(2,1)}), bf16[2048,8,128]{2,0,1:T(8,128)(2,1)}, u32[]{:S(2)}, u32[]{:S(2)}) %all-to-all-start.1) | async-done | bytes 4194336 | tf_op jit(solution)/shard_map/all_to_all | solution.py:110
  197.7 6.2 %copy.193 = bf16[2048,8,128]{2,1,0:T(8,128)(2,1)} copy(bf16[2048,8,128]{2,0,1:T(8,128)(2,1)} %all-to-all-done.1) | data formatting | bytes 8388608 | tf_op jit(solution)/shard_map/all_to_all | solution.py:110
  203.9 7.3 %reshape.625 = bf16[2,4,256,1024]{3,2,1,0:T(8,128)(2,1)} reshape(bf16[2048,8,128]{2,1,0:T(8,128)(2,1)} %copy.193) | data formatting | bytes 8388608 | tf_op jit(solution)/shard_map/reshape | solution.py:113
  211.2 14.5 %fusion.11 = f32[2048,4,256]{2,0,1:T(8,128)} fusion(bf16[2,4,256,1024]{3,2,1,0:T(8,128)(2,1)} %reshape.625, bf16[2048,1,1024]{2,0,1:T(8,128)(2,1)} %get-tuple-element.72, bf16[2048,1,1024]{2,0,1:T(8,128)(2,1)} %get-tuple-element.73), kind=kOutput, calls=%fused_computation.20 | convolution fusion | flops 8606711808 | bytes 20971520 | tf_op jit(solution)/shard_map/dot_general | solution.py:63
  225.7 70.9 %reduce-scatter.2.cloned.1.call-done = f32[512,4,256]{2,0,1:T(8,128)} async-done(((f32[2048,4,256]{2,0,1:T(8,128)}), f32[512,4,256]{2,0,1:T(8,128)}) %reduce-scatter.2.cloned.1.call-update) | async-done | bytes 2097168 | tf_op jit(solution)/shard_map/reduce_scatter | solution.py:117
  296.6 1.8 broadcast_multiply_fusion
  298.4 2.7 copy.195
  (95 shorter events, 11.8 us)
Async XLA Ops:
  48.9 12.3 %copy-start.2 = (s32[4,8]{1,0:T(4,128)S(1)}, s32[4,8]{1,0:T(4,128)}, u32[]{:S(2)}) copy-start(s32[4,8]{1,0:T(4,128)} %param.5) | copy-start | bytes 388
  53.9 16.2 %all-to-all-start = ((bf16[8,2,8192]{2,1,0:T(2,128)(2,1)}), bf16[8,2,8192]{2,1,0:T(2,128)(2,1)S(1)}, u32[]{:S(2)}, u32[]{:S(2)}) async-start(bf16[8,2,8192]{2,1,0:T(2,128)(2,1)} %reshape.682), calls=%async_computation | async-start | bytes 524288 | tf_op jit(solution)/shard_map/all_to_all | solution.py:93
  81.0 5.7 %copy-start = (f32[16,4,1024]{0,1,2:T(4,128)S(1)}, f32[16,4,1024]{0,1,2:T(4,128)}, u32[]{:S(2)}) copy-start(f32[16,4,1024]{0,1,2:T(4,128)} %get-tuple-element.29) | copy-start | bytes 786436
  82.9 4.6 %copy-start.1 = (f32[16,4,1024]{2,0,1:T(8,128)S(1)}, f32[16,4,1024]{2,0,1:T(8,128)}, u32[]{:S(2)}) copy-start(f32[16,4,1024]{2,0,1:T(8,128)} %reshape.627) | copy-start | bytes 786436
  101.2 96.5 %all-to-all-start.1 = ((bf16[2048,8,128]{2,0,1:T(8,128)(2,1)}), bf16[2048,8,128]{2,0,1:T(8,128)(2,1)}, u32[]{:S(2)}, u32[]{:S(2)}) async-start(bf16[2048,8,128]{2,0,1:T(8,128)(2,1)} %copy.192), calls=%async_computation.1 | async-start | bytes 8388608 | tf_op jit(solution)/shard_map/all_to_all | solution.py:110
  105.7 190.9 %reduce-scatter.2.cloned.1.call-start = ((), (), s32[]{:S(2)}) async-start(), calls=%async_computation.3 | async-start | bytes 10485760 | tf_op jit(solution)/shard_map/reduce_scatter | solution.py:117
Sparse Core Ops, SparseCore 0:
  225.8 70.7 reduce-scatter.1
where the time goes:
time: 309 us; the launch traced here: 308 us
  waiting for transfers between devices  136 us (44%)
  other arithmetic  86.5 us (28%)
  local copies, waits for them, and re-layouts  41.2 us (13%)
  matrix products  17.9 us (6%)
  between operations  14.1 us (5%)
  starting transfers between devices  12.1 us (4%)
    reduce_scatter x1, waiting for transfers between devices, per_device(): lax.psum_scatter(apply_lags(table, operand), 'seg', scatter_dimension=0,...  70.9 us
    another operation x6, other arithmetic  69.9 us
    all_to_all x1, waiting for transfers between devices, per_device(): lax.all_to_all(stacked.reshape(2 * ROUNDS * square, NBIN), 'sta', split_a...  56.4 us
    dot_general x1, matrix products, apply_lags(): lax.dot_general(table, operand, (((1, 2), (0, 3)), ((), ())), preferred_e...  14.5 us
    reduce_sum x1, other arithmetic, round_cross(): real_cross = jnp.sum(own_real * other_real + own_imag * other_imag, axis=2)  9.37 us
    all_to_all x1, waiting for transfers between devices, per_device(): lax.all_to_all(whitened, 'sta', split_axis=3, concat_axis=3, tiled=True)  8.87 us
    all_to_all x2, local copies, waits for them, and re-layouts, per_device(): lax.all_to_all(stacked.reshape(2 * ROUNDS * square, NBIN), 'sta', split_a...  8.85 us
    reshape x1, local copies, waits for them, and re-layouts, per_device(): operand = operand.reshape(2, ROUNDS, square, NBIN)  7.28 us
  transfers between devices with their start and end apart: 3, of which 3 were waited for; matrix products, arithmetic and copies ran while one was open for 11% of the time, Pallas kernels for 0%

commit v1 on v0

v1 whole, which is shorter than its diff:
```python
import functools
import math

import jax
import jax.numpy as jnp
import ml_dtypes
import numpy as np
from jax import lax
from jax.experimental import pallas as pl
from jax.experimental.pallas import tpu as pltpu
from jax.sharding import PartitionSpec as P

NBIN = 1024
HALF = 64
ROUNDS = 4
LAGS = 2048
LANES = 128
TILES = NBIN // LANES
BF = jnp.bfloat16
F32 = jnp.float32


def make_table(rows, transform):
    phase = (np.arange(rows)[:, None] * np.arange(NBIN)[None, :]) % transform
    angle = phase * (2.0 * math.pi / transform)
    return np.concatenate([np.cos(angle), -np.sin(angle)], axis=1).astype(ml_dtypes.bfloat16)


def make_band():
    source = np.arange(3 * LANES)[:, None] - LANES
    target = np.arange(LANES)[None, :]
    return (np.abs(source - target) <= HALF).astype(ml_dtypes.bfloat16)


def make_counts(length):
    position = np.arange(length)
    counted = np.minimum(position, HALF) + np.minimum(length - 1 - position, HALF) + 1
    return (1.0 / counted).astype(np.float32)[None, :]


def make_placing(stations, quarter, parts):
    width = stations * quarter
    place = np.zeros((parts, 2 * width, 2 * stations * stations), np.float32)
    for part in range(parts):
        for second in range(2):
            for s in range(stations):
                for t in range(quarter):
                    row = second * width + s * quarter + t
                    column = (second * stations + s) * stations + part * quarter + t
                    place[part, row, column] = 1.0
    return place.astype(ml_dtypes.bfloat16)


def lane_cycle(values):
    phase = lax.broadcasted_iota(jnp.int32, (1, LANES), 1) % 4
    out = jnp.full((1, LANES), values[3], F32)
    for index in range(3):
        out = jnp.where(phase == index, values[index], out)
    return out


def even_lanes(shape):
    return lax.broadcasted_iota(jnp.int32, shape, 1) % 2 == 0


def banded_sum(stack, values, band):
    rows, length = values.shape
    blocks = length // LANES
    zero = jnp.zeros((rows, LANES), BF)
    for j in range(blocks):
        at = pl.ds(j * rows, rows)
        for k in range(3):
            b = j + k - 1
            block = values[:, b * LANES : (b + 1) * LANES] if 0 <= b < blocks else zero
            stack[at, k * LANES : (k + 1) * LANES] = block
    total = jnp.dot(stack[: blocks * rows, :], band, preferred_element_type=F32)
    return [total[j * rows : (j + 1) * rows, :] for j in range(blocks)]


def prep_kernel(
    quarter, records, table_hbm, band, count_t, count_f, white, *rest
):
    parts = len(rest) - 6
    quarters = rest[:parts]
    table, stack, flat, spread, sem, _ = rest[parts:]
    copy = pltpu.make_async_copy(table_hbm, table, sem)
    copy.start()
    stations, windows, length = records.shape
    rows = stations * windows
    half = length // 2
    signal = jnp.concatenate([records[:, w, :] for w in range(windows)], axis=0)
    band_values = band[...]
    sums = banded_sum(stack, jnp.abs(signal).astype(BF), band_values)
    for j, total in enumerate(sums):
        at = slice(j * LANES, (j + 1) * LANES)
        level = total * count_t[:, at]
        value = (signal[:, at] / (level + 1e-05)).astype(BF)
        if j * LANES < half:
            flat[:rows, at] = value
        else:
            flat[rows:, j * LANES - half : (j + 1) * LANES - half] = value
    copy.wait()
    product = jnp.dot(flat[...], table[...], preferred_element_type=F32)
    even = even_lanes((rows, LANES))
    sign_real = lane_cycle([1.0, 1.0, -1.0, -1.0])
    sign_imag = lane_cycle([1.0, -1.0, -1.0, 1.0])
    reals, imags, mags = [], [], []
    for j in range(TILES):
        at = slice(j * LANES, (j + 1) * LANES)
        at_imag = slice(NBIN + j * LANES, NBIN + (j + 1) * LANES)
        later_real, later_imag = product[rows:, at], product[rows:, at_imag]
        real = product[:rows, at] + sign_real * jnp.where(even, later_real, later_imag)
        imag = product[:rows, at_imag] + sign_imag * jnp.where(even, later_imag, later_real)
        reals.append(real)
        imags.append(imag)
        mags.append(jnp.sqrt(real * real + imag * imag).astype(BF))
    sums = banded_sum(stack, jnp.concatenate(mags, axis=1), band_values)
    for j, total in enumerate(sums):
        at = slice(j * LANES, (j + 1) * LANES)
        smooth = total * count_f[:, at] + 1e-06
        spread[pl.ds(j, rows, stride=2 * TILES), :] = reals[j] / smooth
        spread[pl.ds(TILES + j, rows, stride=2 * TILES), :] = imags[j] / smooth
    me = lax.axis_index("seg")
    out = spread[...].reshape(windows, stations, 2 * TILES, LANES).astype(BF)
    white[...] = out
    for j in range(parts):
        first = (me ^ j) * quarter
        for w in range(windows):
            quarters[j][w] = white[w, pl.ds(first, quarter)]


def prepare(records, table, parts):
    stations, windows, length = records.shape
    rows = stations * windows
    quarter = stations // parts
    band = make_band()
    small = jax.ShapeDtypeStruct((windows, quarter, 2 * TILES, LANES), BF)
    vmem = pl.BlockSpec(memory_space=pltpu.VMEM)
    return pl.pallas_call(
        functools.partial(prep_kernel, quarter),
        out_shape=[jax.ShapeDtypeStruct((windows, stations, 2 * TILES, LANES), BF)]
        + [small] * parts,
        in_specs=[vmem, pl.BlockSpec(memory_space=pl.ANY), vmem, vmem, vmem],
        out_specs=[vmem] * (parts + 1),
        scratch_shapes=[
            pltpu.VMEM(table.shape, BF),
            pltpu.VMEM((rows * (length // LANES), 3 * LANES), BF),
            pltpu.VMEM((2 * rows, length // 2), BF),
            pltpu.VMEM((rows * 2 * TILES, LANES), F32),
            pltpu.SemaphoreType.DMA,
            pltpu.SMEM((1,), jnp.int32),
        ],
        compiler_params=pltpu.CompilerParams(vmem_limit_bytes=40 * 2**20),
        cost_estimate=pl.CostEstimate(
            flops=2 * 2 * rows * (length // 2) * 2 * NBIN, bytes_accessed=6 * 2**20, transcendentals=0
        ),
        name="prep",
    )(records, table, band, make_counts(length), make_counts(NBIN))


def ring_place(block, count):
    return jnp.where(block % 2 == 0, block // 2, count - 1 - block // 2)


def partner_steps(plan, count):
    me = lax.axis_index("sta")
    mine = ring_place(me, count)
    steps, keys = [], []
    for number in range(ROUNDS):
        step = (ring_place(plan[number, me], count) - mine + count) % count
        steps.append(step)
        keys.append(jnp.minimum(step, count - step) * ROUNDS + number)
    ranks = []
    for number in range(ROUNDS):
        rank = jnp.int32(0)
        for other in range(ROUNDS):
            if other != number:
                rank = rank + jnp.where(keys[other] < keys[number], 1, 0)
        ranks.append(rank)
    return steps, ranks


def cross_kernel(first_slot, slots, count, scaling, offsets, parts, plan, table_hbm, *rest):
    owns = rest[:parts]
    candidates = rest[parts : parts + len(offsets)]
    rest = rest[parts + len(offsets) :]
    outs = rest[:parts]
    table, own_raw, other_raw, own, other, crossed, operand, result, sems = rest[parts:]
    windows, stations = owns[0].shape[:2]
    all_windows = windows * parts
    quarter = other_raw.shape[2]
    width = stations * quarter
    columns = slots * width

    table_copy = pltpu.make_async_copy(table_hbm, table, sems.at[0])
    steps, ranks = partner_steps(plan, count)
    own_copies = [
        pltpu.make_async_copy(owns[j], own_raw.at[pl.ds(j * windows, windows)], sems.at[1 + j])
        for j in range(parts)
    ]
    for copy in own_copies:
        copy.start()
    for slot in range(slots):
        step = jnp.int32(0)
        for number in range(ROUNDS):
            step = jnp.where(ranks[number] == first_slot + slot, steps[number], step)
        for (offset, start), candidate in zip(offsets, candidates):
            size = candidate.shape[0]

            @pl.when(step == offset)
            def _(candidate=candidate, slot=slot, start=start, size=size):
                pltpu.make_async_copy(
                    candidate, other_raw.at[slot, pl.ds(start, size)], sems.at[1 + parts + slot]
                ).start()

    table_copy.start()
    for copy in own_copies:
        copy.wait()

    def widen_own(w, carry):
        raw = own_raw[w].astype(F32)
        real, imag = raw[:, :TILES], raw[:, TILES:]
        own[0, w] = real + imag
        own[1, w] = real
        own[2, w] = imag
        return carry

    lax.fori_loop(0, all_windows, widen_own, 0)
    for slot in range(slots):
        pltpu.make_async_copy(
            other_raw.at[slot], other_raw.at[slot], sems.at[1 + parts + slot]
        ).wait()

        def widen_other(w, carry, slot=slot):
            raw = other_raw[slot, w].astype(F32)
            real, imag = raw[:, :TILES], raw[:, TILES:]
            other[0, slot, w] = real
            other[1, slot, w] = real + imag
            other[2, slot, w] = imag - real
            return carry

        lax.fori_loop(0, all_windows, widen_other, 0)

    group = 4
    groups = stations // group
    first_bin = (lax.broadcasted_iota(jnp.int32, (TILES, LANES), 0) == 0) & (
        lax.broadcasted_iota(jnp.int32, (TILES, LANES), 1) == 0
    )
    weight = jnp.where(first_bin, 1.0, 2.0).astype(F32)

    def one_group(index, carry):
        slot = index // groups
        first = (index % groups) * group

        def sums(kind):
            totals = [None] * (group * quarter)
            for w in range(all_windows):
                left = [own[kind, w, first + s] for s in range(group)]
                right = [other[kind, slot, w, t] for t in range(quarter)]
                for s in range(group):
                    for t in range(quarter):
                        term = left[s] * right[t]
                        place = s * quarter + t
                        totals[place] = term if w == 0 else totals[place] + term
            return totals

        base = slot * width + first * quarter
        shared = sums(0)
        third = sums(2)
        for place in range(group * quarter):
            at = pl.multiple_of((base + place) * 2 * TILES, 2 * TILES)
            crossed[pl.ds(at, TILES), :] = (shared[place] + third[place]) * weight
        second = sums(1)
        for place in range(group * quarter):
            at = pl.multiple_of((base + place) * 2 * TILES + TILES, TILES)
            crossed[pl.ds(at, TILES), :] = (shared[place] - second[place]) * weight
        return carry

    lax.fori_loop(0, slots * groups, one_group, 0)

    even = even_lanes((columns, LANES))
    sign_real = lane_cycle([1.0, -1.0, -1.0, 1.0])
    sign_imag = lane_cycle([1.0, 1.0, -1.0, -1.0])
    for j in range(TILES):
        at = slice(j * LANES, (j + 1) * LANES)
        at_imag = slice(NBIN + j * LANES, NBIN + (j + 1) * LANES)
        real = crossed[pl.ds(j, columns, stride=2 * TILES), :]
        imag = crossed[pl.ds(TILES + j, columns, stride=2 * TILES), :]
        operand[:columns, at] = real.astype(BF)
        operand[:columns, at_imag] = imag.astype(BF)
        operand[columns:, at] = (sign_real * jnp.where(even, real, imag)).astype(BF)
        operand[columns:, at_imag] = (sign_imag * jnp.where(even, imag, real)).astype(BF)
    table_copy.wait()
    share = outs[0].shape[0]
    per_half = table.shape[0] // share
    for q in range(per_half):
        block = lax.dot_general(
            table[q * share : (q + 1) * share, :],
            operand[...],
            (((1,), (1,)), ((), ())),
            preferred_element_type=F32,
        )
        block = (block * scaling).astype(BF)
        for h in range(2):
            result[h * per_half + q] = block[:, h * columns : (h + 1) * columns]
    me = lax.axis_index("seg")
    for j in range(parts):
        outs[j][...] = result[me ^ j]


def cross_lags(plan, table, owns, offsets, candidates, first_slot, slots, count, scaling):
    parts = len(owns)
    windows, stations = owns[0].shape[:2]
    all_windows = windows * parts
    quarter = candidates[0].shape[1]
    columns = slots * stations * quarter
    share = LAGS // parts
    smem = pl.BlockSpec(memory_space=pltpu.SMEM)
    any_space = pl.BlockSpec(memory_space=pl.ANY)
    vmem = pl.BlockSpec(memory_space=pltpu.VMEM)
    return pl.pallas_call(
        functools.partial(
            cross_kernel, first_slot, slots, count, scaling, tuple(offsets), parts
        ),
        out_shape=[jax.ShapeDtypeStruct((share, columns), BF)] * parts,
        in_specs=[smem] + [any_space] * (1 + parts + len(candidates)),
        out_specs=[vmem] * parts,
        scratch_shapes=[
            pltpu.VMEM(table.shape, BF),
            pltpu.VMEM((all_windows, stations, 2 * TILES, LANES), BF),
            pltpu.VMEM((slots, all_windows, quarter, 2 * TILES, LANES), BF),
            pltpu.VMEM((3, all_windows, stations, TILES, LANES), F32),
            pltpu.VMEM((3, slots, all_windows, quarter, TILES, LANES), F32),
            pltpu.VMEM((columns * 2 * TILES, LANES), F32),
            pltpu.VMEM((2 * columns, 2 * NBIN), BF),
            pltpu.VMEM((parts, share, columns), BF),
            pltpu.SemaphoreType.DMA((1 + parts + slots,)),
        ],
        compiler_params=pltpu.CompilerParams(vmem_limit_bytes=40 * 2**20),
        cost_estimate=pl.CostEstimate(
            flops=2 * LAGS * 2 * NBIN * columns * 2, bytes_accessed=8 * 2**20, transcendentals=0
        ),
        name="cross",
    )(plan, table, *owns, *candidates)


def place_kernel(count, groups, parts, plan, place, *rest):
    pieces = rest[: groups * parts]
    out, result = rest[groups * parts :]
    share, rounds, pairs = out.shape
    me = lax.axis_index("seg")
    _, ranks = partner_steps(plan, count)
    matrix = jnp.concatenate([place[me ^ j] for j in range(parts)], axis=0)
    for p in range(groups):
        joined = jnp.concatenate([pieces[p * parts + j][...] for j in range(parts)], axis=1)
        block = jnp.dot(joined, matrix, preferred_element_type=F32)
        result[2 * p] = block[:, :pairs]
        result[2 * p + 1] = block[:, pairs:]
    for number in range(rounds):
        out[:, number, :] = result[ranks[number]]


def place_lags(plan, pieces, parts, count, stations):
    groups = len(pieces) // parts
    share = pieces[0].shape[0]
    pairs = stations * stations
    vmem = pl.BlockSpec(memory_space=pltpu.VMEM)
    return pl.pallas_call(
        functools.partial(place_kernel, count, groups, parts),
        out_shape=jax.ShapeDtypeStruct((share, ROUNDS, pairs), F32),
        in_specs=[pl.BlockSpec(memory_space=pltpu.SMEM)] + [vmem] * (1 + len(pieces)),
        out_specs=vmem,
        scratch_shapes=[pltpu.VMEM((ROUNDS, share, pairs), F32)],
        compiler_params=pltpu.CompilerParams(vmem_limit_bytes=40 * 2**20),
        cost_estimate=pl.CostEstimate(
            flops=2 * share * 4 * pairs * ROUNDS * pairs, bytes_accessed=4 * 2**20, transcendentals=0
        ),
        name="place",
    )(plan, make_placing(stations, stations // parts, parts), *pieces)


def exchange(pieces):
    parts = len(pieces)
    out = [pieces[0]]
    for j in range(1, parts):
        out.append(lax.ppermute(pieces[j], "seg", [(i, i ^ j) for i in range(parts)]))
    return out


def per_device(records, plan):
    stations, windows, length = records.shape
    count = lax.axis_size("sta")
    parts = lax.axis_size("seg")
    table = jnp.asarray(make_table(length // 2, 2 * length))
    scaling = 1.0 / math.sqrt(4.0 * NBIN * windows * parts)

    white, *quarters = prepare(records, table, parts)
    shared = jnp.concatenate(exchange(quarters), axis=0)
    owns = exchange([white] * parts)

    ring = sorted(range(count), key=lambda b: b // 2 if b % 2 == 0 else count - 1 - b // 2)
    forward = [(ring[i], ring[(i + 1) % count]) for i in range(count)]
    backward = [(ring[i], ring[i - 1]) for i in range(count)]
    offsets, candidates = [], []
    from_left = from_right = shared
    for step in range(1, (count - 1) // 2 + 1):
        from_left = lax.ppermute(from_left, "sta", forward)
        from_right = lax.ppermute(from_right, "sta", backward)
        offsets += [(count - step, 0), (step, 0)]
        candidates += [from_left, from_right]
    early = (list(offsets), list(candidates))
    if count % 2 == 0:
        middle = shared.shape[0] // 2
        offsets += [(count // 2, 0), (count // 2, middle)]
        candidates += [
            lax.ppermute(from_left[:middle], "sta", forward),
            lax.ppermute(from_right[middle:], "sta", backward),
        ]
    pieces = []
    for first_slot, (spots, blocks) in ((0, early), (2, (offsets, candidates))):
        lags = cross_lags(plan, table, owns, spots, blocks, first_slot, 2, count, scaling)
        pieces += exchange(lags)
    return place_lags(plan, pieces, parts, count, stations)


def solution(mesh):
    in_specs = (P("sta", "seg", None), P())
    out_specs = P("seg", None, "sta")
    return jax.shard_map(
        per_device, mesh=mesh, in_specs=in_specs, out_specs=out_specs, check_vma=False
    )
```

time: 309 us -> 71.8 us (0.23)
  waiting for transfers between devices: 136 us -> 31.5 us
  other arithmetic: 86.5 us -> 0 us
  local copies, waits for them, and re-layouts: 41.2 us -> 5.58 us
  matrix products: 17.9 us -> 0 us
  Pallas kernels: 0 us -> 16.4 us
  between operations: 14.1 us -> 0.1 us
  starting transfers between devices: 12.1 us -> 17.5 us
    reduce_scatter x1 -> x0, waiting for transfers between devices: 70.9 us -> none  [per_device(): lax.psum_scatter(apply_lags(table, operand), 'seg', scatter_dimension=0,...]
    another operation x8 -> x0, other arithmetic: 70.5 us -> none
    all_to_all x2 -> x0, waiting for transfers between devices: 65.3 us -> none  [the longest x1 56.4 us: per_device(): lax.all_to_all(stacked.reshape(2 * ROUNDS * square, NBIN), 'sta', split_a...]
    ppermute x0 -> x20, waiting for transfers between devices: none -> 31.5 us  [the longest x12 16.9 us: exchange(): lax.ppermute(pieces[j], 'seg', [(i, i ^ j) for i in range(parts)])]
    dot_general x11 -> x0, matrix products: 17.9 us -> none  [the longest x1 14.5 us: apply_lags(): lax.dot_general(table, operand, (((1, 2), (0, 3)), ((), ())), preferred_e...]
    ppermute x0 -> x20, starting transfers between devices: none -> 17.5 us  [the longest x12 9.22 us: exchange(): lax.ppermute(pieces[j], 'seg', [(i, i ^ j) for i in range(parts)])]
    pallas_call x0 -> x4, Pallas kernels: none -> 16.4 us  [the longest x2 11.2 us: cross_lags(): pl.pallas_call(functools.partial(cross_kernel, first_slot, slots, count,...]
    all_to_all x2 -> x0, starting transfers between devices: 11.8 us -> none  [the longest x1 7.27 us: per_device(): lax.all_to_all(whitened, 'sta', split_axis=3, concat_axis=3, tiled=True)]
  transfers between devices with their start and end apart: 3 -> 20, of which waited for: 3 -> 9; matrix products, arithmetic and copies ran while one was open for 11% -> 0% of each run, Pallas kernels for 0% -> 16%
where the time goes in v1:
time: 71.8 us; the launch traced here: 71.1 us
  waiting for transfers between devices  31.5 us (44%)
  starting transfers between devices  17.5 us (24%)
  Pallas kernels  16.4 us (23%)
  local copies, waits for them, and re-layouts  5.58 us (8%)
    ppermute x12, waiting for transfers between devices, exchange(): lax.ppermute(pieces[j], 'seg', [(i, i ^ j) for i in range(parts)])  16.9 us
    ppermute x3, waiting for transfers between devices, per_device(): from_left = lax.ppermute(from_left, 'sta', forward)  14.6 us
    pallas_call x2, Pallas kernels, cross_lags(): pl.pallas_call(functools.partial(cross_kernel, first_slot, slots, count,...  11.2 us
    ppermute x12, starting transfers between devices, exchange(): lax.ppermute(pieces[j], 'seg', [(i, i ^ j) for i in range(parts)])  9.22 us
    unnamed x19, local copies, waits for them, and re-layouts  5.55 us
    ppermute x3, starting transfers between devices, per_device(): from_left = lax.ppermute(from_left, 'sta', forward)  4.75 us
    pallas_call x1, Pallas kernels, place_lags(): pl.pallas_call(functools.partial(place_kernel, count, groups, parts), out...  3.22 us
    pallas_call x1, Pallas kernels, prepare(): pl.pallas_call(functools.partial(prep_kernel, quarter), out_shape=[jax.Sh...  2.01 us
  transfers between devices with their start and end apart: 20, of which 9 were waited for; matrix products, arithmetic and copies ran while one was open for 0% of the time, Pallas kernels for 16%

profile of v1, /device:TPU:0, one launch (start us, length us, event | category | flops | bytes accessed | tf_op | source)
XLA Modules:
  0.0 71.1 jit_solution(16896028225000417938)
XLA Ops:
  0.0 2.2 %copy-done = bf16[1024,2048]{1,0:T(8,128)(2,1)S(1)} copy-done((bf16[1024,2048]{1,0:T(8,128)(2,1)S(1)}, bf16[1024,2048]{1,0:T(8,128)(2,1)}, u32[]{:S(2)}) %copy-start) | copy-done | bytes 4194328
  2.2 1.0 %copy-done.2 = f32[16,4,2048]{2,1,0:T(4,128)S(1)} copy-done((f32[16,4,2048]{2,1,0:T(4,128)S(1)}, f32[16,4,2048]{2,1,0:T(4,128)}, u32[]{:S(2)}) %copy-start.2) | copy-done | bytes 524312
  3.2 0.9 %copy-done.3 = bf16[384,128]{1,0:T(8,128)(2,1)S(1)} copy-done((bf16[384,128]{1,0:T(8,128)(2,1)S(1)}, bf16[384,128]{1,0:T(8,128)(2,1)}, u32[]{:S(2)}) %copy-start.3) | copy-done | bytes 98328
  4.1 0.7 copy-done.4
  4.8 0.7 copy-done.5
  5.5 2.0 %prep.1 = (bf16[4,16,16,128]{3,2,1,0:T(8,128)(2,1)S(1)}, bf16[4,4,16,128]{3,2,1,0:T(8,128)(2,1)S(1)}, bf16[4,4,16,128]{3,2,1,0:T(8,128)(2,1)S(1)}, bf16[4,4,16,1...) custom-call(f32[16,4,2048]{2,1,0:T(4,128)S(1)} %copy-done.2, bf16[1024,2048]{1,0:T(8,128)(2,1)S(1)} %copy-done, ...), custom_call_target="tpu_custom_call" | custom-call | flops 536870912 | bytes 6291456 | tf_op jit(solution)/shard_map/prep/pallas_call | solution.py:139
  7.5 0.5 collective-permute-start.3
  8.1 2.6 %collective-permute-start.4 = (bf16[4,4,16,128]{3,2,1,0:T(8,128)(2,1)S(1)}, bf16[4,4,16,128]{3,2,1,0:T(8,128)(2,1)S(1)}, u32[]{:S(2)}, u32[]{:S(2)}) collective-permute-start(bf16[4,4,16,128]{3,2,1,0:T(8,128)(2,1)S(1)} %get-tuple-element.21), channel_id=1, source_target_pairs={{0,2},{1,3},{2,0},{3,1},{4,6},{5,7},{6,4},{7,5},{8,10},{9,11},{10,... | collective-permute-start | bytes 196616 | tf_op jit(solution)/shard_map/ppermute | solution.py:386
  10.7 2.6 %collective-permute-done.4 = bf16[4,4,16,128]{3,2,1,0:T(8,128)(2,1)S(1)} collective-permute-done((bf16[4,4,16,128]{3,2,1,0:T(8,128)(2,1)S(1)}, bf16[4,4,16,128]{3,2,1,0:T(8,128)(2,1)S(1)}, u32[]{:S(2)}, u32[]{:S(2)}) %collective-permute-start.4) | collective-permute-done | bytes 65568 | tf_op jit(solution)/shard_map/ppermute | solution.py:386
  13.3 1.3 %collective-permute-done.5 = bf16[4,4,16,128]{3,2,1,0:T(8,128)(2,1)S(1)} collective-permute-done((bf16[4,4,16,128]{3,2,1,0:T(8,128)(2,1)S(1)}, bf16[4,4,16,128]{3,2,1,0:T(8,128)(2,1)S(1)}, u32[]{:S(2)}, u32[]{:S(2)}) %collective-permute-start.5) | collective-permute-done | bytes 65568 | tf_op jit(solution)/shard_map/ppermute | solution.py:386
  14.7 1.6 %collective-permute-start.6 = (bf16[16,4,16,128]{3,2,1,0:T(8,128)(2,1)S(1)}, bf16[16,4,16,128]{3,2,1,0:T(8,128)(2,1)S(1)}, u32[]{:S(2)}, u32[]{:S(2)}) collective-permute-start(bf16[16,4,16,128]{3,2,1,0:T(8,128)(2,1)S(1)} %constant_dynamic-update-slice_fusion), channel_id=1, source_target_pairs={{0,8},{8,16},{16,24},{24,28},{28,20},{20,12},{12,4},{4,0},{1,9},{9... | collective-permute-start | bytes 786440 | tf_op jit(solution)/shard_map/ppermute | solution.py:407
  16.3 0.5 collective-permute-start.7
  16.8 6.4 %collective-permute-done.6.rest_4_ = bf16[16,4,16,128]{3,2,1,0:T(8,128)(2,1)S(1)} collective-permute-done((bf16[16,4,16,128]{3,2,1,0:T(8,128)(2,1)S(1)}, bf16[16,4,16,128]{3,2,1,0:T(8,128)(2,1)S(1)}, u32[]{:S(2)}, u32[]{:S(2)}) %collective-permute-start.6) | collective-permute-done | bytes 262176 | tf_op jit(solution)/shard_map/ppermute | solution.py:407
  23.1 1.6 %collective-permute-start.8 = (bf16[16,4,16,128]{3,2,1,0:T(8,128)(2,1)S(1)}, bf16[16,4,16,128]{3,2,1,0:T(8,128)(2,1)S(1)}, u32[]{:S(2)}, u32[]{:S(2)}) collective-permute-start(bf16[16,4,16,128]{3,2,1,0:T(8,128)(2,1)S(1)} %collective-permute-done.6.rest_4_), channel_id=1, source_target_pairs={{0,8},{8,16},{16,24},{24,28},{28,20},{20,12},{12,4},{4,0},{1,9},{9... | collective-permute-start | bytes 786440 | tf_op jit(solution)/shard_map/ppermute | solution.py:407
  24.7 0.5 collective-permute-start.9
  25.2 5.5 %collective-permute-done.8.rest_6_ = bf16[16,4,16,128]{3,2,1,0:T(8,128)(2,1)S(1)} collective-permute-done((bf16[16,4,16,128]{3,2,1,0:T(8,128)(2,1)S(1)}, bf16[16,4,16,128]{3,2,1,0:T(8,128)(2,1)S(1)}, u32[]{:S(2)}, u32[]{:S(2)}) %collective-permute-start.8) | collective-permute-done | bytes 262176 | tf_op jit(solution)/shard_map/ppermute | solution.py:407
  30.7 1.6 %collective-permute-start.10 = (bf16[16,4,16,128]{3,2,1,0:T(8,128)(2,1)S(1)}, bf16[16,4,16,128]{3,2,1,0:T(8,128)(2,1)S(1)}, u32[]{:S(2)}, u32[]{:S(2)}) collective-permute-start(bf16[16,4,16,128]{3,2,1,0:T(8,128)(2,1)S(1)} %collective-permute-done.8.rest_6_), channel_id=1, source_target_pairs={{0,8},{8,16},{16,24},{24,28},{28,20},{20,12},{12,4},{4,0},{1,9},{9... | collective-permute-start | bytes 786440 | tf_op jit(solution)/shard_map/ppermute | solution.py:407
  32.2 0.5 collective-permute-start.11
  32.7 1.6 %collective-permute-start.1 = (bf16[4,16,16,128]{3,2,1,0:T(8,128)(2,1)S(1)}, bf16[4,16,16,128]{3,2,1,0:T(8,128)(2,1)S(1)}, u32[]{:S(2)}, u32[]{:S(2)}) collective-permute-start(bf16[4,16,16,128]{3,2,1,0:T(8,128)(2,1)S(1)} %get-tuple-element.18.rest_0_), channel_id=1, source_target_pairs={{0,2},{1,3},{2,0},{3,1},{4,6},{5,7},{6,4},{7,5},{8,10},{9,11},{10,... | collective-permute-start | bytes 786440 | tf_op jit(solution)/shard_map/ppermute | solution.py:386
  34.6 2.7 %collective-permute-done.10.rest_8_ = bf16[16,4,16,128]{3,2,1,0:T(8,128)(2,1)S(1)} collective-permute-done((bf16[16,4,16,128]{3,2,1,0:T(8,128)(2,1)S(1)}, bf16[16,4,16,128]{3,2,1,0:T(8,128)(2,1)S(1)}, u32[]{:S(2)}, u32[]{:S(2)}) %collective-permute-start.10) | collective-permute-done | bytes 262176 | tf_op jit(solution)/shard_map/ppermute | solution.py:407
  37.3 1.6 %collective-permute-start.15 = (bf16[8,4,16,128]{3,2,1,0:T(8,128)(2,1)S(1)}, bf16[8,4,16,128]{3,2,1,0:T(8,128)(2,1)S(1)}, u32[]{:S(2)}, u32[]{:S(2)}) collective-permute-start(bf16[8,4,16,128]{3,2,1,0:T(8,128)(2,1)S(1)} %slice.8), channel_id=1, source_target_pairs={{0,8},{8,16},{16,24},{24,28},{28,20},{20,12},{12,4},{4,0},{1,9},{9... | collective-permute-start | bytes 393224 | tf_op jit(solution)/shard_map/ppermute | solution.py:416
  38.9 0.5 collective-permute-start.16
  39.5 2.3 %collective-permute-done.1.rest_2_ = bf16[4,16,16,128]{3,2,1,0:T(8,128)(2,1)S(1)} collective-permute-done((bf16[4,16,16,128]{3,2,1,0:T(8,128)(2,1)S(1)}, bf16[4,16,16,128]{3,2,1,0:T(8,128)(2,1)S(1)}, u32[]{:S(2)}, u32[]{:S(2)}) %collective-permute-start.1) | collective-permute-done | bytes 262176 | tf_op jit(solution)/shard_map/ppermute | solution.py:386
  41.8 4.8 %collective-permute-done.2.rest_3_ = bf16[4,16,16,128]{3,2,1,0:T(8,128)(2,1)S(1)} collective-permute-done((bf16[4,16,16,128]{3,2,1,0:T(8,128)(2,1)S(1)}, bf16[4,16,16,128]{3,2,1,0:T(8,128)(2,1)S(1)}, u32[]{:S(2)}, u32[]{:S(2)}) %collective-permute-start.2) | collective-permute-done | bytes 262176 | tf_op jit(solution)/shard_map/ppermute | solution.py:386
  46.7 5.6 %cross.2 = (bf16[512,128]{1,0:T(8,128)(2,1)S(1)}, bf16[512,128]{1,0:T(8,128)(2,1)S(1)}, bf16[512,128]{1,0:T(8,128)(2,1)S(1)}, bf16[512,128]{1,0:T(8,128)(2,1)S(1)}) custom-call(s32[4,8]{1,0:T(4,128)S(1)} %copy-done.6, bf16[1024,2048]{1,0:T(8,128)(2,1)S(1)} %copy-done.1, bf16[4,16,16,128]{3,2,1,0:T(8,128)(2,1)S(1)} %get-tuple-element.18.rest_0_, ...), custom_call_target="tpu_custom_call" | custom-call | flops 2147483648 | bytes 8388608 | tf_op jit(solution)/shard_map/cross/pallas_call | solution.py:321
  52.6 1.6 %collective-permute-start.13 = (bf16[512,128]{1,0:T(8,128)(2,1)S(1)}, bf16[512,128]{1,0:T(8,128)(2,1)S(1)}, u32[]{:S(2)}, u32[]{:S(2)}) collective-permute-start(bf16[512,128]{1,0:T(8,128)(2,1)S(1)} %get-tuple-element.25), channel_id=1, source_target_pairs={{0,2},{1,3},{2,0},{3,1},{4,6},{5,7},{6,4},{7,5},{8,10},{9,11},{10,... | collective-permute-start | bytes 393224 | tf_op jit(solution)/shard_map/ppermute | solution.py:386
  54.2 5.6 %cross.3 = (bf16[512,128]{1,0:T(8,128)(2,1)S(1)}, bf16[512,128]{1,0:T(8,128)(2,1)S(1)}, bf16[512,128]{1,0:T(8,128)(2,1)S(1)}, bf16[512,128]{1,0:T(8,128)(2,1)S(1)}) custom-call(s32[4,8]{1,0:T(4,128)S(1)} %copy-done.6, bf16[1024,2048]{1,0:T(8,128)(2,1)S(1)} %copy-done.1, bf16[4,16,16,128]{3,2,1,0:T(8,128)(2,1)S(1)} %get-tuple-element.18.rest_0_, ...), custom_call_target="tpu_custom_call" | custom-call | flops 2147483648 | bytes 8388608 | tf_op jit(solution)/shard_map/cross/pallas_call | solution.py:321
  59.8 0.6 collective-permute-start.17
  60.4 1.7 %collective-permute-start.18 = (bf16[512,128]{1,0:T(8,128)(2,1)S(1)}, bf16[512,128]{1,0:T(8,128)(2,1)S(1)}, u32[]{:S(2)}, u32[]{:S(2)}) collective-permute-start(bf16[512,128]{1,0:T(8,128)(2,1)S(1)} %get-tuple-element.29), channel_id=1, source_target_pairs={{0,2},{1,3},{2,0},{3,1},{4,6},{5,7},{6,4},{7,5},{8,10},{9,11},{10,... | collective-permute-start | bytes 393224 | tf_op jit(solution)/shard_map/ppermute | solution.py:386
  62.1 4.6 %collective-permute-done.18.rest_6_ = bf16[512,128]{1,0:T(8,128)(2,1)S(1)} collective-permute-done((bf16[512,128]{1,0:T(8,128)(2,1)S(1)}, bf16[512,128]{1,0:T(8,128)(2,1)S(1)}, u32[]{:S(2)}, u32[]{:S(2)}) %collective-permute-start.18) | collective-permute-done | bytes 131104 | tf_op jit(solution)/shard_map/ppermute | solution.py:386
  66.7 1.2 %collective-permute-done.19.rest_7_ = bf16[512,128]{1,0:T(8,128)(2,1)S(1)} collective-permute-done((bf16[512,128]{1,0:T(8,128)(2,1)S(1)}, bf16[512,128]{1,0:T(8,128)(2,1)S(1)}, u32[]{:S(2)}, u32[]{:S(2)}) %collective-permute-start.19) | collective-permute-done | bytes 131104 | tf_op jit(solution)/shard_map/ppermute | solution.py:386
  67.9 3.2 %place.2 = f32[512,4,256]{2,1,0:T(4,128)} custom-call(s32[4,8]{1,0:T(4,128)S(1)} %copy-done.6, bf16[4,128,512]{2,1,0:T(8,128)(2,1)S(1)} %copy-done.7, bf16[512,128]{1,0:T(8,128)(2,1)S(1)} %get-tuple-element.23.rest_0_, bf16[512,128]{1,0:T(8,128)(2,1)S(1)} %collective-permute-done.12.rest_1_, bf16[512,128]{1,0:T(8,128)(2,1)S(1)} %collective-permute-done.13.rest_2_, ...), custom_call_target="tpu_custom_call" | custom-call | flops 1073741824 | bytes 4194304 | tf_op jit(solution)/shard_map/place/pallas_call | solution.py:368
  (34 shorter events, 0.8 us)
Async XLA Ops:
  0.0 2.2 %copy-start = (bf16[1024,2048]{1,0:T(8,128)(2,1)S(1)}, bf16[1024,2048]{1,0:T(8,128)(2,1)}, u32[]{:S(2)}) copy-start(bf16[1024,2048]{1,0:T(8,128)(2,1)} %constant.10.clone.table_hbm) | copy-start | bytes 12582916
  2.2 1.0 %copy-start.2 = (f32[16,4,2048]{2,1,0:T(4,128)S(1)}, f32[16,4,2048]{2,1,0:T(4,128)}, u32[]{:S(2)}) copy-start(f32[16,4,2048]{2,1,0:T(4,128)} %records.1) | copy-start | bytes 1572868
  3.2 0.9 %copy-start.3 = (bf16[384,128]{1,0:T(8,128)(2,1)S(1)}, bf16[384,128]{1,0:T(8,128)(2,1)}, u32[]{:S(2)}) copy-start(bf16[384,128]{1,0:T(8,128)(2,1)} %constant.11.clone.band) | copy-start | bytes 294916
  4.1 0.7 copy-start.4
  4.8 0.7 copy-start.5
  5.5 41.1 %copy-start.1 = (bf16[1024,2048]{1,0:T(8,128)(2,1)S(1)}, bf16[1024,2048]{1,0:T(8,128)(2,1)}, u32[]{:S(2)}) copy-start(bf16[1024,2048]{1,0:T(8,128)(2,1)} %constant.10.clone.table_hbm) | copy-start | bytes 12582916
  5.5 41.1 %copy-start.6 = (s32[4,8]{1,0:T(4,128)S(1)}, s32[4,8]{1,0:T(4,128)}, u32[]{:S(2)}) copy-start(s32[4,8]{1,0:T(4,128)} %plan.5) | copy-start | bytes 388
  7.5 3.2 %collective-permute-start.3 = (bf16[4,4,16,128]{3,2,1,0:T(8,128)(2,1)S(1)}, bf16[4,4,16,128]{3,2,1,0:T(8,128)(2,1)S(1)}, u32[]{:S(2)}, u32[]{:S(2)}) collective-permute-start(bf16[4,4,16,128]{3,2,1,0:T(8,128)(2,1)S(1)} %get-tuple-element.20), channel_id=1, source_target_pairs={{0,1},{1,0},{2,3},{3,2},{4,5},{5,4},{6,7},{7,6},{8,9},{9,8},{10,11... | collective-permute-start | bytes 196616 | tf_op jit(solution)/shard_map/ppermute | solution.py:386
  8.1 5.3 %collective-permute-start.4 = (bf16[4,4,16,128]{3,2,1,0:T(8,128)(2,1)S(1)}, bf16[4,4,16,128]{3,2,1,0:T(8,128)(2,1)S(1)}, u32[]{:S(2)}, u32[]{:S(2)}) collective-permute-start(bf16[4,4,16,128]{3,2,1,0:T(8,128)(2,1)S(1)} %get-tuple-element.21), channel_id=1, source_target_pairs={{0,2},{1,3},{2,0},{3,1},{4,6},{5,7},{6,4},{7,5},{8,10},{9,11},{10,... | collective-permute-start | bytes 196616 | tf_op jit(solution)/shard_map/ppermute | solution.py:386
  10.6 4.0 %collective-permute-start.5 = (bf16[4,4,16,128]{3,2,1,0:T(8,128)(2,1)S(1)}, bf16[4,4,16,128]{3,2,1,0:T(8,128)(2,1)S(1)}, u32[]{:S(2)}, u32[]{:S(2)}) collective-permute-start(bf16[4,4,16,128]{3,2,1,0:T(8,128)(2,1)S(1)} %get-tuple-element.22), channel_id=1, source_target_pairs={{0,3},{1,2},{2,1},{3,0},{4,7},{5,6},{6,5},{7,4},{8,11},{9,10},{10,... | collective-permute-start | bytes 196616 | tf_op jit(solution)/shard_map/ppermute | solution.py:386
  14.7 8.4 %collective-permute-start.6 = (bf16[16,4,16,128]{3,2,1,0:T(8,128)(2,1)S(1)}, bf16[16,4,16,128]{3,2,1,0:T(8,128)(2,1)S(1)}, u32[]{:S(2)}, u32[]{:S(2)}) collective-permute-start(bf16[16,4,16,128]{3,2,1,0:T(8,128)(2,1)S(1)} %constant_dynamic-update-slice_fusion), channel_id=1, source_target_pairs={{0,8},{8,16},{16,24},{24,28},{28,20},{20,12},{12,4},{4,0},{1,9},{9... | collective-permute-start | bytes 786440 | tf_op jit(solution)/shard_map/ppermute | solution.py:407
  16.3 8.4 %collective-permute-start.7 = (bf16[16,4,16,128]{3,2,1,0:T(8,128)(2,1)S(1)}, bf16[16,4,16,128]{3,2,1,0:T(8,128)(2,1)S(1)}, u32[]{:S(2)}, u32[]{:S(2)}) collective-permute-start(bf16[16,4,16,128]{3,2,1,0:T(8,128)(2,1)S(1)} %constant_dynamic-update-slice_fusion), channel_id=1, source_target_pairs={{0,4},{8,0},{16,8},{24,16},{28,24},{20,28},{12,20},{4,12},{1,5},{9... | collective-permute-start | bytes 786440 | tf_op jit(solution)/shard_map/ppermute | solution.py:408
  23.1 7.5 %collective-permute-start.8 = (bf16[16,4,16,128]{3,2,1,0:T(8,128)(2,1)S(1)}, bf16[16,4,16,128]{3,2,1,0:T(8,128)(2,1)S(1)}, u32[]{:S(2)}, u32[]{:S(2)}) collective-permute-start(bf16[16,4,16,128]{3,2,1,0:T(8,128)(2,1)S(1)} %collective-permute-done.6.rest_4_), channel_id=1, source_target_pairs={{0,8},{8,16},{16,24},{24,28},{28,20},{20,12},{12,4},{4,0},{1,9},{9... | collective-permute-start | bytes 786440 | tf_op jit(solution)/shard_map/ppermute | solution.py:407
  24.7 7.5 %collective-permute-start.9 = (bf16[16,4,16,128]{3,2,1,0:T(8,128)(2,1)S(1)}, bf16[16,4,16,128]{3,2,1,0:T(8,128)(2,1)S(1)}, u32[]{:S(2)}, u32[]{:S(2)}) collective-permute-start(bf16[16,4,16,128]{3,2,1,0:T(8,128)(2,1)S(1)} %collective-permute-done.7.rest_5_), channel_id=1, source_target_pairs={{0,4},{8,0},{16,8},{24,16},{28,24},{20,28},{12,20},{4,12},{1,5},{9... | collective-permute-start | bytes 786440 | tf_op jit(solution)/shard_map/ppermute | solution.py:408
  30.7 6.6 %collective-permute-start.10 = (bf16[16,4,16,128]{3,2,1,0:T(8,128)(2,1)S(1)}, bf16[16,4,16,128]{3,2,1,0:T(8,128)(2,1)S(1)}, u32[]{:S(2)}, u32[]{:S(2)}) collective-permute-start(bf16[16,4,16,128]{3,2,1,0:T(8,128)(2,1)S(1)} %collective-permute-done.8.rest_6_), channel_id=1, source_target_pairs={{0,8},{8,16},{16,24},{24,28},{28,20},{20,12},{12,4},{4,0},{1,9},{9... | collective-permute-start | bytes 786440 | tf_op jit(solution)/shard_map/ppermute | solution.py:407
  32.2 6.7 %collective-permute-start.11 = (bf16[16,4,16,128]{3,2,1,0:T(8,128)(2,1)S(1)}, bf16[16,4,16,128]{3,2,1,0:T(8,128)(2,1)S(1)}, u32[]{:S(2)}, u32[]{:S(2)}) collective-permute-start(bf16[16,4,16,128]{3,2,1,0:T(8,128)(2,1)S(1)} %collective-permute-done.9.rest_7_), channel_id=1, source_target_pairs={{0,4},{8,0},{16,8},{24,16},{28,24},{20,28},{12,20},{4,12},{1,5},{9... | collective-permute-start | bytes 786440 | tf_op jit(solution)/shard_map/ppermute | solution.py:408
  32.7 6.8 %collective-permute-start = (bf16[4,16,16,128]{3,2,1,0:T(8,128)(2,1)S(1)}, bf16[4,16,16,128]{3,2,1,0:T(8,128)(2,1)S(1)}, u32[]{:S(2)}, u32[]{:S(2)}) collective-permute-start(bf16[4,16,16,128]{3,2,1,0:T(8,128)(2,1)S(1)} %get-tuple-element.18.rest_0_), channel_id=1, source_target_pairs={{0,1},{1,0},{2,3},{3,2},{4,5},{5,4},{6,7},{7,6},{8,9},{9,8},{10,11... | collective-permute-start | bytes 786440 | tf_op jit(solution)/shard_map/ppermute | solution.py:386
  32.7 9.1 %collective-permute-start.1 = (bf16[4,16,16,128]{3,2,1,0:T(8,128)(2,1)S(1)}, bf16[4,16,16,128]{3,2,1,0:T(8,128)(2,1)S(1)}, u32[]{:S(2)}, u32[]{:S(2)}) collective-permute-start(bf16[4,16,16,128]{3,2,1,0:T(8,128)(2,1)S(1)} %get-tuple-element.18.rest_0_), channel_id=1, source_target_pairs={{0,2},{1,3},{2,0},{3,1},{4,6},{5,7},{6,4},{7,5},{8,10},{9,11},{10,... | collective-permute-start | bytes 786440 | tf_op jit(solution)/shard_map/ppermute | solution.py:386
  34.3 12.4 %collective-permute-start.2 = (bf16[4,16,16,128]{3,2,1,0:T(8,128)(2,1)S(1)}, bf16[4,16,16,128]{3,2,1,0:T(8,128)(2,1)S(1)}, u32[]{:S(2)}, u32[]{:S(2)}) collective-permute-start(bf16[4,16,16,128]{3,2,1,0:T(8,128)(2,1)S(1)} %get-tuple-element.18.rest_0_), channel_id=1, source_target_pairs={{0,3},{1,2},{2,1},{3,0},{4,7},{5,6},{6,5},{7,4},{8,11},{9,10},{10,... | collective-permute-start | bytes 786440 | tf_op jit(solution)/shard_map/ppermute | solution.py:386
  37.3 16.9 %collective-permute-start.15 = (bf16[8,4,16,128]{3,2,1,0:T(8,128)(2,1)S(1)}, bf16[8,4,16,128]{3,2,1,0:T(8,128)(2,1)S(1)}, u32[]{:S(2)}, u32[]{:S(2)}) collective-permute-start(bf16[8,4,16,128]{3,2,1,0:T(8,128)(2,1)S(1)} %slice.8), channel_id=1, source_target_pairs={{0,8},{8,16},{16,24},{24,28},{28,20},{20,12},{12,4},{4,0},{1,9},{9... | collective-permute-start | bytes 393224 | tf_op jit(solution)/shard_map/ppermute | solution.py:416
  38.9 15.3 %collective-permute-start.16 = (bf16[8,4,16,128]{3,2,1,0:T(8,128)(2,1)S(1)}, bf16[8,4,16,128]{3,2,1,0:T(8,128)(2,1)S(1)}, u32[]{:S(2)}, u32[]{:S(2)}) collective-permute-start(bf16[8,4,16,128]{3,2,1,0:T(8,128)(2,1)S(1)} %slice.9), channel_id=1, source_target_pairs={{0,4},{8,0},{16,8},{24,16},{28,24},{20,28},{12,20},{4,12},{1,5},{9... | collective-permute-start | bytes 393224 | tf_op jit(solution)/shard_map/ppermute | solution.py:417
  52.2 15.6 %copy-start.7 = (bf16[4,128,512]{2,1,0:T(8,128)(2,1)S(1)}, bf16[4,128,512]{2,1,0:T(8,128)(2,1)}, u32[]{:S(2)}) copy-start(bf16[4,128,512]{2,1,0:T(8,128)(2,1)} %constant.14.clone.place) | copy-start | bytes 1572868
  52.3 9.8 %collective-permute-start.12 = (bf16[512,128]{1,0:T(8,128)(2,1)S(1)}, bf16[512,128]{1,0:T(8,128)(2,1)S(1)}, u32[]{:S(2)}, u32[]{:S(2)}) collective-permute-start(bf16[512,128]{1,0:T(8,128)(2,1)S(1)} %get-tuple-element.24), channel_id=1, source_target_pairs={{0,1},{1,0},{2,3},{3,2},{4,5},{5,4},{6,7},{7,6},{8,9},{9,8},{10,11... | collective-permute-start | bytes 393224 | tf_op jit(solution)/shard_map/ppermute | solution.py:386
  52.6 9.5 %collective-permute-start.13 = (bf16[512,128]{1,0:T(8,128)(2,1)S(1)}, bf16[512,128]{1,0:T(8,128)(2,1)S(1)}, u32[]{:S(2)}, u32[]{:S(2)}) collective-permute-start(bf16[512,128]{1,0:T(8,128)(2,1)S(1)} %get-tuple-element.25), channel_id=1, source_target_pairs={{0,2},{1,3},{2,0},{3,1},{4,6},{5,7},{6,4},{7,5},{8,10},{9,11},{10,... | collective-permute-start | bytes 393224 | tf_op jit(solution)/shard_map/ppermute | solution.py:386
  54.2 7.9 %collective-permute-start.14 = (bf16[512,128]{1,0:T(8,128)(2,1)S(1)}, bf16[512,128]{1,0:T(8,128)(2,1)S(1)}, u32[]{:S(2)}, u32[]{:S(2)}) collective-permute-start(bf16[512,128]{1,0:T(8,128)(2,1)S(1)} %get-tuple-element.26), channel_id=1, source_target_pairs={{0,3},{1,2},{2,1},{3,0},{4,7},{5,6},{6,5},{7,4},{8,11},{9,10},{10,... | collective-permute-start | bytes 393224 | tf_op jit(solution)/shard_map/ppermute | solution.py:386
  59.8 2.3 %collective-permute-start.17 = (bf16[512,128]{1,0:T(8,128)(2,1)S(1)}, bf16[512,128]{1,0:T(8,128)(2,1)S(1)}, u32[]{:S(2)}, u32[]{:S(2)}) collective-permute-start(bf16[512,128]{1,0:T(8,128)(2,1)S(1)} %get-tuple-element.28), channel_id=1, source_target_pairs={{0,1},{1,0},{2,3},{3,2},{4,5},{5,4},{6,7},{7,6},{8,9},{9,8},{10,11... | collective-permute-start | bytes 393224 | tf_op jit(solution)/shard_map/ppermute | solution.py:386
  60.4 6.3 %collective-permute-start.18 = (bf16[512,128]{1,0:T(8,128)(2,1)S(1)}, bf16[512,128]{1,0:T(8,128)(2,1)S(1)}, u32[]{:S(2)}, u32[]{:S(2)}) collective-permute-start(bf16[512,128]{1,0:T(8,128)(2,1)S(1)} %get-tuple-element.29), channel_id=1, source_target_pairs={{0,2},{1,3},{2,0},{3,1},{4,6},{5,7},{6,4},{7,5},{8,10},{9,11},{10,... | collective-permute-start | bytes 393224 | tf_op jit(solution)/shard_map/ppermute | solution.py:386
  62.1 5.8 %collective-permute-start.19 = (bf16[512,128]{1,0:T(8,128)(2,1)S(1)}, bf16[512,128]{1,0:T(8,128)(2,1)S(1)}, u32[]{:S(2)}, u32[]{:S(2)}) collective-permute-start(bf16[512,128]{1,0:T(8,128)(2,1)S(1)} %get-tuple-element.30), channel_id=1, source_target_pairs={{0,3},{1,2},{2,1},{3,0},{4,7},{5,6},{6,5},{7,4},{8,11},{9,10},{10,... | collective-permute-start | bytes 393224 | tf_op jit(solution)/shard_map/ppermute | solution.py:386

commit v2 on v1

v2 whole, which is shorter than its diff:
```python
import functools
import math

import jax
import jax.numpy as jnp
import ml_dtypes
import numpy as np
from jax import lax
from jax.experimental import pallas as pl
from jax.experimental.pallas import tpu as pltpu
from jax.sharding import PartitionSpec as P

NBIN = 1024
HALF = 64
ROUNDS = 4
LAGS = 2048
LANES = 128
TILES = NBIN // LANES
BF = jnp.bfloat16
F32 = jnp.float32


def make_table(rows, transform):
    phase = (np.arange(rows)[:, None] * np.arange(NBIN)[None, :]) % transform
    angle = phase * (2.0 * math.pi / transform)
    return np.concatenate([np.cos(angle), -np.sin(angle)], axis=1).astype(ml_dtypes.bfloat16)


def band_matrix():
    source = lax.broadcasted_iota(jnp.int32, (3 * LANES, LANES), 0) - LANES
    target = lax.broadcasted_iota(jnp.int32, (3 * LANES, LANES), 1)
    return jnp.where(jnp.abs(source - target) <= HALF, 1.0, 0.0).astype(BF)


def inverse_count(block, length):
    position = lax.broadcasted_iota(jnp.int32, (1, LANES), 1) + block * LANES
    counted = jnp.minimum(position, HALF) + jnp.minimum(length - 1 - position, HALF) + 1
    return 1.0 / counted.astype(F32)


def make_placing(stations, quarter, parts):
    width = stations * quarter
    place = np.zeros((parts, 2 * width, 2 * stations * stations), np.float32)
    for part in range(parts):
        for second in range(2):
            for s in range(stations):
                for t in range(quarter):
                    row = second * width + s * quarter + t
                    column = (second * stations + s) * stations + part * quarter + t
                    place[part, row, column] = 1.0
    return place.astype(ml_dtypes.bfloat16)


def lane_cycle(values):
    phase = lax.broadcasted_iota(jnp.int32, (1, LANES), 1) % 4
    out = jnp.full((1, LANES), values[3], F32)
    for index in range(3):
        out = jnp.where(phase == index, values[index], out)
    return out


def even_lanes(shape):
    return lax.broadcasted_iota(jnp.int32, shape, 1) % 2 == 0


def banded_sum(stack, values, band):
    rows, length = values.shape
    blocks = length // LANES
    zero = jnp.zeros((rows, LANES), BF)
    for j in range(blocks):
        at = pl.ds(j * rows, rows)
        for k in range(3):
            b = j + k - 1
            block = values[:, b * LANES : (b + 1) * LANES] if 0 <= b < blocks else zero
            stack[at, k * LANES : (k + 1) * LANES] = block
    total = jnp.dot(stack[: blocks * rows, :], band, preferred_element_type=F32)
    return [total[j * rows : (j + 1) * rows, :] for j in range(blocks)]


def prep_kernel(quarter, records_hbm, table_hbm, white, *rest):
    parts = len(rest) - 6
    quarters = rest[:parts]
    records, table, stack, flat, spread, sems = rest[parts:]
    records_copy = pltpu.make_async_copy(records_hbm, records, sems.at[0])
    records_copy.start()
    copy = pltpu.make_async_copy(table_hbm, table, sems.at[1])
    copy.start()
    band_values = band_matrix()
    records_copy.wait()
    stations, windows, length = records.shape
    rows = stations * windows
    half = length // 2
    signal = jnp.concatenate([records[:, w, :] for w in range(windows)], axis=0)
    sums = banded_sum(stack, jnp.abs(signal).astype(BF), band_values)
    for j, total in enumerate(sums):
        at = slice(j * LANES, (j + 1) * LANES)
        level = total * inverse_count(j, length)
        value = (signal[:, at] / (level + 1e-05)).astype(BF)
        if j * LANES < half:
            flat[:rows, at] = value
        else:
            flat[rows:, j * LANES - half : (j + 1) * LANES - half] = value
    copy.wait()
    product = jnp.dot(flat[...], table[...], preferred_element_type=F32)
    even = even_lanes((rows, LANES))
    sign_real = lane_cycle([1.0, 1.0, -1.0, -1.0])
    sign_imag = lane_cycle([1.0, -1.0, -1.0, 1.0])
    reals, imags, mags = [], [], []
    for j in range(TILES):
        at = slice(j * LANES, (j + 1) * LANES)
        at_imag = slice(NBIN + j * LANES, NBIN + (j + 1) * LANES)
        later_real, later_imag = product[rows:, at], product[rows:, at_imag]
        real = product[:rows, at] + sign_real * jnp.where(even, later_real, later_imag)
        imag = product[:rows, at_imag] + sign_imag * jnp.where(even, later_imag, later_real)
        reals.append(real)
        imags.append(imag)
        mags.append(jnp.sqrt(real * real + imag * imag).astype(BF))
    sums = banded_sum(stack, jnp.concatenate(mags, axis=1), band_values)
    for j, total in enumerate(sums):
        at = slice(j * LANES, (j + 1) * LANES)
        smooth = total * inverse_count(j, NBIN) + 1e-06
        spread[pl.ds(j, rows, stride=2 * TILES), :] = reals[j] / smooth
        spread[pl.ds(TILES + j, rows, stride=2 * TILES), :] = imags[j] / smooth
    me = lax.axis_index("seg")
    out = spread[...].reshape(windows, stations, 2 * TILES, LANES).astype(BF)
    white[...] = out
    for j in range(parts):
        first = (me ^ j) * quarter
        for w in range(windows):
            quarters[j][w] = white[w, pl.ds(first, quarter)]


def prepare(records, table, parts):
    stations, windows, length = records.shape
    rows = stations * windows
    quarter = stations // parts
    small = jax.ShapeDtypeStruct((windows, quarter, 2 * TILES, LANES), BF)
    vmem = pl.BlockSpec(memory_space=pltpu.VMEM)
    return pl.pallas_call(
        functools.partial(prep_kernel, quarter),
        out_shape=[jax.ShapeDtypeStruct((windows, stations, 2 * TILES, LANES), BF)]
        + [small] * parts,
        in_specs=[pl.BlockSpec(memory_space=pl.ANY)] * 2,
        out_specs=[vmem] * (parts + 1),
        scratch_shapes=[
            pltpu.VMEM(records.shape, F32),
            pltpu.VMEM(table.shape, BF),
            pltpu.VMEM((rows * (length // LANES), 3 * LANES), BF),
            pltpu.VMEM((2 * rows, length // 2), BF),
            pltpu.VMEM((rows * 2 * TILES, LANES), F32),
            pltpu.SemaphoreType.DMA((2,)),
        ],
        compiler_params=pltpu.CompilerParams(vmem_limit_bytes=58 * 2**20),
        cost_estimate=pl.CostEstimate(
            flops=2 * 2 * rows * (length // 2) * 2 * NBIN, bytes_accessed=6 * 2**20, transcendentals=0
        ),
        name="prep",
    )(records, table)


def cross_kernel(scaling, parts, plan, table, gathered, *rest):
    owns = rest[:parts]
    outs = rest[parts : 2 * parts]
    own, other, crossed, operand, result = rest[2 * parts :]
    windows, stations = owns[0].shape[:2]
    all_windows = windows * parts
    quarter = gathered.shape[2]
    slots = ROUNDS
    width = stations * quarter
    columns = slots * width
    block = lax.axis_index("sta")

    for j in range(parts):

        def widen_own(w, carry, j=j):
            raw = owns[j][w].astype(F32)
            real, imag = raw[:, :TILES], raw[:, TILES:]
            own[0, j * windows + w] = real + imag
            own[1, j * windows + w] = real
            own[2, j * windows + w] = imag
            return carry

        lax.fori_loop(0, windows, widen_own, 0)
    for slot in range(slots):
        partner = plan[slot, block]

        def widen_other(w, carry, slot=slot, partner=partner):
            raw = gathered[partner, w].astype(F32)
            real, imag = raw[:, :TILES], raw[:, TILES:]
            other[0, slot, w] = real
            other[1, slot, w] = real + imag
            other[2, slot, w] = imag - real
            return carry

        lax.fori_loop(0, all_windows, widen_other, 0)

    group = 4
    groups = stations // group
    first_bin = (lax.broadcasted_iota(jnp.int32, (TILES, LANES), 0) == 0) & (
        lax.broadcasted_iota(jnp.int32, (TILES, LANES), 1) == 0
    )
    weight = jnp.where(first_bin, 1.0, 2.0).astype(F32)

    def one_group(index, carry):
        slot = index // groups
        first = (index % groups) * group

        def sums(kind):
            totals = [None] * (group * quarter)
            for w in range(all_windows):
                left = [own[kind, w, first + s] for s in range(group)]
                right = [other[kind, slot, w, t] for t in range(quarter)]
                for s in range(group):
                    for t in range(quarter):
                        term = left[s] * right[t]
                        place = s * quarter + t
                        totals[place] = term if w == 0 else totals[place] + term
            return totals

        base = slot * width + first * quarter
        shared = sums(0)
        third = sums(2)
        for place in range(group * quarter):
            at = pl.multiple_of((base + place) * 2 * TILES, 2 * TILES)
            crossed[pl.ds(at, TILES), :] = (shared[place] + third[place]) * weight
        second = sums(1)
        for place in range(group * quarter):
            at = pl.multiple_of((base + place) * 2 * TILES + TILES, TILES)
            crossed[pl.ds(at, TILES), :] = (shared[place] - second[place]) * weight
        return carry

    lax.fori_loop(0, slots * groups, one_group, 0)

    even = even_lanes((columns, LANES))
    sign_real = lane_cycle([1.0, -1.0, -1.0, 1.0])
    sign_imag = lane_cycle([1.0, 1.0, -1.0, -1.0])
    for j in range(TILES):
        at = slice(j * LANES, (j + 1) * LANES)
        at_imag = slice(NBIN + j * LANES, NBIN + (j + 1) * LANES)
        real = crossed[pl.ds(j, columns, stride=2 * TILES), :]
        imag = crossed[pl.ds(TILES + j, columns, stride=2 * TILES), :]
        operand[:columns, at] = real.astype(BF)
        operand[:columns, at_imag] = imag.astype(BF)
        operand[columns:, at] = (sign_real * jnp.where(even, real, imag)).astype(BF)
        operand[columns:, at_imag] = (sign_imag * jnp.where(even, imag, real)).astype(BF)
    share = outs[0].shape[0]
    per_half = table.shape[0] // share
    for q in range(per_half):
        block = lax.dot_general(
            table[q * share : (q + 1) * share, :],
            operand[...],
            (((1,), (1,)), ((), ())),
            preferred_element_type=F32,
        )
        block = (block * scaling).astype(BF)
        for h in range(2):
            result[h * per_half + q] = block[:, h * columns : (h + 1) * columns]
    me = lax.axis_index("seg")
    for j in range(parts):
        outs[j][...] = result[me ^ j]


def cross_lags(plan, table, owns, gathered, scaling):
    parts = len(owns)
    windows, stations = owns[0].shape[:2]
    all_windows = windows * parts
    quarter = gathered.shape[2]
    slots = ROUNDS
    columns = slots * stations * quarter
    share = LAGS // parts
    smem = pl.BlockSpec(memory_space=pltpu.SMEM)
    vmem = pl.BlockSpec(memory_space=pltpu.VMEM)
    return pl.pallas_call(
        functools.partial(cross_kernel, scaling, parts),
        out_shape=[jax.ShapeDtypeStruct((share, columns), BF)] * parts,
        in_specs=[smem] + [vmem] * (2 + parts),
        out_specs=[vmem] * parts,
        scratch_shapes=[
            pltpu.VMEM((3, all_windows, stations, TILES, LANES), F32),
            pltpu.VMEM((3, slots, all_windows, quarter, TILES, LANES), F32),
            pltpu.VMEM((columns * 2 * TILES, LANES), F32),
            pltpu.VMEM((2 * columns, 2 * NBIN), BF),
            pltpu.VMEM((parts, share, columns), BF),
        ],
        compiler_params=pltpu.CompilerParams(vmem_limit_bytes=32 * 2**20),
        cost_estimate=pl.CostEstimate(
            flops=2 * LAGS * 2 * NBIN * columns * 2, bytes_accessed=8 * 2**20, transcendentals=0
        ),
        name="cross",
    )(plan, table, gathered, *owns)


def place_kernel(parts, place, *rest):
    pieces = rest[:parts]
    out = rest[parts]
    pairs = out.shape[2]
    me = lax.axis_index("seg")
    matrix = jnp.concatenate([place[me ^ j] for j in range(parts)], axis=0)
    for p in range(ROUNDS // 2):
        at = slice(p * pairs // 2, (p + 1) * pairs // 2)
        joined = jnp.concatenate([piece[:, at] for piece in pieces], axis=1)
        block = jnp.dot(joined, matrix, preferred_element_type=F32)
        out[:, 2 * p, :] = block[:, :pairs]
        out[:, 2 * p + 1, :] = block[:, pairs:]


def place_lags(pieces, stations):
    parts = len(pieces)
    share, columns = pieces[0].shape
    pairs = stations * stations
    steps = 4
    rows = share // steps
    place = make_placing(stations, stations // parts, parts)
    return pl.pallas_call(
        functools.partial(place_kernel, parts),
        out_shape=jax.ShapeDtypeStruct((share, ROUNDS, pairs), F32),
        grid=(steps,),
        in_specs=[pl.BlockSpec(place.shape, lambda i: (0, 0, 0))]
        + [pl.BlockSpec((rows, columns), lambda i: (i, 0))] * parts,
        out_specs=pl.BlockSpec((rows, ROUNDS, pairs), lambda i: (i, 0, 0)),
        compiler_params=pltpu.CompilerParams(vmem_limit_bytes=32 * 2**20),
        cost_estimate=pl.CostEstimate(
            flops=2 * share * 4 * pairs * ROUNDS * pairs, bytes_accessed=4 * 2**20, transcendentals=0
        ),
        name="place",
    )(place, *pieces)


def exchange(pieces):
    parts = len(pieces)
    out = [pieces[0]]
    for j in range(1, parts):
        out.append(lax.ppermute(pieces[j], "seg", [(i, i ^ j) for i in range(parts)]))
    return out


def per_device(records, plan):
    stations, windows, length = records.shape
    parts = lax.axis_size("seg")
    table = jnp.asarray(make_table(length // 2, 2 * length))
    scaling = 1.0 / math.sqrt(4.0 * NBIN * windows * parts)

    white, *quarters = prepare(records, table, parts)
    shared = jnp.concatenate(exchange(quarters), axis=0)
    gathered = lax.all_gather(shared, "sta")
    owns = exchange([white] * parts)
    lags = cross_lags(plan, table, owns, gathered, scaling)
    return place_lags(exchange(lags), stations)


def solution(mesh):
    in_specs = (P("sta", "seg", None), P())
    out_specs = P("seg", None, "sta")
    return jax.shard_map(
        per_device, mesh=mesh, in_specs=in_specs, out_specs=out_specs, check_vma=False
    )
```

time: 71.8 us -> 108 us (1.50)
  waiting for transfers between devices: 31.5 us -> 64.8 us
  between operations: 0.1 us -> 13.4 us
  starting transfers between devices: 17.5 us -> 7.05 us
  other arithmetic: 0 us -> 1.58 us
    all_gather x0 -> x1, waiting for transfers between devices: none -> 36 us  [per_device(): gathered = lax.all_gather(shared, 'sta')]
    ppermute x8 -> x0, waiting for transfers between devices: 14.6 us -> none  [the longest x3 14.6 us: per_device(): from_left = lax.ppermute(from_left, 'sta', forward)]
    ppermute x12 -> x9, waiting for transfers between devices: 16.9 us -> 28.8 us  [exchange(): lax.ppermute(pieces[j], 'seg', [(i, i ^ j) for i in range(parts)])]
    ppermute x8 -> x0, starting transfers between devices: 8.26 us -> none  [the longest x3 4.75 us: per_device(): from_left = lax.ppermute(from_left, 'sta', forward)]
    pallas_call x3 -> x2, Pallas kernels: 14.4 us -> 11.3 us  [the longest x1 8.63 us: cross_lags(): pl.pallas_call(functools.partial(cross_kernel, scaling, parts), out_shape...]
    pallas_call x1, Pallas kernels: 2.01 us -> 4.36 us  [prepare(): pl.pallas_call(functools.partial(prep_kernel, quarter), out_shape=[jax.Sh...]
    ppermute x12 -> x9, starting transfers between devices: 9.22 us -> 7.04 us  [exchange(): lax.ppermute(pieces[j], 'seg', [(i, i ^ j) for i in range(parts)])]
    concatenate x0 -> x1, other arithmetic: none -> 1.58 us  [per_device(): shared = jnp.concatenate(exchange(quarters), axis=0)]
  transfers between devices with their start and end apart: 20 -> 10, of which waited for: 9 -> 7; matrix products, arithmetic and copies ran while one was open for 0% -> 0% of each run, Pallas kernels for 16% -> 0%
where the time goes in v2:
time: 108 us; the launch traced here: 107 us
  waiting for transfers between devices  64.8 us (60%)
  Pallas kernels  15.7 us (15%)
  between operations  13.4 us (12%)
  starting transfers between devices  7.05 us (7%)
  local copies, waits for them, and re-layouts  4.74 us (4%)
  other arithmetic  1.58 us (1%)
    all_gather x1, waiting for transfers between devices, per_device(): gathered = lax.all_gather(shared, 'sta')  36 us
    ppermute x9, waiting for transfers between devices, exchange(): lax.ppermute(pieces[j], 'seg', [(i, i ^ j) for i in range(parts)])  28.8 us
    pallas_call x1, Pallas kernels, cross_lags(): pl.pallas_call(functools.partial(cross_kernel, scaling, parts), out_shape...  8.63 us
    ppermute x9, starting transfers between devices, exchange(): lax.ppermute(pieces[j], 'seg', [(i, i ^ j) for i in range(parts)])  7.04 us
    unnamed x10, local copies, waits for them, and re-layouts  4.74 us
    pallas_call x1, Pallas kernels, prepare(): pl.pallas_call(functools.partial(prep_kernel, quarter), out_shape=[jax.Sh...  4.36 us
    pallas_call x1, Pallas kernels, place_lags(): pl.pallas_call(functools.partial(place_kernel, parts), out_shape=jax.Shap...  2.71 us
  transfers between devices with their start and end apart: 10, of which 7 were waited for; matrix products, arithmetic and copies ran while one was open for 0% of the time, Pallas kernels for 0%

profile of v2, /device:TPU:0, one launch (start us, length us, event | category | flops | bytes accessed | tf_op | source)
XLA Modules:
  0.0 107.3 jit_solution(1438022580754618266)
XLA Ops:
  6.5 0.0 copy-start.3
  6.5 0.0 all-gather.3.cloned.1.call-start
  6.5 4.4 %prep.1 = (bf16[4,16,16,128]{3,2,1,0:T(8,128)(2,1)}, bf16[4,4,16,128]{3,2,1,0:T(8,128)(2,1)}, bf16[4,4,16,128]{3,2,1,0:T(8,128)(2,1)}, bf16[4,4,16,128]{3,2,1,0:T(8,128)(2,1)}, bf16[4,4,16,128]{3,2,1,0:T(8,128)(2,1)}) custom-call(f32[16,4,2048]{2,1,0:T(4,128)} %records_hbm.1, bf16[1024,2048]{1,0:T(8,128)(2,1)} %constant.4.clone.table_hbm.table), custom_call_target="tpu_custom_call" | custom-call | flops 536870912 | bytes 6291456 | tf_op jit(solution)/shard_map/prep/pallas_call | solution.py:139
  10.9 0.5 collective-permute-start
  11.4 2.6 %collective-permute-start.1 = (bf16[4,4,16,128]{3,2,1,0:T(8,128)(2,1)}, bf16[4,4,16,128]{3,2,1,0:T(8,128)(2,1)S(1)}, u32[]{:S(2)}, u32[]{:S(2)}) collective-permute-start(bf16[4,4,16,128]{3,2,1,0:T(8,128)(2,1)} %get-tuple-element.16), channel_id=1, source_target_pairs={{0,2},{1,3},{2,0},{3,1},{4,6},{5,7},{6,4},{7,5},{8,10},{9,11},{10,... | collective-permute-start | bytes 196616 | tf_op jit(solution)/shard_map/ppermute | solution.py:333
  14.0 0.1 collective-permute-start.2
  14.1 0.0 collective-permute-done
  14.1 2.8 %collective-permute-done.1 = bf16[4,4,16,128]{3,2,1,0:T(8,128)(2,1)S(1)} collective-permute-done((bf16[4,4,16,128]{3,2,1,0:T(8,128)(2,1)}, bf16[4,4,16,128]{3,2,1,0:T(8,128)(2,1)S(1)}, u32[]{:S(2)}, u32[]{:S(2)}) %collective-permute-start.1) | collective-permute-done | bytes 65568 | tf_op jit(solution)/shard_map/ppermute | solution.py:333
  16.9 1.4 %collective-permute-done.2 = bf16[4,4,16,128]{3,2,1,0:T(8,128)(2,1)S(1)} collective-permute-done((bf16[4,4,16,128]{3,2,1,0:T(8,128)(2,1)}, bf16[4,4,16,128]{3,2,1,0:T(8,128)(2,1)S(1)}, u32[]{:S(2)}, u32[]{:S(2)}) %collective-permute-start.2) | collective-permute-done | bytes 65568 | tf_op jit(solution)/shard_map/ppermute | solution.py:333
  18.3 1.6 %pad_maximum_fusion = bf16[16,4,16,128]{3,2,1,0:T(8,128)(2,1)} fusion(bf16[4,4,16,128]{3,2,1,0:T(8,128)(2,1)S(1)} %collective-permute-done.2, bf16[4,4,16,128]{3,2,1,0:T(8,128)(2,1)S(1)} %collective-permute-done.1, bf16[4,4,16,128]{3,2,1,0:T(8,128)(2,1)S(1)} %collective-permute-done, bf16[4,4,16,128]{3,2,1,0:T(8,128)(2,1)} %get-tuple-element.14), kind=kLoop, calls=%fused_computation | loop fusion | flops 393216 | bytes 524288 | tf_op jit(solution)/shard_map/concatenate | solution.py:344
  19.9 0.0 all-gather.3.cloned.1.call-update
  19.9 1.2 %collective-permute-start.5 = (bf16[4,16,16,128]{3,2,1,0:T(8,128)(2,1)}, bf16[4,16,16,128]{3,2,1,0:T(8,128)(2,1)S(1)}, u32[]{:S(2)}, u32[]{:S(2)}) collective-permute-start(bf16[4,16,16,128]{3,2,1,0:T(8,128)(2,1)} %get-tuple-element.18.rest_0_), channel_id=1, source_target_pairs={{0,3},{1,2},{2,1},{3,0},{4,7},{5,6},{6,5},{7,4},{8,11},{9,10},{10,... | collective-permute-start | bytes 786440 | tf_op jit(solution)/shard_map/ppermute | solution.py:333
  21.1 0.6 collective-permute-start.4
  21.8 0.1 collective-permute-start.3
  21.9 6.6 %collective-permute-done.5.rest_3_ = bf16[4,16,16,128]{3,2,1,0:T(8,128)(2,1)S(1)} collective-permute-done((bf16[4,16,16,128]{3,2,1,0:T(8,128)(2,1)}, bf16[4,16,16,128]{3,2,1,0:T(8,128)(2,1)S(1)}, u32[]{:S(2)}, u32[]{:S(2)}) %collective-permute-start.5) | collective-permute-done | bytes 262176 | tf_op jit(solution)/shard_map/ppermute | solution.py:333
  28.5 5.9 %collective-permute-done.4.rest_2_ = bf16[4,16,16,128]{3,2,1,0:T(8,128)(2,1)S(1)} collective-permute-done((bf16[4,16,16,128]{3,2,1,0:T(8,128)(2,1)}, bf16[4,16,16,128]{3,2,1,0:T(8,128)(2,1)S(1)}, u32[]{:S(2)}, u32[]{:S(2)}) %collective-permute-start.4) | collective-permute-done | bytes 262176 | tf_op jit(solution)/shard_map/ppermute | solution.py:333
  34.4 0.0 collective-permute-done.3.rest_1_
  34.4 36.0 %all-gather.3.cloned.1.call-done = bf16[128,4,16,128]{3,2,1,0:T(8,128)(2,1)} async-done(((bf16[16,4,16,128]{3,2,1,0:T(8,128)(2,1)}), bf16[128,4,16,128]{3,2,1,0:T(8,128)(2,1)}) %all-gather.3.cloned.1.call-update) | async-done | bytes 2097168 | tf_op jit(solution)/shard_map/all_gather | solution.py:345
  70.4 0.0 copy-done.3
  70.4 0.0 copy-start
  70.4 2.2 %copy-done = bf16[1024,2048]{1,0:T(8,128)(2,1)S(1)} copy-done((bf16[1024,2048]{1,0:T(8,128)(2,1)S(1)}, bf16[1024,2048]{1,0:T(8,128)(2,1)}, u32[]{:S(2)}) %copy-start) | copy-done | bytes 4194328
  72.6 1.6 %copy-done.1 = bf16[128,4,16,128]{3,2,1,0:T(8,128)(2,1)S(1)} copy-done((bf16[128,4,16,128]{3,2,1,0:T(8,128)(2,1)S(1)}, bf16[128,4,16,128]{3,2,1,0:T(8,128)(2,1)}, u32[]{:S(2)}) %copy-start.1) | copy-done | bytes 2097176
  74.2 0.9 copy-done.2
  75.1 8.6 %cross.1 = (bf16[512,256]{1,0:T(8,128)(2,1)S(1)}, bf16[512,256]{1,0:T(8,128)(2,1)S(1)}, bf16[512,256]{1,0:T(8,128)(2,1)S(1)}, bf16[512,256]{1,0:T(8,128)(2,1)S(1)}) custom-call(s32[4,8]{1,0:T(4,128)S(1)} %copy-done.3, bf16[1024,2048]{1,0:T(8,128)(2,1)S(1)} %copy-done, bf16[8,16,4,16,128]{4,3,2,1,0:T(8,128)(2,1)S(1)} %bitcast.1, ...), custom_call_target="tpu_custom_call" | custom-call | flops 4294967296 | bytes 8388608 | tf_op jit(solution)/shard_map/cross/pallas_call | solution.py:273
  83.8 0.1 collective-permute-start.6
  83.9 1.5 %collective-permute-start.7 = (bf16[512,256]{1,0:T(8,128)(2,1)S(1)}, bf16[512,256]{1,0:T(8,128)(2,1)S(1)}, u32[]{:S(2)}, u32[]{:S(2)}) collective-permute-start(bf16[512,256]{1,0:T(8,128)(2,1)S(1)} %get-tuple-element.21), channel_id=1, source_target_pairs={{0,2},{1,3},{2,0},{3,1},{4,6},{5,7},{6,4},{7,5},{8,10},{9,11},{10,... | collective-permute-start | bytes 786440 | tf_op jit(solution)/shard_map/ppermute | solution.py:333
  85.4 0.3 collective-permute-start.8
  85.7 0.0 collective-permute-done.6.rest_1_
  85.7 7.3 %collective-permute-done.7.rest_2_ = bf16[512,256]{1,0:T(8,128)(2,1)S(1)} collective-permute-done((bf16[512,256]{1,0:T(8,128)(2,1)S(1)}, bf16[512,256]{1,0:T(8,128)(2,1)S(1)}, u32[]{:S(2)}, u32[]{:S(2)}) %collective-permute-start.7) | collective-permute-done | bytes 262176 | tf_op jit(solution)/shard_map/ppermute | solution.py:333
  93.0 4.7 %collective-permute-done.8.rest_3_ = bf16[512,256]{1,0:T(8,128)(2,1)S(1)} collective-permute-done((bf16[512,256]{1,0:T(8,128)(2,1)S(1)}, bf16[512,256]{1,0:T(8,128)(2,1)S(1)}, u32[]{:S(2)}, u32[]{:S(2)}) %collective-permute-start.8) | collective-permute-done | bytes 262176 | tf_op jit(solution)/shard_map/ppermute | solution.py:333
  97.7 0.0 copy-done.4
  97.7 2.7 %place.2 = f32[512,4,256]{2,1,0:T(4,128)} custom-call(bf16[4,128,512]{2,1,0:T(8,128)(2,1)S(1)} %copy-done.4, bf16[512,256]{1,0:T(8,128)(2,1)S(1)} %get-tuple-element.19.rest_0_, bf16[512,256]{1,0:T(8,128)(2,1)S(1)} %collective-permute-done.6.rest_1_, bf16[512,256]{1,0:T(8,128)(2,1)S(1)} %collective-permute-done.7.rest_2_, ...), custom_call_target="tpu_custom_call" | custom-call | flops 1073741824 | bytes 4194304 | tf_op jit(solution)/shard_map/place/pallas_call | solution.py:314
  (3 shorter events, 0.0 us)
Async XLA Ops:
  6.5 63.9 %copy-start.3 = (s32[4,8]{1,0:T(4,128)S(1)}, s32[4,8]{1,0:T(4,128)}, u32[]{:S(2)}) copy-start(s32[4,8]{1,0:T(4,128)} %plan.1) | copy-start | bytes 388
  6.5 63.9 %all-gather.3.cloned.1.call-start = ((), (), s32[]{:S(2)}) async-start(), calls=%async_computation | async-start | bytes 2359296 | tf_op jit(solution)/shard_map/all_gather | solution.py:345
  10.9 3.2 %collective-permute-start = (bf16[4,4,16,128]{3,2,1,0:T(8,128)(2,1)}, bf16[4,4,16,128]{3,2,1,0:T(8,128)(2,1)S(1)}, u32[]{:S(2)}, u32[]{:S(2)}) collective-permute-start(bf16[4,4,16,128]{3,2,1,0:T(8,128)(2,1)} %get-tuple-element.15), channel_id=1, source_target_pairs={{0,1},{1,0},{2,3},{3,2},{4,5},{5,4},{6,7},{7,6},{8,9},{9,8},{10,11... | collective-permute-start | bytes 196616 | tf_op jit(solution)/shard_map/ppermute | solution.py:333
  11.4 5.5 %collective-permute-start.1 = (bf16[4,4,16,128]{3,2,1,0:T(8,128)(2,1)}, bf16[4,4,16,128]{3,2,1,0:T(8,128)(2,1)S(1)}, u32[]{:S(2)}, u32[]{:S(2)}) collective-permute-start(bf16[4,4,16,128]{3,2,1,0:T(8,128)(2,1)} %get-tuple-element.16), channel_id=1, source_target_pairs={{0,2},{1,3},{2,0},{3,1},{4,6},{5,7},{6,4},{7,5},{8,10},{9,11},{10,... | collective-permute-start | bytes 196616 | tf_op jit(solution)/shard_map/ppermute | solution.py:333
  14.0 4.3 %collective-permute-start.2 = (bf16[4,4,16,128]{3,2,1,0:T(8,128)(2,1)}, bf16[4,4,16,128]{3,2,1,0:T(8,128)(2,1)S(1)}, u32[]{:S(2)}, u32[]{:S(2)}) collective-permute-start(bf16[4,4,16,128]{3,2,1,0:T(8,128)(2,1)} %get-tuple-element.17), channel_id=1, source_target_pairs={{0,3},{1,2},{2,1},{3,0},{4,7},{5,6},{6,5},{7,4},{8,11},{9,10},{10,... | collective-permute-start | bytes 196616 | tf_op jit(solution)/shard_map/ppermute | solution.py:333
  19.9 8.6 %collective-permute-start.5 = (bf16[4,16,16,128]{3,2,1,0:T(8,128)(2,1)}, bf16[4,16,16,128]{3,2,1,0:T(8,128)(2,1)S(1)}, u32[]{:S(2)}, u32[]{:S(2)}) collective-permute-start(bf16[4,16,16,128]{3,2,1,0:T(8,128)(2,1)} %get-tuple-element.18.rest_0_), channel_id=1, source_target_pairs={{0,3},{1,2},{2,1},{3,0},{4,7},{5,6},{6,5},{7,4},{8,11},{9,10},{10,... | collective-permute-start | bytes 786440 | tf_op jit(solution)/shard_map/ppermute | solution.py:333
  21.1 13.3 %collective-permute-start.4 = (bf16[4,16,16,128]{3,2,1,0:T(8,128)(2,1)}, bf16[4,16,16,128]{3,2,1,0:T(8,128)(2,1)S(1)}, u32[]{:S(2)}, u32[]{:S(2)}) collective-permute-start(bf16[4,16,16,128]{3,2,1,0:T(8,128)(2,1)} %get-tuple-element.18.rest_0_), channel_id=1, source_target_pairs={{0,2},{1,3},{2,0},{3,1},{4,6},{5,7},{6,4},{7,5},{8,10},{9,11},{10,... | collective-permute-start | bytes 786440 | tf_op jit(solution)/shard_map/ppermute | solution.py:333
  21.8 12.7 %collective-permute-start.3 = (bf16[4,16,16,128]{3,2,1,0:T(8,128)(2,1)}, bf16[4,16,16,128]{3,2,1,0:T(8,128)(2,1)S(1)}, u32[]{:S(2)}, u32[]{:S(2)}) collective-permute-start(bf16[4,16,16,128]{3,2,1,0:T(8,128)(2,1)} %get-tuple-element.18.rest_0_), channel_id=1, source_target_pairs={{0,1},{1,0},{2,3},{3,2},{4,5},{5,4},{6,7},{7,6},{8,9},{9,8},{10,11... | collective-permute-start | bytes 786440 | tf_op jit(solution)/shard_map/ppermute | solution.py:333
  70.4 2.2 %copy-start = (bf16[1024,2048]{1,0:T(8,128)(2,1)S(1)}, bf16[1024,2048]{1,0:T(8,128)(2,1)}, u32[]{:S(2)}) copy-start(bf16[1024,2048]{1,0:T(8,128)(2,1)} %constant.4.clone.table_hbm.table) | copy-start | bytes 12582916
  72.6 1.6 %copy-start.1 = (bf16[128,4,16,128]{3,2,1,0:T(8,128)(2,1)S(1)}, bf16[128,4,16,128]{3,2,1,0:T(8,128)(2,1)}, u32[]{:S(2)}) copy-start(bf16[128,4,16,128]{3,2,1,0:T(8,128)(2,1)} %all-gather.3.cloned.1.call-done) | copy-start | bytes 6291460
  74.2 0.9 copy-start.2
  75.1 22.6 %copy-start.4 = (bf16[4,128,512]{2,1,0:T(8,128)(2,1)S(1)}, bf16[4,128,512]{2,1,0:T(8,128)(2,1)}, u32[]{:S(2)}) copy-start(bf16[4,128,512]{2,1,0:T(8,128)(2,1)} %constant.5.clone.place) | copy-start | bytes 1572868
  83.8 1.9 %collective-permute-start.6 = (bf16[512,256]{1,0:T(8,128)(2,1)S(1)}, bf16[512,256]{1,0:T(8,128)(2,1)S(1)}, u32[]{:S(2)}, u32[]{:S(2)}) collective-permute-start(bf16[512,256]{1,0:T(8,128)(2,1)S(1)} %get-tuple-element.20), channel_id=1, source_target_pairs={{0,1},{1,0},{2,3},{3,2},{4,5},{5,4},{6,7},{7,6},{8,9},{9,8},{10,11... | collective-permute-start | bytes 786440 | tf_op jit(solution)/shard_map/ppermute | solution.py:333
  83.9 9.2 %collective-permute-start.7 = (bf16[512,256]{1,0:T(8,128)(2,1)S(1)}, bf16[512,256]{1,0:T(8,128)(2,1)S(1)}, u32[]{:S(2)}, u32[]{:S(2)}) collective-permute-start(bf16[512,256]{1,0:T(8,128)(2,1)S(1)} %get-tuple-element.21), channel_id=1, source_target_pairs={{0,2},{1,3},{2,0},{3,1},{4,6},{5,7},{6,4},{7,5},{8,10},{9,11},{10,... | collective-permute-start | bytes 786440 | tf_op jit(solution)/shard_map/ppermute | solution.py:333
  85.4 12.3 %collective-permute-start.8 = (bf16[512,256]{1,0:T(8,128)(2,1)S(1)}, bf16[512,256]{1,0:T(8,128)(2,1)S(1)}, u32[]{:S(2)}, u32[]{:S(2)}) collective-permute-start(bf16[512,256]{1,0:T(8,128)(2,1)S(1)} %get-tuple-element.22), channel_id=1, source_target_pairs={{0,3},{1,2},{2,1},{3,0},{4,7},{5,6},{6,5},{7,4},{8,11},{9,10},{10,... | collective-permute-start | bytes 786440 | tf_op jit(solution)/shard_map/ppermute | solution.py:333
Sparse Core Ops, SparseCore 0:
  20.1 50.2 all-gather.2

commit v3 on v2

v3 whole, which is shorter than its diff:
```python
import functools
import math

import jax
import jax.numpy as jnp
import ml_dtypes
import numpy as np
from jax import lax
from jax.experimental import pallas as pl
from jax.experimental.pallas import tpu as pltpu
from jax.sharding import PartitionSpec as P

NBIN = 1024
HALF = 64
ROUNDS = 4
LAGS = 2048
LANES = 128
TILES = NBIN // LANES
CHUNKS = 4
BF = jnp.bfloat16
F32 = jnp.float32


def make_table(rows, transform):
    phase = (np.arange(rows)[:, None] * np.arange(NBIN)[None, :]) % transform
    angle = phase * (2.0 * math.pi / transform)
    return np.concatenate([np.cos(angle), -np.sin(angle)], axis=1).astype(ml_dtypes.bfloat16)


def band_matrix():
    source = lax.broadcasted_iota(jnp.int32, (3 * LANES, LANES), 0) - LANES
    target = lax.broadcasted_iota(jnp.int32, (3 * LANES, LANES), 1)
    return jnp.where(jnp.abs(source - target) <= HALF, 1.0, 0.0).astype(BF)


def inverse_count(block, length):
    position = lax.broadcasted_iota(jnp.int32, (1, LANES), 1) + block * LANES
    counted = jnp.minimum(position, HALF) + jnp.minimum(length - 1 - position, HALF) + 1
    return 1.0 / counted.astype(F32)


def make_placing(stations, quarter, parts):
    width = stations * quarter
    place = np.zeros((parts, 2 * width, 2 * stations * stations), np.float32)
    for part in range(parts):
        for second in range(2):
            for s in range(stations):
                for t in range(quarter):
                    row = second * width + s * quarter + t
                    column = (second * stations + s) * stations + part * quarter + t
                    place[part, row, column] = 1.0
    return place.astype(ml_dtypes.bfloat16)


def lane_cycle(values):
    period = len(values)
    phase = lax.broadcasted_iota(jnp.int32, (1, LANES), 1) % period
    out = jnp.full((1, LANES), values[-1], F32)
    for index in range(period - 1):
        out = jnp.where(phase == index, values[index], out)
    return out


def even_lanes(shape):
    return lax.broadcasted_iota(jnp.int32, shape, 1) % 2 == 0


def eighth_turn():
    turns = [math.pi * k / 4.0 for k in range(8)]
    return lane_cycle([math.cos(t) for t in turns]), lane_cycle([math.sin(t) for t in turns])


def quarter_turns(real, imag, even, sign_real, sign_imag):
    return sign_real * jnp.where(even, real, imag), sign_imag * jnp.where(even, imag, real)


def banded_sum(stack, values, band):
    rows, length = values.shape
    blocks = length // LANES
    zero = jnp.zeros((rows, LANES), BF)
    for j in range(blocks):
        at = pl.ds(j * rows, rows)
        for k in range(3):
            b = j + k - 1
            block = values[:, b * LANES : (b + 1) * LANES] if 0 <= b < blocks else zero
            stack[at, k * LANES : (k + 1) * LANES] = block
    total = jnp.dot(stack[: blocks * rows, :], band, preferred_element_type=F32)
    return [total[j * rows : (j + 1) * rows, :] for j in range(blocks)]


def prep_kernel(parts, records_hbm, table_hbm, white, mine, *rest):
    others = rest[: parts - 2]
    records, table, stack, flat, spread, sems = rest[parts - 2 :]
    records_copy = pltpu.make_async_copy(records_hbm, records, sems.at[0])
    records_copy.start()
    copy = pltpu.make_async_copy(table_hbm, table, sems.at[1])
    copy.start()
    band_values = band_matrix()
    records_copy.wait()
    stations, windows, length = records.shape
    rows = stations * windows
    chunk = length // CHUNKS
    signal = jnp.concatenate([records[:, w, :] for w in range(windows)], axis=0)
    sums = banded_sum(stack, jnp.abs(signal).astype(BF), band_values)
    for j, total in enumerate(sums):
        at = slice(j * LANES, (j + 1) * LANES)
        level = total * inverse_count(j, length)
        value = (signal[:, at] / (level + 1e-05)).astype(BF)
        q, inside = divmod(j * LANES, chunk)
        flat[q * rows : (q + 1) * rows, inside : inside + LANES] = value
    copy.wait()
    product = jnp.dot(flat[...], table[...], preferred_element_type=F32)
    even = even_lanes((rows, LANES))
    sign_real = lane_cycle([1.0, 1.0, -1.0, -1.0])
    sign_imag = lane_cycle([1.0, -1.0, -1.0, 1.0])
    cosine, sine = eighth_turn()
    reals, imags, mags = [], [], []
    for j in range(TILES):
        at = slice(j * LANES, (j + 1) * LANES)
        at_imag = slice(NBIN + j * LANES, NBIN + (j + 1) * LANES)
        pr = [product[q * rows : (q + 1) * rows, at] for q in range(CHUNKS)]
        pi = [product[q * rows : (q + 1) * rows, at_imag] for q in range(CHUNKS)]
        turned = [
            quarter_turns(pr[q], pi[q], even, sign_real, sign_imag) for q in range(2, CHUNKS)
        ]
        first_real, first_imag = pr[0] + turned[0][0], pi[0] + turned[0][1]
        odd_real, odd_imag = pr[1] + turned[1][0], pi[1] + turned[1][1]
        real = first_real + (odd_real * cosine + odd_imag * sine)
        imag = first_imag + (odd_imag * cosine - odd_real * sine)
        reals.append(real)
        imags.append(imag)
        mags.append(jnp.sqrt(real * real + imag * imag).astype(BF))
    sums = banded_sum(stack, jnp.concatenate(mags, axis=1), band_values)
    for j, total in enumerate(sums):
        at = slice(j * LANES, (j + 1) * LANES)
        smooth = total * inverse_count(j, NBIN) + 1e-06
        spread[pl.ds(j, rows, stride=2 * TILES), :] = reals[j] / smooth
        spread[pl.ds(TILES + j, rows, stride=2 * TILES), :] = imags[j] / smooth
    me = lax.axis_index("seg")
    quarter = stations // parts
    white[...] = spread[...].reshape(windows, stations, 2 * TILES, LANES).astype(BF)
    for j, out in [(0, mine)] + list(zip(range(2, parts), others)):
        for w in range(windows):
            out[w] = white[w, pl.ds((me ^ j) * quarter, quarter)]


def prepare(records, table, parts):
    stations, windows, length = records.shape
    rows = stations * windows
    quarter = stations // parts
    small = jax.ShapeDtypeStruct((windows, quarter, 2 * TILES, LANES), BF)
    vmem = pl.BlockSpec(memory_space=pltpu.VMEM)
    return pl.pallas_call(
        functools.partial(prep_kernel, parts),
        out_shape=[jax.ShapeDtypeStruct((windows, stations, 2 * TILES, LANES), BF)]
        + [small] * (parts - 1),
        in_specs=[pl.BlockSpec(memory_space=pltpu.HBM)] * 2,
        out_specs=[vmem] * parts,
        scratch_shapes=[
            pltpu.VMEM(records.shape, F32),
            pltpu.VMEM(table.shape, BF),
            pltpu.VMEM((rows * (length // LANES), 3 * LANES), BF),
            pltpu.VMEM((CHUNKS * rows, length // CHUNKS), BF),
            pltpu.VMEM((rows * 2 * TILES, LANES), F32),
            pltpu.SemaphoreType.DMA((2,)),
        ],
        compiler_params=pltpu.CompilerParams(vmem_limit_bytes=24 * 2**20),
        cost_estimate=pl.CostEstimate(
            flops=2 * rows * length * 2 * NBIN, bytes_accessed=3 * 2**20, transcendentals=0
        ),
        name="prep",
    )(records, table)


def ring_place(block, count):
    return jnp.where(block % 2 == 0, block // 2, count - 1 - block // 2)


def partner_steps(plan, count):
    me = lax.axis_index("sta")
    mine = ring_place(me, count)
    steps, keys = [], []
    for number in range(ROUNDS):
        step = (ring_place(plan[number, me], count) - mine + count) % count
        steps.append(step)
        keys.append(jnp.minimum(step, count - step) * ROUNDS + number)
    ranks = []
    for number in range(ROUNDS):
        rank = jnp.int32(0)
        for other in range(ROUNDS):
            if other != number:
                rank = rank + jnp.where(keys[other] < keys[number], 1, 0)
        ranks.append(rank)
    return steps, ranks


def cross_kernel(first_slot, slots, count, scaling, offsets, parts, plan, table, *rest):
    owns = rest[:parts]
    candidates = rest[parts : parts + len(offsets)]
    rest = rest[parts + len(offsets) :]
    outs = rest[:parts]
    own, other, crossed, operand, result = rest[parts:]
    windows, stations = owns[0].shape[:2]
    all_windows = windows * parts
    quarter = candidates[0].shape[1]
    width = stations * quarter
    columns = slots * width
    steps, ranks = partner_steps(plan, count)

    for j in range(parts):

        def widen_own(w, carry, j=j):
            raw = owns[j][w].astype(F32)
            real, imag = raw[:, :TILES], raw[:, TILES:]
            own[0, j * windows + w] = real + imag
            own[1, j * windows + w] = real
            own[2, j * windows + w] = imag
            return carry

        lax.fori_loop(0, windows, widen_own, 0)
    for slot in range(slots):
        step = jnp.int32(0)
        for number in range(ROUNDS):
            step = jnp.where(ranks[number] == first_slot + slot, steps[number], step)
        for (offset, start), candidate in zip(offsets, candidates):

            @pl.when(step == offset)
            def _(candidate=candidate, slot=slot, start=start):
                def widen_other(w, carry):
                    raw = candidate[w].astype(F32)
                    real, imag = raw[:, :TILES], raw[:, TILES:]
                    other[0, slot, start + w] = real
                    other[1, slot, start + w] = real + imag
                    other[2, slot, start + w] = imag - real
                    return carry

                lax.fori_loop(0, candidate.shape[0], widen_other, 0)

    group = 4
    groups = stations // group
    first_bin = (lax.broadcasted_iota(jnp.int32, (TILES, LANES), 0) == 0) & (
        lax.broadcasted_iota(jnp.int32, (TILES, LANES), 1) == 0
    )
    weight = jnp.where(first_bin, 1.0, 2.0).astype(F32)

    def one_group(index, carry):
        slot = index // groups
        first = (index % groups) * group

        def sums(kind):
            totals = [None] * (group * quarter)
            for w in range(all_windows):
                left = [own[kind, w, first + s] for s in range(group)]
                right = [other[kind, slot, w, t] for t in range(quarter)]
                for s in range(group):
                    for t in range(quarter):
                        term = left[s] * right[t]
                        place = s * quarter + t
                        totals[place] = term if w == 0 else totals[place] + term
            return totals

        base = slot * width + first * quarter
        shared = sums(0)
        third = sums(2)
        for place in range(group * quarter):
            at = pl.multiple_of((base + place) * 2 * TILES, 2 * TILES)
            crossed[pl.ds(at, TILES), :] = (shared[place] + third[place]) * weight
        second = sums(1)
        for place in range(group * quarter):
            at = pl.multiple_of((base + place) * 2 * TILES + TILES, TILES)
            crossed[pl.ds(at, TILES), :] = (shared[place] - second[place]) * weight
        return carry

    lax.fori_loop(0, slots * groups, one_group, 0)

    even = even_lanes((columns, LANES))
    sign_real = lane_cycle([1.0, -1.0, -1.0, 1.0])
    sign_imag = lane_cycle([1.0, 1.0, -1.0, -1.0])
    cosine, sine = eighth_turn()
    for j in range(TILES):
        at = slice(j * LANES, (j + 1) * LANES)
        at_imag = slice(NBIN + j * LANES, NBIN + (j + 1) * LANES)
        real = crossed[pl.ds(j, columns, stride=2 * TILES), :]
        imag = crossed[pl.ds(TILES + j, columns, stride=2 * TILES), :]
        turned = [(real, imag), (real * cosine - imag * sine, imag * cosine + real * sine)]
        turned += [quarter_turns(r, i, even, sign_real, sign_imag) for r, i in turned]
        for q in range(CHUNKS):
            rows = slice(q * columns, (q + 1) * columns)
            operand[rows, at] = turned[q][0].astype(BF)
            operand[rows, at_imag] = turned[q][1].astype(BF)
    block = lax.dot_general(
        table[...], operand[...], (((1,), (1,)), ((), ())), preferred_element_type=F32
    )
    block = block * scaling
    if slots == 1:
        half = table.shape[0] // 2
        low_lanes = lax.broadcasted_iota(jnp.int32, (half, LANES), 1) < width
        for p in range(CHUNKS // 2):
            at = slice(p * LANES, (p + 1) * LANES)
            low, high = block[:half, at], block[half:, at]
            pair = (
                jnp.where(low_lanes, low, pltpu.roll(high, width, 1)),
                jnp.where(low_lanes, pltpu.roll(low, width, 1), high),
            )
            for second in range(2):
                result[2 * p + second] = pair[second].astype(BF)
    else:
        for q in range(CHUNKS):
            result[q] = block[:, q * columns : (q + 1) * columns].astype(BF)
    me = lax.axis_index("seg")
    for j in range(parts):
        outs[j][...] = result[me ^ j]


def cross_lags(plan, table, owns, offsets, candidates, first_slot, slots, count, scaling):
    parts = len(owns)
    windows, stations = owns[0].shape[:2]
    all_windows = windows * parts
    quarter = candidates[0].shape[1]
    columns = slots * stations * quarter
    share = LAGS // parts
    out = (share, columns) if slots > 1 else (share // 2, 2 * columns)
    smem = pl.BlockSpec(memory_space=pltpu.SMEM)
    vmem = pl.BlockSpec(memory_space=pltpu.VMEM)
    return pl.pallas_call(
        functools.partial(
            cross_kernel, first_slot, slots, count, scaling, tuple(offsets), parts
        ),
        out_shape=[jax.ShapeDtypeStruct(out, BF)] * parts,
        in_specs=[smem] + [vmem] * (1 + parts + len(candidates)),
        out_specs=[vmem] * parts,
        scratch_shapes=[
            pltpu.VMEM((3, all_windows, stations, TILES, LANES), F32),
            pltpu.VMEM((3, slots, all_windows, quarter, TILES, LANES), F32),
            pltpu.VMEM((columns * 2 * TILES, LANES), F32),
            pltpu.VMEM((CHUNKS * columns, 2 * NBIN), BF),
            pltpu.VMEM((parts,) + out, BF),
        ],
        compiler_params=pltpu.CompilerParams(vmem_limit_bytes=24 * 2**20),
        cost_estimate=pl.CostEstimate(
            flops=2 * LAGS * 2 * NBIN * columns * 4, bytes_accessed=2 * 2**20, transcendentals=0
        ),
        name="cross",
    )(plan, table, *owns, *candidates)


def place_kernel(count, parts, groups, plan, place, *rest):
    pieces = rest[: parts * len(groups)]
    out, result = rest[parts * len(groups) :]
    pairs = out.shape[3]
    me = lax.axis_index("seg")
    _, ranks = partner_steps(plan, count)
    matrix = jnp.concatenate([place[me ^ j] for j in range(parts)], axis=0)
    for index, (first_slot, slots) in enumerate(groups):
        joined = jnp.concatenate(
            [piece[...].reshape(-1, LANES) for piece in pieces[index * parts : (index + 1) * parts]],
            axis=1,
        )
        block = jnp.dot(joined, matrix, preferred_element_type=F32)
        half = out.shape[1]
        if slots == 1:
            result[first_slot, 0] = block[:, :pairs]
            result[first_slot, 1] = block[:, pairs:]
        else:
            for slot in range(2):
                for h in range(2):
                    result[first_slot + slot, h] = block[
                        h * half : (h + 1) * half, slot * pairs : (slot + 1) * pairs
                    ]
    for number in range(ROUNDS):
        for h in range(2):
            out[h, :, number, :] = result[ranks[number], h]


def place_lags(plan, groups, pieces, count, stations, parts):
    pairs = stations * stations
    share = LAGS // parts
    half = share // 2
    steps = 4
    rows = half // steps
    place = make_placing(stations, stations // parts, parts)
    blocks, specs = [], []
    for index, (_, slots) in enumerate(groups):
        for piece in pieces[index * parts : (index + 1) * parts]:
            if slots == 1:
                blocks.append(piece)
                specs.append(pl.BlockSpec((rows, LANES), lambda i: (i, 0)))
            else:
                blocks.append(piece.reshape(2, half, LANES))
                specs.append(pl.BlockSpec((2, rows, LANES), lambda i: (0, i, 0)))
    out = pl.pallas_call(
        functools.partial(place_kernel, count, parts, tuple(groups)),
        out_shape=jax.ShapeDtypeStruct((2, half, ROUNDS, pairs), F32),
        grid=(steps,),
        in_specs=[
            pl.BlockSpec(memory_space=pltpu.SMEM),
            pl.BlockSpec(place.shape, lambda i: (0, 0, 0)),
        ]
        + specs,
        out_specs=pl.BlockSpec((2, rows, ROUNDS, pairs), lambda i: (0, i, 0, 0)),
        scratch_shapes=[pltpu.VMEM((ROUNDS, 2, rows, pairs), F32)],
        compiler_params=pltpu.CompilerParams(vmem_limit_bytes=24 * 2**20),
        cost_estimate=pl.CostEstimate(
            flops=2 * share * 4 * pairs * ROUNDS * pairs, bytes_accessed=4 * 2**20, transcendentals=0
        ),
        name="place",
    )(plan, place, *blocks)
    return out.reshape(share, ROUNDS, pairs)


def swap(value, j):
    parts = lax.axis_size("seg")
    return lax.ppermute(value, "seg", [(i, i ^ j) for i in range(parts)])


def exchange(pieces):
    return [pieces[0]] + [swap(pieces[j], j) for j in range(1, len(pieces))]


def per_device(records, plan):
    stations, windows, length = records.shape
    count = lax.axis_size("sta")
    parts = lax.axis_size("seg")
    quarter = stations // parts
    table = jnp.asarray(make_table(length // CHUNKS, 2 * length))
    scaling = 1.0 / math.sqrt(4.0 * NBIN * windows * parts)

    white, mine, *far = prepare(records, table, parts)
    sibling = swap(white, 1)
    first = lax.axis_index("seg") * quarter
    near = jnp.concatenate([mine, lax.dynamic_slice_in_dim(sibling, first, quarter, 1)])
    far = jnp.concatenate([swap(piece, 2 + j) for j, piece in enumerate(far)])
    far, white_far = lax.optimization_barrier((far, white))
    across = swap(white_far, 2)

    ring = sorted(range(count), key=lambda b: b // 2 if b % 2 == 0 else count - 1 - b // 2)
    upward = [(ring[i], ring[(i + 1) % count]) for i in range(count)]
    downward = [(ring[i], ring[i - 1]) for i in range(count)]

    def up(value):
        return lax.ppermute(value, "sta", upward)

    def down(value):
        return lax.ppermute(value, "sta", downward)

    spots, blocks = [], []
    near_up = near_down = near
    far_up = far_down = far
    steps = (count - 1) // 2
    for step in range(1, steps + 1):
        near_up, near_down = up(near_up), down(near_down)
        if step == min(3, steps):
            far_up, far_down, across = lax.optimization_barrier((far_up, far_down, across))
        far_up, far_down = up(far_up), down(far_down)
        spots += [(count - step, 0), (step, 0), (count - step, 2 * windows), (step, 2 * windows)]
        blocks += [near_up, near_down, far_up, far_down]
    owns = [white, sibling, across, swap(across, 1)]
    late_spots, late_blocks = list(spots), list(blocks)
    if count % 2 == 0:
        late_spots += [(count // 2, 0), (count // 2, 2 * windows)]
        late_blocks += [up(near_up), down(far_down)]
    groups = [(0, 2), (2, 2)]
    pieces = []
    for (first_slot, slots), at, values in zip(
        groups, (spots, late_spots), (blocks, late_blocks)
    ):
        lags = cross_lags(plan, table, owns, at, values, first_slot, slots, count, scaling)
        pieces += exchange(lags)
    return place_lags(plan, groups, pieces, count, stations, parts)


def solution(mesh):
    in_specs = (P("sta", "seg", None), P())
    out_specs = P("seg", None, "sta")
    return jax.shard_map(
        per_device, mesh=mesh, in_specs=in_specs, out_specs=out_specs, check_vma=False
    )
```

time: 108 us -> 62.7 us (0.58)
  waiting for transfers between devices: 64.8 us -> 20.4 us
  starting transfers between devices: 7.05 us -> 23.5 us
  between operations: 13.4 us -> 0.1 us
  local copies, waits for them, and re-layouts: 4.74 us -> 2.65 us
  other arithmetic: 1.58 us -> 0.03 us
    all_gather x1 -> x0, waiting for transfers between devices: 36 us -> none  [per_device(): gathered = lax.all_gather(shared, 'sta')]
    ppermute x9 -> x25, starting transfers between devices: 7.04 us -> 23.5 us  [the longest x7 11.7 us: up(): return lax.ppermute(value, 'sta', upward)]
    ppermute x9 -> x25, waiting for transfers between devices: 28.8 us -> 20.4 us  [the longest x11 9.97 us: swap(): return lax.ppermute(value, 'seg', [(i, i ^ j) for i in range(parts)])]
    unnamed x10, local copies, waits for them, and re-layouts: 4.74 us -> 2.64 us
    concatenate x1 -> x2, other arithmetic: 1.58 us -> 0.03 us  [the longest x1 0.02 us: per_device(): jnp.concatenate([mine, lax.dynamic_slice_in_dim(sibling, first, quarter,...]
    pallas_call x3 -> x4, Pallas kernels: 15.7 us -> 15.9 us  [the longest x2 10.2 us: cross_lags(): pl.pallas_call(functools.partial(cross_kernel, first_slot, slots, count,...]
  transfers between devices with their start and end apart: 10 -> 25, of which waited for: 7 -> 10; matrix products, arithmetic and copies ran while one was open for 0% -> 0% of each run, Pallas kernels for 0% -> 16%
where the time goes in v3:
time: 62.7 us; the launch traced here: 62.6 us
  starting transfers between devices  23.5 us (37%)
  waiting for transfers between devices  20.4 us (33%)
  Pallas kernels  15.9 us (25%)
  local copies, waits for them, and re-layouts  2.65 us (4%)
    ppermute x7, starting transfers between devices, up(): return lax.ppermute(value, 'sta', upward)  11.7 us
    pallas_call x2, Pallas kernels, cross_lags(): pl.pallas_call(functools.partial(cross_kernel, first_slot, slots, count,...  10.2 us
    ppermute x11, waiting for transfers between devices, swap(): return lax.ppermute(value, 'seg', [(i, i ^ j) for i in range(parts)])  9.97 us
    ppermute x11, starting transfers between devices, swap(): return lax.ppermute(value, 'seg', [(i, i ^ j) for i in range(parts)])  7.95 us
    ppermute x7, waiting for transfers between devices, up(): return lax.ppermute(value, 'sta', upward)  5.96 us
    ppermute x7, waiting for transfers between devices, down(): return lax.ppermute(value, 'sta', downward)  4.46 us
    ppermute x7, starting transfers between devices, down(): return lax.ppermute(value, 'sta', downward)  3.84 us
    pallas_call x1, Pallas kernels, place_lags(): pl.pallas_call(functools.partial(place_kernel, count, parts, tuple(groups...  3.76 us
  transfers between devices with their start and end apart: 25, of which 10 were waited for; matrix products, arithmetic and copies ran while one was open for 0% of the time, Pallas kernels for 16%

profile of v3, /device:TPU:0, one launch (start us, length us, event | category | flops | bytes accessed | tf_op | source)
XLA Modules:
  0.0 62.6 jit_solution(15389751031947427072)
XLA Ops:
  0.0 1.6 %copy-done = bf16[512,2048]{1,0:T(8,128)(2,1)S(1)} copy-done((bf16[512,2048]{1,0:T(8,128)(2,1)S(1)}, bf16[512,2048]{1,0:T(8,128)(2,1)}, u32[]{:S(2)}) %copy-start) | copy-done | bytes 2097176
  1.6 1.0 %copy-done.2 = f32[16,4,2048]{2,1,0:T(4,128)S(1)} copy-done((f32[16,4,2048]{2,1,0:T(4,128)S(1)}, f32[16,4,2048]{2,1,0:T(4,128)}, u32[]{:S(2)}) %copy-start.2) | copy-done | bytes 524312
  2.6 2.0 %prep.1 = (bf16[4,16,16,128]{3,2,1,0:T(8,128)(2,1)S(1)}, bf16[4,4,16,128]{3,2,1,0:T(8,128)(2,1)S(1)}, bf16[4,4,16,128]{3,2,1,0:T(8,128)(2,1)S(1)}, bf16[4,4,16,128]{3,2,1,0:T(8,128)(2,1)S(1)}) custom-call(f32[16,4,2048]{2,1,0:T(4,128)S(1)} %copy-done.2, bf16[512,2048]{1,0:T(8,128)(2,1)S(1)} %copy-done), custom_call_target="tpu_custom_call" | custom-call | flops 536870912 | bytes 3145728 | tf_op jit(solution)/shard_map/prep/pallas_call | solution.py:153
  4.6 3.0 %collective-permute-start.1 = (bf16[4,4,16,128]{3,2,1,0:T(8,128)(2,1)S(1)}, bf16[4,4,16,128]{3,2,1,0:T(8,128)(2,1)S(1)}, u32[]{:S(2)}, u32[]{:S(2)}) collective-permute-start(bf16[4,4,16,128]{3,2,1,0:T(8,128)(2,1)S(1)} %get-tuple-element.23), channel_id=1, source_target_pairs={{0,2},{1,3},{2,0},{3,1},{4,6},{5,7},{6,4},{7,5},{8,10},{9,11},{10,... | collective-permute-start | bytes 196616 | tf_op jit(solution)/shard_map/ppermute | solution.py:413
  7.8 2.1 %collective-permute-done.1 = bf16[4,4,16,128]{3,2,1,0:T(8,128)(2,1)S(1)} collective-permute-done((bf16[4,4,16,128]{3,2,1,0:T(8,128)(2,1)S(1)}, bf16[4,4,16,128]{3,2,1,0:T(8,128)(2,1)S(1)}, u32[]{:S(2)}, u32[]{:S(2)}) %collective-permute-start.1) | collective-permute-done | bytes 65568 | tf_op jit(solution)/shard_map/ppermute | solution.py:413
  9.9 1.9 %collective-permute-done.2 = bf16[4,4,16,128]{3,2,1,0:T(8,128)(2,1)S(1)} collective-permute-done((bf16[4,4,16,128]{3,2,1,0:T(8,128)(2,1)S(1)}, bf16[4,4,16,128]{3,2,1,0:T(8,128)(2,1)S(1)}, u32[]{:S(2)}, u32[]{:S(2)}) %collective-permute-start.2) | collective-permute-done | bytes 65568 | tf_op jit(solution)/shard_map/ppermute | solution.py:413
  11.8 1.7 %collective-permute-start.3 = (bf16[8,4,16,128]{3,2,1,0:T(8,128)(2,1)S(1)}, bf16[8,4,16,128]{3,2,1,0:T(8,128)(2,1)S(1)}, u32[]{:S(2)}, u32[]{:S(2)}) collective-permute-start(bf16[8,4,16,128]{3,2,1,0:T(8,128)(2,1)S(1)} %pad_maximum_fusion), channel_id=1, source_target_pairs={{0,8},{8,16},{16,24},{24,28},{28,20},{20,12},{12,4},{4,0},{1,9},{9... | collective-permute-start | bytes 393224 | tf_op jit(solution)/shard_map/ppermute | solution.py:441
  13.4 0.4 collective-permute-start.5
  13.8 0.4 collective-permute-start.7
  14.3 2.8 %collective-permute-done.3.rest_6_ = bf16[8,4,16,128]{3,2,1,0:T(8,128)(2,1)S(1)} collective-permute-done((bf16[8,4,16,128]{3,2,1,0:T(8,128)(2,1)S(1)}, bf16[8,4,16,128]{3,2,1,0:T(8,128)(2,1)S(1)}, u32[]{:S(2)}, u32[]{:S(2)}) %collective-permute-start.3) | collective-permute-done | bytes 131104 | tf_op jit(solution)/shard_map/ppermute | solution.py:441
  17.1 1.7 %collective-permute-start.4 = (bf16[8,4,16,128]{3,2,1,0:T(8,128)(2,1)S(1)}, bf16[8,4,16,128]{3,2,1,0:T(8,128)(2,1)S(1)}, u32[]{:S(2)}, u32[]{:S(2)}) collective-permute-start(bf16[8,4,16,128]{3,2,1,0:T(8,128)(2,1)S(1)} %collective-permute-done.3.rest_6_), channel_id=1, source_target_pairs={{0,8},{8,16},{16,24},{24,28},{28,20},{20,12},{12,4},{4,0},{1,9},{9... | collective-permute-start | bytes 393224 | tf_op jit(solution)/shard_map/ppermute | solution.py:441
  19.1 1.7 %collective-permute-start.9 = (bf16[8,4,16,128]{3,2,1,0:T(8,128)(2,1)S(1)}, bf16[8,4,16,128]{3,2,1,0:T(8,128)(2,1)S(1)}, u32[]{:S(2)}, u32[]{:S(2)}) collective-permute-start(bf16[8,4,16,128]{3,2,1,0:T(8,128)(2,1)S(1)} %pad_maximum_fusion.1), channel_id=1, source_target_pairs={{0,8},{8,16},{16,24},{24,28},{28,20},{20,12},{12,4},{4,0},{1,9},{9... | collective-permute-start | bytes 393224 | tf_op jit(solution)/shard_map/ppermute | solution.py:441
  21.2 1.8 %collective-permute-done.4.rest_10_ = bf16[8,4,16,128]{3,2,1,0:T(8,128)(2,1)S(1)} collective-permute-done((bf16[8,4,16,128]{3,2,1,0:T(8,128)(2,1)S(1)}, bf16[8,4,16,128]{3,2,1,0:T(8,128)(2,1)S(1)}, u32[]{:S(2)}, u32[]{:S(2)}) %collective-permute-start.4) | collective-permute-done | bytes 131104 | tf_op jit(solution)/shard_map/ppermute | solution.py:441
  23.0 1.4 %collective-permute-done.6.rest_11_ = bf16[8,4,16,128]{3,2,1,0:T(8,128)(2,1)S(1)} collective-permute-done((bf16[8,4,16,128]{3,2,1,0:T(8,128)(2,1)S(1)}, bf16[8,4,16,128]{3,2,1,0:T(8,128)(2,1)S(1)}, u32[]{:S(2)}, u32[]{:S(2)}) %collective-permute-start.6) | collective-permute-done | bytes 131104 | tf_op jit(solution)/shard_map/ppermute | solution.py:444
  24.5 1.7 %collective-permute-start.11 = (bf16[8,4,16,128]{3,2,1,0:T(8,128)(2,1)S(1)}, bf16[8,4,16,128]{3,2,1,0:T(8,128)(2,1)S(1)}, u32[]{:S(2)}, u32[]{:S(2)}) collective-permute-start(bf16[8,4,16,128]{3,2,1,0:T(8,128)(2,1)S(1)} %collective-permute-done.9.rest_4_), channel_id=1, source_target_pairs={{0,8},{8,16},{16,24},{24,28},{28,20},{20,12},{12,4},{4,0},{1,9},{9... | collective-permute-start | bytes 393224 | tf_op jit(solution)/shard_map/ppermute | solution.py:441
  26.2 0.4 collective-permute-start.12
  26.5 1.6 %collective-permute-start.16 = (bf16[8,4,16,128]{3,2,1,0:T(8,128)(2,1)S(1)}, bf16[8,4,16,128]{3,2,1,0:T(8,128)(2,1)S(1)}, u32[]{:S(2)}, u32[]{:S(2)}) collective-permute-start(bf16[8,4,16,128]{3,2,1,0:T(8,128)(2,1)S(1)} %collective-permute-done.6.rest_11_), channel_id=1, source_target_pairs={{0,4},{8,0},{16,8},{24,16},{28,24},{20,28},{12,20},{4,12},{1,5},{9... | collective-permute-start | bytes 393224 | tf_op jit(solution)/shard_map/ppermute | solution.py:444
  28.2 1.3 %collective-permute-done.11.rest_8_ = bf16[8,4,16,128]{3,2,1,0:T(8,128)(2,1)S(1)} collective-permute-done((bf16[8,4,16,128]{3,2,1,0:T(8,128)(2,1)S(1)}, bf16[8,4,16,128]{3,2,1,0:T(8,128)(2,1)S(1)}, u32[]{:S(2)}, u32[]{:S(2)}) %collective-permute-start.11) | collective-permute-done | bytes 131104 | tf_op jit(solution)/shard_map/ppermute | solution.py:441
  29.5 1.7 %collective-permute-start.13 = (bf16[8,4,16,128]{3,2,1,0:T(8,128)(2,1)S(1)}, bf16[8,4,16,128]{3,2,1,0:T(8,128)(2,1)S(1)}, u32[]{:S(2)}, u32[]{:S(2)}) collective-permute-start(bf16[8,4,16,128]{3,2,1,0:T(8,128)(2,1)S(1)} %collective-permute-done.11.rest_8_), channel_id=1, source_target_pairs={{0,8},{8,16},{16,24},{24,28},{28,20},{20,12},{12,4},{4,0},{1,9},{9... | collective-permute-start | bytes 393224 | tf_op jit(solution)/shard_map/ppermute | solution.py:441
  31.1 1.6 %collective-permute-start.15 = (bf16[8,4,16,128]{3,2,1,0:T(8,128)(2,1)S(1)}, bf16[8,4,16,128]{3,2,1,0:T(8,128)(2,1)S(1)}, u32[]{:S(2)}, u32[]{:S(2)}) collective-permute-start(bf16[8,4,16,128]{3,2,1,0:T(8,128)(2,1)S(1)} %collective-permute-done.4.rest_10_), channel_id=1, source_target_pairs={{0,8},{8,16},{16,24},{24,28},{28,20},{20,12},{12,4},{4,0},{1,9},{9... | collective-permute-start | bytes 393224 | tf_op jit(solution)/shard_map/ppermute | solution.py:441
  32.7 0.4 collective-permute-start.14
  33.2 2.1 %collective-permute-done.16.rest_15_ = bf16[8,4,16,128]{3,2,1,0:T(8,128)(2,1)S(1)} collective-permute-done((bf16[8,4,16,128]{3,2,1,0:T(8,128)(2,1)S(1)}, bf16[8,4,16,128]{3,2,1,0:T(8,128)(2,1)S(1)}, u32[]{:S(2)}, u32[]{:S(2)}) %collective-permute-start.16) | collective-permute-done | bytes 131104 | tf_op jit(solution)/shard_map/ppermute | solution.py:444
  35.3 0.3 collective-permute-start.21
  35.6 1.7 %collective-permute-start.20 = (bf16[8,4,16,128]{3,2,1,0:T(8,128)(2,1)S(1)}, bf16[8,4,16,128]{3,2,1,0:T(8,128)(2,1)S(1)}, u32[]{:S(2)}, u32[]{:S(2)}) collective-permute-start(bf16[8,4,16,128]{3,2,1,0:T(8,128)(2,1)S(1)} %collective-permute-done.13.rest_12_), channel_id=1, source_target_pairs={{0,8},{8,16},{16,24},{24,28},{28,20},{20,12},{12,4},{4,0},{1,9},{9... | collective-permute-start | bytes 393224 | tf_op jit(solution)/shard_map/ppermute | solution.py:441
  37.3 0.9 %collective-permute-done.14.rest_13_ = bf16[8,4,16,128]{3,2,1,0:T(8,128)(2,1)S(1)} collective-permute-done((bf16[8,4,16,128]{3,2,1,0:T(8,128)(2,1)S(1)}, bf16[8,4,16,128]{3,2,1,0:T(8,128)(2,1)S(1)}, u32[]{:S(2)}, u32[]{:S(2)}) %collective-permute-start.14) | collective-permute-done | bytes 131104 | tf_op jit(solution)/shard_map/ppermute | solution.py:444
  38.2 5.1 %cross.2 = (bf16[512,128]{1,0:T(8,128)(2,1)S(1)}, bf16[512,128]{1,0:T(8,128)(2,1)S(1)}, bf16[512,128]{1,0:T(8,128)(2,1)S(1)}, bf16[512,128]{1,0:T(8,128)(2,1)S(1)}) custom-call(s32[4,8]{1,0:T(4,128)S(1)} %copy-done.3, bf16[512,2048]{1,0:T(8,128)(2,1)S(1)} %copy-done.1, bf16[4,16,16,128]{3,2,1,0:T(8,128)(2,1)S(1)} %get-tuple-element.26.rest_0_, ...), custom_call_target="tpu_custom_call" | custom-call | flops 4294967296 | bytes 2097152 | tf_op jit(solution)/shard_map/cross/pallas_call | solution.py:325
  43.4 2.0 %collective-permute-start.18 = (bf16[512,128]{1,0:T(8,128)(2,1)S(1)}, bf16[512,128]{1,0:T(8,128)(2,1)S(1)}, u32[]{:S(2)}, u32[]{:S(2)}) collective-permute-start(bf16[512,128]{1,0:T(8,128)(2,1)S(1)} %get-tuple-element.33), channel_id=1, source_target_pairs={{0,2},{1,3},{2,0},{3,1},{4,6},{5,7},{6,4},{7,5},{8,10},{9,11},{10,... | collective-permute-start | bytes 393224 | tf_op jit(solution)/shard_map/ppermute | solution.py:413
  45.4 5.1 %cross.3 = (bf16[512,128]{1,0:T(8,128)(2,1)S(1)}, bf16[512,128]{1,0:T(8,128)(2,1)S(1)}, bf16[512,128]{1,0:T(8,128)(2,1)S(1)}, bf16[512,128]{1,0:T(8,128)(2,1)S(1)}) custom-call(s32[4,8]{1,0:T(4,128)S(1)} %copy-done.3, bf16[512,2048]{1,0:T(8,128)(2,1)S(1)} %copy-done.1, bf16[4,16,16,128]{3,2,1,0:T(8,128)(2,1)S(1)} %get-tuple-element.26.rest_0_, ...), custom_call_target="tpu_custom_call" | custom-call | flops 4294967296 | bytes 2097152 | tf_op jit(solution)/shard_map/cross/pallas_call | solution.py:325
  50.8 2.0 %collective-permute-start.23 = (bf16[512,128]{1,0:T(8,128)(2,1)S(1)}, bf16[512,128]{1,0:T(8,128)(2,1)S(1)}, u32[]{:S(2)}, u32[]{:S(2)}) collective-permute-start(bf16[512,128]{1,0:T(8,128)(2,1)S(1)} %get-tuple-element.37), channel_id=1, source_target_pairs={{0,2},{1,3},{2,0},{3,1},{4,6},{5,7},{6,4},{7,5},{8,10},{9,11},{10,... | collective-permute-start | bytes 393224 | tf_op jit(solution)/shard_map/ppermute | solution.py:413
  52.8 4.3 %collective-permute-done.23 = bf16[512,128]{1,0:T(8,128)(2,1)S(1)} collective-permute-done((bf16[512,128]{1,0:T(8,128)(2,1)S(1)}, bf16[512,128]{1,0:T(8,128)(2,1)S(1)}, u32[]{:S(2)}, u32[]{:S(2)}) %collective-permute-start.23) | collective-permute-done | bytes 131104 | tf_op jit(solution)/shard_map/ppermute | solution.py:413
  57.1 1.7 %collective-permute-done.24 = bf16[512,128]{1,0:T(8,128)(2,1)S(1)} collective-permute-done((bf16[512,128]{1,0:T(8,128)(2,1)S(1)}, bf16[512,128]{1,0:T(8,128)(2,1)S(1)}, u32[]{:S(2)}, u32[]{:S(2)}) %collective-permute-start.24) | collective-permute-done | bytes 131104 | tf_op jit(solution)/shard_map/ppermute | solution.py:413
  58.8 3.8 %place.2 = f32[2,256,4,256]{3,2,1,0:T(4,128)} custom-call(s32[4,8]{1,0:T(4,128)S(1)} %copy-done.3, bf16[4,128,512]{2,1,0:T(8,128)(2,1)S(1)} %copy-done.4, bf16[2,256,128]{2,1,0:T(8,128)(2,1)S(1)} %bitcast.15, bf16[2,256,128]{2,1,0:T(8,128)(2,1)S(1)} %bitcast.9, bf16[2,256,128]{2,1,0:T(8,128)(2,1)S(1)} %bitcast.10, bf16[2,256,128]{2,1,0:T(8,128)(2,1)S(1)} %bitcast.11, ...), custom_call_target="tpu_custom_call" | custom-call | flops 1073741824 | bytes 4194304 | tf_op jit(solution)/shard_map/place/pallas_call | solution.py:391
  (35 shorter events, 1.3 us)
Async XLA Ops:
  0.0 1.6 %copy-start = (bf16[512,2048]{1,0:T(8,128)(2,1)S(1)}, bf16[512,2048]{1,0:T(8,128)(2,1)}, u32[]{:S(2)}) copy-start(bf16[512,2048]{1,0:T(8,128)(2,1)} %constant.14.clone.table_hbm.table) | copy-start | bytes 6291460
  1.6 1.0 %copy-start.2 = (f32[16,4,2048]{2,1,0:T(4,128)S(1)}, f32[16,4,2048]{2,1,0:T(4,128)}, u32[]{:S(2)}) copy-start(f32[16,4,2048]{2,1,0:T(4,128)} %records_hbm.1) | copy-start | bytes 1572868
  2.6 35.6 %copy-start.1 = (bf16[512,2048]{1,0:T(8,128)(2,1)S(1)}, bf16[512,2048]{1,0:T(8,128)(2,1)}, u32[]{:S(2)}) copy-start(bf16[512,2048]{1,0:T(8,128)(2,1)} %constant.14.clone.table_hbm.table) | copy-start | bytes 6291460
  2.6 35.6 %copy-start.3 = (s32[4,8]{1,0:T(4,128)S(1)}, s32[4,8]{1,0:T(4,128)}, u32[]{:S(2)}) copy-start(s32[4,8]{1,0:T(4,128)} %plan.5) | copy-start | bytes 388
  4.6 5.3 %collective-permute-start.1 = (bf16[4,4,16,128]{3,2,1,0:T(8,128)(2,1)S(1)}, bf16[4,4,16,128]{3,2,1,0:T(8,128)(2,1)S(1)}, u32[]{:S(2)}, u32[]{:S(2)}) collective-permute-start(bf16[4,4,16,128]{3,2,1,0:T(8,128)(2,1)S(1)} %get-tuple-element.23), channel_id=1, source_target_pairs={{0,2},{1,3},{2,0},{3,1},{4,6},{5,7},{6,4},{7,5},{8,10},{9,11},{10,... | collective-permute-start | bytes 196616 | tf_op jit(solution)/shard_map/ppermute | solution.py:413
  7.6 4.1 %collective-permute-start.2 = (bf16[4,4,16,128]{3,2,1,0:T(8,128)(2,1)S(1)}, bf16[4,4,16,128]{3,2,1,0:T(8,128)(2,1)S(1)}, u32[]{:S(2)}, u32[]{:S(2)}) collective-permute-start(bf16[4,4,16,128]{3,2,1,0:T(8,128)(2,1)S(1)} %get-tuple-element.24), channel_id=1, source_target_pairs={{0,3},{1,2},{2,1},{3,0},{4,7},{5,6},{6,5},{7,4},{8,11},{9,10},{10,... | collective-permute-start | bytes 196616 | tf_op jit(solution)/shard_map/ppermute | solution.py:413
  7.6 11.5 %collective-permute-start = (bf16[4,16,16,128]{3,2,1,0:T(8,128)(2,1)S(1)}, bf16[4,16,16,128]{3,2,1,0:T(8,128)(2,1)S(1)}, u32[]{:S(2)}, u32[]{:S(2)}) collective-permute-start(bf16[4,16,16,128]{3,2,1,0:T(8,128)(2,1)S(1)} %get-tuple-element.26.rest_0_), channel_id=1, source_target_pairs={{0,1},{1,0},{2,3},{3,2},{4,5},{5,4},{6,7},{7,6},{8,9},{9,8},{10,11... | collective-permute-start | bytes 786440 | tf_op jit(solution)/shard_map/ppermute | solution.py:413
  11.8 5.3 %collective-permute-start.3 = (bf16[8,4,16,128]{3,2,1,0:T(8,128)(2,1)S(1)}, bf16[8,4,16,128]{3,2,1,0:T(8,128)(2,1)S(1)}, u32[]{:S(2)}, u32[]{:S(2)}) collective-permute-start(bf16[8,4,16,128]{3,2,1,0:T(8,128)(2,1)S(1)} %pad_maximum_fusion), channel_id=1, source_target_pairs={{0,8},{8,16},{16,24},{24,28},{28,20},{20,12},{12,4},{4,0},{1,9},{9... | collective-permute-start | bytes 393224 | tf_op jit(solution)/shard_map/ppermute | solution.py:441
  13.4 5.3 %collective-permute-start.5 = (bf16[8,4,16,128]{3,2,1,0:T(8,128)(2,1)S(1)}, bf16[8,4,16,128]{3,2,1,0:T(8,128)(2,1)S(1)}, u32[]{:S(2)}, u32[]{:S(2)}) collective-permute-start(bf16[8,4,16,128]{3,2,1,0:T(8,128)(2,1)S(1)} %pad_maximum_fusion), channel_id=1, source_target_pairs={{0,4},{8,0},{16,8},{24,16},{28,24},{20,28},{12,20},{4,12},{1,5},{9... | collective-permute-start | bytes 393224 | tf_op jit(solution)/shard_map/ppermute | solution.py:444
  13.8 10.6 %collective-permute-start.7 = (bf16[4,16,16,128]{3,2,1,0:T(8,128)(2,1)S(1)}, bf16[4,16,16,128]{3,2,1,0:T(8,128)(2,1)S(1)}, u32[]{:S(2)}, u32[]{:S(2)}) collective-permute-start(bf16[4,16,16,128]{3,2,1,0:T(8,128)(2,1)S(1)} %get-tuple-element.26.rest_0_), channel_id=1, source_target_pairs={{0,2},{1,3},{2,0},{3,1},{4,6},{5,7},{6,4},{7,5},{8,10},{9,11},{10,... | collective-permute-start | bytes 786440 | tf_op jit(solution)/shard_map/ppermute | solution.py:413
  17.1 6.0 %collective-permute-start.4 = (bf16[8,4,16,128]{3,2,1,0:T(8,128)(2,1)S(1)}, bf16[8,4,16,128]{3,2,1,0:T(8,128)(2,1)S(1)}, u32[]{:S(2)}, u32[]{:S(2)}) collective-permute-start(bf16[8,4,16,128]{3,2,1,0:T(8,128)(2,1)S(1)} %collective-permute-done.3.rest_6_), channel_id=1, source_target_pairs={{0,8},{8,16},{16,24},{24,28},{28,20},{20,12},{12,4},{4,0},{1,9},{9... | collective-permute-start | bytes 393224 | tf_op jit(solution)/shard_map/ppermute | solution.py:441
  18.8 5.7 %collective-permute-start.6 = (bf16[8,4,16,128]{3,2,1,0:T(8,128)(2,1)S(1)}, bf16[8,4,16,128]{3,2,1,0:T(8,128)(2,1)S(1)}, u32[]{:S(2)}, u32[]{:S(2)}) collective-permute-start(bf16[8,4,16,128]{3,2,1,0:T(8,128)(2,1)S(1)} %collective-permute-done.5.rest_7_), channel_id=1, source_target_pairs={{0,4},{8,0},{16,8},{24,16},{28,24},{20,28},{12,20},{4,12},{1,5},{9... | collective-permute-start | bytes 393224 | tf_op jit(solution)/shard_map/ppermute | solution.py:444
  19.1 5.4 %collective-permute-start.9 = (bf16[8,4,16,128]{3,2,1,0:T(8,128)(2,1)S(1)}, bf16[8,4,16,128]{3,2,1,0:T(8,128)(2,1)S(1)}, u32[]{:S(2)}, u32[]{:S(2)}) collective-permute-start(bf16[8,4,16,128]{3,2,1,0:T(8,128)(2,1)S(1)} %pad_maximum_fusion.1), channel_id=1, source_target_pairs={{0,8},{8,16},{16,24},{24,28},{28,20},{20,12},{12,4},{4,0},{1,9},{9... | collective-permute-start | bytes 393224 | tf_op jit(solution)/shard_map/ppermute | solution.py:441
  20.9 5.3 %collective-permute-start.10 = (bf16[8,4,16,128]{3,2,1,0:T(8,128)(2,1)S(1)}, bf16[8,4,16,128]{3,2,1,0:T(8,128)(2,1)S(1)}, u32[]{:S(2)}, u32[]{:S(2)}) collective-permute-start(bf16[8,4,16,128]{3,2,1,0:T(8,128)(2,1)S(1)} %pad_maximum_fusion.1), channel_id=1, source_target_pairs={{0,4},{8,0},{16,8},{24,16},{28,24},{20,28},{12,20},{4,12},{1,5},{9... | collective-permute-start | bytes 393224 | tf_op jit(solution)/shard_map/ppermute | solution.py:444
  24.5 5.0 %collective-permute-start.11 = (bf16[8,4,16,128]{3,2,1,0:T(8,128)(2,1)S(1)}, bf16[8,4,16,128]{3,2,1,0:T(8,128)(2,1)S(1)}, u32[]{:S(2)}, u32[]{:S(2)}) collective-permute-start(bf16[8,4,16,128]{3,2,1,0:T(8,128)(2,1)S(1)} %collective-permute-done.9.rest_4_), channel_id=1, source_target_pairs={{0,8},{8,16},{16,24},{24,28},{28,20},{20,12},{12,4},{4,0},{1,9},{9... | collective-permute-start | bytes 393224 | tf_op jit(solution)/shard_map/ppermute | solution.py:441
  26.2 11.1 %collective-permute-start.8 = (bf16[4,16,16,128]{3,2,1,0:T(8,128)(2,1)S(1)}, bf16[4,16,16,128]{3,2,1,0:T(8,128)(2,1)S(1)}, u32[]{:S(2)}, u32[]{:S(2)}) collective-permute-start(bf16[4,16,16,128]{3,2,1,0:T(8,128)(2,1)S(1)} %collective-permute-done.7.rest_2_), channel_id=1, source_target_pairs={{0,1},{1,0},{2,3},{3,2},{4,5},{5,4},{6,7},{7,6},{8,9},{9,8},{10,11... | collective-permute-start | bytes 786440 | tf_op jit(solution)/shard_map/ppermute | solution.py:413
  26.2 6.5 %collective-permute-start.12 = (bf16[8,4,16,128]{3,2,1,0:T(8,128)(2,1)S(1)}, bf16[8,4,16,128]{3,2,1,0:T(8,128)(2,1)S(1)}, u32[]{:S(2)}, u32[]{:S(2)}) collective-permute-start(bf16[8,4,16,128]{3,2,1,0:T(8,128)(2,1)S(1)} %collective-permute-done.10.rest_5_), channel_id=1, source_target_pairs={{0,4},{8,0},{16,8},{24,16},{28,24},{20,28},{12,20},{4,12},{1,5},{9... | collective-permute-start | bytes 393224 | tf_op jit(solution)/shard_map/ppermute | solution.py:444
  26.5 8.8 %collective-permute-start.16 = (bf16[8,4,16,128]{3,2,1,0:T(8,128)(2,1)S(1)}, bf16[8,4,16,128]{3,2,1,0:T(8,128)(2,1)S(1)}, u32[]{:S(2)}, u32[]{:S(2)}) collective-permute-start(bf16[8,4,16,128]{3,2,1,0:T(8,128)(2,1)S(1)} %collective-permute-done.6.rest_11_), channel_id=1, source_target_pairs={{0,4},{8,0},{16,8},{24,16},{28,24},{20,28},{12,20},{4,12},{1,5},{9... | collective-permute-start | bytes 393224 | tf_op jit(solution)/shard_map/ppermute | solution.py:444
  29.5 6.2 %collective-permute-start.13 = (bf16[8,4,16,128]{3,2,1,0:T(8,128)(2,1)S(1)}, bf16[8,4,16,128]{3,2,1,0:T(8,128)(2,1)S(1)}, u32[]{:S(2)}, u32[]{:S(2)}) collective-permute-start(bf16[8,4,16,128]{3,2,1,0:T(8,128)(2,1)S(1)} %collective-permute-done.11.rest_8_), channel_id=1, source_target_pairs={{0,8},{8,16},{16,24},{24,28},{28,20},{20,12},{12,4},{4,0},{1,9},{9... | collective-permute-start | bytes 393224 | tf_op jit(solution)/shard_map/ppermute | solution.py:441
  31.1 6.2 %collective-permute-start.15 = (bf16[8,4,16,128]{3,2,1,0:T(8,128)(2,1)S(1)}, bf16[8,4,16,128]{3,2,1,0:T(8,128)(2,1)S(1)}, u32[]{:S(2)}, u32[]{:S(2)}) collective-permute-start(bf16[8,4,16,128]{3,2,1,0:T(8,128)(2,1)S(1)} %collective-permute-done.4.rest_10_), channel_id=1, source_target_pairs={{0,8},{8,16},{16,24},{24,28},{28,20},{20,12},{12,4},{4,0},{1,9},{9... | collective-permute-start | bytes 393224 | tf_op jit(solution)/shard_map/ppermute | solution.py:441
  32.7 5.5 %collective-permute-start.14 = (bf16[8,4,16,128]{3,2,1,0:T(8,128)(2,1)S(1)}, bf16[8,4,16,128]{3,2,1,0:T(8,128)(2,1)S(1)}, u32[]{:S(2)}, u32[]{:S(2)}) collective-permute-start(bf16[8,4,16,128]{3,2,1,0:T(8,128)(2,1)S(1)} %collective-permute-done.12.rest_9_), channel_id=1, source_target_pairs={{0,4},{8,0},{16,8},{24,16},{28,24},{20,28},{12,20},{4,12},{1,5},{9... | collective-permute-start | bytes 393224 | tf_op jit(solution)/shard_map/ppermute | solution.py:444
  35.3 10.1 %collective-permute-start.21 = (bf16[8,4,16,128]{3,2,1,0:T(8,128)(2,1)S(1)}, bf16[8,4,16,128]{3,2,1,0:T(8,128)(2,1)S(1)}, u32[]{:S(2)}, u32[]{:S(2)}) collective-permute-start(bf16[8,4,16,128]{3,2,1,0:T(8,128)(2,1)S(1)} %collective-permute-done.16.rest_15_), channel_id=1, source_target_pairs={{0,4},{8,0},{16,8},{24,16},{28,24},{20,28},{12,20},{4,12},{1,5},{9... | collective-permute-start | bytes 393224 | tf_op jit(solution)/shard_map/ppermute | solution.py:444
  35.6 9.8 %collective-permute-start.20 = (bf16[8,4,16,128]{3,2,1,0:T(8,128)(2,1)S(1)}, bf16[8,4,16,128]{3,2,1,0:T(8,128)(2,1)S(1)}, u32[]{:S(2)}, u32[]{:S(2)}) collective-permute-start(bf16[8,4,16,128]{3,2,1,0:T(8,128)(2,1)S(1)} %collective-permute-done.13.rest_12_), channel_id=1, source_target_pairs={{0,8},{8,16},{16,24},{24,28},{28,20},{20,12},{12,4},{4,0},{1,9},{9... | collective-permute-start | bytes 393224 | tf_op jit(solution)/shard_map/ppermute | solution.py:441
  43.3 9.5 %collective-permute-start.17 = (bf16[512,128]{1,0:T(8,128)(2,1)S(1)}, bf16[512,128]{1,0:T(8,128)(2,1)S(1)}, u32[]{:S(2)}, u32[]{:S(2)}) collective-permute-start(bf16[512,128]{1,0:T(8,128)(2,1)S(1)} %get-tuple-element.32), channel_id=1, source_target_pairs={{0,1},{1,0},{2,3},{3,2},{4,5},{5,4},{6,7},{7,6},{8,9},{9,8},{10,11... | collective-permute-start | bytes 393224 | tf_op jit(solution)/shard_map/ppermute | solution.py:413
  43.4 9.4 %collective-permute-start.18 = (bf16[512,128]{1,0:T(8,128)(2,1)S(1)}, bf16[512,128]{1,0:T(8,128)(2,1)S(1)}, u32[]{:S(2)}, u32[]{:S(2)}) collective-permute-start(bf16[512,128]{1,0:T(8,128)(2,1)S(1)} %get-tuple-element.33), channel_id=1, source_target_pairs={{0,2},{1,3},{2,0},{3,1},{4,6},{5,7},{6,4},{7,5},{8,10},{9,11},{10,... | collective-permute-start | bytes 393224 | tf_op jit(solution)/shard_map/ppermute | solution.py:413
  45.4 13.5 %copy-start.4 = (bf16[4,128,512]{2,1,0:T(8,128)(2,1)S(1)}, bf16[4,128,512]{2,1,0:T(8,128)(2,1)}, u32[]{:S(2)}) copy-start(bf16[4,128,512]{2,1,0:T(8,128)(2,1)} %constant.15.clone.place) | copy-start | bytes 1572868
  45.4 7.4 %collective-permute-start.19 = (bf16[512,128]{1,0:T(8,128)(2,1)S(1)}, bf16[512,128]{1,0:T(8,128)(2,1)S(1)}, u32[]{:S(2)}, u32[]{:S(2)}) collective-permute-start(bf16[512,128]{1,0:T(8,128)(2,1)S(1)} %get-tuple-element.34), channel_id=1, source_target_pairs={{0,3},{1,2},{2,1},{3,0},{4,7},{5,6},{6,5},{7,4},{8,11},{9,10},{10,... | collective-permute-start | bytes 393224 | tf_op jit(solution)/shard_map/ppermute | solution.py:413
  50.5 2.2 %collective-permute-start.22 = (bf16[512,128]{1,0:T(8,128)(2,1)S(1)}, bf16[512,128]{1,0:T(8,128)(2,1)S(1)}, u32[]{:S(2)}, u32[]{:S(2)}) collective-permute-start(bf16[512,128]{1,0:T(8,128)(2,1)S(1)} %get-tuple-element.36), channel_id=1, source_target_pairs={{0,1},{1,0},{2,3},{3,2},{4,5},{5,4},{6,7},{7,6},{8,9},{9,8},{10,11... | collective-permute-start | bytes 393224 | tf_op jit(solution)/shard_map/ppermute | solution.py:413
  50.8 6.3 %collective-permute-start.23 = (bf16[512,128]{1,0:T(8,128)(2,1)S(1)}, bf16[512,128]{1,0:T(8,128)(2,1)S(1)}, u32[]{:S(2)}, u32[]{:S(2)}) collective-permute-start(bf16[512,128]{1,0:T(8,128)(2,1)S(1)} %get-tuple-element.37), channel_id=1, source_target_pairs={{0,2},{1,3},{2,0},{3,1},{4,6},{5,7},{6,4},{7,5},{8,10},{9,11},{10,... | collective-permute-start | bytes 393224 | tf_op jit(solution)/shard_map/ppermute | solution.py:413
  52.8 6.1 %collective-permute-start.24 = (bf16[512,128]{1,0:T(8,128)(2,1)S(1)}, bf16[512,128]{1,0:T(8,128)(2,1)S(1)}, u32[]{:S(2)}, u32[]{:S(2)}) collective-permute-start(bf16[512,128]{1,0:T(8,128)(2,1)S(1)} %get-tuple-element.38), channel_id=1, source_target_pairs={{0,3},{1,2},{2,1},{3,0},{4,7},{5,6},{6,5},{7,4},{8,11},{9,10},{10,... | collective-permute-start | bytes 393224 | tf_op jit(solution)/shard_map/ppermute | solution.py:413

commit v4 on v3

--- a/solution.py
+++ b/solution.py
@@ -164,7 +164,7 @@
             pltpu.VMEM((rows * 2 * TILES, LANES), F32),
             pltpu.SemaphoreType.DMA((2,)),
         ],
-        compiler_params=pltpu.CompilerParams(vmem_limit_bytes=24 * 2**20),
+        compiler_params=pltpu.CompilerParams(vmem_limit_bytes=58 * 2**20),
         cost_estimate=pl.CostEstimate(
             flops=2 * rows * length * 2 * NBIN, bytes_accessed=3 * 2**20, transcendentals=0
         ),
@@ -344,67 +344,74 @@
     )(plan, table, *owns, *candidates)
 
 
-def place_kernel(count, parts, groups, plan, place, *rest):
+def place_kernel(count, parts, groups, steps, plan, place, *rest):
     pieces = rest[: parts * len(groups)]
-    out, result = rest[parts * len(groups) :]
+    out_hbm, out, sems = rest[parts * len(groups) :]
     pairs = out.shape[3]
+    half = out.shape[1]
+    rows = half // steps
     me = lax.axis_index("seg")
     _, ranks = partner_steps(plan, count)
+    round_of = []
+    for slot in range(ROUNDS):
+        number = jnp.int32(0)
+        for other in range(1, ROUNDS):
+            number = jnp.where(ranks[other] == slot, other, number)
+        round_of.append(number)
     matrix = jnp.concatenate([place[me ^ j] for j in range(parts)], axis=0)
-    for index, (first_slot, slots) in enumerate(groups):
-        joined = jnp.concatenate(
-            [piece[...].reshape(-1, LANES) for piece in pieces[index * parts : (index + 1) * parts]],
-            axis=1,
-        )
-        block = jnp.dot(joined, matrix, preferred_element_type=F32)
-        half = out.shape[1]
-        if slots == 1:
-            result[first_slot, 0] = block[:, :pairs]
-            result[first_slot, 1] = block[:, pairs:]
-        else:
-            for slot in range(2):
-                for h in range(2):
-                    result[first_slot + slot, h] = block[
-                        h * half : (h + 1) * half, slot * pairs : (slot + 1) * pairs
-                    ]
-    for number in range(ROUNDS):
+    copies = []
+    for step in range(steps):
+        at = slice(step * rows, (step + 1) * rows)
+        for index, (first_slot, slots) in enumerate(groups):
+            own = pieces[index * parts : (index + 1) * parts]
+            lows = [piece[at, :] for piece in own]
+            if slots == 1:
+                joined = jnp.concatenate(lows, axis=1)
+            else:
+                later = slice(half + step * rows, half + (step + 1) * rows)
+                highs = [piece[later, :] for piece in own]
+                joined = jnp.concatenate(
+                    [jnp.concatenate(lows, axis=1), jnp.concatenate(highs, axis=1)], axis=0
+                )
+            block = jnp.dot(joined, matrix, preferred_element_type=F32)
+            if slots == 1:
+                out[0, at, round_of[first_slot], :] = block[:, :pairs]
+                out[1, at, round_of[first_slot], :] = block[:, pairs:]
+            else:
+                for slot in range(2):
+                    columns = slice(slot * pairs, (slot + 1) * pairs)
+                    out[0, at, round_of[first_slot + slot], :] = block[:rows, columns]
+                    out[1, at, round_of[first_slot + slot], :] = block[rows:, columns]
         for h in range(2):
-            out[h, :, number, :] = result[ranks[number], h]
+            copy = pltpu.make_async_copy(
+                out.at[h, at], out_hbm.at[h, at], sems.at[2 * step + h]
+            )
+            copy.start()
+            copies.append(copy)
+    for copy in copies:
+        copy.wait()
 
 
 def place_lags(plan, groups, pieces, count, stations, parts):
     pairs = stations * stations
     share = LAGS // parts
     half = share // 2
-    steps = 4
-    rows = half // steps
+    steps = 2
     place = make_placing(stations, stations // parts, parts)
-    blocks, specs = [], []
-    for index, (_, slots) in enumerate(groups):
-        for piece in pieces[index * parts : (index + 1) * parts]:
-            if slots == 1:
-                blocks.append(piece)
-                specs.append(pl.BlockSpec((rows, LANES), lambda i: (i, 0)))
-            else:
-                blocks.append(piece.reshape(2, half, LANES))
-                specs.append(pl.BlockSpec((2, rows, LANES), lambda i: (0, i, 0)))
+    vmem = pl.BlockSpec(memory_space=pltpu.VMEM)
+    shape = (2, half, ROUNDS, pairs)
     out = pl.pallas_call(
-        functools.partial(place_kernel, count, parts, tuple(groups)),
-        out_shape=jax.ShapeDtypeStruct((2, half, ROUNDS, pairs), F32),
-        grid=(steps,),
-        in_specs=[
-            pl.BlockSpec(memory_space=pltpu.SMEM),
-            pl.BlockSpec(place.shape, lambda i: (0, 0, 0)),
-        ]
-        + specs,
-        out_specs=pl.BlockSpec((2, rows, ROUNDS, pairs), lambda i: (0, i, 0, 0)),
-        scratch_shapes=[pltpu.VMEM((ROUNDS, 2, rows, pairs), F32)],
+        functools.partial(place_kernel, count, parts, tuple(groups), steps),
+        out_shape=jax.ShapeDtypeStruct(shape, F32),
+        in_specs=[pl.BlockSpec(memory_space=pltpu.SMEM)] + [vmem] * (1 + len(pieces)),
+        out_specs=pl.BlockSpec(memory_space=pl.ANY),
+        scratch_shapes=[pltpu.VMEM(shape, F32), pltpu.SemaphoreType.DMA((2 * steps,))],
         compiler_params=pltpu.CompilerParams(vmem_limit_bytes=24 * 2**20),
         cost_estimate=pl.CostEstimate(
             flops=2 * share * 4 * pairs * ROUNDS * pairs, bytes_accessed=4 * 2**20, transcendentals=0
         ),
         name="place",
-    )(plan, place, *blocks)
+    )(plan, place, *pieces)
     return out.reshape(share, ROUNDS, pairs)
 
 
@@ -448,17 +455,33 @@
     far_up = far_down = far
     steps = (count - 1) // 2
     for step in range(1, steps + 1):
-        near_up, near_down = up(near_up), down(near_down)
-        if step == min(3, steps):
-            far_up, far_down, across = lax.optimization_barrier((far_up, far_down, across))
+        if step == 2:
+            near_up, near_down = lax.optimization_barrier((near_up, near_down))
+        elif step > 2:
+            near_up, near_down, last_up, last_down = lax.optimization_barrier(
+                (near_up, near_down, last_up, last_down)
+            )
+        last_up, last_down = far_up, far_down
+        next_near = up(near_up), down(near_down)
+        if step == 3:
+            far_up, far_down, near_up, near_down, across = lax.optimization_barrier(
+                (far_up, far_down, near_up, near_down, across)
+            )
+        elif step > 1:
+            far_up, far_down, near_up, near_down = lax.optimization_barrier(
+                (far_up, far_down, near_up, near_down)
+            )
         far_up, far_down = up(far_up), down(far_down)
+        near_up, near_down = next_near
         spots += [(count - step, 0), (step, 0), (count - step, 2 * windows), (step, 2 * windows)]
         blocks += [near_up, near_down, far_up, far_down]
     owns = [white, sibling, across, swap(across, 1)]
     late_spots, late_blocks = list(spots), list(blocks)
     if count % 2 == 0:
         late_spots += [(count // 2, 0), (count // 2, 2 * windows)]
-        late_blocks += [up(near_up), down(far_down)]
+        middle_up = up(near_up)
+        far_down, near_up, near_down = lax.optimization_barrier((far_down, near_up, near_down))
+        late_blocks += [middle_up, down(far_down)]
     groups = [(0, 2), (2, 2)]
     pieces = []
     for (first_slot, slots), at, values in zip(

time: 62.7 us -> 60.6 us (0.967)
  local copies, waits for them, and re-layouts: 2.65 us -> 0.96 us
  waiting for transfers between devices: 20.4 us -> 19.2 us
  starting transfers between devices: 23.5 us -> 22.6 us
  other arithmetic: 0.03 us -> 0.87 us
  Pallas kernels: 15.9 us -> 16.6 us
    ppermute x7, waiting for transfers between devices: 4.46 us -> 8.4 us  [down(): return lax.ppermute(value, 'sta', downward)]
    ppermute x11, waiting for transfers between devices: 9.97 us -> 7.4 us  [swap(): return lax.ppermute(value, 'seg', [(i, i ^ j) for i in range(parts)])]
    ppermute x7, waiting for transfers between devices: 5.96 us -> 3.43 us  [up(): return lax.ppermute(value, 'sta', upward)]
    pallas_call x1, Pallas kernels: 1.97 us -> 3.89 us  [prepare(): pl.pallas_call(functools.partial(prep_kernel, parts), out_shape=[jax.Shap...]
    unnamed x10 -> x8, local copies, waits for them, and re-layouts: 2.64 us -> 0.96 us
    pallas_call x1, Pallas kernels: 3.76 us -> 2.52 us  [place_lags(): pl.pallas_call(functools.partial(place_kernel, count, parts, tuple(groups...]
    ppermute x7, starting transfers between devices: 11.7 us -> 10.9 us  [up(): return lax.ppermute(value, 'sta', upward)]
    concatenate x1, other arithmetic: 0.02 us -> 0.85 us  [per_device(): jnp.concatenate([mine, lax.dynamic_slice_in_dim(sibling, first, quarter,...]
  transfers between devices with their start and end apart: 25 -> 25, of which waited for: 10 -> 11; matrix products, arithmetic and copies ran while one was open for 0% -> 1% of each run, Pallas kernels for 16% -> 17%
where the time goes in v4:
time: 60.6 us; the launch traced here: 60.3 us
  starting transfers between devices  22.6 us (37%)
  waiting for transfers between devices  19.2 us (32%)
  Pallas kernels  16.6 us (27%)
  local copies, waits for them, and re-layouts  0.96 us (2%)
  other arithmetic  0.87 us (1%)
    ppermute x7, starting transfers between devices, up(): return lax.ppermute(value, 'sta', upward)  10.9 us
    pallas_call x2, Pallas kernels, cross_lags(): pl.pallas_call(functools.partial(cross_kernel, first_slot, slots, count,...  10.1 us
    ppermute x7, waiting for transfers between devices, down(): return lax.ppermute(value, 'sta', downward)  8.4 us
    ppermute x11, starting transfers between devices, swap(): return lax.ppermute(value, 'seg', [(i, i ^ j) for i in range(parts)])  8.26 us
    ppermute x11, waiting for transfers between devices, swap(): return lax.ppermute(value, 'seg', [(i, i ^ j) for i in range(parts)])  7.4 us
    pallas_call x1, Pallas kernels, prepare(): pl.pallas_call(functools.partial(prep_kernel, parts), out_shape=[jax.Shap...  3.89 us
    ppermute x7, waiting for transfers between devices, up(): return lax.ppermute(value, 'sta', upward)  3.43 us
    ppermute x7, starting transfers between devices, down(): return lax.ppermute(value, 'sta', downward)  3.43 us
  transfers between devices with their start and end apart: 25, of which 11 were waited for; matrix products, arithmetic and copies ran while one was open for 1% of the time, Pallas kernels for 17%

profile of v4, /device:TPU:0, one launch (start us, length us, event | category | flops | bytes accessed | tf_op | source)
XLA Modules:
  0.0 60.3 jit_solution(15131114586883197216)
XLA Ops:
  0.0 3.9 %prep.1 = (bf16[4,16,16,128]{3,2,1,0:T(8,128)(2,1)}, bf16[4,4,16,128]{3,2,1,0:T(8,128)(2,1)}, bf16[4,4,16,128]{3,2,1,0:T(8,128)(2,1)}, bf16[4,4,16,128]{3,2,1,0:T(8,128)(2,1)}) custom-call(f32[16,4,2048]{2,1,0:T(4,128)} %records_hbm.1, bf16[512,2048]{1,0:T(8,128)(2,1)} %constant.14.clone.table_hbm.table), custom_call_target="tpu_custom_call" | custom-call | flops 536870912 | bytes 3145728 | tf_op jit(solution)/shard_map/prep/pallas_call | solution.py:153
  3.9 0.5 collective-permute-start
  4.4 2.6 %collective-permute-start.1 = (bf16[4,4,16,128]{3,2,1,0:T(8,128)(2,1)}, bf16[4,4,16,128]{3,2,1,0:T(8,128)(2,1)S(1)}, u32[]{:S(2)}, u32[]{:S(2)}) collective-permute-start(bf16[4,4,16,128]{3,2,1,0:T(8,128)(2,1)} %get-tuple-element.30), channel_id=1, source_target_pairs={{0,2},{1,3},{2,0},{3,1},{4,6},{5,7},{6,4},{7,5},{8,10},{9,11},{10,... | collective-permute-start | bytes 196616 | tf_op jit(solution)/shard_map/ppermute | solution.py:420
  7.1 0.9 %pad_maximum_fusion.1 = bf16[8,4,16,128]{3,2,1,0:T(8,128)(2,1)S(1)} fusion(bf16[4,4,16,128]{3,2,1,0:T(8,128)(2,1)S(1)} %constant_dynamic-slice_fusion, bf16[4,4,16,128]{3,2,1,0:T(8,128)(2,1)} %get-tuple-element.33), kind=kLoop, calls=%fused_computation.1 | loop fusion | flops 65536 | bytes 262144 | tf_op jit(solution)/shard_map/concatenate | solution.py:438
  7.9 1.9 %collective-permute-start.5 = (bf16[8,4,16,128]{3,2,1,0:T(8,128)(2,1)S(1)}, bf16[8,4,16,128]{3,2,1,0:T(8,128)(2,1)S(1)}, u32[]{:S(2)}, u32[]{:S(2)}) collective-permute-start(bf16[8,4,16,128]{3,2,1,0:T(8,128)(2,1)S(1)} %pad_maximum_fusion.1), channel_id=1, source_target_pairs={{0,8},{8,16},{16,24},{24,28},{28,20},{20,12},{12,4},{4,0},{1,9},{9... | collective-permute-start | bytes 393224 | tf_op jit(solution)/shard_map/ppermute | solution.py:448
  10.0 1.3 %collective-permute-done.2 = bf16[4,4,16,128]{3,2,1,0:T(8,128)(2,1)S(1)} collective-permute-done((bf16[4,4,16,128]{3,2,1,0:T(8,128)(2,1)}, bf16[4,4,16,128]{3,2,1,0:T(8,128)(2,1)S(1)}, u32[]{:S(2)}, u32[]{:S(2)}) %collective-permute-start.2) | collective-permute-done | bytes 65568 | tf_op jit(solution)/shard_map/ppermute | solution.py:420
  11.4 1.6 %collective-permute-start.3 = (bf16[8,4,16,128]{3,2,1,0:T(8,128)(2,1)S(1)}, bf16[8,4,16,128]{3,2,1,0:T(8,128)(2,1)S(1)}, u32[]{:S(2)}, u32[]{:S(2)}) collective-permute-start(bf16[8,4,16,128]{3,2,1,0:T(8,128)(2,1)S(1)} %pad_maximum_fusion), channel_id=1, source_target_pairs={{0,8},{8,16},{16,24},{24,28},{28,20},{20,12},{12,4},{4,0},{1,9},{9... | collective-permute-start | bytes 393224 | tf_op jit(solution)/shard_map/ppermute | solution.py:448
  13.0 0.5 collective-permute-start.4
  13.4 1.2 %collective-permute-start.11 = (bf16[4,16,16,128]{3,2,1,0:T(8,128)(2,1)}, bf16[4,16,16,128]{3,2,1,0:T(8,128)(2,1)S(1)}, u32[]{:S(2)}, u32[]{:S(2)}) collective-permute-start(bf16[4,16,16,128]{3,2,1,0:T(8,128)(2,1)} %get-tuple-element.40.rest_0_), channel_id=1, source_target_pairs={{0,2},{1,3},{2,0},{3,1},{4,6},{5,7},{6,4},{7,5},{8,10},{9,11},{10,... | collective-permute-start | bytes 786440 | tf_op jit(solution)/shard_map/ppermute | solution.py:420
  14.7 0.6 collective-permute-done.6.rest_5_
  15.3 1.0 %collective-permute-start.10 = (bf16[8,4,16,128]{3,2,1,0:T(8,128)(2,1)S(1)}, bf16[8,4,16,128]{3,2,1,0:T(8,128)(2,1)S(1)}, u32[]{:S(2)}, u32[]{:S(2)}) collective-permute-start(bf16[8,4,16,128]{3,2,1,0:T(8,128)(2,1)S(1)} %collective-permute-done.6.rest_5_), channel_id=1, source_target_pairs={{0,4},{8,0},{16,8},{24,16},{28,24},{20,28},{12,20},{4,12},{1,5},{9... | collective-permute-start | bytes 393224 | tf_op jit(solution)/shard_map/ppermute | solution.py:451
  16.2 1.1 %collective-permute-start.9 = (bf16[8,4,16,128]{3,2,1,0:T(8,128)(2,1)S(1)}, bf16[8,4,16,128]{3,2,1,0:T(8,128)(2,1)S(1)}, u32[]{:S(2)}, u32[]{:S(2)}) collective-permute-start(bf16[8,4,16,128]{3,2,1,0:T(8,128)(2,1)S(1)} %collective-permute-done.5.rest_4_), channel_id=1, source_target_pairs={{0,8},{8,16},{16,24},{24,28},{28,20},{20,12},{12,4},{4,0},{1,9},{9... | collective-permute-start | bytes 393224 | tf_op jit(solution)/shard_map/ppermute | solution.py:448
  17.3 2.1 %collective-permute-done.4.rest_7_ = bf16[8,4,16,128]{3,2,1,0:T(8,128)(2,1)S(1)} collective-permute-done((bf16[8,4,16,128]{3,2,1,0:T(8,128)(2,1)S(1)}, bf16[8,4,16,128]{3,2,1,0:T(8,128)(2,1)S(1)}, u32[]{:S(2)}, u32[]{:S(2)}) %collective-permute-start.4) | collective-permute-done | bytes 131104 | tf_op jit(solution)/shard_map/ppermute | solution.py:451
  19.4 1.6 %collective-permute-start.7 = (bf16[8,4,16,128]{3,2,1,0:T(8,128)(2,1)S(1)}, bf16[8,4,16,128]{3,2,1,0:T(8,128)(2,1)S(1)}, u32[]{:S(2)}, u32[]{:S(2)}) collective-permute-start(bf16[8,4,16,128]{3,2,1,0:T(8,128)(2,1)S(1)} %collective-permute-done.3.rest_6_), channel_id=1, source_target_pairs={{0,8},{8,16},{16,24},{24,28},{28,20},{20,12},{12,4},{4,0},{1,9},{9... | collective-permute-start | bytes 393224 | tf_op jit(solution)/shard_map/ppermute | solution.py:448
  21.4 1.2 %collective-permute-done.9.rest_8_ = bf16[8,4,16,128]{3,2,1,0:T(8,128)(2,1)S(1)} collective-permute-done((bf16[8,4,16,128]{3,2,1,0:T(8,128)(2,1)S(1)}, bf16[8,4,16,128]{3,2,1,0:T(8,128)(2,1)S(1)}, u32[]{:S(2)}, u32[]{:S(2)}) %collective-permute-start.9) | collective-permute-done | bytes 131104 | tf_op jit(solution)/shard_map/ppermute | solution.py:448
  22.6 1.7 %collective-permute-done.7.rest_10_ = bf16[8,4,16,128]{3,2,1,0:T(8,128)(2,1)S(1)} collective-permute-done((bf16[8,4,16,128]{3,2,1,0:T(8,128)(2,1)S(1)}, bf16[8,4,16,128]{3,2,1,0:T(8,128)(2,1)S(1)}, u32[]{:S(2)}, u32[]{:S(2)}) %collective-permute-start.7) | collective-permute-done | bytes 131104 | tf_op jit(solution)/shard_map/ppermute | solution.py:448
  24.3 1.6 %collective-permute-done.8.rest_11_ = bf16[8,4,16,128]{3,2,1,0:T(8,128)(2,1)S(1)} collective-permute-done((bf16[8,4,16,128]{3,2,1,0:T(8,128)(2,1)S(1)}, bf16[8,4,16,128]{3,2,1,0:T(8,128)(2,1)S(1)}, u32[]{:S(2)}, u32[]{:S(2)}) %collective-permute-start.8) | collective-permute-done | bytes 131104 | tf_op jit(solution)/shard_map/ppermute | solution.py:451
  26.4 1.6 %collective-permute-start.13 = (bf16[8,4,16,128]{3,2,1,0:T(8,128)(2,1)S(1)}, bf16[8,4,16,128]{3,2,1,0:T(8,128)(2,1)S(1)}, u32[]{:S(2)}, u32[]{:S(2)}) collective-permute-start(bf16[8,4,16,128]{3,2,1,0:T(8,128)(2,1)S(1)} %collective-permute-done.9.rest_8_), channel_id=1, source_target_pairs={{0,8},{8,16},{16,24},{24,28},{28,20},{20,12},{12,4},{4,0},{1,9},{9... | collective-permute-start | bytes 393224 | tf_op jit(solution)/shard_map/ppermute | solution.py:448
  28.4 1.6 %collective-permute-start.15 = (bf16[8,4,16,128]{3,2,1,0:T(8,128)(2,1)S(1)}, bf16[8,4,16,128]{3,2,1,0:T(8,128)(2,1)S(1)}, u32[]{:S(2)}, u32[]{:S(2)}) collective-permute-start(bf16[8,4,16,128]{3,2,1,0:T(8,128)(2,1)S(1)} %collective-permute-done.7.rest_10_), channel_id=1, source_target_pairs={{0,8},{8,16},{16,24},{24,28},{28,20},{20,12},{12,4},{4,0},{1,9},{9... | collective-permute-start | bytes 393224 | tf_op jit(solution)/shard_map/ppermute | solution.py:448
  30.0 2.2 %collective-permute-done.16.rest_15_ = bf16[8,4,16,128]{3,2,1,0:T(8,128)(2,1)S(1)} collective-permute-done((bf16[8,4,16,128]{3,2,1,0:T(8,128)(2,1)S(1)}, bf16[8,4,16,128]{3,2,1,0:T(8,128)(2,1)S(1)}, u32[]{:S(2)}, u32[]{:S(2)}) %collective-permute-start.16) | collective-permute-done | bytes 131104 | tf_op jit(solution)/shard_map/ppermute | solution.py:451
  32.2 0.5 collective-permute-done.13.rest_12_
  32.7 1.9 %collective-permute-done.14.rest_13_ = bf16[8,4,16,128]{3,2,1,0:T(8,128)(2,1)S(1)} collective-permute-done((bf16[8,4,16,128]{3,2,1,0:T(8,128)(2,1)S(1)}, bf16[8,4,16,128]{3,2,1,0:T(8,128)(2,1)S(1)}, u32[]{:S(2)}, u32[]{:S(2)}) %collective-permute-start.14) | collective-permute-done | bytes 131104 | tf_op jit(solution)/shard_map/ppermute | solution.py:451
  35.1 1.6 %collective-permute-start.20 = (bf16[8,4,16,128]{3,2,1,0:T(8,128)(2,1)S(1)}, bf16[8,4,16,128]{3,2,1,0:T(8,128)(2,1)S(1)}, u32[]{:S(2)}, u32[]{:S(2)}) collective-permute-start(bf16[8,4,16,128]{3,2,1,0:T(8,128)(2,1)S(1)} %collective-permute-done.13.rest_12_), channel_id=1, source_target_pairs={{0,8},{8,16},{16,24},{24,28},{28,20},{20,12},{12,4},{4,0},{1,9},{9... | collective-permute-start | bytes 393224 | tf_op jit(solution)/shard_map/ppermute | solution.py:448
  36.7 0.9 %copy-done.1 = bf16[4,16,16,128]{3,2,1,0:T(8,128)(2,1)S(1)} copy-done((bf16[4,16,16,128]{3,2,1,0:T(8,128)(2,1)S(1)}, bf16[4,16,16,128]{3,2,1,0:T(8,128)(2,1)}, u32[]{:S(2)}) %copy-start.1) | copy-done | bytes 262168
  37.6 5.0 %cross.2 = (bf16[512,128]{1,0:T(8,128)(2,1)S(1)}, bf16[512,128]{1,0:T(8,128)(2,1)S(1)}, bf16[512,128]{1,0:T(8,128)(2,1)S(1)}, bf16[512,128]{1,0:T(8,128)(2,1)S(1)}) custom-call(s32[4,8]{1,0:T(4,128)S(1)} %copy-done.2, bf16[512,2048]{1,0:T(8,128)(2,1)S(1)} %copy-done, bf16[4,16,16,128]{3,2,1,0:T(8,128)(2,1)S(1)} %copy-done.1, ...), custom_call_target="tpu_custom_call" | custom-call | flops 4294967296 | bytes 2097152 | tf_op jit(solution)/shard_map/cross/pallas_call | solution.py:325
  42.8 1.3 %collective-permute-start.18 = (bf16[512,128]{1,0:T(8,128)(2,1)S(1)}, bf16[512,128]{1,0:T(8,128)(2,1)S(1)}, u32[]{:S(2)}, u32[]{:S(2)}) collective-permute-start(bf16[512,128]{1,0:T(8,128)(2,1)S(1)} %get-tuple-element.46), channel_id=1, source_target_pairs={{0,2},{1,3},{2,0},{3,1},{4,6},{5,7},{6,4},{7,5},{8,10},{9,11},{10,... | collective-permute-start | bytes 393224 | tf_op jit(solution)/shard_map/ppermute | solution.py:420
  44.1 0.5 collective-permute-start.19
  44.6 5.1 %cross.3 = (bf16[512,128]{1,0:T(8,128)(2,1)S(1)}, bf16[512,128]{1,0:T(8,128)(2,1)S(1)}, bf16[512,128]{1,0:T(8,128)(2,1)S(1)}, bf16[512,128]{1,0:T(8,128)(2,1)S(1)}) custom-call(s32[4,8]{1,0:T(4,128)S(1)} %copy-done.2, bf16[512,2048]{1,0:T(8,128)(2,1)S(1)} %copy-done, bf16[4,16,16,128]{3,2,1,0:T(8,128)(2,1)S(1)} %copy-done.1, ...), custom_call_target="tpu_custom_call" | custom-call | flops 4294967296 | bytes 2097152 | tf_op jit(solution)/shard_map/cross/pallas_call | solution.py:325
  50.2 1.3 %collective-permute-start.23 = (bf16[512,128]{1,0:T(8,128)(2,1)S(1)}, bf16[512,128]{1,0:T(8,128)(2,1)S(1)}, u32[]{:S(2)}, u32[]{:S(2)}) collective-permute-start(bf16[512,128]{1,0:T(8,128)(2,1)S(1)} %get-tuple-element.51), channel_id=1, source_target_pairs={{0,2},{1,3},{2,0},{3,1},{4,6},{5,7},{6,4},{7,5},{8,10},{9,11},{10,... | collective-permute-start | bytes 393224 | tf_op jit(solution)/shard_map/ppermute | solution.py:420
  51.7 4.8 %collective-permute-done.23.rest_6_ = bf16[512,128]{1,0:T(8,128)(2,1)S(1)} collective-permute-done((bf16[512,128]{1,0:T(8,128)(2,1)S(1)}, bf16[512,128]{1,0:T(8,128)(2,1)S(1)}, u32[]{:S(2)}, u32[]{:S(2)}) %collective-permute-start.23) | collective-permute-done | bytes 131104 | tf_op jit(solution)/shard_map/ppermute | solution.py:420
  56.5 1.2 %collective-permute-done.24.rest_7_ = bf16[512,128]{1,0:T(8,128)(2,1)S(1)} collective-permute-done((bf16[512,128]{1,0:T(8,128)(2,1)S(1)}, bf16[512,128]{1,0:T(8,128)(2,1)S(1)}, u32[]{:S(2)}, u32[]{:S(2)}) %collective-permute-start.24) | collective-permute-done | bytes 131104 | tf_op jit(solution)/shard_map/ppermute | solution.py:420
  57.8 2.5 %place.2 = f32[2,256,4,256]{3,2,1,0:T(4,128)} custom-call(s32[4,8]{1,0:T(4,128)S(1)} %copy-done.2, bf16[4,128,512]{2,1,0:T(8,128)(2,1)S(1)} %copy-done.3, bf16[512,128]{1,0:T(8,128)(2,1)S(1)} %get-tuple-element.44.rest_0_, bf16[512,128]{1,0:T(8,128)(2,1)S(1)} %collective-permute-done.17.rest_1_, bf16[512,128]{1,0:T(8,128)(2,1)S(1)} %collective-permute-done.18.rest_2_, ...), custom_call_target="tpu_custom_call" | custom-call | flops 1073741824 | bytes 4194304 | tf_op jit(solution)/shard_map/place/pallas_call | solution.py:403
  (33 shorter events, 2.8 us)
Async XLA Ops:
  0.0 36.7 %copy-start = (bf16[512,2048]{1,0:T(8,128)(2,1)S(1)}, bf16[512,2048]{1,0:T(8,128)(2,1)}, u32[]{:S(2)}) copy-start(bf16[512,2048]{1,0:T(8,128)(2,1)} %constant.14.clone.table_hbm.table) | copy-start | bytes 6291460
  0.0 36.7 %copy-start.2 = (s32[4,8]{1,0:T(4,128)S(1)}, s32[4,8]{1,0:T(4,128)}, u32[]{:S(2)}) copy-start(s32[4,8]{1,0:T(4,128)} %plan.5) | copy-start | bytes 388
  3.9 3.2 %collective-permute-start = (bf16[4,16,16,128]{3,2,1,0:T(8,128)(2,1)}, bf16[4,16,16,128]{3,2,1,0:T(8,128)(2,1)S(1)}, u32[]{:S(2)}, u32[]{:S(2)}) collective-permute-start(bf16[4,16,16,128]{3,2,1,0:T(8,128)(2,1)} %get-tuple-element.40.rest_0_), channel_id=1, source_target_pairs={{0,1},{1,0},{2,3},{3,2},{4,5},{5,4},{6,7},{7,6},{8,9},{9,8},{10,11... | collective-permute-start | bytes 786440 | tf_op jit(solution)/shard_map/ppermute | solution.py:420
  4.4 5.6 %collective-permute-start.1 = (bf16[4,4,16,128]{3,2,1,0:T(8,128)(2,1)}, bf16[4,4,16,128]{3,2,1,0:T(8,128)(2,1)S(1)}, u32[]{:S(2)}, u32[]{:S(2)}) collective-permute-start(bf16[4,4,16,128]{3,2,1,0:T(8,128)(2,1)} %get-tuple-element.30), channel_id=1, source_target_pairs={{0,2},{1,3},{2,0},{3,1},{4,6},{5,7},{6,4},{7,5},{8,10},{9,11},{10,... | collective-permute-start | bytes 196616 | tf_op jit(solution)/shard_map/ppermute | solution.py:420
  7.0 4.3 %collective-permute-start.2 = (bf16[4,4,16,128]{3,2,1,0:T(8,128)(2,1)}, bf16[4,4,16,128]{3,2,1,0:T(8,128)(2,1)S(1)}, u32[]{:S(2)}, u32[]{:S(2)}) collective-permute-start(bf16[4,4,16,128]{3,2,1,0:T(8,128)(2,1)} %get-tuple-element.31), channel_id=1, source_target_pairs={{0,3},{1,2},{2,1},{3,0},{4,7},{5,6},{6,5},{7,4},{8,11},{9,10},{10,... | collective-permute-start | bytes 196616 | tf_op jit(solution)/shard_map/ppermute | solution.py:420
  7.9 6.8 %collective-permute-start.5 = (bf16[8,4,16,128]{3,2,1,0:T(8,128)(2,1)S(1)}, bf16[8,4,16,128]{3,2,1,0:T(8,128)(2,1)S(1)}, u32[]{:S(2)}, u32[]{:S(2)}) collective-permute-start(bf16[8,4,16,128]{3,2,1,0:T(8,128)(2,1)S(1)} %pad_maximum_fusion.1), channel_id=1, source_target_pairs={{0,8},{8,16},{16,24},{24,28},{28,20},{20,12},{12,4},{4,0},{1,9},{9... | collective-permute-start | bytes 393224 | tf_op jit(solution)/shard_map/ppermute | solution.py:448
  9.8 5.5 %collective-permute-start.6 = (bf16[8,4,16,128]{3,2,1,0:T(8,128)(2,1)S(1)}, bf16[8,4,16,128]{3,2,1,0:T(8,128)(2,1)S(1)}, u32[]{:S(2)}, u32[]{:S(2)}) collective-permute-start(bf16[8,4,16,128]{3,2,1,0:T(8,128)(2,1)S(1)} %pad_maximum_fusion.1), channel_id=1, source_target_pairs={{0,4},{8,0},{16,8},{24,16},{28,24},{20,28},{12,20},{4,12},{1,5},{9... | collective-permute-start | bytes 393224 | tf_op jit(solution)/shard_map/ppermute | solution.py:451
  11.4 5.9 %collective-permute-start.3 = (bf16[8,4,16,128]{3,2,1,0:T(8,128)(2,1)S(1)}, bf16[8,4,16,128]{3,2,1,0:T(8,128)(2,1)S(1)}, u32[]{:S(2)}, u32[]{:S(2)}) collective-permute-start(bf16[8,4,16,128]{3,2,1,0:T(8,128)(2,1)S(1)} %pad_maximum_fusion), channel_id=1, source_target_pairs={{0,8},{8,16},{16,24},{24,28},{28,20},{20,12},{12,4},{4,0},{1,9},{9... | collective-permute-start | bytes 393224 | tf_op jit(solution)/shard_map/ppermute | solution.py:448
  13.0 6.4 %collective-permute-start.4 = (bf16[8,4,16,128]{3,2,1,0:T(8,128)(2,1)S(1)}, bf16[8,4,16,128]{3,2,1,0:T(8,128)(2,1)S(1)}, u32[]{:S(2)}, u32[]{:S(2)}) collective-permute-start(bf16[8,4,16,128]{3,2,1,0:T(8,128)(2,1)S(1)} %pad_maximum_fusion), channel_id=1, source_target_pairs={{0,4},{8,0},{16,8},{24,16},{28,24},{20,28},{12,20},{4,12},{1,5},{9... | collective-permute-start | bytes 393224 | tf_op jit(solution)/shard_map/ppermute | solution.py:451
  13.4 9.1 %collective-permute-start.11 = (bf16[4,16,16,128]{3,2,1,0:T(8,128)(2,1)}, bf16[4,16,16,128]{3,2,1,0:T(8,128)(2,1)S(1)}, u32[]{:S(2)}, u32[]{:S(2)}) collective-permute-start(bf16[4,16,16,128]{3,2,1,0:T(8,128)(2,1)} %get-tuple-element.40.rest_0_), channel_id=1, source_target_pairs={{0,2},{1,3},{2,0},{3,1},{4,6},{5,7},{6,4},{7,5},{8,10},{9,11},{10,... | collective-permute-start | bytes 786440 | tf_op jit(solution)/shard_map/ppermute | solution.py:420
  15.3 6.1 %collective-permute-start.10 = (bf16[8,4,16,128]{3,2,1,0:T(8,128)(2,1)S(1)}, bf16[8,4,16,128]{3,2,1,0:T(8,128)(2,1)S(1)}, u32[]{:S(2)}, u32[]{:S(2)}) collective-permute-start(bf16[8,4,16,128]{3,2,1,0:T(8,128)(2,1)S(1)} %collective-permute-done.6.rest_5_), channel_id=1, source_target_pairs={{0,4},{8,0},{16,8},{24,16},{28,24},{20,28},{12,20},{4,12},{1,5},{9... | collective-permute-start | bytes 393224 | tf_op jit(solution)/shard_map/ppermute | solution.py:451
  16.2 6.4 %collective-permute-start.9 = (bf16[8,4,16,128]{3,2,1,0:T(8,128)(2,1)S(1)}, bf16[8,4,16,128]{3,2,1,0:T(8,128)(2,1)S(1)}, u32[]{:S(2)}, u32[]{:S(2)}) collective-permute-start(bf16[8,4,16,128]{3,2,1,0:T(8,128)(2,1)S(1)} %collective-permute-done.5.rest_4_), channel_id=1, source_target_pairs={{0,8},{8,16},{16,24},{24,28},{28,20},{20,12},{12,4},{4,0},{1,9},{9... | collective-permute-start | bytes 393224 | tf_op jit(solution)/shard_map/ppermute | solution.py:448
  19.4 5.0 %collective-permute-start.7 = (bf16[8,4,16,128]{3,2,1,0:T(8,128)(2,1)S(1)}, bf16[8,4,16,128]{3,2,1,0:T(8,128)(2,1)S(1)}, u32[]{:S(2)}, u32[]{:S(2)}) collective-permute-start(bf16[8,4,16,128]{3,2,1,0:T(8,128)(2,1)S(1)} %collective-permute-done.3.rest_6_), channel_id=1, source_target_pairs={{0,8},{8,16},{16,24},{24,28},{28,20},{20,12},{12,4},{4,0},{1,9},{9... | collective-permute-start | bytes 393224 | tf_op jit(solution)/shard_map/ppermute | solution.py:448
  20.9 5.0 %collective-permute-start.8 = (bf16[8,4,16,128]{3,2,1,0:T(8,128)(2,1)S(1)}, bf16[8,4,16,128]{3,2,1,0:T(8,128)(2,1)S(1)}, u32[]{:S(2)}, u32[]{:S(2)}) collective-permute-start(bf16[8,4,16,128]{3,2,1,0:T(8,128)(2,1)S(1)} %collective-permute-done.4.rest_7_), channel_id=1, source_target_pairs={{0,4},{8,0},{16,8},{24,16},{28,24},{20,28},{12,20},{4,12},{1,5},{9... | collective-permute-start | bytes 393224 | tf_op jit(solution)/shard_map/ppermute | solution.py:451
  25.9 10.8 %collective-permute-start.12 = (bf16[4,16,16,128]{3,2,1,0:T(8,128)(2,1)S(1)}, bf16[4,16,16,128]{3,2,1,0:T(8,128)(2,1)S(1)}, u32[]{:S(2)}, u32[]{:S(2)}) collective-permute-start(bf16[4,16,16,128]{3,2,1,0:T(8,128)(2,1)S(1)} %collective-permute-done.11.rest_2_), channel_id=1, source_target_pairs={{0,1},{1,0},{2,3},{3,2},{4,5},{5,4},{6,7},{7,6},{8,9},{9,8},{10,11... | collective-permute-start | bytes 786440 | tf_op jit(solution)/shard_map/ppermute | solution.py:420
  25.9 6.3 %collective-permute-start.16 = (bf16[8,4,16,128]{3,2,1,0:T(8,128)(2,1)S(1)}, bf16[8,4,16,128]{3,2,1,0:T(8,128)(2,1)S(1)}, u32[]{:S(2)}, u32[]{:S(2)}) collective-permute-start(bf16[8,4,16,128]{3,2,1,0:T(8,128)(2,1)S(1)} %collective-permute-done.8.rest_11_), channel_id=1, source_target_pairs={{0,4},{8,0},{16,8},{24,16},{28,24},{20,28},{12,20},{4,12},{1,5},{9... | collective-permute-start | bytes 393224 | tf_op jit(solution)/shard_map/ppermute | solution.py:451
  26.4 6.3 %collective-permute-start.13 = (bf16[8,4,16,128]{3,2,1,0:T(8,128)(2,1)S(1)}, bf16[8,4,16,128]{3,2,1,0:T(8,128)(2,1)S(1)}, u32[]{:S(2)}, u32[]{:S(2)}) collective-permute-start(bf16[8,4,16,128]{3,2,1,0:T(8,128)(2,1)S(1)} %collective-permute-done.9.rest_8_), channel_id=1, source_target_pairs={{0,8},{8,16},{16,24},{24,28},{28,20},{20,12},{12,4},{4,0},{1,9},{9... | collective-permute-start | bytes 393224 | tf_op jit(solution)/shard_map/ppermute | solution.py:448
  27.9 6.7 %collective-permute-start.14 = (bf16[8,4,16,128]{3,2,1,0:T(8,128)(2,1)S(1)}, bf16[8,4,16,128]{3,2,1,0:T(8,128)(2,1)S(1)}, u32[]{:S(2)}, u32[]{:S(2)}) collective-permute-start(bf16[8,4,16,128]{3,2,1,0:T(8,128)(2,1)S(1)} %collective-permute-done.10.rest_9_), channel_id=1, source_target_pairs={{0,4},{8,0},{16,8},{24,16},{28,24},{20,28},{12,20},{4,12},{1,5},{9... | collective-permute-start | bytes 393224 | tf_op jit(solution)/shard_map/ppermute | solution.py:451
  28.4 8.3 %collective-permute-start.15 = (bf16[8,4,16,128]{3,2,1,0:T(8,128)(2,1)S(1)}, bf16[8,4,16,128]{3,2,1,0:T(8,128)(2,1)S(1)}, u32[]{:S(2)}, u32[]{:S(2)}) collective-permute-start(bf16[8,4,16,128]{3,2,1,0:T(8,128)(2,1)S(1)} %collective-permute-done.7.rest_10_), channel_id=1, source_target_pairs={{0,8},{8,16},{16,24},{24,28},{28,20},{20,12},{12,4},{4,0},{1,9},{9... | collective-permute-start | bytes 393224 | tf_op jit(solution)/shard_map/ppermute | solution.py:448
  34.6 10.0 %collective-permute-start.21 = (bf16[8,4,16,128]{3,2,1,0:T(8,128)(2,1)S(1)}, bf16[8,4,16,128]{3,2,1,0:T(8,128)(2,1)S(1)}, u32[]{:S(2)}, u32[]{:S(2)}) collective-permute-start(bf16[8,4,16,128]{3,2,1,0:T(8,128)(2,1)S(1)} %collective-permute-done.16.rest_15_), channel_id=1, source_target_pairs={{0,4},{8,0},{16,8},{24,16},{28,24},{20,28},{12,20},{4,12},{1,5},{9... | collective-permute-start | bytes 393224 | tf_op jit(solution)/shard_map/ppermute | solution.py:451
  35.1 9.5 %collective-permute-start.20 = (bf16[8,4,16,128]{3,2,1,0:T(8,128)(2,1)S(1)}, bf16[8,4,16,128]{3,2,1,0:T(8,128)(2,1)S(1)}, u32[]{:S(2)}, u32[]{:S(2)}) collective-permute-start(bf16[8,4,16,128]{3,2,1,0:T(8,128)(2,1)S(1)} %collective-permute-done.13.rest_12_), channel_id=1, source_target_pairs={{0,8},{8,16},{16,24},{24,28},{28,20},{20,12},{12,4},{4,0},{1,9},{9... | collective-permute-start | bytes 393224 | tf_op jit(solution)/shard_map/ppermute | solution.py:448
  36.7 1.0 %copy-start.1 = (bf16[4,16,16,128]{3,2,1,0:T(8,128)(2,1)S(1)}, bf16[4,16,16,128]{3,2,1,0:T(8,128)(2,1)}, u32[]{:S(2)}) copy-start(bf16[4,16,16,128]{3,2,1,0:T(8,128)(2,1)} %get-tuple-element.40.rest_0_) | copy-start | bytes 786436
  42.7 8.8 %collective-permute-start.17 = (bf16[512,128]{1,0:T(8,128)(2,1)S(1)}, bf16[512,128]{1,0:T(8,128)(2,1)S(1)}, u32[]{:S(2)}, u32[]{:S(2)}) collective-permute-start(bf16[512,128]{1,0:T(8,128)(2,1)S(1)} %get-tuple-element.45), channel_id=1, source_target_pairs={{0,1},{1,0},{2,3},{3,2},{4,5},{5,4},{6,7},{7,6},{8,9},{9,8},{10,11... | collective-permute-start | bytes 393224 | tf_op jit(solution)/shard_map/ppermute | solution.py:420
  42.8 8.9 %collective-permute-start.18 = (bf16[512,128]{1,0:T(8,128)(2,1)S(1)}, bf16[512,128]{1,0:T(8,128)(2,1)S(1)}, u32[]{:S(2)}, u32[]{:S(2)}) collective-permute-start(bf16[512,128]{1,0:T(8,128)(2,1)S(1)} %get-tuple-element.46), channel_id=1, source_target_pairs={{0,2},{1,3},{2,0},{3,1},{4,6},{5,7},{6,4},{7,5},{8,10},{9,11},{10,... | collective-permute-start | bytes 393224 | tf_op jit(solution)/shard_map/ppermute | solution.py:420
  44.1 13.7 %copy-start.3 = (bf16[4,128,512]{2,1,0:T(8,128)(2,1)S(1)}, bf16[4,128,512]{2,1,0:T(8,128)(2,1)}, u32[]{:S(2)}) copy-start(bf16[4,128,512]{2,1,0:T(8,128)(2,1)} %constant.15.clone.place) | copy-start | bytes 1572868
  44.1 7.6 %collective-permute-start.19 = (bf16[512,128]{1,0:T(8,128)(2,1)S(1)}, bf16[512,128]{1,0:T(8,128)(2,1)S(1)}, u32[]{:S(2)}, u32[]{:S(2)}) collective-permute-start(bf16[512,128]{1,0:T(8,128)(2,1)S(1)} %get-tuple-element.47), channel_id=1, source_target_pairs={{0,3},{1,2},{2,1},{3,0},{4,7},{5,6},{6,5},{7,4},{8,11},{9,10},{10,... | collective-permute-start | bytes 393224 | tf_op jit(solution)/shard_map/ppermute | solution.py:420
  49.7 1.9 %collective-permute-start.22 = (bf16[512,128]{1,0:T(8,128)(2,1)S(1)}, bf16[512,128]{1,0:T(8,128)(2,1)S(1)}, u32[]{:S(2)}, u32[]{:S(2)}) collective-permute-start(bf16[512,128]{1,0:T(8,128)(2,1)S(1)} %get-tuple-element.50), channel_id=1, source_target_pairs={{0,1},{1,0},{2,3},{3,2},{4,5},{5,4},{6,7},{7,6},{8,9},{9,8},{10,11... | collective-permute-start | bytes 393224 | tf_op jit(solution)/shard_map/ppermute | solution.py:420
  50.2 6.3 %collective-permute-start.23 = (bf16[512,128]{1,0:T(8,128)(2,1)S(1)}, bf16[512,128]{1,0:T(8,128)(2,1)S(1)}, u32[]{:S(2)}, u32[]{:S(2)}) collective-permute-start(bf16[512,128]{1,0:T(8,128)(2,1)S(1)} %get-tuple-element.51), channel_id=1, source_target_pairs={{0,2},{1,3},{2,0},{3,1},{4,6},{5,7},{6,4},{7,5},{8,10},{9,11},{10,... | collective-permute-start | bytes 393224 | tf_op jit(solution)/shard_map/ppermute | solution.py:420
  51.5 6.2 %collective-permute-start.24 = (bf16[512,128]{1,0:T(8,128)(2,1)S(1)}, bf16[512,128]{1,0:T(8,128)(2,1)S(1)}, u32[]{:S(2)}, u32[]{:S(2)}) collective-permute-start(bf16[512,128]{1,0:T(8,128)(2,1)S(1)} %get-tuple-element.52), channel_id=1, source_target_pairs={{0,3},{1,2},{2,1},{3,0},{4,7},{5,6},{6,5},{7,4},{8,11},{9,10},{10,... | collective-permute-start | bytes 393224 | tf_op jit(solution)/shard_map/ppermute | solution.py:420

commit v5 on v4

--- a/solution.py
+++ b/solution.py
@@ -194,54 +194,67 @@
     return steps, ranks
 
 
-def cross_kernel(first_slot, slots, count, scaling, offsets, parts, plan, table, *rest):
-    owns = rest[:parts]
-    candidates = rest[parts : parts + len(offsets)]
-    rest = rest[parts + len(offsets) :]
-    outs = rest[:parts]
-    own, other, crossed, operand, result = rest[parts:]
-    windows, stations = owns[0].shape[:2]
-    all_windows = windows * parts
-    quarter = candidates[0].shape[1]
-    width = stations * quarter
-    columns = slots * width
-    steps, ranks = partner_steps(plan, count)
-
-    for j in range(parts):
-
-        def widen_own(w, carry, j=j):
-            raw = owns[j][w].astype(F32)
+def expected(microseconds):
+    return pl.CostEstimate(
+        flops=int(microseconds * 1.15e9), bytes_accessed=1024, transcendentals=0
+    )
+
+
+def widen_kernel(*refs):
+    blocks, own = refs[:-1], refs[-1]
+    windows = blocks[0].shape[0]
+    for j, block in enumerate(blocks):
+
+        def widen(w, carry, j=j, block=block):
+            raw = block[w].astype(F32)
             real, imag = raw[:, :TILES], raw[:, TILES:]
             own[0, j * windows + w] = real + imag
             own[1, j * windows + w] = real
             own[2, j * windows + w] = imag
             return carry
 
-        lax.fori_loop(0, windows, widen_own, 0)
+        lax.fori_loop(0, windows, widen, 0)
+
+
+def widen_own(blocks):
+    windows, stations = blocks[0].shape[:2]
+    vmem = pl.BlockSpec(memory_space=pltpu.VMEM)
+    return pl.pallas_call(
+        widen_kernel,
+        out_shape=jax.ShapeDtypeStruct((3, len(blocks) * windows, stations, TILES, LANES), F32),
+        in_specs=[vmem] * len(blocks),
+        out_specs=vmem,
+        compiler_params=pltpu.CompilerParams(vmem_limit_bytes=16 * 2**20),
+        cost_estimate=expected(0.6),
+        name="widen",
+    )(*blocks)
+
+
+def sum_windows(first_slot, slots, count, offsets, plan, own, candidates, other, before, crossed):
+    windows, stations = own.shape[1:3]
+    quarter = other.shape[3]
+    width = stations * quarter
+    steps, ranks = partner_steps(plan, count)
     for slot in range(slots):
         step = jnp.int32(0)
         for number in range(ROUNDS):
             step = jnp.where(ranks[number] == first_slot + slot, steps[number], step)
-        for (offset, start), candidate in zip(offsets, candidates):
+        for offset, candidate in zip(offsets, candidates):
 
             @pl.when(step == offset)
-            def _(candidate=candidate, slot=slot, start=start):
+            def _(candidate=candidate, slot=slot):
                 def widen_other(w, carry):
                     raw = candidate[w].astype(F32)
                     real, imag = raw[:, :TILES], raw[:, TILES:]
-                    other[0, slot, start + w] = real
-                    other[1, slot, start + w] = real + imag
-                    other[2, slot, start + w] = imag - real
+                    other[0, slot, w] = real
+                    other[1, slot, w] = real + imag
+                    other[2, slot, w] = imag - real
                     return carry
 
-                lax.fori_loop(0, candidate.shape[0], widen_other, 0)
+                lax.fori_loop(0, windows, widen_other, 0)
 
     group = 4
     groups = stations // group
-    first_bin = (lax.broadcasted_iota(jnp.int32, (TILES, LANES), 0) == 0) & (
-        lax.broadcasted_iota(jnp.int32, (TILES, LANES), 1) == 0
-    )
-    weight = jnp.where(first_bin, 1.0, 2.0).astype(F32)
 
     def one_group(index, carry):
         slot = index // groups
@@ -249,7 +262,7 @@
 
         def sums(kind):
             totals = [None] * (group * quarter)
-            for w in range(all_windows):
+            for w in range(windows):
                 left = [own[kind, w, first + s] for s in range(group)]
                 right = [other[kind, slot, w, t] for t in range(quarter)]
                 for s in range(group):
@@ -259,29 +272,71 @@
                         totals[place] = term if w == 0 else totals[place] + term
             return totals
 
+        def store(place, part, value):
+            at = pl.multiple_of((base + place) * 2 * TILES + part * TILES, TILES)
+            if before is not None:
+                value = value + before[pl.ds(at, TILES), :]
+            crossed[pl.ds(at, TILES), :] = value
+
         base = slot * width + first * quarter
         shared = sums(0)
         third = sums(2)
         for place in range(group * quarter):
-            at = pl.multiple_of((base + place) * 2 * TILES, 2 * TILES)
-            crossed[pl.ds(at, TILES), :] = (shared[place] + third[place]) * weight
+            store(place, 0, shared[place] + third[place])
         second = sums(1)
         for place in range(group * quarter):
-            at = pl.multiple_of((base + place) * 2 * TILES + TILES, TILES)
-            crossed[pl.ds(at, TILES), :] = (shared[place] - second[place]) * weight
+            store(place, 1, shared[place] - second[place])
         return carry
 
     lax.fori_loop(0, slots * groups, one_group, 0)
 
+
+def near_kernel(first_slot, slots, count, offsets, plan, own, *rest):
+    candidates = rest[: len(offsets)]
+    crossed, other = rest[len(offsets) :]
+    sum_windows(
+        first_slot, slots, count, offsets, plan, own, candidates, other, None, crossed
+    )
+
+
+def near_sums(plan, own, offsets, candidates, first_slot, slots, count):
+    windows, stations = own.shape[1:3]
+    quarter = candidates[0].shape[1]
+    columns = slots * stations * quarter
+    vmem = pl.BlockSpec(memory_space=pltpu.VMEM)
+    return pl.pallas_call(
+        functools.partial(near_kernel, first_slot, slots, count, tuple(offsets)),
+        out_shape=jax.ShapeDtypeStruct((columns * 2 * TILES, LANES), F32),
+        in_specs=[pl.BlockSpec(memory_space=pltpu.SMEM)] + [vmem] * (1 + len(candidates)),
+        out_specs=vmem,
+        scratch_shapes=[pltpu.VMEM((3, slots, windows, quarter, TILES, LANES), F32)],
+        compiler_params=pltpu.CompilerParams(vmem_limit_bytes=16 * 2**20),
+        cost_estimate=expected(0.4 + 0.7 * slots),
+        name="near",
+    )(plan, own, *candidates)
+
+
+def far_kernel(first_slot, slots, count, scaling, offsets, parts, plan, table, own, before, *rest):
+    candidates = rest[: len(offsets)]
+    outs = rest[len(offsets) : len(offsets) + parts]
+    other, crossed, operand, result = rest[len(offsets) + parts :]
+    sum_windows(
+        first_slot, slots, count, offsets, plan, own, candidates, other, before, crossed
+    )
+    width = own.shape[2] * other.shape[3]
+    columns = slots * width
     even = even_lanes((columns, LANES))
     sign_real = lane_cycle([1.0, -1.0, -1.0, 1.0])
     sign_imag = lane_cycle([1.0, 1.0, -1.0, -1.0])
     cosine, sine = eighth_turn()
+    lane = lax.broadcasted_iota(jnp.int32, (1, LANES), 1)
+    first_weight = jnp.where(lane == 0, 1.0, 2.0).astype(F32)
     for j in range(TILES):
         at = slice(j * LANES, (j + 1) * LANES)
         at_imag = slice(NBIN + j * LANES, NBIN + (j + 1) * LANES)
-        real = crossed[pl.ds(j, columns, stride=2 * TILES), :]
-        imag = crossed[pl.ds(TILES + j, columns, stride=2 * TILES), :]
+        weight = first_weight if j == 0 else 2.0
+        real = crossed[pl.ds(j, columns, stride=2 * TILES), :] * weight
+        imag = crossed[pl.ds(TILES + j, columns, stride=2 * TILES), :] * weight
         turned = [(real, imag), (real * cosine - imag * sine, imag * cosine + real * sine)]
         turned += [quarter_turns(r, i, even, sign_real, sign_imag) for r, i in turned]
         for q in range(CHUNKS):
@@ -312,10 +367,8 @@
         outs[j][...] = result[me ^ j]
 
 
-def cross_lags(plan, table, owns, offsets, candidates, first_slot, slots, count, scaling):
-    parts = len(owns)
-    windows, stations = owns[0].shape[:2]
-    all_windows = windows * parts
+def cross_lags(plan, table, own, before, offsets, candidates, first_slot, slots, count, parts, scaling):
+    windows, stations = own.shape[1:3]
     quarter = candidates[0].shape[1]
     columns = slots * stations * quarter
     share = LAGS // parts
@@ -324,65 +377,80 @@
     vmem = pl.BlockSpec(memory_space=pltpu.VMEM)
     return pl.pallas_call(
         functools.partial(
-            cross_kernel, first_slot, slots, count, scaling, tuple(offsets), parts
+            far_kernel, first_slot, slots, count, scaling, tuple(offsets), parts
         ),
         out_shape=[jax.ShapeDtypeStruct(out, BF)] * parts,
-        in_specs=[smem] + [vmem] * (1 + parts + len(candidates)),
+        in_specs=[smem] + [vmem] * (3 + len(candidates)),
         out_specs=[vmem] * parts,
         scratch_shapes=[
-            pltpu.VMEM((3, all_windows, stations, TILES, LANES), F32),
-            pltpu.VMEM((3, slots, all_windows, quarter, TILES, LANES), F32),
+            pltpu.VMEM((3, slots, windows, quarter, TILES, LANES), F32),
             pltpu.VMEM((columns * 2 * TILES, LANES), F32),
             pltpu.VMEM((CHUNKS * columns, 2 * NBIN), BF),
             pltpu.VMEM((parts,) + out, BF),
         ],
         compiler_params=pltpu.CompilerParams(vmem_limit_bytes=24 * 2**20),
-        cost_estimate=pl.CostEstimate(
-            flops=2 * LAGS * 2 * NBIN * columns * 4, bytes_accessed=2 * 2**20, transcendentals=0
-        ),
-        name="cross",
-    )(plan, table, *owns, *candidates)
-
-
-def place_kernel(count, parts, groups, steps, plan, place, *rest):
-    pieces = rest[: parts * len(groups)]
-    out_hbm, out, sems = rest[parts * len(groups) :]
-    pairs = out.shape[3]
-    half = out.shape[1]
-    rows = half // steps
-    me = lax.axis_index("seg")
+        cost_estimate=expected(0.5 + 1.2 * slots),
+        name="far",
+    )(plan, table, own, before, *candidates)
+
+
+def slot_rounds(plan, count):
     _, ranks = partner_steps(plan, count)
-    round_of = []
+    rounds = []
     for slot in range(ROUNDS):
         number = jnp.int32(0)
         for other in range(1, ROUNDS):
             number = jnp.where(ranks[other] == slot, other, number)
-        round_of.append(number)
-    matrix = jnp.concatenate([place[me ^ j] for j in range(parts)], axis=0)
+        rounds.append(number)
+    return rounds
+
+
+def placed_block(pieces, matrix, at, half):
+    joined = jnp.concatenate([piece[at, :] for piece in pieces], axis=1)
+    if pieces[0].shape[0] > half:
+        later = slice(half + at.start, half + at.stop)
+        high = jnp.concatenate([piece[later, :] for piece in pieces], axis=1)
+        joined = jnp.concatenate([joined, high], axis=0)
+    return jnp.dot(joined, matrix, preferred_element_type=F32)
+
+
+def joined_matrix(place, parts):
+    me = lax.axis_index("seg")
+    return jnp.concatenate([place[me ^ j] for j in range(parts)], axis=0)
+
+
+def early_kernel(parts, groups, place, *rest):
+    pieces, out = rest[:-1], rest[-1]
+    half, pairs = out.shape[2:]
+    matrix = joined_matrix(place, parts)
+    at = slice(0, half)
+    for index, (first_slot, slots) in enumerate(groups):
+        block = placed_block(pieces[index * parts : (index + 1) * parts], matrix, at, half)
+        if slots == 1:
+            out[first_slot, 0] = block[:, :pairs]
+            out[first_slot, 1] = block[:, pairs:]
+        else:
+            for slot in range(2):
+                columns = slice(slot * pairs, (slot + 1) * pairs)
+                out[first_slot + slot, 0] = block[:half, columns]
+                out[first_slot + slot, 1] = block[half:, columns]
+
+
+def late_kernel(count, parts, steps, plan, place, early, *rest):
+    pieces = rest[:parts]
+    out_hbm, out, sems = rest[parts:]
+    half, _, pairs = out.shape[1:]
+    rows = half // steps
+    rounds = slot_rounds(plan, count)
+    matrix = joined_matrix(place, parts)
     copies = []
     for step in range(steps):
         at = slice(step * rows, (step + 1) * rows)
-        for index, (first_slot, slots) in enumerate(groups):
-            own = pieces[index * parts : (index + 1) * parts]
-            lows = [piece[at, :] for piece in own]
-            if slots == 1:
-                joined = jnp.concatenate(lows, axis=1)
-            else:
-                later = slice(half + step * rows, half + (step + 1) * rows)
-                highs = [piece[later, :] for piece in own]
-                joined = jnp.concatenate(
-                    [jnp.concatenate(lows, axis=1), jnp.concatenate(highs, axis=1)], axis=0
-                )
-            block = jnp.dot(joined, matrix, preferred_element_type=F32)
-            if slots == 1:
-                out[0, at, round_of[first_slot], :] = block[:, :pairs]
-                out[1, at, round_of[first_slot], :] = block[:, pairs:]
-            else:
-                for slot in range(2):
-                    columns = slice(slot * pairs, (slot + 1) * pairs)
-                    out[0, at, round_of[first_slot + slot], :] = block[:rows, columns]
-                    out[1, at, round_of[first_slot + slot], :] = block[rows:, columns]
+        block = placed_block(pieces, matrix, at, half)
         for h in range(2):
+            for slot in range(ROUNDS - 1):
+                out[h, at, rounds[slot], :] = early[slot, h, at, :]
+            out[h, at, rounds[ROUNDS - 1], :] = block[:, h * pairs : (h + 1) * pairs]
             copy = pltpu.make_async_copy(
                 out.at[h, at], out_hbm.at[h, at], sems.at[2 * step + h]
             )
@@ -397,21 +465,28 @@
     share = LAGS // parts
     half = share // 2
     steps = 2
-    place = make_placing(stations, stations // parts, parts)
+    place = jnp.asarray(make_placing(stations, stations // parts, parts))
     vmem = pl.BlockSpec(memory_space=pltpu.VMEM)
+    early = pl.pallas_call(
+        functools.partial(early_kernel, parts, tuple(groups[:-1])),
+        out_shape=jax.ShapeDtypeStruct((ROUNDS - 1, 2, half, pairs), F32),
+        in_specs=[vmem] * (1 + len(pieces) - parts),
+        out_specs=vmem,
+        compiler_params=pltpu.CompilerParams(vmem_limit_bytes=16 * 2**20),
+        cost_estimate=expected(1.0),
+        name="early",
+    )(place, *pieces[:-parts])
     shape = (2, half, ROUNDS, pairs)
     out = pl.pallas_call(
-        functools.partial(place_kernel, count, parts, tuple(groups), steps),
+        functools.partial(late_kernel, count, parts, steps),
         out_shape=jax.ShapeDtypeStruct(shape, F32),
-        in_specs=[pl.BlockSpec(memory_space=pltpu.SMEM)] + [vmem] * (1 + len(pieces)),
+        in_specs=[pl.BlockSpec(memory_space=pltpu.SMEM)] + [vmem] * (2 + parts),
         out_specs=pl.BlockSpec(memory_space=pl.ANY),
         scratch_shapes=[pltpu.VMEM(shape, F32), pltpu.SemaphoreType.DMA((2 * steps,))],
         compiler_params=pltpu.CompilerParams(vmem_limit_bytes=24 * 2**20),
-        cost_estimate=pl.CostEstimate(
-            flops=2 * share * 4 * pairs * ROUNDS * pairs, bytes_accessed=4 * 2**20, transcendentals=0
-        ),
-        name="place",
-    )(plan, place, *pieces)
+        cost_estimate=expected(1.5),
+        name="late",
+    )(plan, place, early, *pieces[-parts:])
     return out.reshape(share, ROUNDS, pairs)
 
 
@@ -422,6 +497,10 @@
 
 def exchange(pieces):
     return [pieces[0]] + [swap(pieces[j], j) for j in range(1, len(pieces))]
+
+
+def after(value, others):
+    return lax.optimization_barrier((value, others))[0]
 
 
 def per_device(records, plan):
@@ -450,10 +529,25 @@
     def down(value):
         return lax.ppermute(value, "sta", downward)
 
-    spots, blocks = [], []
     near_up = near_down = near
     far_up = far_down = far
+    near_own = widen_own([white, sibling])
     steps = (count - 1) // 2
+    groups = [(0, 1), (1, 2), (3, 1)]
+    arrived = []
+    spots, near_blocks, far_blocks = [], [], []
+    lags, pieces = [], []
+
+    def group_lags(index, near_own, far_own):
+        first_slot, slots = groups[index]
+        at, nears, fars = arrived[index - len(groups)]
+        before = near_sums(plan, near_own, at, nears, first_slot, slots, count)
+        if index == 1:
+            before = after(before, pieces)
+        return cross_lags(
+            plan, table, far_own, before, at, fars, first_slot, slots, count, parts, scaling
+        )
+
     for step in range(1, steps + 1):
         if step == 2:
             near_up, near_down = lax.optimization_barrier((near_up, near_down))
@@ -463,7 +557,11 @@
             )
         last_up, last_down = far_up, far_down
         next_near = up(near_up), down(near_down)
-        if step == 3:
+        if step == 2:
+            far_up, far_down, near_up, near_down, near_own = lax.optimization_barrier(
+                (far_up, far_down, near_up, near_down, near_own)
+            )
+        elif step == 3:
             far_up, far_down, near_up, near_down, across = lax.optimization_barrier(
                 (far_up, far_down, near_up, near_down, across)
             )
@@ -473,22 +571,25 @@
             )
         far_up, far_down = up(far_up), down(far_down)
         near_up, near_down = next_near
-        spots += [(count - step, 0), (step, 0), (count - step, 2 * windows), (step, 2 * windows)]
-        blocks += [near_up, near_down, far_up, far_down]
-    owns = [white, sibling, across, swap(across, 1)]
-    late_spots, late_blocks = list(spots), list(blocks)
+        spots += [count - step, step]
+        near_blocks += [near_up, near_down]
+        far_blocks += [far_up, far_down]
+        arrived.append((list(spots), list(near_blocks), list(far_blocks)))
+    far_own = widen_own([across, swap(across, 1)])
+    arrived.append(arrived[-1])
+    lags = group_lags(0, near_own, far_own)
+    pieces = exchange(lags)
     if count % 2 == 0:
-        late_spots += [(count // 2, 0), (count // 2, 2 * windows)]
+        near_up = after(near_up, lags)
         middle_up = up(near_up)
-        far_down, near_up, near_down = lax.optimization_barrier((far_down, near_up, near_down))
-        late_blocks += [middle_up, down(far_down)]
-    groups = [(0, 2), (2, 2)]
-    pieces = []
-    for (first_slot, slots), at, values in zip(
-        groups, (spots, late_spots), (blocks, late_blocks)
-    ):
-        lags = cross_lags(plan, table, owns, at, values, first_slot, slots, count, scaling)
-        pieces += exchange(lags)
+        far_down = after(far_down, (near_up, near_down))
+        arrived[-1] = (
+            spots + [count // 2], near_blocks + [middle_up], far_blocks + [down(far_down)]
+        )
+    for index in range(1, len(groups)):
+        near_own = after(near_own, lags)
+        lags = group_lags(index, near_own, far_own)
+        pieces = pieces + exchange(lags)
     return place_lags(plan, groups, pieces, count, stations, parts)
 
 

time: 60.6 us -> 57.9 us (0.955)
  waiting for transfers between devices: 19.2 us -> 9.62 us
  Pallas kernels: 16.6 us -> 19.9 us
  starting transfers between devices: 22.6 us -> 24.6 us
  local copies, waits for them, and re-layouts: 0.96 us -> 2.44 us
    ppermute x7, waiting for transfers between devices: 8.4 us -> 2.39 us  [down(): return lax.ppermute(value, 'sta', downward)]
    pallas_call x3 -> x10, Pallas kernels: 12.7 us -> 16.1 us  [the longest x3 8.49 us: cross_lags(): pl.pallas_call(functools.partial(far_kernel, first_slot, slots, count, sc...]
    ppermute x11 -> x14, waiting for transfers between devices: 7.4 us -> 4.64 us  [swap(): return lax.ppermute(value, 'seg', [(i, i ^ j) for i in range(parts)])]
    ppermute x7, starting transfers between devices: 3.43 us -> 6.07 us  [down(): return lax.ppermute(value, 'sta', downward)]
    ppermute x7, starting transfers between devices: 10.9 us -> 8.33 us  [up(): return lax.ppermute(value, 'sta', upward)]
    ppermute x11 -> x14, starting transfers between devices: 8.26 us -> 10.2 us  [swap(): return lax.ppermute(value, 'seg', [(i, i ^ j) for i in range(parts)])]
    unnamed x8, local copies, waits for them, and re-layouts: 0.96 us -> 2.44 us
    ppermute x7, waiting for transfers between devices: 3.43 us -> 2.59 us  [up(): return lax.ppermute(value, 'sta', upward)]
  transfers between devices with their start and end apart: 25 -> 28, of which waited for: 11 -> 9; matrix products, arithmetic and copies ran while one was open for 1% -> 2% of each run, Pallas kernels for 17% -> 24%
where the time goes in v5:
time: 57.9 us; the launch traced here: 57.6 us
  starting transfers between devices  24.6 us (42%)
  Pallas kernels  19.9 us (34%)
  waiting for transfers between devices  9.62 us (17%)
  local copies, waits for them, and re-layouts  2.44 us (4%)
  other arithmetic  0.87 us (2%)
    ppermute x14, starting transfers between devices, swap(): return lax.ppermute(value, 'seg', [(i, i ^ j) for i in range(parts)])  10.2 us
    pallas_call x3, Pallas kernels, cross_lags(): pl.pallas_call(functools.partial(far_kernel, first_slot, slots, count, sc...  8.49 us
    ppermute x7, starting transfers between devices, up(): return lax.ppermute(value, 'sta', upward)  8.33 us
    ppermute x7, starting transfers between devices, down(): return lax.ppermute(value, 'sta', downward)  6.07 us
    ppermute x14, waiting for transfers between devices, swap(): return lax.ppermute(value, 'seg', [(i, i ^ j) for i in range(parts)])  4.64 us
    pallas_call x3, Pallas kernels, near_sums(): pl.pallas_call(functools.partial(near_kernel, first_slot, slots, count, t...  4.56 us
    pallas_call x1, Pallas kernels, prepare(): pl.pallas_call(functools.partial(prep_kernel, parts), out_shape=[jax.Shap...  3.76 us
    ppermute x7, waiting for transfers between devices, up(): return lax.ppermute(value, 'sta', upward)  2.59 us
  transfers between devices with their start and end apart: 28, of which 9 were waited for; matrix products, arithmetic and copies ran while one was open for 2% of the time, Pallas kernels for 24%

profile of v5, /device:TPU:0, one launch (start us, length us, event | category | flops | bytes accessed | tf_op | source)
XLA Modules:
  0.0 57.6 jit_solution(15844602828350585653)
XLA Ops:
  0.0 3.8 %prep.1 = (bf16[4,16,16,128]{3,2,1,0:T(8,128)(2,1)}, bf16[4,4,16,128]{3,2,1,0:T(8,128)(2,1)}, bf16[4,4,16,128]{3,2,1,0:T(8,128)(2,1)}, bf16[4,4,16,128]{3,2,1,0:T(8,128)(2,1)}) custom-call(f32[16,4,2048]{2,1,0:T(4,128)} %records_hbm.1, bf16[512,2048]{1,0:T(8,128)(2,1)} %constant.14.clone.table_hbm.table), custom_call_target="tpu_custom_call" | custom-call | flops 536870912 | bytes 3145728 | tf_op jit(solution)/shard_map/prep/pallas_call | solution.py:153
  4.3 2.6 %collective-permute-start = (bf16[4,4,16,128]{3,2,1,0:T(8,128)(2,1)}, bf16[4,4,16,128]{3,2,1,0:T(8,128)(2,1)S(1)}, u32[]{:S(2)}, u32[]{:S(2)}) collective-permute-start(bf16[4,4,16,128]{3,2,1,0:T(8,128)(2,1)} %get-tuple-element.38), channel_id=1, source_target_pairs={{0,2},{1,3},{2,0},{3,1},{4,6},{5,7},{6,4},{7,5},{8,10},{9,11},{10,... | collective-permute-start | bytes 196616 | tf_op jit(solution)/shard_map/ppermute | solution.py:495
  6.9 0.9 %pad_maximum_fusion.1 = bf16[8,4,16,128]{3,2,1,0:T(8,128)(2,1)S(1)} fusion(bf16[4,4,16,128]{3,2,1,0:T(8,128)(2,1)S(1)} %constant_dynamic-slice_fusion, bf16[4,4,16,128]{3,2,1,0:T(8,128)(2,1)} %get-tuple-element.42), kind=kLoop, calls=%fused_computation.1 | loop fusion | flops 65536 | bytes 262144 | tf_op jit(solution)/shard_map/concatenate | solution.py:517
  7.8 1.8 %collective-permute-start.6 = (bf16[8,4,16,128]{3,2,1,0:T(8,128)(2,1)S(1)}, bf16[8,4,16,128]{3,2,1,0:T(8,128)(2,1)S(1)}, u32[]{:S(2)}, u32[]{:S(2)}) collective-permute-start(bf16[8,4,16,128]{3,2,1,0:T(8,128)(2,1)S(1)} %pad_maximum_fusion.1), channel_id=1, source_target_pairs={{0,4},{8,0},{16,8},{24,16},{28,24},{20,28},{12,20},{4,12},{1,5},{9... | collective-permute-start | bytes 393224 | tf_op jit(solution)/shard_map/ppermute | solution.py:530
  9.9 1.3 %collective-permute-done.1 = bf16[4,4,16,128]{3,2,1,0:T(8,128)(2,1)S(1)} collective-permute-done((bf16[4,4,16,128]{3,2,1,0:T(8,128)(2,1)}, bf16[4,4,16,128]{3,2,1,0:T(8,128)(2,1)S(1)}, u32[]{:S(2)}, u32[]{:S(2)}) %collective-permute-start.1) | collective-permute-done | bytes 65568 | tf_op jit(solution)/shard_map/ppermute | solution.py:495
  11.2 1.6 %collective-permute-start.3 = (bf16[8,4,16,128]{3,2,1,0:T(8,128)(2,1)S(1)}, bf16[8,4,16,128]{3,2,1,0:T(8,128)(2,1)S(1)}, u32[]{:S(2)}, u32[]{:S(2)}) collective-permute-start(bf16[8,4,16,128]{3,2,1,0:T(8,128)(2,1)S(1)} %pad_maximum_fusion), channel_id=1, source_target_pairs={{0,4},{8,0},{16,8},{24,16},{28,24},{20,28},{12,20},{4,12},{1,5},{9... | collective-permute-start | bytes 393224 | tf_op jit(solution)/shard_map/ppermute | solution.py:530
  13.3 1.2 %collective-permute-start.11 = (bf16[4,16,16,128]{3,2,1,0:T(8,128)(2,1)}, bf16[4,16,16,128]{3,2,1,0:T(8,128)(2,1)S(1)}, u32[]{:S(2)}, u32[]{:S(2)}) collective-permute-start(bf16[4,16,16,128]{3,2,1,0:T(8,128)(2,1)} %get-tuple-element.49.refs_0_), channel_id=1, source_target_pairs={{0,2},{1,3},{2,0},{3,1},{4,6},{5,7},{6,4},{7,5},{8,10},{9,11},{10,... | collective-permute-start | bytes 786440 | tf_op jit(solution)/shard_map/ppermute | solution.py:495
  14.6 1.0 %copy-done.1 = bf16[4,16,16,128]{3,2,1,0:T(8,128)(2,1)S(1)} copy-done((bf16[4,16,16,128]{3,2,1,0:T(8,128)(2,1)S(1)}, bf16[4,16,16,128]{3,2,1,0:T(8,128)(2,1)}, u32[]{:S(2)}) %copy-start.1) | copy-done | bytes 262168
  15.7 1.6 %collective-permute-start.9 = (bf16[8,4,16,128]{3,2,1,0:T(8,128)(2,1)S(1)}, bf16[8,4,16,128]{3,2,1,0:T(8,128)(2,1)S(1)}, u32[]{:S(2)}, u32[]{:S(2)}) collective-permute-start(bf16[8,4,16,128]{3,2,1,0:T(8,128)(2,1)S(1)} %collective-permute-done.5.rest_0_), channel_id=1, source_target_pairs={{0,8},{8,16},{16,24},{24,28},{28,20},{20,12},{12,4},{4,0},{1,9},{9... | collective-permute-start | bytes 393224 | tf_op jit(solution)/shard_map/ppermute | solution.py:527
  18.2 1.1 %collective-permute-start.7 = (bf16[8,4,16,128]{3,2,1,0:T(8,128)(2,1)S(1)}, bf16[8,4,16,128]{3,2,1,0:T(8,128)(2,1)S(1)}, u32[]{:S(2)}, u32[]{:S(2)}) collective-permute-start(bf16[8,4,16,128]{3,2,1,0:T(8,128)(2,1)S(1)} %collective-permute-done.2.rest_0_), channel_id=1, source_target_pairs={{0,8},{8,16},{16,24},{24,28},{28,20},{20,12},{12,4},{4,0},{1,9},{9... | collective-permute-start | bytes 393224 | tf_op jit(solution)/shard_map/ppermute | solution.py:527
  19.3 0.9 %collective-permute-start.8 = (bf16[8,4,16,128]{3,2,1,0:T(8,128)(2,1)S(1)}, bf16[8,4,16,128]{3,2,1,0:T(8,128)(2,1)S(1)}, u32[]{:S(2)}, u32[]{:S(2)}) collective-permute-start(bf16[8,4,16,128]{3,2,1,0:T(8,128)(2,1)S(1)} %collective-permute-done.3.rest_1_), channel_id=1, source_target_pairs={{0,4},{8,0},{16,8},{24,16},{28,24},{20,28},{12,20},{4,12},{1,5},{9... | collective-permute-start | bytes 393224 | tf_op jit(solution)/shard_map/ppermute | solution.py:530
  20.3 1.8 %collective-permute-done.9.rest_2_ = bf16[8,4,16,128]{3,2,1,0:T(8,128)(2,1)S(1)} collective-permute-done((bf16[8,4,16,128]{3,2,1,0:T(8,128)(2,1)S(1)}, bf16[8,4,16,128]{3,2,1,0:T(8,128)(2,1)S(1)}, u32[]{:S(2)}, u32[]{:S(2)}) %collective-permute-start.9) | collective-permute-done | bytes 131104 | tf_op jit(solution)/shard_map/ppermute | solution.py:527
  22.1 1.3 %collective-permute-done.10.rest_3_ = bf16[8,4,16,128]{3,2,1,0:T(8,128)(2,1)S(1)} collective-permute-done((bf16[8,4,16,128]{3,2,1,0:T(8,128)(2,1)S(1)}, bf16[8,4,16,128]{3,2,1,0:T(8,128)(2,1)S(1)}, u32[]{:S(2)}, u32[]{:S(2)}) %collective-permute-start.10) | collective-permute-done | bytes 131104 | tf_op jit(solution)/shard_map/ppermute | solution.py:530
  23.6 1.1 %collective-permute-done.8.rest_3_ = bf16[8,4,16,128]{3,2,1,0:T(8,128)(2,1)S(1)} collective-permute-done((bf16[8,4,16,128]{3,2,1,0:T(8,128)(2,1)S(1)}, bf16[8,4,16,128]{3,2,1,0:T(8,128)(2,1)S(1)}, u32[]{:S(2)}, u32[]{:S(2)}) %collective-permute-start.8) | collective-permute-done | bytes 131104 | tf_op jit(solution)/shard_map/ppermute | solution.py:530
  24.8 1.6 %collective-permute-start.16 = (bf16[8,4,16,128]{3,2,1,0:T(8,128)(2,1)S(1)}, bf16[8,4,16,128]{3,2,1,0:T(8,128)(2,1)S(1)}, u32[]{:S(2)}, u32[]{:S(2)}) collective-permute-start(bf16[8,4,16,128]{3,2,1,0:T(8,128)(2,1)S(1)} %collective-permute-done.9.rest_2_), channel_id=1, source_target_pairs={{0,8},{8,16},{16,24},{24,28},{28,20},{20,12},{12,4},{4,0},{1,9},{9... | collective-permute-start | bytes 393224 | tf_op jit(solution)/shard_map/ppermute | solution.py:527
  26.8 1.6 %collective-permute-start.18 = (bf16[8,4,16,128]{3,2,1,0:T(8,128)(2,1)S(1)}, bf16[8,4,16,128]{3,2,1,0:T(8,128)(2,1)S(1)}, u32[]{:S(2)}, u32[]{:S(2)}) collective-permute-start(bf16[8,4,16,128]{3,2,1,0:T(8,128)(2,1)S(1)} %collective-permute-done.7.rest_2_), channel_id=1, source_target_pairs={{0,8},{8,16},{16,24},{24,28},{28,20},{20,12},{12,4},{4,0},{1,9},{9... | collective-permute-start | bytes 393224 | tf_op jit(solution)/shard_map/ppermute | solution.py:527
  28.8 1.3 %near.3.before = f32[1024,128]{1,0:T(8,128)S(1)} custom-call(s32[4,8]{1,0:T(4,128)S(1)} %copy-done.2, f32[3,8,16,8,128]{4,3,2,1,0:T(8,128)S(1)} %widen.2.own, bf16[8,4,16,128]{3,2,1,0:T(8,128)(2,1)S(1)} %collective-permute-done.5.rest_0_, bf16[8,4,16,128]{3,2,1,0:T(8,128)(2,1)S(1)} %collective-permute-done.6.rest_1_, ...), custom_call_target="tpu_custom_call" | custom-call | flops 1264999936 | bytes 1024 | tf_op jit(solution)/shard_map/near/pallas_call | solution.py:307
  30.3 1.4 %copy-done = bf16[512,2048]{1,0:T(8,128)(2,1)S(1)} copy-done((bf16[512,2048]{1,0:T(8,128)(2,1)S(1)}, bf16[512,2048]{1,0:T(8,128)(2,1)}, u32[]{:S(2)}) %copy-start) | copy-done | bytes 2097176
  31.7 2.3 %far.3 = (bf16[256,128]{1,0:T(8,128)(2,1)S(1)}, bf16[256,128]{1,0:T(8,128)(2,1)S(1)}, bf16[256,128]{1,0:T(8,128)(2,1)S(1)}, bf16[256,128]{1,0:T(8,128)(2,1)S(1)}) custom-call(s32[4,8]{1,0:T(4,128)S(1)} %copy-done.2, bf16[512,2048]{1,0:T(8,128)(2,1)S(1)} %copy-done, f32[3,8,16,8,128]{4,3,2,1,0:T(8,128)S(1)} %widen.3.own, f32[1024,128]{1,0:T(8,128)S(1)} %near.3.before, ...), custom_call_target="tpu_custom_call" | custom-call | flops 1955000064 | bytes 1024 | tf_op jit(solution)/shard_map/far/pallas_call | solution.py:378
  34.1 1.1 %collective-permute-start.14 = (bf16[256,128]{1,0:T(8,128)(2,1)S(1)}, bf16[256,128]{1,0:T(8,128)(2,1)S(1)}, u32[]{:S(2)}, u32[]{:S(2)}) collective-permute-start(bf16[256,128]{1,0:T(8,128)(2,1)S(1)} %get-tuple-element.54), channel_id=1, source_target_pairs={{0,2},{1,3},{2,0},{3,1},{4,6},{5,7},{6,4},{7,5},{8,10},{9,11},{10,... | collective-permute-start | bytes 196616 | tf_op jit(solution)/shard_map/ppermute | solution.py:495
  35.3 0.8 %collective-permute-start.15 = (bf16[256,128]{1,0:T(8,128)(2,1)S(1)}, bf16[256,128]{1,0:T(8,128)(2,1)S(1)}, u32[]{:S(2)}, u32[]{:S(2)}) collective-permute-start(bf16[256,128]{1,0:T(8,128)(2,1)S(1)} %get-tuple-element.55), channel_id=1, source_target_pairs={{0,3},{1,2},{2,1},{3,0},{4,7},{5,6},{6,5},{7,4},{8,11},{9,10},{10,... | collective-permute-start | bytes 196616 | tf_op jit(solution)/shard_map/ppermute | solution.py:495
  36.0 2.0 %near.4.before = f32[2048,128]{1,0:T(8,128)S(1)} custom-call(s32[4,8]{1,0:T(4,128)S(1)} %copy-done.2, f32[3,8,16,8,128]{4,3,2,1,0:T(8,128)S(1)} %widen.2.own, bf16[8,4,16,128]{3,2,1,0:T(8,128)(2,1)S(1)} %collective-permute-done.5.rest_0_, bf16[8,4,16,128]{3,2,1,0:T(8,128)(2,1)S(1)} %collective-permute-done.6.rest_1_, ...), custom_call_target="tpu_custom_call" | custom-call | flops 2070000000 | bytes 1024 | tf_op jit(solution)/shard_map/near/pallas_call | solution.py:307
  38.0 1.6 %collective-permute-start.23 = (bf16[8,4,16,128]{3,2,1,0:T(8,128)(2,1)S(1)}, bf16[8,4,16,128]{3,2,1,0:T(8,128)(2,1)S(1)}, u32[]{:S(2)}, u32[]{:S(2)}) collective-permute-start(bf16[8,4,16,128]{3,2,1,0:T(8,128)(2,1)S(1)} %collective-permute-done.16.rest_4_), channel_id=1, source_target_pairs={{0,8},{8,16},{16,24},{24,28},{28,20},{20,12},{12,4},{4,0},{1,9},{9... | collective-permute-start | bytes 393224 | tf_op jit(solution)/shard_map/ppermute | solution.py:527
  40.1 3.8 %far.4 = (bf16[512,128]{1,0:T(8,128)(2,1)S(1)}, bf16[512,128]{1,0:T(8,128)(2,1)S(1)}, bf16[512,128]{1,0:T(8,128)(2,1)S(1)}, bf16[512,128]{1,0:T(8,128)(2,1)S(1)}) custom-call(s32[4,8]{1,0:T(4,128)S(1)} %copy-done.2, bf16[512,2048]{1,0:T(8,128)(2,1)S(1)} %copy-done, f32[3,8,16,8,128]{4,3,2,1,0:T(8,128)S(1)} %widen.3.own, f32[2048,128]{1,0:T(8,128)S(1)} %near.4.before, ...), custom_call_target="tpu_custom_call" | custom-call | flops 3335000064 | bytes 1024 | tf_op jit(solution)/shard_map/far/pallas_call | solution.py:378
  43.9 1.1 %collective-permute-start.21 = (bf16[512,128]{1,0:T(8,128)(2,1)S(1)}, bf16[512,128]{1,0:T(8,128)(2,1)S(1)}, u32[]{:S(2)}, u32[]{:S(2)}) collective-permute-start(bf16[512,128]{1,0:T(8,128)(2,1)S(1)} %get-tuple-element.62), channel_id=1, source_target_pairs={{0,2},{1,3},{2,0},{3,1},{4,6},{5,7},{6,4},{7,5},{8,10},{9,11},{10,... | collective-permute-start | bytes 393224 | tf_op jit(solution)/shard_map/ppermute | solution.py:495
  45.8 1.3 %near.5.before = f32[1024,128]{1,0:T(8,128)S(1)} custom-call(s32[4,8]{1,0:T(4,128)S(1)} %copy-done.2, f32[3,8,16,8,128]{4,3,2,1,0:T(8,128)S(1)} %widen.2.own, bf16[8,4,16,128]{3,2,1,0:T(8,128)(2,1)S(1)} %collective-permute-done.5.rest_0_, bf16[8,4,16,128]{3,2,1,0:T(8,128)(2,1)S(1)} %collective-permute-done.6.rest_1_, ...), custom_call_target="tpu_custom_call" | custom-call | flops 1264999936 | bytes 1024 | tf_op jit(solution)/shard_map/near/pallas_call | solution.py:307
  47.1 2.4 %far.5 = (bf16[256,128]{1,0:T(8,128)(2,1)S(1)}, bf16[256,128]{1,0:T(8,128)(2,1)S(1)}, bf16[256,128]{1,0:T(8,128)(2,1)S(1)}, bf16[256,128]{1,0:T(8,128)(2,1)S(1)}) custom-call(s32[4,8]{1,0:T(4,128)S(1)} %copy-done.2, bf16[512,2048]{1,0:T(8,128)(2,1)S(1)} %copy-done, f32[3,8,16,8,128]{4,3,2,1,0:T(8,128)S(1)} %widen.3.own, f32[1024,128]{1,0:T(8,128)S(1)} %near.5.before, ...), custom_call_target="tpu_custom_call" | custom-call | flops 1955000064 | bytes 1024 | tf_op jit(solution)/shard_map/far/pallas_call | solution.py:378
  49.9 1.1 %collective-permute-start.26 = (bf16[256,128]{1,0:T(8,128)(2,1)S(1)}, bf16[256,128]{1,0:T(8,128)(2,1)S(1)}, u32[]{:S(2)}, u32[]{:S(2)}) collective-permute-start(bf16[256,128]{1,0:T(8,128)(2,1)S(1)} %get-tuple-element.69), channel_id=1, source_target_pairs={{0,2},{1,3},{2,0},{3,1},{4,6},{5,7},{6,4},{7,5},{8,10},{9,11},{10,... | collective-permute-start | bytes 196616 | tf_op jit(solution)/shard_map/ppermute | solution.py:495
  51.4 0.8 %collective-permute-done.22.rest_7_ = bf16[512,128]{1,0:T(8,128)(2,1)S(1)} collective-permute-done((bf16[512,128]{1,0:T(8,128)(2,1)S(1)}, bf16[512,128]{1,0:T(8,128)(2,1)S(1)}, u32[]{:S(2)}, u32[]{:S(2)}) %collective-permute-start.22) | collective-permute-done | bytes 131104 | tf_op jit(solution)/shard_map/ppermute | solution.py:495
  52.8 1.6 %collective-permute-done.26.rest_2_ = bf16[256,128]{1,0:T(8,128)(2,1)S(1)} collective-permute-done((bf16[256,128]{1,0:T(8,128)(2,1)S(1)}, bf16[256,128]{1,0:T(8,128)(2,1)S(1)}, u32[]{:S(2)}, u32[]{:S(2)}) %collective-permute-start.26) | collective-permute-done | bytes 65568 | tf_op jit(solution)/shard_map/ppermute | solution.py:495
  54.4 0.9 %collective-permute-done.27.rest_3_ = bf16[256,128]{1,0:T(8,128)(2,1)S(1)} collective-permute-done((bf16[256,128]{1,0:T(8,128)(2,1)S(1)}, bf16[256,128]{1,0:T(8,128)(2,1)S(1)}, u32[]{:S(2)}, u32[]{:S(2)}) %collective-permute-start.27) | collective-permute-done | bytes 65568 | tf_op jit(solution)/shard_map/ppermute | solution.py:495
  55.3 2.3 %late.1 = f32[2,256,4,256]{3,2,1,0:T(4,128)} custom-call(s32[4,8]{1,0:T(4,128)S(1)} %copy-done.2, bf16[4,128,512]{2,1,0:T(8,128)(2,1)S(1)} %copy-done.3, f32[3,2,256,256]{3,2,1,0:T(8,128)S(1)} %early.1, bf16[256,128]{1,0:T(8,128)(2,1)S(1)} %get-tuple-element.67.rest_0_, bf16[256,128]{1,0:T(8,128)(2,1)S(1)} %collective-permute-done.25.rest_1_, ...), custom_call_target="tpu_custom_call" | custom-call | flops 1724999936 | bytes 1024 | tf_op jit(solution)/shard_map/late/pallas_call | solution.py:480
  (46 shorter events, 6.5 us)
Async XLA Ops:
  3.8 3.2 %collective-permute-start.4 = (bf16[4,16,16,128]{3,2,1,0:T(8,128)(2,1)}, bf16[4,16,16,128]{3,2,1,0:T(8,128)(2,1)S(1)}, u32[]{:S(2)}, u32[]{:S(2)}) collective-permute-start(bf16[4,16,16,128]{3,2,1,0:T(8,128)(2,1)} %get-tuple-element.49.refs_0_), channel_id=1, source_target_pairs={{0,1},{1,0},{2,3},{3,2},{4,5},{5,4},{6,7},{7,6},{8,9},{9,8},{10,11... | collective-permute-start | bytes 786440 | tf_op jit(solution)/shard_map/ppermute | solution.py:495
  4.3 5.6 %collective-permute-start = (bf16[4,4,16,128]{3,2,1,0:T(8,128)(2,1)}, bf16[4,4,16,128]{3,2,1,0:T(8,128)(2,1)S(1)}, u32[]{:S(2)}, u32[]{:S(2)}) collective-permute-start(bf16[4,4,16,128]{3,2,1,0:T(8,128)(2,1)} %get-tuple-element.38), channel_id=1, source_target_pairs={{0,2},{1,3},{2,0},{3,1},{4,6},{5,7},{6,4},{7,5},{8,10},{9,11},{10,... | collective-permute-start | bytes 196616 | tf_op jit(solution)/shard_map/ppermute | solution.py:495
  6.9 4.3 %collective-permute-start.1 = (bf16[4,4,16,128]{3,2,1,0:T(8,128)(2,1)}, bf16[4,4,16,128]{3,2,1,0:T(8,128)(2,1)S(1)}, u32[]{:S(2)}, u32[]{:S(2)}) collective-permute-start(bf16[4,4,16,128]{3,2,1,0:T(8,128)(2,1)} %get-tuple-element.39), channel_id=1, source_target_pairs={{0,3},{1,2},{2,1},{3,0},{4,7},{5,6},{6,5},{7,4},{8,11},{9,10},{10,... | collective-permute-start | bytes 196616 | tf_op jit(solution)/shard_map/ppermute | solution.py:495
  6.9 21.9 %copy-start.2 = (s32[4,8]{1,0:T(4,128)S(1)}, s32[4,8]{1,0:T(4,128)}, u32[]{:S(2)}) copy-start(s32[4,8]{1,0:T(4,128)} %plan.13) | copy-start | bytes 388
  7.8 7.9 %collective-permute-start.6 = (bf16[8,4,16,128]{3,2,1,0:T(8,128)(2,1)S(1)}, bf16[8,4,16,128]{3,2,1,0:T(8,128)(2,1)S(1)}, u32[]{:S(2)}, u32[]{:S(2)}) collective-permute-start(bf16[8,4,16,128]{3,2,1,0:T(8,128)(2,1)S(1)} %pad_maximum_fusion.1), channel_id=1, source_target_pairs={{0,4},{8,0},{16,8},{24,16},{28,24},{20,28},{12,20},{4,12},{1,5},{9... | collective-permute-start | bytes 393224 | tf_op jit(solution)/shard_map/ppermute | solution.py:530
  9.6 6.1 %collective-permute-start.5 = (bf16[8,4,16,128]{3,2,1,0:T(8,128)(2,1)S(1)}, bf16[8,4,16,128]{3,2,1,0:T(8,128)(2,1)S(1)}, u32[]{:S(2)}, u32[]{:S(2)}) collective-permute-start(bf16[8,4,16,128]{3,2,1,0:T(8,128)(2,1)S(1)} %pad_maximum_fusion.1), channel_id=1, source_target_pairs={{0,8},{8,16},{16,24},{24,28},{28,20},{20,12},{12,4},{4,0},{1,9},{9... | collective-permute-start | bytes 393224 | tf_op jit(solution)/shard_map/ppermute | solution.py:527
  11.2 6.6 %collective-permute-start.3 = (bf16[8,4,16,128]{3,2,1,0:T(8,128)(2,1)S(1)}, bf16[8,4,16,128]{3,2,1,0:T(8,128)(2,1)S(1)}, u32[]{:S(2)}, u32[]{:S(2)}) collective-permute-start(bf16[8,4,16,128]{3,2,1,0:T(8,128)(2,1)S(1)} %pad_maximum_fusion), channel_id=1, source_target_pairs={{0,4},{8,0},{16,8},{24,16},{28,24},{20,28},{12,20},{4,12},{1,5},{9... | collective-permute-start | bytes 393224 | tf_op jit(solution)/shard_map/ppermute | solution.py:530
  12.8 5.4 %collective-permute-start.2 = (bf16[8,4,16,128]{3,2,1,0:T(8,128)(2,1)S(1)}, bf16[8,4,16,128]{3,2,1,0:T(8,128)(2,1)S(1)}, u32[]{:S(2)}, u32[]{:S(2)}) collective-permute-start(bf16[8,4,16,128]{3,2,1,0:T(8,128)(2,1)S(1)} %pad_maximum_fusion), channel_id=1, source_target_pairs={{0,8},{8,16},{16,24},{24,28},{28,20},{20,12},{12,4},{4,0},{1,9},{9... | collective-permute-start | bytes 393224 | tf_op jit(solution)/shard_map/ppermute | solution.py:527
  13.3 10.0 %collective-permute-start.11 = (bf16[4,16,16,128]{3,2,1,0:T(8,128)(2,1)}, bf16[4,16,16,128]{3,2,1,0:T(8,128)(2,1)S(1)}, u32[]{:S(2)}, u32[]{:S(2)}) collective-permute-start(bf16[4,16,16,128]{3,2,1,0:T(8,128)(2,1)} %get-tuple-element.49.refs_0_), channel_id=1, source_target_pairs={{0,2},{1,3},{2,0},{3,1},{4,6},{5,7},{6,4},{7,5},{8,10},{9,11},{10,... | collective-permute-start | bytes 786440 | tf_op jit(solution)/shard_map/ppermute | solution.py:495
  14.6 1.0 %copy-start.1 = (bf16[4,16,16,128]{3,2,1,0:T(8,128)(2,1)S(1)}, bf16[4,16,16,128]{3,2,1,0:T(8,128)(2,1)}, u32[]{:S(2)}) copy-start(bf16[4,16,16,128]{3,2,1,0:T(8,128)(2,1)} %get-tuple-element.49.refs_0_) | copy-start | bytes 786436
  15.7 6.4 %collective-permute-start.9 = (bf16[8,4,16,128]{3,2,1,0:T(8,128)(2,1)S(1)}, bf16[8,4,16,128]{3,2,1,0:T(8,128)(2,1)S(1)}, u32[]{:S(2)}, u32[]{:S(2)}) collective-permute-start(bf16[8,4,16,128]{3,2,1,0:T(8,128)(2,1)S(1)} %collective-permute-done.5.rest_0_), channel_id=1, source_target_pairs={{0,8},{8,16},{16,24},{24,28},{28,20},{20,12},{12,4},{4,0},{1,9},{9... | collective-permute-start | bytes 393224 | tf_op jit(solution)/shard_map/ppermute | solution.py:527
  17.3 6.0 %collective-permute-start.10 = (bf16[8,4,16,128]{3,2,1,0:T(8,128)(2,1)S(1)}, bf16[8,4,16,128]{3,2,1,0:T(8,128)(2,1)S(1)}, u32[]{:S(2)}, u32[]{:S(2)}) collective-permute-start(bf16[8,4,16,128]{3,2,1,0:T(8,128)(2,1)S(1)} %collective-permute-done.6.rest_1_), channel_id=1, source_target_pairs={{0,4},{8,0},{16,8},{24,16},{28,24},{20,28},{12,20},{4,12},{1,5},{9... | collective-permute-start | bytes 393224 | tf_op jit(solution)/shard_map/ppermute | solution.py:530
  18.2 5.4 %collective-permute-start.7 = (bf16[8,4,16,128]{3,2,1,0:T(8,128)(2,1)S(1)}, bf16[8,4,16,128]{3,2,1,0:T(8,128)(2,1)S(1)}, u32[]{:S(2)}, u32[]{:S(2)}) collective-permute-start(bf16[8,4,16,128]{3,2,1,0:T(8,128)(2,1)S(1)} %collective-permute-done.2.rest_0_), channel_id=1, source_target_pairs={{0,8},{8,16},{16,24},{24,28},{28,20},{20,12},{12,4},{4,0},{1,9},{9... | collective-permute-start | bytes 393224 | tf_op jit(solution)/shard_map/ppermute | solution.py:527
  19.3 5.4 %collective-permute-start.8 = (bf16[8,4,16,128]{3,2,1,0:T(8,128)(2,1)S(1)}, bf16[8,4,16,128]{3,2,1,0:T(8,128)(2,1)S(1)}, u32[]{:S(2)}, u32[]{:S(2)}) collective-permute-start(bf16[8,4,16,128]{3,2,1,0:T(8,128)(2,1)S(1)} %collective-permute-done.3.rest_1_), channel_id=1, source_target_pairs={{0,4},{8,0},{16,8},{24,16},{28,24},{20,28},{12,20},{4,12},{1,5},{9... | collective-permute-start | bytes 393224 | tf_op jit(solution)/shard_map/ppermute | solution.py:530
  24.8 5.4 %collective-permute-start.12 = (bf16[4,16,16,128]{3,2,1,0:T(8,128)(2,1)S(1)}, bf16[4,16,16,128]{3,2,1,0:T(8,128)(2,1)S(1)}, u32[]{:S(2)}, u32[]{:S(2)}) collective-permute-start(bf16[4,16,16,128]{3,2,1,0:T(8,128)(2,1)S(1)} %collective-permute-done.11.refs_0_), channel_id=1, source_target_pairs={{0,1},{1,0},{2,3},{3,2},{4,5},{5,4},{6,7},{7,6},{8,9},{9,8},{10,11... | collective-permute-start | bytes 786440 | tf_op jit(solution)/shard_map/ppermute | solution.py:495
  24.8 9.4 %collective-permute-start.16 = (bf16[8,4,16,128]{3,2,1,0:T(8,128)(2,1)S(1)}, bf16[8,4,16,128]{3,2,1,0:T(8,128)(2,1)S(1)}, u32[]{:S(2)}, u32[]{:S(2)}) collective-permute-start(bf16[8,4,16,128]{3,2,1,0:T(8,128)(2,1)S(1)} %collective-permute-done.9.rest_2_), channel_id=1, source_target_pairs={{0,8},{8,16},{16,24},{24,28},{28,20},{20,12},{12,4},{4,0},{1,9},{9... | collective-permute-start | bytes 393224 | tf_op jit(solution)/shard_map/ppermute | solution.py:527
  26.3 8.9 %collective-permute-start.17 = (bf16[8,4,16,128]{3,2,1,0:T(8,128)(2,1)S(1)}, bf16[8,4,16,128]{3,2,1,0:T(8,128)(2,1)S(1)}, u32[]{:S(2)}, u32[]{:S(2)}) collective-permute-start(bf16[8,4,16,128]{3,2,1,0:T(8,128)(2,1)S(1)} %collective-permute-done.10.rest_3_), channel_id=1, source_target_pairs={{0,4},{8,0},{16,8},{24,16},{28,24},{20,28},{12,20},{4,12},{1,5},{9... | collective-permute-start | bytes 393224 | tf_op jit(solution)/shard_map/ppermute | solution.py:530
  26.8 13.3 %collective-permute-start.18 = (bf16[8,4,16,128]{3,2,1,0:T(8,128)(2,1)S(1)}, bf16[8,4,16,128]{3,2,1,0:T(8,128)(2,1)S(1)}, u32[]{:S(2)}, u32[]{:S(2)}) collective-permute-start(bf16[8,4,16,128]{3,2,1,0:T(8,128)(2,1)S(1)} %collective-permute-done.7.rest_2_), channel_id=1, source_target_pairs={{0,8},{8,16},{16,24},{24,28},{28,20},{20,12},{12,4},{4,0},{1,9},{9... | collective-permute-start | bytes 393224 | tf_op jit(solution)/shard_map/ppermute | solution.py:527
  28.4 9.6 %collective-permute-start.19 = (bf16[8,4,16,128]{3,2,1,0:T(8,128)(2,1)S(1)}, bf16[8,4,16,128]{3,2,1,0:T(8,128)(2,1)S(1)}, u32[]{:S(2)}, u32[]{:S(2)}) collective-permute-start(bf16[8,4,16,128]{3,2,1,0:T(8,128)(2,1)S(1)} %collective-permute-done.8.rest_3_), channel_id=1, source_target_pairs={{0,4},{8,0},{16,8},{24,16},{28,24},{20,28},{12,20},{4,12},{1,5},{9... | collective-permute-start | bytes 393224 | tf_op jit(solution)/shard_map/ppermute | solution.py:530
  30.1 1.6 %copy-start = (bf16[512,2048]{1,0:T(8,128)(2,1)S(1)}, bf16[512,2048]{1,0:T(8,128)(2,1)}, u32[]{:S(2)}) copy-start(bf16[512,2048]{1,0:T(8,128)(2,1)} %constant.14.clone.table_hbm.table) | copy-start | bytes 6291460
  34.1 5.6 %collective-permute-start.13 = (bf16[256,128]{1,0:T(8,128)(2,1)S(1)}, bf16[256,128]{1,0:T(8,128)(2,1)S(1)}, u32[]{:S(2)}, u32[]{:S(2)}) collective-permute-start(bf16[256,128]{1,0:T(8,128)(2,1)S(1)} %get-tuple-element.53), channel_id=1, source_target_pairs={{0,1},{1,0},{2,3},{3,2},{4,5},{5,4},{6,7},{7,6},{8,9},{9,8},{10,11... | collective-permute-start | bytes 196616 | tf_op jit(solution)/shard_map/ppermute | solution.py:495
  34.1 5.9 %collective-permute-start.14 = (bf16[256,128]{1,0:T(8,128)(2,1)S(1)}, bf16[256,128]{1,0:T(8,128)(2,1)S(1)}, u32[]{:S(2)}, u32[]{:S(2)}) collective-permute-start(bf16[256,128]{1,0:T(8,128)(2,1)S(1)} %get-tuple-element.54), channel_id=1, source_target_pairs={{0,2},{1,3},{2,0},{3,1},{4,6},{5,7},{6,4},{7,5},{8,10},{9,11},{10,... | collective-permute-start | bytes 196616 | tf_op jit(solution)/shard_map/ppermute | solution.py:495
  35.3 4.8 %collective-permute-start.15 = (bf16[256,128]{1,0:T(8,128)(2,1)S(1)}, bf16[256,128]{1,0:T(8,128)(2,1)S(1)}, u32[]{:S(2)}, u32[]{:S(2)}) collective-permute-start(bf16[256,128]{1,0:T(8,128)(2,1)S(1)} %get-tuple-element.55), channel_id=1, source_target_pairs={{0,3},{1,2},{2,1},{3,0},{4,7},{5,6},{6,5},{7,4},{8,11},{9,10},{10,... | collective-permute-start | bytes 196616 | tf_op jit(solution)/shard_map/ppermute | solution.py:495
  38.0 7.8 %collective-permute-start.23 = (bf16[8,4,16,128]{3,2,1,0:T(8,128)(2,1)S(1)}, bf16[8,4,16,128]{3,2,1,0:T(8,128)(2,1)S(1)}, u32[]{:S(2)}, u32[]{:S(2)}) collective-permute-start(bf16[8,4,16,128]{3,2,1,0:T(8,128)(2,1)S(1)} %collective-permute-done.16.rest_4_), channel_id=1, source_target_pairs={{0,8},{8,16},{16,24},{24,28},{28,20},{20,12},{12,4},{4,0},{1,9},{9... | collective-permute-start | bytes 393224 | tf_op jit(solution)/shard_map/ppermute | solution.py:527
  39.6 7.5 %collective-permute-start.24 = (bf16[8,4,16,128]{3,2,1,0:T(8,128)(2,1)S(1)}, bf16[8,4,16,128]{3,2,1,0:T(8,128)(2,1)S(1)}, u32[]{:S(2)}, u32[]{:S(2)}) collective-permute-start(bf16[8,4,16,128]{3,2,1,0:T(8,128)(2,1)S(1)} %collective-permute-done.19.rest_5_), channel_id=1, source_target_pairs={{0,4},{8,0},{16,8},{24,16},{28,24},{20,28},{12,20},{4,12},{1,5},{9... | collective-permute-start | bytes 393224 | tf_op jit(solution)/shard_map/ppermute | solution.py:530
  43.8 7.2 %collective-permute-start.20 = (bf16[512,128]{1,0:T(8,128)(2,1)S(1)}, bf16[512,128]{1,0:T(8,128)(2,1)S(1)}, u32[]{:S(2)}, u32[]{:S(2)}) collective-permute-start(bf16[512,128]{1,0:T(8,128)(2,1)S(1)} %get-tuple-element.61), channel_id=1, source_target_pairs={{0,1},{1,0},{2,3},{3,2},{4,5},{5,4},{6,7},{7,6},{8,9},{9,8},{10,11... | collective-permute-start | bytes 393224 | tf_op jit(solution)/shard_map/ppermute | solution.py:495
  43.9 7.5 %collective-permute-start.21 = (bf16[512,128]{1,0:T(8,128)(2,1)S(1)}, bf16[512,128]{1,0:T(8,128)(2,1)S(1)}, u32[]{:S(2)}, u32[]{:S(2)}) collective-permute-start(bf16[512,128]{1,0:T(8,128)(2,1)S(1)} %get-tuple-element.62), channel_id=1, source_target_pairs={{0,2},{1,3},{2,0},{3,1},{4,6},{5,7},{6,4},{7,5},{8,10},{9,11},{10,... | collective-permute-start | bytes 393224 | tf_op jit(solution)/shard_map/ppermute | solution.py:495
  45.1 7.1 %collective-permute-start.22 = (bf16[512,128]{1,0:T(8,128)(2,1)S(1)}, bf16[512,128]{1,0:T(8,128)(2,1)S(1)}, u32[]{:S(2)}, u32[]{:S(2)}) collective-permute-start(bf16[512,128]{1,0:T(8,128)(2,1)S(1)} %get-tuple-element.63), channel_id=1, source_target_pairs={{0,3},{1,2},{2,1},{3,0},{4,7},{5,6},{6,5},{7,4},{8,11},{9,10},{10,... | collective-permute-start | bytes 393224 | tf_op jit(solution)/shard_map/ppermute | solution.py:495
  47.1 5.1 %copy-start.3 = (bf16[4,128,512]{2,1,0:T(8,128)(2,1)S(1)}, bf16[4,128,512]{2,1,0:T(8,128)(2,1)}, u32[]{:S(2)}) copy-start(bf16[4,128,512]{2,1,0:T(8,128)(2,1)} %constant.15.clone.place) | copy-start | bytes 1572868
  49.5 3.3 %collective-permute-start.25 = (bf16[256,128]{1,0:T(8,128)(2,1)S(1)}, bf16[256,128]{1,0:T(8,128)(2,1)S(1)}, u32[]{:S(2)}, u32[]{:S(2)}) collective-permute-start(bf16[256,128]{1,0:T(8,128)(2,1)S(1)} %get-tuple-element.68), channel_id=1, source_target_pairs={{0,1},{1,0},{2,3},{3,2},{4,5},{5,4},{6,7},{7,6},{8,9},{9,8},{10,11... | collective-permute-start | bytes 196616 | tf_op jit(solution)/shard_map/ppermute | solution.py:495
  49.9 4.5 %collective-permute-start.26 = (bf16[256,128]{1,0:T(8,128)(2,1)S(1)}, bf16[256,128]{1,0:T(8,128)(2,1)S(1)}, u32[]{:S(2)}, u32[]{:S(2)}) collective-permute-start(bf16[256,128]{1,0:T(8,128)(2,1)S(1)} %get-tuple-element.69), channel_id=1, source_target_pairs={{0,2},{1,3},{2,0},{3,1},{4,6},{5,7},{6,4},{7,5},{8,10},{9,11},{10,... | collective-permute-start | bytes 196616 | tf_op jit(solution)/shard_map/ppermute | solution.py:495
  51.0 4.3 %collective-permute-start.27 = (bf16[256,128]{1,0:T(8,128)(2,1)S(1)}, bf16[256,128]{1,0:T(8,128)(2,1)S(1)}, u32[]{:S(2)}, u32[]{:S(2)}) collective-permute-start(bf16[256,128]{1,0:T(8,128)(2,1)S(1)} %get-tuple-element.70), channel_id=1, source_target_pairs={{0,3},{1,2},{2,1},{3,0},{4,7},{5,6},{6,5},{7,4},{8,11},{9,10},{10,... | collective-permute-start | bytes 196616 | tf_op jit(solution)/shard_map/ppermute | solution.py:495

commit v6 on v5

--- a/solution.py
+++ b/solution.py
@@ -164,16 +164,20 @@
             pltpu.VMEM((rows * 2 * TILES, LANES), F32),
             pltpu.SemaphoreType.DMA((2,)),
         ],
-        compiler_params=pltpu.CompilerParams(vmem_limit_bytes=58 * 2**20),
+        compiler_params=pltpu.CompilerParams(vmem_limit_bytes=52 * 2**20),
         cost_estimate=pl.CostEstimate(
             flops=2 * rows * length * 2 * NBIN, bytes_accessed=3 * 2**20, transcendentals=0
         ),
         name="prep",
-    )(records, table)
+    )(
+        pltpu.with_memory_space_constraint(records, pltpu.HBM),
+        pltpu.with_memory_space_constraint(table, pltpu.HBM),
+    )
 
 
 def ring_place(block, count):
-    return jnp.where(block % 2 == 0, block // 2, count - 1 - block // 2)
+    half = block >> 1
+    return jnp.where((block & 1) == 0, half, count - 1 - half)
 
 
 def partner_steps(plan, count):
@@ -181,7 +185,8 @@
     mine = ring_place(me, count)
     steps, keys = [], []
     for number in range(ROUNDS):
-        step = (ring_place(plan[number, me], count) - mine + count) % count
+        step = ring_place(plan[number, me], count) - mine
+        step = jnp.where(step < 0, step + count, step)
         steps.append(step)
         keys.append(jnp.minimum(step, count - step) * ROUNDS + number)
     ranks = []
@@ -225,16 +230,14 @@
         in_specs=[vmem] * len(blocks),
         out_specs=vmem,
         compiler_params=pltpu.CompilerParams(vmem_limit_bytes=16 * 2**20),
-        cost_estimate=expected(0.6),
+        cost_estimate=expected(0.05),
         name="widen",
     )(*blocks)
 
 
-def sum_windows(first_slot, slots, count, offsets, plan, own, candidates, other, before, crossed):
-    windows, stations = own.shape[1:3]
-    quarter = other.shape[3]
-    width = stations * quarter
+def widen_others(first_slot, slots, count, offsets, plan, candidates, first, other):
     steps, ranks = partner_steps(plan, count)
+    windows = candidates[0].shape[0]
     for slot in range(slots):
         step = jnp.int32(0)
         for number in range(ROUNDS):
@@ -246,30 +249,36 @@
                 def widen_other(w, carry):
                     raw = candidate[w].astype(F32)
                     real, imag = raw[:, :TILES], raw[:, TILES:]
-                    other[0, slot, w] = real
-                    other[1, slot, w] = real + imag
-                    other[2, slot, w] = imag - real
+                    other[0, slot, first + w] = real
+                    other[1, slot, first + w] = real + imag
+                    other[2, slot, first + w] = imag - real
                     return carry
 
                 lax.fori_loop(0, windows, widen_other, 0)
 
+
+def sum_windows(owns, other, before, crossed):
+    windows, stations = owns[0].shape[1:3]
+    slots, _, quarter = other.shape[1:4]
+    width = stations * quarter
     group = 4
     groups = stations // group
 
-    def one_group(index, carry):
-        slot = index // groups
-        first = (index % groups) * group
+    def one_group(slot, index):
+        first = index * group
 
         def sums(kind):
             totals = [None] * (group * quarter)
-            for w in range(windows):
-                left = [own[kind, w, first + s] for s in range(group)]
-                right = [other[kind, slot, w, t] for t in range(quarter)]
-                for s in range(group):
-                    for t in range(quarter):
-                        term = left[s] * right[t]
-                        place = s * quarter + t
-                        totals[place] = term if w == 0 else totals[place] + term
+            for part, own in enumerate(owns):
+                for w in range(windows):
+                    left = [own[kind, w, first + s] for s in range(group)]
+                    right = [other[kind, slot, part * windows + w, t] for t in range(quarter)]
+                    for s in range(group):
+                        for t in range(quarter):
+                            term = left[s] * right[t]
+                            place = s * quarter + t
+                            old = totals[place]
+                            totals[place] = term if old is None else old + term
             return totals
 
         def store(place, part, value):
@@ -286,17 +295,21 @@
         second = sums(1)
         for place in range(group * quarter):
             store(place, 1, shared[place] - second[place])
-        return carry
-
-    lax.fori_loop(0, slots * groups, one_group, 0)
+
+    for slot in range(slots):
+
+        def body(index, carry, slot=slot):
+            one_group(slot, index)
+            return carry
+
+        lax.fori_loop(0, groups, body, 0)
 
 
 def near_kernel(first_slot, slots, count, offsets, plan, own, *rest):
     candidates = rest[: len(offsets)]
     crossed, other = rest[len(offsets) :]
-    sum_windows(
-        first_slot, slots, count, offsets, plan, own, candidates, other, None, crossed
-    )
+    widen_others(first_slot, slots, count, offsets, plan, candidates, 0, other)
+    sum_windows([own], other, None, crossed)
 
 
 def near_sums(plan, own, offsets, candidates, first_slot, slots, count):
@@ -311,19 +324,28 @@
         out_specs=vmem,
         scratch_shapes=[pltpu.VMEM((3, slots, windows, quarter, TILES, LANES), F32)],
         compiler_params=pltpu.CompilerParams(vmem_limit_bytes=16 * 2**20),
-        cost_estimate=expected(0.4 + 0.7 * slots),
+        cost_estimate=expected(0.05),
         name="near",
     )(plan, own, *candidates)
 
 
-def far_kernel(first_slot, slots, count, scaling, offsets, parts, plan, table, own, before, *rest):
-    candidates = rest[: len(offsets)]
-    outs = rest[len(offsets) : len(offsets) + parts]
-    other, crossed, operand, result = rest[len(offsets) + parts :]
-    sum_windows(
-        first_slot, slots, count, offsets, plan, own, candidates, other, before, crossed
-    )
-    width = own.shape[2] * other.shape[3]
+def cross_kernel(first_slot, slots, count, scaling, offsets, parts, joint, plan, table, *rest):
+    size = len(offsets)
+    owns, rest = rest[: 1 + joint], rest[1 + joint :]
+    before = None
+    if not joint:
+        before, rest = rest[0], rest[1:]
+    others, rest = rest[: size * (1 + joint)], rest[size * (1 + joint) :]
+    outs = rest[:parts]
+    other, crossed, operand, result = rest[parts:]
+    windows, stations = owns[0].shape[1:3]
+    for part in range(1 + joint):
+        widen_others(
+            first_slot, slots, count, offsets, plan, others[part * size : (part + 1) * size],
+            part * windows, other,
+        )
+    sum_windows(owns, other, before, crossed)
+    width = stations * other.shape[3]
     columns = slots * width
     even = even_lanes((columns, LANES))
     sign_real = lane_cycle([1.0, -1.0, -1.0, 1.0])
@@ -367,31 +389,35 @@
         outs[j][...] = result[me ^ j]
 
 
-def cross_lags(plan, table, own, before, offsets, candidates, first_slot, slots, count, parts, scaling):
-    windows, stations = own.shape[1:3]
+def cross_lags(
+    plan, table, owns, before, offsets, candidates, first_slot, slots, count, parts, scaling
+):
+    joint = len(owns) - 1
+    windows, stations = owns[0].shape[1:3]
     quarter = candidates[0].shape[1]
     columns = slots * stations * quarter
     share = LAGS // parts
     out = (share, columns) if slots > 1 else (share // 2, 2 * columns)
     smem = pl.BlockSpec(memory_space=pltpu.SMEM)
     vmem = pl.BlockSpec(memory_space=pltpu.VMEM)
+    operands = [table, *owns] + ([] if joint else [before]) + list(candidates)
     return pl.pallas_call(
         functools.partial(
-            far_kernel, first_slot, slots, count, scaling, tuple(offsets), parts
+            cross_kernel, first_slot, slots, count, scaling, tuple(offsets), parts, joint
         ),
         out_shape=[jax.ShapeDtypeStruct(out, BF)] * parts,
-        in_specs=[smem] + [vmem] * (3 + len(candidates)),
+        in_specs=[smem] + [vmem] * len(operands),
         out_specs=[vmem] * parts,
         scratch_shapes=[
-            pltpu.VMEM((3, slots, windows, quarter, TILES, LANES), F32),
+            pltpu.VMEM((3, slots, (1 + joint) * windows, quarter, TILES, LANES), F32),
             pltpu.VMEM((columns * 2 * TILES, LANES), F32),
             pltpu.VMEM((CHUNKS * columns, 2 * NBIN), BF),
             pltpu.VMEM((parts,) + out, BF),
         ],
         compiler_params=pltpu.CompilerParams(vmem_limit_bytes=24 * 2**20),
-        cost_estimate=expected(0.5 + 1.2 * slots),
-        name="far",
-    )(plan, table, own, before, *candidates)
+        cost_estimate=expected(1 * (0.6 + 2.0 * slots) if joint else 1.7),
+        name="cross",
+    )(plan, *operands)
 
 
 def slot_rounds(plan, count):
@@ -443,14 +469,14 @@
     rows = half // steps
     rounds = slot_rounds(plan, count)
     matrix = joined_matrix(place, parts)
+    block = placed_block(pieces, matrix, slice(0, half), half)
     copies = []
     for step in range(steps):
         at = slice(step * rows, (step + 1) * rows)
-        block = placed_block(pieces, matrix, at, half)
         for h in range(2):
             for slot in range(ROUNDS - 1):
                 out[h, at, rounds[slot], :] = early[slot, h, at, :]
-            out[h, at, rounds[ROUNDS - 1], :] = block[:, h * pairs : (h + 1) * pairs]
+            out[h, at, rounds[ROUNDS - 1], :] = block[at, h * pairs : (h + 1) * pairs]
             copy = pltpu.make_async_copy(
                 out.at[h, at], out_hbm.at[h, at], sems.at[2 * step + h]
             )
@@ -464,7 +490,7 @@
     pairs = stations * stations
     share = LAGS // parts
     half = share // 2
-    steps = 2
+    steps = 4
     place = jnp.asarray(make_placing(stations, stations // parts, parts))
     vmem = pl.BlockSpec(memory_space=pltpu.VMEM)
     early = pl.pallas_call(
@@ -473,7 +499,7 @@
         in_specs=[vmem] * (1 + len(pieces) - parts),
         out_specs=vmem,
         compiler_params=pltpu.CompilerParams(vmem_limit_bytes=16 * 2**20),
-        cost_estimate=expected(1.0),
+        cost_estimate=expected(0.05),
         name="early",
     )(place, *pieces[:-parts])
     shape = (2, half, ROUNDS, pairs)
@@ -484,7 +510,7 @@
         out_specs=pl.BlockSpec(memory_space=pl.ANY),
         scratch_shapes=[pltpu.VMEM(shape, F32), pltpu.SemaphoreType.DMA((2 * steps,))],
         compiler_params=pltpu.CompilerParams(vmem_limit_bytes=24 * 2**20),
-        cost_estimate=expected(1.5),
+        cost_estimate=expected(0.05),
         name="late",
     )(plan, place, early, *pieces[-parts:])
     return out.reshape(share, ROUNDS, pairs)
@@ -516,8 +542,6 @@
     first = lax.axis_index("seg") * quarter
     near = jnp.concatenate([mine, lax.dynamic_slice_in_dim(sibling, first, quarter, 1)])
     far = jnp.concatenate([swap(piece, 2 + j) for j, piece in enumerate(far)])
-    far, white_far = lax.optimization_barrier((far, white))
-    across = swap(white_far, 2)
 
     ring = sorted(range(count), key=lambda b: b // 2 if b % 2 == 0 else count - 1 - b // 2)
     upward = [(ring[i], ring[(i + 1) % count]) for i in range(count)]
@@ -529,6 +553,8 @@
     def down(value):
         return lax.ppermute(value, "sta", downward)
 
+    far, white_far = lax.optimization_barrier((far, white))
+    across = swap(white_far, 2)
     near_up = near_down = near
     far_up = far_down = far
     near_own = widen_own([white, sibling])
@@ -541,11 +567,9 @@
     def group_lags(index, near_own, far_own):
         first_slot, slots = groups[index]
         at, nears, fars = arrived[index - len(groups)]
-        before = near_sums(plan, near_own, at, nears, first_slot, slots, count)
-        if index == 1:
-            before = after(before, pieces)
         return cross_lags(
-            plan, table, far_own, before, at, fars, first_slot, slots, count, parts, scaling
+            plan, table, [near_own, far_own], None, at, nears + fars, first_slot, slots, count,
+            parts, scaling,
         )
 
     for step in range(1, steps + 1):
@@ -565,10 +589,13 @@
             far_up, far_down, near_up, near_down, across = lax.optimization_barrier(
                 (far_up, far_down, near_up, near_down, across)
             )
-        elif step > 1:
+        elif step > 3:
             far_up, far_down, near_up, near_down = lax.optimization_barrier(
                 (far_up, far_down, near_up, near_down)
             )
+        if step == steps and step > 1:
+            at, nears, _ = arrived[-1]
+            first_sums = near_sums(plan, near_own, at, nears, 0, 1, count)
         far_up, far_down = up(far_up), down(far_down)
         near_up, near_down = next_near
         spots += [count - step, step]
@@ -577,7 +604,11 @@
         arrived.append((list(spots), list(near_blocks), list(far_blocks)))
     far_own = widen_own([across, swap(across, 1)])
     arrived.append(arrived[-1])
-    lags = group_lags(0, near_own, far_own)
+    at, _, fars = arrived[-3]
+    first_sums = after(first_sums, (near_up, near_down))
+    lags = cross_lags(
+        plan, table, [far_own], first_sums, at, fars, 0, 1, count, parts, scaling
+    )
     pieces = exchange(lags)
     if count % 2 == 0:
         near_up = after(near_up, lags)
@@ -587,6 +618,8 @@
             spots + [count // 2], near_blocks + [middle_up], far_blocks + [down(far_down)]
         )
     for index in range(1, len(groups)):
+        if index == 1:
+            near_own = after(near_own, pieces[:parts])
         near_own = after(near_own, lags)
         lags = group_lags(index, near_own, far_own)
         pieces = pieces + exchange(lags)

time: 57.9 us -> 58.6 us (1.012)
  waiting for transfers between devices: 9.62 us -> 15.5 us
  local copies, waits for them, and re-layouts: 2.44 us -> 0.02 us
  Pallas kernels: 19.9 us -> 17.6 us
  other arithmetic: 0.87 us -> 0.03 us
    pallas_call x3 -> x1, Pallas kernels: 4.56 us -> 1.21 us  [near_sums(): pl.pallas_call(functools.partial(near_kernel, first_slot, slots, count, t...]
    ppermute x7, waiting for transfers between devices: 2.59 us -> 5.84 us  [up(): return lax.ppermute(value, 'sta', upward)]
    ppermute x14, waiting for transfers between devices: 4.64 us -> 7.59 us  [swap(): return lax.ppermute(value, 'seg', [(i, i ^ j) for i in range(parts)])]
    unnamed x8 -> x6, local copies, waits for them, and re-layouts: 2.44 us -> 0.02 us
    pallas_call x3, Pallas kernels: 8.49 us -> 10.3 us  [cross_lags(): pl.pallas_call(functools.partial(cross_kernel, first_slot, slots, count,...]
    ppermute x7, starting transfers between devices: 8.33 us -> 7.14 us  [up(): return lax.ppermute(value, 'sta', upward)]
    ppermute x7, starting transfers between devices: 6.07 us -> 7.2 us  [down(): return lax.ppermute(value, 'sta', downward)]
    concatenate x1, other arithmetic: 0.85 us -> 0.02 us  [per_device(): jnp.concatenate([mine, lax.dynamic_slice_in_dim(sibling, first, quarter,...]
  transfers between devices with their start and end apart: 28 -> 28, of which waited for: 9 -> 15; matrix products, arithmetic and copies ran while one was open for 2% -> 0% of each run, Pallas kernels for 24% -> 21%
where the time goes in v6:
time: 58.6 us; the launch traced here: 58.4 us
  starting transfers between devices  25.1 us (43%)
  Pallas kernels  17.6 us (30%)
  waiting for transfers between devices  15.5 us (26%)
    ppermute x14, starting transfers between devices, swap(): return lax.ppermute(value, 'seg', [(i, i ^ j) for i in range(parts)])  10.7 us
    pallas_call x3, Pallas kernels, cross_lags(): pl.pallas_call(functools.partial(cross_kernel, first_slot, slots, count,...  10.3 us
    ppermute x14, waiting for transfers between devices, swap(): return lax.ppermute(value, 'seg', [(i, i ^ j) for i in range(parts)])  7.59 us
    ppermute x7, starting transfers between devices, down(): return lax.ppermute(value, 'sta', downward)  7.2 us
    ppermute x7, starting transfers between devices, up(): return lax.ppermute(value, 'sta', upward)  7.14 us
    ppermute x7, waiting for transfers between devices, up(): return lax.ppermute(value, 'sta', upward)  5.84 us
    pallas_call x1, Pallas kernels, prepare(): pl.pallas_call(functools.partial(prep_kernel, parts), out_shape=[jax.Shap...  3.04 us
    pallas_call x1, Pallas kernels, place_lags(): pl.pallas_call(functools.partial(late_kernel, count, parts, steps), out_s...  2.25 us
  transfers between devices with their start and end apart: 28, of which 15 were waited for; matrix products, arithmetic and copies ran while one was open for 0% of the time, Pallas kernels for 21%

profile of v6, /device:TPU:0, one launch (start us, length us, event | category | flops | bytes accessed | tf_op | source)
XLA Modules:
  0.0 58.4 jit_solution(9934451871340289810)
XLA Ops:
  0.0 3.0 %prep.1 = (bf16[4,16,16,128]{3,2,1,0:T(8,128)(2,1)S(1)}, bf16[4,4,16,128]{3,2,1,0:T(8,128)(2,1)S(1)}, bf16[4,4,16,128]{3,2,1,0:T(8,128)(2,1)S(1)}, bf16[4,4,16,128]{3,2,1,0:T(8,128)(2,1)S(1)}) custom-call(f32[16,4,2048]{2,1,0:T(4,128)} %records_hbm.1, bf16[512,2048]{1,0:T(8,128)(2,1)} %constant.14.clone.table_hbm.table), custom_call_target="tpu_custom_call" | custom-call | flops 536870912 | bytes 3145728 | tf_op jit(solution)/shard_map/prep/pallas_call | solution.py:153
  3.6 2.6 %collective-permute-start = (bf16[4,4,16,128]{3,2,1,0:T(8,128)(2,1)S(1)}, bf16[4,4,16,128]{3,2,1,0:T(8,128)(2,1)S(1)}, u32[]{:S(2)}, u32[]{:S(2)}) collective-permute-start(bf16[4,4,16,128]{3,2,1,0:T(8,128)(2,1)S(1)} %get-tuple-element.39), channel_id=1, source_target_pairs={{0,2},{1,3},{2,0},{3,1},{4,6},{5,7},{6,4},{7,5},{8,10},{9,11},{10,... | collective-permute-start | bytes 196616 | tf_op jit(solution)/shard_map/ppermute | solution.py:521
  6.2 1.8 %collective-permute-start.6 = (bf16[8,4,16,128]{3,2,1,0:T(8,128)(2,1)S(1)}, bf16[8,4,16,128]{3,2,1,0:T(8,128)(2,1)S(1)}, u32[]{:S(2)}, u32[]{:S(2)}) collective-permute-start(bf16[8,4,16,128]{3,2,1,0:T(8,128)(2,1)S(1)} %pad_maximum_fusion.1), channel_id=1, source_target_pairs={{0,4},{8,0},{16,8},{24,16},{28,24},{20,28},{12,20},{4,12},{1,5},{9... | collective-permute-start | bytes 393224 | tf_op jit(solution)/shard_map/ppermute | solution.py:554
  8.8 1.4 %collective-permute-done.1 = bf16[4,4,16,128]{3,2,1,0:T(8,128)(2,1)S(1)} collective-permute-done((bf16[4,4,16,128]{3,2,1,0:T(8,128)(2,1)S(1)}, bf16[4,4,16,128]{3,2,1,0:T(8,128)(2,1)S(1)}, u32[]{:S(2)}, u32[]{:S(2)}) %collective-permute-start.1) | collective-permute-done | bytes 65568 | tf_op jit(solution)/shard_map/ppermute | solution.py:521
  10.2 1.6 %collective-permute-start.3 = (bf16[8,4,16,128]{3,2,1,0:T(8,128)(2,1)S(1)}, bf16[8,4,16,128]{3,2,1,0:T(8,128)(2,1)S(1)}, u32[]{:S(2)}, u32[]{:S(2)}) collective-permute-start(bf16[8,4,16,128]{3,2,1,0:T(8,128)(2,1)S(1)} %pad_maximum_fusion), channel_id=1, source_target_pairs={{0,4},{8,0},{16,8},{24,16},{28,24},{20,28},{12,20},{4,12},{1,5},{9... | collective-permute-start | bytes 393224 | tf_op jit(solution)/shard_map/ppermute | solution.py:554
  12.3 1.3 %collective-permute-start.11 = (bf16[4,16,16,128]{3,2,1,0:T(8,128)(2,1)S(1)}, bf16[4,16,16,128]{3,2,1,0:T(8,128)(2,1)S(1)}, u32[]{:S(2)}, u32[]{:S(2)}) collective-permute-start(bf16[4,16,16,128]{3,2,1,0:T(8,128)(2,1)S(1)} %get-tuple-element.50.refs_0_), channel_id=1, source_target_pairs={{0,2},{1,3},{2,0},{3,1},{4,6},{5,7},{6,4},{7,5},{8,10},{9,11},{10,... | collective-permute-start | bytes 786440 | tf_op jit(solution)/shard_map/ppermute | solution.py:521
  13.8 1.6 %collective-permute-start.9 = (bf16[8,4,16,128]{3,2,1,0:T(8,128)(2,1)S(1)}, bf16[8,4,16,128]{3,2,1,0:T(8,128)(2,1)S(1)}, u32[]{:S(2)}, u32[]{:S(2)}) collective-permute-start(bf16[8,4,16,128]{3,2,1,0:T(8,128)(2,1)S(1)} %collective-permute-done.5.rest_0_.rest_2_), channel_id=1, source_target_pairs={{0,8},{8,16},{16,24},{24,28},{28,20},{20,12},{12,4},{4,0},{1,9},{9... | collective-permute-start | bytes 393224 | tf_op jit(solution)/shard_map/ppermute | solution.py:551
  16.1 2.0 %collective-permute-done.2.rest_2_.rest_8_.rest_9_ = bf16[8,4,16,128]{3,2,1,0:T(8,128)(2,1)S(1)} collective-permute-done((bf16[8,4,16,128]{3,2,1,0:T(8,128)(2,1)S(1)}, bf16[8,4,16,128]{3,2,1,0:T(8,128)(2,1)S(1)}, u32[]{:S(2)}, u32[]{:S(2)}) %collective-permute-start.2) | collective-permute-done | bytes 131104 | tf_op jit(solution)/shard_map/ppermute | solution.py:551
  18.1 2.0 %collective-permute-start.8 = (bf16[8,4,16,128]{3,2,1,0:T(8,128)(2,1)S(1)}, bf16[8,4,16,128]{3,2,1,0:T(8,128)(2,1)S(1)}, u32[]{:S(2)}, u32[]{:S(2)}) collective-permute-start(bf16[8,4,16,128]{3,2,1,0:T(8,128)(2,1)S(1)} %collective-permute-done.3.rest_3_.rest_9_.rest_10_), channel_id=1, source_target_pairs={{0,4},{8,0},{16,8},{24,16},{28,24},{20,28},{12,20},{4,12},{1,5},{9... | collective-permute-start | bytes 393224 | tf_op jit(solution)/shard_map/ppermute | solution.py:554
  20.1 0.8 %collective-permute-done.9.rest_2_.rest_4_ = bf16[8,4,16,128]{3,2,1,0:T(8,128)(2,1)S(1)} collective-permute-done((bf16[8,4,16,128]{3,2,1,0:T(8,128)(2,1)S(1)}, bf16[8,4,16,128]{3,2,1,0:T(8,128)(2,1)S(1)}, u32[]{:S(2)}, u32[]{:S(2)}) %collective-permute-start.9) | collective-permute-done | bytes 131104 | tf_op jit(solution)/shard_map/ppermute | solution.py:551
  21.1 2.0 %collective-permute-done.7.rest_4_.rest_10_.rest_11_ = bf16[8,4,16,128]{3,2,1,0:T(8,128)(2,1)S(1)} collective-permute-done((bf16[8,4,16,128]{3,2,1,0:T(8,128)(2,1)S(1)}, bf16[8,4,16,128]{3,2,1,0:T(8,128)(2,1)S(1)}, u32[]{:S(2)}, u32[]{:S(2)}) %collective-permute-start.7) | collective-permute-done | bytes 131104 | tf_op jit(solution)/shard_map/ppermute | solution.py:551
  23.2 1.6 %collective-permute-start.13 = (bf16[8,4,16,128]{3,2,1,0:T(8,128)(2,1)S(1)}, bf16[8,4,16,128]{3,2,1,0:T(8,128)(2,1)S(1)}, u32[]{:S(2)}, u32[]{:S(2)}) collective-permute-start(bf16[8,4,16,128]{3,2,1,0:T(8,128)(2,1)S(1)} %collective-permute-done.9.rest_2_.rest_4_), channel_id=1, source_target_pairs={{0,8},{8,16},{16,24},{24,28},{28,20},{20,12},{12,4},{4,0},{1,9},{9... | collective-permute-start | bytes 393224 | tf_op jit(solution)/shard_map/ppermute | solution.py:551
  25.2 1.6 %collective-permute-start.18 = (bf16[8,4,16,128]{3,2,1,0:T(8,128)(2,1)S(1)}, bf16[8,4,16,128]{3,2,1,0:T(8,128)(2,1)S(1)}, u32[]{:S(2)}, u32[]{:S(2)}) collective-permute-start(bf16[8,4,16,128]{3,2,1,0:T(8,128)(2,1)S(1)} %collective-permute-done.7.rest_4_.rest_10_.rest_11_), channel_id=1, source_target_pairs={{0,8},{8,16},{16,24},{24,28},{28,20},{20,12},{12,4},{4,0},{1,9},{9... | collective-permute-start | bytes 393224 | tf_op jit(solution)/shard_map/ppermute | solution.py:551
  27.2 1.2 %near.1.rest_1_ = f32[1024,128]{1,0:T(8,128)S(1)} custom-call(s32[4,8]{1,0:T(4,128)S(1)} %copy-done.2, f32[3,8,16,8,128]{4,3,2,1,0:T(8,128)S(1)} %widen.2.own.rest_0_, bf16[8,4,16,128]{3,2,1,0:T(8,128)(2,1)S(1)} %collective-permute-done.5.rest_0_.rest_2_, bf16[8,4,16,128]{3,2,1,0:T(8,128)(2,1)S(1)} %collective-permute-done.6.rest_1_.rest_3_, ...), custom_call_target="tpu_custom_call" | custom-call | flops 57500000 | bytes 1024 | tf_op jit(solution)/shard_map/near/pallas_call | solution.py:320
  28.5 1.1 %collective-permute-done.13.rest_6_ = bf16[8,4,16,128]{3,2,1,0:T(8,128)(2,1)S(1)} collective-permute-done((bf16[8,4,16,128]{3,2,1,0:T(8,128)(2,1)S(1)}, bf16[8,4,16,128]{3,2,1,0:T(8,128)(2,1)S(1)}, u32[]{:S(2)}, u32[]{:S(2)}) %collective-permute-start.13) | collective-permute-done | bytes 131104 | tf_op jit(solution)/shard_map/ppermute | solution.py:551
  29.6 1.5 %collective-permute-done.14.rest_7_ = bf16[8,4,16,128]{3,2,1,0:T(8,128)(2,1)S(1)} collective-permute-done((bf16[8,4,16,128]{3,2,1,0:T(8,128)(2,1)S(1)}, bf16[8,4,16,128]{3,2,1,0:T(8,128)(2,1)S(1)}, u32[]{:S(2)}, u32[]{:S(2)}) %collective-permute-start.14) | collective-permute-done | bytes 131104 | tf_op jit(solution)/shard_map/ppermute | solution.py:554
  31.2 2.3 %cross.3 = (bf16[256,128]{1,0:T(8,128)(2,1)S(1)}, bf16[256,128]{1,0:T(8,128)(2,1)S(1)}, bf16[256,128]{1,0:T(8,128)(2,1)S(1)}, bf16[256,128]{1,0:T(8,128)(2,1)S(1)}) custom-call(s32[4,8]{1,0:T(4,128)S(1)} %copy-done.2, bf16[512,2048]{1,0:T(8,128)(2,1)S(1)} %copy-done, f32[3,8,16,8,128]{4,3,2,1,0:T(8,128)S(1)} %widen.3.rest_0_.rest_1_, ...), custom_call_target="tpu_custom_call" | custom-call | flops 1955000064 | bytes 1024 | tf_op jit(solution)/shard_map/cross/pallas_call | solution.py:404
  33.6 1.8 %collective-permute-start.16 = (bf16[256,128]{1,0:T(8,128)(2,1)S(1)}, bf16[256,128]{1,0:T(8,128)(2,1)S(1)}, u32[]{:S(2)}, u32[]{:S(2)}) collective-permute-start(bf16[256,128]{1,0:T(8,128)(2,1)S(1)} %get-tuple-element.56), channel_id=1, source_target_pairs={{0,2},{1,3},{2,0},{3,1},{4,6},{5,7},{6,4},{7,5},{8,10},{9,11},{10,... | collective-permute-start | bytes 196616 | tf_op jit(solution)/shard_map/ppermute | solution.py:521
  35.5 1.6 %collective-permute-start.23 = (bf16[8,4,16,128]{3,2,1,0:T(8,128)(2,1)S(1)}, bf16[8,4,16,128]{3,2,1,0:T(8,128)(2,1)S(1)}, u32[]{:S(2)}, u32[]{:S(2)}) collective-permute-start(bf16[8,4,16,128]{3,2,1,0:T(8,128)(2,1)S(1)} %collective-permute-done.13.rest_6_), channel_id=1, source_target_pairs={{0,8},{8,16},{16,24},{24,28},{28,20},{20,12},{12,4},{4,0},{1,9},{9... | collective-permute-start | bytes 393224 | tf_op jit(solution)/shard_map/ppermute | solution.py:551
  37.5 0.6 %collective-permute-done.16.rest_2_ = bf16[256,128]{1,0:T(8,128)(2,1)S(1)} collective-permute-done((bf16[256,128]{1,0:T(8,128)(2,1)S(1)}, bf16[256,128]{1,0:T(8,128)(2,1)S(1)}, u32[]{:S(2)}, u32[]{:S(2)}) %collective-permute-start.16) | collective-permute-done | bytes 65568 | tf_op jit(solution)/shard_map/ppermute | solution.py:521
  38.1 1.4 %collective-permute-done.17.rest_3_ = bf16[256,128]{1,0:T(8,128)(2,1)S(1)} collective-permute-done((bf16[256,128]{1,0:T(8,128)(2,1)S(1)}, bf16[256,128]{1,0:T(8,128)(2,1)S(1)}, u32[]{:S(2)}, u32[]{:S(2)}) %collective-permute-start.17) | collective-permute-done | bytes 65568 | tf_op jit(solution)/shard_map/ppermute | solution.py:521
  39.5 5.0 %cross.4 = (bf16[512,128]{1,0:T(8,128)(2,1)S(1)}, bf16[512,128]{1,0:T(8,128)(2,1)S(1)}, bf16[512,128]{1,0:T(8,128)(2,1)S(1)}, bf16[512,128]{1,0:T(8,128)(2,1)S(1)}) custom-call(s32[4,8]{1,0:T(4,128)S(1)} %copy-done.2, bf16[512,2048]{1,0:T(8,128)(2,1)S(1)} %copy-done, f32[3,8,16,8,128]{4,3,2,1,0:T(8,128)S(1)} %widen.2.own.rest_0_, ...), custom_call_target="tpu_custom_call" | custom-call | flops 5289999872 | bytes 1024 | tf_op jit(solution)/shard_map/cross/pallas_call | solution.py:404
  44.5 0.5 collective-permute-start.20
  45.0 1.5 %collective-permute-start.21 = (bf16[512,128]{1,0:T(8,128)(2,1)S(1)}, bf16[512,128]{1,0:T(8,128)(2,1)S(1)}, u32[]{:S(2)}, u32[]{:S(2)}) collective-permute-start(bf16[512,128]{1,0:T(8,128)(2,1)S(1)} %get-tuple-element.64), channel_id=1, source_target_pairs={{0,2},{1,3},{2,0},{3,1},{4,6},{5,7},{6,4},{7,5},{8,10},{9,11},{10,... | collective-permute-start | bytes 393224 | tf_op jit(solution)/shard_map/ppermute | solution.py:521
  46.6 3.0 %cross.5 = (bf16[256,128]{1,0:T(8,128)(2,1)S(1)}, bf16[256,128]{1,0:T(8,128)(2,1)S(1)}, bf16[256,128]{1,0:T(8,128)(2,1)S(1)}, bf16[256,128]{1,0:T(8,128)(2,1)S(1)}) custom-call(s32[4,8]{1,0:T(4,128)S(1)} %copy-done.2, bf16[512,2048]{1,0:T(8,128)(2,1)S(1)} %copy-done, f32[3,8,16,8,128]{4,3,2,1,0:T(8,128)S(1)} %widen.2.own.rest_0_, ...), custom_call_target="tpu_custom_call" | custom-call | flops 2990000128 | bytes 1024 | tf_op jit(solution)/shard_map/cross/pallas_call | solution.py:404
  49.6 0.7 %collective-permute-start.25 = (bf16[256,128]{1,0:T(8,128)(2,1)S(1)}, bf16[256,128]{1,0:T(8,128)(2,1)S(1)}, u32[]{:S(2)}, u32[]{:S(2)}) collective-permute-start(bf16[256,128]{1,0:T(8,128)(2,1)S(1)} %get-tuple-element.70), channel_id=1, source_target_pairs={{0,1},{1,0},{2,3},{3,2},{4,5},{5,4},{6,7},{7,6},{8,9},{9,8},{10,11... | collective-permute-start | bytes 196616 | tf_op jit(solution)/shard_map/ppermute | solution.py:521
  50.3 1.5 %collective-permute-start.26 = (bf16[256,128]{1,0:T(8,128)(2,1)S(1)}, bf16[256,128]{1,0:T(8,128)(2,1)S(1)}, u32[]{:S(2)}, u32[]{:S(2)}) collective-permute-start(bf16[256,128]{1,0:T(8,128)(2,1)S(1)} %get-tuple-element.71), channel_id=1, source_target_pairs={{0,2},{1,3},{2,0},{3,1},{4,6},{5,7},{6,4},{7,5},{8,10},{9,11},{10,... | collective-permute-start | bytes 196616 | tf_op jit(solution)/shard_map/ppermute | solution.py:521
  51.8 0.9 %collective-permute-done.22.rest_7_ = bf16[512,128]{1,0:T(8,128)(2,1)S(1)} collective-permute-done((bf16[512,128]{1,0:T(8,128)(2,1)S(1)}, bf16[512,128]{1,0:T(8,128)(2,1)S(1)}, u32[]{:S(2)}, u32[]{:S(2)}) %collective-permute-start.22) | collective-permute-done | bytes 131104 | tf_op jit(solution)/shard_map/ppermute | solution.py:521
  52.7 0.6 early.1
  53.3 1.5 %collective-permute-done.26.rest_2_ = bf16[256,128]{1,0:T(8,128)(2,1)S(1)} collective-permute-done((bf16[256,128]{1,0:T(8,128)(2,1)S(1)}, bf16[256,128]{1,0:T(8,128)(2,1)S(1)}, u32[]{:S(2)}, u32[]{:S(2)}) %collective-permute-start.26) | collective-permute-done | bytes 65568 | tf_op jit(solution)/shard_map/ppermute | solution.py:521
  54.7 1.5 %collective-permute-done.27.rest_3_ = bf16[256,128]{1,0:T(8,128)(2,1)S(1)} collective-permute-done((bf16[256,128]{1,0:T(8,128)(2,1)S(1)}, bf16[256,128]{1,0:T(8,128)(2,1)S(1)}, u32[]{:S(2)}, u32[]{:S(2)}) %collective-permute-start.27) | collective-permute-done | bytes 65568 | tf_op jit(solution)/shard_map/ppermute | solution.py:521
  56.2 2.2 %late.1 = f32[2,256,4,256]{3,2,1,0:T(4,128)} custom-call(s32[4,8]{1,0:T(4,128)S(1)} %copy-done.2, bf16[4,128,512]{2,1,0:T(8,128)(2,1)S(1)} %copy-done.1, f32[3,2,256,256]{3,2,1,0:T(8,128)S(1)} %early.1, bf16[256,128]{1,0:T(8,128)(2,1)S(1)} %get-tuple-element.69.rest_0_, bf16[256,128]{1,0:T(8,128)(2,1)S(1)} %collective-permute-done.25.rest_1_, ...), custom_call_target="tpu_custom_call" | custom-call | flops 57500000 | bytes 1024 | tf_op jit(solution)/shard_map/late/pallas_call | solution.py:506
  (42 shorter events, 4.7 us)
Async XLA Ops:
  3.0 24.2 %copy-start.2 = (s32[4,8]{1,0:T(4,128)S(1)}, s32[4,8]{1,0:T(4,128)}, u32[]{:S(2)}) copy-start(s32[4,8]{1,0:T(4,128)} %plan.9) | copy-start | bytes 388
  3.1 3.2 %collective-permute-start.4 = (bf16[4,16,16,128]{3,2,1,0:T(8,128)(2,1)S(1)}, bf16[4,16,16,128]{3,2,1,0:T(8,128)(2,1)S(1)}, u32[]{:S(2)}, u32[]{:S(2)}) collective-permute-start(bf16[4,16,16,128]{3,2,1,0:T(8,128)(2,1)S(1)} %get-tuple-element.50.refs_0_), channel_id=1, source_target_pairs={{0,1},{1,0},{2,3},{3,2},{4,5},{5,4},{6,7},{7,6},{8,9},{9,8},{10,11... | collective-permute-start | bytes 786440 | tf_op jit(solution)/shard_map/ppermute | solution.py:521
  3.6 5.3 %collective-permute-start = (bf16[4,4,16,128]{3,2,1,0:T(8,128)(2,1)S(1)}, bf16[4,4,16,128]{3,2,1,0:T(8,128)(2,1)S(1)}, u32[]{:S(2)}, u32[]{:S(2)}) collective-permute-start(bf16[4,4,16,128]{3,2,1,0:T(8,128)(2,1)S(1)} %get-tuple-element.39), channel_id=1, source_target_pairs={{0,2},{1,3},{2,0},{3,1},{4,6},{5,7},{6,4},{7,5},{8,10},{9,11},{10,... | collective-permute-start | bytes 196616 | tf_op jit(solution)/shard_map/ppermute | solution.py:521
  6.1 4.0 %collective-permute-start.1 = (bf16[4,4,16,128]{3,2,1,0:T(8,128)(2,1)S(1)}, bf16[4,4,16,128]{3,2,1,0:T(8,128)(2,1)S(1)}, u32[]{:S(2)}, u32[]{:S(2)}) collective-permute-start(bf16[4,4,16,128]{3,2,1,0:T(8,128)(2,1)S(1)} %get-tuple-element.40), channel_id=1, source_target_pairs={{0,3},{1,2},{2,1},{3,0},{4,7},{5,6},{6,5},{7,4},{8,11},{9,10},{10,... | collective-permute-start | bytes 196616 | tf_op jit(solution)/shard_map/ppermute | solution.py:521
  6.2 7.5 %collective-permute-start.6 = (bf16[8,4,16,128]{3,2,1,0:T(8,128)(2,1)S(1)}, bf16[8,4,16,128]{3,2,1,0:T(8,128)(2,1)S(1)}, u32[]{:S(2)}, u32[]{:S(2)}) collective-permute-start(bf16[8,4,16,128]{3,2,1,0:T(8,128)(2,1)S(1)} %pad_maximum_fusion.1), channel_id=1, source_target_pairs={{0,4},{8,0},{16,8},{24,16},{28,24},{20,28},{12,20},{4,12},{1,5},{9... | collective-permute-start | bytes 393224 | tf_op jit(solution)/shard_map/ppermute | solution.py:554
  8.1 5.7 %collective-permute-start.5 = (bf16[8,4,16,128]{3,2,1,0:T(8,128)(2,1)S(1)}, bf16[8,4,16,128]{3,2,1,0:T(8,128)(2,1)S(1)}, u32[]{:S(2)}, u32[]{:S(2)}) collective-permute-start(bf16[8,4,16,128]{3,2,1,0:T(8,128)(2,1)S(1)} %pad_maximum_fusion.1), channel_id=1, source_target_pairs={{0,8},{8,16},{16,24},{24,28},{28,20},{20,12},{12,4},{4,0},{1,9},{9... | collective-permute-start | bytes 393224 | tf_op jit(solution)/shard_map/ppermute | solution.py:551
  10.2 5.9 %collective-permute-start.3 = (bf16[8,4,16,128]{3,2,1,0:T(8,128)(2,1)S(1)}, bf16[8,4,16,128]{3,2,1,0:T(8,128)(2,1)S(1)}, u32[]{:S(2)}, u32[]{:S(2)}) collective-permute-start(bf16[8,4,16,128]{3,2,1,0:T(8,128)(2,1)S(1)} %pad_maximum_fusion), channel_id=1, source_target_pairs={{0,4},{8,0},{16,8},{24,16},{28,24},{20,28},{12,20},{4,12},{1,5},{9... | collective-permute-start | bytes 393224 | tf_op jit(solution)/shard_map/ppermute | solution.py:554
  11.8 6.3 %collective-permute-start.2 = (bf16[8,4,16,128]{3,2,1,0:T(8,128)(2,1)S(1)}, bf16[8,4,16,128]{3,2,1,0:T(8,128)(2,1)S(1)}, u32[]{:S(2)}, u32[]{:S(2)}) collective-permute-start(bf16[8,4,16,128]{3,2,1,0:T(8,128)(2,1)S(1)} %pad_maximum_fusion), channel_id=1, source_target_pairs={{0,8},{8,16},{16,24},{24,28},{28,20},{20,12},{12,4},{4,0},{1,9},{9... | collective-permute-start | bytes 393224 | tf_op jit(solution)/shard_map/ppermute | solution.py:551
  12.3 8.8 %collective-permute-start.11 = (bf16[4,16,16,128]{3,2,1,0:T(8,128)(2,1)S(1)}, bf16[4,16,16,128]{3,2,1,0:T(8,128)(2,1)S(1)}, u32[]{:S(2)}, u32[]{:S(2)}) collective-permute-start(bf16[4,16,16,128]{3,2,1,0:T(8,128)(2,1)S(1)} %get-tuple-element.50.refs_0_), channel_id=1, source_target_pairs={{0,2},{1,3},{2,0},{3,1},{4,6},{5,7},{6,4},{7,5},{8,10},{9,11},{10,... | collective-permute-start | bytes 786440 | tf_op jit(solution)/shard_map/ppermute | solution.py:521
  13.8 7.1 %collective-permute-start.9 = (bf16[8,4,16,128]{3,2,1,0:T(8,128)(2,1)S(1)}, bf16[8,4,16,128]{3,2,1,0:T(8,128)(2,1)S(1)}, u32[]{:S(2)}, u32[]{:S(2)}) collective-permute-start(bf16[8,4,16,128]{3,2,1,0:T(8,128)(2,1)S(1)} %collective-permute-done.5.rest_0_.rest_2_), channel_id=1, source_target_pairs={{0,8},{8,16},{16,24},{24,28},{28,20},{20,12},{12,4},{4,0},{1,9},{9... | collective-permute-start | bytes 393224 | tf_op jit(solution)/shard_map/ppermute | solution.py:551
  15.4 5.7 %collective-permute-start.10 = (bf16[8,4,16,128]{3,2,1,0:T(8,128)(2,1)S(1)}, bf16[8,4,16,128]{3,2,1,0:T(8,128)(2,1)S(1)}, u32[]{:S(2)}, u32[]{:S(2)}) collective-permute-start(bf16[8,4,16,128]{3,2,1,0:T(8,128)(2,1)S(1)} %collective-permute-done.6.rest_1_.rest_3_), channel_id=1, source_target_pairs={{0,4},{8,0},{16,8},{24,16},{28,24},{20,28},{12,20},{4,12},{1,5},{9... | collective-permute-start | bytes 393224 | tf_op jit(solution)/shard_map/ppermute | solution.py:554
  18.1 5.0 %collective-permute-start.7 = (bf16[8,4,16,128]{3,2,1,0:T(8,128)(2,1)S(1)}, bf16[8,4,16,128]{3,2,1,0:T(8,128)(2,1)S(1)}, u32[]{:S(2)}, u32[]{:S(2)}) collective-permute-start(bf16[8,4,16,128]{3,2,1,0:T(8,128)(2,1)S(1)} %collective-permute-done.2.rest_2_.rest_8_.rest_9_), channel_id=1, source_target_pairs={{0,8},{8,16},{16,24},{24,28},{28,20},{20,12},{12,4},{4,0},{1,9},{9... | collective-permute-start | bytes 393224 | tf_op jit(solution)/shard_map/ppermute | solution.py:551
  18.1 5.1 %collective-permute-start.8 = (bf16[8,4,16,128]{3,2,1,0:T(8,128)(2,1)S(1)}, bf16[8,4,16,128]{3,2,1,0:T(8,128)(2,1)S(1)}, u32[]{:S(2)}, u32[]{:S(2)}) collective-permute-start(bf16[8,4,16,128]{3,2,1,0:T(8,128)(2,1)S(1)} %collective-permute-done.3.rest_3_.rest_9_.rest_10_), channel_id=1, source_target_pairs={{0,4},{8,0},{16,8},{24,16},{28,24},{20,28},{12,20},{4,12},{1,5},{9... | collective-permute-start | bytes 393224 | tf_op jit(solution)/shard_map/ppermute | solution.py:554
  23.2 7.9 %collective-permute-start.12 = (bf16[4,16,16,128]{3,2,1,0:T(8,128)(2,1)S(1)}, bf16[4,16,16,128]{3,2,1,0:T(8,128)(2,1)S(1)}, u32[]{:S(2)}, u32[]{:S(2)}) collective-permute-start(bf16[4,16,16,128]{3,2,1,0:T(8,128)(2,1)S(1)} %collective-permute-done.11.refs_0_), channel_id=1, source_target_pairs={{0,1},{1,0},{2,3},{3,2},{4,5},{5,4},{6,7},{7,6},{8,9},{9,8},{10,11... | collective-permute-start | bytes 786440 | tf_op jit(solution)/shard_map/ppermute | solution.py:521
  23.2 6.4 %collective-permute-start.13 = (bf16[8,4,16,128]{3,2,1,0:T(8,128)(2,1)S(1)}, bf16[8,4,16,128]{3,2,1,0:T(8,128)(2,1)S(1)}, u32[]{:S(2)}, u32[]{:S(2)}) collective-permute-start(bf16[8,4,16,128]{3,2,1,0:T(8,128)(2,1)S(1)} %collective-permute-done.9.rest_2_.rest_4_), channel_id=1, source_target_pairs={{0,8},{8,16},{16,24},{24,28},{28,20},{20,12},{12,4},{4,0},{1,9},{9... | collective-permute-start | bytes 393224 | tf_op jit(solution)/shard_map/ppermute | solution.py:551
  24.8 6.3 %collective-permute-start.14 = (bf16[8,4,16,128]{3,2,1,0:T(8,128)(2,1)S(1)}, bf16[8,4,16,128]{3,2,1,0:T(8,128)(2,1)S(1)}, u32[]{:S(2)}, u32[]{:S(2)}) collective-permute-start(bf16[8,4,16,128]{3,2,1,0:T(8,128)(2,1)S(1)} %collective-permute-done.10.rest_3_.rest_5_), channel_id=1, source_target_pairs={{0,4},{8,0},{16,8},{24,16},{28,24},{20,28},{12,20},{4,12},{1,5},{9... | collective-permute-start | bytes 393224 | tf_op jit(solution)/shard_map/ppermute | solution.py:554
  25.2 14.3 %collective-permute-start.18 = (bf16[8,4,16,128]{3,2,1,0:T(8,128)(2,1)S(1)}, bf16[8,4,16,128]{3,2,1,0:T(8,128)(2,1)S(1)}, u32[]{:S(2)}, u32[]{:S(2)}) collective-permute-start(bf16[8,4,16,128]{3,2,1,0:T(8,128)(2,1)S(1)} %collective-permute-done.7.rest_4_.rest_10_.rest_11_), channel_id=1, source_target_pairs={{0,8},{8,16},{16,24},{24,28},{28,20},{20,12},{12,4},{4,0},{1,9},{9... | collective-permute-start | bytes 393224 | tf_op jit(solution)/shard_map/ppermute | solution.py:551
  26.8 8.7 %collective-permute-start.19 = (bf16[8,4,16,128]{3,2,1,0:T(8,128)(2,1)S(1)}, bf16[8,4,16,128]{3,2,1,0:T(8,128)(2,1)S(1)}, u32[]{:S(2)}, u32[]{:S(2)}) collective-permute-start(bf16[8,4,16,128]{3,2,1,0:T(8,128)(2,1)S(1)} %collective-permute-done.8.rest_5_.rest_11_.rest_12_), channel_id=1, source_target_pairs={{0,4},{8,0},{16,8},{24,16},{28,24},{20,28},{12,20},{4,12},{1,5},{9... | collective-permute-start | bytes 393224 | tf_op jit(solution)/shard_map/ppermute | solution.py:554
  28.5 2.8 %copy-start = (bf16[512,2048]{1,0:T(8,128)(2,1)S(1)}, bf16[512,2048]{1,0:T(8,128)(2,1)}, u32[]{:S(2)}) copy-start(bf16[512,2048]{1,0:T(8,128)(2,1)} %constant.14.clone.table_hbm.table) | copy-start | bytes 6291460
  33.5 3.6 %collective-permute-start.15 = (bf16[256,128]{1,0:T(8,128)(2,1)S(1)}, bf16[256,128]{1,0:T(8,128)(2,1)S(1)}, u32[]{:S(2)}, u32[]{:S(2)}) collective-permute-start(bf16[256,128]{1,0:T(8,128)(2,1)S(1)} %get-tuple-element.55), channel_id=1, source_target_pairs={{0,1},{1,0},{2,3},{3,2},{4,5},{5,4},{6,7},{7,6},{8,9},{9,8},{10,11... | collective-permute-start | bytes 196616 | tf_op jit(solution)/shard_map/ppermute | solution.py:521
  33.6 4.5 %collective-permute-start.16 = (bf16[256,128]{1,0:T(8,128)(2,1)S(1)}, bf16[256,128]{1,0:T(8,128)(2,1)S(1)}, u32[]{:S(2)}, u32[]{:S(2)}) collective-permute-start(bf16[256,128]{1,0:T(8,128)(2,1)S(1)} %get-tuple-element.56), channel_id=1, source_target_pairs={{0,2},{1,3},{2,0},{3,1},{4,6},{5,7},{6,4},{7,5},{8,10},{9,11},{10,... | collective-permute-start | bytes 196616 | tf_op jit(solution)/shard_map/ppermute | solution.py:521
  35.4 4.0 %collective-permute-start.17 = (bf16[256,128]{1,0:T(8,128)(2,1)S(1)}, bf16[256,128]{1,0:T(8,128)(2,1)S(1)}, u32[]{:S(2)}, u32[]{:S(2)}) collective-permute-start(bf16[256,128]{1,0:T(8,128)(2,1)S(1)} %get-tuple-element.57), channel_id=1, source_target_pairs={{0,3},{1,2},{2,1},{3,0},{4,7},{5,6},{6,5},{7,4},{8,11},{9,10},{10,... | collective-permute-start | bytes 196616 | tf_op jit(solution)/shard_map/ppermute | solution.py:521
  35.5 11.1 %collective-permute-start.23 = (bf16[8,4,16,128]{3,2,1,0:T(8,128)(2,1)S(1)}, bf16[8,4,16,128]{3,2,1,0:T(8,128)(2,1)S(1)}, u32[]{:S(2)}, u32[]{:S(2)}) collective-permute-start(bf16[8,4,16,128]{3,2,1,0:T(8,128)(2,1)S(1)} %collective-permute-done.13.rest_6_), channel_id=1, source_target_pairs={{0,8},{8,16},{16,24},{24,28},{28,20},{20,12},{12,4},{4,0},{1,9},{9... | collective-permute-start | bytes 393224 | tf_op jit(solution)/shard_map/ppermute | solution.py:551
  37.1 9.5 %collective-permute-start.24 = (bf16[8,4,16,128]{3,2,1,0:T(8,128)(2,1)S(1)}, bf16[8,4,16,128]{3,2,1,0:T(8,128)(2,1)S(1)}, u32[]{:S(2)}, u32[]{:S(2)}) collective-permute-start(bf16[8,4,16,128]{3,2,1,0:T(8,128)(2,1)S(1)} %collective-permute-done.19.rest_13_.rest_14_), channel_id=1, source_target_pairs={{0,4},{8,0},{16,8},{24,16},{28,24},{20,28},{12,20},{4,12},{1,5},{9... | collective-permute-start | bytes 393224 | tf_op jit(solution)/shard_map/ppermute | solution.py:554
  44.5 7.3 %collective-permute-start.20 = (bf16[512,128]{1,0:T(8,128)(2,1)S(1)}, bf16[512,128]{1,0:T(8,128)(2,1)S(1)}, u32[]{:S(2)}, u32[]{:S(2)}) collective-permute-start(bf16[512,128]{1,0:T(8,128)(2,1)S(1)} %get-tuple-element.63), channel_id=1, source_target_pairs={{0,1},{1,0},{2,3},{3,2},{4,5},{5,4},{6,7},{7,6},{8,9},{9,8},{10,11... | collective-permute-start | bytes 393224 | tf_op jit(solution)/shard_map/ppermute | solution.py:521
  45.0 6.8 %collective-permute-start.21 = (bf16[512,128]{1,0:T(8,128)(2,1)S(1)}, bf16[512,128]{1,0:T(8,128)(2,1)S(1)}, u32[]{:S(2)}, u32[]{:S(2)}) collective-permute-start(bf16[512,128]{1,0:T(8,128)(2,1)S(1)} %get-tuple-element.64), channel_id=1, source_target_pairs={{0,2},{1,3},{2,0},{3,1},{4,6},{5,7},{6,4},{7,5},{8,10},{9,11},{10,... | collective-permute-start | bytes 393224 | tf_op jit(solution)/shard_map/ppermute | solution.py:521
  46.5 6.1 %collective-permute-start.22 = (bf16[512,128]{1,0:T(8,128)(2,1)S(1)}, bf16[512,128]{1,0:T(8,128)(2,1)S(1)}, u32[]{:S(2)}, u32[]{:S(2)}) collective-permute-start(bf16[512,128]{1,0:T(8,128)(2,1)S(1)} %get-tuple-element.65), channel_id=1, source_target_pairs={{0,3},{1,2},{2,1},{3,0},{4,7},{5,6},{6,5},{7,4},{8,11},{9,10},{10,... | collective-permute-start | bytes 393224 | tf_op jit(solution)/shard_map/ppermute | solution.py:521
  46.6 6.1 %copy-start.1 = (bf16[4,128,512]{2,1,0:T(8,128)(2,1)S(1)}, bf16[4,128,512]{2,1,0:T(8,128)(2,1)}, u32[]{:S(2)}) copy-start(bf16[4,128,512]{2,1,0:T(8,128)(2,1)} %constant.15.clone.place) | copy-start | bytes 1572868
  49.6 3.7 %collective-permute-start.25 = (bf16[256,128]{1,0:T(8,128)(2,1)S(1)}, bf16[256,128]{1,0:T(8,128)(2,1)S(1)}, u32[]{:S(2)}, u32[]{:S(2)}) collective-permute-start(bf16[256,128]{1,0:T(8,128)(2,1)S(1)} %get-tuple-element.70), channel_id=1, source_target_pairs={{0,1},{1,0},{2,3},{3,2},{4,5},{5,4},{6,7},{7,6},{8,9},{9,8},{10,11... | collective-permute-start | bytes 196616 | tf_op jit(solution)/shard_map/ppermute | solution.py:521
  50.3 4.5 %collective-permute-start.26 = (bf16[256,128]{1,0:T(8,128)(2,1)S(1)}, bf16[256,128]{1,0:T(8,128)(2,1)S(1)}, u32[]{:S(2)}, u32[]{:S(2)}) collective-permute-start(bf16[256,128]{1,0:T(8,128)(2,1)S(1)} %get-tuple-element.71), channel_id=1, source_target_pairs={{0,2},{1,3},{2,0},{3,1},{4,6},{5,7},{6,4},{7,5},{8,10},{9,11},{10,... | collective-permute-start | bytes 196616 | tf_op jit(solution)/shard_map/ppermute | solution.py:521
  51.8 4.4 %collective-permute-start.27 = (bf16[256,128]{1,0:T(8,128)(2,1)S(1)}, bf16[256,128]{1,0:T(8,128)(2,1)S(1)}, u32[]{:S(2)}, u32[]{:S(2)}) collective-permute-start(bf16[256,128]{1,0:T(8,128)(2,1)S(1)} %get-tuple-element.72), channel_id=1, source_target_pairs={{0,3},{1,2},{2,1},{3,0},{4,7},{5,6},{6,5},{7,4},{8,11},{9,10},{10,... | collective-permute-start | bytes 196616 | tf_op jit(solution)/shard_map/ppermute | solution.py:521

commit v7 on v6

--- a/solution.py
+++ b/solution.py
@@ -605,7 +605,6 @@
     far_own = widen_own([across, swap(across, 1)])
     arrived.append(arrived[-1])
     at, _, fars = arrived[-3]
-    first_sums = after(first_sums, (near_up, near_down))
     lags = cross_lags(
         plan, table, [far_own], first_sums, at, fars, 0, 1, count, parts, scaling
     )
@@ -618,7 +617,7 @@
             spots + [count // 2], near_blocks + [middle_up], far_blocks + [down(far_down)]
         )
     for index in range(1, len(groups)):
-        if index == 1:
+        if index == 2:
             near_own = after(near_own, pieces[:parts])
         near_own = after(near_own, lags)
         lags = group_lags(index, near_own, far_own)

time: 58.6 us -> 55.4 us (0.945)
  waiting for transfers between devices: 15.5 us -> 11.1 us
  local copies, waits for them, and re-layouts: 0.02 us -> 1.46 us
    ppermute x14, waiting for transfers between devices: 7.59 us -> 5.74 us  [swap(): return lax.ppermute(value, 'seg', [(i, i ^ j) for i in range(parts)])]
    ppermute x7, waiting for transfers between devices: 2.1 us -> 0.56 us  [down(): return lax.ppermute(value, 'sta', downward)]
    unnamed x6, local copies, waits for them, and re-layouts: 0.02 us -> 1.45 us
    ppermute x7, waiting for transfers between devices: 5.84 us -> 4.76 us  [up(): return lax.ppermute(value, 'sta', upward)]
  transfers between devices with their start and end apart: 28 -> 28, of which waited for: 15 -> 11; matrix products, arithmetic and copies ran while one was open for 0% -> 0% of each run, Pallas kernels for 21% -> 22%
where the time goes in v7:
time: 55.4 us; the launch traced here: 55.3 us
  starting transfers between devices  24.9 us (45%)
  Pallas kernels  17.6 us (32%)
  waiting for transfers between devices  11.1 us (20%)
  local copies, waits for them, and re-layouts  1.46 us (3%)
    ppermute x14, starting transfers between devices, swap(): return lax.ppermute(value, 'seg', [(i, i ^ j) for i in range(parts)])  10.6 us
    pallas_call x3, Pallas kernels, cross_lags(): pl.pallas_call(functools.partial(cross_kernel, first_slot, slots, count,...  10.3 us
    ppermute x7, starting transfers between devices, down(): return lax.ppermute(value, 'sta', downward)  7.2 us
    ppermute x7, starting transfers between devices, up(): return lax.ppermute(value, 'sta', upward)  7.14 us
    ppermute x14, waiting for transfers between devices, swap(): return lax.ppermute(value, 'seg', [(i, i ^ j) for i in range(parts)])  5.74 us
    ppermute x7, waiting for transfers between devices, up(): return lax.ppermute(value, 'sta', upward)  4.76 us
    pallas_call x1, Pallas kernels, prepare(): pl.pallas_call(functools.partial(prep_kernel, parts), out_shape=[jax.Shap...  3.04 us
    pallas_call x1, Pallas kernels, place_lags(): pl.pallas_call(functools.partial(late_kernel, count, parts, steps), out_s...  2.25 us
  transfers between devices with their start and end apart: 28, of which 11 were waited for; matrix products, arithmetic and copies ran while one was open for 0% of the time, Pallas kernels for 22%

profile of v7, /device:TPU:0, one launch (start us, length us, event | category | flops | bytes accessed | tf_op | source)
XLA Modules:
  0.0 55.3 jit_solution(9170094545616646462)
XLA Ops:
  0.0 3.0 %prep.1 = (bf16[4,16,16,128]{3,2,1,0:T(8,128)(2,1)S(1)}, bf16[4,4,16,128]{3,2,1,0:T(8,128)(2,1)S(1)}, bf16[4,4,16,128]{3,2,1,0:T(8,128)(2,1)S(1)}, bf16[4,4,16,128]{3,2,1,0:T(8,128)(2,1)S(1)}) custom-call(f32[16,4,2048]{2,1,0:T(4,128)} %records_hbm.1, bf16[512,2048]{1,0:T(8,128)(2,1)} %constant.14.clone.table_hbm.table), custom_call_target="tpu_custom_call" | custom-call | flops 536870912 | bytes 3145728 | tf_op jit(solution)/shard_map/prep/pallas_call | solution.py:153
  3.1 0.5 collective-permute-start.4
  3.6 2.6 %collective-permute-start = (bf16[4,4,16,128]{3,2,1,0:T(8,128)(2,1)S(1)}, bf16[4,4,16,128]{3,2,1,0:T(8,128)(2,1)S(1)}, u32[]{:S(2)}, u32[]{:S(2)}) collective-permute-start(bf16[4,4,16,128]{3,2,1,0:T(8,128)(2,1)S(1)} %get-tuple-element.38), channel_id=1, source_target_pairs={{0,2},{1,3},{2,0},{3,1},{4,6},{5,7},{6,4},{7,5},{8,10},{9,11},{10,... | collective-permute-start | bytes 196616 | tf_op jit(solution)/shard_map/ppermute | solution.py:521
  6.2 1.8 %collective-permute-start.6 = (bf16[8,4,16,128]{3,2,1,0:T(8,128)(2,1)S(1)}, bf16[8,4,16,128]{3,2,1,0:T(8,128)(2,1)S(1)}, u32[]{:S(2)}, u32[]{:S(2)}) collective-permute-start(bf16[8,4,16,128]{3,2,1,0:T(8,128)(2,1)S(1)} %pad_maximum_fusion.1), channel_id=1, source_target_pairs={{0,4},{8,0},{16,8},{24,16},{28,24},{20,28},{12,20},{4,12},{1,5},{9... | collective-permute-start | bytes 393224 | tf_op jit(solution)/shard_map/ppermute | solution.py:554
  8.3 0.5 collective-permute-done
  8.8 1.4 %collective-permute-done.1 = bf16[4,4,16,128]{3,2,1,0:T(8,128)(2,1)S(1)} collective-permute-done((bf16[4,4,16,128]{3,2,1,0:T(8,128)(2,1)S(1)}, bf16[4,4,16,128]{3,2,1,0:T(8,128)(2,1)S(1)}, u32[]{:S(2)}, u32[]{:S(2)}) %collective-permute-start.1) | collective-permute-done | bytes 65568 | tf_op jit(solution)/shard_map/ppermute | solution.py:521
  10.2 1.6 %collective-permute-start.3 = (bf16[8,4,16,128]{3,2,1,0:T(8,128)(2,1)S(1)}, bf16[8,4,16,128]{3,2,1,0:T(8,128)(2,1)S(1)}, u32[]{:S(2)}, u32[]{:S(2)}) collective-permute-start(bf16[8,4,16,128]{3,2,1,0:T(8,128)(2,1)S(1)} %pad_maximum_fusion), channel_id=1, source_target_pairs={{0,4},{8,0},{16,8},{24,16},{28,24},{20,28},{12,20},{4,12},{1,5},{9... | collective-permute-start | bytes 393224 | tf_op jit(solution)/shard_map/ppermute | solution.py:554
  11.8 0.5 collective-permute-start.2
  12.3 1.3 %collective-permute-start.11 = (bf16[4,16,16,128]{3,2,1,0:T(8,128)(2,1)S(1)}, bf16[4,16,16,128]{3,2,1,0:T(8,128)(2,1)S(1)}, u32[]{:S(2)}, u32[]{:S(2)}) collective-permute-start(bf16[4,16,16,128]{3,2,1,0:T(8,128)(2,1)S(1)} %get-tuple-element.49.refs_0_), channel_id=1, source_target_pairs={{0,2},{1,3},{2,0},{3,1},{4,6},{5,7},{6,4},{7,5},{8,10},{9,11},{10,... | collective-permute-start | bytes 786440 | tf_op jit(solution)/shard_map/ppermute | solution.py:521
  13.8 1.6 %collective-permute-start.9 = (bf16[8,4,16,128]{3,2,1,0:T(8,128)(2,1)S(1)}, bf16[8,4,16,128]{3,2,1,0:T(8,128)(2,1)S(1)}, u32[]{:S(2)}, u32[]{:S(2)}) collective-permute-start(bf16[8,4,16,128]{3,2,1,0:T(8,128)(2,1)S(1)} %collective-permute-done.5.rest_0_.rest_2_), channel_id=1, source_target_pairs={{0,8},{8,16},{16,24},{24,28},{28,20},{20,12},{12,4},{4,0},{1,9},{9... | collective-permute-start | bytes 393224 | tf_op jit(solution)/shard_map/ppermute | solution.py:551
  16.1 2.0 %collective-permute-done.2.rest_2_.rest_8_.rest_9_ = bf16[8,4,16,128]{3,2,1,0:T(8,128)(2,1)S(1)} collective-permute-done((bf16[8,4,16,128]{3,2,1,0:T(8,128)(2,1)S(1)}, bf16[8,4,16,128]{3,2,1,0:T(8,128)(2,1)S(1)}, u32[]{:S(2)}, u32[]{:S(2)}) %collective-permute-start.2) | collective-permute-done | bytes 131104 | tf_op jit(solution)/shard_map/ppermute | solution.py:551
  18.1 2.0 %collective-permute-start.8 = (bf16[8,4,16,128]{3,2,1,0:T(8,128)(2,1)S(1)}, bf16[8,4,16,128]{3,2,1,0:T(8,128)(2,1)S(1)}, u32[]{:S(2)}, u32[]{:S(2)}) collective-permute-start(bf16[8,4,16,128]{3,2,1,0:T(8,128)(2,1)S(1)} %collective-permute-done.3.rest_3_.rest_9_.rest_10_), channel_id=1, source_target_pairs={{0,4},{8,0},{16,8},{24,16},{28,24},{20,28},{12,20},{4,12},{1,5},{9... | collective-permute-start | bytes 393224 | tf_op jit(solution)/shard_map/ppermute | solution.py:554
  20.1 0.8 %collective-permute-done.9.rest_2_.rest_4_ = bf16[8,4,16,128]{3,2,1,0:T(8,128)(2,1)S(1)} collective-permute-done((bf16[8,4,16,128]{3,2,1,0:T(8,128)(2,1)S(1)}, bf16[8,4,16,128]{3,2,1,0:T(8,128)(2,1)S(1)}, u32[]{:S(2)}, u32[]{:S(2)}) %collective-permute-start.9) | collective-permute-done | bytes 131104 | tf_op jit(solution)/shard_map/ppermute | solution.py:551
  21.1 2.0 %collective-permute-done.7.rest_4_.rest_10_.rest_11_ = bf16[8,4,16,128]{3,2,1,0:T(8,128)(2,1)S(1)} collective-permute-done((bf16[8,4,16,128]{3,2,1,0:T(8,128)(2,1)S(1)}, bf16[8,4,16,128]{3,2,1,0:T(8,128)(2,1)S(1)}, u32[]{:S(2)}, u32[]{:S(2)}) %collective-permute-start.7) | collective-permute-done | bytes 131104 | tf_op jit(solution)/shard_map/ppermute | solution.py:551
  23.2 1.6 %collective-permute-start.16 = (bf16[8,4,16,128]{3,2,1,0:T(8,128)(2,1)S(1)}, bf16[8,4,16,128]{3,2,1,0:T(8,128)(2,1)S(1)}, u32[]{:S(2)}, u32[]{:S(2)}) collective-permute-start(bf16[8,4,16,128]{3,2,1,0:T(8,128)(2,1)S(1)} %collective-permute-done.9.rest_2_.rest_4_), channel_id=1, source_target_pairs={{0,8},{8,16},{16,24},{24,28},{28,20},{20,12},{12,4},{4,0},{1,9},{9... | collective-permute-start | bytes 393224 | tf_op jit(solution)/shard_map/ppermute | solution.py:551
  24.8 0.4 collective-permute-start.17
  25.2 1.6 %collective-permute-start.18 = (bf16[8,4,16,128]{3,2,1,0:T(8,128)(2,1)S(1)}, bf16[8,4,16,128]{3,2,1,0:T(8,128)(2,1)S(1)}, u32[]{:S(2)}, u32[]{:S(2)}) collective-permute-start(bf16[8,4,16,128]{3,2,1,0:T(8,128)(2,1)S(1)} %collective-permute-done.7.rest_4_.rest_10_.rest_11_), channel_id=1, source_target_pairs={{0,8},{8,16},{16,24},{24,28},{28,20},{20,12},{12,4},{4,0},{1,9},{9... | collective-permute-start | bytes 393224 | tf_op jit(solution)/shard_map/ppermute | solution.py:551
  26.8 0.4 collective-permute-start.19
  27.2 1.2 %near.1.rest_1_ = f32[1024,128]{1,0:T(8,128)S(1)} custom-call(s32[4,8]{1,0:T(4,128)S(1)} %copy-done.2, f32[3,8,16,8,128]{4,3,2,1,0:T(8,128)S(1)} %widen.2.own.rest_0_, bf16[8,4,16,128]{3,2,1,0:T(8,128)(2,1)S(1)} %collective-permute-done.5.rest_0_.rest_2_, bf16[8,4,16,128]{3,2,1,0:T(8,128)(2,1)S(1)} %collective-permute-done.6.rest_1_.rest_3_, ...), custom_call_target="tpu_custom_call" | custom-call | flops 57500000 | bytes 1024 | tf_op jit(solution)/shard_map/near/pallas_call | solution.py:320
  28.6 1.4 %copy-done = bf16[512,2048]{1,0:T(8,128)(2,1)S(1)} copy-done((bf16[512,2048]{1,0:T(8,128)(2,1)S(1)}, bf16[512,2048]{1,0:T(8,128)(2,1)}, u32[]{:S(2)}) %copy-start) | copy-done | bytes 2097176
  30.1 2.3 %cross.3 = (bf16[256,128]{1,0:T(8,128)(2,1)S(1)}, bf16[256,128]{1,0:T(8,128)(2,1)S(1)}, bf16[256,128]{1,0:T(8,128)(2,1)S(1)}, bf16[256,128]{1,0:T(8,128)(2,1)S(1)}) custom-call(s32[4,8]{1,0:T(4,128)S(1)} %copy-done.2, bf16[512,2048]{1,0:T(8,128)(2,1)S(1)} %copy-done, f32[3,8,16,8,128]{4,3,2,1,0:T(8,128)S(1)} %widen.3.rest_0_.rest_1_, ...), custom_call_target="tpu_custom_call" | custom-call | flops 1955000064 | bytes 1024 | tf_op jit(solution)/shard_map/cross/pallas_call | solution.py:404
  32.4 1.8 %collective-permute-start.14 = (bf16[256,128]{1,0:T(8,128)(2,1)S(1)}, bf16[256,128]{1,0:T(8,128)(2,1)S(1)}, u32[]{:S(2)}, u32[]{:S(2)}) collective-permute-start(bf16[256,128]{1,0:T(8,128)(2,1)S(1)} %get-tuple-element.54), channel_id=1, source_target_pairs={{0,2},{1,3},{2,0},{3,1},{4,6},{5,7},{6,4},{7,5},{8,10},{9,11},{10,... | collective-permute-start | bytes 196616 | tf_op jit(solution)/shard_map/ppermute | solution.py:521
  34.4 1.6 %collective-permute-start.23 = (bf16[8,4,16,128]{3,2,1,0:T(8,128)(2,1)S(1)}, bf16[8,4,16,128]{3,2,1,0:T(8,128)(2,1)S(1)}, u32[]{:S(2)}, u32[]{:S(2)}) collective-permute-start(bf16[8,4,16,128]{3,2,1,0:T(8,128)(2,1)S(1)} %collective-permute-done.16.rest_6_), channel_id=1, source_target_pairs={{0,8},{8,16},{16,24},{24,28},{28,20},{20,12},{12,4},{4,0},{1,9},{9... | collective-permute-start | bytes 393224 | tf_op jit(solution)/shard_map/ppermute | solution.py:551
  36.4 5.0 %cross.4 = (bf16[512,128]{1,0:T(8,128)(2,1)S(1)}, bf16[512,128]{1,0:T(8,128)(2,1)S(1)}, bf16[512,128]{1,0:T(8,128)(2,1)S(1)}, bf16[512,128]{1,0:T(8,128)(2,1)S(1)}) custom-call(s32[4,8]{1,0:T(4,128)S(1)} %copy-done.2, bf16[512,2048]{1,0:T(8,128)(2,1)S(1)} %copy-done, f32[3,8,16,8,128]{4,3,2,1,0:T(8,128)S(1)} %widen.2.own.rest_0_, ...), custom_call_target="tpu_custom_call" | custom-call | flops 5289999872 | bytes 1024 | tf_op jit(solution)/shard_map/cross/pallas_call | solution.py:404
  41.5 1.8 %collective-permute-start.21 = (bf16[512,128]{1,0:T(8,128)(2,1)S(1)}, bf16[512,128]{1,0:T(8,128)(2,1)S(1)}, u32[]{:S(2)}, u32[]{:S(2)}) collective-permute-start(bf16[512,128]{1,0:T(8,128)(2,1)S(1)} %get-tuple-element.61), channel_id=1, source_target_pairs={{0,2},{1,3},{2,0},{3,1},{4,6},{5,7},{6,4},{7,5},{8,10},{9,11},{10,... | collective-permute-start | bytes 393224 | tf_op jit(solution)/shard_map/ppermute | solution.py:521
  43.4 3.0 %cross.5 = (bf16[256,128]{1,0:T(8,128)(2,1)S(1)}, bf16[256,128]{1,0:T(8,128)(2,1)S(1)}, bf16[256,128]{1,0:T(8,128)(2,1)S(1)}, bf16[256,128]{1,0:T(8,128)(2,1)S(1)}) custom-call(s32[4,8]{1,0:T(4,128)S(1)} %copy-done.2, bf16[512,2048]{1,0:T(8,128)(2,1)S(1)} %copy-done, f32[3,8,16,8,128]{4,3,2,1,0:T(8,128)S(1)} %widen.2.own.rest_0_, ...), custom_call_target="tpu_custom_call" | custom-call | flops 2990000128 | bytes 1024 | tf_op jit(solution)/shard_map/cross/pallas_call | solution.py:404
  46.8 1.7 %collective-permute-start.26 = (bf16[256,128]{1,0:T(8,128)(2,1)S(1)}, bf16[256,128]{1,0:T(8,128)(2,1)S(1)}, u32[]{:S(2)}, u32[]{:S(2)}) collective-permute-start(bf16[256,128]{1,0:T(8,128)(2,1)S(1)} %get-tuple-element.69), channel_id=1, source_target_pairs={{0,2},{1,3},{2,0},{3,1},{4,6},{5,7},{6,4},{7,5},{8,10},{9,11},{10,... | collective-permute-start | bytes 196616 | tf_op jit(solution)/shard_map/ppermute | solution.py:521
  48.6 1.4 %collective-permute-done.22.rest_7_ = bf16[512,128]{1,0:T(8,128)(2,1)S(1)} collective-permute-done((bf16[512,128]{1,0:T(8,128)(2,1)S(1)}, bf16[512,128]{1,0:T(8,128)(2,1)S(1)}, u32[]{:S(2)}, u32[]{:S(2)}) %collective-permute-start.22) | collective-permute-done | bytes 131104 | tf_op jit(solution)/shard_map/ppermute | solution.py:521
  49.9 0.6 %early.1 = f32[3,2,256,256]{3,2,1,0:T(8,128)S(1)} custom-call(bf16[4,128,512]{2,1,0:T(8,128)(2,1)S(1)} %copy-done.1, bf16[256,128]{1,0:T(8,128)(2,1)S(1)} %get-tuple-element.52.rest_0_, bf16[256,128]{1,0:T(8,128)(2,1)S(1)} %collective-permute-done.13.rest_1_, bf16[256,128]{1,0:T(8,128)(2,1)S(1)} %collective-permute-done.14.rest_2_, ...), custom_call_target="tpu_custom_call" | custom-call | flops 57500000 | bytes 1024 | tf_op jit(solution)/shard_map/early/pallas_call | solution.py:496
  50.5 1.1 %collective-permute-done.26.rest_2_ = bf16[256,128]{1,0:T(8,128)(2,1)S(1)} collective-permute-done((bf16[256,128]{1,0:T(8,128)(2,1)S(1)}, bf16[256,128]{1,0:T(8,128)(2,1)S(1)}, u32[]{:S(2)}, u32[]{:S(2)}) %collective-permute-start.26) | collective-permute-done | bytes 65568 | tf_op jit(solution)/shard_map/ppermute | solution.py:521
  51.6 1.4 %collective-permute-done.27.rest_3_ = bf16[256,128]{1,0:T(8,128)(2,1)S(1)} collective-permute-done((bf16[256,128]{1,0:T(8,128)(2,1)S(1)}, bf16[256,128]{1,0:T(8,128)(2,1)S(1)}, u32[]{:S(2)}, u32[]{:S(2)}) %collective-permute-start.27) | collective-permute-done | bytes 65568 | tf_op jit(solution)/shard_map/ppermute | solution.py:521
  53.0 2.2 %late.1 = f32[2,256,4,256]{3,2,1,0:T(4,128)} custom-call(s32[4,8]{1,0:T(4,128)S(1)} %copy-done.2, bf16[4,128,512]{2,1,0:T(8,128)(2,1)S(1)} %copy-done.1, f32[3,2,256,256]{3,2,1,0:T(8,128)S(1)} %early.1, bf16[256,128]{1,0:T(8,128)(2,1)S(1)} %get-tuple-element.67.rest_0_, bf16[256,128]{1,0:T(8,128)(2,1)S(1)} %collective-permute-done.25.rest_1_, ...), custom_call_target="tpu_custom_call" | custom-call | flops 57500000 | bytes 1024 | tf_op jit(solution)/shard_map/late/pallas_call | solution.py:506
  (42 shorter events, 2.8 us)
Async XLA Ops:
  3.0 24.2 %copy-start.2 = (s32[4,8]{1,0:T(4,128)S(1)}, s32[4,8]{1,0:T(4,128)}, u32[]{:S(2)}) copy-start(s32[4,8]{1,0:T(4,128)} %plan.9) | copy-start | bytes 388
  3.1 3.2 %collective-permute-start.4 = (bf16[4,16,16,128]{3,2,1,0:T(8,128)(2,1)S(1)}, bf16[4,16,16,128]{3,2,1,0:T(8,128)(2,1)S(1)}, u32[]{:S(2)}, u32[]{:S(2)}) collective-permute-start(bf16[4,16,16,128]{3,2,1,0:T(8,128)(2,1)S(1)} %get-tuple-element.49.refs_0_), channel_id=1, source_target_pairs={{0,1},{1,0},{2,3},{3,2},{4,5},{5,4},{6,7},{7,6},{8,9},{9,8},{10,11... | collective-permute-start | bytes 786440 | tf_op jit(solution)/shard_map/ppermute | solution.py:521
  3.6 5.3 %collective-permute-start = (bf16[4,4,16,128]{3,2,1,0:T(8,128)(2,1)S(1)}, bf16[4,4,16,128]{3,2,1,0:T(8,128)(2,1)S(1)}, u32[]{:S(2)}, u32[]{:S(2)}) collective-permute-start(bf16[4,4,16,128]{3,2,1,0:T(8,128)(2,1)S(1)} %get-tuple-element.38), channel_id=1, source_target_pairs={{0,2},{1,3},{2,0},{3,1},{4,6},{5,7},{6,4},{7,5},{8,10},{9,11},{10,... | collective-permute-start | bytes 196616 | tf_op jit(solution)/shard_map/ppermute | solution.py:521
  6.1 4.0 %collective-permute-start.1 = (bf16[4,4,16,128]{3,2,1,0:T(8,128)(2,1)S(1)}, bf16[4,4,16,128]{3,2,1,0:T(8,128)(2,1)S(1)}, u32[]{:S(2)}, u32[]{:S(2)}) collective-permute-start(bf16[4,4,16,128]{3,2,1,0:T(8,128)(2,1)S(1)} %get-tuple-element.39), channel_id=1, source_target_pairs={{0,3},{1,2},{2,1},{3,0},{4,7},{5,6},{6,5},{7,4},{8,11},{9,10},{10,... | collective-permute-start | bytes 196616 | tf_op jit(solution)/shard_map/ppermute | solution.py:521
  6.2 7.5 %collective-permute-start.6 = (bf16[8,4,16,128]{3,2,1,0:T(8,128)(2,1)S(1)}, bf16[8,4,16,128]{3,2,1,0:T(8,128)(2,1)S(1)}, u32[]{:S(2)}, u32[]{:S(2)}) collective-permute-start(bf16[8,4,16,128]{3,2,1,0:T(8,128)(2,1)S(1)} %pad_maximum_fusion.1), channel_id=1, source_target_pairs={{0,4},{8,0},{16,8},{24,16},{28,24},{20,28},{12,20},{4,12},{1,5},{9... | collective-permute-start | bytes 393224 | tf_op jit(solution)/shard_map/ppermute | solution.py:554
  8.1 5.7 %collective-permute-start.5 = (bf16[8,4,16,128]{3,2,1,0:T(8,128)(2,1)S(1)}, bf16[8,4,16,128]{3,2,1,0:T(8,128)(2,1)S(1)}, u32[]{:S(2)}, u32[]{:S(2)}) collective-permute-start(bf16[8,4,16,128]{3,2,1,0:T(8,128)(2,1)S(1)} %pad_maximum_fusion.1), channel_id=1, source_target_pairs={{0,8},{8,16},{16,24},{24,28},{28,20},{20,12},{12,4},{4,0},{1,9},{9... | collective-permute-start | bytes 393224 | tf_op jit(solution)/shard_map/ppermute | solution.py:551
  10.2 5.9 %collective-permute-start.3 = (bf16[8,4,16,128]{3,2,1,0:T(8,128)(2,1)S(1)}, bf16[8,4,16,128]{3,2,1,0:T(8,128)(2,1)S(1)}, u32[]{:S(2)}, u32[]{:S(2)}) collective-permute-start(bf16[8,4,16,128]{3,2,1,0:T(8,128)(2,1)S(1)} %pad_maximum_fusion), channel_id=1, source_target_pairs={{0,4},{8,0},{16,8},{24,16},{28,24},{20,28},{12,20},{4,12},{1,5},{9... | collective-permute-start | bytes 393224 | tf_op jit(solution)/shard_map/ppermute | solution.py:554
  11.8 6.3 %collective-permute-start.2 = (bf16[8,4,16,128]{3,2,1,0:T(8,128)(2,1)S(1)}, bf16[8,4,16,128]{3,2,1,0:T(8,128)(2,1)S(1)}, u32[]{:S(2)}, u32[]{:S(2)}) collective-permute-start(bf16[8,4,16,128]{3,2,1,0:T(8,128)(2,1)S(1)} %pad_maximum_fusion), channel_id=1, source_target_pairs={{0,8},{8,16},{16,24},{24,28},{28,20},{20,12},{12,4},{4,0},{1,9},{9... | collective-permute-start | bytes 393224 | tf_op jit(solution)/shard_map/ppermute | solution.py:551
  12.3 8.8 %collective-permute-start.11 = (bf16[4,16,16,128]{3,2,1,0:T(8,128)(2,1)S(1)}, bf16[4,16,16,128]{3,2,1,0:T(8,128)(2,1)S(1)}, u32[]{:S(2)}, u32[]{:S(2)}) collective-permute-start(bf16[4,16,16,128]{3,2,1,0:T(8,128)(2,1)S(1)} %get-tuple-element.49.refs_0_), channel_id=1, source_target_pairs={{0,2},{1,3},{2,0},{3,1},{4,6},{5,7},{6,4},{7,5},{8,10},{9,11},{10,... | collective-permute-start | bytes 786440 | tf_op jit(solution)/shard_map/ppermute | solution.py:521
  13.8 7.1 %collective-permute-start.9 = (bf16[8,4,16,128]{3,2,1,0:T(8,128)(2,1)S(1)}, bf16[8,4,16,128]{3,2,1,0:T(8,128)(2,1)S(1)}, u32[]{:S(2)}, u32[]{:S(2)}) collective-permute-start(bf16[8,4,16,128]{3,2,1,0:T(8,128)(2,1)S(1)} %collective-permute-done.5.rest_0_.rest_2_), channel_id=1, source_target_pairs={{0,8},{8,16},{16,24},{24,28},{28,20},{20,12},{12,4},{4,0},{1,9},{9... | collective-permute-start | bytes 393224 | tf_op jit(solution)/shard_map/ppermute | solution.py:551
  15.4 5.7 %collective-permute-start.10 = (bf16[8,4,16,128]{3,2,1,0:T(8,128)(2,1)S(1)}, bf16[8,4,16,128]{3,2,1,0:T(8,128)(2,1)S(1)}, u32[]{:S(2)}, u32[]{:S(2)}) collective-permute-start(bf16[8,4,16,128]{3,2,1,0:T(8,128)(2,1)S(1)} %collective-permute-done.6.rest_1_.rest_3_), channel_id=1, source_target_pairs={{0,4},{8,0},{16,8},{24,16},{28,24},{20,28},{12,20},{4,12},{1,5},{9... | collective-permute-start | bytes 393224 | tf_op jit(solution)/shard_map/ppermute | solution.py:554
  18.1 5.0 %collective-permute-start.7 = (bf16[8,4,16,128]{3,2,1,0:T(8,128)(2,1)S(1)}, bf16[8,4,16,128]{3,2,1,0:T(8,128)(2,1)S(1)}, u32[]{:S(2)}, u32[]{:S(2)}) collective-permute-start(bf16[8,4,16,128]{3,2,1,0:T(8,128)(2,1)S(1)} %collective-permute-done.2.rest_2_.rest_8_.rest_9_), channel_id=1, source_target_pairs={{0,8},{8,16},{16,24},{24,28},{28,20},{20,12},{12,4},{4,0},{1,9},{9... | collective-permute-start | bytes 393224 | tf_op jit(solution)/shard_map/ppermute | solution.py:551
  18.1 5.1 %collective-permute-start.8 = (bf16[8,4,16,128]{3,2,1,0:T(8,128)(2,1)S(1)}, bf16[8,4,16,128]{3,2,1,0:T(8,128)(2,1)S(1)}, u32[]{:S(2)}, u32[]{:S(2)}) collective-permute-start(bf16[8,4,16,128]{3,2,1,0:T(8,128)(2,1)S(1)} %collective-permute-done.3.rest_3_.rest_9_.rest_10_), channel_id=1, source_target_pairs={{0,4},{8,0},{16,8},{24,16},{28,24},{20,28},{12,20},{4,12},{1,5},{9... | collective-permute-start | bytes 393224 | tf_op jit(solution)/shard_map/ppermute | solution.py:554
  23.2 5.3 %collective-permute-start.12 = (bf16[4,16,16,128]{3,2,1,0:T(8,128)(2,1)S(1)}, bf16[4,16,16,128]{3,2,1,0:T(8,128)(2,1)S(1)}, u32[]{:S(2)}, u32[]{:S(2)}) collective-permute-start(bf16[4,16,16,128]{3,2,1,0:T(8,128)(2,1)S(1)} %collective-permute-done.11.refs_0_), channel_id=1, source_target_pairs={{0,1},{1,0},{2,3},{3,2},{4,5},{5,4},{6,7},{7,6},{8,9},{9,8},{10,11... | collective-permute-start | bytes 786440 | tf_op jit(solution)/shard_map/ppermute | solution.py:521
  23.2 9.2 %collective-permute-start.16 = (bf16[8,4,16,128]{3,2,1,0:T(8,128)(2,1)S(1)}, bf16[8,4,16,128]{3,2,1,0:T(8,128)(2,1)S(1)}, u32[]{:S(2)}, u32[]{:S(2)}) collective-permute-start(bf16[8,4,16,128]{3,2,1,0:T(8,128)(2,1)S(1)} %collective-permute-done.9.rest_2_.rest_4_), channel_id=1, source_target_pairs={{0,8},{8,16},{16,24},{24,28},{28,20},{20,12},{12,4},{4,0},{1,9},{9... | collective-permute-start | bytes 393224 | tf_op jit(solution)/shard_map/ppermute | solution.py:551
  24.8 9.5 %collective-permute-start.17 = (bf16[8,4,16,128]{3,2,1,0:T(8,128)(2,1)S(1)}, bf16[8,4,16,128]{3,2,1,0:T(8,128)(2,1)S(1)}, u32[]{:S(2)}, u32[]{:S(2)}) collective-permute-start(bf16[8,4,16,128]{3,2,1,0:T(8,128)(2,1)S(1)} %collective-permute-done.10.rest_3_.rest_5_), channel_id=1, source_target_pairs={{0,4},{8,0},{16,8},{24,16},{28,24},{20,28},{12,20},{4,12},{1,5},{9... | collective-permute-start | bytes 393224 | tf_op jit(solution)/shard_map/ppermute | solution.py:554
  25.2 10.7 %collective-permute-start.18 = (bf16[8,4,16,128]{3,2,1,0:T(8,128)(2,1)S(1)}, bf16[8,4,16,128]{3,2,1,0:T(8,128)(2,1)S(1)}, u32[]{:S(2)}, u32[]{:S(2)}) collective-permute-start(bf16[8,4,16,128]{3,2,1,0:T(8,128)(2,1)S(1)} %collective-permute-done.7.rest_4_.rest_10_.rest_11_), channel_id=1, source_target_pairs={{0,8},{8,16},{16,24},{24,28},{28,20},{20,12},{12,4},{4,0},{1,9},{9... | collective-permute-start | bytes 393224 | tf_op jit(solution)/shard_map/ppermute | solution.py:551
  26.8 7.6 %collective-permute-start.19 = (bf16[8,4,16,128]{3,2,1,0:T(8,128)(2,1)S(1)}, bf16[8,4,16,128]{3,2,1,0:T(8,128)(2,1)S(1)}, u32[]{:S(2)}, u32[]{:S(2)}) collective-permute-start(bf16[8,4,16,128]{3,2,1,0:T(8,128)(2,1)S(1)} %collective-permute-done.8.rest_5_.rest_11_.rest_12_), channel_id=1, source_target_pairs={{0,4},{8,0},{16,8},{24,16},{28,24},{20,28},{12,20},{4,12},{1,5},{9... | collective-permute-start | bytes 393224 | tf_op jit(solution)/shard_map/ppermute | solution.py:554
  28.5 1.6 %copy-start = (bf16[512,2048]{1,0:T(8,128)(2,1)S(1)}, bf16[512,2048]{1,0:T(8,128)(2,1)}, u32[]{:S(2)}) copy-start(bf16[512,2048]{1,0:T(8,128)(2,1)} %constant.14.clone.table_hbm.table) | copy-start | bytes 6291460
  32.3 9.1 %collective-permute-start.13 = (bf16[256,128]{1,0:T(8,128)(2,1)S(1)}, bf16[256,128]{1,0:T(8,128)(2,1)S(1)}, u32[]{:S(2)}, u32[]{:S(2)}) collective-permute-start(bf16[256,128]{1,0:T(8,128)(2,1)S(1)} %get-tuple-element.53), channel_id=1, source_target_pairs={{0,1},{1,0},{2,3},{3,2},{4,5},{5,4},{6,7},{7,6},{8,9},{9,8},{10,11... | collective-permute-start | bytes 196616 | tf_op jit(solution)/shard_map/ppermute | solution.py:521
  32.4 9.1 %collective-permute-start.14 = (bf16[256,128]{1,0:T(8,128)(2,1)S(1)}, bf16[256,128]{1,0:T(8,128)(2,1)S(1)}, u32[]{:S(2)}, u32[]{:S(2)}) collective-permute-start(bf16[256,128]{1,0:T(8,128)(2,1)S(1)} %get-tuple-element.54), channel_id=1, source_target_pairs={{0,2},{1,3},{2,0},{3,1},{4,6},{5,7},{6,4},{7,5},{8,10},{9,11},{10,... | collective-permute-start | bytes 196616 | tf_op jit(solution)/shard_map/ppermute | solution.py:521
  34.2 9.1 %collective-permute-start.15 = (bf16[256,128]{1,0:T(8,128)(2,1)S(1)}, bf16[256,128]{1,0:T(8,128)(2,1)S(1)}, u32[]{:S(2)}, u32[]{:S(2)}) collective-permute-start(bf16[256,128]{1,0:T(8,128)(2,1)S(1)} %get-tuple-element.55), channel_id=1, source_target_pairs={{0,3},{1,2},{2,1},{3,0},{4,7},{5,6},{6,5},{7,4},{8,11},{9,10},{10,... | collective-permute-start | bytes 196616 | tf_op jit(solution)/shard_map/ppermute | solution.py:521
  34.4 9.1 %collective-permute-start.23 = (bf16[8,4,16,128]{3,2,1,0:T(8,128)(2,1)S(1)}, bf16[8,4,16,128]{3,2,1,0:T(8,128)(2,1)S(1)}, u32[]{:S(2)}, u32[]{:S(2)}) collective-permute-start(bf16[8,4,16,128]{3,2,1,0:T(8,128)(2,1)S(1)} %collective-permute-done.16.rest_6_), channel_id=1, source_target_pairs={{0,8},{8,16},{16,24},{24,28},{28,20},{20,12},{12,4},{4,0},{1,9},{9... | collective-permute-start | bytes 393224 | tf_op jit(solution)/shard_map/ppermute | solution.py:551
  35.9 7.5 %collective-permute-start.24 = (bf16[8,4,16,128]{3,2,1,0:T(8,128)(2,1)S(1)}, bf16[8,4,16,128]{3,2,1,0:T(8,128)(2,1)S(1)}, u32[]{:S(2)}, u32[]{:S(2)}) collective-permute-start(bf16[8,4,16,128]{3,2,1,0:T(8,128)(2,1)S(1)} %collective-permute-done.19.rest_13_.rest_14_), channel_id=1, source_target_pairs={{0,4},{8,0},{16,8},{24,16},{28,24},{20,28},{12,20},{4,12},{1,5},{9... | collective-permute-start | bytes 393224 | tf_op jit(solution)/shard_map/ppermute | solution.py:554
  41.4 7.1 %collective-permute-start.20 = (bf16[512,128]{1,0:T(8,128)(2,1)S(1)}, bf16[512,128]{1,0:T(8,128)(2,1)S(1)}, u32[]{:S(2)}, u32[]{:S(2)}) collective-permute-start(bf16[512,128]{1,0:T(8,128)(2,1)S(1)} %get-tuple-element.60), channel_id=1, source_target_pairs={{0,1},{1,0},{2,3},{3,2},{4,5},{5,4},{6,7},{7,6},{8,9},{9,8},{10,11... | collective-permute-start | bytes 393224 | tf_op jit(solution)/shard_map/ppermute | solution.py:521
  41.5 7.1 %collective-permute-start.21 = (bf16[512,128]{1,0:T(8,128)(2,1)S(1)}, bf16[512,128]{1,0:T(8,128)(2,1)S(1)}, u32[]{:S(2)}, u32[]{:S(2)}) collective-permute-start(bf16[512,128]{1,0:T(8,128)(2,1)S(1)} %get-tuple-element.61), channel_id=1, source_target_pairs={{0,2},{1,3},{2,0},{3,1},{4,6},{5,7},{6,4},{7,5},{8,10},{9,11},{10,... | collective-permute-start | bytes 393224 | tf_op jit(solution)/shard_map/ppermute | solution.py:521
  43.3 6.6 %collective-permute-start.22 = (bf16[512,128]{1,0:T(8,128)(2,1)S(1)}, bf16[512,128]{1,0:T(8,128)(2,1)S(1)}, u32[]{:S(2)}, u32[]{:S(2)}) collective-permute-start(bf16[512,128]{1,0:T(8,128)(2,1)S(1)} %get-tuple-element.62), channel_id=1, source_target_pairs={{0,3},{1,2},{2,1},{3,0},{4,7},{5,6},{6,5},{7,4},{8,11},{9,10},{10,... | collective-permute-start | bytes 393224 | tf_op jit(solution)/shard_map/ppermute | solution.py:521
  43.4 6.5 %copy-start.1 = (bf16[4,128,512]{2,1,0:T(8,128)(2,1)S(1)}, bf16[4,128,512]{2,1,0:T(8,128)(2,1)}, u32[]{:S(2)}) copy-start(bf16[4,128,512]{2,1,0:T(8,128)(2,1)} %constant.15.clone.place) | copy-start | bytes 1572868
  46.4 4.1 %collective-permute-start.25 = (bf16[256,128]{1,0:T(8,128)(2,1)S(1)}, bf16[256,128]{1,0:T(8,128)(2,1)S(1)}, u32[]{:S(2)}, u32[]{:S(2)}) collective-permute-start(bf16[256,128]{1,0:T(8,128)(2,1)S(1)} %get-tuple-element.68), channel_id=1, source_target_pairs={{0,1},{1,0},{2,3},{3,2},{4,5},{5,4},{6,7},{7,6},{8,9},{9,8},{10,11... | collective-permute-start | bytes 196616 | tf_op jit(solution)/shard_map/ppermute | solution.py:521
  46.8 4.8 %collective-permute-start.26 = (bf16[256,128]{1,0:T(8,128)(2,1)S(1)}, bf16[256,128]{1,0:T(8,128)(2,1)S(1)}, u32[]{:S(2)}, u32[]{:S(2)}) collective-permute-start(bf16[256,128]{1,0:T(8,128)(2,1)S(1)} %get-tuple-element.69), channel_id=1, source_target_pairs={{0,2},{1,3},{2,0},{3,1},{4,6},{5,7},{6,4},{7,5},{8,10},{9,11},{10,... | collective-permute-start | bytes 196616 | tf_op jit(solution)/shard_map/ppermute | solution.py:521
  48.5 4.5 %collective-permute-start.27 = (bf16[256,128]{1,0:T(8,128)(2,1)S(1)}, bf16[256,128]{1,0:T(8,128)(2,1)S(1)}, u32[]{:S(2)}, u32[]{:S(2)}) collective-permute-start(bf16[256,128]{1,0:T(8,128)(2,1)S(1)} %get-tuple-element.70), channel_id=1, source_target_pairs={{0,3},{1,2},{2,1},{3,0},{4,7},{5,6},{6,5},{7,4},{8,11},{9,10},{10,... | collective-permute-start | bytes 196616 | tf_op jit(solution)/shard_map/ppermute | solution.py:521

commit v8 on v7

--- a/solution.py
+++ b/solution.py
@@ -89,8 +89,8 @@
 
 
 def prep_kernel(parts, records_hbm, table_hbm, white, mine, *rest):
-    others = rest[: parts - 2]
-    records, table, stack, flat, spread, sems = rest[parts - 2 :]
+    others = rest[: parts - 1]
+    records, table, stack, flat, spread, sems = rest[parts - 1 :]
     records_copy = pltpu.make_async_copy(records_hbm, records, sems.at[0])
     records_copy.start()
     copy = pltpu.make_async_copy(table_hbm, table, sems.at[1])
@@ -139,7 +139,7 @@
     me = lax.axis_index("seg")
     quarter = stations // parts
     white[...] = spread[...].reshape(windows, stations, 2 * TILES, LANES).astype(BF)
-    for j, out in [(0, mine)] + list(zip(range(2, parts), others)):
+    for j, out in enumerate((mine, *others)):
         for w in range(windows):
             out[w] = white[w, pl.ds((me ^ j) * quarter, quarter)]
 
@@ -153,9 +153,9 @@
     return pl.pallas_call(
         functools.partial(prep_kernel, parts),
         out_shape=[jax.ShapeDtypeStruct((windows, stations, 2 * TILES, LANES), BF)]
-        + [small] * (parts - 1),
+        + [small] * parts,
         in_specs=[pl.BlockSpec(memory_space=pltpu.HBM)] * 2,
-        out_specs=[vmem] * parts,
+        out_specs=[vmem] * (1 + parts),
         scratch_shapes=[
             pltpu.VMEM(records.shape, F32),
             pltpu.VMEM(table.shape, BF),
@@ -235,17 +235,16 @@
     )(*blocks)
 
 
-def widen_others(first_slot, slots, count, offsets, plan, candidates, first, other):
+def widen_others(first_slot, slots, count, places, plan, candidates, other):
     steps, ranks = partner_steps(plan, count)
-    windows = candidates[0].shape[0]
     for slot in range(slots):
         step = jnp.int32(0)
         for number in range(ROUNDS):
             step = jnp.where(ranks[number] == first_slot + slot, steps[number], step)
-        for offset, candidate in zip(offsets, candidates):
+        for (offset, first), candidate in zip(places, candidates):
 
             @pl.when(step == offset)
-            def _(candidate=candidate, slot=slot):
+            def _(candidate=candidate, slot=slot, first=first):
                 def widen_other(w, carry):
                     raw = candidate[w].astype(F32)
                     real, imag = raw[:, :TILES], raw[:, TILES:]
@@ -254,10 +253,10 @@
                     other[2, slot, first + w] = imag - real
                     return carry
 
-                lax.fori_loop(0, windows, widen_other, 0)
-
-
-def sum_windows(owns, other, before, crossed):
+                lax.fori_loop(0, candidate.shape[0], widen_other, 0)
+
+
+def sum_windows(owns, other, crossed):
     windows, stations = owns[0].shape[1:3]
     slots, _, quarter = other.shape[1:4]
     width = stations * quarter
@@ -283,8 +282,6 @@
 
         def store(place, part, value):
             at = pl.multiple_of((base + place) * 2 * TILES + part * TILES, TILES)
-            if before is not None:
-                value = value + before[pl.ds(at, TILES), :]
             crossed[pl.ds(at, TILES), :] = value
 
         base = slot * width + first * quarter
@@ -305,46 +302,14 @@
         lax.fori_loop(0, groups, body, 0)
 
 
-def near_kernel(first_slot, slots, count, offsets, plan, own, *rest):
-    candidates = rest[: len(offsets)]
-    crossed, other = rest[len(offsets) :]
-    widen_others(first_slot, slots, count, offsets, plan, candidates, 0, other)
-    sum_windows([own], other, None, crossed)
-
-
-def near_sums(plan, own, offsets, candidates, first_slot, slots, count):
-    windows, stations = own.shape[1:3]
-    quarter = candidates[0].shape[1]
-    columns = slots * stations * quarter
-    vmem = pl.BlockSpec(memory_space=pltpu.VMEM)
-    return pl.pallas_call(
-        functools.partial(near_kernel, first_slot, slots, count, tuple(offsets)),
-        out_shape=jax.ShapeDtypeStruct((columns * 2 * TILES, LANES), F32),
-        in_specs=[pl.BlockSpec(memory_space=pltpu.SMEM)] + [vmem] * (1 + len(candidates)),
-        out_specs=vmem,
-        scratch_shapes=[pltpu.VMEM((3, slots, windows, quarter, TILES, LANES), F32)],
-        compiler_params=pltpu.CompilerParams(vmem_limit_bytes=16 * 2**20),
-        cost_estimate=expected(0.05),
-        name="near",
-    )(plan, own, *candidates)
-
-
-def cross_kernel(first_slot, slots, count, scaling, offsets, parts, joint, plan, table, *rest):
-    size = len(offsets)
-    owns, rest = rest[: 1 + joint], rest[1 + joint :]
-    before = None
-    if not joint:
-        before, rest = rest[0], rest[1:]
-    others, rest = rest[: size * (1 + joint)], rest[size * (1 + joint) :]
+def cross_kernel(first_slot, slots, count, scaling, places, parts, plan, table, *rest):
+    owns, rest = rest[:2], rest[2:]
+    others, rest = rest[: len(places)], rest[len(places) :]
     outs = rest[:parts]
     other, crossed, operand, result = rest[parts:]
-    windows, stations = owns[0].shape[1:3]
-    for part in range(1 + joint):
-        widen_others(
-            first_slot, slots, count, offsets, plan, others[part * size : (part + 1) * size],
-            part * windows, other,
-        )
-    sum_windows(owns, other, before, crossed)
+    stations = owns[0].shape[2]
+    widen_others(first_slot, slots, count, places, plan, others, other)
+    sum_windows(owns, other, crossed)
     width = stations * other.shape[3]
     columns = slots * width
     even = even_lanes((columns, LANES))
@@ -389,10 +354,7 @@
         outs[j][...] = result[me ^ j]
 
 
-def cross_lags(
-    plan, table, owns, before, offsets, candidates, first_slot, slots, count, parts, scaling
-):
-    joint = len(owns) - 1
+def cross_lags(plan, table, owns, places, candidates, first_slot, slots, count, parts, scaling):
     windows, stations = owns[0].shape[1:3]
     quarter = candidates[0].shape[1]
     columns = slots * stations * quarter
@@ -400,22 +362,22 @@
     out = (share, columns) if slots > 1 else (share // 2, 2 * columns)
     smem = pl.BlockSpec(memory_space=pltpu.SMEM)
     vmem = pl.BlockSpec(memory_space=pltpu.VMEM)
-    operands = [table, *owns] + ([] if joint else [before]) + list(candidates)
+    operands = [table, *owns, *candidates]
     return pl.pallas_call(
         functools.partial(
-            cross_kernel, first_slot, slots, count, scaling, tuple(offsets), parts, joint
+            cross_kernel, first_slot, slots, count, scaling, tuple(places), parts
         ),
         out_shape=[jax.ShapeDtypeStruct(out, BF)] * parts,
         in_specs=[smem] + [vmem] * len(operands),
         out_specs=[vmem] * parts,
         scratch_shapes=[
-            pltpu.VMEM((3, slots, (1 + joint) * windows, quarter, TILES, LANES), F32),
+            pltpu.VMEM((3, slots, 2 * windows, quarter, TILES, LANES), F32),
             pltpu.VMEM((columns * 2 * TILES, LANES), F32),
             pltpu.VMEM((CHUNKS * columns, 2 * NBIN), BF),
             pltpu.VMEM((parts,) + out, BF),
         ],
         compiler_params=pltpu.CompilerParams(vmem_limit_bytes=24 * 2**20),
-        cost_estimate=expected(1 * (0.6 + 2.0 * slots) if joint else 1.7),
+        cost_estimate=expected(0.6 + 2.0 * slots),
         name="cross",
     )(plan, *operands)
 
@@ -516,6 +478,30 @@
     return out.reshape(share, ROUNDS, pairs)
 
 
+def join_kernel(order, *refs):
+    parts, (out_up, out_down) = refs[:4], refs[4:]
+    near_up, near_down, far_up, far_down = [parts[order.index(k)] for k in range(4)]
+    half = near_up.shape[0]
+    for out, first, second in ((out_up, near_up, far_up), (out_down, near_down, far_down)):
+        out[:half] = first[...]
+        out[half:] = second[...]
+
+
+def join(near_up, near_down, far_up, far_down, order=(0, 1, 2, 3)):
+    values = [near_up, near_down, far_up, far_down]
+    vmem = pl.BlockSpec(memory_space=pltpu.VMEM)
+    shape = (2 * near_up.shape[0],) + near_up.shape[1:]
+    return pl.pallas_call(
+        functools.partial(join_kernel, tuple(order)),
+        out_shape=[jax.ShapeDtypeStruct(shape, BF)] * 2,
+        in_specs=[vmem] * 4,
+        out_specs=[vmem] * 2,
+        compiler_params=pltpu.CompilerParams(vmem_limit_bytes=16 * 2**20),
+        cost_estimate=expected(0.05),
+        name="join",
+    )(*[values[k] for k in order])
+
+
 def swap(value, j):
     parts = lax.axis_size("seg")
     return lax.ppermute(value, "seg", [(i, i ^ j) for i in range(parts)])
@@ -537,11 +523,13 @@
     table = jnp.asarray(make_table(length // CHUNKS, 2 * length))
     scaling = 1.0 / math.sqrt(4.0 * NBIN * windows * parts)
 
-    white, mine, *far = prepare(records, table, parts)
+    white, *quarters = prepare(records, table, parts)
+    near = jnp.concatenate([quarters[0], swap(quarters[1], 1)])
     sibling = swap(white, 1)
-    first = lax.axis_index("seg") * quarter
-    near = jnp.concatenate([mine, lax.dynamic_slice_in_dim(sibling, first, quarter, 1)])
-    far = jnp.concatenate([swap(piece, 2 + j) for j, piece in enumerate(far)])
+    far = jnp.concatenate([swap(quarters[j], j) for j in range(2, parts)])
+    far = after(far, sibling)
+    far, white_far = lax.optimization_barrier((far, white))
+    across = swap(white_far, 2)
 
     ring = sorted(range(count), key=lambda b: b // 2 if b % 2 == 0 else count - 1 - b // 2)
     upward = [(ring[i], ring[(i + 1) % count]) for i in range(count)]
@@ -555,72 +543,47 @@
 
     far, white_far = lax.optimization_barrier((far, white))
     across = swap(white_far, 2)
-    near_up = near_down = near
-    far_up = far_down = far
     near_own = widen_own([white, sibling])
-    steps = (count - 1) // 2
+    half = near.shape[0]
+    places, blocks, arrived = [], [], []
+
+    def arrive(step, first, from_left, from_right):
+        places.extend([(count - step, first), (step, first)])
+        blocks.extend([from_left, from_right])
+
+    near_up, near_down = up(near), down(near)
+    far_up, far_down = up(far), down(far)
+    arrive(1, 0, near_up, near_down)
+    arrive(1, half, far_up, far_down)
+    near_up, near_down, near_own = lax.optimization_barrier((near_up, near_down, near_own))
+    near_up, near_down = up(near_up), down(near_down)
+    far_up, far_down = lax.optimization_barrier((far_up, far_down))
+    far_up, far_down = up(far_up), down(far_down)
+    arrive(2, 0, near_up, near_down)
+    arrive(2, half, far_up, far_down)
+    all_up, all_down = join(near_up, near_down, far_up, far_down)
+    for step in range(3, (count - 1) // 2 + 1):
+        arrived.append((list(places), list(blocks)))
+        all_up, all_down, across = lax.optimization_barrier((all_up, all_down, across))
+        all_up, all_down = up(all_up), down(all_down)
+        arrive(step, 0, all_up, all_down)
+    arrived.append((list(places), list(blocks)))
+    far_own = widen_own([across, swap(across, 1)])
     groups = [(0, 1), (1, 2), (3, 1)]
-    arrived = []
-    spots, near_blocks, far_blocks = [], [], []
-    lags, pieces = [], []
-
-    def group_lags(index, near_own, far_own):
-        first_slot, slots = groups[index]
-        at, nears, fars = arrived[index - len(groups)]
-        return cross_lags(
-            plan, table, [near_own, far_own], None, at, nears + fars, first_slot, slots, count,
-            parts, scaling,
-        )
-
-    for step in range(1, steps + 1):
-        if step == 2:
-            near_up, near_down = lax.optimization_barrier((near_up, near_down))
-        elif step > 2:
-            near_up, near_down, last_up, last_down = lax.optimization_barrier(
-                (near_up, near_down, last_up, last_down)
-            )
-        last_up, last_down = far_up, far_down
-        next_near = up(near_up), down(near_down)
-        if step == 2:
-            far_up, far_down, near_up, near_down, near_own = lax.optimization_barrier(
-                (far_up, far_down, near_up, near_down, near_own)
-            )
-        elif step == 3:
-            far_up, far_down, near_up, near_down, across = lax.optimization_barrier(
-                (far_up, far_down, near_up, near_down, across)
-            )
-        elif step > 3:
-            far_up, far_down, near_up, near_down = lax.optimization_barrier(
-                (far_up, far_down, near_up, near_down)
-            )
-        if step == steps and step > 1:
-            at, nears, _ = arrived[-1]
-            first_sums = near_sums(plan, near_own, at, nears, 0, 1, count)
-        far_up, far_down = up(far_up), down(far_down)
-        near_up, near_down = next_near
-        spots += [count - step, step]
-        near_blocks += [near_up, near_down]
-        far_blocks += [far_up, far_down]
-        arrived.append((list(spots), list(near_blocks), list(far_blocks)))
-    far_own = widen_own([across, swap(across, 1)])
-    arrived.append(arrived[-1])
-    at, _, fars = arrived[-3]
-    lags = cross_lags(
-        plan, table, [far_own], first_sums, at, fars, 0, 1, count, parts, scaling
-    )
-    pieces = exchange(lags)
     if count % 2 == 0:
-        near_up = after(near_up, lags)
-        middle_up = up(near_up)
-        far_down = after(far_down, (near_up, near_down))
-        arrived[-1] = (
-            spots + [count // 2], near_blocks + [middle_up], far_blocks + [down(far_down)]
-        )
-    for index in range(1, len(groups)):
+        places.append((count // 2, 0))
+        blocks.append(up(all_up))
+    arrived.append((places, blocks))
+    pieces = []
+    for index, (first_slot, slots) in enumerate(groups):
         if index == 2:
             near_own = after(near_own, pieces[:parts])
-        near_own = after(near_own, lags)
-        lags = group_lags(index, near_own, far_own)
+        if index > 0:
+            near_own = after(near_own, lags)
+        at, values = arrived[index - len(groups)]
+        lags = cross_lags(
+            plan, table, [near_own, far_own], at, values, first_slot, slots, count, parts, scaling
+        )
         pieces = pieces + exchange(lags)
     return place_lags(plan, groups, pieces, count, stations, parts)
 

time: 55.4 us -> 52.2 us (0.942)
  starting transfers between devices: 24.9 us -> 22.6 us
  waiting for transfers between devices: 11.1 us -> 12.7 us
  local copies, waits for them, and re-layouts: 1.46 us -> 0.04 us
  Pallas kernels: 17.6 us -> 16.5 us
    ppermute x7 -> x6, starting transfers between devices: 7.14 us -> 5.31 us  [up(): return lax.ppermute(value, 'sta', upward)]
    ppermute x7 -> x6, waiting for transfers between devices: 4.76 us -> 6.57 us  [up(): return lax.ppermute(value, 'sta', upward)]
    unnamed x6 -> x7, local copies, waits for them, and re-layouts: 1.45 us -> 0.02 us
    pallas_call x1, Pallas kernels: 1.21 us -> 0.03 us  [join(): pl.pallas_call(functools.partial(join_kernel, tuple(order)), out_shape=[j...]
    ppermute x7 -> x5, starting transfers between devices: 7.2 us -> 6.5 us  [down(): return lax.ppermute(value, 'sta', downward)]
    ppermute x14 -> x15, starting transfers between devices: 10.6 us -> 10.8 us  [swap(): return lax.ppermute(value, 'seg', [(i, i ^ j) for i in range(parts)])]
    ppermute x14 -> x15, waiting for transfers between devices: 5.74 us -> 5.56 us  [swap(): return lax.ppermute(value, 'seg', [(i, i ^ j) for i in range(parts)])]
  transfers between devices with their start and end apart: 28 -> 26, of which waited for: 11 -> 12; matrix products, arithmetic and copies ran while one was open for 0% -> 0% of each run, Pallas kernels for 22% -> 22%
where the time goes in v8:
time: 52.2 us; the launch traced here: 52.1 us
  starting transfers between devices  22.6 us (43%)
  Pallas kernels  16.5 us (32%)
  waiting for transfers between devices  12.7 us (24%)
    ppermute x15, starting transfers between devices, swap(): return lax.ppermute(value, 'seg', [(i, i ^ j) for i in range(parts)])  10.8 us
    pallas_call x3, Pallas kernels, cross_lags(): pl.pallas_call(functools.partial(cross_kernel, first_slot, slots, count,...  10.4 us
    ppermute x6, waiting for transfers between devices, up(): return lax.ppermute(value, 'sta', upward)  6.57 us
    ppermute x5, starting transfers between devices, down(): return lax.ppermute(value, 'sta', downward)  6.5 us
    ppermute x15, waiting for transfers between devices, swap(): return lax.ppermute(value, 'seg', [(i, i ^ j) for i in range(parts)])  5.56 us
    ppermute x6, starting transfers between devices, up(): return lax.ppermute(value, 'sta', upward)  5.31 us
    pallas_call x1, Pallas kernels, prepare(): pl.pallas_call(functools.partial(prep_kernel, parts), out_shape=[jax.Shap...  3.04 us
    pallas_call x1, Pallas kernels, place_lags(): pl.pallas_call(functools.partial(late_kernel, count, parts, steps), out_s...  2.25 us
  transfers between devices with their start and end apart: 26, of which 12 were waited for; matrix products, arithmetic and copies ran while one was open for 0% of the time, Pallas kernels for 22%

profile of v8, /device:TPU:0, one launch (start us, length us, event | category | flops | bytes accessed | tf_op | source)
XLA Modules:
  0.0 52.1 jit_solution(14466684316896707793)
XLA Ops:
  0.0 3.0 %prep.1 = (bf16[4,16,16,128]{3,2,1,0:T(8,128)(2,1)S(1)}, bf16[4,4,16,128]{3,2,1,0:T(8,128)(2,1)S(1)}, bf16[4,4,16,128]{3,2,1,0:T(8,128)(2,1)S(1)}, bf16[4,4,16,1...) custom-call(f32[16,4,2048]{2,1,0:T(4,128)} %records_hbm.1, bf16[512,2048]{1,0:T(8,128)(2,1)} %constant.4.clone.table_hbm.table), custom_call_target="tpu_custom_call" | custom-call | flops 536870912 | bytes 3145728 | tf_op jit(solution)/shard_map/prep/pallas_call | solution.py:153
  3.0 0.5 collective-permute-start
  3.6 2.6 %collective-permute-start.6 = (bf16[4,4,16,128]{3,2,1,0:T(8,128)(2,1)S(1)}, bf16[4,4,16,128]{3,2,1,0:T(8,128)(2,1)S(1)}, u32[]{:S(2)}, u32[]{:S(2)}) collective-permute-start(bf16[4,4,16,128]{3,2,1,0:T(8,128)(2,1)S(1)} %get-tuple-element.45), channel_id=1, source_target_pairs={{0,2},{1,3},{2,0},{3,1},{4,6},{5,7},{6,4},{7,5},{8,10},{9,11},{10,... | collective-permute-start | bytes 196616 | tf_op jit(solution)/shard_map/ppermute | solution.py:507
  6.4 2.0 %collective-permute-start.2 = (bf16[8,4,16,128]{3,2,1,0:T(8,128)(2,1)S(1)}, bf16[8,4,16,128]{3,2,1,0:T(8,128)(2,1)S(1)}, u32[]{:S(2)}, u32[]{:S(2)}) collective-permute-start(bf16[8,4,16,128]{3,2,1,0:T(8,128)(2,1)S(1)} %constant_dynamic-update-slice_fusion), channel_id=1, source_target_pairs={{0,4},{8,0},{16,8},{24,16},{28,24},{20,28},{12,20},{4,12},{1,5},{9... | collective-permute-start | bytes 393224 | tf_op jit(solution)/shard_map/ppermute | solution.py:542
  8.5 0.3 collective-permute-done.6
  8.8 1.4 %collective-permute-done.7 = bf16[4,4,16,128]{3,2,1,0:T(8,128)(2,1)S(1)} collective-permute-done((bf16[4,4,16,128]{3,2,1,0:T(8,128)(2,1)S(1)}, bf16[4,4,16,128]{3,2,1,0:T(8,128)(2,1)S(1)}, u32[]{:S(2)}, u32[]{:S(2)}) %collective-permute-start.7) | collective-permute-done | bytes 65568 | tf_op jit(solution)/shard_map/ppermute | solution.py:507
  10.2 1.6 %collective-permute-start.9 = (bf16[8,4,16,128]{3,2,1,0:T(8,128)(2,1)S(1)}, bf16[8,4,16,128]{3,2,1,0:T(8,128)(2,1)S(1)}, u32[]{:S(2)}, u32[]{:S(2)}) collective-permute-start(bf16[8,4,16,128]{3,2,1,0:T(8,128)(2,1)S(1)} %pad_maximum_fusion), channel_id=1, source_target_pairs={{0,4},{8,0},{16,8},{24,16},{28,24},{20,28},{12,20},{4,12},{1,5},{9... | collective-permute-start | bytes 393224 | tf_op jit(solution)/shard_map/ppermute | solution.py:542
  11.8 0.5 collective-permute-start.8
  12.3 1.3 %collective-permute-start.12 = (bf16[4,16,16,128]{3,2,1,0:T(8,128)(2,1)S(1)}, bf16[4,16,16,128]{3,2,1,0:T(8,128)(2,1)S(1)}, u32[]{:S(2)}, u32[]{:S(2)}) collective-permute-start(bf16[4,16,16,128]{3,2,1,0:T(8,128)(2,1)S(1)} %get-tuple-element.54.refs_0_), channel_id=1, source_target_pairs={{0,2},{1,3},{2,0},{3,1},{4,6},{5,7},{6,4},{7,5},{8,10},{9,11},{10,... | collective-permute-start | bytes 786440 | tf_op jit(solution)/shard_map/ppermute | solution.py:507
  13.8 1.6 %collective-permute-start.4 = (bf16[8,4,16,128]{3,2,1,0:T(8,128)(2,1)S(1)}, bf16[8,4,16,128]{3,2,1,0:T(8,128)(2,1)S(1)}, u32[]{:S(2)}, u32[]{:S(2)}) collective-permute-start(bf16[8,4,16,128]{3,2,1,0:T(8,128)(2,1)S(1)} %collective-permute-done.1.rest_2_), channel_id=1, source_target_pairs={{0,8},{8,16},{16,24},{24,28},{28,20},{20,12},{12,4},{4,0},{1,9},{9... | collective-permute-start | bytes 393224 | tf_op jit(solution)/shard_map/ppermute | solution.py:539
  15.4 0.4 collective-permute-start.5
  15.9 0.2 collective-permute-done.9.rest_5_
  16.1 2.0 %collective-permute-done.8.rest_4_ = bf16[8,4,16,128]{3,2,1,0:T(8,128)(2,1)S(1)} collective-permute-done((bf16[8,4,16,128]{3,2,1,0:T(8,128)(2,1)S(1)}, bf16[8,4,16,128]{3,2,1,0:T(8,128)(2,1)S(1)}, u32[]{:S(2)}, u32[]{:S(2)}) %collective-permute-start.8) | collective-permute-done | bytes 131104 | tf_op jit(solution)/shard_map/ppermute | solution.py:539
  18.1 2.0 %collective-permute-start.11 = (bf16[8,4,16,128]{3,2,1,0:T(8,128)(2,1)S(1)}, bf16[8,4,16,128]{3,2,1,0:T(8,128)(2,1)S(1)}, u32[]{:S(2)}, u32[]{:S(2)}) collective-permute-start(bf16[8,4,16,128]{3,2,1,0:T(8,128)(2,1)S(1)} %collective-permute-done.9.rest_5_), channel_id=1, source_target_pairs={{0,4},{8,0},{16,8},{24,16},{28,24},{20,28},{12,20},{4,12},{1,5},{9... | collective-permute-start | bytes 393224 | tf_op jit(solution)/shard_map/ppermute | solution.py:542
  20.1 0.8 %collective-permute-done.4.refs_0_.rest_6_ = bf16[8,4,16,128]{3,2,1,0:T(8,128)(2,1)S(1)} collective-permute-done((bf16[8,4,16,128]{3,2,1,0:T(8,128)(2,1)S(1)}, bf16[8,4,16,128]{3,2,1,0:T(8,128)(2,1)S(1)}, u32[]{:S(2)}, u32[]{:S(2)}) %collective-permute-start.4) | collective-permute-done | bytes 131104 | tf_op jit(solution)/shard_map/ppermute | solution.py:539
  21.1 1.9 %collective-permute-done.10.refs_2_.rest_8_ = bf16[8,4,16,128]{3,2,1,0:T(8,128)(2,1)S(1)} collective-permute-done((bf16[8,4,16,128]{3,2,1,0:T(8,128)(2,1)S(1)}, bf16[8,4,16,128]{3,2,1,0:T(8,128)(2,1)S(1)}, u32[]{:S(2)}, u32[]{:S(2)}) %collective-permute-start.10) | collective-permute-done | bytes 131104 | tf_op jit(solution)/shard_map/ppermute | solution.py:539
  23.3 1.6 %collective-permute-start.17 = (bf16[16,4,16,128]{3,2,1,0:T(8,128)(2,1)S(1)}, bf16[16,4,16,128]{3,2,1,0:T(8,128)(2,1)S(1)}, u32[]{:S(2)}, u32[]{:S(2)}) collective-permute-start(bf16[16,4,16,128]{3,2,1,0:T(8,128)(2,1)S(1)} %get-tuple-element.61), channel_id=1, source_target_pairs={{0,8},{8,16},{16,24},{24,28},{28,20},{20,12},{12,4},{4,0},{1,9},{9... | collective-permute-start | bytes 786440 | tf_op jit(solution)/shard_map/ppermute | solution.py:539
  25.0 0.4 collective-permute-start.18
  25.6 2.8 %cross.3 = (bf16[256,128]{1,0:T(8,128)(2,1)S(1)}, bf16[256,128]{1,0:T(8,128)(2,1)S(1)}, bf16[256,128]{1,0:T(8,128)(2,1)S(1)}, bf16[256,128]{1,0:T(8,128)(2,1)S(1)}) custom-call(s32[4,8]{1,0:T(4,128)S(1)} %copy-done.2, bf16[512,2048]{1,0:T(8,128)(2,1)S(1)} %copy-done, f32[3,8,16,8,128]{4,3,2,1,0:T(8,128)S(1)} %widen.2.rest_0_, ...), custom_call_target="tpu_custom_call" | custom-call | flops 2990000128 | bytes 1024 | tf_op jit(solution)/shard_map/cross/pallas_call | solution.py:366
  28.5 1.8 %collective-permute-start.15 = (bf16[256,128]{1,0:T(8,128)(2,1)S(1)}, bf16[256,128]{1,0:T(8,128)(2,1)S(1)}, u32[]{:S(2)}, u32[]{:S(2)}) collective-permute-start(bf16[256,128]{1,0:T(8,128)(2,1)S(1)} %get-tuple-element.58), channel_id=1, source_target_pairs={{0,2},{1,3},{2,0},{3,1},{4,6},{5,7},{6,4},{7,5},{8,10},{9,11},{10,... | collective-permute-start | bytes 196616 | tf_op jit(solution)/shard_map/ppermute | solution.py:507
  30.3 1.9 %collective-permute-done.17.rest_10_ = bf16[16,4,16,128]{3,2,1,0:T(8,128)(2,1)S(1)} collective-permute-done((bf16[16,4,16,128]{3,2,1,0:T(8,128)(2,1)S(1)}, bf16[16,4,16,128]{3,2,1,0:T(8,128)(2,1)S(1)}, u32[]{:S(2)}, u32[]{:S(2)}) %collective-permute-start.17) | collective-permute-done | bytes 262176 | tf_op jit(solution)/shard_map/ppermute | solution.py:539
  32.2 1.4 %collective-permute-start.22 = (bf16[16,4,16,128]{3,2,1,0:T(8,128)(2,1)S(1)}, bf16[16,4,16,128]{3,2,1,0:T(8,128)(2,1)S(1)}, u32[]{:S(2)}, u32[]{:S(2)}) collective-permute-start(bf16[16,4,16,128]{3,2,1,0:T(8,128)(2,1)S(1)} %collective-permute-done.17.rest_10_), channel_id=1, source_target_pairs={{0,8},{8,16},{16,24},{24,28},{28,20},{20,12},{12,4},{4,0},{1,9},{9... | collective-permute-start | bytes 786440 | tf_op jit(solution)/shard_map/ppermute | solution.py:539
  33.6 4.7 %cross.4 = (bf16[512,128]{1,0:T(8,128)(2,1)S(1)}, bf16[512,128]{1,0:T(8,128)(2,1)S(1)}, bf16[512,128]{1,0:T(8,128)(2,1)S(1)}, bf16[512,128]{1,0:T(8,128)(2,1)S(1)}) custom-call(s32[4,8]{1,0:T(4,128)S(1)} %copy-done.2, bf16[512,2048]{1,0:T(8,128)(2,1)S(1)} %copy-done, f32[3,8,16,8,128]{4,3,2,1,0:T(8,128)S(1)} %widen.2.rest_0_, ...), custom_call_target="tpu_custom_call" | custom-call | flops 5289999872 | bytes 1024 | tf_op jit(solution)/shard_map/cross/pallas_call | solution.py:366
  38.5 1.8 %collective-permute-start.20 = (bf16[512,128]{1,0:T(8,128)(2,1)S(1)}, bf16[512,128]{1,0:T(8,128)(2,1)S(1)}, u32[]{:S(2)}, u32[]{:S(2)}) collective-permute-start(bf16[512,128]{1,0:T(8,128)(2,1)S(1)} %get-tuple-element.65), channel_id=1, source_target_pairs={{0,2},{1,3},{2,0},{3,1},{4,6},{5,7},{6,4},{7,5},{8,10},{9,11},{10,... | collective-permute-start | bytes 393224 | tf_op jit(solution)/shard_map/ppermute | solution.py:507
  40.4 2.8 %cross.5 = (bf16[256,128]{1,0:T(8,128)(2,1)S(1)}, bf16[256,128]{1,0:T(8,128)(2,1)S(1)}, bf16[256,128]{1,0:T(8,128)(2,1)S(1)}, bf16[256,128]{1,0:T(8,128)(2,1)S(1)}) custom-call(s32[4,8]{1,0:T(4,128)S(1)} %copy-done.2, bf16[512,2048]{1,0:T(8,128)(2,1)S(1)} %copy-done, f32[3,8,16,8,128]{4,3,2,1,0:T(8,128)S(1)} %widen.2.rest_0_, ...), custom_call_target="tpu_custom_call" | custom-call | flops 2990000128 | bytes 1024 | tf_op jit(solution)/shard_map/cross/pallas_call | solution.py:366
  43.2 0.4 collective-permute-start.23
  43.6 1.8 %collective-permute-start.24 = (bf16[256,128]{1,0:T(8,128)(2,1)S(1)}, bf16[256,128]{1,0:T(8,128)(2,1)S(1)}, u32[]{:S(2)}, u32[]{:S(2)}) collective-permute-start(bf16[256,128]{1,0:T(8,128)(2,1)S(1)} %get-tuple-element.71), channel_id=1, source_target_pairs={{0,2},{1,3},{2,0},{3,1},{4,6},{5,7},{6,4},{7,5},{8,10},{9,11},{10,... | collective-permute-start | bytes 196616 | tf_op jit(solution)/shard_map/ppermute | solution.py:507
  45.4 1.5 %collective-permute-done.21.rest_7_ = bf16[512,128]{1,0:T(8,128)(2,1)S(1)} collective-permute-done((bf16[512,128]{1,0:T(8,128)(2,1)S(1)}, bf16[512,128]{1,0:T(8,128)(2,1)S(1)}, u32[]{:S(2)}, u32[]{:S(2)}) %collective-permute-start.21) | collective-permute-done | bytes 131104 | tf_op jit(solution)/shard_map/ppermute | solution.py:507
  46.9 0.6 %early.1 = f32[3,2,256,256]{3,2,1,0:T(8,128)S(1)} custom-call(bf16[4,128,512]{2,1,0:T(8,128)(2,1)S(1)} %copy-done.1, bf16[256,128]{1,0:T(8,128)(2,1)S(1)} %get-tuple-element.56.rest_0_, bf16[256,128]{1,0:T(8,128)(2,1)S(1)} %collective-permute-done.14.rest_1_, bf16[256,128]{1,0:T(8,128)(2,1)S(1)} %collective-permute-done.15.rest_2_, ...), custom_call_target="tpu_custom_call" | custom-call | flops 57500000 | bytes 1024 | tf_op jit(solution)/shard_map/early/pallas_call | solution.py:458
  47.5 1.3 %collective-permute-done.24.rest_2_ = bf16[256,128]{1,0:T(8,128)(2,1)S(1)} collective-permute-done((bf16[256,128]{1,0:T(8,128)(2,1)S(1)}, bf16[256,128]{1,0:T(8,128)(2,1)S(1)}, u32[]{:S(2)}, u32[]{:S(2)}) %collective-permute-start.24) | collective-permute-done | bytes 65568 | tf_op jit(solution)/shard_map/ppermute | solution.py:507
  48.7 1.1 %collective-permute-done.25.rest_3_ = bf16[256,128]{1,0:T(8,128)(2,1)S(1)} collective-permute-done((bf16[256,128]{1,0:T(8,128)(2,1)S(1)}, bf16[256,128]{1,0:T(8,128)(2,1)S(1)}, u32[]{:S(2)}, u32[]{:S(2)}) %collective-permute-start.25) | collective-permute-done | bytes 65568 | tf_op jit(solution)/shard_map/ppermute | solution.py:507
  49.8 2.2 %late.1 = f32[2,256,4,256]{3,2,1,0:T(4,128)} custom-call(s32[4,8]{1,0:T(4,128)S(1)} %copy-done.2, bf16[4,128,512]{2,1,0:T(8,128)(2,1)S(1)} %copy-done.1, f32[3,2,256,256]{3,2,1,0:T(8,128)S(1)} %early.1, bf16[256,128]{1,0:T(8,128)(2,1)S(1)} %get-tuple-element.69.rest_0_, bf16[256,128]{1,0:T(8,128)(2,1)S(1)} %collective-permute-done.23.rest_1_, ...), custom_call_target="tpu_custom_call" | custom-call | flops 57500000 | bytes 1024 | tf_op jit(solution)/shard_map/late/pallas_call | solution.py:468
  (38 shorter events, 1.5 us)
Async XLA Ops:
  3.0 3.3 %collective-permute-start = (bf16[4,4,16,128]{3,2,1,0:T(8,128)(2,1)S(1)}, bf16[4,4,16,128]{3,2,1,0:T(8,128)(2,1)S(1)}, u32[]{:S(2)}, u32[]{:S(2)}) collective-permute-start(bf16[4,4,16,128]{3,2,1,0:T(8,128)(2,1)S(1)} %get-tuple-element.40), channel_id=1, source_target_pairs={{0,1},{1,0},{2,3},{3,2},{4,5},{5,4},{6,7},{7,6},{8,9},{9,8},{10,11... | collective-permute-start | bytes 196616 | tf_op jit(solution)/shard_map/ppermute | solution.py:507
  3.6 5.3 %collective-permute-start.6 = (bf16[4,4,16,128]{3,2,1,0:T(8,128)(2,1)S(1)}, bf16[4,4,16,128]{3,2,1,0:T(8,128)(2,1)S(1)}, u32[]{:S(2)}, u32[]{:S(2)}) collective-permute-start(bf16[4,4,16,128]{3,2,1,0:T(8,128)(2,1)S(1)} %get-tuple-element.45), channel_id=1, source_target_pairs={{0,2},{1,3},{2,0},{3,1},{4,6},{5,7},{6,4},{7,5},{8,10},{9,11},{10,... | collective-permute-start | bytes 196616 | tf_op jit(solution)/shard_map/ppermute | solution.py:507
  6.1 4.0 %collective-permute-start.7 = (bf16[4,4,16,128]{3,2,1,0:T(8,128)(2,1)S(1)}, bf16[4,4,16,128]{3,2,1,0:T(8,128)(2,1)S(1)}, u32[]{:S(2)}, u32[]{:S(2)}) collective-permute-start(bf16[4,4,16,128]{3,2,1,0:T(8,128)(2,1)S(1)} %get-tuple-element.46), channel_id=1, source_target_pairs={{0,3},{1,2},{2,1},{3,0},{4,7},{5,6},{6,5},{7,4},{8,11},{9,10},{10,... | collective-permute-start | bytes 196616 | tf_op jit(solution)/shard_map/ppermute | solution.py:507
  6.2 4.0 %collective-permute-start.3 = (bf16[4,16,16,128]{3,2,1,0:T(8,128)(2,1)S(1)}, bf16[4,16,16,128]{3,2,1,0:T(8,128)(2,1)S(1)}, u32[]{:S(2)}, u32[]{:S(2)}) collective-permute-start(bf16[4,16,16,128]{3,2,1,0:T(8,128)(2,1)S(1)} %get-tuple-element.54.refs_0_), channel_id=1, source_target_pairs={{0,1},{1,0},{2,3},{3,2},{4,5},{5,4},{6,7},{7,6},{8,9},{9,8},{10,11... | collective-permute-start | bytes 786440 | tf_op jit(solution)/shard_map/ppermute | solution.py:507
  6.4 7.4 %collective-permute-start.2 = (bf16[8,4,16,128]{3,2,1,0:T(8,128)(2,1)S(1)}, bf16[8,4,16,128]{3,2,1,0:T(8,128)(2,1)S(1)}, u32[]{:S(2)}, u32[]{:S(2)}) collective-permute-start(bf16[8,4,16,128]{3,2,1,0:T(8,128)(2,1)S(1)} %constant_dynamic-update-slice_fusion), channel_id=1, source_target_pairs={{0,4},{8,0},{16,8},{24,16},{28,24},{20,28},{12,20},{4,12},{1,5},{9... | collective-permute-start | bytes 393224 | tf_op jit(solution)/shard_map/ppermute | solution.py:542
  8.4 5.4 %collective-permute-start.1 = (bf16[8,4,16,128]{3,2,1,0:T(8,128)(2,1)S(1)}, bf16[8,4,16,128]{3,2,1,0:T(8,128)(2,1)S(1)}, u32[]{:S(2)}, u32[]{:S(2)}) collective-permute-start(bf16[8,4,16,128]{3,2,1,0:T(8,128)(2,1)S(1)} %constant_dynamic-update-slice_fusion), channel_id=1, source_target_pairs={{0,8},{8,16},{16,24},{24,28},{28,20},{20,12},{12,4},{4,0},{1,9},{9... | collective-permute-start | bytes 393224 | tf_op jit(solution)/shard_map/ppermute | solution.py:539
  10.2 5.9 %collective-permute-start.9 = (bf16[8,4,16,128]{3,2,1,0:T(8,128)(2,1)S(1)}, bf16[8,4,16,128]{3,2,1,0:T(8,128)(2,1)S(1)}, u32[]{:S(2)}, u32[]{:S(2)}) collective-permute-start(bf16[8,4,16,128]{3,2,1,0:T(8,128)(2,1)S(1)} %pad_maximum_fusion), channel_id=1, source_target_pairs={{0,4},{8,0},{16,8},{24,16},{28,24},{20,28},{12,20},{4,12},{1,5},{9... | collective-permute-start | bytes 393224 | tf_op jit(solution)/shard_map/ppermute | solution.py:542
  11.8 6.3 %collective-permute-start.8 = (bf16[8,4,16,128]{3,2,1,0:T(8,128)(2,1)S(1)}, bf16[8,4,16,128]{3,2,1,0:T(8,128)(2,1)S(1)}, u32[]{:S(2)}, u32[]{:S(2)}) collective-permute-start(bf16[8,4,16,128]{3,2,1,0:T(8,128)(2,1)S(1)} %pad_maximum_fusion), channel_id=1, source_target_pairs={{0,8},{8,16},{16,24},{24,28},{28,20},{20,12},{12,4},{4,0},{1,9},{9... | collective-permute-start | bytes 393224 | tf_op jit(solution)/shard_map/ppermute | solution.py:539
  12.3 11.0 %collective-permute-start.12 = (bf16[4,16,16,128]{3,2,1,0:T(8,128)(2,1)S(1)}, bf16[4,16,16,128]{3,2,1,0:T(8,128)(2,1)S(1)}, u32[]{:S(2)}, u32[]{:S(2)}) collective-permute-start(bf16[4,16,16,128]{3,2,1,0:T(8,128)(2,1)S(1)} %get-tuple-element.54.refs_0_), channel_id=1, source_target_pairs={{0,2},{1,3},{2,0},{3,1},{4,6},{5,7},{6,4},{7,5},{8,10},{9,11},{10,... | collective-permute-start | bytes 786440 | tf_op jit(solution)/shard_map/ppermute | solution.py:507
  13.8 11.8 %copy-start = (bf16[512,2048]{1,0:T(8,128)(2,1)S(1)}, bf16[512,2048]{1,0:T(8,128)(2,1)}, u32[]{:S(2)}) copy-start(bf16[512,2048]{1,0:T(8,128)(2,1)} %constant.4.clone.table_hbm.table) | copy-start | bytes 6291460
  13.8 11.8 %copy-start.2 = (s32[4,8]{1,0:T(4,128)S(1)}, s32[4,8]{1,0:T(4,128)}, u32[]{:S(2)}) copy-start(s32[4,8]{1,0:T(4,128)} %plan.7) | copy-start | bytes 388
  13.8 7.1 %collective-permute-start.4 = (bf16[8,4,16,128]{3,2,1,0:T(8,128)(2,1)S(1)}, bf16[8,4,16,128]{3,2,1,0:T(8,128)(2,1)S(1)}, u32[]{:S(2)}, u32[]{:S(2)}) collective-permute-start(bf16[8,4,16,128]{3,2,1,0:T(8,128)(2,1)S(1)} %collective-permute-done.1.rest_2_), channel_id=1, source_target_pairs={{0,8},{8,16},{16,24},{24,28},{28,20},{20,12},{12,4},{4,0},{1,9},{9... | collective-permute-start | bytes 393224 | tf_op jit(solution)/shard_map/ppermute | solution.py:539
  15.4 5.7 %collective-permute-start.5 = (bf16[8,4,16,128]{3,2,1,0:T(8,128)(2,1)S(1)}, bf16[8,4,16,128]{3,2,1,0:T(8,128)(2,1)S(1)}, u32[]{:S(2)}, u32[]{:S(2)}) collective-permute-start(bf16[8,4,16,128]{3,2,1,0:T(8,128)(2,1)S(1)} %collective-permute-done.2.rest_3_), channel_id=1, source_target_pairs={{0,4},{8,0},{16,8},{24,16},{28,24},{20,28},{12,20},{4,12},{1,5},{9... | collective-permute-start | bytes 393224 | tf_op jit(solution)/shard_map/ppermute | solution.py:542
  18.1 5.0 %collective-permute-start.10 = (bf16[8,4,16,128]{3,2,1,0:T(8,128)(2,1)S(1)}, bf16[8,4,16,128]{3,2,1,0:T(8,128)(2,1)S(1)}, u32[]{:S(2)}, u32[]{:S(2)}) collective-permute-start(bf16[8,4,16,128]{3,2,1,0:T(8,128)(2,1)S(1)} %collective-permute-done.8.rest_4_), channel_id=1, source_target_pairs={{0,8},{8,16},{16,24},{24,28},{28,20},{20,12},{12,4},{4,0},{1,9},{9... | collective-permute-start | bytes 393224 | tf_op jit(solution)/shard_map/ppermute | solution.py:539
  18.1 5.1 %collective-permute-start.11 = (bf16[8,4,16,128]{3,2,1,0:T(8,128)(2,1)S(1)}, bf16[8,4,16,128]{3,2,1,0:T(8,128)(2,1)S(1)}, u32[]{:S(2)}, u32[]{:S(2)}) collective-permute-start(bf16[8,4,16,128]{3,2,1,0:T(8,128)(2,1)S(1)} %collective-permute-done.9.rest_5_), channel_id=1, source_target_pairs={{0,4},{8,0},{16,8},{24,16},{28,24},{20,28},{12,20},{4,12},{1,5},{9... | collective-permute-start | bytes 393224 | tf_op jit(solution)/shard_map/ppermute | solution.py:542
  23.3 2.2 %collective-permute-start.13 = (bf16[4,16,16,128]{3,2,1,0:T(8,128)(2,1)S(1)}, bf16[4,16,16,128]{3,2,1,0:T(8,128)(2,1)S(1)}, u32[]{:S(2)}, u32[]{:S(2)}) collective-permute-start(bf16[4,16,16,128]{3,2,1,0:T(8,128)(2,1)S(1)} %collective-permute-done.12.refs_0_), channel_id=1, source_target_pairs={{0,1},{1,0},{2,3},{3,2},{4,5},{5,4},{6,7},{7,6},{8,9},{9,8},{10,11... | collective-permute-start | bytes 786440 | tf_op jit(solution)/shard_map/ppermute | solution.py:507
  23.3 8.9 %collective-permute-start.17 = (bf16[16,4,16,128]{3,2,1,0:T(8,128)(2,1)S(1)}, bf16[16,4,16,128]{3,2,1,0:T(8,128)(2,1)S(1)}, u32[]{:S(2)}, u32[]{:S(2)}) collective-permute-start(bf16[16,4,16,128]{3,2,1,0:T(8,128)(2,1)S(1)} %get-tuple-element.61), channel_id=1, source_target_pairs={{0,8},{8,16},{16,24},{24,28},{28,20},{20,12},{12,4},{4,0},{1,9},{9... | collective-permute-start | bytes 786440 | tf_op jit(solution)/shard_map/ppermute | solution.py:539
  25.0 8.7 %collective-permute-start.18 = (bf16[16,4,16,128]{3,2,1,0:T(8,128)(2,1)S(1)}, bf16[16,4,16,128]{3,2,1,0:T(8,128)(2,1)S(1)}, u32[]{:S(2)}, u32[]{:S(2)}) collective-permute-start(bf16[16,4,16,128]{3,2,1,0:T(8,128)(2,1)S(1)} %get-tuple-element.62), channel_id=1, source_target_pairs={{0,4},{8,0},{16,8},{24,16},{28,24},{20,28},{12,20},{4,12},{1,5},{9... | collective-permute-start | bytes 786440 | tf_op jit(solution)/shard_map/ppermute | solution.py:542
  28.4 10.1 %collective-permute-start.14 = (bf16[256,128]{1,0:T(8,128)(2,1)S(1)}, bf16[256,128]{1,0:T(8,128)(2,1)S(1)}, u32[]{:S(2)}, u32[]{:S(2)}) collective-permute-start(bf16[256,128]{1,0:T(8,128)(2,1)S(1)} %get-tuple-element.57), channel_id=1, source_target_pairs={{0,1},{1,0},{2,3},{3,2},{4,5},{5,4},{6,7},{7,6},{8,9},{9,8},{10,11... | collective-permute-start | bytes 196616 | tf_op jit(solution)/shard_map/ppermute | solution.py:507
  28.5 11.8 %collective-permute-start.15 = (bf16[256,128]{1,0:T(8,128)(2,1)S(1)}, bf16[256,128]{1,0:T(8,128)(2,1)S(1)}, u32[]{:S(2)}, u32[]{:S(2)}) collective-permute-start(bf16[256,128]{1,0:T(8,128)(2,1)S(1)} %get-tuple-element.58), channel_id=1, source_target_pairs={{0,2},{1,3},{2,0},{3,1},{4,6},{5,7},{6,4},{7,5},{8,10},{9,11},{10,... | collective-permute-start | bytes 196616 | tf_op jit(solution)/shard_map/ppermute | solution.py:507
  30.3 10.1 %collective-permute-start.16 = (bf16[256,128]{1,0:T(8,128)(2,1)S(1)}, bf16[256,128]{1,0:T(8,128)(2,1)S(1)}, u32[]{:S(2)}, u32[]{:S(2)}) collective-permute-start(bf16[256,128]{1,0:T(8,128)(2,1)S(1)} %get-tuple-element.59), channel_id=1, source_target_pairs={{0,3},{1,2},{2,1},{3,0},{4,7},{5,6},{6,5},{7,4},{8,11},{9,10},{10,... | collective-permute-start | bytes 196616 | tf_op jit(solution)/shard_map/ppermute | solution.py:507
  32.2 8.2 %collective-permute-start.22 = (bf16[16,4,16,128]{3,2,1,0:T(8,128)(2,1)S(1)}, bf16[16,4,16,128]{3,2,1,0:T(8,128)(2,1)S(1)}, u32[]{:S(2)}, u32[]{:S(2)}) collective-permute-start(bf16[16,4,16,128]{3,2,1,0:T(8,128)(2,1)S(1)} %collective-permute-done.17.rest_10_), channel_id=1, source_target_pairs={{0,8},{8,16},{16,24},{24,28},{28,20},{20,12},{12,4},{4,0},{1,9},{9... | collective-permute-start | bytes 786440 | tf_op jit(solution)/shard_map/ppermute | solution.py:539
  38.4 7.0 %collective-permute-start.19 = (bf16[512,128]{1,0:T(8,128)(2,1)S(1)}, bf16[512,128]{1,0:T(8,128)(2,1)S(1)}, u32[]{:S(2)}, u32[]{:S(2)}) collective-permute-start(bf16[512,128]{1,0:T(8,128)(2,1)S(1)} %get-tuple-element.64), channel_id=1, source_target_pairs={{0,1},{1,0},{2,3},{3,2},{4,5},{5,4},{6,7},{7,6},{8,9},{9,8},{10,11... | collective-permute-start | bytes 393224 | tf_op jit(solution)/shard_map/ppermute | solution.py:507
  38.5 6.9 %collective-permute-start.20 = (bf16[512,128]{1,0:T(8,128)(2,1)S(1)}, bf16[512,128]{1,0:T(8,128)(2,1)S(1)}, u32[]{:S(2)}, u32[]{:S(2)}) collective-permute-start(bf16[512,128]{1,0:T(8,128)(2,1)S(1)} %get-tuple-element.65), channel_id=1, source_target_pairs={{0,2},{1,3},{2,0},{3,1},{4,6},{5,7},{6,4},{7,5},{8,10},{9,11},{10,... | collective-permute-start | bytes 393224 | tf_op jit(solution)/shard_map/ppermute | solution.py:507
  40.3 6.6 %collective-permute-start.21 = (bf16[512,128]{1,0:T(8,128)(2,1)S(1)}, bf16[512,128]{1,0:T(8,128)(2,1)S(1)}, u32[]{:S(2)}, u32[]{:S(2)}) collective-permute-start(bf16[512,128]{1,0:T(8,128)(2,1)S(1)} %get-tuple-element.66), channel_id=1, source_target_pairs={{0,3},{1,2},{2,1},{3,0},{4,7},{5,6},{6,5},{7,4},{8,11},{9,10},{10,... | collective-permute-start | bytes 393224 | tf_op jit(solution)/shard_map/ppermute | solution.py:507
  40.4 6.5 %copy-start.1 = (bf16[4,128,512]{2,1,0:T(8,128)(2,1)S(1)}, bf16[4,128,512]{2,1,0:T(8,128)(2,1)}, u32[]{:S(2)}) copy-start(bf16[4,128,512]{2,1,0:T(8,128)(2,1)} %constant.5.clone.place) | copy-start | bytes 1572868
  43.2 4.3 %collective-permute-start.23 = (bf16[256,128]{1,0:T(8,128)(2,1)S(1)}, bf16[256,128]{1,0:T(8,128)(2,1)S(1)}, u32[]{:S(2)}, u32[]{:S(2)}) collective-permute-start(bf16[256,128]{1,0:T(8,128)(2,1)S(1)} %get-tuple-element.70), channel_id=1, source_target_pairs={{0,1},{1,0},{2,3},{3,2},{4,5},{5,4},{6,7},{7,6},{8,9},{9,8},{10,11... | collective-permute-start | bytes 196616 | tf_op jit(solution)/shard_map/ppermute | solution.py:507
  43.6 5.1 %collective-permute-start.24 = (bf16[256,128]{1,0:T(8,128)(2,1)S(1)}, bf16[256,128]{1,0:T(8,128)(2,1)S(1)}, u32[]{:S(2)}, u32[]{:S(2)}) collective-permute-start(bf16[256,128]{1,0:T(8,128)(2,1)S(1)} %get-tuple-element.71), channel_id=1, source_target_pairs={{0,2},{1,3},{2,0},{3,1},{4,6},{5,7},{6,4},{7,5},{8,10},{9,11},{10,... | collective-permute-start | bytes 196616 | tf_op jit(solution)/shard_map/ppermute | solution.py:507
  45.4 4.5 %collective-permute-start.25 = (bf16[256,128]{1,0:T(8,128)(2,1)S(1)}, bf16[256,128]{1,0:T(8,128)(2,1)S(1)}, u32[]{:S(2)}, u32[]{:S(2)}) collective-permute-start(bf16[256,128]{1,0:T(8,128)(2,1)S(1)} %get-tuple-element.72), channel_id=1, source_target_pairs={{0,3},{1,2},{2,1},{3,0},{4,7},{5,6},{6,5},{7,4},{8,11},{9,10},{10,... | collective-permute-start | bytes 196616 | tf_op jit(solution)/shard_map/ppermute | solution.py:507

commit v9 on v8

--- a/solution.py
+++ b/solution.py
@@ -262,6 +262,7 @@
     width = stations * quarter
     group = 4
     groups = stations // group
+    shift = groups.bit_length() - 1
 
     def one_group(slot, index):
         first = index * group
@@ -293,20 +294,18 @@
         for place in range(group * quarter):
             store(place, 1, shared[place] - second[place])
 
-    for slot in range(slots):
-
-        def body(index, carry, slot=slot):
-            one_group(slot, index)
-            return carry
-
-        lax.fori_loop(0, groups, body, 0)
+    def body(index, carry):
+        one_group(index >> shift, index & (groups - 1))
+        return carry
+
+    lax.fori_loop(0, slots * groups, body, 0)
 
 
 def cross_kernel(first_slot, slots, count, scaling, places, parts, plan, table, *rest):
     owns, rest = rest[:2], rest[2:]
     others, rest = rest[: len(places)], rest[len(places) :]
     outs = rest[:parts]
-    other, crossed, operand, result = rest[parts:]
+    other, crossed, operand = rest[parts:]
     stations = owns[0].shape[2]
     widen_others(first_slot, slots, count, places, plan, others, other)
     sum_windows(owns, other, crossed)
@@ -318,6 +317,8 @@
     cosine, sine = eighth_turn()
     lane = lax.broadcasted_iota(jnp.int32, (1, LANES), 1)
     first_weight = jnp.where(lane == 0, 1.0, 2.0).astype(F32)
+    me = lax.axis_index("seg")
+    rows = [pl.ds(pl.multiple_of((me ^ q) * columns, columns), columns) for q in range(CHUNKS)]
     for j in range(TILES):
         at = slice(j * LANES, (j + 1) * LANES)
         at_imag = slice(NBIN + j * LANES, NBIN + (j + 1) * LANES)
@@ -327,9 +328,8 @@
         turned = [(real, imag), (real * cosine - imag * sine, imag * cosine + real * sine)]
         turned += [quarter_turns(r, i, even, sign_real, sign_imag) for r, i in turned]
         for q in range(CHUNKS):
-            rows = slice(q * columns, (q + 1) * columns)
-            operand[rows, at] = turned[q][0].astype(BF)
-            operand[rows, at_imag] = turned[q][1].astype(BF)
+            operand[rows[q], at] = turned[q][0].astype(BF)
+            operand[rows[q], at_imag] = turned[q][1].astype(BF)
     block = lax.dot_general(
         table[...], operand[...], (((1,), (1,)), ((), ())), preferred_element_type=F32
     )
@@ -345,13 +345,10 @@
                 jnp.where(low_lanes, pltpu.roll(low, width, 1), high),
             )
             for second in range(2):
-                result[2 * p + second] = pair[second].astype(BF)
+                outs[2 * p + second][...] = pair[second].astype(BF)
     else:
-        for q in range(CHUNKS):
-            result[q] = block[:, q * columns : (q + 1) * columns].astype(BF)
-    me = lax.axis_index("seg")
-    for j in range(parts):
-        outs[j][...] = result[me ^ j]
+        for j in range(parts):
+            outs[j][...] = block[:, j * columns : (j + 1) * columns].astype(BF)
 
 
 def cross_lags(plan, table, owns, places, candidates, first_slot, slots, count, parts, scaling):
@@ -374,7 +371,6 @@
             pltpu.VMEM((3, slots, 2 * windows, quarter, TILES, LANES), F32),
             pltpu.VMEM((columns * 2 * TILES, LANES), F32),
             pltpu.VMEM((CHUNKS * columns, 2 * NBIN), BF),
-            pltpu.VMEM((parts,) + out, BF),
         ],
         compiler_params=pltpu.CompilerParams(vmem_limit_bytes=24 * 2**20),
         cost_estimate=expected(0.6 + 2.0 * slots),
@@ -427,7 +423,9 @@
 def late_kernel(count, parts, steps, plan, place, early, *rest):
     pieces = rest[:parts]
     out_hbm, out, sems = rest[parts:]
-    half, _, pairs = out.shape[1:]
+    half, pairs = early.shape[2:]
+    tiles = pairs // LANES
+    lag_rows = tiles * ROUNDS
     rows = half // steps
     rounds = slot_rounds(plan, count)
     matrix = joined_matrix(place, parts)
@@ -436,11 +434,19 @@
     for step in range(steps):
         at = slice(step * rows, (step + 1) * rows)
         for h in range(2):
-            for slot in range(ROUNDS - 1):
-                out[h, at, rounds[slot], :] = early[slot, h, at, :]
-            out[h, at, rounds[ROUNDS - 1], :] = block[at, h * pairs : (h + 1) * pairs]
+            first = (h * half + step * rows) * lag_rows
+            for slot in range(ROUNDS):
+                for tile in range(tiles):
+                    lanes = slice(tile * LANES, (tile + 1) * LANES)
+                    if slot < ROUNDS - 1:
+                        value = early[slot, h, at, lanes]
+                    else:
+                        value = block[at, h * pairs + lanes.start : h * pairs + lanes.stop]
+                    start = first + tile * ROUNDS + rounds[slot]
+                    out[pl.ds(start, rows, stride=lag_rows), :] = value
+            chunk = pl.ds(first, rows * lag_rows)
             copy = pltpu.make_async_copy(
-                out.at[h, at], out_hbm.at[h, at], sems.at[2 * step + h]
+                out.at[chunk], out_hbm.at[chunk], sems.at[2 * step + h]
             )
             copy.start()
             copies.append(copy)
@@ -464,7 +470,7 @@
         cost_estimate=expected(0.05),
         name="early",
     )(place, *pieces[:-parts])
-    shape = (2, half, ROUNDS, pairs)
+    shape = (share * ROUNDS * pairs // LANES, LANES)
     out = pl.pallas_call(
         functools.partial(late_kernel, count, parts, steps),
         out_shape=jax.ShapeDtypeStruct(shape, F32),
@@ -475,7 +481,8 @@
         cost_estimate=expected(0.05),
         name="late",
     )(plan, place, early, *pieces[-parts:])
-    return out.reshape(share, ROUNDS, pairs)
+    out = out.reshape(share, pairs // LANES, ROUNDS, LANES)
+    return out.transpose(0, 2, 1, 3).reshape(share, ROUNDS, pairs)
 
 
 def join_kernel(order, *refs):

time: 52.2 us -> 53.2 us (1.019)
  Pallas kernels: 16.5 us -> 18 us
    pallas_call x3, Pallas kernels: 10.4 us -> 11.9 us  [cross_lags(): pl.pallas_call(functools.partial(cross_kernel, first_slot, slots, count,...]
  transfers between devices with their start and end apart: 26 -> 26, of which waited for: 12 -> 12; matrix products, arithmetic and copies ran while one was open for 0% -> 0% of each run, Pallas kernels for 22% -> 24%
where the time goes in v9:
time: 53.2 us; the launch traced here: 53 us
  starting transfers between devices  22.5 us (42%)
  Pallas kernels  18 us (34%)
  waiting for transfers between devices  12.3 us (23%)
    pallas_call x3, Pallas kernels, cross_lags(): pl.pallas_call(functools.partial(cross_kernel, first_slot, slots, count,...  11.9 us
    ppermute x15, starting transfers between devices, swap(): return lax.ppermute(value, 'seg', [(i, i ^ j) for i in range(parts)])  10.7 us
    ppermute x5, starting transfers between devices, down(): return lax.ppermute(value, 'sta', downward)  6.5 us
    ppermute x6, waiting for transfers between devices, up(): return lax.ppermute(value, 'sta', upward)  6.24 us
    ppermute x15, waiting for transfers between devices, swap(): return lax.ppermute(value, 'seg', [(i, i ^ j) for i in range(parts)])  5.43 us
    ppermute x6, starting transfers between devices, up(): return lax.ppermute(value, 'sta', upward)  5.31 us
    pallas_call x1, Pallas kernels, prepare(): pl.pallas_call(functools.partial(prep_kernel, parts), out_shape=[jax.Shap...  3.04 us
    pallas_call x1, Pallas kernels, place_lags(): pl.pallas_call(functools.partial(late_kernel, count, parts, steps), out_s...  2.2 us
  transfers between devices with their start and end apart: 26, of which 12 were waited for; matrix products, arithmetic and copies ran while one was open for 0% of the time, Pallas kernels for 24%

profile of v9, /device:TPU:0, one launch (start us, length us, event | category | flops | bytes accessed | tf_op | source)
XLA Modules:
  0.0 53.0 jit_solution(5477610813430872826)
XLA Ops:
  0.0 3.0 %prep.1 = (bf16[4,16,16,128]{3,2,1,0:T(8,128)(2,1)S(1)}, bf16[4,4,16,128]{3,2,1,0:T(8,128)(2,1)S(1)}, bf16[4,4,16,128]{3,2,1,0:T(8,128)(2,1)S(1)}, bf16[4,4,16,1...) custom-call(f32[16,4,2048]{2,1,0:T(4,128)} %records_hbm.1, bf16[512,2048]{1,0:T(8,128)(2,1)} %constant.4.clone.table_hbm.table), custom_call_target="tpu_custom_call" | custom-call | flops 536870912 | bytes 3145728 | tf_op jit(solution)/shard_map/prep/pallas_call | solution.py:153
  3.0 0.5 collective-permute-start
  3.6 2.6 %collective-permute-start.6 = (bf16[4,4,16,128]{3,2,1,0:T(8,128)(2,1)S(1)}, bf16[4,4,16,128]{3,2,1,0:T(8,128)(2,1)S(1)}, u32[]{:S(2)}, u32[]{:S(2)}) collective-permute-start(bf16[4,4,16,128]{3,2,1,0:T(8,128)(2,1)S(1)} %get-tuple-element.45), channel_id=1, source_target_pairs={{0,2},{1,3},{2,0},{3,1},{4,6},{5,7},{6,4},{7,5},{8,10},{9,11},{10,... | collective-permute-start | bytes 196616 | tf_op jit(solution)/shard_map/ppermute | solution.py:514
  6.4 2.0 %collective-permute-start.2 = (bf16[8,4,16,128]{3,2,1,0:T(8,128)(2,1)S(1)}, bf16[8,4,16,128]{3,2,1,0:T(8,128)(2,1)S(1)}, u32[]{:S(2)}, u32[]{:S(2)}) collective-permute-start(bf16[8,4,16,128]{3,2,1,0:T(8,128)(2,1)S(1)} %constant_dynamic-update-slice_fusion), channel_id=1, source_target_pairs={{0,4},{8,0},{16,8},{24,16},{28,24},{20,28},{12,20},{4,12},{1,5},{9... | collective-permute-start | bytes 393224 | tf_op jit(solution)/shard_map/ppermute | solution.py:549
  8.5 0.3 collective-permute-done.6
  8.8 1.4 %collective-permute-done.7 = bf16[4,4,16,128]{3,2,1,0:T(8,128)(2,1)S(1)} collective-permute-done((bf16[4,4,16,128]{3,2,1,0:T(8,128)(2,1)S(1)}, bf16[4,4,16,128]{3,2,1,0:T(8,128)(2,1)S(1)}, u32[]{:S(2)}, u32[]{:S(2)}) %collective-permute-start.7) | collective-permute-done | bytes 65568 | tf_op jit(solution)/shard_map/ppermute | solution.py:514
  10.2 1.6 %collective-permute-start.9 = (bf16[8,4,16,128]{3,2,1,0:T(8,128)(2,1)S(1)}, bf16[8,4,16,128]{3,2,1,0:T(8,128)(2,1)S(1)}, u32[]{:S(2)}, u32[]{:S(2)}) collective-permute-start(bf16[8,4,16,128]{3,2,1,0:T(8,128)(2,1)S(1)} %pad_maximum_fusion), channel_id=1, source_target_pairs={{0,4},{8,0},{16,8},{24,16},{28,24},{20,28},{12,20},{4,12},{1,5},{9... | collective-permute-start | bytes 393224 | tf_op jit(solution)/shard_map/ppermute | solution.py:549
  11.8 0.5 collective-permute-start.8
  12.3 1.3 %collective-permute-start.12 = (bf16[4,16,16,128]{3,2,1,0:T(8,128)(2,1)S(1)}, bf16[4,16,16,128]{3,2,1,0:T(8,128)(2,1)S(1)}, u32[]{:S(2)}, u32[]{:S(2)}) collective-permute-start(bf16[4,16,16,128]{3,2,1,0:T(8,128)(2,1)S(1)} %get-tuple-element.54.refs_0_), channel_id=1, source_target_pairs={{0,2},{1,3},{2,0},{3,1},{4,6},{5,7},{6,4},{7,5},{8,10},{9,11},{10,... | collective-permute-start | bytes 786440 | tf_op jit(solution)/shard_map/ppermute | solution.py:514
  13.8 1.6 %collective-permute-start.4 = (bf16[8,4,16,128]{3,2,1,0:T(8,128)(2,1)S(1)}, bf16[8,4,16,128]{3,2,1,0:T(8,128)(2,1)S(1)}, u32[]{:S(2)}, u32[]{:S(2)}) collective-permute-start(bf16[8,4,16,128]{3,2,1,0:T(8,128)(2,1)S(1)} %collective-permute-done.1.rest_2_), channel_id=1, source_target_pairs={{0,8},{8,16},{16,24},{24,28},{28,20},{20,12},{12,4},{4,0},{1,9},{9... | collective-permute-start | bytes 393224 | tf_op jit(solution)/shard_map/ppermute | solution.py:546
  15.4 0.4 collective-permute-start.5
  15.9 0.2 collective-permute-done.9.rest_5_
  16.1 2.0 %collective-permute-done.8.rest_4_ = bf16[8,4,16,128]{3,2,1,0:T(8,128)(2,1)S(1)} collective-permute-done((bf16[8,4,16,128]{3,2,1,0:T(8,128)(2,1)S(1)}, bf16[8,4,16,128]{3,2,1,0:T(8,128)(2,1)S(1)}, u32[]{:S(2)}, u32[]{:S(2)}) %collective-permute-start.8) | collective-permute-done | bytes 131104 | tf_op jit(solution)/shard_map/ppermute | solution.py:546
  18.1 2.0 %collective-permute-start.11 = (bf16[8,4,16,128]{3,2,1,0:T(8,128)(2,1)S(1)}, bf16[8,4,16,128]{3,2,1,0:T(8,128)(2,1)S(1)}, u32[]{:S(2)}, u32[]{:S(2)}) collective-permute-start(bf16[8,4,16,128]{3,2,1,0:T(8,128)(2,1)S(1)} %collective-permute-done.9.rest_5_), channel_id=1, source_target_pairs={{0,4},{8,0},{16,8},{24,16},{28,24},{20,28},{12,20},{4,12},{1,5},{9... | collective-permute-start | bytes 393224 | tf_op jit(solution)/shard_map/ppermute | solution.py:549
  20.1 0.8 %collective-permute-done.4.refs_0_.rest_6_ = bf16[8,4,16,128]{3,2,1,0:T(8,128)(2,1)S(1)} collective-permute-done((bf16[8,4,16,128]{3,2,1,0:T(8,128)(2,1)S(1)}, bf16[8,4,16,128]{3,2,1,0:T(8,128)(2,1)S(1)}, u32[]{:S(2)}, u32[]{:S(2)}) %collective-permute-start.4) | collective-permute-done | bytes 131104 | tf_op jit(solution)/shard_map/ppermute | solution.py:546
  21.1 1.9 %collective-permute-done.10.refs_2_.rest_8_ = bf16[8,4,16,128]{3,2,1,0:T(8,128)(2,1)S(1)} collective-permute-done((bf16[8,4,16,128]{3,2,1,0:T(8,128)(2,1)S(1)}, bf16[8,4,16,128]{3,2,1,0:T(8,128)(2,1)S(1)}, u32[]{:S(2)}, u32[]{:S(2)}) %collective-permute-start.10) | collective-permute-done | bytes 131104 | tf_op jit(solution)/shard_map/ppermute | solution.py:546
  23.3 1.6 %collective-permute-start.17 = (bf16[16,4,16,128]{3,2,1,0:T(8,128)(2,1)S(1)}, bf16[16,4,16,128]{3,2,1,0:T(8,128)(2,1)S(1)}, u32[]{:S(2)}, u32[]{:S(2)}) collective-permute-start(bf16[16,4,16,128]{3,2,1,0:T(8,128)(2,1)S(1)} %get-tuple-element.61), channel_id=1, source_target_pairs={{0,8},{8,16},{16,24},{24,28},{28,20},{20,12},{12,4},{4,0},{1,9},{9... | collective-permute-start | bytes 786440 | tf_op jit(solution)/shard_map/ppermute | solution.py:546
  25.0 0.4 collective-permute-start.18
  25.6 3.2 %cross.3 = (bf16[256,128]{1,0:T(8,128)(2,1)S(1)}, bf16[256,128]{1,0:T(8,128)(2,1)S(1)}, bf16[256,128]{1,0:T(8,128)(2,1)S(1)}, bf16[256,128]{1,0:T(8,128)(2,1)S(1)}) custom-call(s32[4,8]{1,0:T(4,128)S(1)} %copy-done.2, bf16[512,2048]{1,0:T(8,128)(2,1)S(1)} %copy-done, f32[3,8,16,8,128]{4,3,2,1,0:T(8,128)S(1)} %widen.2.rest_0_, ...), custom_call_target="tpu_custom_call" | custom-call | flops 2990000128 | bytes 1024 | tf_op jit(solution)/shard_map/cross/pallas_call | solution.py:363
  28.8 1.7 %collective-permute-start.15 = (bf16[256,128]{1,0:T(8,128)(2,1)S(1)}, bf16[256,128]{1,0:T(8,128)(2,1)S(1)}, u32[]{:S(2)}, u32[]{:S(2)}) collective-permute-start(bf16[256,128]{1,0:T(8,128)(2,1)S(1)} %get-tuple-element.58), channel_id=1, source_target_pairs={{0,2},{1,3},{2,0},{3,1},{4,6},{5,7},{6,4},{7,5},{8,10},{9,11},{10,... | collective-permute-start | bytes 196616 | tf_op jit(solution)/shard_map/ppermute | solution.py:514
  30.7 1.5 %collective-permute-done.17.rest_10_ = bf16[16,4,16,128]{3,2,1,0:T(8,128)(2,1)S(1)} collective-permute-done((bf16[16,4,16,128]{3,2,1,0:T(8,128)(2,1)S(1)}, bf16[16,4,16,128]{3,2,1,0:T(8,128)(2,1)S(1)}, u32[]{:S(2)}, u32[]{:S(2)}) %collective-permute-start.17) | collective-permute-done | bytes 262176 | tf_op jit(solution)/shard_map/ppermute | solution.py:546
  32.2 1.4 %collective-permute-start.22 = (bf16[16,4,16,128]{3,2,1,0:T(8,128)(2,1)S(1)}, bf16[16,4,16,128]{3,2,1,0:T(8,128)(2,1)S(1)}, u32[]{:S(2)}, u32[]{:S(2)}) collective-permute-start(bf16[16,4,16,128]{3,2,1,0:T(8,128)(2,1)S(1)} %collective-permute-done.17.rest_10_), channel_id=1, source_target_pairs={{0,8},{8,16},{16,24},{24,28},{28,20},{20,12},{12,4},{4,0},{1,9},{9... | collective-permute-start | bytes 786440 | tf_op jit(solution)/shard_map/ppermute | solution.py:546
  33.6 5.5 %cross.4 = (bf16[512,128]{1,0:T(8,128)(2,1)S(1)}, bf16[512,128]{1,0:T(8,128)(2,1)S(1)}, bf16[512,128]{1,0:T(8,128)(2,1)S(1)}, bf16[512,128]{1,0:T(8,128)(2,1)S(1)}) custom-call(s32[4,8]{1,0:T(4,128)S(1)} %copy-done.2, bf16[512,2048]{1,0:T(8,128)(2,1)S(1)} %copy-done, f32[3,8,16,8,128]{4,3,2,1,0:T(8,128)S(1)} %widen.2.rest_0_, ...), custom_call_target="tpu_custom_call" | custom-call | flops 5289999872 | bytes 1024 | tf_op jit(solution)/shard_map/cross/pallas_call | solution.py:363
  39.2 1.8 %collective-permute-start.20 = (bf16[512,128]{1,0:T(8,128)(2,1)S(1)}, bf16[512,128]{1,0:T(8,128)(2,1)S(1)}, u32[]{:S(2)}, u32[]{:S(2)}) collective-permute-start(bf16[512,128]{1,0:T(8,128)(2,1)S(1)} %get-tuple-element.65), channel_id=1, source_target_pairs={{0,2},{1,3},{2,0},{3,1},{4,6},{5,7},{6,4},{7,5},{8,10},{9,11},{10,... | collective-permute-start | bytes 393224 | tf_op jit(solution)/shard_map/ppermute | solution.py:514
  41.1 3.2 %cross.5 = (bf16[256,128]{1,0:T(8,128)(2,1)S(1)}, bf16[256,128]{1,0:T(8,128)(2,1)S(1)}, bf16[256,128]{1,0:T(8,128)(2,1)S(1)}, bf16[256,128]{1,0:T(8,128)(2,1)S(1)}) custom-call(s32[4,8]{1,0:T(4,128)S(1)} %copy-done.2, bf16[512,2048]{1,0:T(8,128)(2,1)S(1)} %copy-done, f32[3,8,16,8,128]{4,3,2,1,0:T(8,128)S(1)} %widen.2.rest_0_, ...), custom_call_target="tpu_custom_call" | custom-call | flops 2990000128 | bytes 1024 | tf_op jit(solution)/shard_map/cross/pallas_call | solution.py:363
  44.4 0.4 collective-permute-start.23
  44.8 1.7 %collective-permute-start.24 = (bf16[256,128]{1,0:T(8,128)(2,1)S(1)}, bf16[256,128]{1,0:T(8,128)(2,1)S(1)}, u32[]{:S(2)}, u32[]{:S(2)}) collective-permute-start(bf16[256,128]{1,0:T(8,128)(2,1)S(1)} %get-tuple-element.71), channel_id=1, source_target_pairs={{0,2},{1,3},{2,0},{3,1},{4,6},{5,7},{6,4},{7,5},{8,10},{9,11},{10,... | collective-permute-start | bytes 196616 | tf_op jit(solution)/shard_map/ppermute | solution.py:514
  46.5 1.1 %collective-permute-done.21.rest_7_ = bf16[512,128]{1,0:T(8,128)(2,1)S(1)} collective-permute-done((bf16[512,128]{1,0:T(8,128)(2,1)S(1)}, bf16[512,128]{1,0:T(8,128)(2,1)S(1)}, u32[]{:S(2)}, u32[]{:S(2)}) %collective-permute-start.21) | collective-permute-done | bytes 131104 | tf_op jit(solution)/shard_map/ppermute | solution.py:514
  47.6 0.6 %early.1 = f32[3,2,256,256]{3,2,1,0:T(8,128)S(1)} custom-call(bf16[4,128,512]{2,1,0:T(8,128)(2,1)S(1)} %copy-done.1, bf16[256,128]{1,0:T(8,128)(2,1)S(1)} %get-tuple-element.56.rest_0_, bf16[256,128]{1,0:T(8,128)(2,1)S(1)} %collective-permute-done.14.rest_1_, bf16[256,128]{1,0:T(8,128)(2,1)S(1)} %collective-permute-done.15.rest_2_, ...), custom_call_target="tpu_custom_call" | custom-call | flops 57500000 | bytes 1024 | tf_op jit(solution)/shard_map/early/pallas_call | solution.py:464
  48.2 1.2 %collective-permute-done.24.rest_2_ = bf16[256,128]{1,0:T(8,128)(2,1)S(1)} collective-permute-done((bf16[256,128]{1,0:T(8,128)(2,1)S(1)}, bf16[256,128]{1,0:T(8,128)(2,1)S(1)}, u32[]{:S(2)}, u32[]{:S(2)}) %collective-permute-start.24) | collective-permute-done | bytes 65568 | tf_op jit(solution)/shard_map/ppermute | solution.py:514
  49.4 1.4 %collective-permute-done.25.rest_3_ = bf16[256,128]{1,0:T(8,128)(2,1)S(1)} collective-permute-done((bf16[256,128]{1,0:T(8,128)(2,1)S(1)}, bf16[256,128]{1,0:T(8,128)(2,1)S(1)}, u32[]{:S(2)}, u32[]{:S(2)}) %collective-permute-start.25) | collective-permute-done | bytes 65568 | tf_op jit(solution)/shard_map/ppermute | solution.py:514
  50.8 2.2 %late.1 = f32[4096,128]{1,0:T(8,128)} custom-call(s32[4,8]{1,0:T(4,128)S(1)} %copy-done.2, bf16[4,128,512]{2,1,0:T(8,128)(2,1)S(1)} %copy-done.1, f32[3,2,256,256]{3,2,1,0:T(8,128)S(1)} %early.1, bf16[256,128]{1,0:T(8,128)(2,1)S(1)} %get-tuple-element.69.rest_0_, bf16[256,128]{1,0:T(8,128)(2,1)S(1)} %collective-permute-done.23.rest_1_, ...), custom_call_target="tpu_custom_call" | custom-call | flops 57500000 | bytes 1024 | tf_op jit(solution)/shard_map/late/pallas_call | solution.py:474
  (38 shorter events, 1.5 us)
Async XLA Ops:
  3.0 3.3 %collective-permute-start = (bf16[4,4,16,128]{3,2,1,0:T(8,128)(2,1)S(1)}, bf16[4,4,16,128]{3,2,1,0:T(8,128)(2,1)S(1)}, u32[]{:S(2)}, u32[]{:S(2)}) collective-permute-start(bf16[4,4,16,128]{3,2,1,0:T(8,128)(2,1)S(1)} %get-tuple-element.40), channel_id=1, source_target_pairs={{0,1},{1,0},{2,3},{3,2},{4,5},{5,4},{6,7},{7,6},{8,9},{9,8},{10,11... | collective-permute-start | bytes 196616 | tf_op jit(solution)/shard_map/ppermute | solution.py:514
  3.6 5.3 %collective-permute-start.6 = (bf16[4,4,16,128]{3,2,1,0:T(8,128)(2,1)S(1)}, bf16[4,4,16,128]{3,2,1,0:T(8,128)(2,1)S(1)}, u32[]{:S(2)}, u32[]{:S(2)}) collective-permute-start(bf16[4,4,16,128]{3,2,1,0:T(8,128)(2,1)S(1)} %get-tuple-element.45), channel_id=1, source_target_pairs={{0,2},{1,3},{2,0},{3,1},{4,6},{5,7},{6,4},{7,5},{8,10},{9,11},{10,... | collective-permute-start | bytes 196616 | tf_op jit(solution)/shard_map/ppermute | solution.py:514
  6.1 4.0 %collective-permute-start.7 = (bf16[4,4,16,128]{3,2,1,0:T(8,128)(2,1)S(1)}, bf16[4,4,16,128]{3,2,1,0:T(8,128)(2,1)S(1)}, u32[]{:S(2)}, u32[]{:S(2)}) collective-permute-start(bf16[4,4,16,128]{3,2,1,0:T(8,128)(2,1)S(1)} %get-tuple-element.46), channel_id=1, source_target_pairs={{0,3},{1,2},{2,1},{3,0},{4,7},{5,6},{6,5},{7,4},{8,11},{9,10},{10,... | collective-permute-start | bytes 196616 | tf_op jit(solution)/shard_map/ppermute | solution.py:514
  6.2 4.0 %collective-permute-start.3 = (bf16[4,16,16,128]{3,2,1,0:T(8,128)(2,1)S(1)}, bf16[4,16,16,128]{3,2,1,0:T(8,128)(2,1)S(1)}, u32[]{:S(2)}, u32[]{:S(2)}) collective-permute-start(bf16[4,16,16,128]{3,2,1,0:T(8,128)(2,1)S(1)} %get-tuple-element.54.refs_0_), channel_id=1, source_target_pairs={{0,1},{1,0},{2,3},{3,2},{4,5},{5,4},{6,7},{7,6},{8,9},{9,8},{10,11... | collective-permute-start | bytes 786440 | tf_op jit(solution)/shard_map/ppermute | solution.py:514
  6.4 7.4 %collective-permute-start.2 = (bf16[8,4,16,128]{3,2,1,0:T(8,128)(2,1)S(1)}, bf16[8,4,16,128]{3,2,1,0:T(8,128)(2,1)S(1)}, u32[]{:S(2)}, u32[]{:S(2)}) collective-permute-start(bf16[8,4,16,128]{3,2,1,0:T(8,128)(2,1)S(1)} %constant_dynamic-update-slice_fusion), channel_id=1, source_target_pairs={{0,4},{8,0},{16,8},{24,16},{28,24},{20,28},{12,20},{4,12},{1,5},{9... | collective-permute-start | bytes 393224 | tf_op jit(solution)/shard_map/ppermute | solution.py:549
  8.4 5.4 %collective-permute-start.1 = (bf16[8,4,16,128]{3,2,1,0:T(8,128)(2,1)S(1)}, bf16[8,4,16,128]{3,2,1,0:T(8,128)(2,1)S(1)}, u32[]{:S(2)}, u32[]{:S(2)}) collective-permute-start(bf16[8,4,16,128]{3,2,1,0:T(8,128)(2,1)S(1)} %constant_dynamic-update-slice_fusion), channel_id=1, source_target_pairs={{0,8},{8,16},{16,24},{24,28},{28,20},{20,12},{12,4},{4,0},{1,9},{9... | collective-permute-start | bytes 393224 | tf_op jit(solution)/shard_map/ppermute | solution.py:546
  10.2 5.9 %collective-permute-start.9 = (bf16[8,4,16,128]{3,2,1,0:T(8,128)(2,1)S(1)}, bf16[8,4,16,128]{3,2,1,0:T(8,128)(2,1)S(1)}, u32[]{:S(2)}, u32[]{:S(2)}) collective-permute-start(bf16[8,4,16,128]{3,2,1,0:T(8,128)(2,1)S(1)} %pad_maximum_fusion), channel_id=1, source_target_pairs={{0,4},{8,0},{16,8},{24,16},{28,24},{20,28},{12,20},{4,12},{1,5},{9... | collective-permute-start | bytes 393224 | tf_op jit(solution)/shard_map/ppermute | solution.py:549
  11.8 6.3 %collective-permute-start.8 = (bf16[8,4,16,128]{3,2,1,0:T(8,128)(2,1)S(1)}, bf16[8,4,16,128]{3,2,1,0:T(8,128)(2,1)S(1)}, u32[]{:S(2)}, u32[]{:S(2)}) collective-permute-start(bf16[8,4,16,128]{3,2,1,0:T(8,128)(2,1)S(1)} %pad_maximum_fusion), channel_id=1, source_target_pairs={{0,8},{8,16},{16,24},{24,28},{28,20},{20,12},{12,4},{4,0},{1,9},{9... | collective-permute-start | bytes 393224 | tf_op jit(solution)/shard_map/ppermute | solution.py:546
  12.3 11.0 %collective-permute-start.12 = (bf16[4,16,16,128]{3,2,1,0:T(8,128)(2,1)S(1)}, bf16[4,16,16,128]{3,2,1,0:T(8,128)(2,1)S(1)}, u32[]{:S(2)}, u32[]{:S(2)}) collective-permute-start(bf16[4,16,16,128]{3,2,1,0:T(8,128)(2,1)S(1)} %get-tuple-element.54.refs_0_), channel_id=1, source_target_pairs={{0,2},{1,3},{2,0},{3,1},{4,6},{5,7},{6,4},{7,5},{8,10},{9,11},{10,... | collective-permute-start | bytes 786440 | tf_op jit(solution)/shard_map/ppermute | solution.py:514
  13.8 11.8 %copy-start = (bf16[512,2048]{1,0:T(8,128)(2,1)S(1)}, bf16[512,2048]{1,0:T(8,128)(2,1)}, u32[]{:S(2)}) copy-start(bf16[512,2048]{1,0:T(8,128)(2,1)} %constant.4.clone.table_hbm.table) | copy-start | bytes 6291460
  13.8 11.8 %copy-start.2 = (s32[4,8]{1,0:T(4,128)S(1)}, s32[4,8]{1,0:T(4,128)}, u32[]{:S(2)}) copy-start(s32[4,8]{1,0:T(4,128)} %plan.7) | copy-start | bytes 388
  13.8 7.1 %collective-permute-start.4 = (bf16[8,4,16,128]{3,2,1,0:T(8,128)(2,1)S(1)}, bf16[8,4,16,128]{3,2,1,0:T(8,128)(2,1)S(1)}, u32[]{:S(2)}, u32[]{:S(2)}) collective-permute-start(bf16[8,4,16,128]{3,2,1,0:T(8,128)(2,1)S(1)} %collective-permute-done.1.rest_2_), channel_id=1, source_target_pairs={{0,8},{8,16},{16,24},{24,28},{28,20},{20,12},{12,4},{4,0},{1,9},{9... | collective-permute-start | bytes 393224 | tf_op jit(solution)/shard_map/ppermute | solution.py:546
  15.4 5.7 %collective-permute-start.5 = (bf16[8,4,16,128]{3,2,1,0:T(8,128)(2,1)S(1)}, bf16[8,4,16,128]{3,2,1,0:T(8,128)(2,1)S(1)}, u32[]{:S(2)}, u32[]{:S(2)}) collective-permute-start(bf16[8,4,16,128]{3,2,1,0:T(8,128)(2,1)S(1)} %collective-permute-done.2.rest_3_), channel_id=1, source_target_pairs={{0,4},{8,0},{16,8},{24,16},{28,24},{20,28},{12,20},{4,12},{1,5},{9... | collective-permute-start | bytes 393224 | tf_op jit(solution)/shard_map/ppermute | solution.py:549
  18.1 5.0 %collective-permute-start.10 = (bf16[8,4,16,128]{3,2,1,0:T(8,128)(2,1)S(1)}, bf16[8,4,16,128]{3,2,1,0:T(8,128)(2,1)S(1)}, u32[]{:S(2)}, u32[]{:S(2)}) collective-permute-start(bf16[8,4,16,128]{3,2,1,0:T(8,128)(2,1)S(1)} %collective-permute-done.8.rest_4_), channel_id=1, source_target_pairs={{0,8},{8,16},{16,24},{24,28},{28,20},{20,12},{12,4},{4,0},{1,9},{9... | collective-permute-start | bytes 393224 | tf_op jit(solution)/shard_map/ppermute | solution.py:546
  18.1 5.1 %collective-permute-start.11 = (bf16[8,4,16,128]{3,2,1,0:T(8,128)(2,1)S(1)}, bf16[8,4,16,128]{3,2,1,0:T(8,128)(2,1)S(1)}, u32[]{:S(2)}, u32[]{:S(2)}) collective-permute-start(bf16[8,4,16,128]{3,2,1,0:T(8,128)(2,1)S(1)} %collective-permute-done.9.rest_5_), channel_id=1, source_target_pairs={{0,4},{8,0},{16,8},{24,16},{28,24},{20,28},{12,20},{4,12},{1,5},{9... | collective-permute-start | bytes 393224 | tf_op jit(solution)/shard_map/ppermute | solution.py:549
  23.3 2.2 %collective-permute-start.13 = (bf16[4,16,16,128]{3,2,1,0:T(8,128)(2,1)S(1)}, bf16[4,16,16,128]{3,2,1,0:T(8,128)(2,1)S(1)}, u32[]{:S(2)}, u32[]{:S(2)}) collective-permute-start(bf16[4,16,16,128]{3,2,1,0:T(8,128)(2,1)S(1)} %collective-permute-done.12.refs_0_), channel_id=1, source_target_pairs={{0,1},{1,0},{2,3},{3,2},{4,5},{5,4},{6,7},{7,6},{8,9},{9,8},{10,11... | collective-permute-start | bytes 786440 | tf_op jit(solution)/shard_map/ppermute | solution.py:514
  23.3 8.9 %collective-permute-start.17 = (bf16[16,4,16,128]{3,2,1,0:T(8,128)(2,1)S(1)}, bf16[16,4,16,128]{3,2,1,0:T(8,128)(2,1)S(1)}, u32[]{:S(2)}, u32[]{:S(2)}) collective-permute-start(bf16[16,4,16,128]{3,2,1,0:T(8,128)(2,1)S(1)} %get-tuple-element.61), channel_id=1, source_target_pairs={{0,8},{8,16},{16,24},{24,28},{28,20},{20,12},{12,4},{4,0},{1,9},{9... | collective-permute-start | bytes 786440 | tf_op jit(solution)/shard_map/ppermute | solution.py:546
  25.0 8.7 %collective-permute-start.18 = (bf16[16,4,16,128]{3,2,1,0:T(8,128)(2,1)S(1)}, bf16[16,4,16,128]{3,2,1,0:T(8,128)(2,1)S(1)}, u32[]{:S(2)}, u32[]{:S(2)}) collective-permute-start(bf16[16,4,16,128]{3,2,1,0:T(8,128)(2,1)S(1)} %get-tuple-element.62), channel_id=1, source_target_pairs={{0,4},{8,0},{16,8},{24,16},{28,24},{20,28},{12,20},{4,12},{1,5},{9... | collective-permute-start | bytes 786440 | tf_op jit(solution)/shard_map/ppermute | solution.py:549
  28.7 10.5 %collective-permute-start.14 = (bf16[256,128]{1,0:T(8,128)(2,1)S(1)}, bf16[256,128]{1,0:T(8,128)(2,1)S(1)}, u32[]{:S(2)}, u32[]{:S(2)}) collective-permute-start(bf16[256,128]{1,0:T(8,128)(2,1)S(1)} %get-tuple-element.57), channel_id=1, source_target_pairs={{0,1},{1,0},{2,3},{3,2},{4,5},{5,4},{6,7},{7,6},{8,9},{9,8},{10,11... | collective-permute-start | bytes 196616 | tf_op jit(solution)/shard_map/ppermute | solution.py:514
  28.8 12.2 %collective-permute-start.15 = (bf16[256,128]{1,0:T(8,128)(2,1)S(1)}, bf16[256,128]{1,0:T(8,128)(2,1)S(1)}, u32[]{:S(2)}, u32[]{:S(2)}) collective-permute-start(bf16[256,128]{1,0:T(8,128)(2,1)S(1)} %get-tuple-element.58), channel_id=1, source_target_pairs={{0,2},{1,3},{2,0},{3,1},{4,6},{5,7},{6,4},{7,5},{8,10},{9,11},{10,... | collective-permute-start | bytes 196616 | tf_op jit(solution)/shard_map/ppermute | solution.py:514
  30.6 10.5 %collective-permute-start.16 = (bf16[256,128]{1,0:T(8,128)(2,1)S(1)}, bf16[256,128]{1,0:T(8,128)(2,1)S(1)}, u32[]{:S(2)}, u32[]{:S(2)}) collective-permute-start(bf16[256,128]{1,0:T(8,128)(2,1)S(1)} %get-tuple-element.59), channel_id=1, source_target_pairs={{0,3},{1,2},{2,1},{3,0},{4,7},{5,6},{6,5},{7,4},{8,11},{9,10},{10,... | collective-permute-start | bytes 196616 | tf_op jit(solution)/shard_map/ppermute | solution.py:514
  32.2 8.9 %collective-permute-start.22 = (bf16[16,4,16,128]{3,2,1,0:T(8,128)(2,1)S(1)}, bf16[16,4,16,128]{3,2,1,0:T(8,128)(2,1)S(1)}, u32[]{:S(2)}, u32[]{:S(2)}) collective-permute-start(bf16[16,4,16,128]{3,2,1,0:T(8,128)(2,1)S(1)} %collective-permute-done.17.rest_10_), channel_id=1, source_target_pairs={{0,8},{8,16},{16,24},{24,28},{28,20},{20,12},{12,4},{4,0},{1,9},{9... | collective-permute-start | bytes 786440 | tf_op jit(solution)/shard_map/ppermute | solution.py:546
  39.2 7.3 %collective-permute-start.19 = (bf16[512,128]{1,0:T(8,128)(2,1)S(1)}, bf16[512,128]{1,0:T(8,128)(2,1)S(1)}, u32[]{:S(2)}, u32[]{:S(2)}) collective-permute-start(bf16[512,128]{1,0:T(8,128)(2,1)S(1)} %get-tuple-element.64), channel_id=1, source_target_pairs={{0,1},{1,0},{2,3},{3,2},{4,5},{5,4},{6,7},{7,6},{8,9},{9,8},{10,11... | collective-permute-start | bytes 393224 | tf_op jit(solution)/shard_map/ppermute | solution.py:514
  39.2 7.2 %collective-permute-start.20 = (bf16[512,128]{1,0:T(8,128)(2,1)S(1)}, bf16[512,128]{1,0:T(8,128)(2,1)S(1)}, u32[]{:S(2)}, u32[]{:S(2)}) collective-permute-start(bf16[512,128]{1,0:T(8,128)(2,1)S(1)} %get-tuple-element.65), channel_id=1, source_target_pairs={{0,2},{1,3},{2,0},{3,1},{4,6},{5,7},{6,4},{7,5},{8,10},{9,11},{10,... | collective-permute-start | bytes 393224 | tf_op jit(solution)/shard_map/ppermute | solution.py:514
  41.0 6.5 %collective-permute-start.21 = (bf16[512,128]{1,0:T(8,128)(2,1)S(1)}, bf16[512,128]{1,0:T(8,128)(2,1)S(1)}, u32[]{:S(2)}, u32[]{:S(2)}) collective-permute-start(bf16[512,128]{1,0:T(8,128)(2,1)S(1)} %get-tuple-element.66), channel_id=1, source_target_pairs={{0,3},{1,2},{2,1},{3,0},{4,7},{5,6},{6,5},{7,4},{8,11},{9,10},{10,... | collective-permute-start | bytes 393224 | tf_op jit(solution)/shard_map/ppermute | solution.py:514
  41.1 6.4 %copy-start.1 = (bf16[4,128,512]{2,1,0:T(8,128)(2,1)S(1)}, bf16[4,128,512]{2,1,0:T(8,128)(2,1)}, u32[]{:S(2)}) copy-start(bf16[4,128,512]{2,1,0:T(8,128)(2,1)} %constant.5.clone.place) | copy-start | bytes 1572868
  44.4 3.8 %collective-permute-start.23 = (bf16[256,128]{1,0:T(8,128)(2,1)S(1)}, bf16[256,128]{1,0:T(8,128)(2,1)S(1)}, u32[]{:S(2)}, u32[]{:S(2)}) collective-permute-start(bf16[256,128]{1,0:T(8,128)(2,1)S(1)} %get-tuple-element.70), channel_id=1, source_target_pairs={{0,1},{1,0},{2,3},{3,2},{4,5},{5,4},{6,7},{7,6},{8,9},{9,8},{10,11... | collective-permute-start | bytes 196616 | tf_op jit(solution)/shard_map/ppermute | solution.py:514
  44.8 4.6 %collective-permute-start.24 = (bf16[256,128]{1,0:T(8,128)(2,1)S(1)}, bf16[256,128]{1,0:T(8,128)(2,1)S(1)}, u32[]{:S(2)}, u32[]{:S(2)}) collective-permute-start(bf16[256,128]{1,0:T(8,128)(2,1)S(1)} %get-tuple-element.71), channel_id=1, source_target_pairs={{0,2},{1,3},{2,0},{3,1},{4,6},{5,7},{6,4},{7,5},{8,10},{9,11},{10,... | collective-permute-start | bytes 196616 | tf_op jit(solution)/shard_map/ppermute | solution.py:514
  46.5 4.3 %collective-permute-start.25 = (bf16[256,128]{1,0:T(8,128)(2,1)S(1)}, bf16[256,128]{1,0:T(8,128)(2,1)S(1)}, u32[]{:S(2)}, u32[]{:S(2)}) collective-permute-start(bf16[256,128]{1,0:T(8,128)(2,1)S(1)} %get-tuple-element.72), channel_id=1, source_target_pairs={{0,3},{1,2},{2,1},{3,0},{4,7},{5,6},{6,5},{7,4},{8,11},{9,10},{10,... | collective-permute-start | bytes 196616 | tf_op jit(solution)/shard_map/ppermute | solution.py:514

commit v10 on v8

--- a/solution.py
+++ b/solution.py
@@ -17,6 +17,7 @@
 LANES = 128
 TILES = NBIN // LANES
 CHUNKS = 4
+GROUP = 4
 BF = jnp.bfloat16
 F32 = jnp.float32
 
@@ -213,9 +214,12 @@
         def widen(w, carry, j=j, block=block):
             raw = block[w].astype(F32)
             real, imag = raw[:, :TILES], raw[:, TILES:]
-            own[0, j * windows + w] = real + imag
-            own[1, j * windows + w] = real
-            own[2, j * windows + w] = imag
+            both = real + imag
+            for group in range(own.shape[0]):
+                at = slice(group * GROUP, (group + 1) * GROUP)
+                own[group, 0, j * windows + w] = both[at]
+                own[group, 1, j * windows + w] = real[at]
+                own[group, 2, j * windows + w] = imag[at]
             return carry
 
         lax.fori_loop(0, windows, widen, 0)
@@ -226,7 +230,9 @@
     vmem = pl.BlockSpec(memory_space=pltpu.VMEM)
     return pl.pallas_call(
         widen_kernel,
-        out_shape=jax.ShapeDtypeStruct((3, len(blocks) * windows, stations, TILES, LANES), F32),
+        out_shape=jax.ShapeDtypeStruct(
+            (stations // GROUP, 3, len(blocks) * windows, GROUP, TILES, LANES), F32
+        ),
         in_specs=[vmem] * len(blocks),
         out_specs=vmem,
         compiler_params=pltpu.CompilerParams(vmem_limit_bytes=16 * 2**20),
@@ -257,20 +263,19 @@
 
 
 def sum_windows(owns, other, crossed):
-    windows, stations = owns[0].shape[1:3]
+    groups, _, windows, group = owns[0].shape[:4]
     slots, _, quarter = other.shape[1:4]
-    width = stations * quarter
-    group = 4
-    groups = stations // group
+    width = groups * group * quarter
 
     def one_group(slot, index):
         first = index * group
+        mine = [own.at[index] for own in owns]
 
         def sums(kind):
             totals = [None] * (group * quarter)
-            for part, own in enumerate(owns):
+            for part, own in enumerate(mine):
                 for w in range(windows):
-                    left = [own[kind, w, first + s] for s in range(group)]
+                    left = [own[kind, w, s] for s in range(group)]
                     right = [other[kind, slot, part * windows + w, t] for t in range(quarter)]
                     for s in range(group):
                         for t in range(quarter):
@@ -307,7 +312,7 @@
     others, rest = rest[: len(places)], rest[len(places) :]
     outs = rest[:parts]
     other, crossed, operand, result = rest[parts:]
-    stations = owns[0].shape[2]
+    stations = owns[0].shape[0] * owns[0].shape[3]
     widen_others(first_slot, slots, count, places, plan, others, other)
     sum_windows(owns, other, crossed)
     width = stations * other.shape[3]
@@ -355,7 +360,7 @@
 
 
 def cross_lags(plan, table, owns, places, candidates, first_slot, slots, count, parts, scaling):
-    windows, stations = owns[0].shape[1:3]
+    windows, stations = owns[0].shape[2], owns[0].shape[0] * owns[0].shape[3]
     quarter = candidates[0].shape[1]
     columns = slots * stations * quarter
     share = LAGS // parts
@@ -407,40 +412,34 @@
     return jnp.concatenate([place[me ^ j] for j in range(parts)], axis=0)
 
 
-def early_kernel(parts, groups, place, *rest):
-    pieces, out = rest[:-1], rest[-1]
-    half, pairs = out.shape[2:]
+def store_rows(rows, block, first):
+    tiles = block.shape[1] // LANES
+    for tile in range(tiles):
+        at = pl.ds(first * tiles + tile, block.shape[0], stride=tiles)
+        rows[at, :] = block[:, tile * LANES : (tile + 1) * LANES]
+
+
+def early_kernel(count, parts, groups, half, plan, place, *rest):
+    pieces = rest[:-3]
+    out_hbm, rows, sems = rest[-3:]
+    pairs = place.shape[2] // 2
+    rounds = slot_rounds(plan, count)
     matrix = joined_matrix(place, parts)
     at = slice(0, half)
+    copies = []
     for index, (first_slot, slots) in enumerate(groups):
         block = placed_block(pieces[index * parts : (index + 1) * parts], matrix, at, half)
-        if slots == 1:
-            out[first_slot, 0] = block[:, :pairs]
-            out[first_slot, 1] = block[:, pairs:]
-        else:
-            for slot in range(2):
+        for slot in range(slots):
+            if slots == 1:
+                low, high = block[:, :pairs], block[:, pairs:]
+            else:
                 columns = slice(slot * pairs, (slot + 1) * pairs)
-                out[first_slot + slot, 0] = block[:half, columns]
-                out[first_slot + slot, 1] = block[half:, columns]
-
-
-def late_kernel(count, parts, steps, plan, place, early, *rest):
-    pieces = rest[:parts]
-    out_hbm, out, sems = rest[parts:]
-    half, _, pairs = out.shape[1:]
-    rows = half // steps
-    rounds = slot_rounds(plan, count)
-    matrix = joined_matrix(place, parts)
-    block = placed_block(pieces, matrix, slice(0, half), half)
-    copies = []
-    for step in range(steps):
-        at = slice(step * rows, (step + 1) * rows)
-        for h in range(2):
-            for slot in range(ROUNDS - 1):
-                out[h, at, rounds[slot], :] = early[slot, h, at, :]
-            out[h, at, rounds[ROUNDS - 1], :] = block[at, h * pairs : (h + 1) * pairs]
+                low, high = block[:half, columns], block[half:, columns]
+            number = first_slot + slot
+            store_rows(rows.at[number], low, 0)
+            store_rows(rows.at[number], high, half)
             copy = pltpu.make_async_copy(
-                out.at[h, at], out_hbm.at[h, at], sems.at[2 * step + h]
+                rows.at[number], out_hbm.at[:, rounds[number], 0], sems.at[number]
             )
             copy.start()
             copies.append(copy)
@@ -448,34 +447,55 @@
         copy.wait()
 
 
+def late_kernel(count, parts, half, plan, place, early, *rest):
+    pieces = rest[:parts]
+    out_hbm, rows, sem = rest[parts:]
+    pairs = place.shape[2] // 2
+    number = slot_rounds(plan, count)[ROUNDS - 1]
+    block = placed_block(pieces, joined_matrix(place, parts), slice(0, half), half)
+    store_rows(rows, block[:, :pairs], 0)
+    store_rows(rows, block[:, pairs:], half)
+    copy = pltpu.make_async_copy(rows, out_hbm.at[:, number, 0], sem)
+    copy.start()
+    copy.wait()
+
+
 def place_lags(plan, groups, pieces, count, stations, parts):
     pairs = stations * stations
     share = LAGS // parts
     half = share // 2
-    steps = 4
+    tiles = pairs // LANES
     place = jnp.asarray(make_placing(stations, stations // parts, parts))
+    smem = pl.BlockSpec(memory_space=pltpu.SMEM)
     vmem = pl.BlockSpec(memory_space=pltpu.VMEM)
+    anywhere = pl.BlockSpec(memory_space=pl.ANY)
+    shape = jax.ShapeDtypeStruct((share * tiles, ROUNDS, 1, LANES), F32)
     early = pl.pallas_call(
-        functools.partial(early_kernel, parts, tuple(groups[:-1])),
-        out_shape=jax.ShapeDtypeStruct((ROUNDS - 1, 2, half, pairs), F32),
-        in_specs=[vmem] * (1 + len(pieces) - parts),
-        out_specs=vmem,
+        functools.partial(early_kernel, count, parts, tuple(groups[:-1]), half),
+        out_shape=shape,
+        in_specs=[smem] + [vmem] * (1 + len(pieces) - parts),
+        out_specs=anywhere,
+        scratch_shapes=[
+            pltpu.VMEM((ROUNDS - 1, share * tiles, LANES), F32),
+            pltpu.SemaphoreType.DMA((ROUNDS - 1,)),
+        ],
         compiler_params=pltpu.CompilerParams(vmem_limit_bytes=16 * 2**20),
         cost_estimate=expected(0.05),
         name="early",
-    )(place, *pieces[:-parts])
-    shape = (2, half, ROUNDS, pairs)
+    )(plan, place, *pieces[:-parts])
     out = pl.pallas_call(
-        functools.partial(late_kernel, count, parts, steps),
-        out_shape=jax.ShapeDtypeStruct(shape, F32),
-        in_specs=[pl.BlockSpec(memory_space=pltpu.SMEM)] + [vmem] * (2 + parts),
-        out_specs=pl.BlockSpec(memory_space=pl.ANY),
-        scratch_shapes=[pltpu.VMEM(shape, F32), pltpu.SemaphoreType.DMA((2 * steps,))],
-        compiler_params=pltpu.CompilerParams(vmem_limit_bytes=24 * 2**20),
+        functools.partial(late_kernel, count, parts, half),
+        out_shape=shape,
+        in_specs=[smem, vmem, anywhere] + [vmem] * parts,
+        out_specs=anywhere,
+        scratch_shapes=[pltpu.VMEM((share * tiles, LANES), F32), pltpu.SemaphoreType.DMA],
+        input_output_aliases={2: 0},
+        compiler_params=pltpu.CompilerParams(vmem_limit_bytes=16 * 2**20),
         cost_estimate=expected(0.05),
         name="late",
     )(plan, place, early, *pieces[-parts:])
-    return out.reshape(share, ROUNDS, pairs)
+    out = out.reshape(share, tiles, ROUNDS, LANES)
+    return out.transpose(0, 2, 1, 3).reshape(share, ROUNDS, pairs)
 
 
 def join_kernel(order, *refs):

time: 52.2 us -> 51.7 us (level)
  waiting for transfers between devices: 12.7 us -> 11.2 us
  Pallas kernels: 16.5 us -> 17.5 us
    ppermute x15, waiting for transfers between devices: 5.56 us -> 3.98 us  [swap(): return lax.ppermute(value, 'seg', [(i, i ^ j) for i in range(parts)])]
    pallas_call x4, Pallas kernels: 3.06 us -> 4.05 us  [the longest x1 2.14 us: place_lags(): pl.pallas_call(functools.partial(early_kernel, count, parts, tuple(groups...]
  transfers between devices with their start and end apart: 26 -> 26, of which waited for: 12 -> 11; matrix products, arithmetic and copies ran while one was open for 0% -> 0% of each run, Pallas kernels for 22% -> 25%
where the time goes in v10:
time: 51.7 us; the launch traced here: 51.5 us
  starting transfers between devices  22.6 us (44%)
  Pallas kernels  17.5 us (34%)
  waiting for transfers between devices  11.2 us (22%)
    ppermute x15, starting transfers between devices, swap(): return lax.ppermute(value, 'seg', [(i, i ^ j) for i in range(parts)])  10.8 us
    pallas_call x3, Pallas kernels, cross_lags(): pl.pallas_call(functools.partial(cross_kernel, first_slot, slots, count,...  10.4 us
    ppermute x6, waiting for transfers between devices, up(): return lax.ppermute(value, 'sta', upward)  6.63 us
    ppermute x5, starting transfers between devices, down(): return lax.ppermute(value, 'sta', downward)  6.5 us
    ppermute x6, starting transfers between devices, up(): return lax.ppermute(value, 'sta', upward)  5.29 us
    ppermute x15, waiting for transfers between devices, swap(): return lax.ppermute(value, 'seg', [(i, i ^ j) for i in range(parts)])  3.98 us
    pallas_call x1, Pallas kernels, prepare(): pl.pallas_call(functools.partial(prep_kernel, parts), out_shape=[jax.Shap...  3.04 us
    pallas_call x1, Pallas kernels, place_lags(): pl.pallas_call(functools.partial(early_kernel, count, parts, tuple(groups...  2.14 us
  transfers between devices with their start and end apart: 26, of which 11 were waited for; matrix products, arithmetic and copies ran while one was open for 0% of the time, Pallas kernels for 25%

profile of v10, /device:TPU:0, one launch (start us, length us, event | category | flops | bytes accessed | tf_op | source)
XLA Modules:
  0.0 51.5 jit_solution(6382736424232883570)
XLA Ops:
  0.0 3.0 %prep.1 = (bf16[4,16,16,128]{3,2,1,0:T(8,128)(2,1)S(1)}, bf16[4,4,16,128]{3,2,1,0:T(8,128)(2,1)S(1)}, bf16[4,4,16,128]{3,2,1,0:T(8,128)(2,1)S(1)}, bf16[4,4,16,1...) custom-call(f32[16,4,2048]{2,1,0:T(4,128)} %records_hbm.1, bf16[512,2048]{1,0:T(8,128)(2,1)} %constant.4.clone.table_hbm.table), custom_call_target="tpu_custom_call" | custom-call | flops 536870912 | bytes 3145728 | tf_op jit(solution)/shard_map/prep/pallas_call | solution.py:154
  3.0 0.5 %collective-permute-start = (bf16[4,4,16,128]{3,2,1,0:T(8,128)(2,1)S(1)}, bf16[4,4,16,128]{3,2,1,0:T(8,128)(2,1)S(1)}, u32[]{:S(2)}, u32[]{:S(2)}) collective-permute-start(bf16[4,4,16,128]{3,2,1,0:T(8,128)(2,1)S(1)} %get-tuple-element.40), channel_id=1, source_target_pairs={{0,1},{1,0},{2,3},{3,2},{4,5},{5,4},{6,7},{7,6},{8,9},{9,8},{10,11... | collective-permute-start | bytes 196616 | tf_op jit(solution)/shard_map/ppermute | solution.py:527
  3.6 2.6 %collective-permute-start.6 = (bf16[4,4,16,128]{3,2,1,0:T(8,128)(2,1)S(1)}, bf16[4,4,16,128]{3,2,1,0:T(8,128)(2,1)S(1)}, u32[]{:S(2)}, u32[]{:S(2)}) collective-permute-start(bf16[4,4,16,128]{3,2,1,0:T(8,128)(2,1)S(1)} %get-tuple-element.45), channel_id=1, source_target_pairs={{0,2},{1,3},{2,0},{3,1},{4,6},{5,7},{6,4},{7,5},{8,10},{9,11},{10,... | collective-permute-start | bytes 196616 | tf_op jit(solution)/shard_map/ppermute | solution.py:527
  6.4 2.0 %collective-permute-start.2 = (bf16[8,4,16,128]{3,2,1,0:T(8,128)(2,1)S(1)}, bf16[8,4,16,128]{3,2,1,0:T(8,128)(2,1)S(1)}, u32[]{:S(2)}, u32[]{:S(2)}) collective-permute-start(bf16[8,4,16,128]{3,2,1,0:T(8,128)(2,1)S(1)} %constant_dynamic-update-slice_fusion), channel_id=1, source_target_pairs={{0,4},{8,0},{16,8},{24,16},{28,24},{20,28},{12,20},{4,12},{1,5},{9... | collective-permute-start | bytes 393224 | tf_op jit(solution)/shard_map/ppermute | solution.py:562
  8.5 0.3 collective-permute-done.6
  8.8 1.4 %collective-permute-done.7 = bf16[4,4,16,128]{3,2,1,0:T(8,128)(2,1)S(1)} collective-permute-done((bf16[4,4,16,128]{3,2,1,0:T(8,128)(2,1)S(1)}, bf16[4,4,16,128]{3,2,1,0:T(8,128)(2,1)S(1)}, u32[]{:S(2)}, u32[]{:S(2)}) %collective-permute-start.7) | collective-permute-done | bytes 65568 | tf_op jit(solution)/shard_map/ppermute | solution.py:527
  10.2 1.6 %collective-permute-start.9 = (bf16[8,4,16,128]{3,2,1,0:T(8,128)(2,1)S(1)}, bf16[8,4,16,128]{3,2,1,0:T(8,128)(2,1)S(1)}, u32[]{:S(2)}, u32[]{:S(2)}) collective-permute-start(bf16[8,4,16,128]{3,2,1,0:T(8,128)(2,1)S(1)} %pad_maximum_fusion), channel_id=1, source_target_pairs={{0,4},{8,0},{16,8},{24,16},{28,24},{20,28},{12,20},{4,12},{1,5},{9... | collective-permute-start | bytes 393224 | tf_op jit(solution)/shard_map/ppermute | solution.py:562
  11.8 0.5 collective-permute-start.8
  12.3 1.3 %collective-permute-start.12 = (bf16[4,16,16,128]{3,2,1,0:T(8,128)(2,1)S(1)}, bf16[4,16,16,128]{3,2,1,0:T(8,128)(2,1)S(1)}, u32[]{:S(2)}, u32[]{:S(2)}) collective-permute-start(bf16[4,16,16,128]{3,2,1,0:T(8,128)(2,1)S(1)} %get-tuple-element.54.refs_0_), channel_id=1, source_target_pairs={{0,2},{1,3},{2,0},{3,1},{4,6},{5,7},{6,4},{7,5},{8,10},{9,11},{10,... | collective-permute-start | bytes 786440 | tf_op jit(solution)/shard_map/ppermute | solution.py:527
  13.8 1.6 %collective-permute-start.4 = (bf16[8,4,16,128]{3,2,1,0:T(8,128)(2,1)S(1)}, bf16[8,4,16,128]{3,2,1,0:T(8,128)(2,1)S(1)}, u32[]{:S(2)}, u32[]{:S(2)}) collective-permute-start(bf16[8,4,16,128]{3,2,1,0:T(8,128)(2,1)S(1)} %collective-permute-done.1.rest_2_), channel_id=1, source_target_pairs={{0,8},{8,16},{16,24},{24,28},{28,20},{20,12},{12,4},{4,0},{1,9},{9... | collective-permute-start | bytes 393224 | tf_op jit(solution)/shard_map/ppermute | solution.py:559
  15.4 0.4 collective-permute-start.5
  15.9 0.3 collective-permute-done.9.rest_5_
  16.1 2.0 %collective-permute-done.8.rest_4_ = bf16[8,4,16,128]{3,2,1,0:T(8,128)(2,1)S(1)} collective-permute-done((bf16[8,4,16,128]{3,2,1,0:T(8,128)(2,1)S(1)}, bf16[8,4,16,128]{3,2,1,0:T(8,128)(2,1)S(1)}, u32[]{:S(2)}, u32[]{:S(2)}) %collective-permute-start.8) | collective-permute-done | bytes 131104 | tf_op jit(solution)/shard_map/ppermute | solution.py:559
  18.1 2.0 %collective-permute-start.11 = (bf16[8,4,16,128]{3,2,1,0:T(8,128)(2,1)S(1)}, bf16[8,4,16,128]{3,2,1,0:T(8,128)(2,1)S(1)}, u32[]{:S(2)}, u32[]{:S(2)}) collective-permute-start(bf16[8,4,16,128]{3,2,1,0:T(8,128)(2,1)S(1)} %collective-permute-done.9.rest_5_), channel_id=1, source_target_pairs={{0,4},{8,0},{16,8},{24,16},{28,24},{20,28},{12,20},{4,12},{1,5},{9... | collective-permute-start | bytes 393224 | tf_op jit(solution)/shard_map/ppermute | solution.py:562
  20.2 0.8 %collective-permute-done.4.refs_0_.rest_6_ = bf16[8,4,16,128]{3,2,1,0:T(8,128)(2,1)S(1)} collective-permute-done((bf16[8,4,16,128]{3,2,1,0:T(8,128)(2,1)S(1)}, bf16[8,4,16,128]{3,2,1,0:T(8,128)(2,1)S(1)}, u32[]{:S(2)}, u32[]{:S(2)}) %collective-permute-start.4) | collective-permute-done | bytes 131104 | tf_op jit(solution)/shard_map/ppermute | solution.py:559
  20.9 0.2 collective-permute-done.5.refs_1_.rest_7_
  21.1 2.0 %collective-permute-done.10.refs_2_.rest_8_ = bf16[8,4,16,128]{3,2,1,0:T(8,128)(2,1)S(1)} collective-permute-done((bf16[8,4,16,128]{3,2,1,0:T(8,128)(2,1)S(1)}, bf16[8,4,16,128]{3,2,1,0:T(8,128)(2,1)S(1)}, u32[]{:S(2)}, u32[]{:S(2)}) %collective-permute-start.10) | collective-permute-done | bytes 131104 | tf_op jit(solution)/shard_map/ppermute | solution.py:559
  23.3 1.6 %collective-permute-start.17 = (bf16[16,4,16,128]{3,2,1,0:T(8,128)(2,1)S(1)}, bf16[16,4,16,128]{3,2,1,0:T(8,128)(2,1)S(1)}, u32[]{:S(2)}, u32[]{:S(2)}) collective-permute-start(bf16[16,4,16,128]{3,2,1,0:T(8,128)(2,1)S(1)} %get-tuple-element.61), channel_id=1, source_target_pairs={{0,8},{8,16},{16,24},{24,28},{28,20},{20,12},{12,4},{4,0},{1,9},{9... | collective-permute-start | bytes 786440 | tf_op jit(solution)/shard_map/ppermute | solution.py:559
  25.0 0.4 collective-permute-start.18
  25.6 2.8 %cross.3 = (bf16[256,128]{1,0:T(8,128)(2,1)S(1)}, bf16[256,128]{1,0:T(8,128)(2,1)S(1)}, bf16[256,128]{1,0:T(8,128)(2,1)S(1)}, bf16[256,128]{1,0:T(8,128)(2,1)S(1)}) custom-call(s32[4,8]{1,0:T(4,128)S(1)} %copy-done.2, bf16[512,2048]{1,0:T(8,128)(2,1)S(1)} %copy-done, f32[4,3,8,4,8,128]{5,4,3,2,1,0:T(8,128)S(1)} %widen.2.rest_0_, ...), custom_call_target="tpu_custom_call" | custom-call | flops 2990000128 | bytes 1024 | tf_op jit(solution)/shard_map/cross/pallas_call | solution.py:371
  28.5 1.8 %collective-permute-start.15 = (bf16[256,128]{1,0:T(8,128)(2,1)S(1)}, bf16[256,128]{1,0:T(8,128)(2,1)S(1)}, u32[]{:S(2)}, u32[]{:S(2)}) collective-permute-start(bf16[256,128]{1,0:T(8,128)(2,1)S(1)} %get-tuple-element.58), channel_id=1, source_target_pairs={{0,2},{1,3},{2,0},{3,1},{4,6},{5,7},{6,4},{7,5},{8,10},{9,11},{10,... | collective-permute-start | bytes 196616 | tf_op jit(solution)/shard_map/ppermute | solution.py:527
  30.4 1.9 %collective-permute-done.17.rest_10_ = bf16[16,4,16,128]{3,2,1,0:T(8,128)(2,1)S(1)} collective-permute-done((bf16[16,4,16,128]{3,2,1,0:T(8,128)(2,1)S(1)}, bf16[16,4,16,128]{3,2,1,0:T(8,128)(2,1)S(1)}, u32[]{:S(2)}, u32[]{:S(2)}) %collective-permute-start.17) | collective-permute-done | bytes 262176 | tf_op jit(solution)/shard_map/ppermute | solution.py:559
  32.2 1.4 %collective-permute-start.22 = (bf16[16,4,16,128]{3,2,1,0:T(8,128)(2,1)S(1)}, bf16[16,4,16,128]{3,2,1,0:T(8,128)(2,1)S(1)}, u32[]{:S(2)}, u32[]{:S(2)}) collective-permute-start(bf16[16,4,16,128]{3,2,1,0:T(8,128)(2,1)S(1)} %collective-permute-done.17.rest_10_), channel_id=1, source_target_pairs={{0,8},{8,16},{16,24},{24,28},{28,20},{20,12},{12,4},{4,0},{1,9},{9... | collective-permute-start | bytes 786440 | tf_op jit(solution)/shard_map/ppermute | solution.py:559
  33.6 4.8 %cross.4 = (bf16[512,128]{1,0:T(8,128)(2,1)S(1)}, bf16[512,128]{1,0:T(8,128)(2,1)S(1)}, bf16[512,128]{1,0:T(8,128)(2,1)S(1)}, bf16[512,128]{1,0:T(8,128)(2,1)S(1)}) custom-call(s32[4,8]{1,0:T(4,128)S(1)} %copy-done.2, bf16[512,2048]{1,0:T(8,128)(2,1)S(1)} %copy-done, f32[4,3,8,4,8,128]{5,4,3,2,1,0:T(8,128)S(1)} %widen.2.rest_0_, ...), custom_call_target="tpu_custom_call" | custom-call | flops 5289999872 | bytes 1024 | tf_op jit(solution)/shard_map/cross/pallas_call | solution.py:371
  38.5 1.8 %collective-permute-start.20 = (bf16[512,128]{1,0:T(8,128)(2,1)S(1)}, bf16[512,128]{1,0:T(8,128)(2,1)S(1)}, u32[]{:S(2)}, u32[]{:S(2)}) collective-permute-start(bf16[512,128]{1,0:T(8,128)(2,1)S(1)} %get-tuple-element.65), channel_id=1, source_target_pairs={{0,2},{1,3},{2,0},{3,1},{4,6},{5,7},{6,4},{7,5},{8,10},{9,11},{10,... | collective-permute-start | bytes 393224 | tf_op jit(solution)/shard_map/ppermute | solution.py:527
  40.5 2.8 %cross.5 = (bf16[256,128]{1,0:T(8,128)(2,1)S(1)}, bf16[256,128]{1,0:T(8,128)(2,1)S(1)}, bf16[256,128]{1,0:T(8,128)(2,1)S(1)}, bf16[256,128]{1,0:T(8,128)(2,1)S(1)}) custom-call(s32[4,8]{1,0:T(4,128)S(1)} %copy-done.2, bf16[512,2048]{1,0:T(8,128)(2,1)S(1)} %copy-done, f32[4,3,8,4,8,128]{5,4,3,2,1,0:T(8,128)S(1)} %widen.2.rest_0_, ...), custom_call_target="tpu_custom_call" | custom-call | flops 2990000128 | bytes 1024 | tf_op jit(solution)/shard_map/cross/pallas_call | solution.py:371
  43.3 0.3 collective-permute-start.23
  43.6 1.8 %collective-permute-start.24 = (bf16[256,128]{1,0:T(8,128)(2,1)S(1)}, bf16[256,128]{1,0:T(8,128)(2,1)S(1)}, u32[]{:S(2)}, u32[]{:S(2)}) collective-permute-start(bf16[256,128]{1,0:T(8,128)(2,1)S(1)} %get-tuple-element.71), channel_id=1, source_target_pairs={{0,2},{1,3},{2,0},{3,1},{4,6},{5,7},{6,4},{7,5},{8,10},{9,11},{10,... | collective-permute-start | bytes 196616 | tf_op jit(solution)/shard_map/ppermute | solution.py:527
  45.4 1.5 %collective-permute-done.21.rest_7_ = bf16[512,128]{1,0:T(8,128)(2,1)S(1)} collective-permute-done((bf16[512,128]{1,0:T(8,128)(2,1)S(1)}, bf16[512,128]{1,0:T(8,128)(2,1)S(1)}, u32[]{:S(2)}, u32[]{:S(2)}) %collective-permute-start.21) | collective-permute-done | bytes 131104 | tf_op jit(solution)/shard_map/ppermute | solution.py:527
  47.0 2.1 %early.1 = f32[1024,4,1,128]{3,2,1,0:T(1,128)} custom-call(s32[4,8]{1,0:T(4,128)S(1)} %copy-done.2, bf16[4,128,512]{2,1,0:T(8,128)(2,1)S(1)} %copy-done.1, bf16[256,128]{1,0:T(8,128)(2,1)S(1)} %get-tuple-element.56.rest_0_, bf16[256,128]{1,0:T(8,128)(2,1)S(1)} %collective-permute-done.14.rest_1_, bf16[256,128]{1,0:T(8,128)(2,1)S(1)} %collective-permute-done.15.rest_2_, ...), custom_call_target="tpu_custom_call" | custom-call | flops 57500000 | bytes 1024 | tf_op jit(solution)/shard_map/early/pallas_call | solution.py:473
  49.1 0.7 %collective-permute-done.25.rest_3_ = bf16[256,128]{1,0:T(8,128)(2,1)S(1)} collective-permute-done((bf16[256,128]{1,0:T(8,128)(2,1)S(1)}, bf16[256,128]{1,0:T(8,128)(2,1)S(1)}, u32[]{:S(2)}, u32[]{:S(2)}) %collective-permute-start.25) | collective-permute-done | bytes 65568 | tf_op jit(solution)/shard_map/ppermute | solution.py:527
  49.9 1.7 %late.1 = f32[1024,4,1,128]{3,2,1,0:T(1,128)} custom-call(s32[4,8]{1,0:T(4,128)S(1)} %copy-done.2, bf16[4,128,512]{2,1,0:T(8,128)(2,1)S(1)} %copy-done.1, f32[1024,4,1,128]{3,2,1,0:T(1,128)} %early.1, bf16[256,128]{1,0:T(8,128)(2,1)S(1)} %get-tuple-element.69.rest_0_, ...), custom_call_target="tpu_custom_call", output_to_operand_aliasing={{}: (2, {})} | custom-call | flops 57500000 | bytes 1024 | tf_op jit(solution)/shard_map/late/pallas_call | solution.py:486
  (38 shorter events, 1.2 us)
Async XLA Ops:
  3.0 3.3 %collective-permute-start = (bf16[4,4,16,128]{3,2,1,0:T(8,128)(2,1)S(1)}, bf16[4,4,16,128]{3,2,1,0:T(8,128)(2,1)S(1)}, u32[]{:S(2)}, u32[]{:S(2)}) collective-permute-start(bf16[4,4,16,128]{3,2,1,0:T(8,128)(2,1)S(1)} %get-tuple-element.40), channel_id=1, source_target_pairs={{0,1},{1,0},{2,3},{3,2},{4,5},{5,4},{6,7},{7,6},{8,9},{9,8},{10,11... | collective-permute-start | bytes 196616 | tf_op jit(solution)/shard_map/ppermute | solution.py:527
  3.6 5.3 %collective-permute-start.6 = (bf16[4,4,16,128]{3,2,1,0:T(8,128)(2,1)S(1)}, bf16[4,4,16,128]{3,2,1,0:T(8,128)(2,1)S(1)}, u32[]{:S(2)}, u32[]{:S(2)}) collective-permute-start(bf16[4,4,16,128]{3,2,1,0:T(8,128)(2,1)S(1)} %get-tuple-element.45), channel_id=1, source_target_pairs={{0,2},{1,3},{2,0},{3,1},{4,6},{5,7},{6,4},{7,5},{8,10},{9,11},{10,... | collective-permute-start | bytes 196616 | tf_op jit(solution)/shard_map/ppermute | solution.py:527
  6.1 4.0 %collective-permute-start.7 = (bf16[4,4,16,128]{3,2,1,0:T(8,128)(2,1)S(1)}, bf16[4,4,16,128]{3,2,1,0:T(8,128)(2,1)S(1)}, u32[]{:S(2)}, u32[]{:S(2)}) collective-permute-start(bf16[4,4,16,128]{3,2,1,0:T(8,128)(2,1)S(1)} %get-tuple-element.46), channel_id=1, source_target_pairs={{0,3},{1,2},{2,1},{3,0},{4,7},{5,6},{6,5},{7,4},{8,11},{9,10},{10,... | collective-permute-start | bytes 196616 | tf_op jit(solution)/shard_map/ppermute | solution.py:527
  6.2 4.0 %collective-permute-start.3 = (bf16[4,16,16,128]{3,2,1,0:T(8,128)(2,1)S(1)}, bf16[4,16,16,128]{3,2,1,0:T(8,128)(2,1)S(1)}, u32[]{:S(2)}, u32[]{:S(2)}) collective-permute-start(bf16[4,16,16,128]{3,2,1,0:T(8,128)(2,1)S(1)} %get-tuple-element.54.refs_0_), channel_id=1, source_target_pairs={{0,1},{1,0},{2,3},{3,2},{4,5},{5,4},{6,7},{7,6},{8,9},{9,8},{10,11... | collective-permute-start | bytes 786440 | tf_op jit(solution)/shard_map/ppermute | solution.py:527
  6.4 7.4 %collective-permute-start.2 = (bf16[8,4,16,128]{3,2,1,0:T(8,128)(2,1)S(1)}, bf16[8,4,16,128]{3,2,1,0:T(8,128)(2,1)S(1)}, u32[]{:S(2)}, u32[]{:S(2)}) collective-permute-start(bf16[8,4,16,128]{3,2,1,0:T(8,128)(2,1)S(1)} %constant_dynamic-update-slice_fusion), channel_id=1, source_target_pairs={{0,4},{8,0},{16,8},{24,16},{28,24},{20,28},{12,20},{4,12},{1,5},{9... | collective-permute-start | bytes 393224 | tf_op jit(solution)/shard_map/ppermute | solution.py:562
  8.4 5.4 %collective-permute-start.1 = (bf16[8,4,16,128]{3,2,1,0:T(8,128)(2,1)S(1)}, bf16[8,4,16,128]{3,2,1,0:T(8,128)(2,1)S(1)}, u32[]{:S(2)}, u32[]{:S(2)}) collective-permute-start(bf16[8,4,16,128]{3,2,1,0:T(8,128)(2,1)S(1)} %constant_dynamic-update-slice_fusion), channel_id=1, source_target_pairs={{0,8},{8,16},{16,24},{24,28},{28,20},{20,12},{12,4},{4,0},{1,9},{9... | collective-permute-start | bytes 393224 | tf_op jit(solution)/shard_map/ppermute | solution.py:559
  10.2 15.4 %copy-start = (bf16[512,2048]{1,0:T(8,128)(2,1)S(1)}, bf16[512,2048]{1,0:T(8,128)(2,1)}, u32[]{:S(2)}) copy-start(bf16[512,2048]{1,0:T(8,128)(2,1)} %constant.4.clone.table_hbm.table) | copy-start | bytes 6291460
  10.2 15.4 %copy-start.2 = (s32[4,8]{1,0:T(4,128)S(1)}, s32[4,8]{1,0:T(4,128)}, u32[]{:S(2)}) copy-start(s32[4,8]{1,0:T(4,128)} %plan.9) | copy-start | bytes 388
  10.2 5.9 %collective-permute-start.9 = (bf16[8,4,16,128]{3,2,1,0:T(8,128)(2,1)S(1)}, bf16[8,4,16,128]{3,2,1,0:T(8,128)(2,1)S(1)}, u32[]{:S(2)}, u32[]{:S(2)}) collective-permute-start(bf16[8,4,16,128]{3,2,1,0:T(8,128)(2,1)S(1)} %pad_maximum_fusion), channel_id=1, source_target_pairs={{0,4},{8,0},{16,8},{24,16},{28,24},{20,28},{12,20},{4,12},{1,5},{9... | collective-permute-start | bytes 393224 | tf_op jit(solution)/shard_map/ppermute | solution.py:562
  11.8 6.3 %collective-permute-start.8 = (bf16[8,4,16,128]{3,2,1,0:T(8,128)(2,1)S(1)}, bf16[8,4,16,128]{3,2,1,0:T(8,128)(2,1)S(1)}, u32[]{:S(2)}, u32[]{:S(2)}) collective-permute-start(bf16[8,4,16,128]{3,2,1,0:T(8,128)(2,1)S(1)} %pad_maximum_fusion), channel_id=1, source_target_pairs={{0,8},{8,16},{16,24},{24,28},{28,20},{20,12},{12,4},{4,0},{1,9},{9... | collective-permute-start | bytes 393224 | tf_op jit(solution)/shard_map/ppermute | solution.py:559
  12.3 10.9 %collective-permute-start.12 = (bf16[4,16,16,128]{3,2,1,0:T(8,128)(2,1)S(1)}, bf16[4,16,16,128]{3,2,1,0:T(8,128)(2,1)S(1)}, u32[]{:S(2)}, u32[]{:S(2)}) collective-permute-start(bf16[4,16,16,128]{3,2,1,0:T(8,128)(2,1)S(1)} %get-tuple-element.54.refs_0_), channel_id=1, source_target_pairs={{0,2},{1,3},{2,0},{3,1},{4,6},{5,7},{6,4},{7,5},{8,10},{9,11},{10,... | collective-permute-start | bytes 786440 | tf_op jit(solution)/shard_map/ppermute | solution.py:527
  13.8 7.1 %collective-permute-start.4 = (bf16[8,4,16,128]{3,2,1,0:T(8,128)(2,1)S(1)}, bf16[8,4,16,128]{3,2,1,0:T(8,128)(2,1)S(1)}, u32[]{:S(2)}, u32[]{:S(2)}) collective-permute-start(bf16[8,4,16,128]{3,2,1,0:T(8,128)(2,1)S(1)} %collective-permute-done.1.rest_2_), channel_id=1, source_target_pairs={{0,8},{8,16},{16,24},{24,28},{28,20},{20,12},{12,4},{4,0},{1,9},{9... | collective-permute-start | bytes 393224 | tf_op jit(solution)/shard_map/ppermute | solution.py:559
  15.4 5.7 %collective-permute-start.5 = (bf16[8,4,16,128]{3,2,1,0:T(8,128)(2,1)S(1)}, bf16[8,4,16,128]{3,2,1,0:T(8,128)(2,1)S(1)}, u32[]{:S(2)}, u32[]{:S(2)}) collective-permute-start(bf16[8,4,16,128]{3,2,1,0:T(8,128)(2,1)S(1)} %collective-permute-done.2.rest_3_), channel_id=1, source_target_pairs={{0,4},{8,0},{16,8},{24,16},{28,24},{20,28},{12,20},{4,12},{1,5},{9... | collective-permute-start | bytes 393224 | tf_op jit(solution)/shard_map/ppermute | solution.py:562
  18.1 5.0 %collective-permute-start.10 = (bf16[8,4,16,128]{3,2,1,0:T(8,128)(2,1)S(1)}, bf16[8,4,16,128]{3,2,1,0:T(8,128)(2,1)S(1)}, u32[]{:S(2)}, u32[]{:S(2)}) collective-permute-start(bf16[8,4,16,128]{3,2,1,0:T(8,128)(2,1)S(1)} %collective-permute-done.8.rest_4_), channel_id=1, source_target_pairs={{0,8},{8,16},{16,24},{24,28},{28,20},{20,12},{12,4},{4,0},{1,9},{9... | collective-permute-start | bytes 393224 | tf_op jit(solution)/shard_map/ppermute | solution.py:559
  18.1 5.1 %collective-permute-start.11 = (bf16[8,4,16,128]{3,2,1,0:T(8,128)(2,1)S(1)}, bf16[8,4,16,128]{3,2,1,0:T(8,128)(2,1)S(1)}, u32[]{:S(2)}, u32[]{:S(2)}) collective-permute-start(bf16[8,4,16,128]{3,2,1,0:T(8,128)(2,1)S(1)} %collective-permute-done.9.rest_5_), channel_id=1, source_target_pairs={{0,4},{8,0},{16,8},{24,16},{28,24},{20,28},{12,20},{4,12},{1,5},{9... | collective-permute-start | bytes 393224 | tf_op jit(solution)/shard_map/ppermute | solution.py:562
  23.3 2.2 %collective-permute-start.13 = (bf16[4,16,16,128]{3,2,1,0:T(8,128)(2,1)S(1)}, bf16[4,16,16,128]{3,2,1,0:T(8,128)(2,1)S(1)}, u32[]{:S(2)}, u32[]{:S(2)}) collective-permute-start(bf16[4,16,16,128]{3,2,1,0:T(8,128)(2,1)S(1)} %collective-permute-done.12.refs_0_), channel_id=1, source_target_pairs={{0,1},{1,0},{2,3},{3,2},{4,5},{5,4},{6,7},{7,6},{8,9},{9,8},{10,11... | collective-permute-start | bytes 786440 | tf_op jit(solution)/shard_map/ppermute | solution.py:527
  23.3 8.9 %collective-permute-start.17 = (bf16[16,4,16,128]{3,2,1,0:T(8,128)(2,1)S(1)}, bf16[16,4,16,128]{3,2,1,0:T(8,128)(2,1)S(1)}, u32[]{:S(2)}, u32[]{:S(2)}) collective-permute-start(bf16[16,4,16,128]{3,2,1,0:T(8,128)(2,1)S(1)} %get-tuple-element.61), channel_id=1, source_target_pairs={{0,8},{8,16},{16,24},{24,28},{28,20},{20,12},{12,4},{4,0},{1,9},{9... | collective-permute-start | bytes 786440 | tf_op jit(solution)/shard_map/ppermute | solution.py:559
  25.0 8.7 %collective-permute-start.18 = (bf16[16,4,16,128]{3,2,1,0:T(8,128)(2,1)S(1)}, bf16[16,4,16,128]{3,2,1,0:T(8,128)(2,1)S(1)}, u32[]{:S(2)}, u32[]{:S(2)}) collective-permute-start(bf16[16,4,16,128]{3,2,1,0:T(8,128)(2,1)S(1)} %get-tuple-element.62), channel_id=1, source_target_pairs={{0,4},{8,0},{16,8},{24,16},{28,24},{20,28},{12,20},{4,12},{1,5},{9... | collective-permute-start | bytes 786440 | tf_op jit(solution)/shard_map/ppermute | solution.py:562
  28.4 10.1 %collective-permute-start.14 = (bf16[256,128]{1,0:T(8,128)(2,1)S(1)}, bf16[256,128]{1,0:T(8,128)(2,1)S(1)}, u32[]{:S(2)}, u32[]{:S(2)}) collective-permute-start(bf16[256,128]{1,0:T(8,128)(2,1)S(1)} %get-tuple-element.57), channel_id=1, source_target_pairs={{0,1},{1,0},{2,3},{3,2},{4,5},{5,4},{6,7},{7,6},{8,9},{9,8},{10,11... | collective-permute-start | bytes 196616 | tf_op jit(solution)/shard_map/ppermute | solution.py:527
  28.5 11.8 %collective-permute-start.15 = (bf16[256,128]{1,0:T(8,128)(2,1)S(1)}, bf16[256,128]{1,0:T(8,128)(2,1)S(1)}, u32[]{:S(2)}, u32[]{:S(2)}) collective-permute-start(bf16[256,128]{1,0:T(8,128)(2,1)S(1)} %get-tuple-element.58), channel_id=1, source_target_pairs={{0,2},{1,3},{2,0},{3,1},{4,6},{5,7},{6,4},{7,5},{8,10},{9,11},{10,... | collective-permute-start | bytes 196616 | tf_op jit(solution)/shard_map/ppermute | solution.py:527
  30.3 10.2 %collective-permute-start.16 = (bf16[256,128]{1,0:T(8,128)(2,1)S(1)}, bf16[256,128]{1,0:T(8,128)(2,1)S(1)}, u32[]{:S(2)}, u32[]{:S(2)}) collective-permute-start(bf16[256,128]{1,0:T(8,128)(2,1)S(1)} %get-tuple-element.59), channel_id=1, source_target_pairs={{0,3},{1,2},{2,1},{3,0},{4,7},{5,6},{6,5},{7,4},{8,11},{9,10},{10,... | collective-permute-start | bytes 196616 | tf_op jit(solution)/shard_map/ppermute | solution.py:527
  32.2 8.2 %collective-permute-start.22 = (bf16[16,4,16,128]{3,2,1,0:T(8,128)(2,1)S(1)}, bf16[16,4,16,128]{3,2,1,0:T(8,128)(2,1)S(1)}, u32[]{:S(2)}, u32[]{:S(2)}) collective-permute-start(bf16[16,4,16,128]{3,2,1,0:T(8,128)(2,1)S(1)} %collective-permute-done.17.rest_10_), channel_id=1, source_target_pairs={{0,8},{8,16},{16,24},{24,28},{28,20},{20,12},{12,4},{4,0},{1,9},{9... | collective-permute-start | bytes 786440 | tf_op jit(solution)/shard_map/ppermute | solution.py:559
  38.4 7.0 %collective-permute-start.19 = (bf16[512,128]{1,0:T(8,128)(2,1)S(1)}, bf16[512,128]{1,0:T(8,128)(2,1)S(1)}, u32[]{:S(2)}, u32[]{:S(2)}) collective-permute-start(bf16[512,128]{1,0:T(8,128)(2,1)S(1)} %get-tuple-element.64), channel_id=1, source_target_pairs={{0,1},{1,0},{2,3},{3,2},{4,5},{5,4},{6,7},{7,6},{8,9},{9,8},{10,11... | collective-permute-start | bytes 393224 | tf_op jit(solution)/shard_map/ppermute | solution.py:527
  38.5 6.9 %collective-permute-start.20 = (bf16[512,128]{1,0:T(8,128)(2,1)S(1)}, bf16[512,128]{1,0:T(8,128)(2,1)S(1)}, u32[]{:S(2)}, u32[]{:S(2)}) collective-permute-start(bf16[512,128]{1,0:T(8,128)(2,1)S(1)} %get-tuple-element.65), channel_id=1, source_target_pairs={{0,2},{1,3},{2,0},{3,1},{4,6},{5,7},{6,4},{7,5},{8,10},{9,11},{10,... | collective-permute-start | bytes 393224 | tf_op jit(solution)/shard_map/ppermute | solution.py:527
  40.3 6.6 %collective-permute-start.21 = (bf16[512,128]{1,0:T(8,128)(2,1)S(1)}, bf16[512,128]{1,0:T(8,128)(2,1)S(1)}, u32[]{:S(2)}, u32[]{:S(2)}) collective-permute-start(bf16[512,128]{1,0:T(8,128)(2,1)S(1)} %get-tuple-element.66), channel_id=1, source_target_pairs={{0,3},{1,2},{2,1},{3,0},{4,7},{5,6},{6,5},{7,4},{8,11},{9,10},{10,... | collective-permute-start | bytes 393224 | tf_op jit(solution)/shard_map/ppermute | solution.py:527
  40.4 6.5 %copy-start.1 = (bf16[4,128,512]{2,1,0:T(8,128)(2,1)S(1)}, bf16[4,128,512]{2,1,0:T(8,128)(2,1)}, u32[]{:S(2)}) copy-start(bf16[4,128,512]{2,1,0:T(8,128)(2,1)} %constant.5.clone.place) | copy-start | bytes 1572868
  43.3 5.8 %collective-permute-start.23 = (bf16[256,128]{1,0:T(8,128)(2,1)S(1)}, bf16[256,128]{1,0:T(8,128)(2,1)S(1)}, u32[]{:S(2)}, u32[]{:S(2)}) collective-permute-start(bf16[256,128]{1,0:T(8,128)(2,1)S(1)} %get-tuple-element.70), channel_id=1, source_target_pairs={{0,1},{1,0},{2,3},{3,2},{4,5},{5,4},{6,7},{7,6},{8,9},{9,8},{10,11... | collective-permute-start | bytes 196616 | tf_op jit(solution)/shard_map/ppermute | solution.py:527
  43.6 5.5 %collective-permute-start.24 = (bf16[256,128]{1,0:T(8,128)(2,1)S(1)}, bf16[256,128]{1,0:T(8,128)(2,1)S(1)}, u32[]{:S(2)}, u32[]{:S(2)}) collective-permute-start(bf16[256,128]{1,0:T(8,128)(2,1)S(1)} %get-tuple-element.71), channel_id=1, source_target_pairs={{0,2},{1,3},{2,0},{3,1},{4,6},{5,7},{6,4},{7,5},{8,10},{9,11},{10,... | collective-permute-start | bytes 196616 | tf_op jit(solution)/shard_map/ppermute | solution.py:527
  45.4 4.5 %collective-permute-start.25 = (bf16[256,128]{1,0:T(8,128)(2,1)S(1)}, bf16[256,128]{1,0:T(8,128)(2,1)S(1)}, u32[]{:S(2)}, u32[]{:S(2)}) collective-permute-start(bf16[256,128]{1,0:T(8,128)(2,1)S(1)} %get-tuple-element.72), channel_id=1, source_target_pairs={{0,3},{1,2},{2,1},{3,0},{4,7},{5,6},{6,5},{7,4},{8,11},{9,10},{10,... | collective-permute-start | bytes 196616 | tf_op jit(solution)/shard_map/ppermute | solution.py:527

commit v11 on v10

--- a/solution.py
+++ b/solution.py
@@ -262,59 +262,46 @@
                 lax.fori_loop(0, candidate.shape[0], widen_other, 0)
 
 
-def sum_windows(owns, other, crossed):
+def sum_windows(owns, other, summed):
     groups, _, windows, group = owns[0].shape[:4]
     slots, _, quarter = other.shape[1:4]
     width = groups * group * quarter
-
-    def one_group(slot, index):
-        first = index * group
-        mine = [own.at[index] for own in owns]
-
-        def sums(kind):
+    shift = groups.bit_length() - 1
+
+    for slot in range(slots):
+
+        def body(index, carry, slot=slot):
+            kind, part = index >> shift, index & (groups - 1)
+            mine = [own.at[part, kind] for own in owns]
+            theirs = other.at[kind, slot]
             totals = [None] * (group * quarter)
-            for part, own in enumerate(mine):
+            for half, own in enumerate(mine):
                 for w in range(windows):
-                    left = [own[kind, w, s] for s in range(group)]
-                    right = [other[kind, slot, part * windows + w, t] for t in range(quarter)]
+                    left = [own[w, s] for s in range(group)]
+                    right = [theirs[half * windows + w, t] for t in range(quarter)]
                     for s in range(group):
                         for t in range(quarter):
                             term = left[s] * right[t]
-                            place = s * quarter + t
-                            old = totals[place]
-                            totals[place] = term if old is None else old + term
-            return totals
-
-        def store(place, part, value):
-            at = pl.multiple_of((base + place) * 2 * TILES + part * TILES, TILES)
-            crossed[pl.ds(at, TILES), :] = value
-
-        base = slot * width + first * quarter
-        shared = sums(0)
-        third = sums(2)
-        for place in range(group * quarter):
-            store(place, 0, shared[place] + third[place])
-        second = sums(1)
-        for place in range(group * quarter):
-            store(place, 1, shared[place] - second[place])
-
-    for slot in range(slots):
-
-        def body(index, carry, slot=slot):
-            one_group(slot, index)
+                            old = totals[s * quarter + t]
+                            totals[s * quarter + t] = term if old is None else old + term
+            rows = summed.at[kind]
+            base = (slot * width + part * (group * quarter)) * TILES
+            for place in range(group * quarter):
+                at = pl.multiple_of(base + place * TILES, TILES)
+                rows[pl.ds(at, TILES), :] = totals[place]
             return carry
 
-        lax.fori_loop(0, groups, body, 0)
+        lax.fori_loop(0, 3 * groups, body, 0)
 
 
 def cross_kernel(first_slot, slots, count, scaling, places, parts, plan, table, *rest):
     owns, rest = rest[:2], rest[2:]
     others, rest = rest[: len(places)], rest[len(places) :]
     outs = rest[:parts]
-    other, crossed, operand, result = rest[parts:]
+    other, summed, operand, result = rest[parts:]
     stations = owns[0].shape[0] * owns[0].shape[3]
     widen_others(first_slot, slots, count, places, plan, others, other)
-    sum_windows(owns, other, crossed)
+    sum_windows(owns, other, summed)
     width = stations * other.shape[3]
     columns = slots * width
     even = even_lanes((columns, LANES))
@@ -322,13 +309,14 @@
     sign_imag = lane_cycle([1.0, 1.0, -1.0, -1.0])
     cosine, sine = eighth_turn()
     lane = lax.broadcasted_iota(jnp.int32, (1, LANES), 1)
-    first_weight = jnp.where(lane == 0, 1.0, 2.0).astype(F32)
+    first_weight = jnp.where(lane == 0, 0.5, 1.0).astype(F32)
     for j in range(TILES):
         at = slice(j * LANES, (j + 1) * LANES)
         at_imag = slice(NBIN + j * LANES, NBIN + (j + 1) * LANES)
-        weight = first_weight if j == 0 else 2.0
-        real = crossed[pl.ds(j, columns, stride=2 * TILES), :] * weight
-        imag = crossed[pl.ds(TILES + j, columns, stride=2 * TILES), :] * weight
+        kinds = [summed[kind, pl.ds(j, columns, stride=TILES), :] for kind in range(3)]
+        real, imag = kinds[0] + kinds[2], kinds[0] - kinds[1]
+        if j == 0:
+            real, imag = real * first_weight, imag * first_weight
         turned = [(real, imag), (real * cosine - imag * sine, imag * cosine + real * sine)]
         turned += [quarter_turns(r, i, even, sign_real, sign_imag) for r, i in turned]
         for q in range(CHUNKS):
@@ -338,7 +326,7 @@
     block = lax.dot_general(
         table[...], operand[...], (((1,), (1,)), ((), ())), preferred_element_type=F32
     )
-    block = block * scaling
+    block = block * (2.0 * scaling)
     if slots == 1:
         half = table.shape[0] // 2
         low_lanes = lax.broadcasted_iota(jnp.int32, (half, LANES), 1) < width
@@ -377,7 +365,7 @@
         out_specs=[vmem] * parts,
         scratch_shapes=[
             pltpu.VMEM((3, slots, 2 * windows, quarter, TILES, LANES), F32),
-            pltpu.VMEM((columns * 2 * TILES, LANES), F32),
+            pltpu.VMEM((3, columns * TILES, LANES), F32),
             pltpu.VMEM((CHUNKS * columns, 2 * NBIN), BF),
             pltpu.VMEM((parts,) + out, BF),
         ],
@@ -449,15 +437,23 @@
 
 def late_kernel(count, parts, half, plan, place, early, *rest):
     pieces = rest[:parts]
-    out_hbm, rows, sem = rest[parts:]
+    out_hbm, rows, sems = rest[parts:]
     pairs = place.shape[2] // 2
     number = slot_rounds(plan, count)[ROUNDS - 1]
-    block = placed_block(pieces, joined_matrix(place, parts), slice(0, half), half)
-    store_rows(rows, block[:, :pairs], 0)
-    store_rows(rows, block[:, pairs:], half)
-    copy = pltpu.make_async_copy(rows, out_hbm.at[:, number, 0], sem)
-    copy.start()
-    copy.wait()
+    matrix = joined_matrix(place, parts)
+    copies = []
+    for h in range(2):
+        block = placed_block(
+            pieces, matrix[:, h * pairs : (h + 1) * pairs], slice(0, half), half
+        )
+        store_rows(rows, block, h * half)
+        size = rows.shape[0] // 2
+        at = pl.ds(h * size, size)
+        copy = pltpu.make_async_copy(rows.at[at], out_hbm.at[at, number, 0], sems.at[h])
+        copy.start()
+        copies.append(copy)
+    for copy in copies:
+        copy.wait()
 
 
 def place_lags(plan, groups, pieces, count, stations, parts):
@@ -488,7 +484,7 @@
         out_shape=shape,
         in_specs=[smem, vmem, anywhere] + [vmem] * parts,
         out_specs=anywhere,
-        scratch_shapes=[pltpu.VMEM((share * tiles, LANES), F32), pltpu.SemaphoreType.DMA],
+        scratch_shapes=[pltpu.VMEM((share * tiles, LANES), F32), pltpu.SemaphoreType.DMA((2,))],
         input_output_aliases={2: 0},
         compiler_params=pltpu.CompilerParams(vmem_limit_bytes=16 * 2**20),
         cost_estimate=expected(0.05),

time: 51.7 us -> 51.6 us (level)
  no operation moved by 1% of the time
where the time goes in v11:
time: 51.6 us; the launch traced here: 51.4 us
  starting transfers between devices  22.6 us (44%)
  Pallas kernels  17.4 us (34%)
  waiting for transfers between devices  11.2 us (22%)
    ppermute x15, starting transfers between devices, swap(): return lax.ppermute(value, 'seg', [(i, i ^ j) for i in range(parts)])  10.8 us
    pallas_call x3, Pallas kernels, cross_lags(): pl.pallas_call(functools.partial(cross_kernel, first_slot, slots, count,...  10.3 us
    ppermute x6, waiting for transfers between devices, up(): return lax.ppermute(value, 'sta', upward)  6.65 us
    ppermute x5, starting transfers between devices, down(): return lax.ppermute(value, 'sta', downward)  6.5 us
    ppermute x6, starting transfers between devices, up(): return lax.ppermute(value, 'sta', upward)  5.29 us
    ppermute x15, waiting for transfers between devices, swap(): return lax.ppermute(value, 'seg', [(i, i ^ j) for i in range(parts)])  3.98 us
    pallas_call x1, Pallas kernels, prepare(): pl.pallas_call(functools.partial(prep_kernel, parts), out_shape=[jax.Shap...  3.04 us
    pallas_call x1, Pallas kernels, place_lags(): pl.pallas_call(functools.partial(early_kernel, count, parts, tuple(groups...  2.14 us
  transfers between devices with their start and end apart: 26, of which 11 were waited for; matrix products, arithmetic and copies ran while one was open for 0% of the time, Pallas kernels for 25%

profile of v11, /device:TPU:0, one launch (start us, length us, event | category | flops | bytes accessed | tf_op | source)
XLA Modules:
  0.0 51.4 jit_solution(14247682877552863940)
XLA Ops:
  0.0 3.0 %prep.1 = (bf16[4,16,16,128]{3,2,1,0:T(8,128)(2,1)S(1)}, bf16[4,4,16,128]{3,2,1,0:T(8,128)(2,1)S(1)}, bf16[4,4,16,128]{3,2,1,0:T(8,128)(2,1)S(1)}, bf16[4,4,16,1...) custom-call(f32[16,4,2048]{2,1,0:T(4,128)} %records_hbm.1, bf16[512,2048]{1,0:T(8,128)(2,1)} %constant.4.clone.table_hbm.table), custom_call_target="tpu_custom_call" | custom-call | flops 536870912 | bytes 3145728 | tf_op jit(solution)/shard_map/prep/pallas_call | solution.py:154
  3.0 0.5 %collective-permute-start = (bf16[4,4,16,128]{3,2,1,0:T(8,128)(2,1)S(1)}, bf16[4,4,16,128]{3,2,1,0:T(8,128)(2,1)S(1)}, u32[]{:S(2)}, u32[]{:S(2)}) collective-permute-start(bf16[4,4,16,128]{3,2,1,0:T(8,128)(2,1)S(1)} %get-tuple-element.40), channel_id=1, source_target_pairs={{0,1},{1,0},{2,3},{3,2},{4,5},{5,4},{6,7},{7,6},{8,9},{9,8},{10,11... | collective-permute-start | bytes 196616 | tf_op jit(solution)/shard_map/ppermute | solution.py:523
  3.6 2.6 %collective-permute-start.6 = (bf16[4,4,16,128]{3,2,1,0:T(8,128)(2,1)S(1)}, bf16[4,4,16,128]{3,2,1,0:T(8,128)(2,1)S(1)}, u32[]{:S(2)}, u32[]{:S(2)}) collective-permute-start(bf16[4,4,16,128]{3,2,1,0:T(8,128)(2,1)S(1)} %get-tuple-element.45), channel_id=1, source_target_pairs={{0,2},{1,3},{2,0},{3,1},{4,6},{5,7},{6,4},{7,5},{8,10},{9,11},{10,... | collective-permute-start | bytes 196616 | tf_op jit(solution)/shard_map/ppermute | solution.py:523
  6.4 2.0 %collective-permute-start.2 = (bf16[8,4,16,128]{3,2,1,0:T(8,128)(2,1)S(1)}, bf16[8,4,16,128]{3,2,1,0:T(8,128)(2,1)S(1)}, u32[]{:S(2)}, u32[]{:S(2)}) collective-permute-start(bf16[8,4,16,128]{3,2,1,0:T(8,128)(2,1)S(1)} %constant_dynamic-update-slice_fusion), channel_id=1, source_target_pairs={{0,4},{8,0},{16,8},{24,16},{28,24},{20,28},{12,20},{4,12},{1,5},{9... | collective-permute-start | bytes 393224 | tf_op jit(solution)/shard_map/ppermute | solution.py:558
  8.5 0.3 collective-permute-done.6
  8.8 1.4 %collective-permute-done.7 = bf16[4,4,16,128]{3,2,1,0:T(8,128)(2,1)S(1)} collective-permute-done((bf16[4,4,16,128]{3,2,1,0:T(8,128)(2,1)S(1)}, bf16[4,4,16,128]{3,2,1,0:T(8,128)(2,1)S(1)}, u32[]{:S(2)}, u32[]{:S(2)}) %collective-permute-start.7) | collective-permute-done | bytes 65568 | tf_op jit(solution)/shard_map/ppermute | solution.py:523
  10.2 1.6 %collective-permute-start.9 = (bf16[8,4,16,128]{3,2,1,0:T(8,128)(2,1)S(1)}, bf16[8,4,16,128]{3,2,1,0:T(8,128)(2,1)S(1)}, u32[]{:S(2)}, u32[]{:S(2)}) collective-permute-start(bf16[8,4,16,128]{3,2,1,0:T(8,128)(2,1)S(1)} %pad_maximum_fusion), channel_id=1, source_target_pairs={{0,4},{8,0},{16,8},{24,16},{28,24},{20,28},{12,20},{4,12},{1,5},{9... | collective-permute-start | bytes 393224 | tf_op jit(solution)/shard_map/ppermute | solution.py:558
  11.8 0.5 collective-permute-start.8
  12.3 1.3 %collective-permute-start.12 = (bf16[4,16,16,128]{3,2,1,0:T(8,128)(2,1)S(1)}, bf16[4,16,16,128]{3,2,1,0:T(8,128)(2,1)S(1)}, u32[]{:S(2)}, u32[]{:S(2)}) collective-permute-start(bf16[4,16,16,128]{3,2,1,0:T(8,128)(2,1)S(1)} %get-tuple-element.54.refs_0_), channel_id=1, source_target_pairs={{0,2},{1,3},{2,0},{3,1},{4,6},{5,7},{6,4},{7,5},{8,10},{9,11},{10,... | collective-permute-start | bytes 786440 | tf_op jit(solution)/shard_map/ppermute | solution.py:523
  13.8 1.6 %collective-permute-start.4 = (bf16[8,4,16,128]{3,2,1,0:T(8,128)(2,1)S(1)}, bf16[8,4,16,128]{3,2,1,0:T(8,128)(2,1)S(1)}, u32[]{:S(2)}, u32[]{:S(2)}) collective-permute-start(bf16[8,4,16,128]{3,2,1,0:T(8,128)(2,1)S(1)} %collective-permute-done.1.rest_2_), channel_id=1, source_target_pairs={{0,8},{8,16},{16,24},{24,28},{28,20},{20,12},{12,4},{4,0},{1,9},{9... | collective-permute-start | bytes 393224 | tf_op jit(solution)/shard_map/ppermute | solution.py:555
  15.4 0.4 collective-permute-start.5
  15.9 0.3 collective-permute-done.9.rest_5_
  16.1 2.0 %collective-permute-done.8.rest_4_ = bf16[8,4,16,128]{3,2,1,0:T(8,128)(2,1)S(1)} collective-permute-done((bf16[8,4,16,128]{3,2,1,0:T(8,128)(2,1)S(1)}, bf16[8,4,16,128]{3,2,1,0:T(8,128)(2,1)S(1)}, u32[]{:S(2)}, u32[]{:S(2)}) %collective-permute-start.8) | collective-permute-done | bytes 131104 | tf_op jit(solution)/shard_map/ppermute | solution.py:555
  18.1 2.0 %collective-permute-start.11 = (bf16[8,4,16,128]{3,2,1,0:T(8,128)(2,1)S(1)}, bf16[8,4,16,128]{3,2,1,0:T(8,128)(2,1)S(1)}, u32[]{:S(2)}, u32[]{:S(2)}) collective-permute-start(bf16[8,4,16,128]{3,2,1,0:T(8,128)(2,1)S(1)} %collective-permute-done.9.rest_5_), channel_id=1, source_target_pairs={{0,4},{8,0},{16,8},{24,16},{28,24},{20,28},{12,20},{4,12},{1,5},{9... | collective-permute-start | bytes 393224 | tf_op jit(solution)/shard_map/ppermute | solution.py:558
  20.2 0.8 %collective-permute-done.4.refs_0_.rest_6_ = bf16[8,4,16,128]{3,2,1,0:T(8,128)(2,1)S(1)} collective-permute-done((bf16[8,4,16,128]{3,2,1,0:T(8,128)(2,1)S(1)}, bf16[8,4,16,128]{3,2,1,0:T(8,128)(2,1)S(1)}, u32[]{:S(2)}, u32[]{:S(2)}) %collective-permute-start.4) | collective-permute-done | bytes 131104 | tf_op jit(solution)/shard_map/ppermute | solution.py:555
  20.9 0.2 collective-permute-done.5.refs_1_.rest_7_
  21.1 2.0 %collective-permute-done.10.refs_2_.rest_8_ = bf16[8,4,16,128]{3,2,1,0:T(8,128)(2,1)S(1)} collective-permute-done((bf16[8,4,16,128]{3,2,1,0:T(8,128)(2,1)S(1)}, bf16[8,4,16,128]{3,2,1,0:T(8,128)(2,1)S(1)}, u32[]{:S(2)}, u32[]{:S(2)}) %collective-permute-start.10) | collective-permute-done | bytes 131104 | tf_op jit(solution)/shard_map/ppermute | solution.py:555
  23.3 1.6 %collective-permute-start.17 = (bf16[16,4,16,128]{3,2,1,0:T(8,128)(2,1)S(1)}, bf16[16,4,16,128]{3,2,1,0:T(8,128)(2,1)S(1)}, u32[]{:S(2)}, u32[]{:S(2)}) collective-permute-start(bf16[16,4,16,128]{3,2,1,0:T(8,128)(2,1)S(1)} %get-tuple-element.61), channel_id=1, source_target_pairs={{0,8},{8,16},{16,24},{24,28},{28,20},{20,12},{12,4},{4,0},{1,9},{9... | collective-permute-start | bytes 786440 | tf_op jit(solution)/shard_map/ppermute | solution.py:555
  25.0 0.4 collective-permute-start.18
  25.6 2.8 %cross.3 = (bf16[256,128]{1,0:T(8,128)(2,1)S(1)}, bf16[256,128]{1,0:T(8,128)(2,1)S(1)}, bf16[256,128]{1,0:T(8,128)(2,1)S(1)}, bf16[256,128]{1,0:T(8,128)(2,1)S(1)}) custom-call(s32[4,8]{1,0:T(4,128)S(1)} %copy-done.2, bf16[512,2048]{1,0:T(8,128)(2,1)S(1)} %copy-done, f32[4,3,8,4,8,128]{5,4,3,2,1,0:T(8,128)S(1)} %widen.2.rest_0_, ...), custom_call_target="tpu_custom_call" | custom-call | flops 2990000128 | bytes 1024 | tf_op jit(solution)/shard_map/cross/pallas_call | solution.py:359
  28.5 1.8 %collective-permute-start.15 = (bf16[256,128]{1,0:T(8,128)(2,1)S(1)}, bf16[256,128]{1,0:T(8,128)(2,1)S(1)}, u32[]{:S(2)}, u32[]{:S(2)}) collective-permute-start(bf16[256,128]{1,0:T(8,128)(2,1)S(1)} %get-tuple-element.58), channel_id=1, source_target_pairs={{0,2},{1,3},{2,0},{3,1},{4,6},{5,7},{6,4},{7,5},{8,10},{9,11},{10,... | collective-permute-start | bytes 196616 | tf_op jit(solution)/shard_map/ppermute | solution.py:523
  30.3 1.9 %collective-permute-done.17.rest_10_ = bf16[16,4,16,128]{3,2,1,0:T(8,128)(2,1)S(1)} collective-permute-done((bf16[16,4,16,128]{3,2,1,0:T(8,128)(2,1)S(1)}, bf16[16,4,16,128]{3,2,1,0:T(8,128)(2,1)S(1)}, u32[]{:S(2)}, u32[]{:S(2)}) %collective-permute-start.17) | collective-permute-done | bytes 262176 | tf_op jit(solution)/shard_map/ppermute | solution.py:555
  32.2 1.4 %collective-permute-start.22 = (bf16[16,4,16,128]{3,2,1,0:T(8,128)(2,1)S(1)}, bf16[16,4,16,128]{3,2,1,0:T(8,128)(2,1)S(1)}, u32[]{:S(2)}, u32[]{:S(2)}) collective-permute-start(bf16[16,4,16,128]{3,2,1,0:T(8,128)(2,1)S(1)} %collective-permute-done.17.rest_10_), channel_id=1, source_target_pairs={{0,8},{8,16},{16,24},{24,28},{28,20},{20,12},{12,4},{4,0},{1,9},{9... | collective-permute-start | bytes 786440 | tf_op jit(solution)/shard_map/ppermute | solution.py:555
  33.6 4.7 %cross.4 = (bf16[512,128]{1,0:T(8,128)(2,1)S(1)}, bf16[512,128]{1,0:T(8,128)(2,1)S(1)}, bf16[512,128]{1,0:T(8,128)(2,1)S(1)}, bf16[512,128]{1,0:T(8,128)(2,1)S(1)}) custom-call(s32[4,8]{1,0:T(4,128)S(1)} %copy-done.2, bf16[512,2048]{1,0:T(8,128)(2,1)S(1)} %copy-done, f32[4,3,8,4,8,128]{5,4,3,2,1,0:T(8,128)S(1)} %widen.2.rest_0_, ...), custom_call_target="tpu_custom_call" | custom-call | flops 5289999872 | bytes 1024 | tf_op jit(solution)/shard_map/cross/pallas_call | solution.py:359
  38.4 1.8 %collective-permute-start.20 = (bf16[512,128]{1,0:T(8,128)(2,1)S(1)}, bf16[512,128]{1,0:T(8,128)(2,1)S(1)}, u32[]{:S(2)}, u32[]{:S(2)}) collective-permute-start(bf16[512,128]{1,0:T(8,128)(2,1)S(1)} %get-tuple-element.65), channel_id=1, source_target_pairs={{0,2},{1,3},{2,0},{3,1},{4,6},{5,7},{6,4},{7,5},{8,10},{9,11},{10,... | collective-permute-start | bytes 393224 | tf_op jit(solution)/shard_map/ppermute | solution.py:523
  40.3 2.9 %cross.5 = (bf16[256,128]{1,0:T(8,128)(2,1)S(1)}, bf16[256,128]{1,0:T(8,128)(2,1)S(1)}, bf16[256,128]{1,0:T(8,128)(2,1)S(1)}, bf16[256,128]{1,0:T(8,128)(2,1)S(1)}) custom-call(s32[4,8]{1,0:T(4,128)S(1)} %copy-done.2, bf16[512,2048]{1,0:T(8,128)(2,1)S(1)} %copy-done, f32[4,3,8,4,8,128]{5,4,3,2,1,0:T(8,128)S(1)} %widen.2.rest_0_, ...), custom_call_target="tpu_custom_call" | custom-call | flops 2990000128 | bytes 1024 | tf_op jit(solution)/shard_map/cross/pallas_call | solution.py:359
  43.2 0.3 collective-permute-start.23
  43.5 1.8 %collective-permute-start.24 = (bf16[256,128]{1,0:T(8,128)(2,1)S(1)}, bf16[256,128]{1,0:T(8,128)(2,1)S(1)}, u32[]{:S(2)}, u32[]{:S(2)}) collective-permute-start(bf16[256,128]{1,0:T(8,128)(2,1)S(1)} %get-tuple-element.71), channel_id=1, source_target_pairs={{0,2},{1,3},{2,0},{3,1},{4,6},{5,7},{6,4},{7,5},{8,10},{9,11},{10,... | collective-permute-start | bytes 196616 | tf_op jit(solution)/shard_map/ppermute | solution.py:523
  45.3 1.5 %collective-permute-done.21.rest_7_ = bf16[512,128]{1,0:T(8,128)(2,1)S(1)} collective-permute-done((bf16[512,128]{1,0:T(8,128)(2,1)S(1)}, bf16[512,128]{1,0:T(8,128)(2,1)S(1)}, u32[]{:S(2)}, u32[]{:S(2)}) %collective-permute-start.21) | collective-permute-done | bytes 131104 | tf_op jit(solution)/shard_map/ppermute | solution.py:523
  46.9 2.1 %early.1 = f32[1024,4,1,128]{3,2,1,0:T(1,128)} custom-call(s32[4,8]{1,0:T(4,128)S(1)} %copy-done.2, bf16[4,128,512]{2,1,0:T(8,128)(2,1)S(1)} %copy-done.1, bf16[256,128]{1,0:T(8,128)(2,1)S(1)} %get-tuple-element.56.rest_0_, bf16[256,128]{1,0:T(8,128)(2,1)S(1)} %collective-permute-done.14.rest_1_, bf16[256,128]{1,0:T(8,128)(2,1)S(1)} %collective-permute-done.15.rest_2_, ...), custom_call_target="tpu_custom_call" | custom-call | flops 57500000 | bytes 1024 | tf_op jit(solution)/shard_map/early/pallas_call | solution.py:469
  49.0 0.8 %collective-permute-done.25.rest_3_ = bf16[256,128]{1,0:T(8,128)(2,1)S(1)} collective-permute-done((bf16[256,128]{1,0:T(8,128)(2,1)S(1)}, bf16[256,128]{1,0:T(8,128)(2,1)S(1)}, u32[]{:S(2)}, u32[]{:S(2)}) %collective-permute-start.25) | collective-permute-done | bytes 65568 | tf_op jit(solution)/shard_map/ppermute | solution.py:523
  49.8 1.7 %late.1 = f32[1024,4,1,128]{3,2,1,0:T(1,128)} custom-call(s32[4,8]{1,0:T(4,128)S(1)} %copy-done.2, bf16[4,128,512]{2,1,0:T(8,128)(2,1)S(1)} %copy-done.1, f32[1024,4,1,128]{3,2,1,0:T(1,128)} %early.1, bf16[256,128]{1,0:T(8,128)(2,1)S(1)} %get-tuple-element.69.rest_0_, ...), custom_call_target="tpu_custom_call", output_to_operand_aliasing={{}: (2, {})} | custom-call | flops 57500000 | bytes 1024 | tf_op jit(solution)/shard_map/late/pallas_call | solution.py:482
  (38 shorter events, 1.2 us)
Async XLA Ops:
  3.0 3.3 %collective-permute-start = (bf16[4,4,16,128]{3,2,1,0:T(8,128)(2,1)S(1)}, bf16[4,4,16,128]{3,2,1,0:T(8,128)(2,1)S(1)}, u32[]{:S(2)}, u32[]{:S(2)}) collective-permute-start(bf16[4,4,16,128]{3,2,1,0:T(8,128)(2,1)S(1)} %get-tuple-element.40), channel_id=1, source_target_pairs={{0,1},{1,0},{2,3},{3,2},{4,5},{5,4},{6,7},{7,6},{8,9},{9,8},{10,11... | collective-permute-start | bytes 196616 | tf_op jit(solution)/shard_map/ppermute | solution.py:523
  3.6 5.3 %collective-permute-start.6 = (bf16[4,4,16,128]{3,2,1,0:T(8,128)(2,1)S(1)}, bf16[4,4,16,128]{3,2,1,0:T(8,128)(2,1)S(1)}, u32[]{:S(2)}, u32[]{:S(2)}) collective-permute-start(bf16[4,4,16,128]{3,2,1,0:T(8,128)(2,1)S(1)} %get-tuple-element.45), channel_id=1, source_target_pairs={{0,2},{1,3},{2,0},{3,1},{4,6},{5,7},{6,4},{7,5},{8,10},{9,11},{10,... | collective-permute-start | bytes 196616 | tf_op jit(solution)/shard_map/ppermute | solution.py:523
  6.1 4.0 %collective-permute-start.7 = (bf16[4,4,16,128]{3,2,1,0:T(8,128)(2,1)S(1)}, bf16[4,4,16,128]{3,2,1,0:T(8,128)(2,1)S(1)}, u32[]{:S(2)}, u32[]{:S(2)}) collective-permute-start(bf16[4,4,16,128]{3,2,1,0:T(8,128)(2,1)S(1)} %get-tuple-element.46), channel_id=1, source_target_pairs={{0,3},{1,2},{2,1},{3,0},{4,7},{5,6},{6,5},{7,4},{8,11},{9,10},{10,... | collective-permute-start | bytes 196616 | tf_op jit(solution)/shard_map/ppermute | solution.py:523
  6.2 4.0 %collective-permute-start.3 = (bf16[4,16,16,128]{3,2,1,0:T(8,128)(2,1)S(1)}, bf16[4,16,16,128]{3,2,1,0:T(8,128)(2,1)S(1)}, u32[]{:S(2)}, u32[]{:S(2)}) collective-permute-start(bf16[4,16,16,128]{3,2,1,0:T(8,128)(2,1)S(1)} %get-tuple-element.54.refs_0_), channel_id=1, source_target_pairs={{0,1},{1,0},{2,3},{3,2},{4,5},{5,4},{6,7},{7,6},{8,9},{9,8},{10,11... | collective-permute-start | bytes 786440 | tf_op jit(solution)/shard_map/ppermute | solution.py:523
  6.4 7.4 %collective-permute-start.2 = (bf16[8,4,16,128]{3,2,1,0:T(8,128)(2,1)S(1)}, bf16[8,4,16,128]{3,2,1,0:T(8,128)(2,1)S(1)}, u32[]{:S(2)}, u32[]{:S(2)}) collective-permute-start(bf16[8,4,16,128]{3,2,1,0:T(8,128)(2,1)S(1)} %constant_dynamic-update-slice_fusion), channel_id=1, source_target_pairs={{0,4},{8,0},{16,8},{24,16},{28,24},{20,28},{12,20},{4,12},{1,5},{9... | collective-permute-start | bytes 393224 | tf_op jit(solution)/shard_map/ppermute | solution.py:558
  8.4 5.4 %collective-permute-start.1 = (bf16[8,4,16,128]{3,2,1,0:T(8,128)(2,1)S(1)}, bf16[8,4,16,128]{3,2,1,0:T(8,128)(2,1)S(1)}, u32[]{:S(2)}, u32[]{:S(2)}) collective-permute-start(bf16[8,4,16,128]{3,2,1,0:T(8,128)(2,1)S(1)} %constant_dynamic-update-slice_fusion), channel_id=1, source_target_pairs={{0,8},{8,16},{16,24},{24,28},{28,20},{20,12},{12,4},{4,0},{1,9},{9... | collective-permute-start | bytes 393224 | tf_op jit(solution)/shard_map/ppermute | solution.py:555
  10.2 15.4 %copy-start = (bf16[512,2048]{1,0:T(8,128)(2,1)S(1)}, bf16[512,2048]{1,0:T(8,128)(2,1)}, u32[]{:S(2)}) copy-start(bf16[512,2048]{1,0:T(8,128)(2,1)} %constant.4.clone.table_hbm.table) | copy-start | bytes 6291460
  10.2 15.4 %copy-start.2 = (s32[4,8]{1,0:T(4,128)S(1)}, s32[4,8]{1,0:T(4,128)}, u32[]{:S(2)}) copy-start(s32[4,8]{1,0:T(4,128)} %plan.9) | copy-start | bytes 388
  10.2 5.9 %collective-permute-start.9 = (bf16[8,4,16,128]{3,2,1,0:T(8,128)(2,1)S(1)}, bf16[8,4,16,128]{3,2,1,0:T(8,128)(2,1)S(1)}, u32[]{:S(2)}, u32[]{:S(2)}) collective-permute-start(bf16[8,4,16,128]{3,2,1,0:T(8,128)(2,1)S(1)} %pad_maximum_fusion), channel_id=1, source_target_pairs={{0,4},{8,0},{16,8},{24,16},{28,24},{20,28},{12,20},{4,12},{1,5},{9... | collective-permute-start | bytes 393224 | tf_op jit(solution)/shard_map/ppermute | solution.py:558
  11.8 6.3 %collective-permute-start.8 = (bf16[8,4,16,128]{3,2,1,0:T(8,128)(2,1)S(1)}, bf16[8,4,16,128]{3,2,1,0:T(8,128)(2,1)S(1)}, u32[]{:S(2)}, u32[]{:S(2)}) collective-permute-start(bf16[8,4,16,128]{3,2,1,0:T(8,128)(2,1)S(1)} %pad_maximum_fusion), channel_id=1, source_target_pairs={{0,8},{8,16},{16,24},{24,28},{28,20},{20,12},{12,4},{4,0},{1,9},{9... | collective-permute-start | bytes 393224 | tf_op jit(solution)/shard_map/ppermute | solution.py:555
  12.3 10.9 %collective-permute-start.12 = (bf16[4,16,16,128]{3,2,1,0:T(8,128)(2,1)S(1)}, bf16[4,16,16,128]{3,2,1,0:T(8,128)(2,1)S(1)}, u32[]{:S(2)}, u32[]{:S(2)}) collective-permute-start(bf16[4,16,16,128]{3,2,1,0:T(8,128)(2,1)S(1)} %get-tuple-element.54.refs_0_), channel_id=1, source_target_pairs={{0,2},{1,3},{2,0},{3,1},{4,6},{5,7},{6,4},{7,5},{8,10},{9,11},{10,... | collective-permute-start | bytes 786440 | tf_op jit(solution)/shard_map/ppermute | solution.py:523
  13.8 7.1 %collective-permute-start.4 = (bf16[8,4,16,128]{3,2,1,0:T(8,128)(2,1)S(1)}, bf16[8,4,16,128]{3,2,1,0:T(8,128)(2,1)S(1)}, u32[]{:S(2)}, u32[]{:S(2)}) collective-permute-start(bf16[8,4,16,128]{3,2,1,0:T(8,128)(2,1)S(1)} %collective-permute-done.1.rest_2_), channel_id=1, source_target_pairs={{0,8},{8,16},{16,24},{24,28},{28,20},{20,12},{12,4},{4,0},{1,9},{9... | collective-permute-start | bytes 393224 | tf_op jit(solution)/shard_map/ppermute | solution.py:555
  15.4 5.7 %collective-permute-start.5 = (bf16[8,4,16,128]{3,2,1,0:T(8,128)(2,1)S(1)}, bf16[8,4,16,128]{3,2,1,0:T(8,128)(2,1)S(1)}, u32[]{:S(2)}, u32[]{:S(2)}) collective-permute-start(bf16[8,4,16,128]{3,2,1,0:T(8,128)(2,1)S(1)} %collective-permute-done.2.rest_3_), channel_id=1, source_target_pairs={{0,4},{8,0},{16,8},{24,16},{28,24},{20,28},{12,20},{4,12},{1,5},{9... | collective-permute-start | bytes 393224 | tf_op jit(solution)/shard_map/ppermute | solution.py:558
  18.1 5.0 %collective-permute-start.10 = (bf16[8,4,16,128]{3,2,1,0:T(8,128)(2,1)S(1)}, bf16[8,4,16,128]{3,2,1,0:T(8,128)(2,1)S(1)}, u32[]{:S(2)}, u32[]{:S(2)}) collective-permute-start(bf16[8,4,16,128]{3,2,1,0:T(8,128)(2,1)S(1)} %collective-permute-done.8.rest_4_), channel_id=1, source_target_pairs={{0,8},{8,16},{16,24},{24,28},{28,20},{20,12},{12,4},{4,0},{1,9},{9... | collective-permute-start | bytes 393224 | tf_op jit(solution)/shard_map/ppermute | solution.py:555
  18.1 5.1 %collective-permute-start.11 = (bf16[8,4,16,128]{3,2,1,0:T(8,128)(2,1)S(1)}, bf16[8,4,16,128]{3,2,1,0:T(8,128)(2,1)S(1)}, u32[]{:S(2)}, u32[]{:S(2)}) collective-permute-start(bf16[8,4,16,128]{3,2,1,0:T(8,128)(2,1)S(1)} %collective-permute-done.9.rest_5_), channel_id=1, source_target_pairs={{0,4},{8,0},{16,8},{24,16},{28,24},{20,28},{12,20},{4,12},{1,5},{9... | collective-permute-start | bytes 393224 | tf_op jit(solution)/shard_map/ppermute | solution.py:558
  23.3 2.2 %collective-permute-start.13 = (bf16[4,16,16,128]{3,2,1,0:T(8,128)(2,1)S(1)}, bf16[4,16,16,128]{3,2,1,0:T(8,128)(2,1)S(1)}, u32[]{:S(2)}, u32[]{:S(2)}) collective-permute-start(bf16[4,16,16,128]{3,2,1,0:T(8,128)(2,1)S(1)} %collective-permute-done.12.refs_0_), channel_id=1, source_target_pairs={{0,1},{1,0},{2,3},{3,2},{4,5},{5,4},{6,7},{7,6},{8,9},{9,8},{10,11... | collective-permute-start | bytes 786440 | tf_op jit(solution)/shard_map/ppermute | solution.py:523
  23.3 8.9 %collective-permute-start.17 = (bf16[16,4,16,128]{3,2,1,0:T(8,128)(2,1)S(1)}, bf16[16,4,16,128]{3,2,1,0:T(8,128)(2,1)S(1)}, u32[]{:S(2)}, u32[]{:S(2)}) collective-permute-start(bf16[16,4,16,128]{3,2,1,0:T(8,128)(2,1)S(1)} %get-tuple-element.61), channel_id=1, source_target_pairs={{0,8},{8,16},{16,24},{24,28},{28,20},{20,12},{12,4},{4,0},{1,9},{9... | collective-permute-start | bytes 786440 | tf_op jit(solution)/shard_map/ppermute | solution.py:555
  25.0 8.7 %collective-permute-start.18 = (bf16[16,4,16,128]{3,2,1,0:T(8,128)(2,1)S(1)}, bf16[16,4,16,128]{3,2,1,0:T(8,128)(2,1)S(1)}, u32[]{:S(2)}, u32[]{:S(2)}) collective-permute-start(bf16[16,4,16,128]{3,2,1,0:T(8,128)(2,1)S(1)} %get-tuple-element.62), channel_id=1, source_target_pairs={{0,4},{8,0},{16,8},{24,16},{28,24},{20,28},{12,20},{4,12},{1,5},{9... | collective-permute-start | bytes 786440 | tf_op jit(solution)/shard_map/ppermute | solution.py:558
  28.4 10.0 %collective-permute-start.14 = (bf16[256,128]{1,0:T(8,128)(2,1)S(1)}, bf16[256,128]{1,0:T(8,128)(2,1)S(1)}, u32[]{:S(2)}, u32[]{:S(2)}) collective-permute-start(bf16[256,128]{1,0:T(8,128)(2,1)S(1)} %get-tuple-element.57), channel_id=1, source_target_pairs={{0,1},{1,0},{2,3},{3,2},{4,5},{5,4},{6,7},{7,6},{8,9},{9,8},{10,11... | collective-permute-start | bytes 196616 | tf_op jit(solution)/shard_map/ppermute | solution.py:523
  28.5 11.7 %collective-permute-start.15 = (bf16[256,128]{1,0:T(8,128)(2,1)S(1)}, bf16[256,128]{1,0:T(8,128)(2,1)S(1)}, u32[]{:S(2)}, u32[]{:S(2)}) collective-permute-start(bf16[256,128]{1,0:T(8,128)(2,1)S(1)} %get-tuple-element.58), channel_id=1, source_target_pairs={{0,2},{1,3},{2,0},{3,1},{4,6},{5,7},{6,4},{7,5},{8,10},{9,11},{10,... | collective-permute-start | bytes 196616 | tf_op jit(solution)/shard_map/ppermute | solution.py:523
  30.3 10.1 %collective-permute-start.16 = (bf16[256,128]{1,0:T(8,128)(2,1)S(1)}, bf16[256,128]{1,0:T(8,128)(2,1)S(1)}, u32[]{:S(2)}, u32[]{:S(2)}) collective-permute-start(bf16[256,128]{1,0:T(8,128)(2,1)S(1)} %get-tuple-element.59), channel_id=1, source_target_pairs={{0,3},{1,2},{2,1},{3,0},{4,7},{5,6},{6,5},{7,4},{8,11},{9,10},{10,... | collective-permute-start | bytes 196616 | tf_op jit(solution)/shard_map/ppermute | solution.py:523
  32.2 8.1 %collective-permute-start.22 = (bf16[16,4,16,128]{3,2,1,0:T(8,128)(2,1)S(1)}, bf16[16,4,16,128]{3,2,1,0:T(8,128)(2,1)S(1)}, u32[]{:S(2)}, u32[]{:S(2)}) collective-permute-start(bf16[16,4,16,128]{3,2,1,0:T(8,128)(2,1)S(1)} %collective-permute-done.17.rest_10_), channel_id=1, source_target_pairs={{0,8},{8,16},{16,24},{24,28},{28,20},{20,12},{12,4},{4,0},{1,9},{9... | collective-permute-start | bytes 786440 | tf_op jit(solution)/shard_map/ppermute | solution.py:555
  38.3 7.0 %collective-permute-start.19 = (bf16[512,128]{1,0:T(8,128)(2,1)S(1)}, bf16[512,128]{1,0:T(8,128)(2,1)S(1)}, u32[]{:S(2)}, u32[]{:S(2)}) collective-permute-start(bf16[512,128]{1,0:T(8,128)(2,1)S(1)} %get-tuple-element.64), channel_id=1, source_target_pairs={{0,1},{1,0},{2,3},{3,2},{4,5},{5,4},{6,7},{7,6},{8,9},{9,8},{10,11... | collective-permute-start | bytes 393224 | tf_op jit(solution)/shard_map/ppermute | solution.py:523
  38.4 6.9 %collective-permute-start.20 = (bf16[512,128]{1,0:T(8,128)(2,1)S(1)}, bf16[512,128]{1,0:T(8,128)(2,1)S(1)}, u32[]{:S(2)}, u32[]{:S(2)}) collective-permute-start(bf16[512,128]{1,0:T(8,128)(2,1)S(1)} %get-tuple-element.65), channel_id=1, source_target_pairs={{0,2},{1,3},{2,0},{3,1},{4,6},{5,7},{6,4},{7,5},{8,10},{9,11},{10,... | collective-permute-start | bytes 393224 | tf_op jit(solution)/shard_map/ppermute | solution.py:523
  40.2 6.6 %collective-permute-start.21 = (bf16[512,128]{1,0:T(8,128)(2,1)S(1)}, bf16[512,128]{1,0:T(8,128)(2,1)S(1)}, u32[]{:S(2)}, u32[]{:S(2)}) collective-permute-start(bf16[512,128]{1,0:T(8,128)(2,1)S(1)} %get-tuple-element.66), channel_id=1, source_target_pairs={{0,3},{1,2},{2,1},{3,0},{4,7},{5,6},{6,5},{7,4},{8,11},{9,10},{10,... | collective-permute-start | bytes 393224 | tf_op jit(solution)/shard_map/ppermute | solution.py:523
  40.3 6.5 %copy-start.1 = (bf16[4,128,512]{2,1,0:T(8,128)(2,1)S(1)}, bf16[4,128,512]{2,1,0:T(8,128)(2,1)}, u32[]{:S(2)}) copy-start(bf16[4,128,512]{2,1,0:T(8,128)(2,1)} %constant.5.clone.place) | copy-start | bytes 1572868
  43.2 5.8 %collective-permute-start.23 = (bf16[256,128]{1,0:T(8,128)(2,1)S(1)}, bf16[256,128]{1,0:T(8,128)(2,1)S(1)}, u32[]{:S(2)}, u32[]{:S(2)}) collective-permute-start(bf16[256,128]{1,0:T(8,128)(2,1)S(1)} %get-tuple-element.70), channel_id=1, source_target_pairs={{0,1},{1,0},{2,3},{3,2},{4,5},{5,4},{6,7},{7,6},{8,9},{9,8},{10,11... | collective-permute-start | bytes 196616 | tf_op jit(solution)/shard_map/ppermute | solution.py:523
  43.5 5.5 %collective-permute-start.24 = (bf16[256,128]{1,0:T(8,128)(2,1)S(1)}, bf16[256,128]{1,0:T(8,128)(2,1)S(1)}, u32[]{:S(2)}, u32[]{:S(2)}) collective-permute-start(bf16[256,128]{1,0:T(8,128)(2,1)S(1)} %get-tuple-element.71), channel_id=1, source_target_pairs={{0,2},{1,3},{2,0},{3,1},{4,6},{5,7},{6,4},{7,5},{8,10},{9,11},{10,... | collective-permute-start | bytes 196616 | tf_op jit(solution)/shard_map/ppermute | solution.py:523
  45.3 4.5 %collective-permute-start.25 = (bf16[256,128]{1,0:T(8,128)(2,1)S(1)}, bf16[256,128]{1,0:T(8,128)(2,1)S(1)}, u32[]{:S(2)}, u32[]{:S(2)}) collective-permute-start(bf16[256,128]{1,0:T(8,128)(2,1)S(1)} %get-tuple-element.72), channel_id=1, source_target_pairs={{0,3},{1,2},{2,1},{3,0},{4,7},{5,6},{6,5},{7,4},{8,11},{9,10},{10,... | collective-permute-start | bytes 196616 | tf_op jit(solution)/shard_map/ppermute | solution.py:523

commit v12 on v11

--- a/solution.py
+++ b/solution.py
@@ -35,6 +35,8 @@
 
 
 def inverse_count(block, length):
+    if 0 < block < length // LANES - 1:
+        return 1.0 / (2 * HALF + 1)
     position = lax.broadcasted_iota(jnp.int32, (1, LANES), 1) + block * LANES
     counted = jnp.minimum(position, HALF) + jnp.minimum(length - 1 - position, HALF) + 1
     return 1.0 / counted.astype(F32)
@@ -76,20 +78,19 @@
 
 
 def banded_sum(stack, values, band):
-    rows, length = values.shape
-    blocks = length // LANES
+    blocks, rows = len(values), values[0].shape[0]
     zero = jnp.zeros((rows, LANES), BF)
     for j in range(blocks):
         at = pl.ds(j * rows, rows)
         for k in range(3):
             b = j + k - 1
-            block = values[:, b * LANES : (b + 1) * LANES] if 0 <= b < blocks else zero
+            block = values[b] if 0 <= b < blocks else zero
             stack[at, k * LANES : (k + 1) * LANES] = block
     total = jnp.dot(stack[: blocks * rows, :], band, preferred_element_type=F32)
     return [total[j * rows : (j + 1) * rows, :] for j in range(blocks)]
 
 
-def prep_kernel(parts, records_hbm, table_hbm, white, mine, *rest):
+def prep_kernel(parts, windows, records_hbm, table_hbm, white, mine, *rest):
     others = rest[: parts - 1]
     records, table, stack, flat, spread, sems = rest[parts - 1 :]
     records_copy = pltpu.make_async_copy(records_hbm, records, sems.at[0])
@@ -98,15 +99,26 @@
     copy.start()
     band_values = band_matrix()
     records_copy.wait()
-    stations, windows, length = records.shape
+    stations = white.shape[1]
     rows = stations * windows
+    blocks = records.shape[0] // rows
+    length = blocks * LANES
     chunk = length // CHUNKS
-    signal = jnp.concatenate([records[:, w, :] for w in range(windows)], axis=0)
-    sums = banded_sum(stack, jnp.abs(signal).astype(BF), band_values)
+    signal = [
+        jnp.concatenate(
+            [
+                records[pl.ds(j * windows + w, stations, stride=blocks * windows), :]
+                for w in range(windows)
+            ],
+            axis=0,
+        )
+        for j in range(blocks)
+    ]
+    sums = banded_sum(stack, [jnp.abs(block).astype(BF) for block in signal], band_values)
     for j, total in enumerate(sums):
         at = slice(j * LANES, (j + 1) * LANES)
         level = total * inverse_count(j, length)
-        value = (signal[:, at] / (level + 1e-05)).astype(BF)
+        value = (signal[j] / (level + 1e-05)).astype(BF)
         q, inside = divmod(j * LANES, chunk)
         flat[q * rows : (q + 1) * rows, inside : inside + LANES] = value
     copy.wait()
@@ -131,12 +143,12 @@
         reals.append(real)
         imags.append(imag)
         mags.append(jnp.sqrt(real * real + imag * imag).astype(BF))
-    sums = banded_sum(stack, jnp.concatenate(mags, axis=1), band_values)
+    sums = banded_sum(stack, mags, band_values)
     for j, total in enumerate(sums):
         at = slice(j * LANES, (j + 1) * LANES)
-        smooth = total * inverse_count(j, NBIN) + 1e-06
-        spread[pl.ds(j, rows, stride=2 * TILES), :] = reals[j] / smooth
-        spread[pl.ds(TILES + j, rows, stride=2 * TILES), :] = imags[j] / smooth
+        inverse = 1.0 / (total * inverse_count(j, NBIN) + 1e-06)
+        spread[pl.ds(j, rows, stride=2 * TILES), :] = reals[j] * inverse
+        spread[pl.ds(TILES + j, rows, stride=2 * TILES), :] = imags[j] * inverse
     me = lax.axis_index("seg")
     quarter = stations // parts
     white[...] = spread[...].reshape(windows, stations, 2 * TILES, LANES).astype(BF)
@@ -149,16 +161,19 @@
     stations, windows, length = records.shape
     rows = stations * windows
     quarter = stations // parts
+    blocks = length // LANES
+    flat_records = records.reshape(stations, windows, blocks, LANES).transpose(0, 2, 1, 3)
+    flat_records = flat_records.reshape(rows * blocks, LANES)
     small = jax.ShapeDtypeStruct((windows, quarter, 2 * TILES, LANES), BF)
     vmem = pl.BlockSpec(memory_space=pltpu.VMEM)
     return pl.pallas_call(
-        functools.partial(prep_kernel, parts),
+        functools.partial(prep_kernel, parts, windows),
         out_shape=[jax.ShapeDtypeStruct((windows, stations, 2 * TILES, LANES), BF)]
         + [small] * parts,
         in_specs=[pl.BlockSpec(memory_space=pltpu.HBM)] * 2,
         out_specs=[vmem] * (1 + parts),
         scratch_shapes=[
-            pltpu.VMEM(records.shape, F32),
+            pltpu.VMEM(flat_records.shape, F32),
             pltpu.VMEM(table.shape, BF),
             pltpu.VMEM((rows * (length // LANES), 3 * LANES), BF),
             pltpu.VMEM((CHUNKS * rows, length // CHUNKS), BF),
@@ -171,7 +186,7 @@
         ),
         name="prep",
     )(
-        pltpu.with_memory_space_constraint(records, pltpu.HBM),
+        pltpu.with_memory_space_constraint(flat_records, pltpu.HBM),
         pltpu.with_memory_space_constraint(table, pltpu.HBM),
     )
 

time: 51.6 us -> 51.6 us (level)
  no operation moved by 1% of the time
where the time goes in v12:
time: 51.6 us; the launch traced here: 51.5 us
  starting transfers between devices  22.6 us (44%)
  Pallas kernels  17.5 us (34%)
  waiting for transfers between devices  11.2 us (22%)
    ppermute x15, starting transfers between devices, swap(): return lax.ppermute(value, 'seg', [(i, i ^ j) for i in range(parts)])  10.8 us
    pallas_call x3, Pallas kernels, cross_lags(): pl.pallas_call(functools.partial(cross_kernel, first_slot, slots, count,...  10.4 us
    ppermute x6, waiting for transfers between devices, up(): return lax.ppermute(value, 'sta', upward)  6.65 us
    ppermute x5, starting transfers between devices, down(): return lax.ppermute(value, 'sta', downward)  6.51 us
    ppermute x6, starting transfers between devices, up(): return lax.ppermute(value, 'sta', upward)  5.28 us
    ppermute x15, waiting for transfers between devices, swap(): return lax.ppermute(value, 'seg', [(i, i ^ j) for i in range(parts)])  3.98 us
    pallas_call x1, Pallas kernels, prepare(): pl.pallas_call(functools.partial(prep_kernel, parts, windows), out_shape=...  3.04 us
    pallas_call x1, Pallas kernels, place_lags(): pl.pallas_call(functools.partial(early_kernel, count, parts, tuple(groups...  2.14 us
  transfers between devices with their start and end apart: 26, of which 11 were waited for; matrix products, arithmetic and copies ran while one was open for 0% of the time, Pallas kernels for 25%

profile of v12, /device:TPU:0, one launch (start us, length us, event | category | flops | bytes accessed | tf_op | source)
XLA Modules:
  0.0 51.5 jit_solution(9670575221847146946)
XLA Ops:
  0.0 3.0 %prep.1 = (bf16[4,16,16,128]{3,2,1,0:T(8,128)(2,1)S(1)}, bf16[4,4,16,128]{3,2,1,0:T(8,128)(2,1)S(1)}, bf16[4,4,16,128]{3,2,1,0:T(8,128)(2,1)S(1)}, bf16[4,4,16,1...) custom-call(f32[1024,128]{1,0:T(8,128)} %bitcast.10, bf16[512,2048]{1,0:T(8,128)(2,1)} %constant.4.clone.table_hbm.table), custom_call_target="tpu_custom_call" | custom-call | flops 536870912 | bytes 3145728 | tf_op jit(solution)/shard_map/prep/pallas_call | solution.py:169
  3.0 0.5 %collective-permute-start = (bf16[4,4,16,128]{3,2,1,0:T(8,128)(2,1)S(1)}, bf16[4,4,16,128]{3,2,1,0:T(8,128)(2,1)S(1)}, u32[]{:S(2)}, u32[]{:S(2)}) collective-permute-start(bf16[4,4,16,128]{3,2,1,0:T(8,128)(2,1)S(1)} %get-tuple-element.40), channel_id=1, source_target_pairs={{0,1},{1,0},{2,3},{3,2},{4,5},{5,4},{6,7},{7,6},{8,9},{9,8},{10,11... | collective-permute-start | bytes 196616 | tf_op jit(solution)/shard_map/ppermute | solution.py:538
  3.6 2.6 %collective-permute-start.6 = (bf16[4,4,16,128]{3,2,1,0:T(8,128)(2,1)S(1)}, bf16[4,4,16,128]{3,2,1,0:T(8,128)(2,1)S(1)}, u32[]{:S(2)}, u32[]{:S(2)}) collective-permute-start(bf16[4,4,16,128]{3,2,1,0:T(8,128)(2,1)S(1)} %get-tuple-element.45), channel_id=1, source_target_pairs={{0,2},{1,3},{2,0},{3,1},{4,6},{5,7},{6,4},{7,5},{8,10},{9,11},{10,... | collective-permute-start | bytes 196616 | tf_op jit(solution)/shard_map/ppermute | solution.py:538
  6.4 2.0 %collective-permute-start.2 = (bf16[8,4,16,128]{3,2,1,0:T(8,128)(2,1)S(1)}, bf16[8,4,16,128]{3,2,1,0:T(8,128)(2,1)S(1)}, u32[]{:S(2)}, u32[]{:S(2)}) collective-permute-start(bf16[8,4,16,128]{3,2,1,0:T(8,128)(2,1)S(1)} %constant_dynamic-update-slice_fusion), channel_id=1, source_target_pairs={{0,4},{8,0},{16,8},{24,16},{28,24},{20,28},{12,20},{4,12},{1,5},{9... | collective-permute-start | bytes 393224 | tf_op jit(solution)/shard_map/ppermute | solution.py:573
  8.5 0.3 collective-permute-done.6
  8.8 1.4 %collective-permute-done.7 = bf16[4,4,16,128]{3,2,1,0:T(8,128)(2,1)S(1)} collective-permute-done((bf16[4,4,16,128]{3,2,1,0:T(8,128)(2,1)S(1)}, bf16[4,4,16,128]{3,2,1,0:T(8,128)(2,1)S(1)}, u32[]{:S(2)}, u32[]{:S(2)}) %collective-permute-start.7) | collective-permute-done | bytes 65568 | tf_op jit(solution)/shard_map/ppermute | solution.py:538
  10.2 1.6 %collective-permute-start.9 = (bf16[8,4,16,128]{3,2,1,0:T(8,128)(2,1)S(1)}, bf16[8,4,16,128]{3,2,1,0:T(8,128)(2,1)S(1)}, u32[]{:S(2)}, u32[]{:S(2)}) collective-permute-start(bf16[8,4,16,128]{3,2,1,0:T(8,128)(2,1)S(1)} %pad_maximum_fusion), channel_id=1, source_target_pairs={{0,4},{8,0},{16,8},{24,16},{28,24},{20,28},{12,20},{4,12},{1,5},{9... | collective-permute-start | bytes 393224 | tf_op jit(solution)/shard_map/ppermute | solution.py:573
  11.8 0.5 collective-permute-start.8
  12.3 1.3 %collective-permute-start.12 = (bf16[4,16,16,128]{3,2,1,0:T(8,128)(2,1)S(1)}, bf16[4,16,16,128]{3,2,1,0:T(8,128)(2,1)S(1)}, u32[]{:S(2)}, u32[]{:S(2)}) collective-permute-start(bf16[4,16,16,128]{3,2,1,0:T(8,128)(2,1)S(1)} %get-tuple-element.54.refs_0_), channel_id=1, source_target_pairs={{0,2},{1,3},{2,0},{3,1},{4,6},{5,7},{6,4},{7,5},{8,10},{9,11},{10,... | collective-permute-start | bytes 786440 | tf_op jit(solution)/shard_map/ppermute | solution.py:538
  13.8 1.6 %collective-permute-start.4 = (bf16[8,4,16,128]{3,2,1,0:T(8,128)(2,1)S(1)}, bf16[8,4,16,128]{3,2,1,0:T(8,128)(2,1)S(1)}, u32[]{:S(2)}, u32[]{:S(2)}) collective-permute-start(bf16[8,4,16,128]{3,2,1,0:T(8,128)(2,1)S(1)} %collective-permute-done.1.rest_2_), channel_id=1, source_target_pairs={{0,8},{8,16},{16,24},{24,28},{28,20},{20,12},{12,4},{4,0},{1,9},{9... | collective-permute-start | bytes 393224 | tf_op jit(solution)/shard_map/ppermute | solution.py:570
  15.4 0.4 collective-permute-start.5
  15.9 0.3 collective-permute-done.9.rest_5_
  16.1 2.0 %collective-permute-done.8.rest_4_ = bf16[8,4,16,128]{3,2,1,0:T(8,128)(2,1)S(1)} collective-permute-done((bf16[8,4,16,128]{3,2,1,0:T(8,128)(2,1)S(1)}, bf16[8,4,16,128]{3,2,1,0:T(8,128)(2,1)S(1)}, u32[]{:S(2)}, u32[]{:S(2)}) %collective-permute-start.8) | collective-permute-done | bytes 131104 | tf_op jit(solution)/shard_map/ppermute | solution.py:570
  18.1 2.0 %collective-permute-start.11 = (bf16[8,4,16,128]{3,2,1,0:T(8,128)(2,1)S(1)}, bf16[8,4,16,128]{3,2,1,0:T(8,128)(2,1)S(1)}, u32[]{:S(2)}, u32[]{:S(2)}) collective-permute-start(bf16[8,4,16,128]{3,2,1,0:T(8,128)(2,1)S(1)} %collective-permute-done.9.rest_5_), channel_id=1, source_target_pairs={{0,4},{8,0},{16,8},{24,16},{28,24},{20,28},{12,20},{4,12},{1,5},{9... | collective-permute-start | bytes 393224 | tf_op jit(solution)/shard_map/ppermute | solution.py:573
  20.2 0.8 %collective-permute-done.4.refs_0_.rest_6_ = bf16[8,4,16,128]{3,2,1,0:T(8,128)(2,1)S(1)} collective-permute-done((bf16[8,4,16,128]{3,2,1,0:T(8,128)(2,1)S(1)}, bf16[8,4,16,128]{3,2,1,0:T(8,128)(2,1)S(1)}, u32[]{:S(2)}, u32[]{:S(2)}) %collective-permute-start.4) | collective-permute-done | bytes 131104 | tf_op jit(solution)/shard_map/ppermute | solution.py:570
  20.9 0.2 collective-permute-done.5.refs_1_.rest_7_
  21.1 2.0 %collective-permute-done.10.refs_2_.rest_8_ = bf16[8,4,16,128]{3,2,1,0:T(8,128)(2,1)S(1)} collective-permute-done((bf16[8,4,16,128]{3,2,1,0:T(8,128)(2,1)S(1)}, bf16[8,4,16,128]{3,2,1,0:T(8,128)(2,1)S(1)}, u32[]{:S(2)}, u32[]{:S(2)}) %collective-permute-start.10) | collective-permute-done | bytes 131104 | tf_op jit(solution)/shard_map/ppermute | solution.py:570
  23.3 1.6 %collective-permute-start.17 = (bf16[16,4,16,128]{3,2,1,0:T(8,128)(2,1)S(1)}, bf16[16,4,16,128]{3,2,1,0:T(8,128)(2,1)S(1)}, u32[]{:S(2)}, u32[]{:S(2)}) collective-permute-start(bf16[16,4,16,128]{3,2,1,0:T(8,128)(2,1)S(1)} %get-tuple-element.61), channel_id=1, source_target_pairs={{0,8},{8,16},{16,24},{24,28},{28,20},{20,12},{12,4},{4,0},{1,9},{9... | collective-permute-start | bytes 786440 | tf_op jit(solution)/shard_map/ppermute | solution.py:570
  25.0 0.5 collective-permute-start.18
  25.6 2.8 %cross.3 = (bf16[256,128]{1,0:T(8,128)(2,1)S(1)}, bf16[256,128]{1,0:T(8,128)(2,1)S(1)}, bf16[256,128]{1,0:T(8,128)(2,1)S(1)}, bf16[256,128]{1,0:T(8,128)(2,1)S(1)}) custom-call(s32[4,8]{1,0:T(4,128)S(1)} %copy-done.2, bf16[512,2048]{1,0:T(8,128)(2,1)S(1)} %copy-done, f32[4,3,8,4,8,128]{5,4,3,2,1,0:T(8,128)S(1)} %widen.2.rest_0_, ...), custom_call_target="tpu_custom_call" | custom-call | flops 2990000128 | bytes 1024 | tf_op jit(solution)/shard_map/cross/pallas_call | solution.py:374
  28.5 1.8 %collective-permute-start.15 = (bf16[256,128]{1,0:T(8,128)(2,1)S(1)}, bf16[256,128]{1,0:T(8,128)(2,1)S(1)}, u32[]{:S(2)}, u32[]{:S(2)}) collective-permute-start(bf16[256,128]{1,0:T(8,128)(2,1)S(1)} %get-tuple-element.58), channel_id=1, source_target_pairs={{0,2},{1,3},{2,0},{3,1},{4,6},{5,7},{6,4},{7,5},{8,10},{9,11},{10,... | collective-permute-start | bytes 196616 | tf_op jit(solution)/shard_map/ppermute | solution.py:538
  30.3 1.9 %collective-permute-done.17.rest_10_ = bf16[16,4,16,128]{3,2,1,0:T(8,128)(2,1)S(1)} collective-permute-done((bf16[16,4,16,128]{3,2,1,0:T(8,128)(2,1)S(1)}, bf16[16,4,16,128]{3,2,1,0:T(8,128)(2,1)S(1)}, u32[]{:S(2)}, u32[]{:S(2)}) %collective-permute-start.17) | collective-permute-done | bytes 262176 | tf_op jit(solution)/shard_map/ppermute | solution.py:570
  32.2 1.4 %collective-permute-start.22 = (bf16[16,4,16,128]{3,2,1,0:T(8,128)(2,1)S(1)}, bf16[16,4,16,128]{3,2,1,0:T(8,128)(2,1)S(1)}, u32[]{:S(2)}, u32[]{:S(2)}) collective-permute-start(bf16[16,4,16,128]{3,2,1,0:T(8,128)(2,1)S(1)} %collective-permute-done.17.rest_10_), channel_id=1, source_target_pairs={{0,8},{8,16},{16,24},{24,28},{28,20},{20,12},{12,4},{4,0},{1,9},{9... | collective-permute-start | bytes 786440 | tf_op jit(solution)/shard_map/ppermute | solution.py:570
  33.6 4.7 %cross.4 = (bf16[512,128]{1,0:T(8,128)(2,1)S(1)}, bf16[512,128]{1,0:T(8,128)(2,1)S(1)}, bf16[512,128]{1,0:T(8,128)(2,1)S(1)}, bf16[512,128]{1,0:T(8,128)(2,1)S(1)}) custom-call(s32[4,8]{1,0:T(4,128)S(1)} %copy-done.2, bf16[512,2048]{1,0:T(8,128)(2,1)S(1)} %copy-done, f32[4,3,8,4,8,128]{5,4,3,2,1,0:T(8,128)S(1)} %widen.2.rest_0_, ...), custom_call_target="tpu_custom_call" | custom-call | flops 5289999872 | bytes 1024 | tf_op jit(solution)/shard_map/cross/pallas_call | solution.py:374
  38.4 1.8 %collective-permute-start.20 = (bf16[512,128]{1,0:T(8,128)(2,1)S(1)}, bf16[512,128]{1,0:T(8,128)(2,1)S(1)}, u32[]{:S(2)}, u32[]{:S(2)}) collective-permute-start(bf16[512,128]{1,0:T(8,128)(2,1)S(1)} %get-tuple-element.65), channel_id=1, source_target_pairs={{0,2},{1,3},{2,0},{3,1},{4,6},{5,7},{6,4},{7,5},{8,10},{9,11},{10,... | collective-permute-start | bytes 393224 | tf_op jit(solution)/shard_map/ppermute | solution.py:538
  40.4 2.9 %cross.5 = (bf16[256,128]{1,0:T(8,128)(2,1)S(1)}, bf16[256,128]{1,0:T(8,128)(2,1)S(1)}, bf16[256,128]{1,0:T(8,128)(2,1)S(1)}, bf16[256,128]{1,0:T(8,128)(2,1)S(1)}) custom-call(s32[4,8]{1,0:T(4,128)S(1)} %copy-done.2, bf16[512,2048]{1,0:T(8,128)(2,1)S(1)} %copy-done, f32[4,3,8,4,8,128]{5,4,3,2,1,0:T(8,128)S(1)} %widen.2.rest_0_, ...), custom_call_target="tpu_custom_call" | custom-call | flops 2990000128 | bytes 1024 | tf_op jit(solution)/shard_map/cross/pallas_call | solution.py:374
  43.2 0.3 collective-permute-start.23
  43.6 1.8 %collective-permute-start.24 = (bf16[256,128]{1,0:T(8,128)(2,1)S(1)}, bf16[256,128]{1,0:T(8,128)(2,1)S(1)}, u32[]{:S(2)}, u32[]{:S(2)}) collective-permute-start(bf16[256,128]{1,0:T(8,128)(2,1)S(1)} %get-tuple-element.71), channel_id=1, source_target_pairs={{0,2},{1,3},{2,0},{3,1},{4,6},{5,7},{6,4},{7,5},{8,10},{9,11},{10,... | collective-permute-start | bytes 196616 | tf_op jit(solution)/shard_map/ppermute | solution.py:538
  45.4 1.5 %collective-permute-done.21.rest_7_ = bf16[512,128]{1,0:T(8,128)(2,1)S(1)} collective-permute-done((bf16[512,128]{1,0:T(8,128)(2,1)S(1)}, bf16[512,128]{1,0:T(8,128)(2,1)S(1)}, u32[]{:S(2)}, u32[]{:S(2)}) %collective-permute-start.21) | collective-permute-done | bytes 131104 | tf_op jit(solution)/shard_map/ppermute | solution.py:538
  46.9 2.1 %early.1 = f32[1024,4,1,128]{3,2,1,0:T(1,128)} custom-call(s32[4,8]{1,0:T(4,128)S(1)} %copy-done.2, bf16[4,128,512]{2,1,0:T(8,128)(2,1)S(1)} %copy-done.1, bf16[256,128]{1,0:T(8,128)(2,1)S(1)} %get-tuple-element.56.rest_0_, bf16[256,128]{1,0:T(8,128)(2,1)S(1)} %collective-permute-done.14.rest_1_, bf16[256,128]{1,0:T(8,128)(2,1)S(1)} %collective-permute-done.15.rest_2_, ...), custom_call_target="tpu_custom_call" | custom-call | flops 57500000 | bytes 1024 | tf_op jit(solution)/shard_map/early/pallas_call | solution.py:484
  49.1 0.8 %collective-permute-done.25.rest_3_ = bf16[256,128]{1,0:T(8,128)(2,1)S(1)} collective-permute-done((bf16[256,128]{1,0:T(8,128)(2,1)S(1)}, bf16[256,128]{1,0:T(8,128)(2,1)S(1)}, u32[]{:S(2)}, u32[]{:S(2)}) %collective-permute-start.25) | collective-permute-done | bytes 65568 | tf_op jit(solution)/shard_map/ppermute | solution.py:538
  49.8 1.7 %late.1 = f32[1024,4,1,128]{3,2,1,0:T(1,128)} custom-call(s32[4,8]{1,0:T(4,128)S(1)} %copy-done.2, bf16[4,128,512]{2,1,0:T(8,128)(2,1)S(1)} %copy-done.1, f32[1024,4,1,128]{3,2,1,0:T(1,128)} %early.1, bf16[256,128]{1,0:T(8,128)(2,1)S(1)} %get-tuple-element.69.rest_0_, ...), custom_call_target="tpu_custom_call", output_to_operand_aliasing={{}: (2, {})} | custom-call | flops 57500000 | bytes 1024 | tf_op jit(solution)/shard_map/late/pallas_call | solution.py:497
  (38 shorter events, 1.2 us)
Async XLA Ops:
  3.0 3.3 %collective-permute-start = (bf16[4,4,16,128]{3,2,1,0:T(8,128)(2,1)S(1)}, bf16[4,4,16,128]{3,2,1,0:T(8,128)(2,1)S(1)}, u32[]{:S(2)}, u32[]{:S(2)}) collective-permute-start(bf16[4,4,16,128]{3,2,1,0:T(8,128)(2,1)S(1)} %get-tuple-element.40), channel_id=1, source_target_pairs={{0,1},{1,0},{2,3},{3,2},{4,5},{5,4},{6,7},{7,6},{8,9},{9,8},{10,11... | collective-permute-start | bytes 196616 | tf_op jit(solution)/shard_map/ppermute | solution.py:538
  3.6 5.3 %collective-permute-start.6 = (bf16[4,4,16,128]{3,2,1,0:T(8,128)(2,1)S(1)}, bf16[4,4,16,128]{3,2,1,0:T(8,128)(2,1)S(1)}, u32[]{:S(2)}, u32[]{:S(2)}) collective-permute-start(bf16[4,4,16,128]{3,2,1,0:T(8,128)(2,1)S(1)} %get-tuple-element.45), channel_id=1, source_target_pairs={{0,2},{1,3},{2,0},{3,1},{4,6},{5,7},{6,4},{7,5},{8,10},{9,11},{10,... | collective-permute-start | bytes 196616 | tf_op jit(solution)/shard_map/ppermute | solution.py:538
  6.1 4.0 %collective-permute-start.7 = (bf16[4,4,16,128]{3,2,1,0:T(8,128)(2,1)S(1)}, bf16[4,4,16,128]{3,2,1,0:T(8,128)(2,1)S(1)}, u32[]{:S(2)}, u32[]{:S(2)}) collective-permute-start(bf16[4,4,16,128]{3,2,1,0:T(8,128)(2,1)S(1)} %get-tuple-element.46), channel_id=1, source_target_pairs={{0,3},{1,2},{2,1},{3,0},{4,7},{5,6},{6,5},{7,4},{8,11},{9,10},{10,... | collective-permute-start | bytes 196616 | tf_op jit(solution)/shard_map/ppermute | solution.py:538
  6.2 4.0 %collective-permute-start.3 = (bf16[4,16,16,128]{3,2,1,0:T(8,128)(2,1)S(1)}, bf16[4,16,16,128]{3,2,1,0:T(8,128)(2,1)S(1)}, u32[]{:S(2)}, u32[]{:S(2)}) collective-permute-start(bf16[4,16,16,128]{3,2,1,0:T(8,128)(2,1)S(1)} %get-tuple-element.54.refs_0_), channel_id=1, source_target_pairs={{0,1},{1,0},{2,3},{3,2},{4,5},{5,4},{6,7},{7,6},{8,9},{9,8},{10,11... | collective-permute-start | bytes 786440 | tf_op jit(solution)/shard_map/ppermute | solution.py:538
  6.4 7.4 %collective-permute-start.2 = (bf16[8,4,16,128]{3,2,1,0:T(8,128)(2,1)S(1)}, bf16[8,4,16,128]{3,2,1,0:T(8,128)(2,1)S(1)}, u32[]{:S(2)}, u32[]{:S(2)}) collective-permute-start(bf16[8,4,16,128]{3,2,1,0:T(8,128)(2,1)S(1)} %constant_dynamic-update-slice_fusion), channel_id=1, source_target_pairs={{0,4},{8,0},{16,8},{24,16},{28,24},{20,28},{12,20},{4,12},{1,5},{9... | collective-permute-start | bytes 393224 | tf_op jit(solution)/shard_map/ppermute | solution.py:573
  8.4 5.4 %collective-permute-start.1 = (bf16[8,4,16,128]{3,2,1,0:T(8,128)(2,1)S(1)}, bf16[8,4,16,128]{3,2,1,0:T(8,128)(2,1)S(1)}, u32[]{:S(2)}, u32[]{:S(2)}) collective-permute-start(bf16[8,4,16,128]{3,2,1,0:T(8,128)(2,1)S(1)} %constant_dynamic-update-slice_fusion), channel_id=1, source_target_pairs={{0,8},{8,16},{16,24},{24,28},{28,20},{20,12},{12,4},{4,0},{1,9},{9... | collective-permute-start | bytes 393224 | tf_op jit(solution)/shard_map/ppermute | solution.py:570
  10.2 15.4 %copy-start = (bf16[512,2048]{1,0:T(8,128)(2,1)S(1)}, bf16[512,2048]{1,0:T(8,128)(2,1)}, u32[]{:S(2)}) copy-start(bf16[512,2048]{1,0:T(8,128)(2,1)} %constant.4.clone.table_hbm.table) | copy-start | bytes 6291460
  10.2 15.4 %copy-start.2 = (s32[4,8]{1,0:T(4,128)S(1)}, s32[4,8]{1,0:T(4,128)}, u32[]{:S(2)}) copy-start(s32[4,8]{1,0:T(4,128)} %plan.9) | copy-start | bytes 388
  10.2 5.9 %collective-permute-start.9 = (bf16[8,4,16,128]{3,2,1,0:T(8,128)(2,1)S(1)}, bf16[8,4,16,128]{3,2,1,0:T(8,128)(2,1)S(1)}, u32[]{:S(2)}, u32[]{:S(2)}) collective-permute-start(bf16[8,4,16,128]{3,2,1,0:T(8,128)(2,1)S(1)} %pad_maximum_fusion), channel_id=1, source_target_pairs={{0,4},{8,0},{16,8},{24,16},{28,24},{20,28},{12,20},{4,12},{1,5},{9... | collective-permute-start | bytes 393224 | tf_op jit(solution)/shard_map/ppermute | solution.py:573
  11.8 6.3 %collective-permute-start.8 = (bf16[8,4,16,128]{3,2,1,0:T(8,128)(2,1)S(1)}, bf16[8,4,16,128]{3,2,1,0:T(8,128)(2,1)S(1)}, u32[]{:S(2)}, u32[]{:S(2)}) collective-permute-start(bf16[8,4,16,128]{3,2,1,0:T(8,128)(2,1)S(1)} %pad_maximum_fusion), channel_id=1, source_target_pairs={{0,8},{8,16},{16,24},{24,28},{28,20},{20,12},{12,4},{4,0},{1,9},{9... | collective-permute-start | bytes 393224 | tf_op jit(solution)/shard_map/ppermute | solution.py:570
  12.3 10.9 %collective-permute-start.12 = (bf16[4,16,16,128]{3,2,1,0:T(8,128)(2,1)S(1)}, bf16[4,16,16,128]{3,2,1,0:T(8,128)(2,1)S(1)}, u32[]{:S(2)}, u32[]{:S(2)}) collective-permute-start(bf16[4,16,16,128]{3,2,1,0:T(8,128)(2,1)S(1)} %get-tuple-element.54.refs_0_), channel_id=1, source_target_pairs={{0,2},{1,3},{2,0},{3,1},{4,6},{5,7},{6,4},{7,5},{8,10},{9,11},{10,... | collective-permute-start | bytes 786440 | tf_op jit(solution)/shard_map/ppermute | solution.py:538
  13.8 7.1 %collective-permute-start.4 = (bf16[8,4,16,128]{3,2,1,0:T(8,128)(2,1)S(1)}, bf16[8,4,16,128]{3,2,1,0:T(8,128)(2,1)S(1)}, u32[]{:S(2)}, u32[]{:S(2)}) collective-permute-start(bf16[8,4,16,128]{3,2,1,0:T(8,128)(2,1)S(1)} %collective-permute-done.1.rest_2_), channel_id=1, source_target_pairs={{0,8},{8,16},{16,24},{24,28},{28,20},{20,12},{12,4},{4,0},{1,9},{9... | collective-permute-start | bytes 393224 | tf_op jit(solution)/shard_map/ppermute | solution.py:570
  15.4 5.7 %collective-permute-start.5 = (bf16[8,4,16,128]{3,2,1,0:T(8,128)(2,1)S(1)}, bf16[8,4,16,128]{3,2,1,0:T(8,128)(2,1)S(1)}, u32[]{:S(2)}, u32[]{:S(2)}) collective-permute-start(bf16[8,4,16,128]{3,2,1,0:T(8,128)(2,1)S(1)} %collective-permute-done.2.rest_3_), channel_id=1, source_target_pairs={{0,4},{8,0},{16,8},{24,16},{28,24},{20,28},{12,20},{4,12},{1,5},{9... | collective-permute-start | bytes 393224 | tf_op jit(solution)/shard_map/ppermute | solution.py:573
  18.1 5.0 %collective-permute-start.10 = (bf16[8,4,16,128]{3,2,1,0:T(8,128)(2,1)S(1)}, bf16[8,4,16,128]{3,2,1,0:T(8,128)(2,1)S(1)}, u32[]{:S(2)}, u32[]{:S(2)}) collective-permute-start(bf16[8,4,16,128]{3,2,1,0:T(8,128)(2,1)S(1)} %collective-permute-done.8.rest_4_), channel_id=1, source_target_pairs={{0,8},{8,16},{16,24},{24,28},{28,20},{20,12},{12,4},{4,0},{1,9},{9... | collective-permute-start | bytes 393224 | tf_op jit(solution)/shard_map/ppermute | solution.py:570
  18.1 5.1 %collective-permute-start.11 = (bf16[8,4,16,128]{3,2,1,0:T(8,128)(2,1)S(1)}, bf16[8,4,16,128]{3,2,1,0:T(8,128)(2,1)S(1)}, u32[]{:S(2)}, u32[]{:S(2)}) collective-permute-start(bf16[8,4,16,128]{3,2,1,0:T(8,128)(2,1)S(1)} %collective-permute-done.9.rest_5_), channel_id=1, source_target_pairs={{0,4},{8,0},{16,8},{24,16},{28,24},{20,28},{12,20},{4,12},{1,5},{9... | collective-permute-start | bytes 393224 | tf_op jit(solution)/shard_map/ppermute | solution.py:573
  23.3 2.2 %collective-permute-start.13 = (bf16[4,16,16,128]{3,2,1,0:T(8,128)(2,1)S(1)}, bf16[4,16,16,128]{3,2,1,0:T(8,128)(2,1)S(1)}, u32[]{:S(2)}, u32[]{:S(2)}) collective-permute-start(bf16[4,16,16,128]{3,2,1,0:T(8,128)(2,1)S(1)} %collective-permute-done.12.refs_0_), channel_id=1, source_target_pairs={{0,1},{1,0},{2,3},{3,2},{4,5},{5,4},{6,7},{7,6},{8,9},{9,8},{10,11... | collective-permute-start | bytes 786440 | tf_op jit(solution)/shard_map/ppermute | solution.py:538
  23.3 8.9 %collective-permute-start.17 = (bf16[16,4,16,128]{3,2,1,0:T(8,128)(2,1)S(1)}, bf16[16,4,16,128]{3,2,1,0:T(8,128)(2,1)S(1)}, u32[]{:S(2)}, u32[]{:S(2)}) collective-permute-start(bf16[16,4,16,128]{3,2,1,0:T(8,128)(2,1)S(1)} %get-tuple-element.61), channel_id=1, source_target_pairs={{0,8},{8,16},{16,24},{24,28},{28,20},{20,12},{12,4},{4,0},{1,9},{9... | collective-permute-start | bytes 786440 | tf_op jit(solution)/shard_map/ppermute | solution.py:570
  25.0 8.7 %collective-permute-start.18 = (bf16[16,4,16,128]{3,2,1,0:T(8,128)(2,1)S(1)}, bf16[16,4,16,128]{3,2,1,0:T(8,128)(2,1)S(1)}, u32[]{:S(2)}, u32[]{:S(2)}) collective-permute-start(bf16[16,4,16,128]{3,2,1,0:T(8,128)(2,1)S(1)} %get-tuple-element.62), channel_id=1, source_target_pairs={{0,4},{8,0},{16,8},{24,16},{28,24},{20,28},{12,20},{4,12},{1,5},{9... | collective-permute-start | bytes 786440 | tf_op jit(solution)/shard_map/ppermute | solution.py:573
  28.4 10.1 %collective-permute-start.14 = (bf16[256,128]{1,0:T(8,128)(2,1)S(1)}, bf16[256,128]{1,0:T(8,128)(2,1)S(1)}, u32[]{:S(2)}, u32[]{:S(2)}) collective-permute-start(bf16[256,128]{1,0:T(8,128)(2,1)S(1)} %get-tuple-element.57), channel_id=1, source_target_pairs={{0,1},{1,0},{2,3},{3,2},{4,5},{5,4},{6,7},{7,6},{8,9},{9,8},{10,11... | collective-permute-start | bytes 196616 | tf_op jit(solution)/shard_map/ppermute | solution.py:538
  28.5 11.8 %collective-permute-start.15 = (bf16[256,128]{1,0:T(8,128)(2,1)S(1)}, bf16[256,128]{1,0:T(8,128)(2,1)S(1)}, u32[]{:S(2)}, u32[]{:S(2)}) collective-permute-start(bf16[256,128]{1,0:T(8,128)(2,1)S(1)} %get-tuple-element.58), channel_id=1, source_target_pairs={{0,2},{1,3},{2,0},{3,1},{4,6},{5,7},{6,4},{7,5},{8,10},{9,11},{10,... | collective-permute-start | bytes 196616 | tf_op jit(solution)/shard_map/ppermute | solution.py:538
  30.3 10.1 %collective-permute-start.16 = (bf16[256,128]{1,0:T(8,128)(2,1)S(1)}, bf16[256,128]{1,0:T(8,128)(2,1)S(1)}, u32[]{:S(2)}, u32[]{:S(2)}) collective-permute-start(bf16[256,128]{1,0:T(8,128)(2,1)S(1)} %get-tuple-element.59), channel_id=1, source_target_pairs={{0,3},{1,2},{2,1},{3,0},{4,7},{5,6},{6,5},{7,4},{8,11},{9,10},{10,... | collective-permute-start | bytes 196616 | tf_op jit(solution)/shard_map/ppermute | solution.py:538
  32.2 8.1 %collective-permute-start.22 = (bf16[16,4,16,128]{3,2,1,0:T(8,128)(2,1)S(1)}, bf16[16,4,16,128]{3,2,1,0:T(8,128)(2,1)S(1)}, u32[]{:S(2)}, u32[]{:S(2)}) collective-permute-start(bf16[16,4,16,128]{3,2,1,0:T(8,128)(2,1)S(1)} %collective-permute-done.17.rest_10_), channel_id=1, source_target_pairs={{0,8},{8,16},{16,24},{24,28},{28,20},{20,12},{12,4},{4,0},{1,9},{9... | collective-permute-start | bytes 786440 | tf_op jit(solution)/shard_map/ppermute | solution.py:570
  38.4 7.0 %collective-permute-start.19 = (bf16[512,128]{1,0:T(8,128)(2,1)S(1)}, bf16[512,128]{1,0:T(8,128)(2,1)S(1)}, u32[]{:S(2)}, u32[]{:S(2)}) collective-permute-start(bf16[512,128]{1,0:T(8,128)(2,1)S(1)} %get-tuple-element.64), channel_id=1, source_target_pairs={{0,1},{1,0},{2,3},{3,2},{4,5},{5,4},{6,7},{7,6},{8,9},{9,8},{10,11... | collective-permute-start | bytes 393224 | tf_op jit(solution)/shard_map/ppermute | solution.py:538
  38.4 6.9 %collective-permute-start.20 = (bf16[512,128]{1,0:T(8,128)(2,1)S(1)}, bf16[512,128]{1,0:T(8,128)(2,1)S(1)}, u32[]{:S(2)}, u32[]{:S(2)}) collective-permute-start(bf16[512,128]{1,0:T(8,128)(2,1)S(1)} %get-tuple-element.65), channel_id=1, source_target_pairs={{0,2},{1,3},{2,0},{3,1},{4,6},{5,7},{6,4},{7,5},{8,10},{9,11},{10,... | collective-permute-start | bytes 393224 | tf_op jit(solution)/shard_map/ppermute | solution.py:538
  40.3 6.6 %collective-permute-start.21 = (bf16[512,128]{1,0:T(8,128)(2,1)S(1)}, bf16[512,128]{1,0:T(8,128)(2,1)S(1)}, u32[]{:S(2)}, u32[]{:S(2)}) collective-permute-start(bf16[512,128]{1,0:T(8,128)(2,1)S(1)} %get-tuple-element.66), channel_id=1, source_target_pairs={{0,3},{1,2},{2,1},{3,0},{4,7},{5,6},{6,5},{7,4},{8,11},{9,10},{10,... | collective-permute-start | bytes 393224 | tf_op jit(solution)/shard_map/ppermute | solution.py:538
  40.4 6.5 %copy-start.1 = (bf16[4,128,512]{2,1,0:T(8,128)(2,1)S(1)}, bf16[4,128,512]{2,1,0:T(8,128)(2,1)}, u32[]{:S(2)}) copy-start(bf16[4,128,512]{2,1,0:T(8,128)(2,1)} %constant.5.clone.place) | copy-start | bytes 1572868
  43.2 5.8 %collective-permute-start.23 = (bf16[256,128]{1,0:T(8,128)(2,1)S(1)}, bf16[256,128]{1,0:T(8,128)(2,1)S(1)}, u32[]{:S(2)}, u32[]{:S(2)}) collective-permute-start(bf16[256,128]{1,0:T(8,128)(2,1)S(1)} %get-tuple-element.70), channel_id=1, source_target_pairs={{0,1},{1,0},{2,3},{3,2},{4,5},{5,4},{6,7},{7,6},{8,9},{9,8},{10,11... | collective-permute-start | bytes 196616 | tf_op jit(solution)/shard_map/ppermute | solution.py:538
  43.6 5.5 %collective-permute-start.24 = (bf16[256,128]{1,0:T(8,128)(2,1)S(1)}, bf16[256,128]{1,0:T(8,128)(2,1)S(1)}, u32[]{:S(2)}, u32[]{:S(2)}) collective-permute-start(bf16[256,128]{1,0:T(8,128)(2,1)S(1)} %get-tuple-element.71), channel_id=1, source_target_pairs={{0,2},{1,3},{2,0},{3,1},{4,6},{5,7},{6,4},{7,5},{8,10},{9,11},{10,... | collective-permute-start | bytes 196616 | tf_op jit(solution)/shard_map/ppermute | solution.py:538
  45.4 4.5 %collective-permute-start.25 = (bf16[256,128]{1,0:T(8,128)(2,1)S(1)}, bf16[256,128]{1,0:T(8,128)(2,1)S(1)}, u32[]{:S(2)}, u32[]{:S(2)}) collective-permute-start(bf16[256,128]{1,0:T(8,128)(2,1)S(1)} %get-tuple-element.72), channel_id=1, source_target_pairs={{0,3},{1,2},{2,1},{3,0},{4,7},{5,6},{6,5},{7,4},{8,11},{9,10},{10,... | collective-permute-start | bytes 196616 | tf_op jit(solution)/shard_map/ppermute | solution.py:538

commit v13 on v12

--- a/solution.py
+++ b/solution.py
@@ -92,11 +92,16 @@
 
 def prep_kernel(parts, windows, records_hbm, table_hbm, white, mine, *rest):
     others = rest[: parts - 1]
-    records, table, stack, flat, spread, sems = rest[parts - 1 :]
+    records, table, stack, flat, product, spread, sems = rest[parts - 1 :]
     records_copy = pltpu.make_async_copy(records_hbm, records, sems.at[0])
     records_copy.start()
-    copy = pltpu.make_async_copy(table_hbm, table, sems.at[1])
-    copy.start()
+    width = table.shape[1] // CHUNKS
+    copies = []
+    for q in range(CHUNKS):
+        at = pl.ds(q * width, width)
+        copy = pltpu.make_async_copy(table_hbm.at[:, at], table.at[:, at], sems.at[1 + q])
+        copy.start()
+        copies.append(copy)
     band_values = band_matrix()
     records_copy.wait()
     stations = white.shape[1]
@@ -121,8 +126,10 @@
         value = (signal[j] / (level + 1e-05)).astype(BF)
         q, inside = divmod(j * LANES, chunk)
         flat[q * rows : (q + 1) * rows, inside : inside + LANES] = value
-    copy.wait()
-    product = jnp.dot(flat[...], table[...], preferred_element_type=F32)
+    for q in range(CHUNKS):
+        at = slice(q * width, (q + 1) * width)
+        copies[q].wait()
+        product[:, at] = jnp.dot(flat[...], table[:, at], preferred_element_type=F32)
     even = even_lanes((rows, LANES))
     sign_real = lane_cycle([1.0, 1.0, -1.0, -1.0])
     sign_imag = lane_cycle([1.0, -1.0, -1.0, 1.0])
@@ -177,8 +184,9 @@
             pltpu.VMEM(table.shape, BF),
             pltpu.VMEM((rows * (length // LANES), 3 * LANES), BF),
             pltpu.VMEM((CHUNKS * rows, length // CHUNKS), BF),
+            pltpu.VMEM((CHUNKS * rows, 2 * NBIN), F32),
             pltpu.VMEM((rows * 2 * TILES, LANES), F32),
-            pltpu.SemaphoreType.DMA((2,)),
+            pltpu.SemaphoreType.DMA((1 + CHUNKS,)),
         ],
         compiler_params=pltpu.CompilerParams(vmem_limit_bytes=52 * 2**20),
         cost_estimate=pl.CostEstimate(
@@ -221,42 +229,41 @@
     )
 
 
-def widen_kernel(*refs):
+def turn_kernel(*refs):
     blocks, own = refs[:-1], refs[-1]
     windows = blocks[0].shape[0]
     for j, block in enumerate(blocks):
 
-        def widen(w, carry, j=j, block=block):
-            raw = block[w].astype(F32)
-            real, imag = raw[:, :TILES], raw[:, TILES:]
-            both = real + imag
+        def turn(w, carry, j=j, block=block):
+            plain = block[w]
+            raw = plain.astype(F32)
+            turned = jnp.concatenate([raw[:, TILES:], -raw[:, :TILES]], axis=1).astype(BF)
             for group in range(own.shape[0]):
                 at = slice(group * GROUP, (group + 1) * GROUP)
-                own[group, 0, j * windows + w] = both[at]
-                own[group, 1, j * windows + w] = real[at]
-                own[group, 2, j * windows + w] = imag[at]
+                own[group, 0, j * windows + w] = plain[at]
+                own[group, 1, j * windows + w] = turned[at]
             return carry
 
-        lax.fori_loop(0, windows, widen, 0)
-
-
-def widen_own(blocks):
+        lax.fori_loop(0, windows, turn, 0)
+
+
+def turn_own(blocks):
     windows, stations = blocks[0].shape[:2]
     vmem = pl.BlockSpec(memory_space=pltpu.VMEM)
     return pl.pallas_call(
-        widen_kernel,
+        turn_kernel,
         out_shape=jax.ShapeDtypeStruct(
-            (stations // GROUP, 3, len(blocks) * windows, GROUP, TILES, LANES), F32
+            (stations // GROUP, 2, len(blocks) * windows, GROUP, 2 * TILES, LANES), BF
         ),
         in_specs=[vmem] * len(blocks),
         out_specs=vmem,
         compiler_params=pltpu.CompilerParams(vmem_limit_bytes=16 * 2**20),
         cost_estimate=expected(0.05),
-        name="widen",
+        name="turn",
     )(*blocks)
 
 
-def widen_others(first_slot, slots, count, places, plan, candidates, other):
+def pick_others(first_slot, slots, count, places, plan, candidates, other):
     steps, ranks = partner_steps(plan, count)
     for slot in range(slots):
         step = jnp.int32(0)
@@ -266,58 +273,58 @@
 
             @pl.when(step == offset)
             def _(candidate=candidate, slot=slot, first=first):
-                def widen_other(w, carry):
-                    raw = candidate[w].astype(F32)
-                    real, imag = raw[:, :TILES], raw[:, TILES:]
-                    other[0, slot, first + w] = real
-                    other[1, slot, first + w] = real + imag
-                    other[2, slot, first + w] = imag - real
+                def pick(w, carry):
+                    other[slot, first + w] = candidate[w]
                     return carry
 
-                lax.fori_loop(0, candidate.shape[0], widen_other, 0)
-
-
-def sum_windows(owns, other, summed):
+                lax.fori_loop(0, candidate.shape[0], pick, 0)
+
+
+def sum_windows(owns, other, crossed):
     groups, _, windows, group = owns[0].shape[:4]
-    slots, _, quarter = other.shape[1:4]
+    slots, _, quarter = other.shape[:3]
     width = groups * group * quarter
-    shift = groups.bit_length() - 1
+    size = 2 * TILES
 
     for slot in range(slots):
 
         def body(index, carry, slot=slot):
-            kind, part = index >> shift, index & (groups - 1)
-            mine = [own.at[part, kind] for own in owns]
-            theirs = other.at[kind, slot]
-            totals = [None] * (group * quarter)
-            for half, own in enumerate(mine):
+            base = (slot * width + index * (group * quarter)) * size
+            for half, own in enumerate(owns):
+                mine = own.at[index]
+                totals = [None] * (2 * group * quarter)
                 for w in range(windows):
-                    left = [own[w, s] for s in range(group)]
-                    right = [theirs[half * windows + w, t] for t in range(quarter)]
-                    for s in range(group):
-                        for t in range(quarter):
-                            term = left[s] * right[t]
-                            old = totals[s * quarter + t]
-                            totals[s * quarter + t] = term if old is None else old + term
-            rows = summed.at[kind]
-            base = (slot * width + part * (group * quarter)) * TILES
-            for place in range(group * quarter):
-                at = pl.multiple_of(base + place * TILES, TILES)
-                rows[pl.ds(at, TILES), :] = totals[place]
+                    left = [[mine[kind, w, s] for s in range(group)] for kind in range(2)]
+                    right = [other[slot, half * windows + w, t] for t in range(quarter)]
+                    for kind in range(2):
+                        for s in range(group):
+                            for t in range(quarter):
+                                term = left[kind][s] * right[t]
+                                place = (s * quarter + t) * 2 + kind
+                                old = totals[place]
+                                totals[place] = term if old is None else old + term
+                for place in range(group * quarter):
+                    sums = []
+                    for kind in range(2):
+                        wide = totals[2 * place + kind].astype(F32)
+                        sums.append(wide[:TILES] + wide[TILES:])
+                    at = pl.ds(pl.multiple_of(base + place * size, size), size)
+                    value = jnp.concatenate(sums, axis=0)
+                    crossed[at, :] = value if half == 0 else crossed[at, :] + value
             return carry
 
-        lax.fori_loop(0, 3 * groups, body, 0)
+        lax.fori_loop(0, groups, body, 0)
 
 
 def cross_kernel(first_slot, slots, count, scaling, places, parts, plan, table, *rest):
     owns, rest = rest[:2], rest[2:]
     others, rest = rest[: len(places)], rest[len(places) :]
     outs = rest[:parts]
-    other, summed, operand, result = rest[parts:]
+    other, crossed, operand, result = rest[parts:]
     stations = owns[0].shape[0] * owns[0].shape[3]
-    widen_others(first_slot, slots, count, places, plan, others, other)
-    sum_windows(owns, other, summed)
-    width = stations * other.shape[3]
+    pick_others(first_slot, slots, count, places, plan, others, other)
+    sum_windows(owns, other, crossed)
+    width = stations * other.shape[2]
     columns = slots * width
     even = even_lanes((columns, LANES))
     sign_real = lane_cycle([1.0, -1.0, -1.0, 1.0])
@@ -328,8 +335,8 @@
     for j in range(TILES):
         at = slice(j * LANES, (j + 1) * LANES)
         at_imag = slice(NBIN + j * LANES, NBIN + (j + 1) * LANES)
-        kinds = [summed[kind, pl.ds(j, columns, stride=TILES), :] for kind in range(3)]
-        real, imag = kinds[0] + kinds[2], kinds[0] - kinds[1]
+        real = crossed[pl.ds(j, columns, stride=2 * TILES), :]
+        imag = crossed[pl.ds(TILES + j, columns, stride=2 * TILES), :]
         if j == 0:
             real, imag = real * first_weight, imag * first_weight
         turned = [(real, imag), (real * cosine - imag * sine, imag * cosine + real * sine)]
@@ -379,8 +386,8 @@
         in_specs=[smem] + [vmem] * len(operands),
         out_specs=[vmem] * parts,
         scratch_shapes=[
-            pltpu.VMEM((3, slots, 2 * windows, quarter, TILES, LANES), F32),
-            pltpu.VMEM((3, columns * TILES, LANES), F32),
+            pltpu.VMEM((slots, 2 * windows, quarter, 2 * TILES, LANES), BF),
+            pltpu.VMEM((columns * 2 * TILES, LANES), F32),
             pltpu.VMEM((CHUNKS * columns, 2 * NBIN), BF),
             pltpu.VMEM((parts,) + out, BF),
         ],
@@ -574,7 +581,7 @@
 
     far, white_far = lax.optimization_barrier((far, white))
     across = swap(white_far, 2)
-    near_own = widen_own([white, sibling])
+    near_own = turn_own([white, sibling])
     half = near.shape[0]
     places, blocks, arrived = [], [], []
 
@@ -599,7 +606,7 @@
         all_up, all_down = up(all_up), down(all_down)
         arrive(step, 0, all_up, all_down)
     arrived.append((list(places), list(blocks)))
-    far_own = widen_own([across, swap(across, 1)])
+    far_own = turn_own([across, swap(across, 1)])
     groups = [(0, 1), (1, 2), (3, 1)]
     if count % 2 == 0:
         places.append((count // 2, 0))

time: 51.6 us -> 53.7 us (1.041)
  Pallas kernels: 17.5 us -> 20.3 us
  waiting for transfers between devices: 11.2 us -> 10.4 us
    pallas_call x3, Pallas kernels: 10.4 us -> 12.5 us  [cross_lags(): pl.pallas_call(functools.partial(cross_kernel, first_slot, slots, count,...]
    ppermute x6, waiting for transfers between devices: 6.65 us -> 5.98 us  [up(): return lax.ppermute(value, 'sta', upward)]
    pallas_call x1, Pallas kernels: 3.04 us -> 3.59 us  [prepare(): pl.pallas_call(functools.partial(prep_kernel, parts, windows), out_shape=...]
  transfers between devices with their start and end apart: 26 -> 26, of which waited for: 11 -> 11; matrix products, arithmetic and copies ran while one was open for 0% -> 0% of each run, Pallas kernels for 25% -> 28%
where the time goes in v13:
time: 53.7 us; the launch traced here: 53.5 us
  starting transfers between devices  22.6 us (42%)
  Pallas kernels  20.3 us (38%)
  waiting for transfers between devices  10.4 us (19%)
    pallas_call x3, Pallas kernels, cross_lags(): pl.pallas_call(functools.partial(cross_kernel, first_slot, slots, count,...  12.5 us
    ppermute x15, starting transfers between devices, swap(): return lax.ppermute(value, 'seg', [(i, i ^ j) for i in range(parts)])  10.8 us
    ppermute x5, starting transfers between devices, down(): return lax.ppermute(value, 'sta', downward)  6.5 us
    ppermute x6, waiting for transfers between devices, up(): return lax.ppermute(value, 'sta', upward)  5.98 us
    ppermute x6, starting transfers between devices, up(): return lax.ppermute(value, 'sta', upward)  5.31 us
    ppermute x15, waiting for transfers between devices, swap(): return lax.ppermute(value, 'seg', [(i, i ^ j) for i in range(parts)])  3.83 us
    pallas_call x1, Pallas kernels, prepare(): pl.pallas_call(functools.partial(prep_kernel, parts, windows), out_shape=...  3.59 us
    pallas_call x1, Pallas kernels, place_lags(): pl.pallas_call(functools.partial(early_kernel, count, parts, tuple(groups...  2.14 us
  transfers between devices with their start and end apart: 26, of which 11 were waited for; matrix products, arithmetic and copies ran while one was open for 0% of the time, Pallas kernels for 28%

profile of v13, /device:TPU:0, one launch (start us, length us, event | category | flops | bytes accessed | tf_op | source)
XLA Modules:
  0.0 53.5 jit_solution(9939166445861487041)
XLA Ops:
  0.0 3.6 %prep.1 = (bf16[4,16,16,128]{3,2,1,0:T(8,128)(2,1)S(1)}, bf16[4,4,16,128]{3,2,1,0:T(8,128)(2,1)S(1)}, bf16[4,4,16,128]{3,2,1,0:T(8,128)(2,1)S(1)}, bf16[4,4,16,1...) custom-call(f32[1024,128]{1,0:T(8,128)} %bitcast.10, bf16[512,2048]{1,0:T(8,128)(2,1)} %constant.4.clone.table_hbm.table), custom_call_target="tpu_custom_call" | custom-call | flops 536870912 | bytes 3145728 | tf_op jit(solution)/shard_map/prep/pallas_call | solution.py:176
  3.6 0.5 collective-permute-start
  4.1 2.6 %collective-permute-start.6 = (bf16[4,4,16,128]{3,2,1,0:T(8,128)(2,1)S(1)}, bf16[4,4,16,128]{3,2,1,0:T(8,128)(2,1)S(1)}, u32[]{:S(2)}, u32[]{:S(2)}) collective-permute-start(bf16[4,4,16,128]{3,2,1,0:T(8,128)(2,1)S(1)} %get-tuple-element.45), channel_id=1, source_target_pairs={{0,2},{1,3},{2,0},{3,1},{4,6},{5,7},{6,4},{7,5},{8,10},{9,11},{10,... | collective-permute-start | bytes 196616 | tf_op jit(solution)/shard_map/ppermute | solution.py:545
  6.9 2.0 %collective-permute-start.2 = (bf16[8,4,16,128]{3,2,1,0:T(8,128)(2,1)S(1)}, bf16[8,4,16,128]{3,2,1,0:T(8,128)(2,1)S(1)}, u32[]{:S(2)}, u32[]{:S(2)}) collective-permute-start(bf16[8,4,16,128]{3,2,1,0:T(8,128)(2,1)S(1)} %constant_dynamic-update-slice_fusion), channel_id=1, source_target_pairs={{0,4},{8,0},{16,8},{24,16},{28,24},{20,28},{12,20},{4,12},{1,5},{9... | collective-permute-start | bytes 393224 | tf_op jit(solution)/shard_map/ppermute | solution.py:580
  9.1 0.3 collective-permute-done.6
  9.4 1.4 %collective-permute-done.7 = bf16[4,4,16,128]{3,2,1,0:T(8,128)(2,1)S(1)} collective-permute-done((bf16[4,4,16,128]{3,2,1,0:T(8,128)(2,1)S(1)}, bf16[4,4,16,128]{3,2,1,0:T(8,128)(2,1)S(1)}, u32[]{:S(2)}, u32[]{:S(2)}) %collective-permute-start.7) | collective-permute-done | bytes 65568 | tf_op jit(solution)/shard_map/ppermute | solution.py:545
  10.8 1.6 %collective-permute-start.9 = (bf16[8,4,16,128]{3,2,1,0:T(8,128)(2,1)S(1)}, bf16[8,4,16,128]{3,2,1,0:T(8,128)(2,1)S(1)}, u32[]{:S(2)}, u32[]{:S(2)}) collective-permute-start(bf16[8,4,16,128]{3,2,1,0:T(8,128)(2,1)S(1)} %pad_maximum_fusion), channel_id=1, source_target_pairs={{0,4},{8,0},{16,8},{24,16},{28,24},{20,28},{12,20},{4,12},{1,5},{9... | collective-permute-start | bytes 393224 | tf_op jit(solution)/shard_map/ppermute | solution.py:580
  12.3 0.5 collective-permute-start.8
  12.8 1.3 %collective-permute-start.12 = (bf16[4,16,16,128]{3,2,1,0:T(8,128)(2,1)S(1)}, bf16[4,16,16,128]{3,2,1,0:T(8,128)(2,1)S(1)}, u32[]{:S(2)}, u32[]{:S(2)}) collective-permute-start(bf16[4,16,16,128]{3,2,1,0:T(8,128)(2,1)S(1)} %get-tuple-element.54.refs_0_), channel_id=1, source_target_pairs={{0,2},{1,3},{2,0},{3,1},{4,6},{5,7},{6,4},{7,5},{8,10},{9,11},{10,... | collective-permute-start | bytes 786440 | tf_op jit(solution)/shard_map/ppermute | solution.py:545
  14.4 1.6 %collective-permute-start.4 = (bf16[8,4,16,128]{3,2,1,0:T(8,128)(2,1)S(1)}, bf16[8,4,16,128]{3,2,1,0:T(8,128)(2,1)S(1)}, u32[]{:S(2)}, u32[]{:S(2)}) collective-permute-start(bf16[8,4,16,128]{3,2,1,0:T(8,128)(2,1)S(1)} %collective-permute-done.1.rest_2_), channel_id=1, source_target_pairs={{0,8},{8,16},{16,24},{24,28},{28,20},{20,12},{12,4},{4,0},{1,9},{9... | collective-permute-start | bytes 393224 | tf_op jit(solution)/shard_map/ppermute | solution.py:577
  16.0 0.4 collective-permute-start.5
  16.4 0.2 collective-permute-done.9.rest_5_
  16.7 2.0 %collective-permute-done.8.rest_4_ = bf16[8,4,16,128]{3,2,1,0:T(8,128)(2,1)S(1)} collective-permute-done((bf16[8,4,16,128]{3,2,1,0:T(8,128)(2,1)S(1)}, bf16[8,4,16,128]{3,2,1,0:T(8,128)(2,1)S(1)}, u32[]{:S(2)}, u32[]{:S(2)}) %collective-permute-start.8) | collective-permute-done | bytes 131104 | tf_op jit(solution)/shard_map/ppermute | solution.py:577
  18.7 2.0 %collective-permute-start.11 = (bf16[8,4,16,128]{3,2,1,0:T(8,128)(2,1)S(1)}, bf16[8,4,16,128]{3,2,1,0:T(8,128)(2,1)S(1)}, u32[]{:S(2)}, u32[]{:S(2)}) collective-permute-start(bf16[8,4,16,128]{3,2,1,0:T(8,128)(2,1)S(1)} %collective-permute-done.9.rest_5_), channel_id=1, source_target_pairs={{0,4},{8,0},{16,8},{24,16},{28,24},{20,28},{12,20},{4,12},{1,5},{9... | collective-permute-start | bytes 393224 | tf_op jit(solution)/shard_map/ppermute | solution.py:580
  20.7 0.8 %collective-permute-done.4.refs_0_.rest_6_ = bf16[8,4,16,128]{3,2,1,0:T(8,128)(2,1)S(1)} collective-permute-done((bf16[8,4,16,128]{3,2,1,0:T(8,128)(2,1)S(1)}, bf16[8,4,16,128]{3,2,1,0:T(8,128)(2,1)S(1)}, u32[]{:S(2)}, u32[]{:S(2)}) %collective-permute-start.4) | collective-permute-done | bytes 131104 | tf_op jit(solution)/shard_map/ppermute | solution.py:577
  21.5 0.2 collective-permute-done.5.refs_1_.rest_7_
  21.7 1.9 %collective-permute-done.10.refs_2_.rest_8_ = bf16[8,4,16,128]{3,2,1,0:T(8,128)(2,1)S(1)} collective-permute-done((bf16[8,4,16,128]{3,2,1,0:T(8,128)(2,1)S(1)}, bf16[8,4,16,128]{3,2,1,0:T(8,128)(2,1)S(1)}, u32[]{:S(2)}, u32[]{:S(2)}) %collective-permute-start.10) | collective-permute-done | bytes 131104 | tf_op jit(solution)/shard_map/ppermute | solution.py:577
  23.9 1.6 %collective-permute-start.17 = (bf16[16,4,16,128]{3,2,1,0:T(8,128)(2,1)S(1)}, bf16[16,4,16,128]{3,2,1,0:T(8,128)(2,1)S(1)}, u32[]{:S(2)}, u32[]{:S(2)}) collective-permute-start(bf16[16,4,16,128]{3,2,1,0:T(8,128)(2,1)S(1)} %get-tuple-element.61), channel_id=1, source_target_pairs={{0,8},{8,16},{16,24},{24,28},{28,20},{20,12},{12,4},{4,0},{1,9},{9... | collective-permute-start | bytes 786440 | tf_op jit(solution)/shard_map/ppermute | solution.py:577
  25.5 0.4 collective-permute-start.18
  26.2 3.4 %cross.3 = (bf16[256,128]{1,0:T(8,128)(2,1)S(1)}, bf16[256,128]{1,0:T(8,128)(2,1)S(1)}, bf16[256,128]{1,0:T(8,128)(2,1)S(1)}, bf16[256,128]{1,0:T(8,128)(2,1)S(1)}) custom-call(s32[4,8]{1,0:T(4,128)S(1)} %copy-done.2, bf16[512,2048]{1,0:T(8,128)(2,1)S(1)} %copy-done, bf16[4,2,8,4,16,128]{5,4,3,2,1,0:T(8,128)(2,1)S(1)} %turn.2.rest_0_, ...), custom_call_target="tpu_custom_call" | custom-call | flops 2990000128 | bytes 1024 | tf_op jit(solution)/shard_map/cross/pallas_call | solution.py:381
  29.6 1.8 %collective-permute-start.15 = (bf16[256,128]{1,0:T(8,128)(2,1)S(1)}, bf16[256,128]{1,0:T(8,128)(2,1)S(1)}, u32[]{:S(2)}, u32[]{:S(2)}) collective-permute-start(bf16[256,128]{1,0:T(8,128)(2,1)S(1)} %get-tuple-element.58), channel_id=1, source_target_pairs={{0,2},{1,3},{2,0},{3,1},{4,6},{5,7},{6,4},{7,5},{8,10},{9,11},{10,... | collective-permute-start | bytes 196616 | tf_op jit(solution)/shard_map/ppermute | solution.py:545
  31.5 1.3 %collective-permute-done.17.rest_10_ = bf16[16,4,16,128]{3,2,1,0:T(8,128)(2,1)S(1)} collective-permute-done((bf16[16,4,16,128]{3,2,1,0:T(8,128)(2,1)S(1)}, bf16[16,4,16,128]{3,2,1,0:T(8,128)(2,1)S(1)}, u32[]{:S(2)}, u32[]{:S(2)}) %collective-permute-start.17) | collective-permute-done | bytes 262176 | tf_op jit(solution)/shard_map/ppermute | solution.py:577
  32.8 1.4 %collective-permute-start.22 = (bf16[16,4,16,128]{3,2,1,0:T(8,128)(2,1)S(1)}, bf16[16,4,16,128]{3,2,1,0:T(8,128)(2,1)S(1)}, u32[]{:S(2)}, u32[]{:S(2)}) collective-permute-start(bf16[16,4,16,128]{3,2,1,0:T(8,128)(2,1)S(1)} %collective-permute-done.17.rest_10_), channel_id=1, source_target_pairs={{0,8},{8,16},{16,24},{24,28},{28,20},{20,12},{12,4},{4,0},{1,9},{9... | collective-permute-start | bytes 786440 | tf_op jit(solution)/shard_map/ppermute | solution.py:577
  34.2 5.8 %cross.4 = (bf16[512,128]{1,0:T(8,128)(2,1)S(1)}, bf16[512,128]{1,0:T(8,128)(2,1)S(1)}, bf16[512,128]{1,0:T(8,128)(2,1)S(1)}, bf16[512,128]{1,0:T(8,128)(2,1)S(1)}) custom-call(s32[4,8]{1,0:T(4,128)S(1)} %copy-done.2, bf16[512,2048]{1,0:T(8,128)(2,1)S(1)} %copy-done, bf16[4,2,8,4,16,128]{5,4,3,2,1,0:T(8,128)(2,1)S(1)} %turn.2.rest_0_, ...), custom_call_target="tpu_custom_call" | custom-call | flops 5289999872 | bytes 1024 | tf_op jit(solution)/shard_map/cross/pallas_call | solution.py:381
  40.1 1.8 %collective-permute-start.20 = (bf16[512,128]{1,0:T(8,128)(2,1)S(1)}, bf16[512,128]{1,0:T(8,128)(2,1)S(1)}, u32[]{:S(2)}, u32[]{:S(2)}) collective-permute-start(bf16[512,128]{1,0:T(8,128)(2,1)S(1)} %get-tuple-element.65), channel_id=1, source_target_pairs={{0,2},{1,3},{2,0},{3,1},{4,6},{5,7},{6,4},{7,5},{8,10},{9,11},{10,... | collective-permute-start | bytes 393224 | tf_op jit(solution)/shard_map/ppermute | solution.py:545
  42.0 3.4 %cross.5 = (bf16[256,128]{1,0:T(8,128)(2,1)S(1)}, bf16[256,128]{1,0:T(8,128)(2,1)S(1)}, bf16[256,128]{1,0:T(8,128)(2,1)S(1)}, bf16[256,128]{1,0:T(8,128)(2,1)S(1)}) custom-call(s32[4,8]{1,0:T(4,128)S(1)} %copy-done.2, bf16[512,2048]{1,0:T(8,128)(2,1)S(1)} %copy-done, bf16[4,2,8,4,16,128]{5,4,3,2,1,0:T(8,128)(2,1)S(1)} %turn.2.rest_0_, ...), custom_call_target="tpu_custom_call" | custom-call | flops 2990000128 | bytes 1024 | tf_op jit(solution)/shard_map/cross/pallas_call | solution.py:381
  45.4 0.4 collective-permute-start.23
  45.7 1.8 %collective-permute-start.24 = (bf16[256,128]{1,0:T(8,128)(2,1)S(1)}, bf16[256,128]{1,0:T(8,128)(2,1)S(1)}, u32[]{:S(2)}, u32[]{:S(2)}) collective-permute-start(bf16[256,128]{1,0:T(8,128)(2,1)S(1)} %get-tuple-element.71), channel_id=1, source_target_pairs={{0,2},{1,3},{2,0},{3,1},{4,6},{5,7},{6,4},{7,5},{8,10},{9,11},{10,... | collective-permute-start | bytes 196616 | tf_op jit(solution)/shard_map/ppermute | solution.py:545
  47.5 0.8 %collective-permute-done.21.rest_7_ = bf16[512,128]{1,0:T(8,128)(2,1)S(1)} collective-permute-done((bf16[512,128]{1,0:T(8,128)(2,1)S(1)}, bf16[512,128]{1,0:T(8,128)(2,1)S(1)}, u32[]{:S(2)}, u32[]{:S(2)}) %collective-permute-start.21) | collective-permute-done | bytes 131104 | tf_op jit(solution)/shard_map/ppermute | solution.py:545
  48.3 2.1 %early.1 = f32[1024,4,1,128]{3,2,1,0:T(1,128)} custom-call(s32[4,8]{1,0:T(4,128)S(1)} %copy-done.2, bf16[4,128,512]{2,1,0:T(8,128)(2,1)S(1)} %copy-done.1, bf16[256,128]{1,0:T(8,128)(2,1)S(1)} %get-tuple-element.56.rest_0_, bf16[256,128]{1,0:T(8,128)(2,1)S(1)} %collective-permute-done.14.rest_1_, bf16[256,128]{1,0:T(8,128)(2,1)S(1)} %collective-permute-done.15.rest_2_, ...), custom_call_target="tpu_custom_call" | custom-call | flops 57500000 | bytes 1024 | tf_op jit(solution)/shard_map/early/pallas_call | solution.py:491
  50.5 1.4 %collective-permute-done.25.rest_3_ = bf16[256,128]{1,0:T(8,128)(2,1)S(1)} collective-permute-done((bf16[256,128]{1,0:T(8,128)(2,1)S(1)}, bf16[256,128]{1,0:T(8,128)(2,1)S(1)}, u32[]{:S(2)}, u32[]{:S(2)}) %collective-permute-start.25) | collective-permute-done | bytes 65568 | tf_op jit(solution)/shard_map/ppermute | solution.py:545
  51.8 1.7 %late.1 = f32[1024,4,1,128]{3,2,1,0:T(1,128)} custom-call(s32[4,8]{1,0:T(4,128)S(1)} %copy-done.2, bf16[4,128,512]{2,1,0:T(8,128)(2,1)S(1)} %copy-done.1, f32[1024,4,1,128]{3,2,1,0:T(1,128)} %early.1, bf16[256,128]{1,0:T(8,128)(2,1)S(1)} %get-tuple-element.69.rest_0_, ...), custom_call_target="tpu_custom_call", output_to_operand_aliasing={{}: (2, {})} | custom-call | flops 57500000 | bytes 1024 | tf_op jit(solution)/shard_map/late/pallas_call | solution.py:504
  (38 shorter events, 1.3 us)
Async XLA Ops:
  3.6 3.3 %collective-permute-start = (bf16[4,4,16,128]{3,2,1,0:T(8,128)(2,1)S(1)}, bf16[4,4,16,128]{3,2,1,0:T(8,128)(2,1)S(1)}, u32[]{:S(2)}, u32[]{:S(2)}) collective-permute-start(bf16[4,4,16,128]{3,2,1,0:T(8,128)(2,1)S(1)} %get-tuple-element.40), channel_id=1, source_target_pairs={{0,1},{1,0},{2,3},{3,2},{4,5},{5,4},{6,7},{7,6},{8,9},{9,8},{10,11... | collective-permute-start | bytes 196616 | tf_op jit(solution)/shard_map/ppermute | solution.py:545
  4.1 5.3 %collective-permute-start.6 = (bf16[4,4,16,128]{3,2,1,0:T(8,128)(2,1)S(1)}, bf16[4,4,16,128]{3,2,1,0:T(8,128)(2,1)S(1)}, u32[]{:S(2)}, u32[]{:S(2)}) collective-permute-start(bf16[4,4,16,128]{3,2,1,0:T(8,128)(2,1)S(1)} %get-tuple-element.45), channel_id=1, source_target_pairs={{0,2},{1,3},{2,0},{3,1},{4,6},{5,7},{6,4},{7,5},{8,10},{9,11},{10,... | collective-permute-start | bytes 196616 | tf_op jit(solution)/shard_map/ppermute | solution.py:545
  6.7 4.0 %collective-permute-start.7 = (bf16[4,4,16,128]{3,2,1,0:T(8,128)(2,1)S(1)}, bf16[4,4,16,128]{3,2,1,0:T(8,128)(2,1)S(1)}, u32[]{:S(2)}, u32[]{:S(2)}) collective-permute-start(bf16[4,4,16,128]{3,2,1,0:T(8,128)(2,1)S(1)} %get-tuple-element.46), channel_id=1, source_target_pairs={{0,3},{1,2},{2,1},{3,0},{4,7},{5,6},{6,5},{7,4},{8,11},{9,10},{10,... | collective-permute-start | bytes 196616 | tf_op jit(solution)/shard_map/ppermute | solution.py:545
  6.8 4.0 %collective-permute-start.3 = (bf16[4,16,16,128]{3,2,1,0:T(8,128)(2,1)S(1)}, bf16[4,16,16,128]{3,2,1,0:T(8,128)(2,1)S(1)}, u32[]{:S(2)}, u32[]{:S(2)}) collective-permute-start(bf16[4,16,16,128]{3,2,1,0:T(8,128)(2,1)S(1)} %get-tuple-element.54.refs_0_), channel_id=1, source_target_pairs={{0,1},{1,0},{2,3},{3,2},{4,5},{5,4},{6,7},{7,6},{8,9},{9,8},{10,11... | collective-permute-start | bytes 786440 | tf_op jit(solution)/shard_map/ppermute | solution.py:545
  6.9 19.2 %copy-start = (bf16[512,2048]{1,0:T(8,128)(2,1)S(1)}, bf16[512,2048]{1,0:T(8,128)(2,1)}, u32[]{:S(2)}) copy-start(bf16[512,2048]{1,0:T(8,128)(2,1)} %constant.4.clone.table_hbm.table) | copy-start | bytes 6291460
  6.9 19.2 %copy-start.2 = (s32[4,8]{1,0:T(4,128)S(1)}, s32[4,8]{1,0:T(4,128)}, u32[]{:S(2)}) copy-start(s32[4,8]{1,0:T(4,128)} %plan.9) | copy-start | bytes 388
  6.9 7.4 %collective-permute-start.2 = (bf16[8,4,16,128]{3,2,1,0:T(8,128)(2,1)S(1)}, bf16[8,4,16,128]{3,2,1,0:T(8,128)(2,1)S(1)}, u32[]{:S(2)}, u32[]{:S(2)}) collective-permute-start(bf16[8,4,16,128]{3,2,1,0:T(8,128)(2,1)S(1)} %constant_dynamic-update-slice_fusion), channel_id=1, source_target_pairs={{0,4},{8,0},{16,8},{24,16},{28,24},{20,28},{12,20},{4,12},{1,5},{9... | collective-permute-start | bytes 393224 | tf_op jit(solution)/shard_map/ppermute | solution.py:580
  9.0 5.4 %collective-permute-start.1 = (bf16[8,4,16,128]{3,2,1,0:T(8,128)(2,1)S(1)}, bf16[8,4,16,128]{3,2,1,0:T(8,128)(2,1)S(1)}, u32[]{:S(2)}, u32[]{:S(2)}) collective-permute-start(bf16[8,4,16,128]{3,2,1,0:T(8,128)(2,1)S(1)} %constant_dynamic-update-slice_fusion), channel_id=1, source_target_pairs={{0,8},{8,16},{16,24},{24,28},{28,20},{20,12},{12,4},{4,0},{1,9},{9... | collective-permute-start | bytes 393224 | tf_op jit(solution)/shard_map/ppermute | solution.py:577
  10.8 5.9 %collective-permute-start.9 = (bf16[8,4,16,128]{3,2,1,0:T(8,128)(2,1)S(1)}, bf16[8,4,16,128]{3,2,1,0:T(8,128)(2,1)S(1)}, u32[]{:S(2)}, u32[]{:S(2)}) collective-permute-start(bf16[8,4,16,128]{3,2,1,0:T(8,128)(2,1)S(1)} %pad_maximum_fusion), channel_id=1, source_target_pairs={{0,4},{8,0},{16,8},{24,16},{28,24},{20,28},{12,20},{4,12},{1,5},{9... | collective-permute-start | bytes 393224 | tf_op jit(solution)/shard_map/ppermute | solution.py:580
  12.3 6.3 %collective-permute-start.8 = (bf16[8,4,16,128]{3,2,1,0:T(8,128)(2,1)S(1)}, bf16[8,4,16,128]{3,2,1,0:T(8,128)(2,1)S(1)}, u32[]{:S(2)}, u32[]{:S(2)}) collective-permute-start(bf16[8,4,16,128]{3,2,1,0:T(8,128)(2,1)S(1)} %pad_maximum_fusion), channel_id=1, source_target_pairs={{0,8},{8,16},{16,24},{24,28},{28,20},{20,12},{12,4},{4,0},{1,9},{9... | collective-permute-start | bytes 393224 | tf_op jit(solution)/shard_map/ppermute | solution.py:577
  12.8 11.0 %collective-permute-start.12 = (bf16[4,16,16,128]{3,2,1,0:T(8,128)(2,1)S(1)}, bf16[4,16,16,128]{3,2,1,0:T(8,128)(2,1)S(1)}, u32[]{:S(2)}, u32[]{:S(2)}) collective-permute-start(bf16[4,16,16,128]{3,2,1,0:T(8,128)(2,1)S(1)} %get-tuple-element.54.refs_0_), channel_id=1, source_target_pairs={{0,2},{1,3},{2,0},{3,1},{4,6},{5,7},{6,4},{7,5},{8,10},{9,11},{10,... | collective-permute-start | bytes 786440 | tf_op jit(solution)/shard_map/ppermute | solution.py:545
  14.4 7.1 %collective-permute-start.4 = (bf16[8,4,16,128]{3,2,1,0:T(8,128)(2,1)S(1)}, bf16[8,4,16,128]{3,2,1,0:T(8,128)(2,1)S(1)}, u32[]{:S(2)}, u32[]{:S(2)}) collective-permute-start(bf16[8,4,16,128]{3,2,1,0:T(8,128)(2,1)S(1)} %collective-permute-done.1.rest_2_), channel_id=1, source_target_pairs={{0,8},{8,16},{16,24},{24,28},{28,20},{20,12},{12,4},{4,0},{1,9},{9... | collective-permute-start | bytes 393224 | tf_op jit(solution)/shard_map/ppermute | solution.py:577
  16.0 5.7 %collective-permute-start.5 = (bf16[8,4,16,128]{3,2,1,0:T(8,128)(2,1)S(1)}, bf16[8,4,16,128]{3,2,1,0:T(8,128)(2,1)S(1)}, u32[]{:S(2)}, u32[]{:S(2)}) collective-permute-start(bf16[8,4,16,128]{3,2,1,0:T(8,128)(2,1)S(1)} %collective-permute-done.2.rest_3_), channel_id=1, source_target_pairs={{0,4},{8,0},{16,8},{24,16},{28,24},{20,28},{12,20},{4,12},{1,5},{9... | collective-permute-start | bytes 393224 | tf_op jit(solution)/shard_map/ppermute | solution.py:580
  18.7 5.0 %collective-permute-start.10 = (bf16[8,4,16,128]{3,2,1,0:T(8,128)(2,1)S(1)}, bf16[8,4,16,128]{3,2,1,0:T(8,128)(2,1)S(1)}, u32[]{:S(2)}, u32[]{:S(2)}) collective-permute-start(bf16[8,4,16,128]{3,2,1,0:T(8,128)(2,1)S(1)} %collective-permute-done.8.rest_4_), channel_id=1, source_target_pairs={{0,8},{8,16},{16,24},{24,28},{28,20},{20,12},{12,4},{4,0},{1,9},{9... | collective-permute-start | bytes 393224 | tf_op jit(solution)/shard_map/ppermute | solution.py:577
  18.7 5.1 %collective-permute-start.11 = (bf16[8,4,16,128]{3,2,1,0:T(8,128)(2,1)S(1)}, bf16[8,4,16,128]{3,2,1,0:T(8,128)(2,1)S(1)}, u32[]{:S(2)}, u32[]{:S(2)}) collective-permute-start(bf16[8,4,16,128]{3,2,1,0:T(8,128)(2,1)S(1)} %collective-permute-done.9.rest_5_), channel_id=1, source_target_pairs={{0,4},{8,0},{16,8},{24,16},{28,24},{20,28},{12,20},{4,12},{1,5},{9... | collective-permute-start | bytes 393224 | tf_op jit(solution)/shard_map/ppermute | solution.py:580
  23.8 2.2 %collective-permute-start.13 = (bf16[4,16,16,128]{3,2,1,0:T(8,128)(2,1)S(1)}, bf16[4,16,16,128]{3,2,1,0:T(8,128)(2,1)S(1)}, u32[]{:S(2)}, u32[]{:S(2)}) collective-permute-start(bf16[4,16,16,128]{3,2,1,0:T(8,128)(2,1)S(1)} %collective-permute-done.12.refs_0_), channel_id=1, source_target_pairs={{0,1},{1,0},{2,3},{3,2},{4,5},{5,4},{6,7},{7,6},{8,9},{9,8},{10,11... | collective-permute-start | bytes 786440 | tf_op jit(solution)/shard_map/ppermute | solution.py:545
  23.9 8.9 %collective-permute-start.17 = (bf16[16,4,16,128]{3,2,1,0:T(8,128)(2,1)S(1)}, bf16[16,4,16,128]{3,2,1,0:T(8,128)(2,1)S(1)}, u32[]{:S(2)}, u32[]{:S(2)}) collective-permute-start(bf16[16,4,16,128]{3,2,1,0:T(8,128)(2,1)S(1)} %get-tuple-element.61), channel_id=1, source_target_pairs={{0,8},{8,16},{16,24},{24,28},{28,20},{20,12},{12,4},{4,0},{1,9},{9... | collective-permute-start | bytes 786440 | tf_op jit(solution)/shard_map/ppermute | solution.py:577
  25.5 8.7 %collective-permute-start.18 = (bf16[16,4,16,128]{3,2,1,0:T(8,128)(2,1)S(1)}, bf16[16,4,16,128]{3,2,1,0:T(8,128)(2,1)S(1)}, u32[]{:S(2)}, u32[]{:S(2)}) collective-permute-start(bf16[16,4,16,128]{3,2,1,0:T(8,128)(2,1)S(1)} %get-tuple-element.62), channel_id=1, source_target_pairs={{0,4},{8,0},{16,8},{24,16},{28,24},{20,28},{12,20},{4,12},{1,5},{9... | collective-permute-start | bytes 786440 | tf_op jit(solution)/shard_map/ppermute | solution.py:580
  29.5 10.5 %collective-permute-start.14 = (bf16[256,128]{1,0:T(8,128)(2,1)S(1)}, bf16[256,128]{1,0:T(8,128)(2,1)S(1)}, u32[]{:S(2)}, u32[]{:S(2)}) collective-permute-start(bf16[256,128]{1,0:T(8,128)(2,1)S(1)} %get-tuple-element.57), channel_id=1, source_target_pairs={{0,1},{1,0},{2,3},{3,2},{4,5},{5,4},{6,7},{7,6},{8,9},{9,8},{10,11... | collective-permute-start | bytes 196616 | tf_op jit(solution)/shard_map/ppermute | solution.py:545
  29.6 12.3 %collective-permute-start.15 = (bf16[256,128]{1,0:T(8,128)(2,1)S(1)}, bf16[256,128]{1,0:T(8,128)(2,1)S(1)}, u32[]{:S(2)}, u32[]{:S(2)}) collective-permute-start(bf16[256,128]{1,0:T(8,128)(2,1)S(1)} %get-tuple-element.58), channel_id=1, source_target_pairs={{0,2},{1,3},{2,0},{3,1},{4,6},{5,7},{6,4},{7,5},{8,10},{9,11},{10,... | collective-permute-start | bytes 196616 | tf_op jit(solution)/shard_map/ppermute | solution.py:545
  31.4 10.6 %collective-permute-start.16 = (bf16[256,128]{1,0:T(8,128)(2,1)S(1)}, bf16[256,128]{1,0:T(8,128)(2,1)S(1)}, u32[]{:S(2)}, u32[]{:S(2)}) collective-permute-start(bf16[256,128]{1,0:T(8,128)(2,1)S(1)} %get-tuple-element.59), channel_id=1, source_target_pairs={{0,3},{1,2},{2,1},{3,0},{4,7},{5,6},{6,5},{7,4},{8,11},{9,10},{10,... | collective-permute-start | bytes 196616 | tf_op jit(solution)/shard_map/ppermute | solution.py:545
  32.8 9.2 %collective-permute-start.22 = (bf16[16,4,16,128]{3,2,1,0:T(8,128)(2,1)S(1)}, bf16[16,4,16,128]{3,2,1,0:T(8,128)(2,1)S(1)}, u32[]{:S(2)}, u32[]{:S(2)}) collective-permute-start(bf16[16,4,16,128]{3,2,1,0:T(8,128)(2,1)S(1)} %collective-permute-done.17.rest_10_), channel_id=1, source_target_pairs={{0,8},{8,16},{16,24},{24,28},{28,20},{20,12},{12,4},{4,0},{1,9},{9... | collective-permute-start | bytes 786440 | tf_op jit(solution)/shard_map/ppermute | solution.py:577
  40.0 7.5 %collective-permute-start.19 = (bf16[512,128]{1,0:T(8,128)(2,1)S(1)}, bf16[512,128]{1,0:T(8,128)(2,1)S(1)}, u32[]{:S(2)}, u32[]{:S(2)}) collective-permute-start(bf16[512,128]{1,0:T(8,128)(2,1)S(1)} %get-tuple-element.64), channel_id=1, source_target_pairs={{0,1},{1,0},{2,3},{3,2},{4,5},{5,4},{6,7},{7,6},{8,9},{9,8},{10,11... | collective-permute-start | bytes 393224 | tf_op jit(solution)/shard_map/ppermute | solution.py:545
  40.1 7.5 %collective-permute-start.20 = (bf16[512,128]{1,0:T(8,128)(2,1)S(1)}, bf16[512,128]{1,0:T(8,128)(2,1)S(1)}, u32[]{:S(2)}, u32[]{:S(2)}) collective-permute-start(bf16[512,128]{1,0:T(8,128)(2,1)S(1)} %get-tuple-element.65), channel_id=1, source_target_pairs={{0,2},{1,3},{2,0},{3,1},{4,6},{5,7},{6,4},{7,5},{8,10},{9,11},{10,... | collective-permute-start | bytes 393224 | tf_op jit(solution)/shard_map/ppermute | solution.py:545
  41.9 6.4 %collective-permute-start.21 = (bf16[512,128]{1,0:T(8,128)(2,1)S(1)}, bf16[512,128]{1,0:T(8,128)(2,1)S(1)}, u32[]{:S(2)}, u32[]{:S(2)}) collective-permute-start(bf16[512,128]{1,0:T(8,128)(2,1)S(1)} %get-tuple-element.66), channel_id=1, source_target_pairs={{0,3},{1,2},{2,1},{3,0},{4,7},{5,6},{6,5},{7,4},{8,11},{9,10},{10,... | collective-permute-start | bytes 393224 | tf_op jit(solution)/shard_map/ppermute | solution.py:545
  42.0 6.3 %copy-start.1 = (bf16[4,128,512]{2,1,0:T(8,128)(2,1)S(1)}, bf16[4,128,512]{2,1,0:T(8,128)(2,1)}, u32[]{:S(2)}) copy-start(bf16[4,128,512]{2,1,0:T(8,128)(2,1)} %constant.5.clone.place) | copy-start | bytes 1572868
  45.4 5.1 %collective-permute-start.23 = (bf16[256,128]{1,0:T(8,128)(2,1)S(1)}, bf16[256,128]{1,0:T(8,128)(2,1)S(1)}, u32[]{:S(2)}, u32[]{:S(2)}) collective-permute-start(bf16[256,128]{1,0:T(8,128)(2,1)S(1)} %get-tuple-element.70), channel_id=1, source_target_pairs={{0,1},{1,0},{2,3},{3,2},{4,5},{5,4},{6,7},{7,6},{8,9},{9,8},{10,11... | collective-permute-start | bytes 196616 | tf_op jit(solution)/shard_map/ppermute | solution.py:545
  45.7 4.7 %collective-permute-start.24 = (bf16[256,128]{1,0:T(8,128)(2,1)S(1)}, bf16[256,128]{1,0:T(8,128)(2,1)S(1)}, u32[]{:S(2)}, u32[]{:S(2)}) collective-permute-start(bf16[256,128]{1,0:T(8,128)(2,1)S(1)} %get-tuple-element.71), channel_id=1, source_target_pairs={{0,2},{1,3},{2,0},{3,1},{4,6},{5,7},{6,4},{7,5},{8,10},{9,11},{10,... | collective-permute-start | bytes 196616 | tf_op jit(solution)/shard_map/ppermute | solution.py:545
  47.5 4.3 %collective-permute-start.25 = (bf16[256,128]{1,0:T(8,128)(2,1)S(1)}, bf16[256,128]{1,0:T(8,128)(2,1)S(1)}, u32[]{:S(2)}, u32[]{:S(2)}) collective-permute-start(bf16[256,128]{1,0:T(8,128)(2,1)S(1)} %get-tuple-element.72), channel_id=1, source_target_pairs={{0,3},{1,2},{2,1},{3,0},{4,7},{5,6},{6,5},{7,4},{8,11},{9,10},{10,... | collective-permute-start | bytes 196616 | tf_op jit(solution)/shard_map/ppermute | solution.py:545

commit v14 on v12

--- a/solution.py
+++ b/solution.py
@@ -277,48 +277,48 @@
                 lax.fori_loop(0, candidate.shape[0], widen_other, 0)
 
 
-def sum_windows(owns, other, summed):
+def sum_windows(owns, other, slot, crossed, beside=None):
     groups, _, windows, group = owns[0].shape[:4]
-    slots, _, quarter = other.shape[1:4]
-    width = groups * group * quarter
-    shift = groups.bit_length() - 1
-
-    for slot in range(slots):
-
-        def body(index, carry, slot=slot):
-            kind, part = index >> shift, index & (groups - 1)
-            mine = [own.at[part, kind] for own in owns]
-            theirs = other.at[kind, slot]
+    quarter = other.shape[3]
+    size = 2 * TILES
+
+    def body(index, carry):
+        mine = [own.at[index] for own in owns]
+
+        def sums(kind):
             totals = [None] * (group * quarter)
             for half, own in enumerate(mine):
                 for w in range(windows):
-                    left = [own[w, s] for s in range(group)]
-                    right = [theirs[half * windows + w, t] for t in range(quarter)]
+                    left = [own[kind, w, s] for s in range(group)]
+                    right = [other[kind, slot, half * windows + w, t] for t in range(quarter)]
                     for s in range(group):
                         for t in range(quarter):
                             term = left[s] * right[t]
                             old = totals[s * quarter + t]
                             totals[s * quarter + t] = term if old is None else old + term
-            rows = summed.at[kind]
-            base = (slot * width + part * (group * quarter)) * TILES
-            for place in range(group * quarter):
-                at = pl.multiple_of(base + place * TILES, TILES)
-                rows[pl.ds(at, TILES), :] = totals[place]
-            return carry
-
-        lax.fori_loop(0, 3 * groups, body, 0)
-
-
-def cross_kernel(first_slot, slots, count, scaling, places, parts, plan, table, *rest):
-    owns, rest = rest[:2], rest[2:]
-    others, rest = rest[: len(places)], rest[len(places) :]
-    outs = rest[:parts]
-    other, summed, operand, result = rest[parts:]
-    stations = owns[0].shape[0] * owns[0].shape[3]
-    widen_others(first_slot, slots, count, places, plan, others, other)
-    sum_windows(owns, other, summed)
-    width = stations * other.shape[3]
-    columns = slots * width
+            return totals
+
+        def store(place, part, value):
+            at = pl.multiple_of(base + place * size + part * TILES, TILES)
+            crossed[pl.ds(at, TILES), :] = value
+
+        if beside is not None:
+            beside(index)
+        base = index * (group * quarter * size)
+        shared = sums(0)
+        third = sums(2)
+        for place in range(group * quarter):
+            store(place, 0, shared[place] + third[place])
+        second = sums(1)
+        for place in range(group * quarter):
+            store(place, 1, shared[place] - second[place])
+        return carry
+
+    lax.fori_loop(0, groups, body, 0)
+
+
+def fill_operand(crossed, operand):
+    columns = operand.shape[0] // CHUNKS
     even = even_lanes((columns, LANES))
     sign_real = lane_cycle([1.0, -1.0, -1.0, 1.0])
     sign_imag = lane_cycle([1.0, 1.0, -1.0, -1.0])
@@ -328,8 +328,8 @@
     for j in range(TILES):
         at = slice(j * LANES, (j + 1) * LANES)
         at_imag = slice(NBIN + j * LANES, NBIN + (j + 1) * LANES)
-        kinds = [summed[kind, pl.ds(j, columns, stride=TILES), :] for kind in range(3)]
-        real, imag = kinds[0] + kinds[2], kinds[0] - kinds[1]
+        real = crossed[pl.ds(j, columns, stride=2 * TILES), :]
+        imag = crossed[pl.ds(TILES + j, columns, stride=2 * TILES), :]
         if j == 0:
             real, imag = real * first_weight, imag * first_weight
         turned = [(real, imag), (real * cosine - imag * sine, imag * cosine + real * sine)]
@@ -338,25 +338,49 @@
             rows = slice(q * columns, (q + 1) * columns)
             operand[rows, at] = turned[q][0].astype(BF)
             operand[rows, at_imag] = turned[q][1].astype(BF)
-    block = lax.dot_general(
-        table[...], operand[...], (((1,), (1,)), ((), ())), preferred_element_type=F32
-    )
-    block = block * (2.0 * scaling)
-    if slots == 1:
-        half = table.shape[0] // 2
-        low_lanes = lax.broadcasted_iota(jnp.int32, (half, LANES), 1) < width
-        for p in range(CHUNKS // 2):
-            at = slice(p * LANES, (p + 1) * LANES)
-            low, high = block[:half, at], block[half:, at]
-            pair = (
-                jnp.where(low_lanes, low, pltpu.roll(high, width, 1)),
-                jnp.where(low_lanes, pltpu.roll(low, width, 1), high),
-            )
-            for second in range(2):
-                result[2 * p + second] = pair[second].astype(BF)
+
+
+def cross_kernel(first_slot, slots, count, scaling, places, parts, plan, table, *rest):
+    owns, rest = rest[:2], rest[2:]
+    others, rest = rest[: len(places)], rest[len(places) :]
+    outs = rest[:parts]
+    other, crossed, operand, result, *stash = rest[parts:]
+    groups = owns[0].shape[0]
+    widen_others(first_slot, slots, count, places, plan, others, other)
+    width = operand.shape[0] // CHUNKS
+    share = table.shape[0]
+
+    def lags(first, size):
+        block = lax.dot_general(
+            table[pl.ds(first, size), :],
+            operand[...],
+            (((1,), (1,)), ((), ())),
+            preferred_element_type=F32,
+        )
+        return block * (2.0 * scaling)
+
+    sum_windows(owns, other, 0, crossed)
+    fill_operand(crossed, operand)
+    if slots == 2:
+        size = share // groups
+
+        def beside(index):
+            first = pl.multiple_of(index * size, size)
+            stash[0][pl.ds(first, size), :] = lags(first, size)
+
+        sum_windows(owns, other, 1, crossed, beside)
+        fill_operand(crossed, operand)
+    block = lags(0, share)
+    if slots == 2:
+        low_block, high_block = stash[0][...], block
     else:
-        for q in range(CHUNKS):
-            result[q] = block[:, q * columns : (q + 1) * columns].astype(BF)
+        low_block, high_block = block[: share // 2], block[share // 2 :]
+    low_lanes = lax.broadcasted_iota(jnp.int32, (low_block.shape[0], LANES), 1) < width
+    for p in range(CHUNKS // 2):
+        at = slice(p * LANES, (p + 1) * LANES)
+        low, high = low_block[:, at], high_block[:, at]
+        result[2 * p] = jnp.where(low_lanes, low, pltpu.roll(high, width, 1)).astype(BF)
+        result[2 * p + 1] = jnp.where(low_lanes, pltpu.roll(low, width, 1), high).astype(BF)
     me = lax.axis_index("seg")
     for j in range(parts):
         outs[j][...] = result[me ^ j]
@@ -380,10 +404,11 @@
         out_specs=[vmem] * parts,
         scratch_shapes=[
             pltpu.VMEM((3, slots, 2 * windows, quarter, TILES, LANES), F32),
-            pltpu.VMEM((3, columns * TILES, LANES), F32),
-            pltpu.VMEM((CHUNKS * columns, 2 * NBIN), BF),
+            pltpu.VMEM((columns // slots * 2 * TILES, LANES), F32),
+            pltpu.VMEM((CHUNKS * columns // slots, 2 * NBIN), BF),
             pltpu.VMEM((parts,) + out, BF),
-        ],
+        ]
+        + [pltpu.VMEM((share, CHUNKS * columns // slots), F32)] * (slots - 1),
         compiler_params=pltpu.CompilerParams(vmem_limit_bytes=24 * 2**20),
         cost_estimate=expected(0.6 + 2.0 * slots),
         name="cross",
@@ -461,12 +486,16 @@
         block = placed_block(
             pieces, matrix[:, h * pairs : (h + 1) * pairs], slice(0, half), half
         )
-        store_rows(rows, block, h * half)
-        size = rows.shape[0] // 2
-        at = pl.ds(h * size, size)
-        copy = pltpu.make_async_copy(rows.at[at], out_hbm.at[at, number, 0], sems.at[h])
-        copy.start()
-        copies.append(copy)
+        size = rows.shape[0] // 4
+        for q in range(2):
+            lags = half // 2
+            store_rows(rows, block[q * lags : (q + 1) * lags], h * half + q * lags)
+            at = pl.ds((2 * h + q) * size, size)
+            copy = pltpu.make_async_copy(
+                rows.at[at], out_hbm.at[at, number, 0], sems.at[2 * h + q]
+            )
+            copy.start()
+            copies.append(copy)
     for copy in copies:
         copy.wait()
 
@@ -499,7 +528,7 @@
         out_shape=shape,
         in_specs=[smem, vmem, anywhere] + [vmem] * parts,
         out_specs=anywhere,
-        scratch_shapes=[pltpu.VMEM((share * tiles, LANES), F32), pltpu.SemaphoreType.DMA((2,))],
+        scratch_shapes=[pltpu.VMEM((share * tiles, LANES), F32), pltpu.SemaphoreType.DMA((4,))],
         input_output_aliases={2: 0},
         compiler_params=pltpu.CompilerParams(vmem_limit_bytes=16 * 2**20),
         cost_estimate=expected(0.05),

time: 51.6 us -> 52.9 us (1.025)
  Pallas kernels: 17.5 us -> 18.7 us
    pallas_call x3, Pallas kernels: 10.4 us -> 11.6 us  [cross_lags(): pl.pallas_call(functools.partial(cross_kernel, first_slot, slots, count,...]
  transfers between devices with their start and end apart: 26 -> 26, of which waited for: 11 -> 11; matrix products, arithmetic and copies ran while one was open for 0% -> 0% of each run, Pallas kernels for 25% -> 27%
where the time goes in v14:
time: 52.9 us; the launch traced here: 52.7 us
  starting transfers between devices  22.6 us (43%)
  Pallas kernels  18.7 us (35%)
  waiting for transfers between devices  11.2 us (21%)
    pallas_call x3, Pallas kernels, cross_lags(): pl.pallas_call(functools.partial(cross_kernel, first_slot, slots, count,...  11.6 us
    ppermute x15, starting transfers between devices, swap(): return lax.ppermute(value, 'seg', [(i, i ^ j) for i in range(parts)])  10.8 us
    ppermute x6, waiting for transfers between devices, up(): return lax.ppermute(value, 'sta', upward)  6.65 us
    ppermute x5, starting transfers between devices, down(): return lax.ppermute(value, 'sta', downward)  6.51 us
    ppermute x6, starting transfers between devices, up(): return lax.ppermute(value, 'sta', upward)  5.28 us
    ppermute x15, waiting for transfers between devices, swap(): return lax.ppermute(value, 'seg', [(i, i ^ j) for i in range(parts)])  3.98 us
    pallas_call x1, Pallas kernels, prepare(): pl.pallas_call(functools.partial(prep_kernel, parts, windows), out_shape=...  3.04 us
    pallas_call x1, Pallas kernels, place_lags(): pl.pallas_call(functools.partial(early_kernel, count, parts, tuple(groups...  2.14 us
  transfers between devices with their start and end apart: 26, of which 11 were waited for; matrix products, arithmetic and copies ran while one was open for 0% of the time, Pallas kernels for 27%

profile of v14, /device:TPU:0, one launch (start us, length us, event | category | flops | bytes accessed | tf_op | source)
XLA Modules:
  0.0 52.7 jit_solution(15946744489456983191)
XLA Ops:
  0.0 3.0 %prep.1 = (bf16[4,16,16,128]{3,2,1,0:T(8,128)(2,1)S(1)}, bf16[4,4,16,128]{3,2,1,0:T(8,128)(2,1)S(1)}, bf16[4,4,16,128]{3,2,1,0:T(8,128)(2,1)S(1)}, bf16[4,4,16,1...) custom-call(f32[1024,128]{1,0:T(8,128)} %bitcast.10, bf16[512,2048]{1,0:T(8,128)(2,1)} %constant.4.clone.table_hbm.table), custom_call_target="tpu_custom_call" | custom-call | flops 536870912 | bytes 3145728 | tf_op jit(solution)/shard_map/prep/pallas_call | solution.py:169
  3.0 0.5 collective-permute-start
  3.6 2.6 %collective-permute-start.6 = (bf16[4,4,16,128]{3,2,1,0:T(8,128)(2,1)S(1)}, bf16[4,4,16,128]{3,2,1,0:T(8,128)(2,1)S(1)}, u32[]{:S(2)}, u32[]{:S(2)}) collective-permute-start(bf16[4,4,16,128]{3,2,1,0:T(8,128)(2,1)S(1)} %get-tuple-element.45), channel_id=1, source_target_pairs={{0,2},{1,3},{2,0},{3,1},{4,6},{5,7},{6,4},{7,5},{8,10},{9,11},{10,... | collective-permute-start | bytes 196616 | tf_op jit(solution)/shard_map/ppermute | solution.py:567
  6.4 2.0 %collective-permute-start.2 = (bf16[8,4,16,128]{3,2,1,0:T(8,128)(2,1)S(1)}, bf16[8,4,16,128]{3,2,1,0:T(8,128)(2,1)S(1)}, u32[]{:S(2)}, u32[]{:S(2)}) collective-permute-start(bf16[8,4,16,128]{3,2,1,0:T(8,128)(2,1)S(1)} %constant_dynamic-update-slice_fusion), channel_id=1, source_target_pairs={{0,4},{8,0},{16,8},{24,16},{28,24},{20,28},{12,20},{4,12},{1,5},{9... | collective-permute-start | bytes 393224 | tf_op jit(solution)/shard_map/ppermute | solution.py:602
  8.5 0.3 collective-permute-done.6
  8.8 1.4 %collective-permute-done.7 = bf16[4,4,16,128]{3,2,1,0:T(8,128)(2,1)S(1)} collective-permute-done((bf16[4,4,16,128]{3,2,1,0:T(8,128)(2,1)S(1)}, bf16[4,4,16,128]{3,2,1,0:T(8,128)(2,1)S(1)}, u32[]{:S(2)}, u32[]{:S(2)}) %collective-permute-start.7) | collective-permute-done | bytes 65568 | tf_op jit(solution)/shard_map/ppermute | solution.py:567
  10.2 1.6 %collective-permute-start.9 = (bf16[8,4,16,128]{3,2,1,0:T(8,128)(2,1)S(1)}, bf16[8,4,16,128]{3,2,1,0:T(8,128)(2,1)S(1)}, u32[]{:S(2)}, u32[]{:S(2)}) collective-permute-start(bf16[8,4,16,128]{3,2,1,0:T(8,128)(2,1)S(1)} %pad_maximum_fusion), channel_id=1, source_target_pairs={{0,4},{8,0},{16,8},{24,16},{28,24},{20,28},{12,20},{4,12},{1,5},{9... | collective-permute-start | bytes 393224 | tf_op jit(solution)/shard_map/ppermute | solution.py:602
  11.8 0.5 collective-permute-start.8
  12.3 1.3 %collective-permute-start.12 = (bf16[4,16,16,128]{3,2,1,0:T(8,128)(2,1)S(1)}, bf16[4,16,16,128]{3,2,1,0:T(8,128)(2,1)S(1)}, u32[]{:S(2)}, u32[]{:S(2)}) collective-permute-start(bf16[4,16,16,128]{3,2,1,0:T(8,128)(2,1)S(1)} %get-tuple-element.54.refs_0_), channel_id=1, source_target_pairs={{0,2},{1,3},{2,0},{3,1},{4,6},{5,7},{6,4},{7,5},{8,10},{9,11},{10,... | collective-permute-start | bytes 786440 | tf_op jit(solution)/shard_map/ppermute | solution.py:567
  13.8 1.6 %collective-permute-start.4 = (bf16[8,4,16,128]{3,2,1,0:T(8,128)(2,1)S(1)}, bf16[8,4,16,128]{3,2,1,0:T(8,128)(2,1)S(1)}, u32[]{:S(2)}, u32[]{:S(2)}) collective-permute-start(bf16[8,4,16,128]{3,2,1,0:T(8,128)(2,1)S(1)} %collective-permute-done.1.rest_2_), channel_id=1, source_target_pairs={{0,8},{8,16},{16,24},{24,28},{28,20},{20,12},{12,4},{4,0},{1,9},{9... | collective-permute-start | bytes 393224 | tf_op jit(solution)/shard_map/ppermute | solution.py:599
  15.4 0.4 collective-permute-start.5
  15.9 0.3 collective-permute-done.9.rest_5_
  16.1 2.0 %collective-permute-done.8.rest_4_ = bf16[8,4,16,128]{3,2,1,0:T(8,128)(2,1)S(1)} collective-permute-done((bf16[8,4,16,128]{3,2,1,0:T(8,128)(2,1)S(1)}, bf16[8,4,16,128]{3,2,1,0:T(8,128)(2,1)S(1)}, u32[]{:S(2)}, u32[]{:S(2)}) %collective-permute-start.8) | collective-permute-done | bytes 131104 | tf_op jit(solution)/shard_map/ppermute | solution.py:599
  18.1 2.0 %collective-permute-start.11 = (bf16[8,4,16,128]{3,2,1,0:T(8,128)(2,1)S(1)}, bf16[8,4,16,128]{3,2,1,0:T(8,128)(2,1)S(1)}, u32[]{:S(2)}, u32[]{:S(2)}) collective-permute-start(bf16[8,4,16,128]{3,2,1,0:T(8,128)(2,1)S(1)} %collective-permute-done.9.rest_5_), channel_id=1, source_target_pairs={{0,4},{8,0},{16,8},{24,16},{28,24},{20,28},{12,20},{4,12},{1,5},{9... | collective-permute-start | bytes 393224 | tf_op jit(solution)/shard_map/ppermute | solution.py:602
  20.2 0.8 %collective-permute-done.4.refs_0_.rest_6_ = bf16[8,4,16,128]{3,2,1,0:T(8,128)(2,1)S(1)} collective-permute-done((bf16[8,4,16,128]{3,2,1,0:T(8,128)(2,1)S(1)}, bf16[8,4,16,128]{3,2,1,0:T(8,128)(2,1)S(1)}, u32[]{:S(2)}, u32[]{:S(2)}) %collective-permute-start.4) | collective-permute-done | bytes 131104 | tf_op jit(solution)/shard_map/ppermute | solution.py:599
  20.9 0.2 collective-permute-done.5.refs_1_.rest_7_
  21.1 2.0 %collective-permute-done.10.refs_2_.rest_8_ = bf16[8,4,16,128]{3,2,1,0:T(8,128)(2,1)S(1)} collective-permute-done((bf16[8,4,16,128]{3,2,1,0:T(8,128)(2,1)S(1)}, bf16[8,4,16,128]{3,2,1,0:T(8,128)(2,1)S(1)}, u32[]{:S(2)}, u32[]{:S(2)}) %collective-permute-start.10) | collective-permute-done | bytes 131104 | tf_op jit(solution)/shard_map/ppermute | solution.py:599
  23.3 1.6 %collective-permute-start.17 = (bf16[16,4,16,128]{3,2,1,0:T(8,128)(2,1)S(1)}, bf16[16,4,16,128]{3,2,1,0:T(8,128)(2,1)S(1)}, u32[]{:S(2)}, u32[]{:S(2)}) collective-permute-start(bf16[16,4,16,128]{3,2,1,0:T(8,128)(2,1)S(1)} %get-tuple-element.61), channel_id=1, source_target_pairs={{0,8},{8,16},{16,24},{24,28},{28,20},{20,12},{12,4},{4,0},{1,9},{9... | collective-permute-start | bytes 786440 | tf_op jit(solution)/shard_map/ppermute | solution.py:599
  25.0 0.5 collective-permute-start.18
  25.6 2.8 %cross.3 = (bf16[256,128]{1,0:T(8,128)(2,1)S(1)}, bf16[256,128]{1,0:T(8,128)(2,1)S(1)}, bf16[256,128]{1,0:T(8,128)(2,1)S(1)}, bf16[256,128]{1,0:T(8,128)(2,1)S(1)}) custom-call(s32[4,8]{1,0:T(4,128)S(1)} %copy-done.2, bf16[512,2048]{1,0:T(8,128)(2,1)S(1)} %copy-done, f32[4,3,8,4,8,128]{5,4,3,2,1,0:T(8,128)S(1)} %widen.2.rest_0_, ...), custom_call_target="tpu_custom_call" | custom-call | flops 2990000128 | bytes 1024 | tf_op jit(solution)/shard_map/cross/pallas_call | solution.py:398
  28.5 1.8 %collective-permute-start.15 = (bf16[256,128]{1,0:T(8,128)(2,1)S(1)}, bf16[256,128]{1,0:T(8,128)(2,1)S(1)}, u32[]{:S(2)}, u32[]{:S(2)}) collective-permute-start(bf16[256,128]{1,0:T(8,128)(2,1)S(1)} %get-tuple-element.58), channel_id=1, source_target_pairs={{0,2},{1,3},{2,0},{3,1},{4,6},{5,7},{6,4},{7,5},{8,10},{9,11},{10,... | collective-permute-start | bytes 196616 | tf_op jit(solution)/shard_map/ppermute | solution.py:567
  30.3 1.9 %collective-permute-done.17.rest_10_ = bf16[16,4,16,128]{3,2,1,0:T(8,128)(2,1)S(1)} collective-permute-done((bf16[16,4,16,128]{3,2,1,0:T(8,128)(2,1)S(1)}, bf16[16,4,16,128]{3,2,1,0:T(8,128)(2,1)S(1)}, u32[]{:S(2)}, u32[]{:S(2)}) %collective-permute-start.17) | collective-permute-done | bytes 262176 | tf_op jit(solution)/shard_map/ppermute | solution.py:599
  32.2 1.4 %collective-permute-start.22 = (bf16[16,4,16,128]{3,2,1,0:T(8,128)(2,1)S(1)}, bf16[16,4,16,128]{3,2,1,0:T(8,128)(2,1)S(1)}, u32[]{:S(2)}, u32[]{:S(2)}) collective-permute-start(bf16[16,4,16,128]{3,2,1,0:T(8,128)(2,1)S(1)} %collective-permute-done.17.rest_10_), channel_id=1, source_target_pairs={{0,8},{8,16},{16,24},{24,28},{28,20},{20,12},{12,4},{4,0},{1,9},{9... | collective-permute-start | bytes 786440 | tf_op jit(solution)/shard_map/ppermute | solution.py:599
  33.6 6.0 %cross.4 = (bf16[512,128]{1,0:T(8,128)(2,1)S(1)}, bf16[512,128]{1,0:T(8,128)(2,1)S(1)}, bf16[512,128]{1,0:T(8,128)(2,1)S(1)}, bf16[512,128]{1,0:T(8,128)(2,1)S(1)}) custom-call(s32[4,8]{1,0:T(4,128)S(1)} %copy-done.2, bf16[512,2048]{1,0:T(8,128)(2,1)S(1)} %copy-done, f32[4,3,8,4,8,128]{5,4,3,2,1,0:T(8,128)S(1)} %widen.2.rest_0_, ...), custom_call_target="tpu_custom_call" | custom-call | flops 5289999872 | bytes 1024 | tf_op jit(solution)/shard_map/cross/pallas_call | solution.py:398
  39.7 1.8 %collective-permute-start.20 = (bf16[512,128]{1,0:T(8,128)(2,1)S(1)}, bf16[512,128]{1,0:T(8,128)(2,1)S(1)}, u32[]{:S(2)}, u32[]{:S(2)}) collective-permute-start(bf16[512,128]{1,0:T(8,128)(2,1)S(1)} %get-tuple-element.65), channel_id=1, source_target_pairs={{0,2},{1,3},{2,0},{3,1},{4,6},{5,7},{6,4},{7,5},{8,10},{9,11},{10,... | collective-permute-start | bytes 393224 | tf_op jit(solution)/shard_map/ppermute | solution.py:567
  41.7 2.8 %cross.5 = (bf16[256,128]{1,0:T(8,128)(2,1)S(1)}, bf16[256,128]{1,0:T(8,128)(2,1)S(1)}, bf16[256,128]{1,0:T(8,128)(2,1)S(1)}, bf16[256,128]{1,0:T(8,128)(2,1)S(1)}) custom-call(s32[4,8]{1,0:T(4,128)S(1)} %copy-done.2, bf16[512,2048]{1,0:T(8,128)(2,1)S(1)} %copy-done, f32[4,3,8,4,8,128]{5,4,3,2,1,0:T(8,128)S(1)} %widen.2.rest_0_, ...), custom_call_target="tpu_custom_call" | custom-call | flops 2990000128 | bytes 1024 | tf_op jit(solution)/shard_map/cross/pallas_call | solution.py:398
  44.5 0.3 collective-permute-start.23
  44.8 1.8 %collective-permute-start.24 = (bf16[256,128]{1,0:T(8,128)(2,1)S(1)}, bf16[256,128]{1,0:T(8,128)(2,1)S(1)}, u32[]{:S(2)}, u32[]{:S(2)}) collective-permute-start(bf16[256,128]{1,0:T(8,128)(2,1)S(1)} %get-tuple-element.71), channel_id=1, source_target_pairs={{0,2},{1,3},{2,0},{3,1},{4,6},{5,7},{6,4},{7,5},{8,10},{9,11},{10,... | collective-permute-start | bytes 196616 | tf_op jit(solution)/shard_map/ppermute | solution.py:567
  46.6 1.6 %collective-permute-done.21.rest_7_ = bf16[512,128]{1,0:T(8,128)(2,1)S(1)} collective-permute-done((bf16[512,128]{1,0:T(8,128)(2,1)S(1)}, bf16[512,128]{1,0:T(8,128)(2,1)S(1)}, u32[]{:S(2)}, u32[]{:S(2)}) %collective-permute-start.21) | collective-permute-done | bytes 131104 | tf_op jit(solution)/shard_map/ppermute | solution.py:567
  48.2 2.1 %early.1 = f32[1024,4,1,128]{3,2,1,0:T(1,128)} custom-call(s32[4,8]{1,0:T(4,128)S(1)} %copy-done.2, bf16[4,128,512]{2,1,0:T(8,128)(2,1)S(1)} %copy-done.1, bf16[256,128]{1,0:T(8,128)(2,1)S(1)} %get-tuple-element.56.rest_0_, bf16[256,128]{1,0:T(8,128)(2,1)S(1)} %collective-permute-done.14.rest_1_, bf16[256,128]{1,0:T(8,128)(2,1)S(1)} %collective-permute-done.15.rest_2_, ...), custom_call_target="tpu_custom_call" | custom-call | flops 57500000 | bytes 1024 | tf_op jit(solution)/shard_map/early/pallas_call | solution.py:513
  50.4 0.7 %collective-permute-done.25.rest_3_ = bf16[256,128]{1,0:T(8,128)(2,1)S(1)} collective-permute-done((bf16[256,128]{1,0:T(8,128)(2,1)S(1)}, bf16[256,128]{1,0:T(8,128)(2,1)S(1)}, u32[]{:S(2)}, u32[]{:S(2)}) %collective-permute-start.25) | collective-permute-done | bytes 65568 | tf_op jit(solution)/shard_map/ppermute | solution.py:567
  51.1 1.7 %late.1 = f32[1024,4,1,128]{3,2,1,0:T(1,128)} custom-call(s32[4,8]{1,0:T(4,128)S(1)} %copy-done.2, bf16[4,128,512]{2,1,0:T(8,128)(2,1)S(1)} %copy-done.1, f32[1024,4,1,128]{3,2,1,0:T(1,128)} %early.1, bf16[256,128]{1,0:T(8,128)(2,1)S(1)} %get-tuple-element.69.rest_0_, ...), custom_call_target="tpu_custom_call", output_to_operand_aliasing={{}: (2, {})} | custom-call | flops 57500000 | bytes 1024 | tf_op jit(solution)/shard_map/late/pallas_call | solution.py:526
  (38 shorter events, 1.2 us)
Async XLA Ops:
  3.0 3.3 %collective-permute-start = (bf16[4,4,16,128]{3,2,1,0:T(8,128)(2,1)S(1)}, bf16[4,4,16,128]{3,2,1,0:T(8,128)(2,1)S(1)}, u32[]{:S(2)}, u32[]{:S(2)}) collective-permute-start(bf16[4,4,16,128]{3,2,1,0:T(8,128)(2,1)S(1)} %get-tuple-element.40), channel_id=1, source_target_pairs={{0,1},{1,0},{2,3},{3,2},{4,5},{5,4},{6,7},{7,6},{8,9},{9,8},{10,11... | collective-permute-start | bytes 196616 | tf_op jit(solution)/shard_map/ppermute | solution.py:567
  3.6 5.3 %collective-permute-start.6 = (bf16[4,4,16,128]{3,2,1,0:T(8,128)(2,1)S(1)}, bf16[4,4,16,128]{3,2,1,0:T(8,128)(2,1)S(1)}, u32[]{:S(2)}, u32[]{:S(2)}) collective-permute-start(bf16[4,4,16,128]{3,2,1,0:T(8,128)(2,1)S(1)} %get-tuple-element.45), channel_id=1, source_target_pairs={{0,2},{1,3},{2,0},{3,1},{4,6},{5,7},{6,4},{7,5},{8,10},{9,11},{10,... | collective-permute-start | bytes 196616 | tf_op jit(solution)/shard_map/ppermute | solution.py:567
  6.1 4.0 %collective-permute-start.7 = (bf16[4,4,16,128]{3,2,1,0:T(8,128)(2,1)S(1)}, bf16[4,4,16,128]{3,2,1,0:T(8,128)(2,1)S(1)}, u32[]{:S(2)}, u32[]{:S(2)}) collective-permute-start(bf16[4,4,16,128]{3,2,1,0:T(8,128)(2,1)S(1)} %get-tuple-element.46), channel_id=1, source_target_pairs={{0,3},{1,2},{2,1},{3,0},{4,7},{5,6},{6,5},{7,4},{8,11},{9,10},{10,... | collective-permute-start | bytes 196616 | tf_op jit(solution)/shard_map/ppermute | solution.py:567
  6.2 4.0 %collective-permute-start.3 = (bf16[4,16,16,128]{3,2,1,0:T(8,128)(2,1)S(1)}, bf16[4,16,16,128]{3,2,1,0:T(8,128)(2,1)S(1)}, u32[]{:S(2)}, u32[]{:S(2)}) collective-permute-start(bf16[4,16,16,128]{3,2,1,0:T(8,128)(2,1)S(1)} %get-tuple-element.54.refs_0_), channel_id=1, source_target_pairs={{0,1},{1,0},{2,3},{3,2},{4,5},{5,4},{6,7},{7,6},{8,9},{9,8},{10,11... | collective-permute-start | bytes 786440 | tf_op jit(solution)/shard_map/ppermute | solution.py:567
  6.4 7.4 %collective-permute-start.2 = (bf16[8,4,16,128]{3,2,1,0:T(8,128)(2,1)S(1)}, bf16[8,4,16,128]{3,2,1,0:T(8,128)(2,1)S(1)}, u32[]{:S(2)}, u32[]{:S(2)}) collective-permute-start(bf16[8,4,16,128]{3,2,1,0:T(8,128)(2,1)S(1)} %constant_dynamic-update-slice_fusion), channel_id=1, source_target_pairs={{0,4},{8,0},{16,8},{24,16},{28,24},{20,28},{12,20},{4,12},{1,5},{9... | collective-permute-start | bytes 393224 | tf_op jit(solution)/shard_map/ppermute | solution.py:602
  8.4 5.4 %collective-permute-start.1 = (bf16[8,4,16,128]{3,2,1,0:T(8,128)(2,1)S(1)}, bf16[8,4,16,128]{3,2,1,0:T(8,128)(2,1)S(1)}, u32[]{:S(2)}, u32[]{:S(2)}) collective-permute-start(bf16[8,4,16,128]{3,2,1,0:T(8,128)(2,1)S(1)} %constant_dynamic-update-slice_fusion), channel_id=1, source_target_pairs={{0,8},{8,16},{16,24},{24,28},{28,20},{20,12},{12,4},{4,0},{1,9},{9... | collective-permute-start | bytes 393224 | tf_op jit(solution)/shard_map/ppermute | solution.py:599
  10.2 15.4 %copy-start = (bf16[512,2048]{1,0:T(8,128)(2,1)S(1)}, bf16[512,2048]{1,0:T(8,128)(2,1)}, u32[]{:S(2)}) copy-start(bf16[512,2048]{1,0:T(8,128)(2,1)} %constant.4.clone.table_hbm.table) | copy-start | bytes 6291460
  10.2 15.4 %copy-start.2 = (s32[4,8]{1,0:T(4,128)S(1)}, s32[4,8]{1,0:T(4,128)}, u32[]{:S(2)}) copy-start(s32[4,8]{1,0:T(4,128)} %plan.9) | copy-start | bytes 388
  10.2 5.9 %collective-permute-start.9 = (bf16[8,4,16,128]{3,2,1,0:T(8,128)(2,1)S(1)}, bf16[8,4,16,128]{3,2,1,0:T(8,128)(2,1)S(1)}, u32[]{:S(2)}, u32[]{:S(2)}) collective-permute-start(bf16[8,4,16,128]{3,2,1,0:T(8,128)(2,1)S(1)} %pad_maximum_fusion), channel_id=1, source_target_pairs={{0,4},{8,0},{16,8},{24,16},{28,24},{20,28},{12,20},{4,12},{1,5},{9... | collective-permute-start | bytes 393224 | tf_op jit(solution)/shard_map/ppermute | solution.py:602
  11.8 6.3 %collective-permute-start.8 = (bf16[8,4,16,128]{3,2,1,0:T(8,128)(2,1)S(1)}, bf16[8,4,16,128]{3,2,1,0:T(8,128)(2,1)S(1)}, u32[]{:S(2)}, u32[]{:S(2)}) collective-permute-start(bf16[8,4,16,128]{3,2,1,0:T(8,128)(2,1)S(1)} %pad_maximum_fusion), channel_id=1, source_target_pairs={{0,8},{8,16},{16,24},{24,28},{28,20},{20,12},{12,4},{4,0},{1,9},{9... | collective-permute-start | bytes 393224 | tf_op jit(solution)/shard_map/ppermute | solution.py:599
  12.3 10.9 %collective-permute-start.12 = (bf16[4,16,16,128]{3,2,1,0:T(8,128)(2,1)S(1)}, bf16[4,16,16,128]{3,2,1,0:T(8,128)(2,1)S(1)}, u32[]{:S(2)}, u32[]{:S(2)}) collective-permute-start(bf16[4,16,16,128]{3,2,1,0:T(8,128)(2,1)S(1)} %get-tuple-element.54.refs_0_), channel_id=1, source_target_pairs={{0,2},{1,3},{2,0},{3,1},{4,6},{5,7},{6,4},{7,5},{8,10},{9,11},{10,... | collective-permute-start | bytes 786440 | tf_op jit(solution)/shard_map/ppermute | solution.py:567
  13.8 7.1 %collective-permute-start.4 = (bf16[8,4,16,128]{3,2,1,0:T(8,128)(2,1)S(1)}, bf16[8,4,16,128]{3,2,1,0:T(8,128)(2,1)S(1)}, u32[]{:S(2)}, u32[]{:S(2)}) collective-permute-start(bf16[8,4,16,128]{3,2,1,0:T(8,128)(2,1)S(1)} %collective-permute-done.1.rest_2_), channel_id=1, source_target_pairs={{0,8},{8,16},{16,24},{24,28},{28,20},{20,12},{12,4},{4,0},{1,9},{9... | collective-permute-start | bytes 393224 | tf_op jit(solution)/shard_map/ppermute | solution.py:599
  15.4 5.7 %collective-permute-start.5 = (bf16[8,4,16,128]{3,2,1,0:T(8,128)(2,1)S(1)}, bf16[8,4,16,128]{3,2,1,0:T(8,128)(2,1)S(1)}, u32[]{:S(2)}, u32[]{:S(2)}) collective-permute-start(bf16[8,4,16,128]{3,2,1,0:T(8,128)(2,1)S(1)} %collective-permute-done.2.rest_3_), channel_id=1, source_target_pairs={{0,4},{8,0},{16,8},{24,16},{28,24},{20,28},{12,20},{4,12},{1,5},{9... | collective-permute-start | bytes 393224 | tf_op jit(solution)/shard_map/ppermute | solution.py:602
  18.1 5.0 %collective-permute-start.10 = (bf16[8,4,16,128]{3,2,1,0:T(8,128)(2,1)S(1)}, bf16[8,4,16,128]{3,2,1,0:T(8,128)(2,1)S(1)}, u32[]{:S(2)}, u32[]{:S(2)}) collective-permute-start(bf16[8,4,16,128]{3,2,1,0:T(8,128)(2,1)S(1)} %collective-permute-done.8.rest_4_), channel_id=1, source_target_pairs={{0,8},{8,16},{16,24},{24,28},{28,20},{20,12},{12,4},{4,0},{1,9},{9... | collective-permute-start | bytes 393224 | tf_op jit(solution)/shard_map/ppermute | solution.py:599
  18.1 5.1 %collective-permute-start.11 = (bf16[8,4,16,128]{3,2,1,0:T(8,128)(2,1)S(1)}, bf16[8,4,16,128]{3,2,1,0:T(8,128)(2,1)S(1)}, u32[]{:S(2)}, u32[]{:S(2)}) collective-permute-start(bf16[8,4,16,128]{3,2,1,0:T(8,128)(2,1)S(1)} %collective-permute-done.9.rest_5_), channel_id=1, source_target_pairs={{0,4},{8,0},{16,8},{24,16},{28,24},{20,28},{12,20},{4,12},{1,5},{9... | collective-permute-start | bytes 393224 | tf_op jit(solution)/shard_map/ppermute | solution.py:602
  23.3 2.2 %collective-permute-start.13 = (bf16[4,16,16,128]{3,2,1,0:T(8,128)(2,1)S(1)}, bf16[4,16,16,128]{3,2,1,0:T(8,128)(2,1)S(1)}, u32[]{:S(2)}, u32[]{:S(2)}) collective-permute-start(bf16[4,16,16,128]{3,2,1,0:T(8,128)(2,1)S(1)} %collective-permute-done.12.refs_0_), channel_id=1, source_target_pairs={{0,1},{1,0},{2,3},{3,2},{4,5},{5,4},{6,7},{7,6},{8,9},{9,8},{10,11... | collective-permute-start | bytes 786440 | tf_op jit(solution)/shard_map/ppermute | solution.py:567
  23.3 8.9 %collective-permute-start.17 = (bf16[16,4,16,128]{3,2,1,0:T(8,128)(2,1)S(1)}, bf16[16,4,16,128]{3,2,1,0:T(8,128)(2,1)S(1)}, u32[]{:S(2)}, u32[]{:S(2)}) collective-permute-start(bf16[16,4,16,128]{3,2,1,0:T(8,128)(2,1)S(1)} %get-tuple-element.61), channel_id=1, source_target_pairs={{0,8},{8,16},{16,24},{24,28},{28,20},{20,12},{12,4},{4,0},{1,9},{9... | collective-permute-start | bytes 786440 | tf_op jit(solution)/shard_map/ppermute | solution.py:599
  25.0 8.7 %collective-permute-start.18 = (bf16[16,4,16,128]{3,2,1,0:T(8,128)(2,1)S(1)}, bf16[16,4,16,128]{3,2,1,0:T(8,128)(2,1)S(1)}, u32[]{:S(2)}, u32[]{:S(2)}) collective-permute-start(bf16[16,4,16,128]{3,2,1,0:T(8,128)(2,1)S(1)} %get-tuple-element.62), channel_id=1, source_target_pairs={{0,4},{8,0},{16,8},{24,16},{28,24},{20,28},{12,20},{4,12},{1,5},{9... | collective-permute-start | bytes 786440 | tf_op jit(solution)/shard_map/ppermute | solution.py:602
  28.4 11.3 %collective-permute-start.14 = (bf16[256,128]{1,0:T(8,128)(2,1)S(1)}, bf16[256,128]{1,0:T(8,128)(2,1)S(1)}, u32[]{:S(2)}, u32[]{:S(2)}) collective-permute-start(bf16[256,128]{1,0:T(8,128)(2,1)S(1)} %get-tuple-element.57), channel_id=1, source_target_pairs={{0,1},{1,0},{2,3},{3,2},{4,5},{5,4},{6,7},{7,6},{8,9},{9,8},{10,11... | collective-permute-start | bytes 196616 | tf_op jit(solution)/shard_map/ppermute | solution.py:567
  28.5 13.1 %collective-permute-start.15 = (bf16[256,128]{1,0:T(8,128)(2,1)S(1)}, bf16[256,128]{1,0:T(8,128)(2,1)S(1)}, u32[]{:S(2)}, u32[]{:S(2)}) collective-permute-start(bf16[256,128]{1,0:T(8,128)(2,1)S(1)} %get-tuple-element.58), channel_id=1, source_target_pairs={{0,2},{1,3},{2,0},{3,1},{4,6},{5,7},{6,4},{7,5},{8,10},{9,11},{10,... | collective-permute-start | bytes 196616 | tf_op jit(solution)/shard_map/ppermute | solution.py:567
  30.3 11.4 %collective-permute-start.16 = (bf16[256,128]{1,0:T(8,128)(2,1)S(1)}, bf16[256,128]{1,0:T(8,128)(2,1)S(1)}, u32[]{:S(2)}, u32[]{:S(2)}) collective-permute-start(bf16[256,128]{1,0:T(8,128)(2,1)S(1)} %get-tuple-element.59), channel_id=1, source_target_pairs={{0,3},{1,2},{2,1},{3,0},{4,7},{5,6},{6,5},{7,4},{8,11},{9,10},{10,... | collective-permute-start | bytes 196616 | tf_op jit(solution)/shard_map/ppermute | solution.py:567
  32.2 9.4 %collective-permute-start.22 = (bf16[16,4,16,128]{3,2,1,0:T(8,128)(2,1)S(1)}, bf16[16,4,16,128]{3,2,1,0:T(8,128)(2,1)S(1)}, u32[]{:S(2)}, u32[]{:S(2)}) collective-permute-start(bf16[16,4,16,128]{3,2,1,0:T(8,128)(2,1)S(1)} %collective-permute-done.17.rest_10_), channel_id=1, source_target_pairs={{0,8},{8,16},{16,24},{24,28},{28,20},{20,12},{12,4},{4,0},{1,9},{9... | collective-permute-start | bytes 786440 | tf_op jit(solution)/shard_map/ppermute | solution.py:599
  39.6 7.0 %collective-permute-start.19 = (bf16[512,128]{1,0:T(8,128)(2,1)S(1)}, bf16[512,128]{1,0:T(8,128)(2,1)S(1)}, u32[]{:S(2)}, u32[]{:S(2)}) collective-permute-start(bf16[512,128]{1,0:T(8,128)(2,1)S(1)} %get-tuple-element.64), channel_id=1, source_target_pairs={{0,1},{1,0},{2,3},{3,2},{4,5},{5,4},{6,7},{7,6},{8,9},{9,8},{10,11... | collective-permute-start | bytes 393224 | tf_op jit(solution)/shard_map/ppermute | solution.py:567
  39.7 6.9 %collective-permute-start.20 = (bf16[512,128]{1,0:T(8,128)(2,1)S(1)}, bf16[512,128]{1,0:T(8,128)(2,1)S(1)}, u32[]{:S(2)}, u32[]{:S(2)}) collective-permute-start(bf16[512,128]{1,0:T(8,128)(2,1)S(1)} %get-tuple-element.65), channel_id=1, source_target_pairs={{0,2},{1,3},{2,0},{3,1},{4,6},{5,7},{6,4},{7,5},{8,10},{9,11},{10,... | collective-permute-start | bytes 393224 | tf_op jit(solution)/shard_map/ppermute | solution.py:567
  41.6 6.6 %collective-permute-start.21 = (bf16[512,128]{1,0:T(8,128)(2,1)S(1)}, bf16[512,128]{1,0:T(8,128)(2,1)S(1)}, u32[]{:S(2)}, u32[]{:S(2)}) collective-permute-start(bf16[512,128]{1,0:T(8,128)(2,1)S(1)} %get-tuple-element.66), channel_id=1, source_target_pairs={{0,3},{1,2},{2,1},{3,0},{4,7},{5,6},{6,5},{7,4},{8,11},{9,10},{10,... | collective-permute-start | bytes 393224 | tf_op jit(solution)/shard_map/ppermute | solution.py:567
  41.7 6.5 %copy-start.1 = (bf16[4,128,512]{2,1,0:T(8,128)(2,1)S(1)}, bf16[4,128,512]{2,1,0:T(8,128)(2,1)}, u32[]{:S(2)}) copy-start(bf16[4,128,512]{2,1,0:T(8,128)(2,1)} %constant.5.clone.place) | copy-start | bytes 1572868
  44.5 5.8 %collective-permute-start.23 = (bf16[256,128]{1,0:T(8,128)(2,1)S(1)}, bf16[256,128]{1,0:T(8,128)(2,1)S(1)}, u32[]{:S(2)}, u32[]{:S(2)}) collective-permute-start(bf16[256,128]{1,0:T(8,128)(2,1)S(1)} %get-tuple-element.70), channel_id=1, source_target_pairs={{0,1},{1,0},{2,3},{3,2},{4,5},{5,4},{6,7},{7,6},{8,9},{9,8},{10,11... | collective-permute-start | bytes 196616 | tf_op jit(solution)/shard_map/ppermute | solution.py:567
  44.8 5.5 %collective-permute-start.24 = (bf16[256,128]{1,0:T(8,128)(2,1)S(1)}, bf16[256,128]{1,0:T(8,128)(2,1)S(1)}, u32[]{:S(2)}, u32[]{:S(2)}) collective-permute-start(bf16[256,128]{1,0:T(8,128)(2,1)S(1)} %get-tuple-element.71), channel_id=1, source_target_pairs={{0,2},{1,3},{2,0},{3,1},{4,6},{5,7},{6,4},{7,5},{8,10},{9,11},{10,... | collective-permute-start | bytes 196616 | tf_op jit(solution)/shard_map/ppermute | solution.py:567
  46.6 4.5 %collective-permute-start.25 = (bf16[256,128]{1,0:T(8,128)(2,1)S(1)}, bf16[256,128]{1,0:T(8,128)(2,1)S(1)}, u32[]{:S(2)}, u32[]{:S(2)}) collective-permute-start(bf16[256,128]{1,0:T(8,128)(2,1)S(1)} %get-tuple-element.72), channel_id=1, source_target_pairs={{0,3},{1,2},{2,1},{3,0},{4,7},{5,6},{6,5},{7,4},{8,11},{9,10},{10,... | collective-permute-start | bytes 196616 | tf_op jit(solution)/shard_map/ppermute | solution.py:567

commit v15 on v12

--- a/solution.py
+++ b/solution.py
@@ -338,25 +338,10 @@
             rows = slice(q * columns, (q + 1) * columns)
             operand[rows, at] = turned[q][0].astype(BF)
             operand[rows, at_imag] = turned[q][1].astype(BF)
-    block = lax.dot_general(
-        table[...], operand[...], (((1,), (1,)), ((), ())), preferred_element_type=F32
-    )
+    block = jnp.dot(operand[...], table[...], preferred_element_type=F32)
     block = block * (2.0 * scaling)
-    if slots == 1:
-        half = table.shape[0] // 2
-        low_lanes = lax.broadcasted_iota(jnp.int32, (half, LANES), 1) < width
-        for p in range(CHUNKS // 2):
-            at = slice(p * LANES, (p + 1) * LANES)
-            low, high = block[:half, at], block[half:, at]
-            pair = (
-                jnp.where(low_lanes, low, pltpu.roll(high, width, 1)),
-                jnp.where(low_lanes, pltpu.roll(low, width, 1), high),
-            )
-            for second in range(2):
-                result[2 * p + second] = pair[second].astype(BF)
-    else:
-        for q in range(CHUNKS):
-            result[q] = block[:, q * columns : (q + 1) * columns].astype(BF)
+    for q in range(CHUNKS):
+        result[q] = block[q * columns : (q + 1) * columns].astype(BF)
     me = lax.axis_index("seg")
     for j in range(parts):
         outs[j][...] = result[me ^ j]
@@ -367,7 +352,7 @@
     quarter = candidates[0].shape[1]
     columns = slots * stations * quarter
     share = LAGS // parts
-    out = (share, columns) if slots > 1 else (share // 2, 2 * columns)
+    out = (columns, share)
     smem = pl.BlockSpec(memory_space=pltpu.SMEM)
     vmem = pl.BlockSpec(memory_space=pltpu.VMEM)
     operands = [table, *owns, *candidates]
@@ -401,18 +386,17 @@
     return rounds
 
 
-def placed_block(pieces, matrix, at, half):
-    joined = jnp.concatenate([piece[at, :] for piece in pieces], axis=1)
-    if pieces[0].shape[0] > half:
-        later = slice(half + at.start, half + at.stop)
-        high = jnp.concatenate([piece[later, :] for piece in pieces], axis=1)
-        joined = jnp.concatenate([joined, high], axis=0)
-    return jnp.dot(joined, matrix, preferred_element_type=F32)
-
-
-def joined_matrix(place, parts):
+def placed_block(pieces, matrix, at):
+    joined = jnp.concatenate([piece[:, at] for piece in pieces], axis=0)
+    return lax.dot_general(
+        joined, matrix, (((0,), (0,)), ((), ())), preferred_element_type=F32
+    )
+
+
+def joined_matrix(place, parts, slots):
     me = lax.axis_index("seg")
-    return jnp.concatenate([place[me ^ j] for j in range(parts)], axis=0)
+    rows, columns = place.shape[1] * slots // 2, place.shape[2] * slots // 2
+    return jnp.concatenate([place[me ^ j, :rows, :columns] for j in range(parts)], axis=0)
 
 
 def store_rows(rows, block, first):
@@ -422,25 +406,18 @@
         rows[at, :] = block[:, tile * LANES : (tile + 1) * LANES]
 
 
-def early_kernel(count, parts, groups, half, plan, place, *rest):
+def early_kernel(count, parts, groups, plan, place, *rest):
     pieces = rest[:-3]
     out_hbm, rows, sems = rest[-3:]
     pairs = place.shape[2] // 2
     rounds = slot_rounds(plan, count)
-    matrix = joined_matrix(place, parts)
-    at = slice(0, half)
     copies = []
     for index, (first_slot, slots) in enumerate(groups):
-        block = placed_block(pieces[index * parts : (index + 1) * parts], matrix, at, half)
+        own = pieces[index * parts : (index + 1) * parts]
+        block = placed_block(own, joined_matrix(place, parts, slots), slice(None))
         for slot in range(slots):
-            if slots == 1:
-                low, high = block[:, :pairs], block[:, pairs:]
-            else:
-                columns = slice(slot * pairs, (slot + 1) * pairs)
-                low, high = block[:half, columns], block[half:, columns]
             number = first_slot + slot
-            store_rows(rows.at[number], low, 0)
-            store_rows(rows.at[number], high, half)
+            store_rows(rows.at[number], block[:, slot * pairs : (slot + 1) * pairs], 0)
             copy = pltpu.make_async_copy(
                 rows.at[number], out_hbm.at[:, rounds[number], 0], sems.at[number]
             )
@@ -450,19 +427,17 @@
         copy.wait()
 
 
-def late_kernel(count, parts, half, plan, place, early, *rest):
+def late_kernel(count, parts, plan, place, early, *rest):
     pieces = rest[:parts]
     out_hbm, rows, sems = rest[parts:]
-    pairs = place.shape[2] // 2
     number = slot_rounds(plan, count)[ROUNDS - 1]
-    matrix = joined_matrix(place, parts)
+    matrix = joined_matrix(place, parts, 1)
+    half = pieces[0].shape[1] // 2
+    size = rows.shape[0] // 2
     copies = []
     for h in range(2):
-        block = placed_block(
-            pieces, matrix[:, h * pairs : (h + 1) * pairs], slice(0, half), half
-        )
+        block = placed_block(pieces, matrix, slice(h * half, (h + 1) * half))
         store_rows(rows, block, h * half)
-        size = rows.shape[0] // 2
         at = pl.ds(h * size, size)
         copy = pltpu.make_async_copy(rows.at[at], out_hbm.at[at, number, 0], sems.at[h])
         copy.start()
@@ -474,7 +449,6 @@
 def place_lags(plan, groups, pieces, count, stations, parts):
     pairs = stations * stations
     share = LAGS // parts
-    half = share // 2
     tiles = pairs // LANES
     place = jnp.asarray(make_placing(stations, stations // parts, parts))
     smem = pl.BlockSpec(memory_space=pltpu.SMEM)
@@ -482,7 +456,7 @@
     anywhere = pl.BlockSpec(memory_space=pl.ANY)
     shape = jax.ShapeDtypeStruct((share * tiles, ROUNDS, 1, LANES), F32)
     early = pl.pallas_call(
-        functools.partial(early_kernel, count, parts, tuple(groups[:-1]), half),
+        functools.partial(early_kernel, count, parts, tuple(groups[:-1])),
         out_shape=shape,
         in_specs=[smem] + [vmem] * (1 + len(pieces) - parts),
         out_specs=anywhere,
@@ -495,7 +469,7 @@
         name="early",
     )(plan, place, *pieces[:-parts])
     out = pl.pallas_call(
-        functools.partial(late_kernel, count, parts, half),
+        functools.partial(late_kernel, count, parts),
         out_shape=shape,
         in_specs=[smem, vmem, anywhere] + [vmem] * parts,
         out_specs=anywhere,
@@ -551,7 +525,8 @@
     count = lax.axis_size("sta")
     parts = lax.axis_size("seg")
     quarter = stations // parts
-    table = jnp.asarray(make_table(length // CHUNKS, 2 * length))
+    constants = make_table(length // CHUNKS, 2 * length)
+    table, lag_table = jnp.asarray(constants), jnp.asarray(constants.T.copy())
     scaling = 1.0 / math.sqrt(4.0 * NBIN * windows * parts)
 
     white, *quarters = prepare(records, table, parts)
@@ -613,7 +588,7 @@
             near_own = after(near_own, lags)
         at, values = arrived[index - len(groups)]
         lags = cross_lags(
-            plan, table, [near_own, far_own], at, values, first_slot, slots, count, parts, scaling
+            plan, lag_table, [near_own, far_own], at, values, first_slot, slots, count, parts, scaling
         )
         pieces = pieces + exchange(lags)
     return place_lags(plan, groups, pieces, count, stations, parts)

time: 51.6 us -> 51.3 us (level)
  transfers between devices with their start and end apart: 26 -> 26, of which waited for: 11 -> 12; matrix products, arithmetic and copies ran while one was open for 0% -> 0% of each run, Pallas kernels for 25% -> 24%
where the time goes in v15:
time: 51.3 us; the launch traced here: 51.1 us
  starting transfers between devices  22.4 us (44%)
  Pallas kernels  17 us (33%)
  waiting for transfers between devices  11.5 us (22%)
    ppermute x15, starting transfers between devices, swap(): return lax.ppermute(value, 'seg', [(i, i ^ j) for i in range(parts)])  10.6 us
    pallas_call x3, Pallas kernels, cross_lags(): pl.pallas_call(functools.partial(cross_kernel, first_slot, slots, count,...  9.97 us
    ppermute x6, waiting for transfers between devices, up(): return lax.ppermute(value, 'sta', upward)  6.88 us
    ppermute x5, starting transfers between devices, down(): return lax.ppermute(value, 'sta', downward)  6.51 us
    ppermute x6, starting transfers between devices, up(): return lax.ppermute(value, 'sta', upward)  5.28 us
    ppermute x15, waiting for transfers between devices, swap(): return lax.ppermute(value, 'seg', [(i, i ^ j) for i in range(parts)])  4.02 us
    pallas_call x1, Pallas kernels, prepare(): pl.pallas_call(functools.partial(prep_kernel, parts, windows), out_shape=...  3.04 us
    pallas_call x1, Pallas kernels, place_lags(): pl.pallas_call(functools.partial(early_kernel, count, parts, tuple(groups...  2.1 us
  transfers between devices with their start and end apart: 26, of which 12 were waited for; matrix products, arithmetic and copies ran while one was open for 0% of the time, Pallas kernels for 24%

profile of v15, /device:TPU:0, one launch (start us, length us, event | category | flops | bytes accessed | tf_op | source)
XLA Modules:
  0.0 51.1 jit_solution(4656579344863385341)
XLA Ops:
  0.0 3.0 %prep.1 = (bf16[4,16,16,128]{3,2,1,0:T(8,128)(2,1)S(1)}, bf16[4,4,16,128]{3,2,1,0:T(8,128)(2,1)S(1)}, bf16[4,4,16,128]{3,2,1,0:T(8,128)(2,1)S(1)}, bf16[4,4,16,1...) custom-call(f32[1024,128]{1,0:T(8,128)} %bitcast.10, bf16[512,2048]{1,0:T(8,128)(2,1)} %constant.6.clone.table_hbm), custom_call_target="tpu_custom_call" | custom-call | flops 536870912 | bytes 3145728 | tf_op jit(solution)/shard_map/prep/pallas_call | solution.py:169
  3.0 0.5 %collective-permute-start = (bf16[4,4,16,128]{3,2,1,0:T(8,128)(2,1)S(1)}, bf16[4,4,16,128]{3,2,1,0:T(8,128)(2,1)S(1)}, u32[]{:S(2)}, u32[]{:S(2)}) collective-permute-start(bf16[4,4,16,128]{3,2,1,0:T(8,128)(2,1)S(1)} %get-tuple-element.40), channel_id=1, source_target_pairs={{0,1},{1,0},{2,3},{3,2},{4,5},{5,4},{6,7},{7,6},{8,9},{9,8},{10,11... | collective-permute-start | bytes 196616 | tf_op jit(solution)/shard_map/ppermute | solution.py:512
  3.6 2.6 %collective-permute-start.6 = (bf16[4,4,16,128]{3,2,1,0:T(8,128)(2,1)S(1)}, bf16[4,4,16,128]{3,2,1,0:T(8,128)(2,1)S(1)}, u32[]{:S(2)}, u32[]{:S(2)}) collective-permute-start(bf16[4,4,16,128]{3,2,1,0:T(8,128)(2,1)S(1)} %get-tuple-element.45), channel_id=1, source_target_pairs={{0,2},{1,3},{2,0},{3,1},{4,6},{5,7},{6,4},{7,5},{8,10},{9,11},{10,... | collective-permute-start | bytes 196616 | tf_op jit(solution)/shard_map/ppermute | solution.py:512
  6.4 2.0 %collective-permute-start.2 = (bf16[8,4,16,128]{3,2,1,0:T(8,128)(2,1)S(1)}, bf16[8,4,16,128]{3,2,1,0:T(8,128)(2,1)S(1)}, u32[]{:S(2)}, u32[]{:S(2)}) collective-permute-start(bf16[8,4,16,128]{3,2,1,0:T(8,128)(2,1)S(1)} %constant_dynamic-update-slice_fusion), channel_id=1, source_target_pairs={{0,4},{8,0},{16,8},{24,16},{28,24},{20,28},{12,20},{4,12},{1,5},{9... | collective-permute-start | bytes 393224 | tf_op jit(solution)/shard_map/ppermute | solution.py:548
  8.5 0.3 collective-permute-done.6
  8.8 1.4 %collective-permute-done.7 = bf16[4,4,16,128]{3,2,1,0:T(8,128)(2,1)S(1)} collective-permute-done((bf16[4,4,16,128]{3,2,1,0:T(8,128)(2,1)S(1)}, bf16[4,4,16,128]{3,2,1,0:T(8,128)(2,1)S(1)}, u32[]{:S(2)}, u32[]{:S(2)}) %collective-permute-start.7) | collective-permute-done | bytes 65568 | tf_op jit(solution)/shard_map/ppermute | solution.py:512
  10.2 1.6 %collective-permute-start.9 = (bf16[8,4,16,128]{3,2,1,0:T(8,128)(2,1)S(1)}, bf16[8,4,16,128]{3,2,1,0:T(8,128)(2,1)S(1)}, u32[]{:S(2)}, u32[]{:S(2)}) collective-permute-start(bf16[8,4,16,128]{3,2,1,0:T(8,128)(2,1)S(1)} %pad_maximum_fusion), channel_id=1, source_target_pairs={{0,4},{8,0},{16,8},{24,16},{28,24},{20,28},{12,20},{4,12},{1,5},{9... | collective-permute-start | bytes 393224 | tf_op jit(solution)/shard_map/ppermute | solution.py:548
  11.8 0.5 collective-permute-start.8
  12.3 1.3 %collective-permute-start.12 = (bf16[4,16,16,128]{3,2,1,0:T(8,128)(2,1)S(1)}, bf16[4,16,16,128]{3,2,1,0:T(8,128)(2,1)S(1)}, u32[]{:S(2)}, u32[]{:S(2)}) collective-permute-start(bf16[4,16,16,128]{3,2,1,0:T(8,128)(2,1)S(1)} %get-tuple-element.54.refs_0_), channel_id=1, source_target_pairs={{0,2},{1,3},{2,0},{3,1},{4,6},{5,7},{6,4},{7,5},{8,10},{9,11},{10,... | collective-permute-start | bytes 786440 | tf_op jit(solution)/shard_map/ppermute | solution.py:512
  13.8 1.6 %collective-permute-start.4 = (bf16[8,4,16,128]{3,2,1,0:T(8,128)(2,1)S(1)}, bf16[8,4,16,128]{3,2,1,0:T(8,128)(2,1)S(1)}, u32[]{:S(2)}, u32[]{:S(2)}) collective-permute-start(bf16[8,4,16,128]{3,2,1,0:T(8,128)(2,1)S(1)} %collective-permute-done.1.rest_2_), channel_id=1, source_target_pairs={{0,8},{8,16},{16,24},{24,28},{28,20},{20,12},{12,4},{4,0},{1,9},{9... | collective-permute-start | bytes 393224 | tf_op jit(solution)/shard_map/ppermute | solution.py:545
  15.4 0.4 collective-permute-start.5
  15.9 0.3 collective-permute-done.9.rest_5_
  16.1 2.0 %collective-permute-done.8.rest_4_ = bf16[8,4,16,128]{3,2,1,0:T(8,128)(2,1)S(1)} collective-permute-done((bf16[8,4,16,128]{3,2,1,0:T(8,128)(2,1)S(1)}, bf16[8,4,16,128]{3,2,1,0:T(8,128)(2,1)S(1)}, u32[]{:S(2)}, u32[]{:S(2)}) %collective-permute-start.8) | collective-permute-done | bytes 131104 | tf_op jit(solution)/shard_map/ppermute | solution.py:545
  18.1 2.0 %collective-permute-start.11 = (bf16[8,4,16,128]{3,2,1,0:T(8,128)(2,1)S(1)}, bf16[8,4,16,128]{3,2,1,0:T(8,128)(2,1)S(1)}, u32[]{:S(2)}, u32[]{:S(2)}) collective-permute-start(bf16[8,4,16,128]{3,2,1,0:T(8,128)(2,1)S(1)} %collective-permute-done.9.rest_5_), channel_id=1, source_target_pairs={{0,4},{8,0},{16,8},{24,16},{28,24},{20,28},{12,20},{4,12},{1,5},{9... | collective-permute-start | bytes 393224 | tf_op jit(solution)/shard_map/ppermute | solution.py:548
  20.2 0.8 %collective-permute-done.4.refs_0_.rest_6_ = bf16[8,4,16,128]{3,2,1,0:T(8,128)(2,1)S(1)} collective-permute-done((bf16[8,4,16,128]{3,2,1,0:T(8,128)(2,1)S(1)}, bf16[8,4,16,128]{3,2,1,0:T(8,128)(2,1)S(1)}, u32[]{:S(2)}, u32[]{:S(2)}) %collective-permute-start.4) | collective-permute-done | bytes 131104 | tf_op jit(solution)/shard_map/ppermute | solution.py:545
  20.9 0.2 collective-permute-done.5.refs_1_.rest_7_
  21.1 2.0 %collective-permute-done.10.refs_2_.rest_8_ = bf16[8,4,16,128]{3,2,1,0:T(8,128)(2,1)S(1)} collective-permute-done((bf16[8,4,16,128]{3,2,1,0:T(8,128)(2,1)S(1)}, bf16[8,4,16,128]{3,2,1,0:T(8,128)(2,1)S(1)}, u32[]{:S(2)}, u32[]{:S(2)}) %collective-permute-start.10) | collective-permute-done | bytes 131104 | tf_op jit(solution)/shard_map/ppermute | solution.py:545
  23.3 1.6 %collective-permute-start.17 = (bf16[16,4,16,128]{3,2,1,0:T(8,128)(2,1)S(1)}, bf16[16,4,16,128]{3,2,1,0:T(8,128)(2,1)S(1)}, u32[]{:S(2)}, u32[]{:S(2)}) collective-permute-start(bf16[16,4,16,128]{3,2,1,0:T(8,128)(2,1)S(1)} %get-tuple-element.61), channel_id=1, source_target_pairs={{0,8},{8,16},{16,24},{24,28},{28,20},{20,12},{12,4},{4,0},{1,9},{9... | collective-permute-start | bytes 786440 | tf_op jit(solution)/shard_map/ppermute | solution.py:545
  25.0 0.5 collective-permute-start.18
  25.6 2.7 %cross.3 = (bf16[64,512]{1,0:T(8,128)(2,1)S(1)}, bf16[64,512]{1,0:T(8,128)(2,1)S(1)}, bf16[64,512]{1,0:T(8,128)(2,1)S(1)}, bf16[64,512]{1,0:T(8,128)(2,1)S(1)}) custom-call(s32[4,8]{1,0:T(4,128)S(1)} %copy-done.1, bf16[2048,512]{1,0:T(8,128)(2,1)S(1)} %copy-done.2, f32[4,3,8,4,8,128]{5,4,3,2,1,0:T(8,128)S(1)} %widen.2.rest_0_, ...), custom_call_target="tpu_custom_call" | custom-call | flops 2990000128 | bytes 1024 | tf_op jit(solution)/shard_map/cross/pallas_call | solution.py:359
  28.4 1.7 %collective-permute-start.15 = (bf16[64,512]{1,0:T(8,128)(2,1)S(1)}, bf16[64,512]{1,0:T(8,128)(2,1)S(1)}, u32[]{:S(2)}, u32[]{:S(2)}) collective-permute-start(bf16[64,512]{1,0:T(8,128)(2,1)S(1)} %get-tuple-element.58), channel_id=1, source_target_pairs={{0,2},{1,3},{2,0},{3,1},{4,6},{5,7},{6,4},{7,5},{8,10},{9,11},{10,... | collective-permute-start | bytes 196616 | tf_op jit(solution)/shard_map/ppermute | solution.py:512
  30.2 2.0 %collective-permute-done.17.rest_10_ = bf16[16,4,16,128]{3,2,1,0:T(8,128)(2,1)S(1)} collective-permute-done((bf16[16,4,16,128]{3,2,1,0:T(8,128)(2,1)S(1)}, bf16[16,4,16,128]{3,2,1,0:T(8,128)(2,1)S(1)}, u32[]{:S(2)}, u32[]{:S(2)}) %collective-permute-start.17) | collective-permute-done | bytes 262176 | tf_op jit(solution)/shard_map/ppermute | solution.py:545
  32.2 1.4 %collective-permute-start.22 = (bf16[16,4,16,128]{3,2,1,0:T(8,128)(2,1)S(1)}, bf16[16,4,16,128]{3,2,1,0:T(8,128)(2,1)S(1)}, u32[]{:S(2)}, u32[]{:S(2)}) collective-permute-start(bf16[16,4,16,128]{3,2,1,0:T(8,128)(2,1)S(1)} %collective-permute-done.17.rest_10_), channel_id=1, source_target_pairs={{0,8},{8,16},{16,24},{24,28},{28,20},{20,12},{12,4},{4,0},{1,9},{9... | collective-permute-start | bytes 786440 | tf_op jit(solution)/shard_map/ppermute | solution.py:545
  33.6 4.5 %cross.4 = (bf16[128,512]{1,0:T(8,128)(2,1)S(1)}, bf16[128,512]{1,0:T(8,128)(2,1)S(1)}, bf16[128,512]{1,0:T(8,128)(2,1)S(1)}, bf16[128,512]{1,0:T(8,128)(2,1)S(1)}) custom-call(s32[4,8]{1,0:T(4,128)S(1)} %copy-done.1, bf16[2048,512]{1,0:T(8,128)(2,1)S(1)} %copy-done.2, f32[4,3,8,4,8,128]{5,4,3,2,1,0:T(8,128)S(1)} %widen.2.rest_0_, ...), custom_call_target="tpu_custom_call" | custom-call | flops 5289999872 | bytes 1024 | tf_op jit(solution)/shard_map/cross/pallas_call | solution.py:359
  38.3 1.8 %collective-permute-start.20 = (bf16[128,512]{1,0:T(8,128)(2,1)S(1)}, bf16[128,512]{1,0:T(8,128)(2,1)S(1)}, u32[]{:S(2)}, u32[]{:S(2)}) collective-permute-start(bf16[128,512]{1,0:T(8,128)(2,1)S(1)} %get-tuple-element.65), channel_id=1, source_target_pairs={{0,2},{1,3},{2,0},{3,1},{4,6},{5,7},{6,4},{7,5},{8,10},{9,11},{10,... | collective-permute-start | bytes 393224 | tf_op jit(solution)/shard_map/ppermute | solution.py:512
  40.3 2.7 %cross.5 = (bf16[64,512]{1,0:T(8,128)(2,1)S(1)}, bf16[64,512]{1,0:T(8,128)(2,1)S(1)}, bf16[64,512]{1,0:T(8,128)(2,1)S(1)}, bf16[64,512]{1,0:T(8,128)(2,1)S(1)}) custom-call(s32[4,8]{1,0:T(4,128)S(1)} %copy-done.1, bf16[2048,512]{1,0:T(8,128)(2,1)S(1)} %copy-done.2, f32[4,3,8,4,8,128]{5,4,3,2,1,0:T(8,128)S(1)} %widen.2.rest_0_, ...), custom_call_target="tpu_custom_call" | custom-call | flops 2990000128 | bytes 1024 | tf_op jit(solution)/shard_map/cross/pallas_call | solution.py:359
  43.0 0.3 collective-permute-start.23
  43.3 1.7 %collective-permute-start.24 = (bf16[64,512]{1,0:T(8,128)(2,1)S(1)}, bf16[64,512]{1,0:T(8,128)(2,1)S(1)}, u32[]{:S(2)}, u32[]{:S(2)}) collective-permute-start(bf16[64,512]{1,0:T(8,128)(2,1)S(1)} %get-tuple-element.71), channel_id=1, source_target_pairs={{0,2},{1,3},{2,0},{3,1},{4,6},{5,7},{6,4},{7,5},{8,10},{9,11},{10,... | collective-permute-start | bytes 196616 | tf_op jit(solution)/shard_map/ppermute | solution.py:512
  45.1 1.6 %collective-permute-done.21.rest_7_ = bf16[128,512]{1,0:T(8,128)(2,1)S(1)} collective-permute-done((bf16[128,512]{1,0:T(8,128)(2,1)S(1)}, bf16[128,512]{1,0:T(8,128)(2,1)S(1)}, u32[]{:S(2)}, u32[]{:S(2)}) %collective-permute-start.21) | collective-permute-done | bytes 131104 | tf_op jit(solution)/shard_map/ppermute | solution.py:512
  46.7 2.1 %early.1 = f32[1024,4,1,128]{3,2,1,0:T(1,128)} custom-call(s32[4,8]{1,0:T(4,128)S(1)} %copy-done.1, bf16[4,128,512]{2,1,0:T(8,128)(2,1)S(1)} %copy-done, bf16[64,512]{1,0:T(8,128)(2,1)S(1)} %get-tuple-element.56.rest_0_, bf16[64,512]{1,0:T(8,128)(2,1)S(1)} %collective-permute-done.14.rest_1_, bf16[64,512]{1,0:T(8,128)(2,1)S(1)} %collective-permute-done.15.rest_2_, ...), custom_call_target="tpu_custom_call" | custom-call | flops 57500000 | bytes 1024 | tf_op jit(solution)/shard_map/early/pallas_call | solution.py:458
  48.8 0.7 %collective-permute-done.25.rest_3_ = bf16[64,512]{1,0:T(8,128)(2,1)S(1)} collective-permute-done((bf16[64,512]{1,0:T(8,128)(2,1)S(1)}, bf16[64,512]{1,0:T(8,128)(2,1)S(1)}, u32[]{:S(2)}, u32[]{:S(2)}) %collective-permute-start.25) | collective-permute-done | bytes 65568 | tf_op jit(solution)/shard_map/ppermute | solution.py:512
  49.5 1.6 %late.1 = f32[1024,4,1,128]{3,2,1,0:T(1,128)} custom-call(s32[4,8]{1,0:T(4,128)S(1)} %copy-done.1, bf16[4,128,512]{2,1,0:T(8,128)(2,1)S(1)} %copy-done, f32[1024,4,1,128]{3,2,1,0:T(1,128)} %early.1, bf16[64,512]{1,0:T(8,128)(2,1)S(1)} %get-tuple-element.69.rest_0_, ...), custom_call_target="tpu_custom_call", output_to_operand_aliasing={{}: (2, {})} | custom-call | flops 57500000 | bytes 1024 | tf_op jit(solution)/shard_map/late/pallas_call | solution.py:471
  (38 shorter events, 1.4 us)
Async XLA Ops:
  3.0 3.3 %collective-permute-start = (bf16[4,4,16,128]{3,2,1,0:T(8,128)(2,1)S(1)}, bf16[4,4,16,128]{3,2,1,0:T(8,128)(2,1)S(1)}, u32[]{:S(2)}, u32[]{:S(2)}) collective-permute-start(bf16[4,4,16,128]{3,2,1,0:T(8,128)(2,1)S(1)} %get-tuple-element.40), channel_id=1, source_target_pairs={{0,1},{1,0},{2,3},{3,2},{4,5},{5,4},{6,7},{7,6},{8,9},{9,8},{10,11... | collective-permute-start | bytes 196616 | tf_op jit(solution)/shard_map/ppermute | solution.py:512
  3.6 5.3 %collective-permute-start.6 = (bf16[4,4,16,128]{3,2,1,0:T(8,128)(2,1)S(1)}, bf16[4,4,16,128]{3,2,1,0:T(8,128)(2,1)S(1)}, u32[]{:S(2)}, u32[]{:S(2)}) collective-permute-start(bf16[4,4,16,128]{3,2,1,0:T(8,128)(2,1)S(1)} %get-tuple-element.45), channel_id=1, source_target_pairs={{0,2},{1,3},{2,0},{3,1},{4,6},{5,7},{6,4},{7,5},{8,10},{9,11},{10,... | collective-permute-start | bytes 196616 | tf_op jit(solution)/shard_map/ppermute | solution.py:512
  6.1 4.0 %collective-permute-start.7 = (bf16[4,4,16,128]{3,2,1,0:T(8,128)(2,1)S(1)}, bf16[4,4,16,128]{3,2,1,0:T(8,128)(2,1)S(1)}, u32[]{:S(2)}, u32[]{:S(2)}) collective-permute-start(bf16[4,4,16,128]{3,2,1,0:T(8,128)(2,1)S(1)} %get-tuple-element.46), channel_id=1, source_target_pairs={{0,3},{1,2},{2,1},{3,0},{4,7},{5,6},{6,5},{7,4},{8,11},{9,10},{10,... | collective-permute-start | bytes 196616 | tf_op jit(solution)/shard_map/ppermute | solution.py:512
  6.2 4.0 %collective-permute-start.3 = (bf16[4,16,16,128]{3,2,1,0:T(8,128)(2,1)S(1)}, bf16[4,16,16,128]{3,2,1,0:T(8,128)(2,1)S(1)}, u32[]{:S(2)}, u32[]{:S(2)}) collective-permute-start(bf16[4,16,16,128]{3,2,1,0:T(8,128)(2,1)S(1)} %get-tuple-element.54.refs_0_), channel_id=1, source_target_pairs={{0,1},{1,0},{2,3},{3,2},{4,5},{5,4},{6,7},{7,6},{8,9},{9,8},{10,11... | collective-permute-start | bytes 786440 | tf_op jit(solution)/shard_map/ppermute | solution.py:512
  6.4 7.4 %collective-permute-start.2 = (bf16[8,4,16,128]{3,2,1,0:T(8,128)(2,1)S(1)}, bf16[8,4,16,128]{3,2,1,0:T(8,128)(2,1)S(1)}, u32[]{:S(2)}, u32[]{:S(2)}) collective-permute-start(bf16[8,4,16,128]{3,2,1,0:T(8,128)(2,1)S(1)} %constant_dynamic-update-slice_fusion), channel_id=1, source_target_pairs={{0,4},{8,0},{16,8},{24,16},{28,24},{20,28},{12,20},{4,12},{1,5},{9... | collective-permute-start | bytes 393224 | tf_op jit(solution)/shard_map/ppermute | solution.py:548
  8.4 5.4 %collective-permute-start.1 = (bf16[8,4,16,128]{3,2,1,0:T(8,128)(2,1)S(1)}, bf16[8,4,16,128]{3,2,1,0:T(8,128)(2,1)S(1)}, u32[]{:S(2)}, u32[]{:S(2)}) collective-permute-start(bf16[8,4,16,128]{3,2,1,0:T(8,128)(2,1)S(1)} %constant_dynamic-update-slice_fusion), channel_id=1, source_target_pairs={{0,8},{8,16},{16,24},{24,28},{28,20},{20,12},{12,4},{4,0},{1,9},{9... | collective-permute-start | bytes 393224 | tf_op jit(solution)/shard_map/ppermute | solution.py:545
  10.2 15.4 %copy-start.1 = (s32[4,8]{1,0:T(4,128)S(1)}, s32[4,8]{1,0:T(4,128)}, u32[]{:S(2)}) copy-start(s32[4,8]{1,0:T(4,128)} %plan.9) | copy-start | bytes 388
  10.2 15.4 %copy-start.2 = (bf16[2048,512]{1,0:T(8,128)(2,1)S(1)}, bf16[2048,512]{1,0:T(8,128)(2,1)}, u32[]{:S(2)}) copy-start(bf16[2048,512]{1,0:T(8,128)(2,1)} %constant.7.clone.table) | copy-start | bytes 6291460
  10.2 5.9 %collective-permute-start.9 = (bf16[8,4,16,128]{3,2,1,0:T(8,128)(2,1)S(1)}, bf16[8,4,16,128]{3,2,1,0:T(8,128)(2,1)S(1)}, u32[]{:S(2)}, u32[]{:S(2)}) collective-permute-start(bf16[8,4,16,128]{3,2,1,0:T(8,128)(2,1)S(1)} %pad_maximum_fusion), channel_id=1, source_target_pairs={{0,4},{8,0},{16,8},{24,16},{28,24},{20,28},{12,20},{4,12},{1,5},{9... | collective-permute-start | bytes 393224 | tf_op jit(solution)/shard_map/ppermute | solution.py:548
  11.8 6.3 %collective-permute-start.8 = (bf16[8,4,16,128]{3,2,1,0:T(8,128)(2,1)S(1)}, bf16[8,4,16,128]{3,2,1,0:T(8,128)(2,1)S(1)}, u32[]{:S(2)}, u32[]{:S(2)}) collective-permute-start(bf16[8,4,16,128]{3,2,1,0:T(8,128)(2,1)S(1)} %pad_maximum_fusion), channel_id=1, source_target_pairs={{0,8},{8,16},{16,24},{24,28},{28,20},{20,12},{12,4},{4,0},{1,9},{9... | collective-permute-start | bytes 393224 | tf_op jit(solution)/shard_map/ppermute | solution.py:545
  12.3 10.9 %collective-permute-start.12 = (bf16[4,16,16,128]{3,2,1,0:T(8,128)(2,1)S(1)}, bf16[4,16,16,128]{3,2,1,0:T(8,128)(2,1)S(1)}, u32[]{:S(2)}, u32[]{:S(2)}) collective-permute-start(bf16[4,16,16,128]{3,2,1,0:T(8,128)(2,1)S(1)} %get-tuple-element.54.refs_0_), channel_id=1, source_target_pairs={{0,2},{1,3},{2,0},{3,1},{4,6},{5,7},{6,4},{7,5},{8,10},{9,11},{10,... | collective-permute-start | bytes 786440 | tf_op jit(solution)/shard_map/ppermute | solution.py:512
  13.8 7.1 %collective-permute-start.4 = (bf16[8,4,16,128]{3,2,1,0:T(8,128)(2,1)S(1)}, bf16[8,4,16,128]{3,2,1,0:T(8,128)(2,1)S(1)}, u32[]{:S(2)}, u32[]{:S(2)}) collective-permute-start(bf16[8,4,16,128]{3,2,1,0:T(8,128)(2,1)S(1)} %collective-permute-done.1.rest_2_), channel_id=1, source_target_pairs={{0,8},{8,16},{16,24},{24,28},{28,20},{20,12},{12,4},{4,0},{1,9},{9... | collective-permute-start | bytes 393224 | tf_op jit(solution)/shard_map/ppermute | solution.py:545
  15.4 5.7 %collective-permute-start.5 = (bf16[8,4,16,128]{3,2,1,0:T(8,128)(2,1)S(1)}, bf16[8,4,16,128]{3,2,1,0:T(8,128)(2,1)S(1)}, u32[]{:S(2)}, u32[]{:S(2)}) collective-permute-start(bf16[8,4,16,128]{3,2,1,0:T(8,128)(2,1)S(1)} %collective-permute-done.2.rest_3_), channel_id=1, source_target_pairs={{0,4},{8,0},{16,8},{24,16},{28,24},{20,28},{12,20},{4,12},{1,5},{9... | collective-permute-start | bytes 393224 | tf_op jit(solution)/shard_map/ppermute | solution.py:548
  18.1 5.0 %collective-permute-start.10 = (bf16[8,4,16,128]{3,2,1,0:T(8,128)(2,1)S(1)}, bf16[8,4,16,128]{3,2,1,0:T(8,128)(2,1)S(1)}, u32[]{:S(2)}, u32[]{:S(2)}) collective-permute-start(bf16[8,4,16,128]{3,2,1,0:T(8,128)(2,1)S(1)} %collective-permute-done.8.rest_4_), channel_id=1, source_target_pairs={{0,8},{8,16},{16,24},{24,28},{28,20},{20,12},{12,4},{4,0},{1,9},{9... | collective-permute-start | bytes 393224 | tf_op jit(solution)/shard_map/ppermute | solution.py:545
  18.1 5.1 %collective-permute-start.11 = (bf16[8,4,16,128]{3,2,1,0:T(8,128)(2,1)S(1)}, bf16[8,4,16,128]{3,2,1,0:T(8,128)(2,1)S(1)}, u32[]{:S(2)}, u32[]{:S(2)}) collective-permute-start(bf16[8,4,16,128]{3,2,1,0:T(8,128)(2,1)S(1)} %collective-permute-done.9.rest_5_), channel_id=1, source_target_pairs={{0,4},{8,0},{16,8},{24,16},{28,24},{20,28},{12,20},{4,12},{1,5},{9... | collective-permute-start | bytes 393224 | tf_op jit(solution)/shard_map/ppermute | solution.py:548
  23.3 2.2 %collective-permute-start.13 = (bf16[4,16,16,128]{3,2,1,0:T(8,128)(2,1)S(1)}, bf16[4,16,16,128]{3,2,1,0:T(8,128)(2,1)S(1)}, u32[]{:S(2)}, u32[]{:S(2)}) collective-permute-start(bf16[4,16,16,128]{3,2,1,0:T(8,128)(2,1)S(1)} %collective-permute-done.12.refs_0_), channel_id=1, source_target_pairs={{0,1},{1,0},{2,3},{3,2},{4,5},{5,4},{6,7},{7,6},{8,9},{9,8},{10,11... | collective-permute-start | bytes 786440 | tf_op jit(solution)/shard_map/ppermute | solution.py:512
  23.3 8.9 %collective-permute-start.17 = (bf16[16,4,16,128]{3,2,1,0:T(8,128)(2,1)S(1)}, bf16[16,4,16,128]{3,2,1,0:T(8,128)(2,1)S(1)}, u32[]{:S(2)}, u32[]{:S(2)}) collective-permute-start(bf16[16,4,16,128]{3,2,1,0:T(8,128)(2,1)S(1)} %get-tuple-element.61), channel_id=1, source_target_pairs={{0,8},{8,16},{16,24},{24,28},{28,20},{20,12},{12,4},{4,0},{1,9},{9... | collective-permute-start | bytes 786440 | tf_op jit(solution)/shard_map/ppermute | solution.py:545
  25.0 8.7 %collective-permute-start.18 = (bf16[16,4,16,128]{3,2,1,0:T(8,128)(2,1)S(1)}, bf16[16,4,16,128]{3,2,1,0:T(8,128)(2,1)S(1)}, u32[]{:S(2)}, u32[]{:S(2)}) collective-permute-start(bf16[16,4,16,128]{3,2,1,0:T(8,128)(2,1)S(1)} %get-tuple-element.62), channel_id=1, source_target_pairs={{0,4},{8,0},{16,8},{24,16},{28,24},{20,28},{12,20},{4,12},{1,5},{9... | collective-permute-start | bytes 786440 | tf_op jit(solution)/shard_map/ppermute | solution.py:548
  28.3 10.0 %collective-permute-start.14 = (bf16[64,512]{1,0:T(8,128)(2,1)S(1)}, bf16[64,512]{1,0:T(8,128)(2,1)S(1)}, u32[]{:S(2)}, u32[]{:S(2)}) collective-permute-start(bf16[64,512]{1,0:T(8,128)(2,1)S(1)} %get-tuple-element.57), channel_id=1, source_target_pairs={{0,1},{1,0},{2,3},{3,2},{4,5},{5,4},{6,7},{7,6},{8,9},{9,8},{10,11... | collective-permute-start | bytes 196616 | tf_op jit(solution)/shard_map/ppermute | solution.py:512
  28.4 11.7 %collective-permute-start.15 = (bf16[64,512]{1,0:T(8,128)(2,1)S(1)}, bf16[64,512]{1,0:T(8,128)(2,1)S(1)}, u32[]{:S(2)}, u32[]{:S(2)}) collective-permute-start(bf16[64,512]{1,0:T(8,128)(2,1)S(1)} %get-tuple-element.58), channel_id=1, source_target_pairs={{0,2},{1,3},{2,0},{3,1},{4,6},{5,7},{6,4},{7,5},{8,10},{9,11},{10,... | collective-permute-start | bytes 196616 | tf_op jit(solution)/shard_map/ppermute | solution.py:512
  30.1 10.0 %collective-permute-start.16 = (bf16[64,512]{1,0:T(8,128)(2,1)S(1)}, bf16[64,512]{1,0:T(8,128)(2,1)S(1)}, u32[]{:S(2)}, u32[]{:S(2)}) collective-permute-start(bf16[64,512]{1,0:T(8,128)(2,1)S(1)} %get-tuple-element.59), channel_id=1, source_target_pairs={{0,3},{1,2},{2,1},{3,0},{4,7},{5,6},{6,5},{7,4},{8,11},{9,10},{10,... | collective-permute-start | bytes 196616 | tf_op jit(solution)/shard_map/ppermute | solution.py:512
  32.2 8.1 %collective-permute-start.22 = (bf16[16,4,16,128]{3,2,1,0:T(8,128)(2,1)S(1)}, bf16[16,4,16,128]{3,2,1,0:T(8,128)(2,1)S(1)}, u32[]{:S(2)}, u32[]{:S(2)}) collective-permute-start(bf16[16,4,16,128]{3,2,1,0:T(8,128)(2,1)S(1)} %collective-permute-done.17.rest_10_), channel_id=1, source_target_pairs={{0,8},{8,16},{16,24},{24,28},{28,20},{20,12},{12,4},{4,0},{1,9},{9... | collective-permute-start | bytes 786440 | tf_op jit(solution)/shard_map/ppermute | solution.py:545
  38.2 6.9 %collective-permute-start.19 = (bf16[128,512]{1,0:T(8,128)(2,1)S(1)}, bf16[128,512]{1,0:T(8,128)(2,1)S(1)}, u32[]{:S(2)}, u32[]{:S(2)}) collective-permute-start(bf16[128,512]{1,0:T(8,128)(2,1)S(1)} %get-tuple-element.64), channel_id=1, source_target_pairs={{0,1},{1,0},{2,3},{3,2},{4,5},{5,4},{6,7},{7,6},{8,9},{9,8},{10,11... | collective-permute-start | bytes 393224 | tf_op jit(solution)/shard_map/ppermute | solution.py:512
  38.3 6.8 %collective-permute-start.20 = (bf16[128,512]{1,0:T(8,128)(2,1)S(1)}, bf16[128,512]{1,0:T(8,128)(2,1)S(1)}, u32[]{:S(2)}, u32[]{:S(2)}) collective-permute-start(bf16[128,512]{1,0:T(8,128)(2,1)S(1)} %get-tuple-element.65), channel_id=1, source_target_pairs={{0,2},{1,3},{2,0},{3,1},{4,6},{5,7},{6,4},{7,5},{8,10},{9,11},{10,... | collective-permute-start | bytes 393224 | tf_op jit(solution)/shard_map/ppermute | solution.py:512
  40.1 6.6 %collective-permute-start.21 = (bf16[128,512]{1,0:T(8,128)(2,1)S(1)}, bf16[128,512]{1,0:T(8,128)(2,1)S(1)}, u32[]{:S(2)}, u32[]{:S(2)}) collective-permute-start(bf16[128,512]{1,0:T(8,128)(2,1)S(1)} %get-tuple-element.66), channel_id=1, source_target_pairs={{0,3},{1,2},{2,1},{3,0},{4,7},{5,6},{6,5},{7,4},{8,11},{9,10},{10,... | collective-permute-start | bytes 393224 | tf_op jit(solution)/shard_map/ppermute | solution.py:512
  40.2 6.5 %copy-start = (bf16[4,128,512]{2,1,0:T(8,128)(2,1)S(1)}, bf16[4,128,512]{2,1,0:T(8,128)(2,1)}, u32[]{:S(2)}) copy-start(bf16[4,128,512]{2,1,0:T(8,128)(2,1)} %constant.8.clone.place) | copy-start | bytes 1572868
  43.0 5.8 %collective-permute-start.23 = (bf16[64,512]{1,0:T(8,128)(2,1)S(1)}, bf16[64,512]{1,0:T(8,128)(2,1)S(1)}, u32[]{:S(2)}, u32[]{:S(2)}) collective-permute-start(bf16[64,512]{1,0:T(8,128)(2,1)S(1)} %get-tuple-element.70), channel_id=1, source_target_pairs={{0,1},{1,0},{2,3},{3,2},{4,5},{5,4},{6,7},{7,6},{8,9},{9,8},{10,11... | collective-permute-start | bytes 196616 | tf_op jit(solution)/shard_map/ppermute | solution.py:512
  43.3 5.5 %collective-permute-start.24 = (bf16[64,512]{1,0:T(8,128)(2,1)S(1)}, bf16[64,512]{1,0:T(8,128)(2,1)S(1)}, u32[]{:S(2)}, u32[]{:S(2)}) collective-permute-start(bf16[64,512]{1,0:T(8,128)(2,1)S(1)} %get-tuple-element.71), channel_id=1, source_target_pairs={{0,2},{1,3},{2,0},{3,1},{4,6},{5,7},{6,4},{7,5},{8,10},{9,11},{10,... | collective-permute-start | bytes 196616 | tf_op jit(solution)/shard_map/ppermute | solution.py:512
  45.1 4.5 %collective-permute-start.25 = (bf16[64,512]{1,0:T(8,128)(2,1)S(1)}, bf16[64,512]{1,0:T(8,128)(2,1)S(1)}, u32[]{:S(2)}, u32[]{:S(2)}) collective-permute-start(bf16[64,512]{1,0:T(8,128)(2,1)S(1)} %get-tuple-element.72), channel_id=1, source_target_pairs={{0,3},{1,2},{2,1},{3,0},{4,7},{5,6},{6,5},{7,4},{8,11},{9,10},{10,... | collective-permute-start | bytes 196616 | tf_op jit(solution)/shard_map/ppermute | solution.py:512

commit v16 on v15

--- a/solution.py
+++ b/solution.py
@@ -266,59 +266,64 @@
 
             @pl.when(step == offset)
             def _(candidate=candidate, slot=slot, first=first):
-                def widen_other(w, carry):
-                    raw = candidate[w].astype(F32)
-                    real, imag = raw[:, :TILES], raw[:, TILES:]
-                    other[0, slot, first + w] = real
-                    other[1, slot, first + w] = real + imag
-                    other[2, slot, first + w] = imag - real
+                def widen_other(turn, carry):
+                    raw = candidate[pl.ds(turn * GROUP, GROUP)].astype(F32)
+                    real, imag = raw[:, :, :TILES], raw[:, :, TILES:]
+                    at = pl.ds(first + turn * GROUP, GROUP)
+                    other[0, slot, at] = real
+                    other[1, slot, at] = real + imag
+                    other[2, slot, at] = imag - real
                     return carry
 
-                lax.fori_loop(0, candidate.shape[0], widen_other, 0)
-
-
-def sum_windows(owns, other, summed):
+                lax.fori_loop(0, candidate.shape[0] // GROUP, widen_other, 0)
+
+
+def sum_windows(owns, other, slot, crossed, turns, beside=None):
     groups, _, windows, group = owns[0].shape[:4]
-    slots, _, quarter = other.shape[1:4]
-    width = groups * group * quarter
-    shift = groups.bit_length() - 1
-
-    for slot in range(slots):
-
-        def body(index, carry, slot=slot):
-            kind, part = index >> shift, index & (groups - 1)
-            mine = [own.at[part, kind] for own in owns]
-            theirs = other.at[kind, slot]
+    quarter = other.shape[3]
+    size = 2 * TILES
+
+    def one_group(index):
+        mine = [own.at[index] for own in owns]
+
+        def sums(kind):
             totals = [None] * (group * quarter)
             for half, own in enumerate(mine):
                 for w in range(windows):
-                    left = [own[w, s] for s in range(group)]
-                    right = [theirs[half * windows + w, t] for t in range(quarter)]
+                    left = [own[kind, w, s] for s in range(group)]
+                    right = [other[kind, slot, half * windows + w, t] for t in range(quarter)]
                     for s in range(group):
                         for t in range(quarter):
                             term = left[s] * right[t]
                             old = totals[s * quarter + t]
                             totals[s * quarter + t] = term if old is None else old + term
-            rows = summed.at[kind]
-            base = (slot * width + part * (group * quarter)) * TILES
-            for place in range(group * quarter):
-                at = pl.multiple_of(base + place * TILES, TILES)
-                rows[pl.ds(at, TILES), :] = totals[place]
-            return carry
-
-        lax.fori_loop(0, 3 * groups, body, 0)
-
-
-def cross_kernel(first_slot, slots, count, scaling, places, parts, plan, table, *rest):
-    owns, rest = rest[:2], rest[2:]
-    others, rest = rest[: len(places)], rest[len(places) :]
-    outs = rest[:parts]
-    other, summed, operand, result = rest[parts:]
-    stations = owns[0].shape[0] * owns[0].shape[3]
-    widen_others(first_slot, slots, count, places, plan, others, other)
-    sum_windows(owns, other, summed)
-    width = stations * other.shape[3]
-    columns = slots * width
+            return totals
+
+        def store(place, part, value):
+            at = pl.multiple_of(base + place * size + part * TILES, TILES)
+            crossed[pl.ds(at, TILES), :] = value
+
+        base = index * (group * quarter * size)
+        shared = sums(0)
+        third = sums(2)
+        for place in range(group * quarter):
+            store(place, 0, shared[place] + third[place])
+        second = sums(1)
+        for place in range(group * quarter):
+            store(place, 1, shared[place] - second[place])
+
+    def body(turn, carry):
+        if beside is not None:
+            beside(turn)
+        for index in range(groups // turns):
+            one_group(turn * (groups // turns) + index)
+        return carry
+
+    lax.fori_loop(0, turns, body, 0)
+
+
+def fill_operand(crossed, operand):
+    columns = operand.shape[0] // CHUNKS
     even = even_lanes((columns, LANES))
     sign_real = lane_cycle([1.0, -1.0, -1.0, 1.0])
     sign_imag = lane_cycle([1.0, 1.0, -1.0, -1.0])
@@ -328,8 +333,8 @@
     for j in range(TILES):
         at = slice(j * LANES, (j + 1) * LANES)
         at_imag = slice(NBIN + j * LANES, NBIN + (j + 1) * LANES)
-        kinds = [summed[kind, pl.ds(j, columns, stride=TILES), :] for kind in range(3)]
-        real, imag = kinds[0] + kinds[2], kinds[0] - kinds[1]
+        real = crossed[pl.ds(j, columns, stride=2 * TILES), :]
+        imag = crossed[pl.ds(TILES + j, columns, stride=2 * TILES), :]
         if j == 0:
             real, imag = real * first_weight, imag * first_weight
         turned = [(real, imag), (real * cosine - imag * sine, imag * cosine + real * sine)]
@@ -338,10 +343,36 @@
             rows = slice(q * columns, (q + 1) * columns)
             operand[rows, at] = turned[q][0].astype(BF)
             operand[rows, at_imag] = turned[q][1].astype(BF)
-    block = jnp.dot(operand[...], table[...], preferred_element_type=F32)
-    block = block * (2.0 * scaling)
-    for q in range(CHUNKS):
-        result[q] = block[q * columns : (q + 1) * columns].astype(BF)
+
+
+def cross_kernel(first_slot, slots, count, scaling, places, parts, plan, table, *rest):
+    owns, rest = rest[:2], rest[2:]
+    others, rest = rest[: len(places)], rest[len(places) :]
+    outs = rest[:parts]
+    other, crossed, operand, result = rest[parts:]
+    groups = owns[0].shape[0]
+    widen_others(first_slot, slots, count, places, plan, others, other)
+    width = operand.shape[0] // CHUNKS
+    share = table.shape[1]
+
+    def lags(slot, at):
+        block = jnp.dot(operand[...], table[:, at], preferred_element_type=F32)
+        block = (block * (2.0 * scaling)).astype(BF)
+        for q in range(CHUNKS):
+            result[q, slot * width : (slot + 1) * width, at] = block[q * width : (q + 1) * width]
+
+    sum_windows(owns, other, 0, crossed, groups)
+    fill_operand(crossed, operand)
+    for slot in range(1, slots):
+        turns = 2
+        size = share // turns
+
+        def beside(turn, slot=slot, size=size):
+            lags(slot - 1, pl.ds(pl.multiple_of(turn * size, size), size))
+
+        sum_windows(owns, other, slot, crossed, turns, beside)
+        fill_operand(crossed, operand)
+    lags(slots - 1, slice(None))
     me = lax.axis_index("seg")
     for j in range(parts):
         outs[j][...] = result[me ^ j]
@@ -365,8 +396,8 @@
         out_specs=[vmem] * parts,
         scratch_shapes=[
             pltpu.VMEM((3, slots, 2 * windows, quarter, TILES, LANES), F32),
-            pltpu.VMEM((3, columns * TILES, LANES), F32),
-            pltpu.VMEM((CHUNKS * columns, 2 * NBIN), BF),
+            pltpu.VMEM((columns // slots * 2 * TILES, LANES), F32),
+            pltpu.VMEM((CHUNKS * columns // slots, 2 * NBIN), BF),
             pltpu.VMEM((parts,) + out, BF),
         ],
         compiler_params=pltpu.CompilerParams(vmem_limit_bytes=24 * 2**20),

time: 51.3 us -> 51.5 us (level)
  transfers between devices with their start and end apart: 26 -> 26, of which waited for: 12 -> 11; matrix products, arithmetic and copies ran while one was open for 0% -> 0% of each run, Pallas kernels for 24% -> 25%
where the time goes in v16:
time: 51.5 us; the launch traced here: 51.4 us
  starting transfers between devices  22.5 us (44%)
  Pallas kernels  17.3 us (34%)
  waiting for transfers between devices  11.4 us (22%)
    ppermute x15, starting transfers between devices, swap(): return lax.ppermute(value, 'seg', [(i, i ^ j) for i in range(parts)])  10.7 us
    pallas_call x3, Pallas kernels, cross_lags(): pl.pallas_call(functools.partial(cross_kernel, first_slot, slots, count,...  10.2 us
    ppermute x6, waiting for transfers between devices, up(): return lax.ppermute(value, 'sta', upward)  6.79 us
    ppermute x5, starting transfers between devices, down(): return lax.ppermute(value, 'sta', downward)  6.51 us
    ppermute x6, starting transfers between devices, up(): return lax.ppermute(value, 'sta', upward)  5.28 us
    ppermute x15, waiting for transfers between devices, swap(): return lax.ppermute(value, 'seg', [(i, i ^ j) for i in range(parts)])  4.02 us
    pallas_call x1, Pallas kernels, prepare(): pl.pallas_call(functools.partial(prep_kernel, parts, windows), out_shape=...  3.04 us
    pallas_call x1, Pallas kernels, place_lags(): pl.pallas_call(functools.partial(early_kernel, count, parts, tuple(groups...  2.1 us
  transfers between devices with their start and end apart: 26, of which 11 were waited for; matrix products, arithmetic and copies ran while one was open for 0% of the time, Pallas kernels for 25%

profile of v16, /device:TPU:0, one launch (start us, length us, event | category | flops | bytes accessed | tf_op | source)
XLA Modules:
  0.0 51.4 jit_solution(2801180280875864386)
XLA Ops:
  0.0 3.0 %prep.1 = (bf16[4,16,16,128]{3,2,1,0:T(8,128)(2,1)S(1)}, bf16[4,4,16,128]{3,2,1,0:T(8,128)(2,1)S(1)}, bf16[4,4,16,128]{3,2,1,0:T(8,128)(2,1)S(1)}, bf16[4,4,16,1...) custom-call(f32[1024,128]{1,0:T(8,128)} %bitcast.10, bf16[512,2048]{1,0:T(8,128)(2,1)} %constant.6.clone.table_hbm), custom_call_target="tpu_custom_call" | custom-call | flops 536870912 | bytes 3145728 | tf_op jit(solution)/shard_map/prep/pallas_call | solution.py:169
  3.0 0.5 %collective-permute-start = (bf16[4,4,16,128]{3,2,1,0:T(8,128)(2,1)S(1)}, bf16[4,4,16,128]{3,2,1,0:T(8,128)(2,1)S(1)}, u32[]{:S(2)}, u32[]{:S(2)}) collective-permute-start(bf16[4,4,16,128]{3,2,1,0:T(8,128)(2,1)S(1)} %get-tuple-element.40), channel_id=1, source_target_pairs={{0,1},{1,0},{2,3},{3,2},{4,5},{5,4},{6,7},{7,6},{8,9},{9,8},{10,11... | collective-permute-start | bytes 196616 | tf_op jit(solution)/shard_map/ppermute | solution.py:543
  3.6 2.6 %collective-permute-start.6 = (bf16[4,4,16,128]{3,2,1,0:T(8,128)(2,1)S(1)}, bf16[4,4,16,128]{3,2,1,0:T(8,128)(2,1)S(1)}, u32[]{:S(2)}, u32[]{:S(2)}) collective-permute-start(bf16[4,4,16,128]{3,2,1,0:T(8,128)(2,1)S(1)} %get-tuple-element.45), channel_id=1, source_target_pairs={{0,2},{1,3},{2,0},{3,1},{4,6},{5,7},{6,4},{7,5},{8,10},{9,11},{10,... | collective-permute-start | bytes 196616 | tf_op jit(solution)/shard_map/ppermute | solution.py:543
  6.4 2.0 %collective-permute-start.2 = (bf16[8,4,16,128]{3,2,1,0:T(8,128)(2,1)S(1)}, bf16[8,4,16,128]{3,2,1,0:T(8,128)(2,1)S(1)}, u32[]{:S(2)}, u32[]{:S(2)}) collective-permute-start(bf16[8,4,16,128]{3,2,1,0:T(8,128)(2,1)S(1)} %constant_dynamic-update-slice_fusion), channel_id=1, source_target_pairs={{0,4},{8,0},{16,8},{24,16},{28,24},{20,28},{12,20},{4,12},{1,5},{9... | collective-permute-start | bytes 393224 | tf_op jit(solution)/shard_map/ppermute | solution.py:579
  8.5 0.3 collective-permute-done.6
  8.8 1.4 %collective-permute-done.7 = bf16[4,4,16,128]{3,2,1,0:T(8,128)(2,1)S(1)} collective-permute-done((bf16[4,4,16,128]{3,2,1,0:T(8,128)(2,1)S(1)}, bf16[4,4,16,128]{3,2,1,0:T(8,128)(2,1)S(1)}, u32[]{:S(2)}, u32[]{:S(2)}) %collective-permute-start.7) | collective-permute-done | bytes 65568 | tf_op jit(solution)/shard_map/ppermute | solution.py:543
  10.2 1.6 %collective-permute-start.9 = (bf16[8,4,16,128]{3,2,1,0:T(8,128)(2,1)S(1)}, bf16[8,4,16,128]{3,2,1,0:T(8,128)(2,1)S(1)}, u32[]{:S(2)}, u32[]{:S(2)}) collective-permute-start(bf16[8,4,16,128]{3,2,1,0:T(8,128)(2,1)S(1)} %pad_maximum_fusion), channel_id=1, source_target_pairs={{0,4},{8,0},{16,8},{24,16},{28,24},{20,28},{12,20},{4,12},{1,5},{9... | collective-permute-start | bytes 393224 | tf_op jit(solution)/shard_map/ppermute | solution.py:579
  11.8 0.5 collective-permute-start.8
  12.3 1.3 %collective-permute-start.12 = (bf16[4,16,16,128]{3,2,1,0:T(8,128)(2,1)S(1)}, bf16[4,16,16,128]{3,2,1,0:T(8,128)(2,1)S(1)}, u32[]{:S(2)}, u32[]{:S(2)}) collective-permute-start(bf16[4,16,16,128]{3,2,1,0:T(8,128)(2,1)S(1)} %get-tuple-element.54.refs_0_), channel_id=1, source_target_pairs={{0,2},{1,3},{2,0},{3,1},{4,6},{5,7},{6,4},{7,5},{8,10},{9,11},{10,... | collective-permute-start | bytes 786440 | tf_op jit(solution)/shard_map/ppermute | solution.py:543
  13.8 1.6 %collective-permute-start.4 = (bf16[8,4,16,128]{3,2,1,0:T(8,128)(2,1)S(1)}, bf16[8,4,16,128]{3,2,1,0:T(8,128)(2,1)S(1)}, u32[]{:S(2)}, u32[]{:S(2)}) collective-permute-start(bf16[8,4,16,128]{3,2,1,0:T(8,128)(2,1)S(1)} %collective-permute-done.1.rest_2_), channel_id=1, source_target_pairs={{0,8},{8,16},{16,24},{24,28},{28,20},{20,12},{12,4},{4,0},{1,9},{9... | collective-permute-start | bytes 393224 | tf_op jit(solution)/shard_map/ppermute | solution.py:576
  15.4 0.4 collective-permute-start.5
  15.9 0.3 collective-permute-done.9.rest_5_
  16.1 2.0 %collective-permute-done.8.rest_4_ = bf16[8,4,16,128]{3,2,1,0:T(8,128)(2,1)S(1)} collective-permute-done((bf16[8,4,16,128]{3,2,1,0:T(8,128)(2,1)S(1)}, bf16[8,4,16,128]{3,2,1,0:T(8,128)(2,1)S(1)}, u32[]{:S(2)}, u32[]{:S(2)}) %collective-permute-start.8) | collective-permute-done | bytes 131104 | tf_op jit(solution)/shard_map/ppermute | solution.py:576
  18.1 2.0 %collective-permute-start.11 = (bf16[8,4,16,128]{3,2,1,0:T(8,128)(2,1)S(1)}, bf16[8,4,16,128]{3,2,1,0:T(8,128)(2,1)S(1)}, u32[]{:S(2)}, u32[]{:S(2)}) collective-permute-start(bf16[8,4,16,128]{3,2,1,0:T(8,128)(2,1)S(1)} %collective-permute-done.9.rest_5_), channel_id=1, source_target_pairs={{0,4},{8,0},{16,8},{24,16},{28,24},{20,28},{12,20},{4,12},{1,5},{9... | collective-permute-start | bytes 393224 | tf_op jit(solution)/shard_map/ppermute | solution.py:579
  20.2 0.8 %collective-permute-done.4.refs_0_.rest_6_ = bf16[8,4,16,128]{3,2,1,0:T(8,128)(2,1)S(1)} collective-permute-done((bf16[8,4,16,128]{3,2,1,0:T(8,128)(2,1)S(1)}, bf16[8,4,16,128]{3,2,1,0:T(8,128)(2,1)S(1)}, u32[]{:S(2)}, u32[]{:S(2)}) %collective-permute-start.4) | collective-permute-done | bytes 131104 | tf_op jit(solution)/shard_map/ppermute | solution.py:576
  20.9 0.2 collective-permute-done.5.refs_1_.rest_7_
  21.1 2.0 %collective-permute-done.10.refs_2_.rest_8_ = bf16[8,4,16,128]{3,2,1,0:T(8,128)(2,1)S(1)} collective-permute-done((bf16[8,4,16,128]{3,2,1,0:T(8,128)(2,1)S(1)}, bf16[8,4,16,128]{3,2,1,0:T(8,128)(2,1)S(1)}, u32[]{:S(2)}, u32[]{:S(2)}) %collective-permute-start.10) | collective-permute-done | bytes 131104 | tf_op jit(solution)/shard_map/ppermute | solution.py:576
  23.3 1.6 %collective-permute-start.17 = (bf16[16,4,16,128]{3,2,1,0:T(8,128)(2,1)S(1)}, bf16[16,4,16,128]{3,2,1,0:T(8,128)(2,1)S(1)}, u32[]{:S(2)}, u32[]{:S(2)}) collective-permute-start(bf16[16,4,16,128]{3,2,1,0:T(8,128)(2,1)S(1)} %get-tuple-element.61), channel_id=1, source_target_pairs={{0,8},{8,16},{16,24},{24,28},{28,20},{20,12},{12,4},{4,0},{1,9},{9... | collective-permute-start | bytes 786440 | tf_op jit(solution)/shard_map/ppermute | solution.py:576
  25.0 0.5 collective-permute-start.18
  25.6 2.7 %cross.3 = (bf16[64,512]{1,0:T(8,128)(2,1)S(1)}, bf16[64,512]{1,0:T(8,128)(2,1)S(1)}, bf16[64,512]{1,0:T(8,128)(2,1)S(1)}, bf16[64,512]{1,0:T(8,128)(2,1)S(1)}) custom-call(s32[4,8]{1,0:T(4,128)S(1)} %copy-done.1, bf16[2048,512]{1,0:T(8,128)(2,1)S(1)} %copy-done.2, f32[4,3,8,4,8,128]{5,4,3,2,1,0:T(8,128)S(1)} %widen.2.rest_0_, ...), custom_call_target="tpu_custom_call" | custom-call | flops 2990000128 | bytes 1024 | tf_op jit(solution)/shard_map/cross/pallas_call | solution.py:390
  28.4 1.8 %collective-permute-start.15 = (bf16[64,512]{1,0:T(8,128)(2,1)S(1)}, bf16[64,512]{1,0:T(8,128)(2,1)S(1)}, u32[]{:S(2)}, u32[]{:S(2)}) collective-permute-start(bf16[64,512]{1,0:T(8,128)(2,1)S(1)} %get-tuple-element.58), channel_id=1, source_target_pairs={{0,2},{1,3},{2,0},{3,1},{4,6},{5,7},{6,4},{7,5},{8,10},{9,11},{10,... | collective-permute-start | bytes 196616 | tf_op jit(solution)/shard_map/ppermute | solution.py:543
  30.2 2.0 %collective-permute-done.17.rest_10_ = bf16[16,4,16,128]{3,2,1,0:T(8,128)(2,1)S(1)} collective-permute-done((bf16[16,4,16,128]{3,2,1,0:T(8,128)(2,1)S(1)}, bf16[16,4,16,128]{3,2,1,0:T(8,128)(2,1)S(1)}, u32[]{:S(2)}, u32[]{:S(2)}) %collective-permute-start.17) | collective-permute-done | bytes 262176 | tf_op jit(solution)/shard_map/ppermute | solution.py:576
  32.2 1.4 %collective-permute-start.22 = (bf16[16,4,16,128]{3,2,1,0:T(8,128)(2,1)S(1)}, bf16[16,4,16,128]{3,2,1,0:T(8,128)(2,1)S(1)}, u32[]{:S(2)}, u32[]{:S(2)}) collective-permute-start(bf16[16,4,16,128]{3,2,1,0:T(8,128)(2,1)S(1)} %collective-permute-done.17.rest_10_), channel_id=1, source_target_pairs={{0,8},{8,16},{16,24},{24,28},{28,20},{20,12},{12,4},{4,0},{1,9},{9... | collective-permute-start | bytes 786440 | tf_op jit(solution)/shard_map/ppermute | solution.py:576
  33.6 4.9 %cross.4 = (bf16[128,512]{1,0:T(8,128)(2,1)S(1)}, bf16[128,512]{1,0:T(8,128)(2,1)S(1)}, bf16[128,512]{1,0:T(8,128)(2,1)S(1)}, bf16[128,512]{1,0:T(8,128)(2,1)S(1)}) custom-call(s32[4,8]{1,0:T(4,128)S(1)} %copy-done.1, bf16[2048,512]{1,0:T(8,128)(2,1)S(1)} %copy-done.2, f32[4,3,8,4,8,128]{5,4,3,2,1,0:T(8,128)S(1)} %widen.2.rest_0_, ...), custom_call_target="tpu_custom_call" | custom-call | flops 5289999872 | bytes 1024 | tf_op jit(solution)/shard_map/cross/pallas_call | solution.py:390
  38.6 1.8 %collective-permute-start.20 = (bf16[128,512]{1,0:T(8,128)(2,1)S(1)}, bf16[128,512]{1,0:T(8,128)(2,1)S(1)}, u32[]{:S(2)}, u32[]{:S(2)}) collective-permute-start(bf16[128,512]{1,0:T(8,128)(2,1)S(1)} %get-tuple-element.65), channel_id=1, source_target_pairs={{0,2},{1,3},{2,0},{3,1},{4,6},{5,7},{6,4},{7,5},{8,10},{9,11},{10,... | collective-permute-start | bytes 393224 | tf_op jit(solution)/shard_map/ppermute | solution.py:543
  40.5 2.7 %cross.5 = (bf16[64,512]{1,0:T(8,128)(2,1)S(1)}, bf16[64,512]{1,0:T(8,128)(2,1)S(1)}, bf16[64,512]{1,0:T(8,128)(2,1)S(1)}, bf16[64,512]{1,0:T(8,128)(2,1)S(1)}) custom-call(s32[4,8]{1,0:T(4,128)S(1)} %copy-done.1, bf16[2048,512]{1,0:T(8,128)(2,1)S(1)} %copy-done.2, f32[4,3,8,4,8,128]{5,4,3,2,1,0:T(8,128)S(1)} %widen.2.rest_0_, ...), custom_call_target="tpu_custom_call" | custom-call | flops 2990000128 | bytes 1024 | tf_op jit(solution)/shard_map/cross/pallas_call | solution.py:390
  43.2 0.4 collective-permute-start.23
  43.6 1.7 %collective-permute-start.24 = (bf16[64,512]{1,0:T(8,128)(2,1)S(1)}, bf16[64,512]{1,0:T(8,128)(2,1)S(1)}, u32[]{:S(2)}, u32[]{:S(2)}) collective-permute-start(bf16[64,512]{1,0:T(8,128)(2,1)S(1)} %get-tuple-element.71), channel_id=1, source_target_pairs={{0,2},{1,3},{2,0},{3,1},{4,6},{5,7},{6,4},{7,5},{8,10},{9,11},{10,... | collective-permute-start | bytes 196616 | tf_op jit(solution)/shard_map/ppermute | solution.py:543
  45.3 1.7 %collective-permute-done.21.rest_7_ = bf16[128,512]{1,0:T(8,128)(2,1)S(1)} collective-permute-done((bf16[128,512]{1,0:T(8,128)(2,1)S(1)}, bf16[128,512]{1,0:T(8,128)(2,1)S(1)}, u32[]{:S(2)}, u32[]{:S(2)}) %collective-permute-start.21) | collective-permute-done | bytes 131104 | tf_op jit(solution)/shard_map/ppermute | solution.py:543
  47.0 2.1 %early.1 = f32[1024,4,1,128]{3,2,1,0:T(1,128)} custom-call(s32[4,8]{1,0:T(4,128)S(1)} %copy-done.1, bf16[4,128,512]{2,1,0:T(8,128)(2,1)S(1)} %copy-done, bf16[64,512]{1,0:T(8,128)(2,1)S(1)} %get-tuple-element.56.rest_0_, bf16[64,512]{1,0:T(8,128)(2,1)S(1)} %collective-permute-done.14.rest_1_, bf16[64,512]{1,0:T(8,128)(2,1)S(1)} %collective-permute-done.15.rest_2_, ...), custom_call_target="tpu_custom_call" | custom-call | flops 57500000 | bytes 1024 | tf_op jit(solution)/shard_map/early/pallas_call | solution.py:489
  49.2 0.6 %collective-permute-done.25.rest_3_ = bf16[64,512]{1,0:T(8,128)(2,1)S(1)} collective-permute-done((bf16[64,512]{1,0:T(8,128)(2,1)S(1)}, bf16[64,512]{1,0:T(8,128)(2,1)S(1)}, u32[]{:S(2)}, u32[]{:S(2)}) %collective-permute-start.25) | collective-permute-done | bytes 65568 | tf_op jit(solution)/shard_map/ppermute | solution.py:543
  49.8 1.6 %late.1 = f32[1024,4,1,128]{3,2,1,0:T(1,128)} custom-call(s32[4,8]{1,0:T(4,128)S(1)} %copy-done.1, bf16[4,128,512]{2,1,0:T(8,128)(2,1)S(1)} %copy-done, f32[1024,4,1,128]{3,2,1,0:T(1,128)} %early.1, bf16[64,512]{1,0:T(8,128)(2,1)S(1)} %get-tuple-element.69.rest_0_, ...), custom_call_target="tpu_custom_call", output_to_operand_aliasing={{}: (2, {})} | custom-call | flops 57500000 | bytes 1024 | tf_op jit(solution)/shard_map/late/pallas_call | solution.py:502
  (38 shorter events, 1.2 us)
Async XLA Ops:
  3.0 3.3 %collective-permute-start = (bf16[4,4,16,128]{3,2,1,0:T(8,128)(2,1)S(1)}, bf16[4,4,16,128]{3,2,1,0:T(8,128)(2,1)S(1)}, u32[]{:S(2)}, u32[]{:S(2)}) collective-permute-start(bf16[4,4,16,128]{3,2,1,0:T(8,128)(2,1)S(1)} %get-tuple-element.40), channel_id=1, source_target_pairs={{0,1},{1,0},{2,3},{3,2},{4,5},{5,4},{6,7},{7,6},{8,9},{9,8},{10,11... | collective-permute-start | bytes 196616 | tf_op jit(solution)/shard_map/ppermute | solution.py:543
  3.6 5.3 %collective-permute-start.6 = (bf16[4,4,16,128]{3,2,1,0:T(8,128)(2,1)S(1)}, bf16[4,4,16,128]{3,2,1,0:T(8,128)(2,1)S(1)}, u32[]{:S(2)}, u32[]{:S(2)}) collective-permute-start(bf16[4,4,16,128]{3,2,1,0:T(8,128)(2,1)S(1)} %get-tuple-element.45), channel_id=1, source_target_pairs={{0,2},{1,3},{2,0},{3,1},{4,6},{5,7},{6,4},{7,5},{8,10},{9,11},{10,... | collective-permute-start | bytes 196616 | tf_op jit(solution)/shard_map/ppermute | solution.py:543
  6.1 4.0 %collective-permute-start.7 = (bf16[4,4,16,128]{3,2,1,0:T(8,128)(2,1)S(1)}, bf16[4,4,16,128]{3,2,1,0:T(8,128)(2,1)S(1)}, u32[]{:S(2)}, u32[]{:S(2)}) collective-permute-start(bf16[4,4,16,128]{3,2,1,0:T(8,128)(2,1)S(1)} %get-tuple-element.46), channel_id=1, source_target_pairs={{0,3},{1,2},{2,1},{3,0},{4,7},{5,6},{6,5},{7,4},{8,11},{9,10},{10,... | collective-permute-start | bytes 196616 | tf_op jit(solution)/shard_map/ppermute | solution.py:543
  6.2 4.0 %collective-permute-start.3 = (bf16[4,16,16,128]{3,2,1,0:T(8,128)(2,1)S(1)}, bf16[4,16,16,128]{3,2,1,0:T(8,128)(2,1)S(1)}, u32[]{:S(2)}, u32[]{:S(2)}) collective-permute-start(bf16[4,16,16,128]{3,2,1,0:T(8,128)(2,1)S(1)} %get-tuple-element.54.refs_0_), channel_id=1, source_target_pairs={{0,1},{1,0},{2,3},{3,2},{4,5},{5,4},{6,7},{7,6},{8,9},{9,8},{10,11... | collective-permute-start | bytes 786440 | tf_op jit(solution)/shard_map/ppermute | solution.py:543
  6.4 7.4 %collective-permute-start.2 = (bf16[8,4,16,128]{3,2,1,0:T(8,128)(2,1)S(1)}, bf16[8,4,16,128]{3,2,1,0:T(8,128)(2,1)S(1)}, u32[]{:S(2)}, u32[]{:S(2)}) collective-permute-start(bf16[8,4,16,128]{3,2,1,0:T(8,128)(2,1)S(1)} %constant_dynamic-update-slice_fusion), channel_id=1, source_target_pairs={{0,4},{8,0},{16,8},{24,16},{28,24},{20,28},{12,20},{4,12},{1,5},{9... | collective-permute-start | bytes 393224 | tf_op jit(solution)/shard_map/ppermute | solution.py:579
  8.4 5.4 %collective-permute-start.1 = (bf16[8,4,16,128]{3,2,1,0:T(8,128)(2,1)S(1)}, bf16[8,4,16,128]{3,2,1,0:T(8,128)(2,1)S(1)}, u32[]{:S(2)}, u32[]{:S(2)}) collective-permute-start(bf16[8,4,16,128]{3,2,1,0:T(8,128)(2,1)S(1)} %constant_dynamic-update-slice_fusion), channel_id=1, source_target_pairs={{0,8},{8,16},{16,24},{24,28},{28,20},{20,12},{12,4},{4,0},{1,9},{9... | collective-permute-start | bytes 393224 | tf_op jit(solution)/shard_map/ppermute | solution.py:576
  10.2 15.4 %copy-start.1 = (s32[4,8]{1,0:T(4,128)S(1)}, s32[4,8]{1,0:T(4,128)}, u32[]{:S(2)}) copy-start(s32[4,8]{1,0:T(4,128)} %plan.9) | copy-start | bytes 388
  10.2 15.4 %copy-start.2 = (bf16[2048,512]{1,0:T(8,128)(2,1)S(1)}, bf16[2048,512]{1,0:T(8,128)(2,1)}, u32[]{:S(2)}) copy-start(bf16[2048,512]{1,0:T(8,128)(2,1)} %constant.7.clone.table) | copy-start | bytes 6291460
  10.2 5.9 %collective-permute-start.9 = (bf16[8,4,16,128]{3,2,1,0:T(8,128)(2,1)S(1)}, bf16[8,4,16,128]{3,2,1,0:T(8,128)(2,1)S(1)}, u32[]{:S(2)}, u32[]{:S(2)}) collective-permute-start(bf16[8,4,16,128]{3,2,1,0:T(8,128)(2,1)S(1)} %pad_maximum_fusion), channel_id=1, source_target_pairs={{0,4},{8,0},{16,8},{24,16},{28,24},{20,28},{12,20},{4,12},{1,5},{9... | collective-permute-start | bytes 393224 | tf_op jit(solution)/shard_map/ppermute | solution.py:579
  11.8 6.3 %collective-permute-start.8 = (bf16[8,4,16,128]{3,2,1,0:T(8,128)(2,1)S(1)}, bf16[8,4,16,128]{3,2,1,0:T(8,128)(2,1)S(1)}, u32[]{:S(2)}, u32[]{:S(2)}) collective-permute-start(bf16[8,4,16,128]{3,2,1,0:T(8,128)(2,1)S(1)} %pad_maximum_fusion), channel_id=1, source_target_pairs={{0,8},{8,16},{16,24},{24,28},{28,20},{20,12},{12,4},{4,0},{1,9},{9... | collective-permute-start | bytes 393224 | tf_op jit(solution)/shard_map/ppermute | solution.py:576
  12.3 10.9 %collective-permute-start.12 = (bf16[4,16,16,128]{3,2,1,0:T(8,128)(2,1)S(1)}, bf16[4,16,16,128]{3,2,1,0:T(8,128)(2,1)S(1)}, u32[]{:S(2)}, u32[]{:S(2)}) collective-permute-start(bf16[4,16,16,128]{3,2,1,0:T(8,128)(2,1)S(1)} %get-tuple-element.54.refs_0_), channel_id=1, source_target_pairs={{0,2},{1,3},{2,0},{3,1},{4,6},{5,7},{6,4},{7,5},{8,10},{9,11},{10,... | collective-permute-start | bytes 786440 | tf_op jit(solution)/shard_map/ppermute | solution.py:543
  13.8 7.1 %collective-permute-start.4 = (bf16[8,4,16,128]{3,2,1,0:T(8,128)(2,1)S(1)}, bf16[8,4,16,128]{3,2,1,0:T(8,128)(2,1)S(1)}, u32[]{:S(2)}, u32[]{:S(2)}) collective-permute-start(bf16[8,4,16,128]{3,2,1,0:T(8,128)(2,1)S(1)} %collective-permute-done.1.rest_2_), channel_id=1, source_target_pairs={{0,8},{8,16},{16,24},{24,28},{28,20},{20,12},{12,4},{4,0},{1,9},{9... | collective-permute-start | bytes 393224 | tf_op jit(solution)/shard_map/ppermute | solution.py:576
  15.4 5.7 %collective-permute-start.5 = (bf16[8,4,16,128]{3,2,1,0:T(8,128)(2,1)S(1)}, bf16[8,4,16,128]{3,2,1,0:T(8,128)(2,1)S(1)}, u32[]{:S(2)}, u32[]{:S(2)}) collective-permute-start(bf16[8,4,16,128]{3,2,1,0:T(8,128)(2,1)S(1)} %collective-permute-done.2.rest_3_), channel_id=1, source_target_pairs={{0,4},{8,0},{16,8},{24,16},{28,24},{20,28},{12,20},{4,12},{1,5},{9... | collective-permute-start | bytes 393224 | tf_op jit(solution)/shard_map/ppermute | solution.py:579
  18.1 5.0 %collective-permute-start.10 = (bf16[8,4,16,128]{3,2,1,0:T(8,128)(2,1)S(1)}, bf16[8,4,16,128]{3,2,1,0:T(8,128)(2,1)S(1)}, u32[]{:S(2)}, u32[]{:S(2)}) collective-permute-start(bf16[8,4,16,128]{3,2,1,0:T(8,128)(2,1)S(1)} %collective-permute-done.8.rest_4_), channel_id=1, source_target_pairs={{0,8},{8,16},{16,24},{24,28},{28,20},{20,12},{12,4},{4,0},{1,9},{9... | collective-permute-start | bytes 393224 | tf_op jit(solution)/shard_map/ppermute | solution.py:576
  18.1 5.1 %collective-permute-start.11 = (bf16[8,4,16,128]{3,2,1,0:T(8,128)(2,1)S(1)}, bf16[8,4,16,128]{3,2,1,0:T(8,128)(2,1)S(1)}, u32[]{:S(2)}, u32[]{:S(2)}) collective-permute-start(bf16[8,4,16,128]{3,2,1,0:T(8,128)(2,1)S(1)} %collective-permute-done.9.rest_5_), channel_id=1, source_target_pairs={{0,4},{8,0},{16,8},{24,16},{28,24},{20,28},{12,20},{4,12},{1,5},{9... | collective-permute-start | bytes 393224 | tf_op jit(solution)/shard_map/ppermute | solution.py:579
  23.3 2.2 %collective-permute-start.13 = (bf16[4,16,16,128]{3,2,1,0:T(8,128)(2,1)S(1)}, bf16[4,16,16,128]{3,2,1,0:T(8,128)(2,1)S(1)}, u32[]{:S(2)}, u32[]{:S(2)}) collective-permute-start(bf16[4,16,16,128]{3,2,1,0:T(8,128)(2,1)S(1)} %collective-permute-done.12.refs_0_), channel_id=1, source_target_pairs={{0,1},{1,0},{2,3},{3,2},{4,5},{5,4},{6,7},{7,6},{8,9},{9,8},{10,11... | collective-permute-start | bytes 786440 | tf_op jit(solution)/shard_map/ppermute | solution.py:543
  23.3 8.9 %collective-permute-start.17 = (bf16[16,4,16,128]{3,2,1,0:T(8,128)(2,1)S(1)}, bf16[16,4,16,128]{3,2,1,0:T(8,128)(2,1)S(1)}, u32[]{:S(2)}, u32[]{:S(2)}) collective-permute-start(bf16[16,4,16,128]{3,2,1,0:T(8,128)(2,1)S(1)} %get-tuple-element.61), channel_id=1, source_target_pairs={{0,8},{8,16},{16,24},{24,28},{28,20},{20,12},{12,4},{4,0},{1,9},{9... | collective-permute-start | bytes 786440 | tf_op jit(solution)/shard_map/ppermute | solution.py:576
  25.0 8.7 %collective-permute-start.18 = (bf16[16,4,16,128]{3,2,1,0:T(8,128)(2,1)S(1)}, bf16[16,4,16,128]{3,2,1,0:T(8,128)(2,1)S(1)}, u32[]{:S(2)}, u32[]{:S(2)}) collective-permute-start(bf16[16,4,16,128]{3,2,1,0:T(8,128)(2,1)S(1)} %get-tuple-element.62), channel_id=1, source_target_pairs={{0,4},{8,0},{16,8},{24,16},{28,24},{20,28},{12,20},{4,12},{1,5},{9... | collective-permute-start | bytes 786440 | tf_op jit(solution)/shard_map/ppermute | solution.py:579
  28.2 10.3 %collective-permute-start.14 = (bf16[64,512]{1,0:T(8,128)(2,1)S(1)}, bf16[64,512]{1,0:T(8,128)(2,1)S(1)}, u32[]{:S(2)}, u32[]{:S(2)}) collective-permute-start(bf16[64,512]{1,0:T(8,128)(2,1)S(1)} %get-tuple-element.57), channel_id=1, source_target_pairs={{0,1},{1,0},{2,3},{3,2},{4,5},{5,4},{6,7},{7,6},{8,9},{9,8},{10,11... | collective-permute-start | bytes 196616 | tf_op jit(solution)/shard_map/ppermute | solution.py:543
  28.4 12.0 %collective-permute-start.15 = (bf16[64,512]{1,0:T(8,128)(2,1)S(1)}, bf16[64,512]{1,0:T(8,128)(2,1)S(1)}, u32[]{:S(2)}, u32[]{:S(2)}) collective-permute-start(bf16[64,512]{1,0:T(8,128)(2,1)S(1)} %get-tuple-element.58), channel_id=1, source_target_pairs={{0,2},{1,3},{2,0},{3,1},{4,6},{5,7},{6,4},{7,5},{8,10},{9,11},{10,... | collective-permute-start | bytes 196616 | tf_op jit(solution)/shard_map/ppermute | solution.py:543
  30.1 10.4 %collective-permute-start.16 = (bf16[64,512]{1,0:T(8,128)(2,1)S(1)}, bf16[64,512]{1,0:T(8,128)(2,1)S(1)}, u32[]{:S(2)}, u32[]{:S(2)}) collective-permute-start(bf16[64,512]{1,0:T(8,128)(2,1)S(1)} %get-tuple-element.59), channel_id=1, source_target_pairs={{0,3},{1,2},{2,1},{3,0},{4,7},{5,6},{6,5},{7,4},{8,11},{9,10},{10,... | collective-permute-start | bytes 196616 | tf_op jit(solution)/shard_map/ppermute | solution.py:543
  32.2 8.3 %collective-permute-start.22 = (bf16[16,4,16,128]{3,2,1,0:T(8,128)(2,1)S(1)}, bf16[16,4,16,128]{3,2,1,0:T(8,128)(2,1)S(1)}, u32[]{:S(2)}, u32[]{:S(2)}) collective-permute-start(bf16[16,4,16,128]{3,2,1,0:T(8,128)(2,1)S(1)} %collective-permute-done.17.rest_10_), channel_id=1, source_target_pairs={{0,8},{8,16},{16,24},{24,28},{28,20},{20,12},{12,4},{4,0},{1,9},{9... | collective-permute-start | bytes 786440 | tf_op jit(solution)/shard_map/ppermute | solution.py:576
  38.5 6.8 %collective-permute-start.19 = (bf16[128,512]{1,0:T(8,128)(2,1)S(1)}, bf16[128,512]{1,0:T(8,128)(2,1)S(1)}, u32[]{:S(2)}, u32[]{:S(2)}) collective-permute-start(bf16[128,512]{1,0:T(8,128)(2,1)S(1)} %get-tuple-element.64), channel_id=1, source_target_pairs={{0,1},{1,0},{2,3},{3,2},{4,5},{5,4},{6,7},{7,6},{8,9},{9,8},{10,11... | collective-permute-start | bytes 393224 | tf_op jit(solution)/shard_map/ppermute | solution.py:543
  38.6 6.8 %collective-permute-start.20 = (bf16[128,512]{1,0:T(8,128)(2,1)S(1)}, bf16[128,512]{1,0:T(8,128)(2,1)S(1)}, u32[]{:S(2)}, u32[]{:S(2)}) collective-permute-start(bf16[128,512]{1,0:T(8,128)(2,1)S(1)} %get-tuple-element.65), channel_id=1, source_target_pairs={{0,2},{1,3},{2,0},{3,1},{4,6},{5,7},{6,4},{7,5},{8,10},{9,11},{10,... | collective-permute-start | bytes 393224 | tf_op jit(solution)/shard_map/ppermute | solution.py:543
  40.4 6.6 %collective-permute-start.21 = (bf16[128,512]{1,0:T(8,128)(2,1)S(1)}, bf16[128,512]{1,0:T(8,128)(2,1)S(1)}, u32[]{:S(2)}, u32[]{:S(2)}) collective-permute-start(bf16[128,512]{1,0:T(8,128)(2,1)S(1)} %get-tuple-element.66), channel_id=1, source_target_pairs={{0,3},{1,2},{2,1},{3,0},{4,7},{5,6},{6,5},{7,4},{8,11},{9,10},{10,... | collective-permute-start | bytes 393224 | tf_op jit(solution)/shard_map/ppermute | solution.py:543
  40.5 6.5 %copy-start = (bf16[4,128,512]{2,1,0:T(8,128)(2,1)S(1)}, bf16[4,128,512]{2,1,0:T(8,128)(2,1)}, u32[]{:S(2)}) copy-start(bf16[4,128,512]{2,1,0:T(8,128)(2,1)} %constant.8.clone.place) | copy-start | bytes 1572868
  43.2 5.9 %collective-permute-start.23 = (bf16[64,512]{1,0:T(8,128)(2,1)S(1)}, bf16[64,512]{1,0:T(8,128)(2,1)S(1)}, u32[]{:S(2)}, u32[]{:S(2)}) collective-permute-start(bf16[64,512]{1,0:T(8,128)(2,1)S(1)} %get-tuple-element.70), channel_id=1, source_target_pairs={{0,1},{1,0},{2,3},{3,2},{4,5},{5,4},{6,7},{7,6},{8,9},{9,8},{10,11... | collective-permute-start | bytes 196616 | tf_op jit(solution)/shard_map/ppermute | solution.py:543
  43.6 5.6 %collective-permute-start.24 = (bf16[64,512]{1,0:T(8,128)(2,1)S(1)}, bf16[64,512]{1,0:T(8,128)(2,1)S(1)}, u32[]{:S(2)}, u32[]{:S(2)}) collective-permute-start(bf16[64,512]{1,0:T(8,128)(2,1)S(1)} %get-tuple-element.71), channel_id=1, source_target_pairs={{0,2},{1,3},{2,0},{3,1},{4,6},{5,7},{6,4},{7,5},{8,10},{9,11},{10,... | collective-permute-start | bytes 196616 | tf_op jit(solution)/shard_map/ppermute | solution.py:543
  45.3 4.5 %collective-permute-start.25 = (bf16[64,512]{1,0:T(8,128)(2,1)S(1)}, bf16[64,512]{1,0:T(8,128)(2,1)S(1)}, u32[]{:S(2)}, u32[]{:S(2)}) collective-permute-start(bf16[64,512]{1,0:T(8,128)(2,1)S(1)} %get-tuple-element.72), channel_id=1, source_target_pairs={{0,3},{1,2},{2,1},{3,0},{4,7},{5,6},{6,5},{7,4},{8,11},{9,10},{10,... | collective-permute-start | bytes 196616 | tf_op jit(solution)/shard_map/ppermute | solution.py:543

commit v17 on v15

--- a/solution.py
+++ b/solution.py
@@ -17,7 +17,7 @@
 LANES = 128
 TILES = NBIN // LANES
 CHUNKS = 4
-GROUP = 4
+GROUP = 8
 BF = jnp.bfloat16
 F32 = jnp.float32
 

time: 51.3 us -> 51.1 us (level)
  no operation moved by 1% of the time
where the time goes in v17:
time: 51.1 us; the launch traced here: 50.9 us
  starting transfers between devices  22.4 us (44%)
  Pallas kernels  16.7 us (33%)
  waiting for transfers between devices  11.6 us (23%)
    ppermute x15, starting transfers between devices, swap(): return lax.ppermute(value, 'seg', [(i, i ^ j) for i in range(parts)])  10.6 us
    pallas_call x3, Pallas kernels, cross_lags(): pl.pallas_call(functools.partial(cross_kernel, first_slot, slots, count,...  9.65 us
    ppermute x6, waiting for transfers between devices, up(): return lax.ppermute(value, 'sta', upward)  7.12 us
    ppermute x5, starting transfers between devices, down(): return lax.ppermute(value, 'sta', downward)  6.51 us
    ppermute x6, starting transfers between devices, up(): return lax.ppermute(value, 'sta', upward)  5.28 us
    ppermute x15, waiting for transfers between devices, swap(): return lax.ppermute(value, 'seg', [(i, i ^ j) for i in range(parts)])  3.95 us
    pallas_call x1, Pallas kernels, prepare(): pl.pallas_call(functools.partial(prep_kernel, parts, windows), out_shape=...  3.04 us
    pallas_call x1, Pallas kernels, place_lags(): pl.pallas_call(functools.partial(early_kernel, count, parts, tuple(groups...  2.1 us
  transfers between devices with their start and end apart: 26, of which 12 were waited for; matrix products, arithmetic and copies ran while one was open for 0% of the time, Pallas kernels for 24%

profile of v17, /device:TPU:0, one launch (start us, length us, event | category | flops | bytes accessed | tf_op | source)
XLA Modules:
  0.0 50.9 jit_solution(14498668440415781199)
XLA Ops:
  0.0 3.0 %prep.1 = (bf16[4,16,16,128]{3,2,1,0:T(8,128)(2,1)S(1)}, bf16[4,4,16,128]{3,2,1,0:T(8,128)(2,1)S(1)}, bf16[4,4,16,128]{3,2,1,0:T(8,128)(2,1)S(1)}, bf16[4,4,16,1...) custom-call(f32[1024,128]{1,0:T(8,128)} %bitcast.10, bf16[512,2048]{1,0:T(8,128)(2,1)} %constant.6.clone.table_hbm), custom_call_target="tpu_custom_call" | custom-call | flops 536870912 | bytes 3145728 | tf_op jit(solution)/shard_map/prep/pallas_call | solution.py:169
  3.0 0.5 %collective-permute-start = (bf16[4,4,16,128]{3,2,1,0:T(8,128)(2,1)S(1)}, bf16[4,4,16,128]{3,2,1,0:T(8,128)(2,1)S(1)}, u32[]{:S(2)}, u32[]{:S(2)}) collective-permute-start(bf16[4,4,16,128]{3,2,1,0:T(8,128)(2,1)S(1)} %get-tuple-element.40), channel_id=1, source_target_pairs={{0,1},{1,0},{2,3},{3,2},{4,5},{5,4},{6,7},{7,6},{8,9},{9,8},{10,11... | collective-permute-start | bytes 196616 | tf_op jit(solution)/shard_map/ppermute | solution.py:512
  3.6 2.6 %collective-permute-start.6 = (bf16[4,4,16,128]{3,2,1,0:T(8,128)(2,1)S(1)}, bf16[4,4,16,128]{3,2,1,0:T(8,128)(2,1)S(1)}, u32[]{:S(2)}, u32[]{:S(2)}) collective-permute-start(bf16[4,4,16,128]{3,2,1,0:T(8,128)(2,1)S(1)} %get-tuple-element.45), channel_id=1, source_target_pairs={{0,2},{1,3},{2,0},{3,1},{4,6},{5,7},{6,4},{7,5},{8,10},{9,11},{10,... | collective-permute-start | bytes 196616 | tf_op jit(solution)/shard_map/ppermute | solution.py:512
  6.4 2.0 %collective-permute-start.2 = (bf16[8,4,16,128]{3,2,1,0:T(8,128)(2,1)S(1)}, bf16[8,4,16,128]{3,2,1,0:T(8,128)(2,1)S(1)}, u32[]{:S(2)}, u32[]{:S(2)}) collective-permute-start(bf16[8,4,16,128]{3,2,1,0:T(8,128)(2,1)S(1)} %constant_dynamic-update-slice_fusion), channel_id=1, source_target_pairs={{0,4},{8,0},{16,8},{24,16},{28,24},{20,28},{12,20},{4,12},{1,5},{9... | collective-permute-start | bytes 393224 | tf_op jit(solution)/shard_map/ppermute | solution.py:548
  8.5 0.3 collective-permute-done.6
  8.8 1.4 %collective-permute-done.7 = bf16[4,4,16,128]{3,2,1,0:T(8,128)(2,1)S(1)} collective-permute-done((bf16[4,4,16,128]{3,2,1,0:T(8,128)(2,1)S(1)}, bf16[4,4,16,128]{3,2,1,0:T(8,128)(2,1)S(1)}, u32[]{:S(2)}, u32[]{:S(2)}) %collective-permute-start.7) | collective-permute-done | bytes 65568 | tf_op jit(solution)/shard_map/ppermute | solution.py:512
  10.2 1.6 %collective-permute-start.9 = (bf16[8,4,16,128]{3,2,1,0:T(8,128)(2,1)S(1)}, bf16[8,4,16,128]{3,2,1,0:T(8,128)(2,1)S(1)}, u32[]{:S(2)}, u32[]{:S(2)}) collective-permute-start(bf16[8,4,16,128]{3,2,1,0:T(8,128)(2,1)S(1)} %pad_maximum_fusion), channel_id=1, source_target_pairs={{0,4},{8,0},{16,8},{24,16},{28,24},{20,28},{12,20},{4,12},{1,5},{9... | collective-permute-start | bytes 393224 | tf_op jit(solution)/shard_map/ppermute | solution.py:548
  11.8 0.5 collective-permute-start.8
  12.3 1.3 %collective-permute-start.12 = (bf16[4,16,16,128]{3,2,1,0:T(8,128)(2,1)S(1)}, bf16[4,16,16,128]{3,2,1,0:T(8,128)(2,1)S(1)}, u32[]{:S(2)}, u32[]{:S(2)}) collective-permute-start(bf16[4,16,16,128]{3,2,1,0:T(8,128)(2,1)S(1)} %get-tuple-element.54.refs_0_), channel_id=1, source_target_pairs={{0,2},{1,3},{2,0},{3,1},{4,6},{5,7},{6,4},{7,5},{8,10},{9,11},{10,... | collective-permute-start | bytes 786440 | tf_op jit(solution)/shard_map/ppermute | solution.py:512
  13.8 1.6 %collective-permute-start.4 = (bf16[8,4,16,128]{3,2,1,0:T(8,128)(2,1)S(1)}, bf16[8,4,16,128]{3,2,1,0:T(8,128)(2,1)S(1)}, u32[]{:S(2)}, u32[]{:S(2)}) collective-permute-start(bf16[8,4,16,128]{3,2,1,0:T(8,128)(2,1)S(1)} %collective-permute-done.1.rest_2_), channel_id=1, source_target_pairs={{0,8},{8,16},{16,24},{24,28},{28,20},{20,12},{12,4},{4,0},{1,9},{9... | collective-permute-start | bytes 393224 | tf_op jit(solution)/shard_map/ppermute | solution.py:545
  15.4 0.4 collective-permute-start.5
  15.9 0.3 collective-permute-done.9.rest_5_
  16.1 2.0 %collective-permute-done.8.rest_4_ = bf16[8,4,16,128]{3,2,1,0:T(8,128)(2,1)S(1)} collective-permute-done((bf16[8,4,16,128]{3,2,1,0:T(8,128)(2,1)S(1)}, bf16[8,4,16,128]{3,2,1,0:T(8,128)(2,1)S(1)}, u32[]{:S(2)}, u32[]{:S(2)}) %collective-permute-start.8) | collective-permute-done | bytes 131104 | tf_op jit(solution)/shard_map/ppermute | solution.py:545
  18.1 2.0 %collective-permute-start.11 = (bf16[8,4,16,128]{3,2,1,0:T(8,128)(2,1)S(1)}, bf16[8,4,16,128]{3,2,1,0:T(8,128)(2,1)S(1)}, u32[]{:S(2)}, u32[]{:S(2)}) collective-permute-start(bf16[8,4,16,128]{3,2,1,0:T(8,128)(2,1)S(1)} %collective-permute-done.9.rest_5_), channel_id=1, source_target_pairs={{0,4},{8,0},{16,8},{24,16},{28,24},{20,28},{12,20},{4,12},{1,5},{9... | collective-permute-start | bytes 393224 | tf_op jit(solution)/shard_map/ppermute | solution.py:548
  20.2 0.8 %collective-permute-done.4.refs_0_.rest_6_ = bf16[8,4,16,128]{3,2,1,0:T(8,128)(2,1)S(1)} collective-permute-done((bf16[8,4,16,128]{3,2,1,0:T(8,128)(2,1)S(1)}, bf16[8,4,16,128]{3,2,1,0:T(8,128)(2,1)S(1)}, u32[]{:S(2)}, u32[]{:S(2)}) %collective-permute-start.4) | collective-permute-done | bytes 131104 | tf_op jit(solution)/shard_map/ppermute | solution.py:545
  20.9 0.2 collective-permute-done.5.refs_1_.rest_7_
  21.1 2.0 %collective-permute-done.10.refs_2_.rest_8_ = bf16[8,4,16,128]{3,2,1,0:T(8,128)(2,1)S(1)} collective-permute-done((bf16[8,4,16,128]{3,2,1,0:T(8,128)(2,1)S(1)}, bf16[8,4,16,128]{3,2,1,0:T(8,128)(2,1)S(1)}, u32[]{:S(2)}, u32[]{:S(2)}) %collective-permute-start.10) | collective-permute-done | bytes 131104 | tf_op jit(solution)/shard_map/ppermute | solution.py:545
  23.3 1.6 %collective-permute-start.17 = (bf16[16,4,16,128]{3,2,1,0:T(8,128)(2,1)S(1)}, bf16[16,4,16,128]{3,2,1,0:T(8,128)(2,1)S(1)}, u32[]{:S(2)}, u32[]{:S(2)}) collective-permute-start(bf16[16,4,16,128]{3,2,1,0:T(8,128)(2,1)S(1)} %get-tuple-element.61), channel_id=1, source_target_pairs={{0,8},{8,16},{16,24},{24,28},{28,20},{20,12},{12,4},{4,0},{1,9},{9... | collective-permute-start | bytes 786440 | tf_op jit(solution)/shard_map/ppermute | solution.py:545
  25.0 0.5 collective-permute-start.18
  25.6 2.6 %cross.3 = (bf16[64,512]{1,0:T(8,128)(2,1)S(1)}, bf16[64,512]{1,0:T(8,128)(2,1)S(1)}, bf16[64,512]{1,0:T(8,128)(2,1)S(1)}, bf16[64,512]{1,0:T(8,128)(2,1)S(1)}) custom-call(s32[4,8]{1,0:T(4,128)S(1)} %copy-done.1, bf16[2048,512]{1,0:T(8,128)(2,1)S(1)} %copy-done.2, f32[2,3,8,8,8,128]{5,4,3,2,1,0:T(8,128)S(1)} %widen.2.rest_0_, ...), custom_call_target="tpu_custom_call" | custom-call | flops 2990000128 | bytes 1024 | tf_op jit(solution)/shard_map/cross/pallas_call | solution.py:359
  28.3 1.7 %collective-permute-start.15 = (bf16[64,512]{1,0:T(8,128)(2,1)S(1)}, bf16[64,512]{1,0:T(8,128)(2,1)S(1)}, u32[]{:S(2)}, u32[]{:S(2)}) collective-permute-start(bf16[64,512]{1,0:T(8,128)(2,1)S(1)} %get-tuple-element.58), channel_id=1, source_target_pairs={{0,2},{1,3},{2,0},{3,1},{4,6},{5,7},{6,4},{7,5},{8,10},{9,11},{10,... | collective-permute-start | bytes 196616 | tf_op jit(solution)/shard_map/ppermute | solution.py:512
  30.1 2.1 %collective-permute-done.17.rest_10_ = bf16[16,4,16,128]{3,2,1,0:T(8,128)(2,1)S(1)} collective-permute-done((bf16[16,4,16,128]{3,2,1,0:T(8,128)(2,1)S(1)}, bf16[16,4,16,128]{3,2,1,0:T(8,128)(2,1)S(1)}, u32[]{:S(2)}, u32[]{:S(2)}) %collective-permute-start.17) | collective-permute-done | bytes 262176 | tf_op jit(solution)/shard_map/ppermute | solution.py:545
  32.2 1.4 %collective-permute-start.22 = (bf16[16,4,16,128]{3,2,1,0:T(8,128)(2,1)S(1)}, bf16[16,4,16,128]{3,2,1,0:T(8,128)(2,1)S(1)}, u32[]{:S(2)}, u32[]{:S(2)}) collective-permute-start(bf16[16,4,16,128]{3,2,1,0:T(8,128)(2,1)S(1)} %collective-permute-done.17.rest_10_), channel_id=1, source_target_pairs={{0,8},{8,16},{16,24},{24,28},{28,20},{20,12},{12,4},{4,0},{1,9},{9... | collective-permute-start | bytes 786440 | tf_op jit(solution)/shard_map/ppermute | solution.py:545
  33.6 4.4 %cross.4 = (bf16[128,512]{1,0:T(8,128)(2,1)S(1)}, bf16[128,512]{1,0:T(8,128)(2,1)S(1)}, bf16[128,512]{1,0:T(8,128)(2,1)S(1)}, bf16[128,512]{1,0:T(8,128)(2,1)S(1)}) custom-call(s32[4,8]{1,0:T(4,128)S(1)} %copy-done.1, bf16[2048,512]{1,0:T(8,128)(2,1)S(1)} %copy-done.2, f32[2,3,8,8,8,128]{5,4,3,2,1,0:T(8,128)S(1)} %widen.2.rest_0_, ...), custom_call_target="tpu_custom_call" | custom-call | flops 5289999872 | bytes 1024 | tf_op jit(solution)/shard_map/cross/pallas_call | solution.py:359
  38.1 1.8 %collective-permute-start.20 = (bf16[128,512]{1,0:T(8,128)(2,1)S(1)}, bf16[128,512]{1,0:T(8,128)(2,1)S(1)}, u32[]{:S(2)}, u32[]{:S(2)}) collective-permute-start(bf16[128,512]{1,0:T(8,128)(2,1)S(1)} %get-tuple-element.65), channel_id=1, source_target_pairs={{0,2},{1,3},{2,0},{3,1},{4,6},{5,7},{6,4},{7,5},{8,10},{9,11},{10,... | collective-permute-start | bytes 393224 | tf_op jit(solution)/shard_map/ppermute | solution.py:512
  40.0 0.3 collective-permute-done.22.rest_12_
  40.3 2.7 %cross.5 = (bf16[64,512]{1,0:T(8,128)(2,1)S(1)}, bf16[64,512]{1,0:T(8,128)(2,1)S(1)}, bf16[64,512]{1,0:T(8,128)(2,1)S(1)}, bf16[64,512]{1,0:T(8,128)(2,1)S(1)}) custom-call(s32[4,8]{1,0:T(4,128)S(1)} %copy-done.1, bf16[2048,512]{1,0:T(8,128)(2,1)S(1)} %copy-done.2, f32[2,3,8,8,8,128]{5,4,3,2,1,0:T(8,128)S(1)} %widen.2.rest_0_, ...), custom_call_target="tpu_custom_call" | custom-call | flops 2990000128 | bytes 1024 | tf_op jit(solution)/shard_map/cross/pallas_call | solution.py:359
  43.1 1.7 %collective-permute-start.24 = (bf16[64,512]{1,0:T(8,128)(2,1)S(1)}, bf16[64,512]{1,0:T(8,128)(2,1)S(1)}, u32[]{:S(2)}, u32[]{:S(2)}) collective-permute-start(bf16[64,512]{1,0:T(8,128)(2,1)S(1)} %get-tuple-element.71), channel_id=1, source_target_pairs={{0,2},{1,3},{2,0},{3,1},{4,6},{5,7},{6,4},{7,5},{8,10},{9,11},{10,... | collective-permute-start | bytes 196616 | tf_op jit(solution)/shard_map/ppermute | solution.py:512
  44.9 1.6 %collective-permute-done.21.rest_7_ = bf16[128,512]{1,0:T(8,128)(2,1)S(1)} collective-permute-done((bf16[128,512]{1,0:T(8,128)(2,1)S(1)}, bf16[128,512]{1,0:T(8,128)(2,1)S(1)}, u32[]{:S(2)}, u32[]{:S(2)}) %collective-permute-start.21) | collective-permute-done | bytes 131104 | tf_op jit(solution)/shard_map/ppermute | solution.py:512
  46.6 2.1 %early.1 = f32[1024,4,1,128]{3,2,1,0:T(1,128)} custom-call(s32[4,8]{1,0:T(4,128)S(1)} %copy-done.1, bf16[4,128,512]{2,1,0:T(8,128)(2,1)S(1)} %copy-done, bf16[64,512]{1,0:T(8,128)(2,1)S(1)} %get-tuple-element.56.rest_0_, bf16[64,512]{1,0:T(8,128)(2,1)S(1)} %collective-permute-done.14.rest_1_, bf16[64,512]{1,0:T(8,128)(2,1)S(1)} %collective-permute-done.15.rest_2_, ...), custom_call_target="tpu_custom_call" | custom-call | flops 57500000 | bytes 1024 | tf_op jit(solution)/shard_map/early/pallas_call | solution.py:458
  48.7 0.6 %collective-permute-done.25.rest_3_ = bf16[64,512]{1,0:T(8,128)(2,1)S(1)} collective-permute-done((bf16[64,512]{1,0:T(8,128)(2,1)S(1)}, bf16[64,512]{1,0:T(8,128)(2,1)S(1)}, u32[]{:S(2)}, u32[]{:S(2)}) %collective-permute-start.25) | collective-permute-done | bytes 65568 | tf_op jit(solution)/shard_map/ppermute | solution.py:512
  49.3 1.6 %late.1 = f32[1024,4,1,128]{3,2,1,0:T(1,128)} custom-call(s32[4,8]{1,0:T(4,128)S(1)} %copy-done.1, bf16[4,128,512]{2,1,0:T(8,128)(2,1)S(1)} %copy-done, f32[1024,4,1,128]{3,2,1,0:T(1,128)} %early.1, bf16[64,512]{1,0:T(8,128)(2,1)S(1)} %get-tuple-element.69.rest_0_, ...), custom_call_target="tpu_custom_call", output_to_operand_aliasing={{}: (2, {})} | custom-call | flops 57500000 | bytes 1024 | tf_op jit(solution)/shard_map/late/pallas_call | solution.py:471
  (38 shorter events, 1.4 us)
Async XLA Ops:
  3.0 3.3 %collective-permute-start = (bf16[4,4,16,128]{3,2,1,0:T(8,128)(2,1)S(1)}, bf16[4,4,16,128]{3,2,1,0:T(8,128)(2,1)S(1)}, u32[]{:S(2)}, u32[]{:S(2)}) collective-permute-start(bf16[4,4,16,128]{3,2,1,0:T(8,128)(2,1)S(1)} %get-tuple-element.40), channel_id=1, source_target_pairs={{0,1},{1,0},{2,3},{3,2},{4,5},{5,4},{6,7},{7,6},{8,9},{9,8},{10,11... | collective-permute-start | bytes 196616 | tf_op jit(solution)/shard_map/ppermute | solution.py:512
  3.6 5.3 %collective-permute-start.6 = (bf16[4,4,16,128]{3,2,1,0:T(8,128)(2,1)S(1)}, bf16[4,4,16,128]{3,2,1,0:T(8,128)(2,1)S(1)}, u32[]{:S(2)}, u32[]{:S(2)}) collective-permute-start(bf16[4,4,16,128]{3,2,1,0:T(8,128)(2,1)S(1)} %get-tuple-element.45), channel_id=1, source_target_pairs={{0,2},{1,3},{2,0},{3,1},{4,6},{5,7},{6,4},{7,5},{8,10},{9,11},{10,... | collective-permute-start | bytes 196616 | tf_op jit(solution)/shard_map/ppermute | solution.py:512
  6.1 4.0 %collective-permute-start.7 = (bf16[4,4,16,128]{3,2,1,0:T(8,128)(2,1)S(1)}, bf16[4,4,16,128]{3,2,1,0:T(8,128)(2,1)S(1)}, u32[]{:S(2)}, u32[]{:S(2)}) collective-permute-start(bf16[4,4,16,128]{3,2,1,0:T(8,128)(2,1)S(1)} %get-tuple-element.46), channel_id=1, source_target_pairs={{0,3},{1,2},{2,1},{3,0},{4,7},{5,6},{6,5},{7,4},{8,11},{9,10},{10,... | collective-permute-start | bytes 196616 | tf_op jit(solution)/shard_map/ppermute | solution.py:512
  6.2 4.0 %collective-permute-start.3 = (bf16[4,16,16,128]{3,2,1,0:T(8,128)(2,1)S(1)}, bf16[4,16,16,128]{3,2,1,0:T(8,128)(2,1)S(1)}, u32[]{:S(2)}, u32[]{:S(2)}) collective-permute-start(bf16[4,16,16,128]{3,2,1,0:T(8,128)(2,1)S(1)} %get-tuple-element.54.refs_0_), channel_id=1, source_target_pairs={{0,1},{1,0},{2,3},{3,2},{4,5},{5,4},{6,7},{7,6},{8,9},{9,8},{10,11... | collective-permute-start | bytes 786440 | tf_op jit(solution)/shard_map/ppermute | solution.py:512
  6.4 7.4 %collective-permute-start.2 = (bf16[8,4,16,128]{3,2,1,0:T(8,128)(2,1)S(1)}, bf16[8,4,16,128]{3,2,1,0:T(8,128)(2,1)S(1)}, u32[]{:S(2)}, u32[]{:S(2)}) collective-permute-start(bf16[8,4,16,128]{3,2,1,0:T(8,128)(2,1)S(1)} %constant_dynamic-update-slice_fusion), channel_id=1, source_target_pairs={{0,4},{8,0},{16,8},{24,16},{28,24},{20,28},{12,20},{4,12},{1,5},{9... | collective-permute-start | bytes 393224 | tf_op jit(solution)/shard_map/ppermute | solution.py:548
  8.4 5.4 %collective-permute-start.1 = (bf16[8,4,16,128]{3,2,1,0:T(8,128)(2,1)S(1)}, bf16[8,4,16,128]{3,2,1,0:T(8,128)(2,1)S(1)}, u32[]{:S(2)}, u32[]{:S(2)}) collective-permute-start(bf16[8,4,16,128]{3,2,1,0:T(8,128)(2,1)S(1)} %constant_dynamic-update-slice_fusion), channel_id=1, source_target_pairs={{0,8},{8,16},{16,24},{24,28},{28,20},{20,12},{12,4},{4,0},{1,9},{9... | collective-permute-start | bytes 393224 | tf_op jit(solution)/shard_map/ppermute | solution.py:545
  10.2 15.4 %copy-start.1 = (s32[4,8]{1,0:T(4,128)S(1)}, s32[4,8]{1,0:T(4,128)}, u32[]{:S(2)}) copy-start(s32[4,8]{1,0:T(4,128)} %plan.9) | copy-start | bytes 388
  10.2 15.4 %copy-start.2 = (bf16[2048,512]{1,0:T(8,128)(2,1)S(1)}, bf16[2048,512]{1,0:T(8,128)(2,1)}, u32[]{:S(2)}) copy-start(bf16[2048,512]{1,0:T(8,128)(2,1)} %constant.7.clone.table) | copy-start | bytes 6291460
  10.2 5.9 %collective-permute-start.9 = (bf16[8,4,16,128]{3,2,1,0:T(8,128)(2,1)S(1)}, bf16[8,4,16,128]{3,2,1,0:T(8,128)(2,1)S(1)}, u32[]{:S(2)}, u32[]{:S(2)}) collective-permute-start(bf16[8,4,16,128]{3,2,1,0:T(8,128)(2,1)S(1)} %pad_maximum_fusion), channel_id=1, source_target_pairs={{0,4},{8,0},{16,8},{24,16},{28,24},{20,28},{12,20},{4,12},{1,5},{9... | collective-permute-start | bytes 393224 | tf_op jit(solution)/shard_map/ppermute | solution.py:548
  11.8 6.3 %collective-permute-start.8 = (bf16[8,4,16,128]{3,2,1,0:T(8,128)(2,1)S(1)}, bf16[8,4,16,128]{3,2,1,0:T(8,128)(2,1)S(1)}, u32[]{:S(2)}, u32[]{:S(2)}) collective-permute-start(bf16[8,4,16,128]{3,2,1,0:T(8,128)(2,1)S(1)} %pad_maximum_fusion), channel_id=1, source_target_pairs={{0,8},{8,16},{16,24},{24,28},{28,20},{20,12},{12,4},{4,0},{1,9},{9... | collective-permute-start | bytes 393224 | tf_op jit(solution)/shard_map/ppermute | solution.py:545
  12.3 10.9 %collective-permute-start.12 = (bf16[4,16,16,128]{3,2,1,0:T(8,128)(2,1)S(1)}, bf16[4,16,16,128]{3,2,1,0:T(8,128)(2,1)S(1)}, u32[]{:S(2)}, u32[]{:S(2)}) collective-permute-start(bf16[4,16,16,128]{3,2,1,0:T(8,128)(2,1)S(1)} %get-tuple-element.54.refs_0_), channel_id=1, source_target_pairs={{0,2},{1,3},{2,0},{3,1},{4,6},{5,7},{6,4},{7,5},{8,10},{9,11},{10,... | collective-permute-start | bytes 786440 | tf_op jit(solution)/shard_map/ppermute | solution.py:512
  13.8 7.1 %collective-permute-start.4 = (bf16[8,4,16,128]{3,2,1,0:T(8,128)(2,1)S(1)}, bf16[8,4,16,128]{3,2,1,0:T(8,128)(2,1)S(1)}, u32[]{:S(2)}, u32[]{:S(2)}) collective-permute-start(bf16[8,4,16,128]{3,2,1,0:T(8,128)(2,1)S(1)} %collective-permute-done.1.rest_2_), channel_id=1, source_target_pairs={{0,8},{8,16},{16,24},{24,28},{28,20},{20,12},{12,4},{4,0},{1,9},{9... | collective-permute-start | bytes 393224 | tf_op jit(solution)/shard_map/ppermute | solution.py:545
  15.4 5.7 %collective-permute-start.5 = (bf16[8,4,16,128]{3,2,1,0:T(8,128)(2,1)S(1)}, bf16[8,4,16,128]{3,2,1,0:T(8,128)(2,1)S(1)}, u32[]{:S(2)}, u32[]{:S(2)}) collective-permute-start(bf16[8,4,16,128]{3,2,1,0:T(8,128)(2,1)S(1)} %collective-permute-done.2.rest_3_), channel_id=1, source_target_pairs={{0,4},{8,0},{16,8},{24,16},{28,24},{20,28},{12,20},{4,12},{1,5},{9... | collective-permute-start | bytes 393224 | tf_op jit(solution)/shard_map/ppermute | solution.py:548
  18.1 5.0 %collective-permute-start.10 = (bf16[8,4,16,128]{3,2,1,0:T(8,128)(2,1)S(1)}, bf16[8,4,16,128]{3,2,1,0:T(8,128)(2,1)S(1)}, u32[]{:S(2)}, u32[]{:S(2)}) collective-permute-start(bf16[8,4,16,128]{3,2,1,0:T(8,128)(2,1)S(1)} %collective-permute-done.8.rest_4_), channel_id=1, source_target_pairs={{0,8},{8,16},{16,24},{24,28},{28,20},{20,12},{12,4},{4,0},{1,9},{9... | collective-permute-start | bytes 393224 | tf_op jit(solution)/shard_map/ppermute | solution.py:545
  18.1 5.1 %collective-permute-start.11 = (bf16[8,4,16,128]{3,2,1,0:T(8,128)(2,1)S(1)}, bf16[8,4,16,128]{3,2,1,0:T(8,128)(2,1)S(1)}, u32[]{:S(2)}, u32[]{:S(2)}) collective-permute-start(bf16[8,4,16,128]{3,2,1,0:T(8,128)(2,1)S(1)} %collective-permute-done.9.rest_5_), channel_id=1, source_target_pairs={{0,4},{8,0},{16,8},{24,16},{28,24},{20,28},{12,20},{4,12},{1,5},{9... | collective-permute-start | bytes 393224 | tf_op jit(solution)/shard_map/ppermute | solution.py:548
  23.3 2.2 %collective-permute-start.13 = (bf16[4,16,16,128]{3,2,1,0:T(8,128)(2,1)S(1)}, bf16[4,16,16,128]{3,2,1,0:T(8,128)(2,1)S(1)}, u32[]{:S(2)}, u32[]{:S(2)}) collective-permute-start(bf16[4,16,16,128]{3,2,1,0:T(8,128)(2,1)S(1)} %collective-permute-done.12.refs_0_), channel_id=1, source_target_pairs={{0,1},{1,0},{2,3},{3,2},{4,5},{5,4},{6,7},{7,6},{8,9},{9,8},{10,11... | collective-permute-start | bytes 786440 | tf_op jit(solution)/shard_map/ppermute | solution.py:512
  23.3 8.9 %collective-permute-start.17 = (bf16[16,4,16,128]{3,2,1,0:T(8,128)(2,1)S(1)}, bf16[16,4,16,128]{3,2,1,0:T(8,128)(2,1)S(1)}, u32[]{:S(2)}, u32[]{:S(2)}) collective-permute-start(bf16[16,4,16,128]{3,2,1,0:T(8,128)(2,1)S(1)} %get-tuple-element.61), channel_id=1, source_target_pairs={{0,8},{8,16},{16,24},{24,28},{28,20},{20,12},{12,4},{4,0},{1,9},{9... | collective-permute-start | bytes 786440 | tf_op jit(solution)/shard_map/ppermute | solution.py:545
  25.0 8.7 %collective-permute-start.18 = (bf16[16,4,16,128]{3,2,1,0:T(8,128)(2,1)S(1)}, bf16[16,4,16,128]{3,2,1,0:T(8,128)(2,1)S(1)}, u32[]{:S(2)}, u32[]{:S(2)}) collective-permute-start(bf16[16,4,16,128]{3,2,1,0:T(8,128)(2,1)S(1)} %get-tuple-element.62), channel_id=1, source_target_pairs={{0,4},{8,0},{16,8},{24,16},{28,24},{20,28},{12,20},{4,12},{1,5},{9... | collective-permute-start | bytes 786440 | tf_op jit(solution)/shard_map/ppermute | solution.py:548
  28.2 9.9 %collective-permute-start.14 = (bf16[64,512]{1,0:T(8,128)(2,1)S(1)}, bf16[64,512]{1,0:T(8,128)(2,1)S(1)}, u32[]{:S(2)}, u32[]{:S(2)}) collective-permute-start(bf16[64,512]{1,0:T(8,128)(2,1)S(1)} %get-tuple-element.57), channel_id=1, source_target_pairs={{0,1},{1,0},{2,3},{3,2},{4,5},{5,4},{6,7},{7,6},{8,9},{9,8},{10,11... | collective-permute-start | bytes 196616 | tf_op jit(solution)/shard_map/ppermute | solution.py:512
  28.3 11.6 %collective-permute-start.15 = (bf16[64,512]{1,0:T(8,128)(2,1)S(1)}, bf16[64,512]{1,0:T(8,128)(2,1)S(1)}, u32[]{:S(2)}, u32[]{:S(2)}) collective-permute-start(bf16[64,512]{1,0:T(8,128)(2,1)S(1)} %get-tuple-element.58), channel_id=1, source_target_pairs={{0,2},{1,3},{2,0},{3,1},{4,6},{5,7},{6,4},{7,5},{8,10},{9,11},{10,... | collective-permute-start | bytes 196616 | tf_op jit(solution)/shard_map/ppermute | solution.py:512
  30.1 10.0 %collective-permute-start.16 = (bf16[64,512]{1,0:T(8,128)(2,1)S(1)}, bf16[64,512]{1,0:T(8,128)(2,1)S(1)}, u32[]{:S(2)}, u32[]{:S(2)}) collective-permute-start(bf16[64,512]{1,0:T(8,128)(2,1)S(1)} %get-tuple-element.59), channel_id=1, source_target_pairs={{0,3},{1,2},{2,1},{3,0},{4,7},{5,6},{6,5},{7,4},{8,11},{9,10},{10,... | collective-permute-start | bytes 196616 | tf_op jit(solution)/shard_map/ppermute | solution.py:512
  32.2 8.1 %collective-permute-start.22 = (bf16[16,4,16,128]{3,2,1,0:T(8,128)(2,1)S(1)}, bf16[16,4,16,128]{3,2,1,0:T(8,128)(2,1)S(1)}, u32[]{:S(2)}, u32[]{:S(2)}) collective-permute-start(bf16[16,4,16,128]{3,2,1,0:T(8,128)(2,1)S(1)} %collective-permute-done.17.rest_10_), channel_id=1, source_target_pairs={{0,8},{8,16},{16,24},{24,28},{28,20},{20,12},{12,4},{4,0},{1,9},{9... | collective-permute-start | bytes 786440 | tf_op jit(solution)/shard_map/ppermute | solution.py:545
  38.0 6.8 %collective-permute-start.19 = (bf16[128,512]{1,0:T(8,128)(2,1)S(1)}, bf16[128,512]{1,0:T(8,128)(2,1)S(1)}, u32[]{:S(2)}, u32[]{:S(2)}) collective-permute-start(bf16[128,512]{1,0:T(8,128)(2,1)S(1)} %get-tuple-element.64), channel_id=1, source_target_pairs={{0,1},{1,0},{2,3},{3,2},{4,5},{5,4},{6,7},{7,6},{8,9},{9,8},{10,11... | collective-permute-start | bytes 393224 | tf_op jit(solution)/shard_map/ppermute | solution.py:512
  38.1 6.8 %collective-permute-start.20 = (bf16[128,512]{1,0:T(8,128)(2,1)S(1)}, bf16[128,512]{1,0:T(8,128)(2,1)S(1)}, u32[]{:S(2)}, u32[]{:S(2)}) collective-permute-start(bf16[128,512]{1,0:T(8,128)(2,1)S(1)} %get-tuple-element.65), channel_id=1, source_target_pairs={{0,2},{1,3},{2,0},{3,1},{4,6},{5,7},{6,4},{7,5},{8,10},{9,11},{10,... | collective-permute-start | bytes 393224 | tf_op jit(solution)/shard_map/ppermute | solution.py:512
  39.9 6.6 %collective-permute-start.21 = (bf16[128,512]{1,0:T(8,128)(2,1)S(1)}, bf16[128,512]{1,0:T(8,128)(2,1)S(1)}, u32[]{:S(2)}, u32[]{:S(2)}) collective-permute-start(bf16[128,512]{1,0:T(8,128)(2,1)S(1)} %get-tuple-element.66), channel_id=1, source_target_pairs={{0,3},{1,2},{2,1},{3,0},{4,7},{5,6},{6,5},{7,4},{8,11},{9,10},{10,... | collective-permute-start | bytes 393224 | tf_op jit(solution)/shard_map/ppermute | solution.py:512
  40.0 6.5 %copy-start = (bf16[4,128,512]{2,1,0:T(8,128)(2,1)S(1)}, bf16[4,128,512]{2,1,0:T(8,128)(2,1)}, u32[]{:S(2)}) copy-start(bf16[4,128,512]{2,1,0:T(8,128)(2,1)} %constant.8.clone.place) | copy-start | bytes 1572868
  43.0 5.7 %collective-permute-start.23 = (bf16[64,512]{1,0:T(8,128)(2,1)S(1)}, bf16[64,512]{1,0:T(8,128)(2,1)S(1)}, u32[]{:S(2)}, u32[]{:S(2)}) collective-permute-start(bf16[64,512]{1,0:T(8,128)(2,1)S(1)} %get-tuple-element.70), channel_id=1, source_target_pairs={{0,1},{1,0},{2,3},{3,2},{4,5},{5,4},{6,7},{7,6},{8,9},{9,8},{10,11... | collective-permute-start | bytes 196616 | tf_op jit(solution)/shard_map/ppermute | solution.py:512
  43.1 5.6 %collective-permute-start.24 = (bf16[64,512]{1,0:T(8,128)(2,1)S(1)}, bf16[64,512]{1,0:T(8,128)(2,1)S(1)}, u32[]{:S(2)}, u32[]{:S(2)}) collective-permute-start(bf16[64,512]{1,0:T(8,128)(2,1)S(1)} %get-tuple-element.71), channel_id=1, source_target_pairs={{0,2},{1,3},{2,0},{3,1},{4,6},{5,7},{6,4},{7,5},{8,10},{9,11},{10,... | collective-permute-start | bytes 196616 | tf_op jit(solution)/shard_map/ppermute | solution.py:512
  44.8 4.5 %collective-permute-start.25 = (bf16[64,512]{1,0:T(8,128)(2,1)S(1)}, bf16[64,512]{1,0:T(8,128)(2,1)S(1)}, u32[]{:S(2)}, u32[]{:S(2)}) collective-permute-start(bf16[64,512]{1,0:T(8,128)(2,1)S(1)} %get-tuple-element.72), channel_id=1, source_target_pairs={{0,3},{1,2},{2,1},{3,0},{4,7},{5,6},{6,5},{7,4},{8,11},{9,10},{10,... | collective-permute-start | bytes 196616 | tf_op jit(solution)/shard_map/ppermute | solution.py:512

commit v18 on v17

--- a/solution.py
+++ b/solution.py
@@ -266,15 +266,16 @@
 
             @pl.when(step == offset)
             def _(candidate=candidate, slot=slot, first=first):
-                def widen_other(w, carry):
-                    raw = candidate[w].astype(F32)
-                    real, imag = raw[:, :TILES], raw[:, TILES:]
-                    other[0, slot, first + w] = real
-                    other[1, slot, first + w] = real + imag
-                    other[2, slot, first + w] = imag - real
+                def widen_other(turn, carry):
+                    raw = candidate[pl.ds(turn * 4, 4)].astype(F32)
+                    real, imag = raw[:, :, :TILES], raw[:, :, TILES:]
+                    at = pl.ds(first + turn * 4, 4)
+                    other[0, slot, at] = real
+                    other[1, slot, at] = real + imag
+                    other[2, slot, at] = imag - real
                     return carry
 
-                lax.fori_loop(0, candidate.shape[0], widen_other, 0)
+                lax.fori_loop(0, candidate.shape[0] // 4, widen_other, 0)
 
 
 def sum_windows(owns, other, summed):
@@ -313,7 +314,7 @@
     owns, rest = rest[:2], rest[2:]
     others, rest = rest[: len(places)], rest[len(places) :]
     outs = rest[:parts]
-    other, summed, operand, result = rest[parts:]
+    other, summed, operand = rest[parts:]
     stations = owns[0].shape[0] * owns[0].shape[3]
     widen_others(first_slot, slots, count, places, plan, others, other)
     sum_windows(owns, other, summed)
@@ -339,12 +340,15 @@
             operand[rows, at] = turned[q][0].astype(BF)
             operand[rows, at_imag] = turned[q][1].astype(BF)
     block = jnp.dot(operand[...], table[...], preferred_element_type=F32)
-    block = block * (2.0 * scaling)
-    for q in range(CHUNKS):
-        result[q] = block[q * columns : (q + 1) * columns].astype(BF)
+    block = (block * (2.0 * scaling)).astype(BF)
     me = lax.axis_index("seg")
-    for j in range(parts):
-        outs[j][...] = result[me ^ j]
+    for place in range(parts):
+
+        @pl.when(me == place)
+        def _(place=place):
+            for j in range(parts):
+                q = place ^ j
+                outs[j][...] = block[q * columns : (q + 1) * columns]
 
 
 def cross_lags(plan, table, owns, places, candidates, first_slot, slots, count, parts, scaling):
@@ -367,7 +371,6 @@
             pltpu.VMEM((3, slots, 2 * windows, quarter, TILES, LANES), F32),
             pltpu.VMEM((3, columns * TILES, LANES), F32),
             pltpu.VMEM((CHUNKS * columns, 2 * NBIN), BF),
-            pltpu.VMEM((parts,) + out, BF),
         ],
         compiler_params=pltpu.CompilerParams(vmem_limit_bytes=24 * 2**20),
         cost_estimate=expected(0.6 + 2.0 * slots),

time: 51.1 us -> 50.9 us (level)
  transfers between devices with their start and end apart: 26 -> 26, of which waited for: 12 -> 12; matrix products, arithmetic and copies ran while one was open for 0% -> 0% of each run, Pallas kernels for 24% -> 23%
where the time goes in v18:
time: 50.9 us; the launch traced here: 50.7 us
  starting transfers between devices  22.3 us (44%)
  Pallas kernels  16.6 us (33%)
  waiting for transfers between devices  11.6 us (23%)
    ppermute x15, starting transfers between devices, swap(): return lax.ppermute(value, 'seg', [(i, i ^ j) for i in range(parts)])  10.6 us
    pallas_call x3, Pallas kernels, cross_lags(): pl.pallas_call(functools.partial(cross_kernel, first_slot, slots, count,...  9.52 us
    ppermute x6, waiting for transfers between devices, up(): return lax.ppermute(value, 'sta', upward)  7.2 us
    ppermute x5, starting transfers between devices, down(): return lax.ppermute(value, 'sta', downward)  6.51 us
    ppermute x6, starting transfers between devices, up(): return lax.ppermute(value, 'sta', upward)  5.28 us
    ppermute x15, waiting for transfers between devices, swap(): return lax.ppermute(value, 'seg', [(i, i ^ j) for i in range(parts)])  3.84 us
    pallas_call x1, Pallas kernels, prepare(): pl.pallas_call(functools.partial(prep_kernel, parts, windows), out_shape=...  3.04 us
    pallas_call x1, Pallas kernels, place_lags(): pl.pallas_call(functools.partial(early_kernel, count, parts, tuple(groups...  2.1 us
  transfers between devices with their start and end apart: 26, of which 12 were waited for; matrix products, arithmetic and copies ran while one was open for 0% of the time, Pallas kernels for 23%

profile of v18, /device:TPU:0, one launch (start us, length us, event | category | flops | bytes accessed | tf_op | source)
XLA Modules:
  0.0 50.7 jit_solution(10689149851530765327)
XLA Ops:
  0.0 3.0 %prep.1 = (bf16[4,16,16,128]{3,2,1,0:T(8,128)(2,1)S(1)}, bf16[4,4,16,128]{3,2,1,0:T(8,128)(2,1)S(1)}, bf16[4,4,16,128]{3,2,1,0:T(8,128)(2,1)S(1)}, bf16[4,4,16,1...) custom-call(f32[1024,128]{1,0:T(8,128)} %bitcast.10, bf16[512,2048]{1,0:T(8,128)(2,1)} %constant.6.clone.table_hbm), custom_call_target="tpu_custom_call" | custom-call | flops 536870912 | bytes 3145728 | tf_op jit(solution)/shard_map/prep/pallas_call | solution.py:169
  3.0 0.5 %collective-permute-start = (bf16[4,4,16,128]{3,2,1,0:T(8,128)(2,1)S(1)}, bf16[4,4,16,128]{3,2,1,0:T(8,128)(2,1)S(1)}, u32[]{:S(2)}, u32[]{:S(2)}) collective-permute-start(bf16[4,4,16,128]{3,2,1,0:T(8,128)(2,1)S(1)} %get-tuple-element.40), channel_id=1, source_target_pairs={{0,1},{1,0},{2,3},{3,2},{4,5},{5,4},{6,7},{7,6},{8,9},{9,8},{10,11... | collective-permute-start | bytes 196616 | tf_op jit(solution)/shard_map/ppermute | solution.py:515
  3.6 2.6 %collective-permute-start.6 = (bf16[4,4,16,128]{3,2,1,0:T(8,128)(2,1)S(1)}, bf16[4,4,16,128]{3,2,1,0:T(8,128)(2,1)S(1)}, u32[]{:S(2)}, u32[]{:S(2)}) collective-permute-start(bf16[4,4,16,128]{3,2,1,0:T(8,128)(2,1)S(1)} %get-tuple-element.45), channel_id=1, source_target_pairs={{0,2},{1,3},{2,0},{3,1},{4,6},{5,7},{6,4},{7,5},{8,10},{9,11},{10,... | collective-permute-start | bytes 196616 | tf_op jit(solution)/shard_map/ppermute | solution.py:515
  6.4 2.0 %collective-permute-start.2 = (bf16[8,4,16,128]{3,2,1,0:T(8,128)(2,1)S(1)}, bf16[8,4,16,128]{3,2,1,0:T(8,128)(2,1)S(1)}, u32[]{:S(2)}, u32[]{:S(2)}) collective-permute-start(bf16[8,4,16,128]{3,2,1,0:T(8,128)(2,1)S(1)} %constant_dynamic-update-slice_fusion), channel_id=1, source_target_pairs={{0,4},{8,0},{16,8},{24,16},{28,24},{20,28},{12,20},{4,12},{1,5},{9... | collective-permute-start | bytes 393224 | tf_op jit(solution)/shard_map/ppermute | solution.py:551
  8.5 0.3 collective-permute-done.6
  8.8 1.4 %collective-permute-done.7 = bf16[4,4,16,128]{3,2,1,0:T(8,128)(2,1)S(1)} collective-permute-done((bf16[4,4,16,128]{3,2,1,0:T(8,128)(2,1)S(1)}, bf16[4,4,16,128]{3,2,1,0:T(8,128)(2,1)S(1)}, u32[]{:S(2)}, u32[]{:S(2)}) %collective-permute-start.7) | collective-permute-done | bytes 65568 | tf_op jit(solution)/shard_map/ppermute | solution.py:515
  10.2 1.6 %collective-permute-start.9 = (bf16[8,4,16,128]{3,2,1,0:T(8,128)(2,1)S(1)}, bf16[8,4,16,128]{3,2,1,0:T(8,128)(2,1)S(1)}, u32[]{:S(2)}, u32[]{:S(2)}) collective-permute-start(bf16[8,4,16,128]{3,2,1,0:T(8,128)(2,1)S(1)} %pad_maximum_fusion), channel_id=1, source_target_pairs={{0,4},{8,0},{16,8},{24,16},{28,24},{20,28},{12,20},{4,12},{1,5},{9... | collective-permute-start | bytes 393224 | tf_op jit(solution)/shard_map/ppermute | solution.py:551
  11.8 0.5 collective-permute-start.8
  12.3 1.3 %collective-permute-start.12 = (bf16[4,16,16,128]{3,2,1,0:T(8,128)(2,1)S(1)}, bf16[4,16,16,128]{3,2,1,0:T(8,128)(2,1)S(1)}, u32[]{:S(2)}, u32[]{:S(2)}) collective-permute-start(bf16[4,16,16,128]{3,2,1,0:T(8,128)(2,1)S(1)} %get-tuple-element.54.refs_0_), channel_id=1, source_target_pairs={{0,2},{1,3},{2,0},{3,1},{4,6},{5,7},{6,4},{7,5},{8,10},{9,11},{10,... | collective-permute-start | bytes 786440 | tf_op jit(solution)/shard_map/ppermute | solution.py:515
  13.8 1.6 %collective-permute-start.4 = (bf16[8,4,16,128]{3,2,1,0:T(8,128)(2,1)S(1)}, bf16[8,4,16,128]{3,2,1,0:T(8,128)(2,1)S(1)}, u32[]{:S(2)}, u32[]{:S(2)}) collective-permute-start(bf16[8,4,16,128]{3,2,1,0:T(8,128)(2,1)S(1)} %collective-permute-done.1.rest_2_), channel_id=1, source_target_pairs={{0,8},{8,16},{16,24},{24,28},{28,20},{20,12},{12,4},{4,0},{1,9},{9... | collective-permute-start | bytes 393224 | tf_op jit(solution)/shard_map/ppermute | solution.py:548
  15.4 0.4 collective-permute-start.5
  15.9 0.3 collective-permute-done.9.rest_5_
  16.1 2.0 %collective-permute-done.8.rest_4_ = bf16[8,4,16,128]{3,2,1,0:T(8,128)(2,1)S(1)} collective-permute-done((bf16[8,4,16,128]{3,2,1,0:T(8,128)(2,1)S(1)}, bf16[8,4,16,128]{3,2,1,0:T(8,128)(2,1)S(1)}, u32[]{:S(2)}, u32[]{:S(2)}) %collective-permute-start.8) | collective-permute-done | bytes 131104 | tf_op jit(solution)/shard_map/ppermute | solution.py:548
  18.1 2.0 %collective-permute-start.11 = (bf16[8,4,16,128]{3,2,1,0:T(8,128)(2,1)S(1)}, bf16[8,4,16,128]{3,2,1,0:T(8,128)(2,1)S(1)}, u32[]{:S(2)}, u32[]{:S(2)}) collective-permute-start(bf16[8,4,16,128]{3,2,1,0:T(8,128)(2,1)S(1)} %collective-permute-done.9.rest_5_), channel_id=1, source_target_pairs={{0,4},{8,0},{16,8},{24,16},{28,24},{20,28},{12,20},{4,12},{1,5},{9... | collective-permute-start | bytes 393224 | tf_op jit(solution)/shard_map/ppermute | solution.py:551
  20.2 0.8 %collective-permute-done.4.refs_0_.rest_6_ = bf16[8,4,16,128]{3,2,1,0:T(8,128)(2,1)S(1)} collective-permute-done((bf16[8,4,16,128]{3,2,1,0:T(8,128)(2,1)S(1)}, bf16[8,4,16,128]{3,2,1,0:T(8,128)(2,1)S(1)}, u32[]{:S(2)}, u32[]{:S(2)}) %collective-permute-start.4) | collective-permute-done | bytes 131104 | tf_op jit(solution)/shard_map/ppermute | solution.py:548
  20.9 0.2 collective-permute-done.5.refs_1_.rest_7_
  21.1 2.0 %collective-permute-done.10.refs_2_.rest_8_ = bf16[8,4,16,128]{3,2,1,0:T(8,128)(2,1)S(1)} collective-permute-done((bf16[8,4,16,128]{3,2,1,0:T(8,128)(2,1)S(1)}, bf16[8,4,16,128]{3,2,1,0:T(8,128)(2,1)S(1)}, u32[]{:S(2)}, u32[]{:S(2)}) %collective-permute-start.10) | collective-permute-done | bytes 131104 | tf_op jit(solution)/shard_map/ppermute | solution.py:548
  23.3 1.6 %collective-permute-start.17 = (bf16[16,4,16,128]{3,2,1,0:T(8,128)(2,1)S(1)}, bf16[16,4,16,128]{3,2,1,0:T(8,128)(2,1)S(1)}, u32[]{:S(2)}, u32[]{:S(2)}) collective-permute-start(bf16[16,4,16,128]{3,2,1,0:T(8,128)(2,1)S(1)} %get-tuple-element.61), channel_id=1, source_target_pairs={{0,8},{8,16},{16,24},{24,28},{28,20},{20,12},{12,4},{4,0},{1,9},{9... | collective-permute-start | bytes 786440 | tf_op jit(solution)/shard_map/ppermute | solution.py:548
  25.0 0.5 collective-permute-start.18
  25.6 2.6 %cross.3 = (bf16[64,512]{1,0:T(8,128)(2,1)S(1)}, bf16[64,512]{1,0:T(8,128)(2,1)S(1)}, bf16[64,512]{1,0:T(8,128)(2,1)S(1)}, bf16[64,512]{1,0:T(8,128)(2,1)S(1)}) custom-call(s32[4,8]{1,0:T(4,128)S(1)} %copy-done.1, bf16[2048,512]{1,0:T(8,128)(2,1)S(1)} %copy-done.2, f32[2,3,8,8,8,128]{5,4,3,2,1,0:T(8,128)S(1)} %widen.2.rest_0_, ...), custom_call_target="tpu_custom_call" | custom-call | flops 2990000128 | bytes 1024 | tf_op jit(solution)/shard_map/cross/pallas_call | solution.py:363
  28.3 1.7 %collective-permute-start.15 = (bf16[64,512]{1,0:T(8,128)(2,1)S(1)}, bf16[64,512]{1,0:T(8,128)(2,1)S(1)}, u32[]{:S(2)}, u32[]{:S(2)}) collective-permute-start(bf16[64,512]{1,0:T(8,128)(2,1)S(1)} %get-tuple-element.58), channel_id=1, source_target_pairs={{0,2},{1,3},{2,0},{3,1},{4,6},{5,7},{6,4},{7,5},{8,10},{9,11},{10,... | collective-permute-start | bytes 196616 | tf_op jit(solution)/shard_map/ppermute | solution.py:515
  30.1 2.1 %collective-permute-done.17.rest_10_ = bf16[16,4,16,128]{3,2,1,0:T(8,128)(2,1)S(1)} collective-permute-done((bf16[16,4,16,128]{3,2,1,0:T(8,128)(2,1)S(1)}, bf16[16,4,16,128]{3,2,1,0:T(8,128)(2,1)S(1)}, u32[]{:S(2)}, u32[]{:S(2)}) %collective-permute-start.17) | collective-permute-done | bytes 262176 | tf_op jit(solution)/shard_map/ppermute | solution.py:548
  32.2 1.4 %collective-permute-start.22 = (bf16[16,4,16,128]{3,2,1,0:T(8,128)(2,1)S(1)}, bf16[16,4,16,128]{3,2,1,0:T(8,128)(2,1)S(1)}, u32[]{:S(2)}, u32[]{:S(2)}) collective-permute-start(bf16[16,4,16,128]{3,2,1,0:T(8,128)(2,1)S(1)} %collective-permute-done.17.rest_10_), channel_id=1, source_target_pairs={{0,8},{8,16},{16,24},{24,28},{28,20},{20,12},{12,4},{4,0},{1,9},{9... | collective-permute-start | bytes 786440 | tf_op jit(solution)/shard_map/ppermute | solution.py:548
  33.6 4.3 %cross.4 = (bf16[128,512]{1,0:T(8,128)(2,1)S(1)}, bf16[128,512]{1,0:T(8,128)(2,1)S(1)}, bf16[128,512]{1,0:T(8,128)(2,1)S(1)}, bf16[128,512]{1,0:T(8,128)(2,1)S(1)}) custom-call(s32[4,8]{1,0:T(4,128)S(1)} %copy-done.1, bf16[2048,512]{1,0:T(8,128)(2,1)S(1)} %copy-done.2, f32[2,3,8,8,8,128]{5,4,3,2,1,0:T(8,128)S(1)} %widen.2.rest_0_, ...), custom_call_target="tpu_custom_call" | custom-call | flops 5289999872 | bytes 1024 | tf_op jit(solution)/shard_map/cross/pallas_call | solution.py:363
  38.1 1.8 %collective-permute-start.20 = (bf16[128,512]{1,0:T(8,128)(2,1)S(1)}, bf16[128,512]{1,0:T(8,128)(2,1)S(1)}, u32[]{:S(2)}, u32[]{:S(2)}) collective-permute-start(bf16[128,512]{1,0:T(8,128)(2,1)S(1)} %get-tuple-element.65), channel_id=1, source_target_pairs={{0,2},{1,3},{2,0},{3,1},{4,6},{5,7},{6,4},{7,5},{8,10},{9,11},{10,... | collective-permute-start | bytes 393224 | tf_op jit(solution)/shard_map/ppermute | solution.py:515
  40.0 0.3 collective-permute-done.22.rest_12_
  40.3 2.6 %cross.5 = (bf16[64,512]{1,0:T(8,128)(2,1)S(1)}, bf16[64,512]{1,0:T(8,128)(2,1)S(1)}, bf16[64,512]{1,0:T(8,128)(2,1)S(1)}, bf16[64,512]{1,0:T(8,128)(2,1)S(1)}) custom-call(s32[4,8]{1,0:T(4,128)S(1)} %copy-done.1, bf16[2048,512]{1,0:T(8,128)(2,1)S(1)} %copy-done.2, f32[2,3,8,8,8,128]{5,4,3,2,1,0:T(8,128)S(1)} %widen.2.rest_0_, ...), custom_call_target="tpu_custom_call" | custom-call | flops 2990000128 | bytes 1024 | tf_op jit(solution)/shard_map/cross/pallas_call | solution.py:363
  43.0 1.7 %collective-permute-start.24 = (bf16[64,512]{1,0:T(8,128)(2,1)S(1)}, bf16[64,512]{1,0:T(8,128)(2,1)S(1)}, u32[]{:S(2)}, u32[]{:S(2)}) collective-permute-start(bf16[64,512]{1,0:T(8,128)(2,1)S(1)} %get-tuple-element.71), channel_id=1, source_target_pairs={{0,2},{1,3},{2,0},{3,1},{4,6},{5,7},{6,4},{7,5},{8,10},{9,11},{10,... | collective-permute-start | bytes 196616 | tf_op jit(solution)/shard_map/ppermute | solution.py:515
  44.9 1.6 %collective-permute-done.21.rest_7_ = bf16[128,512]{1,0:T(8,128)(2,1)S(1)} collective-permute-done((bf16[128,512]{1,0:T(8,128)(2,1)S(1)}, bf16[128,512]{1,0:T(8,128)(2,1)S(1)}, u32[]{:S(2)}, u32[]{:S(2)}) %collective-permute-start.21) | collective-permute-done | bytes 131104 | tf_op jit(solution)/shard_map/ppermute | solution.py:515
  46.5 2.1 %early.1 = f32[1024,4,1,128]{3,2,1,0:T(1,128)} custom-call(s32[4,8]{1,0:T(4,128)S(1)} %copy-done.1, bf16[4,128,512]{2,1,0:T(8,128)(2,1)S(1)} %copy-done, bf16[64,512]{1,0:T(8,128)(2,1)S(1)} %get-tuple-element.56.rest_0_, bf16[64,512]{1,0:T(8,128)(2,1)S(1)} %collective-permute-done.14.rest_1_, bf16[64,512]{1,0:T(8,128)(2,1)S(1)} %collective-permute-done.15.rest_2_, ...), custom_call_target="tpu_custom_call" | custom-call | flops 57500000 | bytes 1024 | tf_op jit(solution)/shard_map/early/pallas_call | solution.py:461
  48.6 0.5 collective-permute-done.25.rest_3_
  49.1 1.6 %late.1 = f32[1024,4,1,128]{3,2,1,0:T(1,128)} custom-call(s32[4,8]{1,0:T(4,128)S(1)} %copy-done.1, bf16[4,128,512]{2,1,0:T(8,128)(2,1)S(1)} %copy-done, f32[1024,4,1,128]{3,2,1,0:T(1,128)} %early.1, bf16[64,512]{1,0:T(8,128)(2,1)S(1)} %get-tuple-element.69.rest_0_, ...), custom_call_target="tpu_custom_call", output_to_operand_aliasing={{}: (2, {})} | custom-call | flops 57500000 | bytes 1024 | tf_op jit(solution)/shard_map/late/pallas_call | solution.py:474
  (38 shorter events, 1.5 us)
Async XLA Ops:
  3.0 3.3 %collective-permute-start = (bf16[4,4,16,128]{3,2,1,0:T(8,128)(2,1)S(1)}, bf16[4,4,16,128]{3,2,1,0:T(8,128)(2,1)S(1)}, u32[]{:S(2)}, u32[]{:S(2)}) collective-permute-start(bf16[4,4,16,128]{3,2,1,0:T(8,128)(2,1)S(1)} %get-tuple-element.40), channel_id=1, source_target_pairs={{0,1},{1,0},{2,3},{3,2},{4,5},{5,4},{6,7},{7,6},{8,9},{9,8},{10,11... | collective-permute-start | bytes 196616 | tf_op jit(solution)/shard_map/ppermute | solution.py:515
  3.6 5.3 %collective-permute-start.6 = (bf16[4,4,16,128]{3,2,1,0:T(8,128)(2,1)S(1)}, bf16[4,4,16,128]{3,2,1,0:T(8,128)(2,1)S(1)}, u32[]{:S(2)}, u32[]{:S(2)}) collective-permute-start(bf16[4,4,16,128]{3,2,1,0:T(8,128)(2,1)S(1)} %get-tuple-element.45), channel_id=1, source_target_pairs={{0,2},{1,3},{2,0},{3,1},{4,6},{5,7},{6,4},{7,5},{8,10},{9,11},{10,... | collective-permute-start | bytes 196616 | tf_op jit(solution)/shard_map/ppermute | solution.py:515
  6.1 4.0 %collective-permute-start.7 = (bf16[4,4,16,128]{3,2,1,0:T(8,128)(2,1)S(1)}, bf16[4,4,16,128]{3,2,1,0:T(8,128)(2,1)S(1)}, u32[]{:S(2)}, u32[]{:S(2)}) collective-permute-start(bf16[4,4,16,128]{3,2,1,0:T(8,128)(2,1)S(1)} %get-tuple-element.46), channel_id=1, source_target_pairs={{0,3},{1,2},{2,1},{3,0},{4,7},{5,6},{6,5},{7,4},{8,11},{9,10},{10,... | collective-permute-start | bytes 196616 | tf_op jit(solution)/shard_map/ppermute | solution.py:515
  6.2 4.0 %collective-permute-start.3 = (bf16[4,16,16,128]{3,2,1,0:T(8,128)(2,1)S(1)}, bf16[4,16,16,128]{3,2,1,0:T(8,128)(2,1)S(1)}, u32[]{:S(2)}, u32[]{:S(2)}) collective-permute-start(bf16[4,16,16,128]{3,2,1,0:T(8,128)(2,1)S(1)} %get-tuple-element.54.refs_0_), channel_id=1, source_target_pairs={{0,1},{1,0},{2,3},{3,2},{4,5},{5,4},{6,7},{7,6},{8,9},{9,8},{10,11... | collective-permute-start | bytes 786440 | tf_op jit(solution)/shard_map/ppermute | solution.py:515
  6.4 7.4 %collective-permute-start.2 = (bf16[8,4,16,128]{3,2,1,0:T(8,128)(2,1)S(1)}, bf16[8,4,16,128]{3,2,1,0:T(8,128)(2,1)S(1)}, u32[]{:S(2)}, u32[]{:S(2)}) collective-permute-start(bf16[8,4,16,128]{3,2,1,0:T(8,128)(2,1)S(1)} %constant_dynamic-update-slice_fusion), channel_id=1, source_target_pairs={{0,4},{8,0},{16,8},{24,16},{28,24},{20,28},{12,20},{4,12},{1,5},{9... | collective-permute-start | bytes 393224 | tf_op jit(solution)/shard_map/ppermute | solution.py:551
  8.4 5.4 %collective-permute-start.1 = (bf16[8,4,16,128]{3,2,1,0:T(8,128)(2,1)S(1)}, bf16[8,4,16,128]{3,2,1,0:T(8,128)(2,1)S(1)}, u32[]{:S(2)}, u32[]{:S(2)}) collective-permute-start(bf16[8,4,16,128]{3,2,1,0:T(8,128)(2,1)S(1)} %constant_dynamic-update-slice_fusion), channel_id=1, source_target_pairs={{0,8},{8,16},{16,24},{24,28},{28,20},{20,12},{12,4},{4,0},{1,9},{9... | collective-permute-start | bytes 393224 | tf_op jit(solution)/shard_map/ppermute | solution.py:548
  10.2 15.4 %copy-start.1 = (s32[4,8]{1,0:T(4,128)S(1)}, s32[4,8]{1,0:T(4,128)}, u32[]{:S(2)}) copy-start(s32[4,8]{1,0:T(4,128)} %plan.9) | copy-start | bytes 388
  10.2 15.4 %copy-start.2 = (bf16[2048,512]{1,0:T(8,128)(2,1)S(1)}, bf16[2048,512]{1,0:T(8,128)(2,1)}, u32[]{:S(2)}) copy-start(bf16[2048,512]{1,0:T(8,128)(2,1)} %constant.7.clone.table) | copy-start | bytes 6291460
  10.2 5.9 %collective-permute-start.9 = (bf16[8,4,16,128]{3,2,1,0:T(8,128)(2,1)S(1)}, bf16[8,4,16,128]{3,2,1,0:T(8,128)(2,1)S(1)}, u32[]{:S(2)}, u32[]{:S(2)}) collective-permute-start(bf16[8,4,16,128]{3,2,1,0:T(8,128)(2,1)S(1)} %pad_maximum_fusion), channel_id=1, source_target_pairs={{0,4},{8,0},{16,8},{24,16},{28,24},{20,28},{12,20},{4,12},{1,5},{9... | collective-permute-start | bytes 393224 | tf_op jit(solution)/shard_map/ppermute | solution.py:551
  11.8 6.3 %collective-permute-start.8 = (bf16[8,4,16,128]{3,2,1,0:T(8,128)(2,1)S(1)}, bf16[8,4,16,128]{3,2,1,0:T(8,128)(2,1)S(1)}, u32[]{:S(2)}, u32[]{:S(2)}) collective-permute-start(bf16[8,4,16,128]{3,2,1,0:T(8,128)(2,1)S(1)} %pad_maximum_fusion), channel_id=1, source_target_pairs={{0,8},{8,16},{16,24},{24,28},{28,20},{20,12},{12,4},{4,0},{1,9},{9... | collective-permute-start | bytes 393224 | tf_op jit(solution)/shard_map/ppermute | solution.py:548
  12.3 10.9 %collective-permute-start.12 = (bf16[4,16,16,128]{3,2,1,0:T(8,128)(2,1)S(1)}, bf16[4,16,16,128]{3,2,1,0:T(8,128)(2,1)S(1)}, u32[]{:S(2)}, u32[]{:S(2)}) collective-permute-start(bf16[4,16,16,128]{3,2,1,0:T(8,128)(2,1)S(1)} %get-tuple-element.54.refs_0_), channel_id=1, source_target_pairs={{0,2},{1,3},{2,0},{3,1},{4,6},{5,7},{6,4},{7,5},{8,10},{9,11},{10,... | collective-permute-start | bytes 786440 | tf_op jit(solution)/shard_map/ppermute | solution.py:515
  13.8 7.1 %collective-permute-start.4 = (bf16[8,4,16,128]{3,2,1,0:T(8,128)(2,1)S(1)}, bf16[8,4,16,128]{3,2,1,0:T(8,128)(2,1)S(1)}, u32[]{:S(2)}, u32[]{:S(2)}) collective-permute-start(bf16[8,4,16,128]{3,2,1,0:T(8,128)(2,1)S(1)} %collective-permute-done.1.rest_2_), channel_id=1, source_target_pairs={{0,8},{8,16},{16,24},{24,28},{28,20},{20,12},{12,4},{4,0},{1,9},{9... | collective-permute-start | bytes 393224 | tf_op jit(solution)/shard_map/ppermute | solution.py:548
  15.4 5.7 %collective-permute-start.5 = (bf16[8,4,16,128]{3,2,1,0:T(8,128)(2,1)S(1)}, bf16[8,4,16,128]{3,2,1,0:T(8,128)(2,1)S(1)}, u32[]{:S(2)}, u32[]{:S(2)}) collective-permute-start(bf16[8,4,16,128]{3,2,1,0:T(8,128)(2,1)S(1)} %collective-permute-done.2.rest_3_), channel_id=1, source_target_pairs={{0,4},{8,0},{16,8},{24,16},{28,24},{20,28},{12,20},{4,12},{1,5},{9... | collective-permute-start | bytes 393224 | tf_op jit(solution)/shard_map/ppermute | solution.py:551
  18.1 5.0 %collective-permute-start.10 = (bf16[8,4,16,128]{3,2,1,0:T(8,128)(2,1)S(1)}, bf16[8,4,16,128]{3,2,1,0:T(8,128)(2,1)S(1)}, u32[]{:S(2)}, u32[]{:S(2)}) collective-permute-start(bf16[8,4,16,128]{3,2,1,0:T(8,128)(2,1)S(1)} %collective-permute-done.8.rest_4_), channel_id=1, source_target_pairs={{0,8},{8,16},{16,24},{24,28},{28,20},{20,12},{12,4},{4,0},{1,9},{9... | collective-permute-start | bytes 393224 | tf_op jit(solution)/shard_map/ppermute | solution.py:548
  18.1 5.1 %collective-permute-start.11 = (bf16[8,4,16,128]{3,2,1,0:T(8,128)(2,1)S(1)}, bf16[8,4,16,128]{3,2,1,0:T(8,128)(2,1)S(1)}, u32[]{:S(2)}, u32[]{:S(2)}) collective-permute-start(bf16[8,4,16,128]{3,2,1,0:T(8,128)(2,1)S(1)} %collective-permute-done.9.rest_5_), channel_id=1, source_target_pairs={{0,4},{8,0},{16,8},{24,16},{28,24},{20,28},{12,20},{4,12},{1,5},{9... | collective-permute-start | bytes 393224 | tf_op jit(solution)/shard_map/ppermute | solution.py:551
  23.3 2.2 %collective-permute-start.13 = (bf16[4,16,16,128]{3,2,1,0:T(8,128)(2,1)S(1)}, bf16[4,16,16,128]{3,2,1,0:T(8,128)(2,1)S(1)}, u32[]{:S(2)}, u32[]{:S(2)}) collective-permute-start(bf16[4,16,16,128]{3,2,1,0:T(8,128)(2,1)S(1)} %collective-permute-done.12.refs_0_), channel_id=1, source_target_pairs={{0,1},{1,0},{2,3},{3,2},{4,5},{5,4},{6,7},{7,6},{8,9},{9,8},{10,11... | collective-permute-start | bytes 786440 | tf_op jit(solution)/shard_map/ppermute | solution.py:515
  23.3 8.9 %collective-permute-start.17 = (bf16[16,4,16,128]{3,2,1,0:T(8,128)(2,1)S(1)}, bf16[16,4,16,128]{3,2,1,0:T(8,128)(2,1)S(1)}, u32[]{:S(2)}, u32[]{:S(2)}) collective-permute-start(bf16[16,4,16,128]{3,2,1,0:T(8,128)(2,1)S(1)} %get-tuple-element.61), channel_id=1, source_target_pairs={{0,8},{8,16},{16,24},{24,28},{28,20},{20,12},{12,4},{4,0},{1,9},{9... | collective-permute-start | bytes 786440 | tf_op jit(solution)/shard_map/ppermute | solution.py:548
  25.0 8.7 %collective-permute-start.18 = (bf16[16,4,16,128]{3,2,1,0:T(8,128)(2,1)S(1)}, bf16[16,4,16,128]{3,2,1,0:T(8,128)(2,1)S(1)}, u32[]{:S(2)}, u32[]{:S(2)}) collective-permute-start(bf16[16,4,16,128]{3,2,1,0:T(8,128)(2,1)S(1)} %get-tuple-element.62), channel_id=1, source_target_pairs={{0,4},{8,0},{16,8},{24,16},{28,24},{20,28},{12,20},{4,12},{1,5},{9... | collective-permute-start | bytes 786440 | tf_op jit(solution)/shard_map/ppermute | solution.py:551
  28.2 9.9 %collective-permute-start.14 = (bf16[64,512]{1,0:T(8,128)(2,1)S(1)}, bf16[64,512]{1,0:T(8,128)(2,1)S(1)}, u32[]{:S(2)}, u32[]{:S(2)}) collective-permute-start(bf16[64,512]{1,0:T(8,128)(2,1)S(1)} %get-tuple-element.57), channel_id=1, source_target_pairs={{0,1},{1,0},{2,3},{3,2},{4,5},{5,4},{6,7},{7,6},{8,9},{9,8},{10,11... | collective-permute-start | bytes 196616 | tf_op jit(solution)/shard_map/ppermute | solution.py:515
  28.3 11.6 %collective-permute-start.15 = (bf16[64,512]{1,0:T(8,128)(2,1)S(1)}, bf16[64,512]{1,0:T(8,128)(2,1)S(1)}, u32[]{:S(2)}, u32[]{:S(2)}) collective-permute-start(bf16[64,512]{1,0:T(8,128)(2,1)S(1)} %get-tuple-element.58), channel_id=1, source_target_pairs={{0,2},{1,3},{2,0},{3,1},{4,6},{5,7},{6,4},{7,5},{8,10},{9,11},{10,... | collective-permute-start | bytes 196616 | tf_op jit(solution)/shard_map/ppermute | solution.py:515
  30.0 9.9 %collective-permute-start.16 = (bf16[64,512]{1,0:T(8,128)(2,1)S(1)}, bf16[64,512]{1,0:T(8,128)(2,1)S(1)}, u32[]{:S(2)}, u32[]{:S(2)}) collective-permute-start(bf16[64,512]{1,0:T(8,128)(2,1)S(1)} %get-tuple-element.59), channel_id=1, source_target_pairs={{0,3},{1,2},{2,1},{3,0},{4,7},{5,6},{6,5},{7,4},{8,11},{9,10},{10,... | collective-permute-start | bytes 196616 | tf_op jit(solution)/shard_map/ppermute | solution.py:515
  32.2 8.1 %collective-permute-start.22 = (bf16[16,4,16,128]{3,2,1,0:T(8,128)(2,1)S(1)}, bf16[16,4,16,128]{3,2,1,0:T(8,128)(2,1)S(1)}, u32[]{:S(2)}, u32[]{:S(2)}) collective-permute-start(bf16[16,4,16,128]{3,2,1,0:T(8,128)(2,1)S(1)} %collective-permute-done.17.rest_10_), channel_id=1, source_target_pairs={{0,8},{8,16},{16,24},{24,28},{28,20},{20,12},{12,4},{4,0},{1,9},{9... | collective-permute-start | bytes 786440 | tf_op jit(solution)/shard_map/ppermute | solution.py:548
  38.0 6.7 %collective-permute-start.19 = (bf16[128,512]{1,0:T(8,128)(2,1)S(1)}, bf16[128,512]{1,0:T(8,128)(2,1)S(1)}, u32[]{:S(2)}, u32[]{:S(2)}) collective-permute-start(bf16[128,512]{1,0:T(8,128)(2,1)S(1)} %get-tuple-element.64), channel_id=1, source_target_pairs={{0,1},{1,0},{2,3},{3,2},{4,5},{5,4},{6,7},{7,6},{8,9},{9,8},{10,11... | collective-permute-start | bytes 393224 | tf_op jit(solution)/shard_map/ppermute | solution.py:515
  38.1 6.8 %collective-permute-start.20 = (bf16[128,512]{1,0:T(8,128)(2,1)S(1)}, bf16[128,512]{1,0:T(8,128)(2,1)S(1)}, u32[]{:S(2)}, u32[]{:S(2)}) collective-permute-start(bf16[128,512]{1,0:T(8,128)(2,1)S(1)} %get-tuple-element.65), channel_id=1, source_target_pairs={{0,2},{1,3},{2,0},{3,1},{4,6},{5,7},{6,4},{7,5},{8,10},{9,11},{10,... | collective-permute-start | bytes 393224 | tf_op jit(solution)/shard_map/ppermute | solution.py:515
  39.9 6.6 %collective-permute-start.21 = (bf16[128,512]{1,0:T(8,128)(2,1)S(1)}, bf16[128,512]{1,0:T(8,128)(2,1)S(1)}, u32[]{:S(2)}, u32[]{:S(2)}) collective-permute-start(bf16[128,512]{1,0:T(8,128)(2,1)S(1)} %get-tuple-element.66), channel_id=1, source_target_pairs={{0,3},{1,2},{2,1},{3,0},{4,7},{5,6},{6,5},{7,4},{8,11},{9,10},{10,... | collective-permute-start | bytes 393224 | tf_op jit(solution)/shard_map/ppermute | solution.py:515
  40.0 6.5 %copy-start = (bf16[4,128,512]{2,1,0:T(8,128)(2,1)S(1)}, bf16[4,128,512]{2,1,0:T(8,128)(2,1)}, u32[]{:S(2)}) copy-start(bf16[4,128,512]{2,1,0:T(8,128)(2,1)} %constant.8.clone.place) | copy-start | bytes 1572868
  42.9 5.7 %collective-permute-start.23 = (bf16[64,512]{1,0:T(8,128)(2,1)S(1)}, bf16[64,512]{1,0:T(8,128)(2,1)S(1)}, u32[]{:S(2)}, u32[]{:S(2)}) collective-permute-start(bf16[64,512]{1,0:T(8,128)(2,1)S(1)} %get-tuple-element.70), channel_id=1, source_target_pairs={{0,1},{1,0},{2,3},{3,2},{4,5},{5,4},{6,7},{7,6},{8,9},{9,8},{10,11... | collective-permute-start | bytes 196616 | tf_op jit(solution)/shard_map/ppermute | solution.py:515
  43.0 5.7 %collective-permute-start.24 = (bf16[64,512]{1,0:T(8,128)(2,1)S(1)}, bf16[64,512]{1,0:T(8,128)(2,1)S(1)}, u32[]{:S(2)}, u32[]{:S(2)}) collective-permute-start(bf16[64,512]{1,0:T(8,128)(2,1)S(1)} %get-tuple-element.71), channel_id=1, source_target_pairs={{0,2},{1,3},{2,0},{3,1},{4,6},{5,7},{6,4},{7,5},{8,10},{9,11},{10,... | collective-permute-start | bytes 196616 | tf_op jit(solution)/shard_map/ppermute | solution.py:515
  44.7 4.4 %collective-permute-start.25 = (bf16[64,512]{1,0:T(8,128)(2,1)S(1)}, bf16[64,512]{1,0:T(8,128)(2,1)S(1)}, u32[]{:S(2)}, u32[]{:S(2)}) collective-permute-start(bf16[64,512]{1,0:T(8,128)(2,1)S(1)} %get-tuple-element.72), channel_id=1, source_target_pairs={{0,3},{1,2},{2,1},{3,0},{4,7},{5,6},{6,5},{7,4},{8,11},{9,10},{10,... | collective-permute-start | bytes 196616 | tf_op jit(solution)/shard_map/ppermute | solution.py:515

commit v19 on v18

--- a/solution.py
+++ b/solution.py
@@ -221,13 +221,13 @@
     )
 
 
-def widen_kernel(*refs):
+def widen_kernel(scale, *refs):
     blocks, own = refs[:-1], refs[-1]
     windows = blocks[0].shape[0]
     for j, block in enumerate(blocks):
 
         def widen(w, carry, j=j, block=block):
-            raw = block[w].astype(F32)
+            raw = block[w].astype(F32) * scale
             real, imag = raw[:, :TILES], raw[:, TILES:]
             both = real + imag
             for group in range(own.shape[0]):
@@ -240,11 +240,11 @@
         lax.fori_loop(0, windows, widen, 0)
 
 
-def widen_own(blocks):
+def widen_own(blocks, scale):
     windows, stations = blocks[0].shape[:2]
     vmem = pl.BlockSpec(memory_space=pltpu.VMEM)
     return pl.pallas_call(
-        widen_kernel,
+        functools.partial(widen_kernel, scale),
         out_shape=jax.ShapeDtypeStruct(
             (stations // GROUP, 3, len(blocks) * windows, GROUP, TILES, LANES), F32
         ),
@@ -310,7 +310,7 @@
         lax.fori_loop(0, 3 * groups, body, 0)
 
 
-def cross_kernel(first_slot, slots, count, scaling, places, parts, plan, table, *rest):
+def cross_kernel(first_slot, slots, count, places, parts, plan, table, *rest):
     owns, rest = rest[:2], rest[2:]
     others, rest = rest[: len(places)], rest[len(places) :]
     outs = rest[:parts]
@@ -340,7 +340,7 @@
             operand[rows, at] = turned[q][0].astype(BF)
             operand[rows, at_imag] = turned[q][1].astype(BF)
     block = jnp.dot(operand[...], table[...], preferred_element_type=F32)
-    block = (block * (2.0 * scaling)).astype(BF)
+    block = block.astype(BF)
     me = lax.axis_index("seg")
     for place in range(parts):
 
@@ -351,7 +351,7 @@
                 outs[j][...] = block[q * columns : (q + 1) * columns]
 
 
-def cross_lags(plan, table, owns, places, candidates, first_slot, slots, count, parts, scaling):
+def cross_lags(plan, table, owns, places, candidates, first_slot, slots, count, parts):
     windows, stations = owns[0].shape[2], owns[0].shape[0] * owns[0].shape[3]
     quarter = candidates[0].shape[1]
     columns = slots * stations * quarter
@@ -362,7 +362,7 @@
     operands = [table, *owns, *candidates]
     return pl.pallas_call(
         functools.partial(
-            cross_kernel, first_slot, slots, count, scaling, tuple(places), parts
+            cross_kernel, first_slot, slots, count, tuple(places), parts
         ),
         out_shape=[jax.ShapeDtypeStruct(out, BF)] * parts,
         in_specs=[smem] + [vmem] * len(operands),
@@ -552,7 +552,7 @@
 
     far, white_far = lax.optimization_barrier((far, white))
     across = swap(white_far, 2)
-    near_own = widen_own([white, sibling])
+    near_own = widen_own([white, sibling], 2.0 * scaling)
     half = near.shape[0]
     places, blocks, arrived = [], [], []
 
@@ -577,7 +577,7 @@
         all_up, all_down = up(all_up), down(all_down)
         arrive(step, 0, all_up, all_down)
     arrived.append((list(places), list(blocks)))
-    far_own = widen_own([across, swap(across, 1)])
+    far_own = widen_own([across, swap(across, 1)], 2.0 * scaling)
     groups = [(0, 1), (1, 2), (3, 1)]
     if count % 2 == 0:
         places.append((count // 2, 0))
@@ -591,7 +591,7 @@
             near_own = after(near_own, lags)
         at, values = arrived[index - len(groups)]
         lags = cross_lags(
-            plan, lag_table, [near_own, far_own], at, values, first_slot, slots, count, parts, scaling
+            plan, lag_table, [near_own, far_own], at, values, first_slot, slots, count, parts
         )
         pieces = pieces + exchange(lags)
     return place_lags(plan, groups, pieces, count, stations, parts)

time: 50.9 us -> 50.9 us (level)
  no operation moved by 1% of the time
where the time goes in v19:
time: 50.9 us; the launch traced here: 50.7 us
  starting transfers between devices  22.3 us (44%)
  Pallas kernels  16.6 us (33%)
  waiting for transfers between devices  11.6 us (23%)
    ppermute x15, starting transfers between devices, swap(): return lax.ppermute(value, 'seg', [(i, i ^ j) for i in range(parts)])  10.5 us
    pallas_call x3, Pallas kernels, cross_lags(): pl.pallas_call(functools.partial(cross_kernel, first_slot, slots, count,...  9.51 us
    ppermute x6, waiting for transfers between devices, up(): return lax.ppermute(value, 'sta', upward)  7.19 us
    ppermute x5, starting transfers between devices, down(): return lax.ppermute(value, 'sta', downward)  6.51 us
    ppermute x6, starting transfers between devices, up(): return lax.ppermute(value, 'sta', upward)  5.29 us
    ppermute x15, waiting for transfers between devices, swap(): return lax.ppermute(value, 'seg', [(i, i ^ j) for i in range(parts)])  3.85 us
    pallas_call x1, Pallas kernels, prepare(): pl.pallas_call(functools.partial(prep_kernel, parts, windows), out_shape=...  3.04 us
    pallas_call x1, Pallas kernels, place_lags(): pl.pallas_call(functools.partial(early_kernel, count, parts, tuple(groups...  2.1 us
  transfers between devices with their start and end apart: 26, of which 12 were waited for; matrix products, arithmetic and copies ran while one was open for 0% of the time, Pallas kernels for 23%

profile of v19, /device:TPU:0, one launch (start us, length us, event | category | flops | bytes accessed | tf_op | source)
XLA Modules:
  0.0 50.7 jit_solution(842358612577297492)
XLA Ops:
  0.0 3.0 %prep.1 = (bf16[4,16,16,128]{3,2,1,0:T(8,128)(2,1)S(1)}, bf16[4,4,16,128]{3,2,1,0:T(8,128)(2,1)S(1)}, bf16[4,4,16,128]{3,2,1,0:T(8,128)(2,1)S(1)}, bf16[4,4,16,1...) custom-call(f32[1024,128]{1,0:T(8,128)} %bitcast.10, bf16[512,2048]{1,0:T(8,128)(2,1)} %constant.6.clone.table_hbm), custom_call_target="tpu_custom_call" | custom-call | flops 536870912 | bytes 3145728 | tf_op jit(solution)/shard_map/prep/pallas_call | solution.py:169
  3.0 0.5 %collective-permute-start = (bf16[4,4,16,128]{3,2,1,0:T(8,128)(2,1)S(1)}, bf16[4,4,16,128]{3,2,1,0:T(8,128)(2,1)S(1)}, u32[]{:S(2)}, u32[]{:S(2)}) collective-permute-start(bf16[4,4,16,128]{3,2,1,0:T(8,128)(2,1)S(1)} %get-tuple-element.40), channel_id=1, source_target_pairs={{0,1},{1,0},{2,3},{3,2},{4,5},{5,4},{6,7},{7,6},{8,9},{9,8},{10,11... | collective-permute-start | bytes 196616 | tf_op jit(solution)/shard_map/ppermute | solution.py:515
  3.6 2.6 %collective-permute-start.6 = (bf16[4,4,16,128]{3,2,1,0:T(8,128)(2,1)S(1)}, bf16[4,4,16,128]{3,2,1,0:T(8,128)(2,1)S(1)}, u32[]{:S(2)}, u32[]{:S(2)}) collective-permute-start(bf16[4,4,16,128]{3,2,1,0:T(8,128)(2,1)S(1)} %get-tuple-element.45), channel_id=1, source_target_pairs={{0,2},{1,3},{2,0},{3,1},{4,6},{5,7},{6,4},{7,5},{8,10},{9,11},{10,... | collective-permute-start | bytes 196616 | tf_op jit(solution)/shard_map/ppermute | solution.py:515
  6.4 2.0 %collective-permute-start.2 = (bf16[8,4,16,128]{3,2,1,0:T(8,128)(2,1)S(1)}, bf16[8,4,16,128]{3,2,1,0:T(8,128)(2,1)S(1)}, u32[]{:S(2)}, u32[]{:S(2)}) collective-permute-start(bf16[8,4,16,128]{3,2,1,0:T(8,128)(2,1)S(1)} %constant_dynamic-update-slice_fusion), channel_id=1, source_target_pairs={{0,4},{8,0},{16,8},{24,16},{28,24},{20,28},{12,20},{4,12},{1,5},{9... | collective-permute-start | bytes 393224 | tf_op jit(solution)/shard_map/ppermute | solution.py:551
  8.5 0.3 collective-permute-done.6
  8.8 1.4 %collective-permute-done.7 = bf16[4,4,16,128]{3,2,1,0:T(8,128)(2,1)S(1)} collective-permute-done((bf16[4,4,16,128]{3,2,1,0:T(8,128)(2,1)S(1)}, bf16[4,4,16,128]{3,2,1,0:T(8,128)(2,1)S(1)}, u32[]{:S(2)}, u32[]{:S(2)}) %collective-permute-start.7) | collective-permute-done | bytes 65568 | tf_op jit(solution)/shard_map/ppermute | solution.py:515
  10.2 1.6 %collective-permute-start.9 = (bf16[8,4,16,128]{3,2,1,0:T(8,128)(2,1)S(1)}, bf16[8,4,16,128]{3,2,1,0:T(8,128)(2,1)S(1)}, u32[]{:S(2)}, u32[]{:S(2)}) collective-permute-start(bf16[8,4,16,128]{3,2,1,0:T(8,128)(2,1)S(1)} %pad_maximum_fusion), channel_id=1, source_target_pairs={{0,4},{8,0},{16,8},{24,16},{28,24},{20,28},{12,20},{4,12},{1,5},{9... | collective-permute-start | bytes 393224 | tf_op jit(solution)/shard_map/ppermute | solution.py:551
  11.8 0.5 collective-permute-start.8
  12.3 1.3 %collective-permute-start.12 = (bf16[4,16,16,128]{3,2,1,0:T(8,128)(2,1)S(1)}, bf16[4,16,16,128]{3,2,1,0:T(8,128)(2,1)S(1)}, u32[]{:S(2)}, u32[]{:S(2)}) collective-permute-start(bf16[4,16,16,128]{3,2,1,0:T(8,128)(2,1)S(1)} %get-tuple-element.54.refs_0_), channel_id=1, source_target_pairs={{0,2},{1,3},{2,0},{3,1},{4,6},{5,7},{6,4},{7,5},{8,10},{9,11},{10,... | collective-permute-start | bytes 786440 | tf_op jit(solution)/shard_map/ppermute | solution.py:515
  13.8 1.6 %collective-permute-start.4 = (bf16[8,4,16,128]{3,2,1,0:T(8,128)(2,1)S(1)}, bf16[8,4,16,128]{3,2,1,0:T(8,128)(2,1)S(1)}, u32[]{:S(2)}, u32[]{:S(2)}) collective-permute-start(bf16[8,4,16,128]{3,2,1,0:T(8,128)(2,1)S(1)} %collective-permute-done.1.rest_2_), channel_id=1, source_target_pairs={{0,8},{8,16},{16,24},{24,28},{28,20},{20,12},{12,4},{4,0},{1,9},{9... | collective-permute-start | bytes 393224 | tf_op jit(solution)/shard_map/ppermute | solution.py:548
  15.4 0.4 collective-permute-start.5
  15.9 0.3 collective-permute-done.9.rest_5_
  16.1 2.0 %collective-permute-done.8.rest_4_ = bf16[8,4,16,128]{3,2,1,0:T(8,128)(2,1)S(1)} collective-permute-done((bf16[8,4,16,128]{3,2,1,0:T(8,128)(2,1)S(1)}, bf16[8,4,16,128]{3,2,1,0:T(8,128)(2,1)S(1)}, u32[]{:S(2)}, u32[]{:S(2)}) %collective-permute-start.8) | collective-permute-done | bytes 131104 | tf_op jit(solution)/shard_map/ppermute | solution.py:548
  18.1 2.0 %collective-permute-start.11 = (bf16[8,4,16,128]{3,2,1,0:T(8,128)(2,1)S(1)}, bf16[8,4,16,128]{3,2,1,0:T(8,128)(2,1)S(1)}, u32[]{:S(2)}, u32[]{:S(2)}) collective-permute-start(bf16[8,4,16,128]{3,2,1,0:T(8,128)(2,1)S(1)} %collective-permute-done.9.rest_5_), channel_id=1, source_target_pairs={{0,4},{8,0},{16,8},{24,16},{28,24},{20,28},{12,20},{4,12},{1,5},{9... | collective-permute-start | bytes 393224 | tf_op jit(solution)/shard_map/ppermute | solution.py:551
  20.2 0.8 %collective-permute-done.4.refs_0_.rest_6_ = bf16[8,4,16,128]{3,2,1,0:T(8,128)(2,1)S(1)} collective-permute-done((bf16[8,4,16,128]{3,2,1,0:T(8,128)(2,1)S(1)}, bf16[8,4,16,128]{3,2,1,0:T(8,128)(2,1)S(1)}, u32[]{:S(2)}, u32[]{:S(2)}) %collective-permute-start.4) | collective-permute-done | bytes 131104 | tf_op jit(solution)/shard_map/ppermute | solution.py:548
  20.9 0.2 collective-permute-done.5.refs_1_.rest_7_
  21.1 2.0 %collective-permute-done.10.refs_2_.rest_8_ = bf16[8,4,16,128]{3,2,1,0:T(8,128)(2,1)S(1)} collective-permute-done((bf16[8,4,16,128]{3,2,1,0:T(8,128)(2,1)S(1)}, bf16[8,4,16,128]{3,2,1,0:T(8,128)(2,1)S(1)}, u32[]{:S(2)}, u32[]{:S(2)}) %collective-permute-start.10) | collective-permute-done | bytes 131104 | tf_op jit(solution)/shard_map/ppermute | solution.py:548
  23.3 1.6 %collective-permute-start.17 = (bf16[16,4,16,128]{3,2,1,0:T(8,128)(2,1)S(1)}, bf16[16,4,16,128]{3,2,1,0:T(8,128)(2,1)S(1)}, u32[]{:S(2)}, u32[]{:S(2)}) collective-permute-start(bf16[16,4,16,128]{3,2,1,0:T(8,128)(2,1)S(1)} %get-tuple-element.61), channel_id=1, source_target_pairs={{0,8},{8,16},{16,24},{24,28},{28,20},{20,12},{12,4},{4,0},{1,9},{9... | collective-permute-start | bytes 786440 | tf_op jit(solution)/shard_map/ppermute | solution.py:548
  25.0 0.5 collective-permute-start.18
  25.6 2.6 %cross.3 = (bf16[64,512]{1,0:T(8,128)(2,1)S(1)}, bf16[64,512]{1,0:T(8,128)(2,1)S(1)}, bf16[64,512]{1,0:T(8,128)(2,1)S(1)}, bf16[64,512]{1,0:T(8,128)(2,1)S(1)}) custom-call(s32[4,8]{1,0:T(4,128)S(1)} %copy-done.1, bf16[2048,512]{1,0:T(8,128)(2,1)S(1)} %copy-done.2, f32[2,3,8,8,8,128]{5,4,3,2,1,0:T(8,128)S(1)} %widen.2.rest_0_, ...), custom_call_target="tpu_custom_call" | custom-call | flops 2990000128 | bytes 1024 | tf_op jit(solution)/shard_map/cross/pallas_call | solution.py:363
  28.3 1.7 %collective-permute-start.15 = (bf16[64,512]{1,0:T(8,128)(2,1)S(1)}, bf16[64,512]{1,0:T(8,128)(2,1)S(1)}, u32[]{:S(2)}, u32[]{:S(2)}) collective-permute-start(bf16[64,512]{1,0:T(8,128)(2,1)S(1)} %get-tuple-element.58), channel_id=1, source_target_pairs={{0,2},{1,3},{2,0},{3,1},{4,6},{5,7},{6,4},{7,5},{8,10},{9,11},{10,... | collective-permute-start | bytes 196616 | tf_op jit(solution)/shard_map/ppermute | solution.py:515
  30.1 2.1 %collective-permute-done.17.rest_10_ = bf16[16,4,16,128]{3,2,1,0:T(8,128)(2,1)S(1)} collective-permute-done((bf16[16,4,16,128]{3,2,1,0:T(8,128)(2,1)S(1)}, bf16[16,4,16,128]{3,2,1,0:T(8,128)(2,1)S(1)}, u32[]{:S(2)}, u32[]{:S(2)}) %collective-permute-start.17) | collective-permute-done | bytes 262176 | tf_op jit(solution)/shard_map/ppermute | solution.py:548
  32.2 1.4 %collective-permute-start.22 = (bf16[16,4,16,128]{3,2,1,0:T(8,128)(2,1)S(1)}, bf16[16,4,16,128]{3,2,1,0:T(8,128)(2,1)S(1)}, u32[]{:S(2)}, u32[]{:S(2)}) collective-permute-start(bf16[16,4,16,128]{3,2,1,0:T(8,128)(2,1)S(1)} %collective-permute-done.17.rest_10_), channel_id=1, source_target_pairs={{0,8},{8,16},{16,24},{24,28},{28,20},{20,12},{12,4},{4,0},{1,9},{9... | collective-permute-start | bytes 786440 | tf_op jit(solution)/shard_map/ppermute | solution.py:548
  33.6 4.3 %cross.4 = (bf16[128,512]{1,0:T(8,128)(2,1)S(1)}, bf16[128,512]{1,0:T(8,128)(2,1)S(1)}, bf16[128,512]{1,0:T(8,128)(2,1)S(1)}, bf16[128,512]{1,0:T(8,128)(2,1)S(1)}) custom-call(s32[4,8]{1,0:T(4,128)S(1)} %copy-done.1, bf16[2048,512]{1,0:T(8,128)(2,1)S(1)} %copy-done.2, f32[2,3,8,8,8,128]{5,4,3,2,1,0:T(8,128)S(1)} %widen.2.rest_0_, ...), custom_call_target="tpu_custom_call" | custom-call | flops 5289999872 | bytes 1024 | tf_op jit(solution)/shard_map/cross/pallas_call | solution.py:363
  38.1 1.8 %collective-permute-start.20 = (bf16[128,512]{1,0:T(8,128)(2,1)S(1)}, bf16[128,512]{1,0:T(8,128)(2,1)S(1)}, u32[]{:S(2)}, u32[]{:S(2)}) collective-permute-start(bf16[128,512]{1,0:T(8,128)(2,1)S(1)} %get-tuple-element.65), channel_id=1, source_target_pairs={{0,2},{1,3},{2,0},{3,1},{4,6},{5,7},{6,4},{7,5},{8,10},{9,11},{10,... | collective-permute-start | bytes 393224 | tf_op jit(solution)/shard_map/ppermute | solution.py:515
  40.0 0.3 collective-permute-done.22.rest_12_
  40.3 2.6 %cross.5 = (bf16[64,512]{1,0:T(8,128)(2,1)S(1)}, bf16[64,512]{1,0:T(8,128)(2,1)S(1)}, bf16[64,512]{1,0:T(8,128)(2,1)S(1)}, bf16[64,512]{1,0:T(8,128)(2,1)S(1)}) custom-call(s32[4,8]{1,0:T(4,128)S(1)} %copy-done.1, bf16[2048,512]{1,0:T(8,128)(2,1)S(1)} %copy-done.2, f32[2,3,8,8,8,128]{5,4,3,2,1,0:T(8,128)S(1)} %widen.2.rest_0_, ...), custom_call_target="tpu_custom_call" | custom-call | flops 2990000128 | bytes 1024 | tf_op jit(solution)/shard_map/cross/pallas_call | solution.py:363
  43.0 1.7 %collective-permute-start.24 = (bf16[64,512]{1,0:T(8,128)(2,1)S(1)}, bf16[64,512]{1,0:T(8,128)(2,1)S(1)}, u32[]{:S(2)}, u32[]{:S(2)}) collective-permute-start(bf16[64,512]{1,0:T(8,128)(2,1)S(1)} %get-tuple-element.71), channel_id=1, source_target_pairs={{0,2},{1,3},{2,0},{3,1},{4,6},{5,7},{6,4},{7,5},{8,10},{9,11},{10,... | collective-permute-start | bytes 196616 | tf_op jit(solution)/shard_map/ppermute | solution.py:515
  44.9 1.6 %collective-permute-done.21.rest_7_ = bf16[128,512]{1,0:T(8,128)(2,1)S(1)} collective-permute-done((bf16[128,512]{1,0:T(8,128)(2,1)S(1)}, bf16[128,512]{1,0:T(8,128)(2,1)S(1)}, u32[]{:S(2)}, u32[]{:S(2)}) %collective-permute-start.21) | collective-permute-done | bytes 131104 | tf_op jit(solution)/shard_map/ppermute | solution.py:515
  46.5 2.1 %early.1 = f32[1024,4,1,128]{3,2,1,0:T(1,128)} custom-call(s32[4,8]{1,0:T(4,128)S(1)} %copy-done.1, bf16[4,128,512]{2,1,0:T(8,128)(2,1)S(1)} %copy-done, bf16[64,512]{1,0:T(8,128)(2,1)S(1)} %get-tuple-element.56.rest_0_, bf16[64,512]{1,0:T(8,128)(2,1)S(1)} %collective-permute-done.14.rest_1_, bf16[64,512]{1,0:T(8,128)(2,1)S(1)} %collective-permute-done.15.rest_2_, ...), custom_call_target="tpu_custom_call" | custom-call | flops 57500000 | bytes 1024 | tf_op jit(solution)/shard_map/early/pallas_call | solution.py:461
  48.6 0.5 collective-permute-done.25.rest_3_
  49.1 1.6 %late.1 = f32[1024,4,1,128]{3,2,1,0:T(1,128)} custom-call(s32[4,8]{1,0:T(4,128)S(1)} %copy-done.1, bf16[4,128,512]{2,1,0:T(8,128)(2,1)S(1)} %copy-done, f32[1024,4,1,128]{3,2,1,0:T(1,128)} %early.1, bf16[64,512]{1,0:T(8,128)(2,1)S(1)} %get-tuple-element.69.rest_0_, ...), custom_call_target="tpu_custom_call", output_to_operand_aliasing={{}: (2, {})} | custom-call | flops 57500000 | bytes 1024 | tf_op jit(solution)/shard_map/late/pallas_call | solution.py:474
  (38 shorter events, 1.5 us)
Async XLA Ops:
  3.0 3.3 %collective-permute-start = (bf16[4,4,16,128]{3,2,1,0:T(8,128)(2,1)S(1)}, bf16[4,4,16,128]{3,2,1,0:T(8,128)(2,1)S(1)}, u32[]{:S(2)}, u32[]{:S(2)}) collective-permute-start(bf16[4,4,16,128]{3,2,1,0:T(8,128)(2,1)S(1)} %get-tuple-element.40), channel_id=1, source_target_pairs={{0,1},{1,0},{2,3},{3,2},{4,5},{5,4},{6,7},{7,6},{8,9},{9,8},{10,11... | collective-permute-start | bytes 196616 | tf_op jit(solution)/shard_map/ppermute | solution.py:515
  3.6 5.3 %collective-permute-start.6 = (bf16[4,4,16,128]{3,2,1,0:T(8,128)(2,1)S(1)}, bf16[4,4,16,128]{3,2,1,0:T(8,128)(2,1)S(1)}, u32[]{:S(2)}, u32[]{:S(2)}) collective-permute-start(bf16[4,4,16,128]{3,2,1,0:T(8,128)(2,1)S(1)} %get-tuple-element.45), channel_id=1, source_target_pairs={{0,2},{1,3},{2,0},{3,1},{4,6},{5,7},{6,4},{7,5},{8,10},{9,11},{10,... | collective-permute-start | bytes 196616 | tf_op jit(solution)/shard_map/ppermute | solution.py:515
  6.1 4.0 %collective-permute-start.7 = (bf16[4,4,16,128]{3,2,1,0:T(8,128)(2,1)S(1)}, bf16[4,4,16,128]{3,2,1,0:T(8,128)(2,1)S(1)}, u32[]{:S(2)}, u32[]{:S(2)}) collective-permute-start(bf16[4,4,16,128]{3,2,1,0:T(8,128)(2,1)S(1)} %get-tuple-element.46), channel_id=1, source_target_pairs={{0,3},{1,2},{2,1},{3,0},{4,7},{5,6},{6,5},{7,4},{8,11},{9,10},{10,... | collective-permute-start | bytes 196616 | tf_op jit(solution)/shard_map/ppermute | solution.py:515
  6.2 4.0 %collective-permute-start.3 = (bf16[4,16,16,128]{3,2,1,0:T(8,128)(2,1)S(1)}, bf16[4,16,16,128]{3,2,1,0:T(8,128)(2,1)S(1)}, u32[]{:S(2)}, u32[]{:S(2)}) collective-permute-start(bf16[4,16,16,128]{3,2,1,0:T(8,128)(2,1)S(1)} %get-tuple-element.54.refs_0_), channel_id=1, source_target_pairs={{0,1},{1,0},{2,3},{3,2},{4,5},{5,4},{6,7},{7,6},{8,9},{9,8},{10,11... | collective-permute-start | bytes 786440 | tf_op jit(solution)/shard_map/ppermute | solution.py:515
  6.4 7.4 %collective-permute-start.2 = (bf16[8,4,16,128]{3,2,1,0:T(8,128)(2,1)S(1)}, bf16[8,4,16,128]{3,2,1,0:T(8,128)(2,1)S(1)}, u32[]{:S(2)}, u32[]{:S(2)}) collective-permute-start(bf16[8,4,16,128]{3,2,1,0:T(8,128)(2,1)S(1)} %constant_dynamic-update-slice_fusion), channel_id=1, source_target_pairs={{0,4},{8,0},{16,8},{24,16},{28,24},{20,28},{12,20},{4,12},{1,5},{9... | collective-permute-start | bytes 393224 | tf_op jit(solution)/shard_map/ppermute | solution.py:551
  8.4 5.4 %collective-permute-start.1 = (bf16[8,4,16,128]{3,2,1,0:T(8,128)(2,1)S(1)}, bf16[8,4,16,128]{3,2,1,0:T(8,128)(2,1)S(1)}, u32[]{:S(2)}, u32[]{:S(2)}) collective-permute-start(bf16[8,4,16,128]{3,2,1,0:T(8,128)(2,1)S(1)} %constant_dynamic-update-slice_fusion), channel_id=1, source_target_pairs={{0,8},{8,16},{16,24},{24,28},{28,20},{20,12},{12,4},{4,0},{1,9},{9... | collective-permute-start | bytes 393224 | tf_op jit(solution)/shard_map/ppermute | solution.py:548
  10.2 15.4 %copy-start.1 = (s32[4,8]{1,0:T(4,128)S(1)}, s32[4,8]{1,0:T(4,128)}, u32[]{:S(2)}) copy-start(s32[4,8]{1,0:T(4,128)} %plan.9) | copy-start | bytes 388
  10.2 15.4 %copy-start.2 = (bf16[2048,512]{1,0:T(8,128)(2,1)S(1)}, bf16[2048,512]{1,0:T(8,128)(2,1)}, u32[]{:S(2)}) copy-start(bf16[2048,512]{1,0:T(8,128)(2,1)} %constant.7.clone.table) | copy-start | bytes 6291460
  10.2 5.9 %collective-permute-start.9 = (bf16[8,4,16,128]{3,2,1,0:T(8,128)(2,1)S(1)}, bf16[8,4,16,128]{3,2,1,0:T(8,128)(2,1)S(1)}, u32[]{:S(2)}, u32[]{:S(2)}) collective-permute-start(bf16[8,4,16,128]{3,2,1,0:T(8,128)(2,1)S(1)} %pad_maximum_fusion), channel_id=1, source_target_pairs={{0,4},{8,0},{16,8},{24,16},{28,24},{20,28},{12,20},{4,12},{1,5},{9... | collective-permute-start | bytes 393224 | tf_op jit(solution)/shard_map/ppermute | solution.py:551
  11.8 6.3 %collective-permute-start.8 = (bf16[8,4,16,128]{3,2,1,0:T(8,128)(2,1)S(1)}, bf16[8,4,16,128]{3,2,1,0:T(8,128)(2,1)S(1)}, u32[]{:S(2)}, u32[]{:S(2)}) collective-permute-start(bf16[8,4,16,128]{3,2,1,0:T(8,128)(2,1)S(1)} %pad_maximum_fusion), channel_id=1, source_target_pairs={{0,8},{8,16},{16,24},{24,28},{28,20},{20,12},{12,4},{4,0},{1,9},{9... | collective-permute-start | bytes 393224 | tf_op jit(solution)/shard_map/ppermute | solution.py:548
  12.3 10.9 %collective-permute-start.12 = (bf16[4,16,16,128]{3,2,1,0:T(8,128)(2,1)S(1)}, bf16[4,16,16,128]{3,2,1,0:T(8,128)(2,1)S(1)}, u32[]{:S(2)}, u32[]{:S(2)}) collective-permute-start(bf16[4,16,16,128]{3,2,1,0:T(8,128)(2,1)S(1)} %get-tuple-element.54.refs_0_), channel_id=1, source_target_pairs={{0,2},{1,3},{2,0},{3,1},{4,6},{5,7},{6,4},{7,5},{8,10},{9,11},{10,... | collective-permute-start | bytes 786440 | tf_op jit(solution)/shard_map/ppermute | solution.py:515
  13.8 7.1 %collective-permute-start.4 = (bf16[8,4,16,128]{3,2,1,0:T(8,128)(2,1)S(1)}, bf16[8,4,16,128]{3,2,1,0:T(8,128)(2,1)S(1)}, u32[]{:S(2)}, u32[]{:S(2)}) collective-permute-start(bf16[8,4,16,128]{3,2,1,0:T(8,128)(2,1)S(1)} %collective-permute-done.1.rest_2_), channel_id=1, source_target_pairs={{0,8},{8,16},{16,24},{24,28},{28,20},{20,12},{12,4},{4,0},{1,9},{9... | collective-permute-start | bytes 393224 | tf_op jit(solution)/shard_map/ppermute | solution.py:548
  15.4 5.7 %collective-permute-start.5 = (bf16[8,4,16,128]{3,2,1,0:T(8,128)(2,1)S(1)}, bf16[8,4,16,128]{3,2,1,0:T(8,128)(2,1)S(1)}, u32[]{:S(2)}, u32[]{:S(2)}) collective-permute-start(bf16[8,4,16,128]{3,2,1,0:T(8,128)(2,1)S(1)} %collective-permute-done.2.rest_3_), channel_id=1, source_target_pairs={{0,4},{8,0},{16,8},{24,16},{28,24},{20,28},{12,20},{4,12},{1,5},{9... | collective-permute-start | bytes 393224 | tf_op jit(solution)/shard_map/ppermute | solution.py:551
  18.1 5.0 %collective-permute-start.10 = (bf16[8,4,16,128]{3,2,1,0:T(8,128)(2,1)S(1)}, bf16[8,4,16,128]{3,2,1,0:T(8,128)(2,1)S(1)}, u32[]{:S(2)}, u32[]{:S(2)}) collective-permute-start(bf16[8,4,16,128]{3,2,1,0:T(8,128)(2,1)S(1)} %collective-permute-done.8.rest_4_), channel_id=1, source_target_pairs={{0,8},{8,16},{16,24},{24,28},{28,20},{20,12},{12,4},{4,0},{1,9},{9... | collective-permute-start | bytes 393224 | tf_op jit(solution)/shard_map/ppermute | solution.py:548
  18.1 5.1 %collective-permute-start.11 = (bf16[8,4,16,128]{3,2,1,0:T(8,128)(2,1)S(1)}, bf16[8,4,16,128]{3,2,1,0:T(8,128)(2,1)S(1)}, u32[]{:S(2)}, u32[]{:S(2)}) collective-permute-start(bf16[8,4,16,128]{3,2,1,0:T(8,128)(2,1)S(1)} %collective-permute-done.9.rest_5_), channel_id=1, source_target_pairs={{0,4},{8,0},{16,8},{24,16},{28,24},{20,28},{12,20},{4,12},{1,5},{9... | collective-permute-start | bytes 393224 | tf_op jit(solution)/shard_map/ppermute | solution.py:551
  23.3 2.2 %collective-permute-start.13 = (bf16[4,16,16,128]{3,2,1,0:T(8,128)(2,1)S(1)}, bf16[4,16,16,128]{3,2,1,0:T(8,128)(2,1)S(1)}, u32[]{:S(2)}, u32[]{:S(2)}) collective-permute-start(bf16[4,16,16,128]{3,2,1,0:T(8,128)(2,1)S(1)} %collective-permute-done.12.refs_0_), channel_id=1, source_target_pairs={{0,1},{1,0},{2,3},{3,2},{4,5},{5,4},{6,7},{7,6},{8,9},{9,8},{10,11... | collective-permute-start | bytes 786440 | tf_op jit(solution)/shard_map/ppermute | solution.py:515
  23.3 8.9 %collective-permute-start.17 = (bf16[16,4,16,128]{3,2,1,0:T(8,128)(2,1)S(1)}, bf16[16,4,16,128]{3,2,1,0:T(8,128)(2,1)S(1)}, u32[]{:S(2)}, u32[]{:S(2)}) collective-permute-start(bf16[16,4,16,128]{3,2,1,0:T(8,128)(2,1)S(1)} %get-tuple-element.61), channel_id=1, source_target_pairs={{0,8},{8,16},{16,24},{24,28},{28,20},{20,12},{12,4},{4,0},{1,9},{9... | collective-permute-start | bytes 786440 | tf_op jit(solution)/shard_map/ppermute | solution.py:548
  25.0 8.7 %collective-permute-start.18 = (bf16[16,4,16,128]{3,2,1,0:T(8,128)(2,1)S(1)}, bf16[16,4,16,128]{3,2,1,0:T(8,128)(2,1)S(1)}, u32[]{:S(2)}, u32[]{:S(2)}) collective-permute-start(bf16[16,4,16,128]{3,2,1,0:T(8,128)(2,1)S(1)} %get-tuple-element.62), channel_id=1, source_target_pairs={{0,4},{8,0},{16,8},{24,16},{28,24},{20,28},{12,20},{4,12},{1,5},{9... | collective-permute-start | bytes 786440 | tf_op jit(solution)/shard_map/ppermute | solution.py:551
  28.2 9.9 %collective-permute-start.14 = (bf16[64,512]{1,0:T(8,128)(2,1)S(1)}, bf16[64,512]{1,0:T(8,128)(2,1)S(1)}, u32[]{:S(2)}, u32[]{:S(2)}) collective-permute-start(bf16[64,512]{1,0:T(8,128)(2,1)S(1)} %get-tuple-element.57), channel_id=1, source_target_pairs={{0,1},{1,0},{2,3},{3,2},{4,5},{5,4},{6,7},{7,6},{8,9},{9,8},{10,11... | collective-permute-start | bytes 196616 | tf_op jit(solution)/shard_map/ppermute | solution.py:515
  28.3 11.5 %collective-permute-start.15 = (bf16[64,512]{1,0:T(8,128)(2,1)S(1)}, bf16[64,512]{1,0:T(8,128)(2,1)S(1)}, u32[]{:S(2)}, u32[]{:S(2)}) collective-permute-start(bf16[64,512]{1,0:T(8,128)(2,1)S(1)} %get-tuple-element.58), channel_id=1, source_target_pairs={{0,2},{1,3},{2,0},{3,1},{4,6},{5,7},{6,4},{7,5},{8,10},{9,11},{10,... | collective-permute-start | bytes 196616 | tf_op jit(solution)/shard_map/ppermute | solution.py:515
  30.0 9.9 %collective-permute-start.16 = (bf16[64,512]{1,0:T(8,128)(2,1)S(1)}, bf16[64,512]{1,0:T(8,128)(2,1)S(1)}, u32[]{:S(2)}, u32[]{:S(2)}) collective-permute-start(bf16[64,512]{1,0:T(8,128)(2,1)S(1)} %get-tuple-element.59), channel_id=1, source_target_pairs={{0,3},{1,2},{2,1},{3,0},{4,7},{5,6},{6,5},{7,4},{8,11},{9,10},{10,... | collective-permute-start | bytes 196616 | tf_op jit(solution)/shard_map/ppermute | solution.py:515
  32.2 8.1 %collective-permute-start.22 = (bf16[16,4,16,128]{3,2,1,0:T(8,128)(2,1)S(1)}, bf16[16,4,16,128]{3,2,1,0:T(8,128)(2,1)S(1)}, u32[]{:S(2)}, u32[]{:S(2)}) collective-permute-start(bf16[16,4,16,128]{3,2,1,0:T(8,128)(2,1)S(1)} %collective-permute-done.17.rest_10_), channel_id=1, source_target_pairs={{0,8},{8,16},{16,24},{24,28},{28,20},{20,12},{12,4},{4,0},{1,9},{9... | collective-permute-start | bytes 786440 | tf_op jit(solution)/shard_map/ppermute | solution.py:548
  38.0 6.7 %collective-permute-start.19 = (bf16[128,512]{1,0:T(8,128)(2,1)S(1)}, bf16[128,512]{1,0:T(8,128)(2,1)S(1)}, u32[]{:S(2)}, u32[]{:S(2)}) collective-permute-start(bf16[128,512]{1,0:T(8,128)(2,1)S(1)} %get-tuple-element.64), channel_id=1, source_target_pairs={{0,1},{1,0},{2,3},{3,2},{4,5},{5,4},{6,7},{7,6},{8,9},{9,8},{10,11... | collective-permute-start | bytes 393224 | tf_op jit(solution)/shard_map/ppermute | solution.py:515
  38.1 6.8 %collective-permute-start.20 = (bf16[128,512]{1,0:T(8,128)(2,1)S(1)}, bf16[128,512]{1,0:T(8,128)(2,1)S(1)}, u32[]{:S(2)}, u32[]{:S(2)}) collective-permute-start(bf16[128,512]{1,0:T(8,128)(2,1)S(1)} %get-tuple-element.65), channel_id=1, source_target_pairs={{0,2},{1,3},{2,0},{3,1},{4,6},{5,7},{6,4},{7,5},{8,10},{9,11},{10,... | collective-permute-start | bytes 393224 | tf_op jit(solution)/shard_map/ppermute | solution.py:515
  39.8 6.6 %collective-permute-start.21 = (bf16[128,512]{1,0:T(8,128)(2,1)S(1)}, bf16[128,512]{1,0:T(8,128)(2,1)S(1)}, u32[]{:S(2)}, u32[]{:S(2)}) collective-permute-start(bf16[128,512]{1,0:T(8,128)(2,1)S(1)} %get-tuple-element.66), channel_id=1, source_target_pairs={{0,3},{1,2},{2,1},{3,0},{4,7},{5,6},{6,5},{7,4},{8,11},{9,10},{10,... | collective-permute-start | bytes 393224 | tf_op jit(solution)/shard_map/ppermute | solution.py:515
  40.0 6.5 %copy-start = (bf16[4,128,512]{2,1,0:T(8,128)(2,1)S(1)}, bf16[4,128,512]{2,1,0:T(8,128)(2,1)}, u32[]{:S(2)}) copy-start(bf16[4,128,512]{2,1,0:T(8,128)(2,1)} %constant.8.clone.place) | copy-start | bytes 1572868
  42.9 5.7 %collective-permute-start.23 = (bf16[64,512]{1,0:T(8,128)(2,1)S(1)}, bf16[64,512]{1,0:T(8,128)(2,1)S(1)}, u32[]{:S(2)}, u32[]{:S(2)}) collective-permute-start(bf16[64,512]{1,0:T(8,128)(2,1)S(1)} %get-tuple-element.70), channel_id=1, source_target_pairs={{0,1},{1,0},{2,3},{3,2},{4,5},{5,4},{6,7},{7,6},{8,9},{9,8},{10,11... | collective-permute-start | bytes 196616 | tf_op jit(solution)/shard_map/ppermute | solution.py:515
  43.0 5.7 %collective-permute-start.24 = (bf16[64,512]{1,0:T(8,128)(2,1)S(1)}, bf16[64,512]{1,0:T(8,128)(2,1)S(1)}, u32[]{:S(2)}, u32[]{:S(2)}) collective-permute-start(bf16[64,512]{1,0:T(8,128)(2,1)S(1)} %get-tuple-element.71), channel_id=1, source_target_pairs={{0,2},{1,3},{2,0},{3,1},{4,6},{5,7},{6,4},{7,5},{8,10},{9,11},{10,... | collective-permute-start | bytes 196616 | tf_op jit(solution)/shard_map/ppermute | solution.py:515
  44.7 4.4 %collective-permute-start.25 = (bf16[64,512]{1,0:T(8,128)(2,1)S(1)}, bf16[64,512]{1,0:T(8,128)(2,1)S(1)}, u32[]{:S(2)}, u32[]{:S(2)}) collective-permute-start(bf16[64,512]{1,0:T(8,128)(2,1)S(1)} %get-tuple-element.72), channel_id=1, source_target_pairs={{0,3},{1,2},{2,1},{3,0},{4,7},{5,6},{6,5},{7,4},{8,11},{9,10},{10,... | collective-permute-start | bytes 196616 | tf_op jit(solution)/shard_map/ppermute | solution.py:515
